TPU v7x, 32 devices: a whole 2x2x4 slice. The times are simulated.
32 devices in a mesh: step: 8 (over z, x), seq: 4 (over y, core).
Axes of the slice: x: 2, y: 2, z: 4, core: 2. Of those that a mesh axis runs over, the one named last changes fastest.
Arguments:
- trajectory: float32 [8, 512, 3072], P('step', 'seq'), may hold values from -6 to 6
- x_start: float32 [512, 3072], P('seq'), may hold values from -6 to 6
- t_idx: int32 [8], P('step'), may hold values from 0 to 49
- mod_table: float32 [50, 9216], replicated, may hold values from -3 to 3
- step_sizes: float32 [50], replicated, may hold values from 0.05 to 0.3
- q_gain: float32 [128], replicated, may hold values from 1 to 10, as said below
- k_gain: float32 [128], replicated, may hold values from 1 to 10, as said below
- w_qkv: bfloat16 [3, 3072, 2048], P(None, None, 'seq'), may hold values from -0.109375 to 0.109375
- w_mlp_in: bfloat16 [3072, 6144], P(None, 'seq'), may hold values from -0.109375 to 0.109375
- w_out_attn: bfloat16 [2048, 3072], P('seq'), may hold values from -0.0625 to 0.0625
- w_out_mlp: bfloat16 [6144, 3072], P('seq'), may hold values from -0.0625 to 0.0625
Outputs:
- x_next: float32 [8, 512, 3072], P('step', 'seq')
Inputs may be any that keep to these rules, and one draw needn't show every extreme that they name: `q_gain`: positive gains. `k_gain`: positive gains.
All inputs are finite; a program needn't handle non-finite values.
Results may differ from a plain program's by a relative error of at most 0.011.
Values may be sent and summed in bfloat16 or wider, within the bound.
No kernel may reach another device: no remote copies, remote signals or barrier semaphores. Data moves between devices by JAX's collectives and lax.ppermute only.
A program may use at most 128 MiB of HBM per device.

v0:
```python
import math

import jax
import jax.numpy as jnp
from jax import lax
from jax.sharding import PartitionSpec as P

eps = 1e-06


def prefix(shard, axis, join, neutral):
    place = lax.axis_index(axis)
    gathered = lax.all_gather(shard.astype(jnp.bfloat16), axis)
    state = jnp.zeros_like(shard) + jnp.asarray(neutral, shard.dtype)

    def one(lap, state):
        return join(state, lax.dynamic_index_in_dim(gathered, lap, 0, False).astype(shard.dtype))

    return lax.fori_loop(0, place, one, state)


def layer_norm(state):
    center = state - jnp.mean(state, axis=-1, keepdims=True)
    spread = jnp.mean(center * center, axis=-1, keepdims=True)
    return center * lax.rsqrt(spread + eps)


def head_norm(projected, gain):
    square = jnp.mean(projected * projected, axis=-1, keepdims=True)
    return (projected * lax.rsqrt(square + eps) * gain).astype(jnp.bfloat16)


def add_terms(earlier, later):
    return earlier + later


def per_device(
    trajectory,
    x_start,
    t_idx,
    mod_table,
    step_sizes,
    q_gain,
    k_gain,
    w_qkv,
    w_mlp_in,
    w_out_attn,
    w_out_mlp,
):
    state = trajectory[0]
    width = state.shape[1]
    head_dim = q_gain.shape[0]
    local_cols = w_qkv.shape[2]
    local_heads = local_cols // head_dim
    table_rows = mod_table.shape[0]
    one_hot = (jnp.arange(table_rows, dtype=jnp.int32) == t_idx[0]).astype(jnp.float32)
    modulation = jnp.dot(
        one_hot[None, :],
        mod_table,
        precision=lax.Precision.HIGHEST,
        preferred_element_type=jnp.float32,
    )[0]
    step_size = jnp.sum(one_hot * step_sizes)
    shift_mod = modulation[:width]
    scale_mod = modulation[width : 2 * width]
    gate_mod = modulation[2 * width :]
    modulated = (layer_norm(state) * (1.0 + scale_mod) + shift_mod).astype(jnp.bfloat16)
    piece = lax.all_gather(modulated, "seq", axis=0, tiled=True)
    piece_rows = piece.shape[0]

    def heads_of(which):
        return jnp.dot(piece, w_qkv[which], preferred_element_type=jnp.float32).reshape(
            piece_rows, local_heads, head_dim
        )

    queries = head_norm(heads_of(0), q_gain).reshape(piece_rows, local_cols)
    key_rows = head_norm(heads_of(1), k_gain).reshape(piece_rows, local_cols)
    value_rows = jnp.dot(piece, w_qkv[2], preferred_element_type=jnp.float32).astype(jnp.bfloat16)
    project_activated = jax.nn.gelu(
        jnp.dot(piece, w_mlp_in, preferred_element_type=jnp.float32), approximate=True
    ).astype(jnp.bfloat16)
    joined = jnp.concatenate([queries, key_rows, value_rows, project_activated], axis=1)
    all_rows = joined.shape[0]
    queries = joined[:, :local_cols].reshape(all_rows, local_heads, head_dim)
    key_rows = joined[:, local_cols : 2 * local_cols].reshape(all_rows, local_heads, head_dim)
    value_rows = joined[:, 2 * local_cols : 3 * local_cols].reshape(all_rows, local_heads, head_dim)
    activated = joined[:, 3 * local_cols :]
    scores = jnp.einsum(
        "qhd,khd->hqk", queries, key_rows, preferred_element_type=jnp.float32
    ) / math.sqrt(head_dim)
    probs = jax.nn.softmax(scores, axis=-1).astype(jnp.bfloat16)
    attended = (
        jnp.einsum("hqk,khd->qhd", probs, value_rows, preferred_element_type=jnp.float32)
        .astype(jnp.bfloat16)
        .reshape(all_rows, local_cols)
    )
    total = jnp.dot(attended, w_out_attn, preferred_element_type=jnp.float32)
    branch = lax.psum_scatter(
        (total + jnp.dot(activated, w_out_mlp, preferred_element_type=jnp.float32)).astype(
            jnp.bfloat16
        ),
        "seq",
        scatter_dimension=0,
        tiled=True,
    ).astype(jnp.float32)
    drift = step_size * (gate_mod * branch)
    earlier = prefix(drift, "step", add_terms, jnp.zeros_like(drift))
    result = x_start + earlier + drift
    return result[None]


def solution(mesh):
    placed = (
        P("step", "seq", None),
        P("seq", None),
        P("step"),
        P(),
        P(),
        P(),
        P(),
        P(None, None, "seq"),
        P(None, "seq"),
        P("seq", None),
        P("seq", None),
    )
    return jax.shard_map(
        per_device, mesh=mesh, in_specs=placed, out_specs=P("step", "seq", None), check_vma=False
    )
```

profile of v0, /device:TPU:27, one launch (start us, length us, event | category | flops | bytes accessed | tf_op | source)
XLA Modules:
  0.0 263.5 jit_solution(6290339036008417570)
XLA Ops:
  6.5 0.0 copy-start
  6.5 0.0 all-gather.4.cloned.1.call-start
  7.3 2.5 fusion.41
  9.9 1.6 reduce_sum.55
  11.4 1.7 multiply_reduce_fusion.1
  13.2 2.6 add_convert_fusion.1
  15.8 0.0 all-gather.4.cloned.1.call-update
  15.8 0.0 reduce-scatter.2.cloned.1.call-start
  15.9 5.9 %slice_bitcast_fusion = (bf16[512,3072]{0,1:T(8,128)(2,1)}, bf16[512,3072]{0,1:T(8,128)(2,1)}) fusion(bf16[3,3072,512]{2,1,0:T(8,128)(2,1)} %param.20), kind=kLoop, calls=%fused_computation.22 | loop fusion | bytes 12582912 | tf_op jit(solution)/shard_map/dot_general | solution.py:72
  21.8 4.8 %copy.13 = bf16[512,3072]{1,0:T(8,128)(2,1)} copy(bf16[512,3072]{0,1:T(8,128)(2,1)} %get-tuple-element.37) | data formatting | bytes 6291456 | tf_op jit(solution)/shard_map/dot_general | solution.py:72
  26.6 4.6 %copy.12 = bf16[512,3072]{1,0:T(8,128)(2,1)} copy(bf16[512,3072]{0,1:T(8,128)(2,1)} %get-tuple-element.38) | data formatting | bytes 6291456 | tf_op jit(solution)/shard_map/dot_general | solution.py:72
  31.2 14.6 %all-gather.4.cloned.1.call-done = bf16[512,3072]{1,0:T(8,128)(2,1)} async-done(((bf16[128,3072]{1,0:T(8,128)(2,1)}), bf16[512,3072]{1,0:T(8,128)(2,1)}) %all-gather.4.cloned.1.call-update) | async-done | bytes 3145744 | tf_op jit(solution)/shard_map/all_gather | solution.py:68
  45.9 0.0 copy-start.2
  45.9 0.0 copy-start.5
  45.9 4.8 %multiply_reduce_fusion.2 = (f32[512,4]{0,1:T(4,128)S(1)}, f32[512,4,128]{0,2,1:T(8,128)S(1)}) fusion(bf16[4,128,3072]{2,1,0:T(8,128)(2,1)} %bitcast.60, bf16[512,3072]{1,0:T(8,128)(2,1)} %all-gather.4.cloned.1.call-done), kind=kOutput, calls=%fused_computation.41 | convolution fusion | flops 1611134976 | bytes 7348224 | tf_op jit(solution)/shard_map/dot_general | solution.py:72
  50.7 0.0 copy-done.2
  50.7 0.0 copy-done.5
  50.7 0.0 copy-start.3
  50.7 0.0 copy-start.4
  50.7 1.9 multiply_reduce_fusion.3
  52.6 0.0 copy-done.3
  52.6 0.0 copy-done.4
  52.6 0.8 fusion.32
  53.5 0.0 copy-start.1
  53.5 1.9 copy-done.1
  55.4 1.1 fusion.56
  56.5 4.5 %fusion.28 = bf16[512,512]{0,1:T(8,128)(2,1)} fusion(bf16[512,3072]{1,0:T(8,128)(2,1)S(1)} %copy-done.5, bf16[3,3072,512]{2,1,0:T(8,128)(2,1)} %param.20), kind=kOutput, calls=%fused_computation.38 | convolution fusion | flops 1610874880 | bytes 6815744 | tf_op jit(solution)/shard_map/dot_general | solution.py:78
  61.0 6.0 %fusion.31 = bf16[4,128,512]{2,1,0:T(8,128)(2,1)} fusion(bf16[512,4,128]{0,2,1:T(8,128)(2,1)} %bitcast.64, f32[4,512]{1,0:T(4,128)S(1)} %fusion.56, f32[4,512,512]{1,2,0:T(8,128)} %copy-done.1), kind=kOutput, calls=%fused_computation.39 | convolution fusion | flops 273943040 | bytes 5251072 | tf_op jit(solution)/shard_map/hqk,khd->qhd/dot_general | solution.py:93
  67.0 20.4 %fusion.21 = f32[512,3072]{1,0:T(8,128)} fusion(bf16[1536,3072]{1,0:T(8,128)(2,1)} %param.23, bf16[512,3072]{1,0:T(8,128)(2,1)} %all-gather.4.cloned.1.call-done, bf16[3072,1536]{1,0:T(8,128)(2,1)} %param.21), kind=kOutput, calls=%fused_computation.27 | convolution fusion | flops 9670754304 | bytes 28311552 | tf_op jit(solution)/shard_map/dot_general | solution.py:99
  87.4 0.0 copy-done
  87.4 6.5 %add_convert_fusion = bf16[512,3072]{1,0:T(8,128)(2,1)} fusion(f32[512,3072]{1,0:T(8,128)} %fusion.21, bf16[512,512]{0,1:T(8,128)(2,1)} %bitcast.62, bf16[512,3072]{1,0:T(8,128)(2,1)S(1)} %copy-done), kind=kOutput, calls=%fused_computation.2 | convolution fusion | flops 1613758464 | bytes 13107200 | tf_op jit(solution)/shard_map/dot_general | solution.py:97
  94.0 0.0 copy-start.6
  94.0 0.0 reduce-scatter.2.cloned.1.call-update
  94.0 0.0 all-gather.6.cloned.1.call-start
  94.0 0.6 copy-done.6
  94.6 0.7 fusion.45
  95.3 36.4 %reduce-scatter.2.cloned.1.call-done = bf16[128,3072]{1,0:T(8,128)(2,1)} async-done(((bf16[512,3072]{1,0:T(8,128)(2,1)}), bf16[128,3072]{1,0:T(8,128)(2,1)}) %reduce-scatter.2.cloned.1.call-update) | async-done | bytes 786448 | tf_op jit(solution)/shard_map/reduce_scatter | solution.py:98
  131.7 2.8 %fusion.23 = bf16[128,3072]{1,0:T(8,128)(2,1)} fusion(bf16[128,3072]{1,0:T(8,128)(2,1)} %reduce-scatter.2.cloned.1.call-done, f32[3072]{0:T(1024)S(1)} %get-tuple-element.39, f32[]{:T(128)} %fusion.45), kind=kLoop, calls=%fused_computation.31 | loop fusion | flops 1572864 | bytes 1585156 | tf_op jit(solution)/shard_map/convert_element_type | solution.py:13
  134.6 0.0 all-gather.6.cloned.1.call-update
  134.6 96.6 %all-gather.6.cloned.1.call-done = bf16[1024,3072]{1,0:T(8,128)(2,1)} async-done(((bf16[128,3072]{1,0:T(8,128)(2,1)}), bf16[1024,3072]{1,0:T(8,128)(2,1)}) %all-gather.6.cloned.1.call-update) | async-done | bytes 6291472 | tf_op jit(solution)/shard_map/all_gather | solution.py:13
  231.2 1.3 broadcast_in_dim.4
  232.5 20.4 %while.10 = (s32[]{:T(128)}, f32[128,3072]{1,0:T(8,128)}, s32[]{:T(128)}, bf16[8,128,3072]{2,1,0:T(8,128)(2,1)}, s32[]{:T(128)}, /*index=5*/s32[]{:T(128)}, s32[]{:T(128)}) while((s32[]{:T(128)}, f32[128,3072]{1,0:T(8,128)}, s32[]{:T(128)}, bf16[8,128,3072]{2,1,0:T(8,128)(2,1)}, s32[]{:T(128)}, /*index=5*/s32[]{:T(128)}, s32[]{:T(128)}) %tuple.33), condition=%wide.region_9.10_spmd, body=%wide.region_8.9_spmd.sunk | while | flops 786437 | bytes 3932275 | solution.py:19
  232.5 2.9 %convert_add_fusion.2 = f32[128,3072]{1,0:T(8,128)} fusion(f32[128,3072]{1,0:T(8,128)} %get-tuple-element.82, bf16[8,128,3072]{2,1,0:T(8,128)(2,1)} %get-tuple-element.91, s32[]{:T(128)S(6)} %select_n.5), kind=kLoop, calls=%fused_computation.clone.1 | loop fusion | flops 786432 | bytes 3932164 | tf_op jit(solution)/shard_map/while/body/add | solution.py:34
  235.4 2.9 %convert_add_fusion.2 = f32[128,3072]{1,0:T(8,128)} fusion(f32[128,3072]{1,0:T(8,128)} %get-tuple-element.82, bf16[8,128,3072]{2,1,0:T(8,128)(2,1)} %get-tuple-element.91, s32[]{:T(128)S(6)} %select_n.5), kind=kLoop, calls=%fused_computation.clone.1 | loop fusion | flops 786432 | bytes 3932164 | tf_op jit(solution)/shard_map/while/body/add | solution.py:34
  238.3 2.9 %convert_add_fusion.2 = f32[128,3072]{1,0:T(8,128)} fusion(f32[128,3072]{1,0:T(8,128)} %get-tuple-element.82, bf16[8,128,3072]{2,1,0:T(8,128)(2,1)} %get-tuple-element.91, s32[]{:T(128)S(6)} %select_n.5), kind=kLoop, calls=%fused_computation.clone.1 | loop fusion | flops 786432 | bytes 3932164 | tf_op jit(solution)/shard_map/while/body/add | solution.py:34
  241.2 2.9 %convert_add_fusion.2 = f32[128,3072]{1,0:T(8,128)} fusion(f32[128,3072]{1,0:T(8,128)} %get-tuple-element.82, bf16[8,128,3072]{2,1,0:T(8,128)(2,1)} %get-tuple-element.91, s32[]{:T(128)S(6)} %select_n.5), kind=kLoop, calls=%fused_computation.clone.1 | loop fusion | flops 786432 | bytes 3932164 | tf_op jit(solution)/shard_map/while/body/add | solution.py:34
  244.1 2.9 %convert_add_fusion.2 = f32[128,3072]{1,0:T(8,128)} fusion(f32[128,3072]{1,0:T(8,128)} %get-tuple-element.82, bf16[8,128,3072]{2,1,0:T(8,128)(2,1)} %get-tuple-element.91, s32[]{:T(128)S(6)} %select_n.5), kind=kLoop, calls=%fused_computation.clone.1 | loop fusion | flops 786432 | bytes 3932164 | tf_op jit(solution)/shard_map/while/body/add | solution.py:34
  247.0 2.9 %convert_add_fusion.2 = f32[128,3072]{1,0:T(8,128)} fusion(f32[128,3072]{1,0:T(8,128)} %get-tuple-element.82, bf16[8,128,3072]{2,1,0:T(8,128)(2,1)} %get-tuple-element.91, s32[]{:T(128)S(6)} %select_n.5), kind=kLoop, calls=%fused_computation.clone.1 | loop fusion | flops 786432 | bytes 3932164 | tf_op jit(solution)/shard_map/while/body/add | solution.py:34
  249.9 2.9 %convert_add_fusion.2 = f32[128,3072]{1,0:T(8,128)} fusion(f32[128,3072]{1,0:T(8,128)} %get-tuple-element.82, bf16[8,128,3072]{2,1,0:T(8,128)(2,1)} %get-tuple-element.91, s32[]{:T(128)S(6)} %select_n.5), kind=kLoop, calls=%fused_computation.clone.1 | loop fusion | flops 786432 | bytes 3932164 | tf_op jit(solution)/shard_map/while/body/add | solution.py:34
  252.8 4.2 %add_bitcast_fusion = f32[1,128,3072]{2,1,0:T(8,128)} fusion(f32[128,3072]{1,0:T(8,128)} %param.14, f32[128,3072]{1,0:T(8,128)} %get-tuple-element.28, bf16[128,3072]{1,0:T(8,128)(2,1)} %reduce-scatter.2.cloned.1.call-done, f32[3072]{0:T(1024)S(1)} %get-tuple-element.39, f32[]{:T(128)} %fusion.45), kind=kLoop, calls=%fused_computation.29 | loop fusion | flops 1966080 | bytes 5517316 | tf_op jit(solution)/shard_map/broadcast_in_dim | solution.py:109
  (4 shorter events, 0.0 us)
Async XLA Ops:
  6.5 80.9 %copy-start = (bf16[512,3072]{1,0:T(8,128)(2,1)S(1)}, bf16[512,3072]{1,0:T(8,128)(2,1)}, u32[]{:S(2)}) copy-start(bf16[512,3072]{1,0:T(8,128)(2,1)} %param.22) | copy-start | bytes 9437188
  6.5 39.3 %all-gather.4.cloned.1.call-start = ((), (), s32[]{:S(2)}) async-start(), calls=%async_computation.1 | async-start | bytes 3932160 | tf_op jit(solution)/shard_map/all_gather | solution.py:68
  15.8 115.9 %reduce-scatter.2.cloned.1.call-start = ((), (), s32[]{:S(2)}) async-start(), calls=%async_computation.2 | async-start | bytes 3932160 | tf_op jit(solution)/shard_map/reduce_scatter | solution.py:98
  45.9 4.8 %copy-start.2 = (bf16[512,3072]{1,0:T(8,128)(2,1)S(1)}, bf16[512,3072]{1,0:T(8,128)(2,1)}, u32[]{:S(2)}) copy-start(bf16[512,3072]{1,0:T(8,128)(2,1)} %copy.12) | copy-start | bytes 9437188
  45.9 4.8 %copy-start.5 = (bf16[512,3072]{1,0:T(8,128)(2,1)S(1)}, bf16[512,3072]{1,0:T(8,128)(2,1)}, u32[]{:S(2)}) copy-start(bf16[512,3072]{1,0:T(8,128)(2,1)} %all-gather.4.cloned.1.call-done) | copy-start | bytes 9437188
  50.7 1.9 copy-start.3
  50.7 1.9 copy-start.4
  53.5 1.9 copy-start.1
  94.0 0.7 copy-start.6
  94.0 137.2 %all-gather.6.cloned.1.call-start = ((), (), s32[]{:S(2)}) async-start(), calls=%async_computation.3 | async-start | bytes 7077888 | tf_op jit(solution)/shard_map/all_gather | solution.py:13
Sparse Core Ops, SparseCore 0:
  15.9 29.8 all-gather.3
  94.1 37.5 reduce-scatter.1
  134.7 96.4 all-gather.5
where the time goes:
time: 264 us
  waiting for transfers between devices  148 us (56%)
  matrix products  47.5 us (18%)
  other arithmetic  35.1 us (13%)
  local copies, waits for them, and re-layouts  19.2 us (7%)
  between operations  14 us (5%)
    all_gather x1, waiting for transfers between devices, prefix(): gathered = lax.all_gather(shard.astype(jnp.bfloat16), axis)  96.6 us
    reduce_scatter x1, waiting for transfers between devices, per_device(): lax.psum_scatter((total + jnp.dot(activated, w_out_mlp, preferred_element...  36.4 us
    dot_general x1, matrix products, per_device(): jnp.dot(activated, w_out_mlp, preferred_element_type=jnp.float32)  20.4 us
    add x7, other arithmetic, add_terms(): return earlier + later  20.4 us
    dot_general x3, local copies, waits for them, and re-layouts, heads_of(): jnp.dot(piece, w_qkv[which], preferred_element_type=jnp.float32)  15.4 us
    all_gather x1, waiting for transfers between devices, per_device(): piece = lax.all_gather(modulated, 'seq', axis=0, tiled=True)  14.6 us
    dot_general x2, matrix products, heads_of(): jnp.dot(piece, w_qkv[which], preferred_element_type=jnp.float32)  6.68 us
    dot_general x1, matrix products, per_device(): total = jnp.dot(attended, w_out_attn, preferred_element_type=jnp.float32)  6.51 us
  transfers between devices with their start and end apart: 3, of which 3 were waited for; matrix products, arithmetic and copies ran while one was open for 6% of the time, Pallas kernels for 0%

commit v1 on v0

v1 whole, which is shorter than its diff:
```python
import functools
import math

import jax
import jax.numpy as jnp
from jax import lax
from jax.experimental import pallas as pl
from jax.experimental.pallas import tpu as pltpu
from jax.sharding import PartitionSpec as P

eps = 1e-06
f32 = jnp.float32
bf16 = jnp.bfloat16
VM = pltpu.VMEM
VMEM_BYTES = 48 * 1024 * 1024


def params():
    return pltpu.CompilerParams(vmem_limit_bytes=VMEM_BYTES)


def norm_kernel(t_ref, x_ref, mod_ref, size_ref, m_ref, sg_ref):
    width = x_ref.shape[-1]
    row = lax.rem(t_ref[0], 8)
    shift = mod_ref[pl.ds(row, 1), :width]
    scale = mod_ref[pl.ds(row, 1), width : 2 * width]
    gate = mod_ref[pl.ds(row, 1), 2 * width :]
    sg_ref[...] = size_ref[t_ref[0]] * gate
    x = x_ref[0]
    center = x - jnp.mean(x, axis=-1, keepdims=True)
    spread = jnp.mean(center * center, axis=-1, keepdims=True)
    m_ref[...] = (center * lax.rsqrt(spread + eps) * (1.0 + scale) + shift).astype(bf16)


def norm_call(t_idx, trajectory, mod_table, step_sizes):
    _, rows, width = trajectory.shape
    block = 64
    return pl.pallas_call(
        norm_kernel,
        grid_spec=pltpu.PrefetchScalarGridSpec(
            num_scalar_prefetch=1,
            grid=(rows // block,),
            in_specs=[
                pl.BlockSpec((1, block, width), lambda i, t: (0, i, 0)),
                pl.BlockSpec((8, 3 * width), lambda i, t: (t[0] // 8, 0)),
                pl.BlockSpec(memory_space=pltpu.SMEM),
            ],
            out_specs=[
                pl.BlockSpec((block, width), lambda i, t: (i, 0)),
                pl.BlockSpec((1, width), lambda i, t: (0, 0)),
            ],
        ),
        out_shape=[
            jax.ShapeDtypeStruct((rows, width), bf16),
            jax.ShapeDtypeStruct((1, width), f32),
        ],
        compiler_params=params(),
        name="norm",
    )(t_idx, trajectory, mod_table, step_sizes)


def project_kernel(tile, m0, m1, qg, kg, wq_hbm, wm_hbm, q, k, v, act, rows, wq, wm, sem_q, sem_m):
    half = m0.shape[0]
    head = qg.shape[1]
    n_q = wq.shape[2] // tile
    n_m = wm.shape[1] // tile
    copies = []
    for which in range(3):
        for i in range(n_q):
            cols = pl.ds(i * tile, tile)
            copies.append(
                pltpu.make_async_copy(
                    wq_hbm.at[which, :, cols], wq.at[which, :, cols], sem_q.at[which * n_q + i]
                )
            )
    for i in range(n_m):
        cols = pl.ds(i * tile, tile)
        copies.append(pltpu.make_async_copy(wm_hbm.at[:, cols], wm.at[:, cols], sem_m.at[i]))
    for copy in copies:
        copy.start()
    rows[:half] = m0[...]
    rows[half:] = m1[...]
    x = rows[...]

    def normed(y, gain):
        parts = []
        for h in range(tile // head):
            one = y[:, h * head : (h + 1) * head]
            square = jnp.mean(one * one, axis=-1, keepdims=True)
            parts.append((one * lax.rsqrt(square + eps) * gain).astype(bf16))
        return jnp.concatenate(parts, axis=1)

    for which in range(3):
        for i in range(n_q):
            copies[which * n_q + i].wait()
            cols = slice(i * tile, (i + 1) * tile)
            y = jnp.dot(x, wq[which, :, cols], preferred_element_type=f32)
            if which == 0:
                q[:, cols] = normed(y, qg[...])
            elif which == 1:
                k[:, cols] = normed(y, kg[...])
            else:
                v[:, cols] = y.astype(bf16)
    for i in range(n_m):
        copies[3 * n_q + i].wait()
        cols = slice(i * tile, (i + 1) * tile)
        y = jnp.dot(x, wm[:, cols], preferred_element_type=f32)
        act[:, cols] = jax.nn.gelu(y, approximate=True).astype(bf16)


def project_call(m0, m1, q_gain, k_gain, w_qkv, w_mlp_in):
    half, width = m0.shape
    heads = w_qkv.shape[2]
    hidden = w_mlp_in.shape[1]
    tile = 256
    rows = 2 * half
    vm = pl.BlockSpec(memory_space=VM)
    hbm = pl.BlockSpec(memory_space=pl.ANY)
    return pl.pallas_call(
        functools.partial(project_kernel, tile),
        in_specs=[vm, vm, vm, vm, hbm, hbm],
        out_specs=[vm] * 4,
        out_shape=[jax.ShapeDtypeStruct((rows, heads), bf16)] * 3
        + [jax.ShapeDtypeStruct((rows, hidden), bf16)],
        scratch_shapes=[
            VM((rows, width), bf16),
            VM((3, width, heads), bf16),
            VM((width, hidden), bf16),
            pltpu.SemaphoreType.DMA((3 * heads // tile,)),
            pltpu.SemaphoreType.DMA((hidden // tile,)),
        ],
        compiler_params=params(),
        name="project",
    )(m0, m1, q_gain, k_gain, w_qkv, w_mlp_in)


def attend_kernel(pairs, head, *refs):
    q_ref = refs[0]
    k_refs = refs[1 : 1 + pairs]
    v_refs = refs[1 + pairs : 1 + 2 * pairs]
    out = refs[1 + 2 * pairs]
    scale = math.log2(math.e) / math.sqrt(head)
    for h in range(q_ref.shape[1] // head):
        cols = slice(h * head, (h + 1) * head)
        q = q_ref[:, cols]
        scores = [
            lax.dot_general(q, k[:, cols], (((1,), (1,)), ((), ())), preferred_element_type=f32)
            for k in k_refs
        ]
        top = functools.reduce(
            jnp.maximum, [jnp.max(s, axis=-1, keepdims=True) for s in scores]
        )
        weights = [jnp.exp2((s - top) * scale) for s in scores]
        total = sum(jnp.sum(w, axis=-1, keepdims=True) for w in weights)
        inverse = 1.0 / total
        mixed = sum(
            jnp.dot((w * inverse).astype(bf16), v[:, cols], preferred_element_type=f32)
            for w, v in zip(weights, v_refs)
        )
        out[:, cols] = mixed.astype(bf16)


def attend_call(q, ks, vs, head):
    vm = pl.BlockSpec(memory_space=VM)
    return pl.pallas_call(
        functools.partial(attend_kernel, len(ks), head),
        in_specs=[vm] * (1 + 2 * len(ks)),
        out_specs=vm,
        out_shape=jax.ShapeDtypeStruct(q.shape, bf16),
        compiler_params=params(),
        name="attend",
    )(q, *ks, *vs)


def out_kernel(tile, first, a, b, wa_hbm, wb_hbm, keep, send, wa, wb, sem_a, sem_b):
    half = keep.shape[0]
    n = keep.shape[1] // tile
    copies = []
    for i in range(n):
        here = pl.ds(i * tile, tile)
        there = pl.ds(first + i * tile, tile)
        copies.append(
            (
                pltpu.make_async_copy(wa_hbm.at[:, there], wa.at[:, here], sem_a.at[i]),
                pltpu.make_async_copy(wb_hbm.at[:, there], wb.at[:, here], sem_b.at[i]),
            )
        )
    for pair in copies:
        pair[0].start()
        pair[1].start()
    for i in range(n):
        cols = slice(i * tile, (i + 1) * tile)
        copies[i][0].wait()
        copies[i][1].wait()
        y = jnp.dot(a[...], wa[:, cols], preferred_element_type=f32)
        y = y + jnp.dot(b[...], wb[:, cols], preferred_element_type=f32)
        keep[:, cols] = y[:half]
        send[:, cols] = y[half:].astype(bf16)


def out_call(a, b, w_out_attn, w_out_mlp, first, count):
    half = a.shape[0] // 2
    tile = 256
    vm = pl.BlockSpec(memory_space=VM)
    hbm = pl.BlockSpec(memory_space=pl.ANY)
    return pl.pallas_call(
        functools.partial(out_kernel, tile, first),
        in_specs=[vm, vm, hbm, hbm],
        out_specs=[vm, vm],
        out_shape=[
            jax.ShapeDtypeStruct((half, count), f32),
            jax.ShapeDtypeStruct((half, count), bf16),
        ],
        scratch_shapes=[
            VM((a.shape[1], count), bf16),
            VM((b.shape[1], count), bf16),
            pltpu.SemaphoreType.DMA((count // tile,)),
            pltpu.SemaphoreType.DMA((count // tile,)),
        ],
        compiler_params=params(),
        name="project_out",
    )(a, b, w_out_attn, w_out_mlp)


def per_device(
    n_step,
    n_seq,
    trajectory,
    x_start,
    t_idx,
    mod_table,
    step_sizes,
    q_gain,
    k_gain,
    w_qkv,
    w_mlp_in,
    w_out_attn,
    w_out_mlp,
):
    head = q_gain.shape[0]
    rows, width = x_start.shape
    chips = n_seq // 2
    groups = n_step // 2
    chunks = 4
    count = width // chunks
    half = rows // 2
    qg, kg = q_gain[None, :], k_gain[None, :]

    def to_core(x):
        return lax.ppermute(x, "seq", [(i, i ^ 1) for i in range(n_seq)])

    def to_chip(x, offset):
        return lax.ppermute(x, "seq", [(i, (i + 2 * offset) % n_seq) for i in range(n_seq)])

    def to_pair(x):
        return lax.ppermute(x, "step", [(i, i ^ 1) for i in range(n_step)])

    mine, sg = norm_call(t_idx, trajectory, mod_table, step_sizes)
    blocks = [mine] + [to_chip(mine, j) for j in range(1, chips)]
    pairs = [(block, to_core(block)) for block in blocks]
    projected = [project_call(a, b, qg, kg, w_qkv, w_mlp_in) for a, b in pairs]
    ks = [p[1] for p in projected]
    vs = [p[2] for p in projected]

    parity = lax.rem(lax.axis_index("step"), 2)
    order = list(range(1, chips)) + [0]
    attended = {j: attend_call(projected[j][0], ks, vs, head) for j in order}

    results = []
    for c in range(chunks):
        first = c * count
        sums = {}
        for j in order:
            keep, send = out_call(attended[j], projected[j][3], w_out_attn, w_out_mlp, first, count)
            sums[j] = keep + to_core(send).astype(f32)
        branch = sums[0]
        for j in range(1, chips):
            branch = branch + to_chip(sums[j].astype(bf16), chips - j).astype(f32)
        drift = sg[:, first : first + count] * branch
        kept = lax.dynamic_slice_in_dim(drift, parity * half, half, 0)
        other = lax.dynamic_slice_in_dim(drift, (1 - parity) * half, half, 0)
        got = to_pair(other.astype(bf16)).astype(f32)
        total = kept + got
        earlier = jnp.zeros_like(total)
        for g in range(1, groups):
            moves = [(2 * (g - 1) + x, 2 * g + x) for x in range(2)]
            earlier = earlier + lax.ppermute((earlier + total).astype(bf16), "step", moves).astype(f32)
        even = (parity == 0).astype(f32)
        back = to_pair((earlier + even * kept).astype(bf16)).astype(f32)
        own = earlier + kept + (1.0 - even) * got
        rest = back + other
        low = jnp.where(parity == 0, own, rest)
        high = jnp.where(parity == 0, rest, own)
        results.append(x_start[:, first : first + count] + jnp.concatenate([low, high], axis=0))
    return jnp.concatenate(results, axis=1)[None]


def solution(mesh):
    placed = (
        P("step", "seq", None),
        P("seq", None),
        P("step"),
        P(),
        P(),
        P(),
        P(),
        P(None, None, "seq"),
        P(None, "seq"),
        P("seq", None),
        P("seq", None),
    )
    return jax.shard_map(
        functools.partial(per_device, mesh.shape["step"], mesh.shape["seq"]),
        mesh=mesh,
        in_specs=placed,
        out_specs=P("step", "seq", None),
        check_vma=False,
    )
```

time: 264 us -> 140 us (0.53)
  the two profiles are of different devices: /device:TPU:27 before, /device:TPU:0 now
where the time goes in v1:
time: 140 us; the launch traced here: 139 us
  Pallas kernels  57.5 us (41%)
  waiting for transfers between devices  36.6 us (26%)
  starting transfers between devices  32.2 us (23%)
  local copies, waits for them, and re-layouts  6.94 us (5%)
  other arithmetic  4.04 us (3%)
    ppermute x5, waiting for transfers between devices, to_chip(): lax.ppermute(x, 'seq', [(i, (i + 2 * offset) % n_seq) for i in range(n_se...  28.9 us
    pallas_call x2, Pallas kernels, project_call(): pl.pallas_call(functools.partial(project_kernel, tile), in_specs=[vm, vm,...  27.6 us
    pallas_call x8, Pallas kernels, out_call(): pl.pallas_call(functools.partial(out_kernel, tile, first), in_specs=[vm,...  25.2 us
    ppermute x12, starting transfers between devices, per_device(): lax.ppermute((earlier + total).astype(bf16), 'step', moves).astype(f32)  12.7 us
    ppermute x8, starting transfers between devices, to_pair(): return lax.ppermute(x, 'step', [(i, i ^ 1) for i in range(n_step)])  9.95 us
    ppermute x5, starting transfers between devices, to_chip(): lax.ppermute(x, 'seq', [(i, (i + 2 * offset) % n_seq) for i in range(n_se...  7.23 us
    unnamed x48, local copies, waits for them, and re-layouts  6.82 us
    ppermute x8, waiting for transfers between devices, to_pair(): return lax.ppermute(x, 'step', [(i, i ^ 1) for i in range(n_step)])  5 us
  transfers between devices with their start and end apart: 35, of which 13 were waited for; matrix products, arithmetic and copies ran while one was open for 2% of the time, Pallas kernels for 27%

profile of v1, /device:TPU:0, one launch (start us, length us, event | category | flops | bytes accessed | tf_op | source)
XLA Modules:
  0.0 138.7 jit_solution(10474985363253539851)
XLA Ops:
  0.7 1.6 %copy-done.6 = f32[50,9216]{1,0:T(8,128)S(1)} copy-done((f32[50,9216]{1,0:T(8,128)S(1)}, f32[50,9216]{1,0:T(8,128)}, u32[]{:S(2)}) %copy-start.6) | copy-done | bytes 1843224
  2.2 1.4 %copy-done.7 = f32[1,128,3072]{2,1,0:T(8,128)S(1)} copy-done((f32[1,128,3072]{2,1,0:T(8,128)S(1)}, f32[1,128,3072]{2,1,0:T(8,128)}, u32[]{:S(2)}) %copy-start.7) | copy-done | bytes 1572888
  3.6 0.7 copy-done.22
  4.3 1.2 norm.1
  5.5 3.0 %collective-permute-start.1 = (bf16[128,3072]{1,0:T(8,128)(2,1)S(1)}, bf16[128,3072]{1,0:T(8,128)(2,1)S(1)}, u32[]{:S(2)}, u32[]{:S(2)}) collective-permute-start(bf16[128,3072]{1,0:T(8,128)(2,1)S(1)} %get-tuple-element.32.m0), channel_id=1, source_target_pairs={{0,2},{1,3},{2,0},{3,1},{4,6},{5,7},{6,4},{7,5},{8,10},{9,11},{10,... | collective-permute-start | bytes 2359304 | tf_op jit(solution)/shard_map/ppermute | solution.py:253
  8.6 17.5 %collective-permute-done.1.m0 = bf16[128,3072]{1,0:T(8,128)(2,1)S(1)} collective-permute-done((bf16[128,3072]{1,0:T(8,128)(2,1)S(1)}, bf16[128,3072]{1,0:T(8,128)(2,1)S(1)}, u32[]{:S(2)}, u32[]{:S(2)}) %collective-permute-start.1) | collective-permute-done | bytes 786464 | tf_op jit(solution)/shard_map/ppermute | solution.py:253
  26.1 13.5 %project.2 = (bf16[256,512]{1,0:T(8,128)(2,1)S(1)}, bf16[256,512]{1,0:T(8,128)(2,1)S(1)}, bf16[256,512]{1,0:T(8,128)(2,1)S(1)}, bf16[256,1536]{1,0:T(8,128)(2,1)S(1)}) custom-call(bf16[128,3072]{1,0:T(8,128)(2,1)S(1)} %get-tuple-element.32.m0, bf16[128,3072]{1,0:T(8,128)(2,1)S(1)} %collective-permute-done.m1, f32[1,128]{1,0:T(1,128)S(1)} %bitcast.4, ...), custom_call_target="tpu_custom_call" | custom-call | tf_op jit(solution)/shard_map/project/pallas_call | solution.py:119
  39.7 0.9 copy-done.1
  40.6 14.0 %project.3 = (bf16[256,512]{1,0:T(8,128)(2,1)S(1)}, bf16[256,512]{1,0:T(8,128)(2,1)S(1)}, bf16[256,512]{1,0:T(8,128)(2,1)S(1)}, bf16[256,1536]{1,0:T(8,128)(2,1)S(1)}) custom-call(bf16[128,3072]{1,0:T(8,128)(2,1)S(1)} %collective-permute-done.1.m0, bf16[128,3072]{1,0:T(8,128)(2,1)S(1)} %collective-permute-done.2.m1, f32[1,128]{1,0:T(1,128)S(1)} %bitcast.5, ...), custom_call_target="tpu_custom_call" | custom-call | tf_op jit(solution)/shard_map/project/pallas_call | solution.py:119
  54.7 1.7 %attend.3.a = bf16[256,512]{1,0:T(8,128)(2,1)S(1)} custom-call(bf16[256,512]{1,0:T(8,128)(2,1)S(1)} %get-tuple-element.41.refs_0_, bf16[256,512]{1,0:T(8,128)(2,1)S(1)} %get-tuple-element.34.refs_1_, bf16[256,512]{1,0:T(8,128)(2,1)S(1)} %get-tuple-element.35.refs_2_, bf16[256,512]{1,0:T(8,128)(2,1)S(1)} %get-tuple-element.36.refs_3_, ...), custom_call_target="tpu_custom_call" | custom-call | tf_op jit(solution)/shard_map/attend/pallas_call | solution.py:165
  56.5 3.7 %project_out.13 = (f32[128,768]{1,0:T(8,128)S(1)}, bf16[128,768]{1,0:T(8,128)(2,1)}) custom-call(bf16[256,512]{1,0:T(8,128)(2,1)S(1)} %attend.3.a, bf16[256,1536]{1,0:T(8,128)(2,1)S(1)} %get-tuple-element.42.b, bf16[512,3072]{1,0:T(8,128)(2,1)S(1)} %copy-done, bf16[1536,3072]{1,0:T(8,128)(2,1)} %wb_hbm.15), custom_call_target="tpu_custom_call" | custom-call | tf_op jit(solution)/shard_map/project_out/pallas_call | solution.py:206
  60.2 0.7 copy-done.16
  61.0 0.5 collective-permute-start.20
  61.5 1.1 copy-done.4
  62.7 3.1 %project_out.15 = (f32[128,768]{1,0:T(8,128)S(1)}, bf16[128,768]{1,0:T(8,128)(2,1)S(1)}) custom-call(bf16[256,512]{1,0:T(8,128)(2,1)S(1)} %attend.3.a, bf16[256,1536]{1,0:T(8,128)(2,1)S(1)} %copy-done.4, bf16[512,3072]{1,0:T(8,128)(2,1)S(1)} %copy-done, bf16[1536,3072]{1,0:T(8,128)(2,1)} %wb_hbm.15), custom_call_target="tpu_custom_call" | custom-call | tf_op jit(solution)/shard_map/project_out/pallas_call | solution.py:206
  65.9 1.7 %attend.2.a = bf16[256,512]{1,0:T(8,128)(2,1)S(1)} custom-call(bf16[256,512]{1,0:T(8,128)(2,1)S(1)} %copy-done.19, bf16[256,512]{1,0:T(8,128)(2,1)S(1)} %copy-done.9, bf16[256,512]{1,0:T(8,128)(2,1)S(1)} %copy-done.13, bf16[256,512]{1,0:T(8,128)(2,1)S(1)} %copy-done.11, bf16[256,512]{1,0:T(8,128)(2,1)S(1)} %copy-done.15), custom_call_target="tpu_custom_call" | custom-call | tf_op jit(solution)/shard_map/attend/pallas_call | solution.py:165
  67.6 3.0 %project_out.12 = (f32[128,768]{1,0:T(8,128)S(1)}, bf16[128,768]{1,0:T(8,128)(2,1)S(1)}) custom-call(bf16[256,512]{1,0:T(8,128)(2,1)S(1)} %attend.2.a, bf16[256,1536]{1,0:T(8,128)(2,1)S(1)} %copy-done.2, bf16[512,3072]{1,0:T(8,128)(2,1)S(1)} %copy-done, bf16[1536,3072]{1,0:T(8,128)(2,1)} %wb_hbm.15), custom_call_target="tpu_custom_call" | custom-call | tf_op jit(solution)/shard_map/project_out/pallas_call | solution.py:206
  70.7 3.1 %project_out.14 = (f32[128,768]{1,0:T(8,128)S(1)}, bf16[128,768]{1,0:T(8,128)(2,1)S(1)}) custom-call(bf16[256,512]{1,0:T(8,128)(2,1)S(1)} %attend.2.a, bf16[256,1536]{1,0:T(8,128)(2,1)S(1)} %copy-done.2, bf16[512,3072]{1,0:T(8,128)(2,1)S(1)} %copy-done, bf16[1536,3072]{1,0:T(8,128)(2,1)} %wb_hbm.15), custom_call_target="tpu_custom_call" | custom-call | tf_op jit(solution)/shard_map/project_out/pallas_call | solution.py:206
  73.8 3.0 %project_out.11 = (f32[128,768]{1,0:T(8,128)S(1)}, bf16[128,768]{1,0:T(8,128)(2,1)S(1)}) custom-call(bf16[256,512]{1,0:T(8,128)(2,1)S(1)} %attend.3.a, bf16[256,1536]{1,0:T(8,128)(2,1)S(1)} %copy-done.5, bf16[512,3072]{1,0:T(8,128)(2,1)S(1)} %copy-done, bf16[1536,3072]{1,0:T(8,128)(2,1)} %wb_hbm.15), custom_call_target="tpu_custom_call" | custom-call | tf_op jit(solution)/shard_map/project_out/pallas_call | solution.py:206
  76.8 3.0 %project_out.10 = (f32[128,768]{1,0:T(8,128)S(1)}, bf16[128,768]{1,0:T(8,128)(2,1)S(1)}) custom-call(bf16[256,512]{1,0:T(8,128)(2,1)S(1)} %attend.2.a, bf16[256,1536]{1,0:T(8,128)(2,1)S(1)} %copy-done.2, bf16[512,3072]{1,0:T(8,128)(2,1)S(1)} %copy-done, bf16[1536,3072]{1,0:T(8,128)(2,1)} %wb_hbm.15), custom_call_target="tpu_custom_call" | custom-call | tf_op jit(solution)/shard_map/project_out/pallas_call | solution.py:206
  79.9 3.0 %project_out.9 = (f32[128,768]{1,0:T(8,128)S(1)}, bf16[128,768]{1,0:T(8,128)(2,1)S(1)}) custom-call(bf16[256,512]{1,0:T(8,128)(2,1)S(1)} %attend.3.a, bf16[256,1536]{1,0:T(8,128)(2,1)S(1)} %copy-done.5, bf16[512,3072]{1,0:T(8,128)(2,1)S(1)} %copy-done, bf16[1536,3072]{1,0:T(8,128)(2,1)} %wb_hbm.15), custom_call_target="tpu_custom_call" | custom-call | tf_op jit(solution)/shard_map/project_out/pallas_call | solution.py:206
  83.0 3.1 %project_out.8 = (f32[128,768]{1,0:T(8,128)S(1)}, bf16[128,768]{1,0:T(8,128)(2,1)S(1)}) custom-call(bf16[256,512]{1,0:T(8,128)(2,1)S(1)} %attend.2.a, bf16[256,1536]{1,0:T(8,128)(2,1)S(1)} %copy-done.2, bf16[512,3072]{1,0:T(8,128)(2,1)S(1)} %copy-done, bf16[1536,3072]{1,0:T(8,128)(2,1)} %wb_hbm.15), custom_call_target="tpu_custom_call" | custom-call | tf_op jit(solution)/shard_map/project_out/pallas_call | solution.py:206
  86.1 0.5 collective-permute-start.28
  86.7 0.4 collective-permute-start.12
  87.2 1.0 add_convert_fusion.1
  88.2 0.5 collective-permute-start.4
  88.9 0.8 collective-permute-done.4
  89.8 1.8 %collective-permute-start.21 = (bf16[128,768]{1,0:T(8,128)(2,1)S(1)}, bf16[128,768]{1,0:T(8,128)(2,1)S(1)}, u32[]{:S(2)}, u32[]{:S(2)}) collective-permute-start(bf16[128,768]{1,0:T(8,128)(2,1)S(1)} %add_convert_fusion.1), channel_id=1, source_target_pairs={{0,2},{1,3},{2,0},{3,1},{4,6},{5,7},{6,4},{7,5},{8,10},{9,11},{10,... | collective-permute-start | bytes 589832 | tf_op jit(solution)/shard_map/ppermute | solution.py:253
  91.6 0.4 collective-permute-start.29
  91.9 5.6 %collective-permute-done.21 = bf16[128,768]{1,0:T(8,128)(2,1)S(1)} collective-permute-done((bf16[128,768]{1,0:T(8,128)(2,1)S(1)}, bf16[128,768]{1,0:T(8,128)(2,1)S(1)}, u32[]{:S(2)}, u32[]{:S(2)}) %collective-permute-start.21) | collective-permute-done | bytes 196640 | tf_op jit(solution)/shard_map/ppermute | solution.py:253
  97.5 1.7 %collective-permute-start.13 = (bf16[128,768]{1,0:T(8,128)(2,1)S(1)}, bf16[128,768]{1,0:T(8,128)(2,1)S(1)}, u32[]{:S(2)}, u32[]{:S(2)}) collective-permute-start(bf16[128,768]{1,0:T(8,128)(2,1)S(1)} %add_convert_fusion.2), channel_id=1, source_target_pairs={{0,2},{1,3},{2,0},{3,1},{4,6},{5,7},{6,4},{7,5},{8,10},{9,11},{10,... | collective-permute-start | bytes 589832 | tf_op jit(solution)/shard_map/ppermute | solution.py:253
  99.4 0.4 collective-permute-start.5
  99.7 2.0 %collective-permute-done.29 = bf16[128,768]{1,0:T(8,128)(2,1)S(1)} collective-permute-done((bf16[128,768]{1,0:T(8,128)(2,1)S(1)}, bf16[128,768]{1,0:T(8,128)(2,1)S(1)}, u32[]{:S(2)}, u32[]{:S(2)}) %collective-permute-start.29) | collective-permute-done | bytes 196640 | tf_op jit(solution)/shard_map/ppermute | solution.py:253
  101.7 1.7 %collective-permute-start.22 = (bf16[64,768]{1,0:T(8,128)(2,1)S(1)}, bf16[64,768]{1,0:T(8,128)(2,1)S(1)}, u32[]{:S(2)}, u32[]{:S(2)}) collective-permute-start(bf16[64,768]{1,0:T(8,128)(2,1)S(1)} %dynamic-slice_convert_fusion.1), channel_id=1, source_target_pairs={{0,4},{4,0},{8,12},{12,8},{16,20},{20,16},{24,28},{28,24},{1,5},{5... | collective-permute-start | bytes 294920 | tf_op jit(solution)/shard_map/ppermute | solution.py:256
  103.5 0.4 collective-permute-start.30
  103.9 2.0 %collective-permute-done.13 = bf16[128,768]{1,0:T(8,128)(2,1)S(1)} collective-permute-done((bf16[128,768]{1,0:T(8,128)(2,1)S(1)}, bf16[128,768]{1,0:T(8,128)(2,1)S(1)}, u32[]{:S(2)}, u32[]{:S(2)}) %collective-permute-start.13) | collective-permute-done | bytes 196640 | tf_op jit(solution)/shard_map/ppermute | solution.py:253
  106.0 1.8 %collective-permute-start.14 = (bf16[64,768]{1,0:T(8,128)(2,1)S(1)}, bf16[64,768]{1,0:T(8,128)(2,1)S(1)}, u32[]{:S(2)}, u32[]{:S(2)}) collective-permute-start(bf16[64,768]{1,0:T(8,128)(2,1)S(1)} %dynamic-slice_convert_fusion.2), channel_id=1, source_target_pairs={{0,4},{4,0},{8,12},{12,8},{16,20},{20,16},{24,28},{28,24},{1,5},{5... | collective-permute-start | bytes 294920 | tf_op jit(solution)/shard_map/ppermute | solution.py:256
  107.8 1.8 %collective-permute-done.5 = bf16[128,768]{1,0:T(8,128)(2,1)S(1)} collective-permute-done((bf16[128,768]{1,0:T(8,128)(2,1)S(1)}, bf16[128,768]{1,0:T(8,128)(2,1)S(1)}, u32[]{:S(2)}, u32[]{:S(2)}) %collective-permute-start.5) | collective-permute-done | bytes 196640 | tf_op jit(solution)/shard_map/ppermute | solution.py:253
  109.7 1.8 %collective-permute-start.6 = (bf16[64,768]{1,0:T(8,128)(2,1)S(1)}, bf16[64,768]{1,0:T(8,128)(2,1)S(1)}, u32[]{:S(2)}, u32[]{:S(2)}) collective-permute-start(bf16[64,768]{1,0:T(8,128)(2,1)S(1)} %dynamic-slice_convert_fusion.3), channel_id=1, source_target_pairs={{0,4},{4,0},{8,12},{12,8},{16,20},{20,16},{24,28},{28,24},{1,5},{5... | collective-permute-start | bytes 294920 | tf_op jit(solution)/shard_map/ppermute | solution.py:256
  111.5 3.5 %collective-permute-start.23 = (bf16[64,768]{1,0:T(8,128)(2,1)S(1)}, bf16[64,768]{1,0:T(8,128)(2,1)S(1)}, u32[]{:S(2)}, u32[]{:S(2)}) collective-permute-start(bf16[64,768]{1,0:T(8,128)(2,1)S(1)} %fusion.18), channel_id=1, source_target_pairs={{0,8},{4,12},{1,9},{5,13},{2,10},{6,14},{3,11},{7,15}} | collective-permute-start | bytes 294920 | tf_op jit(solution)/shard_map/ppermute | solution.py:287
  115.0 1.3 collective-permute-start.31
  116.4 1.3 collective-permute-start.15
  117.7 1.3 collective-permute-start.7
  119.1 0.7 collective-permute-start.24
  119.8 0.4 collective-permute-done.31
  120.2 0.7 collective-permute-start.32
  120.9 1.1 collective-permute-done.15
  122.1 0.7 collective-permute-start.16
  122.7 0.3 collective-permute-done.7
  123.1 0.7 collective-permute-start.8
  123.9 0.7 collective-permute-start.25
  124.6 0.7 collective-permute-start.33
  125.3 0.7 collective-permute-start.17
  126.1 0.7 collective-permute-start.9
  126.8 0.6 collective-permute-start.26
  127.5 1.6 %collective-permute-start.34 = (bf16[64,768]{1,0:T(8,128)(2,1)S(1)}, bf16[64,768]{1,0:T(8,128)(2,1)S(1)}, u32[]{:S(2)}, u32[]{:S(2)}) collective-permute-start(bf16[64,768]{1,0:T(8,128)(2,1)S(1)} %add_convert_fusion.4), channel_id=1, source_target_pairs={{0,4},{4,0},{8,12},{12,8},{16,20},{20,16},{24,28},{28,24},{1,5},{5... | collective-permute-start | bytes 294920 | tf_op jit(solution)/shard_map/ppermute | solution.py:256
  129.1 0.6 collective-permute-start.18
  129.8 1.6 %collective-permute-start.10 = (bf16[64,768]{1,0:T(8,128)(2,1)S(1)}, bf16[64,768]{1,0:T(8,128)(2,1)S(1)}, u32[]{:S(2)}, u32[]{:S(2)}) collective-permute-start(bf16[64,768]{1,0:T(8,128)(2,1)S(1)} %add_convert_fusion.10), channel_id=1, source_target_pairs={{0,4},{4,0},{8,12},{12,8},{16,20},{20,16},{24,28},{28,24},{1,5},{5... | collective-permute-start | bytes 294920 | tf_op jit(solution)/shard_map/ppermute | solution.py:256
  131.3 1.3 collective-permute-done.26
  132.8 1.8 %collective-permute-done.34 = bf16[64,768]{1,0:T(8,128)(2,1)S(1)} collective-permute-done((bf16[64,768]{1,0:T(8,128)(2,1)S(1)}, bf16[64,768]{1,0:T(8,128)(2,1)S(1)}, u32[]{:S(2)}, u32[]{:S(2)}) %collective-permute-start.34) | collective-permute-done | bytes 98336 | tf_op jit(solution)/shard_map/ppermute | solution.py:256
  134.7 0.9 collective-permute-done.18
  135.8 0.9 collective-permute-done.10
  136.8 0.3 copy-done.23
  137.4 1.3 maximum_bitcast_fusion
  (106 shorter events, 2.4 us)
Async XLA Ops:
  0.7 1.6 %copy-start.6 = (f32[50,9216]{1,0:T(8,128)S(1)}, f32[50,9216]{1,0:T(8,128)}, u32[]{:S(2)}) copy-start(f32[50,9216]{1,0:T(8,128)} %mod_ref.1) | copy-start | bytes 5529604
  2.2 1.4 %copy-start.7 = (f32[1,128,3072]{2,1,0:T(8,128)S(1)}, f32[1,128,3072]{2,1,0:T(8,128)}, u32[]{:S(2)}) copy-start(f32[1,128,3072]{2,1,0:T(8,128)} %x_ref.1) | copy-start | bytes 4718596
  3.6 0.7 copy-start.22
  4.3 21.8 %copy-start.20 = (f32[128]{0:T(128)S(1)}, f32[128]{0:T(128)}, u32[]{:S(2)}) copy-start(f32[128]{0:T(128)} %param.16) | copy-start | bytes 1540
  4.3 21.8 %copy-start.21 = (f32[128]{0:T(128)S(1)}, f32[128]{0:T(128)}, u32[]{:S(2)}) copy-start(f32[128]{0:T(128)} %param.17) | copy-start | bytes 1540
  5.5 20.6 %collective-permute-start.1 = (bf16[128,3072]{1,0:T(8,128)(2,1)S(1)}, bf16[128,3072]{1,0:T(8,128)(2,1)S(1)}, u32[]{:S(2)}, u32[]{:S(2)}) collective-permute-start(bf16[128,3072]{1,0:T(8,128)(2,1)S(1)} %get-tuple-element.32.m0), channel_id=1, source_target_pairs={{0,2},{1,3},{2,0},{3,1},{4,6},{5,7},{6,4},{7,5},{8,10},{9,11},{10,... | collective-permute-start | bytes 2359304 | tf_op jit(solution)/shard_map/ppermute | solution.py:253
  8.6 17.5 %collective-permute-start = (bf16[128,3072]{1,0:T(8,128)(2,1)S(1)}, bf16[128,3072]{1,0:T(8,128)(2,1)S(1)}, u32[]{:S(2)}, u32[]{:S(2)}) collective-permute-start(bf16[128,3072]{1,0:T(8,128)(2,1)S(1)} %get-tuple-element.32.m0), channel_id=1, source_target_pairs={{0,1},{1,0},{2,3},{3,2},{4,5},{5,4},{6,7},{7,6},{8,9},{9,8},{10,11... | collective-permute-start | bytes 2359304 | tf_op jit(solution)/shard_map/ppermute | solution.py:250
  26.1 14.5 %collective-permute-start.2 = (bf16[128,3072]{1,0:T(8,128)(2,1)S(1)}, bf16[128,3072]{1,0:T(8,128)(2,1)S(1)}, u32[]{:S(2)}, u32[]{:S(2)}) collective-permute-start(bf16[128,3072]{1,0:T(8,128)(2,1)S(1)} %collective-permute-done.1.m0), channel_id=1, source_target_pairs={{0,1},{1,0},{2,3},{3,2},{4,5},{5,4},{6,7},{7,6},{8,9},{9,8},{10,11... | collective-permute-start | bytes 2359304 | tf_op jit(solution)/shard_map/ppermute | solution.py:250
  39.7 0.9 copy-start.1
  40.6 14.1 %copy-start.18 = (bf16[256,512]{1,0:T(8,128)(2,1)}, bf16[256,512]{1,0:T(8,128)(2,1)S(1)}, u32[]{:S(2)}) copy-start(bf16[256,512]{1,0:T(8,128)(2,1)S(1)} %get-tuple-element.33.refs_0_) | copy-start | bytes 786436
  40.6 14.1 %copy-start.8 = (bf16[256,512]{1,0:T(8,128)(2,1)}, bf16[256,512]{1,0:T(8,128)(2,1)S(1)}, u32[]{:S(2)}) copy-start(bf16[256,512]{1,0:T(8,128)(2,1)S(1)} %get-tuple-element.34.refs_1_) | copy-start | bytes 786436
  40.6 14.1 %copy-start.10 = (bf16[256,512]{1,0:T(8,128)(2,1)}, bf16[256,512]{1,0:T(8,128)(2,1)S(1)}, u32[]{:S(2)}) copy-start(bf16[256,512]{1,0:T(8,128)(2,1)S(1)} %get-tuple-element.36.refs_3_) | copy-start | bytes 786436
  40.6 15.8 %copy-start = (bf16[512,3072]{1,0:T(8,128)(2,1)S(1)}, bf16[512,3072]{1,0:T(8,128)(2,1)}, u32[]{:S(2)}) copy-start(bf16[512,3072]{1,0:T(8,128)(2,1)} %wa_hbm.15) | copy-start | bytes 9437188
  54.7 5.5 %copy-start.3 = (bf16[256,1536]{1,0:T(8,128)(2,1)}, bf16[256,1536]{1,0:T(8,128)(2,1)S(1)}, u32[]{:S(2)}) copy-start(bf16[256,1536]{1,0:T(8,128)(2,1)S(1)} %get-tuple-element.42.b) | copy-start | bytes 2359300
  54.7 5.5 %copy-start.12 = (bf16[256,512]{1,0:T(8,128)(2,1)}, bf16[256,512]{1,0:T(8,128)(2,1)S(1)}, u32[]{:S(2)}) copy-start(bf16[256,512]{1,0:T(8,128)(2,1)S(1)} %get-tuple-element.35.refs_2_) | copy-start | bytes 786436
  54.7 5.5 %copy-start.14 = (bf16[256,512]{1,0:T(8,128)(2,1)}, bf16[256,512]{1,0:T(8,128)(2,1)S(1)}, u32[]{:S(2)}) copy-start(bf16[256,512]{1,0:T(8,128)(2,1)S(1)} %get-tuple-element.37.refs_4_) | copy-start | bytes 786436
  60.2 0.8 copy-start.16
  61.0 26.2 %collective-permute-start.20 = (bf16[128,768]{1,0:T(8,128)(2,1)}, bf16[128,768]{1,0:T(8,128)(2,1)}, u32[]{:S(2)}, u32[]{:S(2)}) collective-permute-start(bf16[128,768]{1,0:T(8,128)(2,1)} %get-tuple-element.52), channel_id=1, source_target_pairs={{0,1},{1,0},{2,3},{3,2},{4,5},{5,4},{6,7},{7,6},{8,9},{9,8},{10,11... | collective-permute-start | bytes 589832 | tf_op jit(solution)/shard_map/ppermute | solution.py:250
  61.5 1.1 copy-start.4
  62.6 3.2 %copy-start.9 = (bf16[256,512]{1,0:T(8,128)(2,1)S(1)}, bf16[256,512]{1,0:T(8,128)(2,1)}, u32[]{:S(2)}) copy-start(bf16[256,512]{1,0:T(8,128)(2,1)} %copy-done.8) | copy-start | bytes 786436
  62.6 3.2 %copy-start.11 = (bf16[256,512]{1,0:T(8,128)(2,1)S(1)}, bf16[256,512]{1,0:T(8,128)(2,1)}, u32[]{:S(2)}) copy-start(bf16[256,512]{1,0:T(8,128)(2,1)} %copy-done.10) | copy-start | bytes 786436
  62.6 3.2 %copy-start.13 = (bf16[256,512]{1,0:T(8,128)(2,1)S(1)}, bf16[256,512]{1,0:T(8,128)(2,1)}, u32[]{:S(2)}) copy-start(bf16[256,512]{1,0:T(8,128)(2,1)} %copy-done.12) | copy-start | bytes 786436
  62.6 3.2 %copy-start.15 = (bf16[256,512]{1,0:T(8,128)(2,1)S(1)}, bf16[256,512]{1,0:T(8,128)(2,1)}, u32[]{:S(2)}) copy-start(bf16[256,512]{1,0:T(8,128)(2,1)} %copy-done.14) | copy-start | bytes 786436
  62.6 3.2 %copy-start.19 = (bf16[256,512]{1,0:T(8,128)(2,1)S(1)}, bf16[256,512]{1,0:T(8,128)(2,1)}, u32[]{:S(2)}) copy-start(bf16[256,512]{1,0:T(8,128)(2,1)} %copy-done.18) | copy-start | bytes 786436
  65.8 1.8 %copy-start.2 = (bf16[256,1536]{1,0:T(8,128)(2,1)S(1)}, bf16[256,1536]{1,0:T(8,128)(2,1)}, u32[]{:S(2)}) copy-start(bf16[256,1536]{1,0:T(8,128)(2,1)} %copy-done.1) | copy-start | bytes 2359300
  70.6 3.1 %copy-start.5 = (bf16[256,1536]{1,0:T(8,128)(2,1)S(1)}, bf16[256,1536]{1,0:T(8,128)(2,1)}, u32[]{:S(2)}) copy-start(bf16[256,1536]{1,0:T(8,128)(2,1)} %copy-done.3) | copy-start | bytes 2359300
  82.9 4.3 %copy-start.17 = (f32[128,768]{1,0:T(8,128)S(1)}, f32[128,768]{1,0:T(8,128)}, u32[]{:S(2)}) copy-start(f32[128,768]{1,0:T(8,128)} %copy-done.16) | copy-start | bytes 1179652
  86.1 5.5 %collective-permute-start.19 = (bf16[128,768]{1,0:T(8,128)(2,1)S(1)}, bf16[128,768]{1,0:T(8,128)(2,1)S(1)}, u32[]{:S(2)}, u32[]{:S(2)}) collective-permute-start(bf16[128,768]{1,0:T(8,128)(2,1)S(1)} %get-tuple-element.50), channel_id=1, source_target_pairs={{0,1},{1,0},{2,3},{3,2},{4,5},{5,4},{6,7},{7,6},{8,9},{9,8},{10,11... | collective-permute-start | bytes 589832 | tf_op jit(solution)/shard_map/ppermute | solution.py:250
  86.1 2.1 %collective-permute-start.28 = (bf16[128,768]{1,0:T(8,128)(2,1)S(1)}, bf16[128,768]{1,0:T(8,128)(2,1)S(1)}, u32[]{:S(2)}, u32[]{:S(2)}) collective-permute-start(bf16[128,768]{1,0:T(8,128)(2,1)S(1)} %get-tuple-element.56), channel_id=1, source_target_pairs={{0,1},{1,0},{2,3},{3,2},{4,5},{5,4},{6,7},{7,6},{8,9},{9,8},{10,11... | collective-permute-start | bytes 589832 | tf_op jit(solution)/shard_map/ppermute | solution.py:250
  86.6 12.7 %collective-permute-start.27 = (bf16[128,768]{1,0:T(8,128)(2,1)S(1)}, bf16[128,768]{1,0:T(8,128)(2,1)S(1)}, u32[]{:S(2)}, u32[]{:S(2)}) collective-permute-start(bf16[128,768]{1,0:T(8,128)(2,1)S(1)} %get-tuple-element.54), channel_id=1, source_target_pairs={{0,1},{1,0},{2,3},{3,2},{4,5},{5,4},{6,7},{7,6},{8,9},{9,8},{10,11... | collective-permute-start | bytes 589832 | tf_op jit(solution)/shard_map/ppermute | solution.py:250
  86.7 2.0 %collective-permute-start.12 = (bf16[128,768]{1,0:T(8,128)(2,1)S(1)}, bf16[128,768]{1,0:T(8,128)(2,1)S(1)}, u32[]{:S(2)}, u32[]{:S(2)}) collective-permute-start(bf16[128,768]{1,0:T(8,128)(2,1)S(1)} %get-tuple-element.48), channel_id=1, source_target_pairs={{0,1},{1,0},{2,3},{3,2},{4,5},{5,4},{6,7},{7,6},{8,9},{9,8},{10,11... | collective-permute-start | bytes 589832 | tf_op jit(solution)/shard_map/ppermute | solution.py:250
  87.1 16.4 %collective-permute-start.11 = (bf16[128,768]{1,0:T(8,128)(2,1)S(1)}, bf16[128,768]{1,0:T(8,128)(2,1)S(1)}, u32[]{:S(2)}, u32[]{:S(2)}) collective-permute-start(bf16[128,768]{1,0:T(8,128)(2,1)S(1)} %get-tuple-element.46), channel_id=1, source_target_pairs={{0,1},{1,0},{2,3},{3,2},{4,5},{5,4},{6,7},{7,6},{8,9},{9,8},{10,11... | collective-permute-start | bytes 589832 | tf_op jit(solution)/shard_map/ppermute | solution.py:250
  88.2 1.6 %collective-permute-start.4 = (bf16[128,768]{1,0:T(8,128)(2,1)S(1)}, bf16[128,768]{1,0:T(8,128)(2,1)S(1)}, u32[]{:S(2)}, u32[]{:S(2)}) collective-permute-start(bf16[128,768]{1,0:T(8,128)(2,1)S(1)} %get-tuple-element.44), channel_id=1, source_target_pairs={{0,1},{1,0},{2,3},{3,2},{4,5},{5,4},{6,7},{7,6},{8,9},{9,8},{10,11... | collective-permute-start | bytes 589832 | tf_op jit(solution)/shard_map/ppermute | solution.py:250
  88.7 19.1 %collective-permute-start.3 = (bf16[128,768]{1,0:T(8,128)(2,1)S(1)}, bf16[128,768]{1,0:T(8,128)(2,1)S(1)}, u32[]{:S(2)}, u32[]{:S(2)}) collective-permute-start(bf16[128,768]{1,0:T(8,128)(2,1)S(1)} %get-tuple-element.40), channel_id=1, source_target_pairs={{0,1},{1,0},{2,3},{3,2},{4,5},{5,4},{6,7},{7,6},{8,9},{9,8},{10,11... | collective-permute-start | bytes 589832 | tf_op jit(solution)/shard_map/ppermute | solution.py:250
  89.8 7.7 %collective-permute-start.21 = (bf16[128,768]{1,0:T(8,128)(2,1)S(1)}, bf16[128,768]{1,0:T(8,128)(2,1)S(1)}, u32[]{:S(2)}, u32[]{:S(2)}) collective-permute-start(bf16[128,768]{1,0:T(8,128)(2,1)S(1)} %add_convert_fusion.1), channel_id=1, source_target_pairs={{0,2},{1,3},{2,0},{3,1},{4,6},{5,7},{6,4},{7,5},{8,10},{9,11},{10,... | collective-permute-start | bytes 589832 | tf_op jit(solution)/shard_map/ppermute | solution.py:253
  91.6 10.1 %collective-permute-start.29 = (bf16[128,768]{1,0:T(8,128)(2,1)S(1)}, bf16[128,768]{1,0:T(8,128)(2,1)S(1)}, u32[]{:S(2)}, u32[]{:S(2)}) collective-permute-start(bf16[128,768]{1,0:T(8,128)(2,1)S(1)} %add_convert_fusion), channel_id=1, source_target_pairs={{0,2},{1,3},{2,0},{3,1},{4,6},{5,7},{6,4},{7,5},{8,10},{9,11},{10,... | collective-permute-start | bytes 589832 | tf_op jit(solution)/shard_map/ppermute | solution.py:253
  97.5 8.4 %collective-permute-start.13 = (bf16[128,768]{1,0:T(8,128)(2,1)S(1)}, bf16[128,768]{1,0:T(8,128)(2,1)S(1)}, u32[]{:S(2)}, u32[]{:S(2)}) collective-permute-start(bf16[128,768]{1,0:T(8,128)(2,1)S(1)} %add_convert_fusion.2), channel_id=1, source_target_pairs={{0,2},{1,3},{2,0},{3,1},{4,6},{5,7},{6,4},{7,5},{8,10},{9,11},{10,... | collective-permute-start | bytes 589832 | tf_op jit(solution)/shard_map/ppermute | solution.py:253
  99.4 10.2 %collective-permute-start.5 = (bf16[128,768]{1,0:T(8,128)(2,1)S(1)}, bf16[128,768]{1,0:T(8,128)(2,1)S(1)}, u32[]{:S(2)}, u32[]{:S(2)}) collective-permute-start(bf16[128,768]{1,0:T(8,128)(2,1)S(1)} %add_convert_fusion.3), channel_id=1, source_target_pairs={{0,2},{1,3},{2,0},{3,1},{4,6},{5,7},{6,4},{7,5},{8,10},{9,11},{10,... | collective-permute-start | bytes 589832 | tf_op jit(solution)/shard_map/ppermute | solution.py:253
  101.7 9.8 %collective-permute-start.22 = (bf16[64,768]{1,0:T(8,128)(2,1)S(1)}, bf16[64,768]{1,0:T(8,128)(2,1)S(1)}, u32[]{:S(2)}, u32[]{:S(2)}) collective-permute-start(bf16[64,768]{1,0:T(8,128)(2,1)S(1)} %dynamic-slice_convert_fusion.1), channel_id=1, source_target_pairs={{0,4},{4,0},{8,12},{12,8},{16,20},{20,16},{24,28},{28,24},{1,5},{5... | collective-permute-start | bytes 294920 | tf_op jit(solution)/shard_map/ppermute | solution.py:256
  103.5 11.5 %collective-permute-start.30 = (bf16[64,768]{1,0:T(8,128)(2,1)S(1)}, bf16[64,768]{1,0:T(8,128)(2,1)S(1)}, u32[]{:S(2)}, u32[]{:S(2)}) collective-permute-start(bf16[64,768]{1,0:T(8,128)(2,1)S(1)} %dynamic-slice_convert_fusion), channel_id=1, source_target_pairs={{0,4},{4,0},{8,12},{12,8},{16,20},{20,16},{24,28},{28,24},{1,5},{5... | collective-permute-start | bytes 294920 | tf_op jit(solution)/shard_map/ppermute | solution.py:256
  106.0 10.3 %collective-permute-start.14 = (bf16[64,768]{1,0:T(8,128)(2,1)S(1)}, bf16[64,768]{1,0:T(8,128)(2,1)S(1)}, u32[]{:S(2)}, u32[]{:S(2)}) collective-permute-start(bf16[64,768]{1,0:T(8,128)(2,1)S(1)} %dynamic-slice_convert_fusion.2), channel_id=1, source_target_pairs={{0,4},{4,0},{8,12},{12,8},{16,20},{20,16},{24,28},{28,24},{1,5},{5... | collective-permute-start | bytes 294920 | tf_op jit(solution)/shard_map/ppermute | solution.py:256
  109.7 8.0 %collective-permute-start.6 = (bf16[64,768]{1,0:T(8,128)(2,1)S(1)}, bf16[64,768]{1,0:T(8,128)(2,1)S(1)}, u32[]{:S(2)}, u32[]{:S(2)}) collective-permute-start(bf16[64,768]{1,0:T(8,128)(2,1)S(1)} %dynamic-slice_convert_fusion.3), channel_id=1, source_target_pairs={{0,4},{4,0},{8,12},{12,8},{16,20},{20,16},{24,28},{28,24},{1,5},{5... | collective-permute-start | bytes 294920 | tf_op jit(solution)/shard_map/ppermute | solution.py:256
  111.5 7.5 %collective-permute-start.23 = (bf16[64,768]{1,0:T(8,128)(2,1)S(1)}, bf16[64,768]{1,0:T(8,128)(2,1)S(1)}, u32[]{:S(2)}, u32[]{:S(2)}) collective-permute-start(bf16[64,768]{1,0:T(8,128)(2,1)S(1)} %fusion.18), channel_id=1, source_target_pairs={{0,8},{4,12},{1,9},{5,13},{2,10},{6,14},{3,11},{7,15}} | collective-permute-start | bytes 294920 | tf_op jit(solution)/shard_map/ppermute | solution.py:287
  115.0 5.1 %collective-permute-start.31 = (bf16[64,768]{1,0:T(8,128)(2,1)S(1)}, bf16[64,768]{1,0:T(8,128)(2,1)S(1)}, u32[]{:S(2)}, u32[]{:S(2)}) collective-permute-start(bf16[64,768]{1,0:T(8,128)(2,1)S(1)} %fusion.19), channel_id=1, source_target_pairs={{0,8},{4,12},{1,9},{5,13},{2,10},{6,14},{3,11},{7,15}} | collective-permute-start | bytes 294920 | tf_op jit(solution)/shard_map/ppermute | solution.py:287
  116.4 5.6 %collective-permute-start.15 = (bf16[64,768]{1,0:T(8,128)(2,1)S(1)}, bf16[64,768]{1,0:T(8,128)(2,1)S(1)}, u32[]{:S(2)}, u32[]{:S(2)}) collective-permute-start(bf16[64,768]{1,0:T(8,128)(2,1)S(1)} %fusion.17), channel_id=1, source_target_pairs={{0,8},{4,12},{1,9},{5,13},{2,10},{6,14},{3,11},{7,15}} | collective-permute-start | bytes 294920 | tf_op jit(solution)/shard_map/ppermute | solution.py:287
  117.7 5.4 %collective-permute-start.7 = (bf16[64,768]{1,0:T(8,128)(2,1)S(1)}, bf16[64,768]{1,0:T(8,128)(2,1)S(1)}, u32[]{:S(2)}, u32[]{:S(2)}) collective-permute-start(bf16[64,768]{1,0:T(8,128)(2,1)S(1)} %fusion.16), channel_id=1, source_target_pairs={{0,8},{4,12},{1,9},{5,13},{2,10},{6,14},{3,11},{7,15}} | collective-permute-start | bytes 294920 | tf_op jit(solution)/shard_map/ppermute | solution.py:287
  119.1 4.7 %collective-permute-start.24 = (bf16[64,768]{1,0:T(8,128)(2,1)S(1)}, bf16[64,768]{1,0:T(8,128)(2,1)S(1)}, u32[]{:S(2)}, u32[]{:S(2)}) collective-permute-start(bf16[64,768]{1,0:T(8,128)(2,1)S(1)} %fusion.5), channel_id=1, source_target_pairs={{8,16},{12,20},{9,17},{13,21},{10,18},{14,22},{11,19},{15,23}} | collective-permute-start | bytes 294920 | tf_op jit(solution)/shard_map/ppermute | solution.py:287
  120.2 4.3 %collective-permute-start.32 = (bf16[64,768]{1,0:T(8,128)(2,1)S(1)}, bf16[64,768]{1,0:T(8,128)(2,1)S(1)}, u32[]{:S(2)}, u32[]{:S(2)}) collective-permute-start(bf16[64,768]{1,0:T(8,128)(2,1)S(1)} %fusion.7), channel_id=1, source_target_pairs={{8,16},{12,20},{9,17},{13,21},{10,18},{14,22},{11,19},{15,23}} | collective-permute-start | bytes 294920 | tf_op jit(solution)/shard_map/ppermute | solution.py:287
  122.1 3.2 %collective-permute-start.16 = (bf16[64,768]{1,0:T(8,128)(2,1)S(1)}, bf16[64,768]{1,0:T(8,128)(2,1)S(1)}, u32[]{:S(2)}, u32[]{:S(2)}) collective-permute-start(bf16[64,768]{1,0:T(8,128)(2,1)S(1)} %fusion.3), channel_id=1, source_target_pairs={{8,16},{12,20},{9,17},{13,21},{10,18},{14,22},{11,19},{15,23}} | collective-permute-start | bytes 294920 | tf_op jit(solution)/shard_map/ppermute | solution.py:287
  123.1 2.9 %collective-permute-start.8 = (bf16[64,768]{1,0:T(8,128)(2,1)S(1)}, bf16[64,768]{1,0:T(8,128)(2,1)S(1)}, u32[]{:S(2)}, u32[]{:S(2)}) collective-permute-start(bf16[64,768]{1,0:T(8,128)(2,1)S(1)} %fusion.1), channel_id=1, source_target_pairs={{8,16},{12,20},{9,17},{13,21},{10,18},{14,22},{11,19},{15,23}} | collective-permute-start | bytes 294920 | tf_op jit(solution)/shard_map/ppermute | solution.py:287
  123.9 2.9 %collective-permute-start.25 = (bf16[64,768]{1,0:T(8,128)(2,1)S(1)}, bf16[64,768]{1,0:T(8,128)(2,1)S(1)}, u32[]{:S(2)}, u32[]{:S(2)}) collective-permute-start(bf16[64,768]{1,0:T(8,128)(2,1)S(1)} %add_convert_fusion.7), channel_id=1, source_target_pairs={{16,24},{20,28},{17,25},{21,29},{18,26},{22,30},{19,27},{23,31}} | collective-permute-start | bytes 294920 | tf_op jit(solution)/shard_map/ppermute | solution.py:287
  124.6 2.8 %collective-permute-start.33 = (bf16[64,768]{1,0:T(8,128)(2,1)S(1)}, bf16[64,768]{1,0:T(8,128)(2,1)S(1)}, u32[]{:S(2)}, u32[]{:S(2)}) collective-permute-start(bf16[64,768]{1,0:T(8,128)(2,1)S(1)} %add_convert_fusion.5), channel_id=1, source_target_pairs={{16,24},{20,28},{17,25},{21,29},{18,26},{22,30},{19,27},{23,31}} | collective-permute-start | bytes 294920 | tf_op jit(solution)/shard_map/ppermute | solution.py:287
  125.3 3.7 %collective-permute-start.17 = (bf16[64,768]{1,0:T(8,128)(2,1)S(1)}, bf16[64,768]{1,0:T(8,128)(2,1)S(1)}, u32[]{:S(2)}, u32[]{:S(2)}) collective-permute-start(bf16[64,768]{1,0:T(8,128)(2,1)S(1)} %add_convert_fusion.9), channel_id=1, source_target_pairs={{16,24},{20,28},{17,25},{21,29},{18,26},{22,30},{19,27},{23,31}} | collective-permute-start | bytes 294920 | tf_op jit(solution)/shard_map/ppermute | solution.py:287
  126.1 3.6 %collective-permute-start.9 = (bf16[64,768]{1,0:T(8,128)(2,1)S(1)}, bf16[64,768]{1,0:T(8,128)(2,1)S(1)}, u32[]{:S(2)}, u32[]{:S(2)}) collective-permute-start(bf16[64,768]{1,0:T(8,128)(2,1)S(1)} %add_convert_fusion.11), channel_id=1, source_target_pairs={{16,24},{20,28},{17,25},{21,29},{18,26},{22,30},{19,27},{23,31}} | collective-permute-start | bytes 294920 | tf_op jit(solution)/shard_map/ppermute | solution.py:287
  126.8 5.8 %collective-permute-start.26 = (bf16[64,768]{1,0:T(8,128)(2,1)S(1)}, bf16[64,768]{1,0:T(8,128)(2,1)S(1)}, u32[]{:S(2)}, u32[]{:S(2)}) collective-permute-start(bf16[64,768]{1,0:T(8,128)(2,1)S(1)} %add_convert_fusion.6), channel_id=1, source_target_pairs={{0,4},{4,0},{8,12},{12,8},{16,20},{20,16},{24,28},{28,24},{1,5},{5... | collective-permute-start | bytes 294920 | tf_op jit(solution)/shard_map/ppermute | solution.py:256
  127.5 7.1 %collective-permute-start.34 = (bf16[64,768]{1,0:T(8,128)(2,1)S(1)}, bf16[64,768]{1,0:T(8,128)(2,1)S(1)}, u32[]{:S(2)}, u32[]{:S(2)}) collective-permute-start(bf16[64,768]{1,0:T(8,128)(2,1)S(1)} %add_convert_fusion.4), channel_id=1, source_target_pairs={{0,4},{4,0},{8,12},{12,8},{16,20},{20,16},{24,28},{28,24},{1,5},{5... | collective-permute-start | bytes 294920 | tf_op jit(solution)/shard_map/ppermute | solution.py:256
  129.1 6.6 %collective-permute-start.18 = (bf16[64,768]{1,0:T(8,128)(2,1)S(1)}, bf16[64,768]{1,0:T(8,128)(2,1)S(1)}, u32[]{:S(2)}, u32[]{:S(2)}) collective-permute-start(bf16[64,768]{1,0:T(8,128)(2,1)S(1)} %add_convert_fusion.8), channel_id=1, source_target_pairs={{0,4},{4,0},{8,12},{12,8},{16,20},{20,16},{24,28},{28,24},{1,5},{5... | collective-permute-start | bytes 294920 | tf_op jit(solution)/shard_map/ppermute | solution.py:256
  129.8 7.0 %collective-permute-start.10 = (bf16[64,768]{1,0:T(8,128)(2,1)S(1)}, bf16[64,768]{1,0:T(8,128)(2,1)S(1)}, u32[]{:S(2)}, u32[]{:S(2)}) collective-permute-start(bf16[64,768]{1,0:T(8,128)(2,1)S(1)} %add_convert_fusion.10), channel_id=1, source_target_pairs={{0,4},{4,0},{8,12},{12,8},{16,20},{20,16},{24,28},{28,24},{1,5},{5... | collective-permute-start | bytes 294920 | tf_op jit(solution)/shard_map/ppermute | solution.py:256
  135.8 1.4 %copy-start.23 = (f32[128,3072]{1,0:T(8,128)S(1)}, f32[128,3072]{1,0:T(8,128)}, u32[]{:S(2)}) copy-start(f32[128,3072]{1,0:T(8,128)} %param.12) | copy-start | bytes 4718596

commit v2 on v1

v2 whole, which is shorter than its diff:
```python
import functools
import math

import jax
import jax.numpy as jnp
from jax import lax
from jax.experimental import pallas as pl
from jax.experimental.pallas import tpu as pltpu
from jax.sharding import PartitionSpec as P

eps = 1e-06
f32 = jnp.float32
bf16 = jnp.bfloat16
VM = pltpu.VMEM
MIB = 1024 * 1024


def params(mib):
    return pltpu.CompilerParams(vmem_limit_bytes=mib * MIB)


def cost(flops, moved):
    return pl.CostEstimate(flops=flops, transcendentals=0, bytes_accessed=moved)


def norm_kernel(t_ref, x_hbm, mod_ref, size_ref, m_ref, sg_ref, x_ref, sem):
    width = x_hbm.shape[-1]
    pieces = sem.shape[0]
    block = x_hbm.shape[1] // pieces
    copies = []
    for i in range(pieces):
        here = pl.ds(i * block, block)
        copies.append(pltpu.make_async_copy(x_hbm.at[0, here, :], x_ref.at[here, :], sem.at[i]))
        copies[i].start()
    row = lax.rem(t_ref[0], 8)
    shift = mod_ref[pl.ds(row, 1), :width]
    scale = 1.0 + mod_ref[pl.ds(row, 1), width : 2 * width]
    gate = mod_ref[pl.ds(row, 1), 2 * width :]
    sg_ref[...] = size_ref[t_ref[0]] * gate
    for i in range(pieces):
        copies[i].wait()
        here = slice(i * block, (i + 1) * block)
        x = x_ref[here, :]
        center = x - jnp.mean(x, axis=-1, keepdims=True)
        spread = jnp.mean(center * center, axis=-1, keepdims=True)
        m_ref[here, :] = (center * lax.rsqrt(spread + eps) * scale + shift).astype(bf16)


def norm_call(t_idx, trajectory, mod_table, step_sizes):
    _, rows, width = trajectory.shape
    return pl.pallas_call(
        norm_kernel,
        grid_spec=pltpu.PrefetchScalarGridSpec(
            num_scalar_prefetch=1,
            grid=(1,),
            in_specs=[
                pl.BlockSpec(memory_space=pltpu.HBM),
                pl.BlockSpec((8, 3 * width), lambda i, t: (t[0] // 8, 0)),
                pl.BlockSpec(memory_space=pltpu.SMEM),
            ],
            out_specs=[
                pl.BlockSpec((rows, width), lambda i, t: (0, 0)),
                pl.BlockSpec((1, width), lambda i, t: (0, 0)),
            ],
            scratch_shapes=[VM((rows, width), f32), pltpu.SemaphoreType.DMA((4,))],
        ),
        out_shape=[
            jax.ShapeDtypeStruct((rows, width), bf16),
            jax.ShapeDtypeStruct((1, width), f32),
        ],
        compiler_params=params(60),
        cost_estimate=cost(10 * rows * width, 0),
        name="norm",
    )(t_idx, trajectory, mod_table, step_sizes)


def project_kernel(tile, m0, m1, qg, kg, wq_hbm, wm_hbm, q, k, v, act, rows, wq, wm, sem_q, sem_m):
    half = m0.shape[0]
    head = qg.shape[1]
    n_q = wq.shape[2] // tile
    n_m = wm.shape[1] // tile
    copies = []
    for which in range(3):
        for i in range(n_q):
            cols = pl.ds(i * tile, tile)
            copies.append(
                pltpu.make_async_copy(
                    wq_hbm.at[which, :, cols], wq.at[which, :, cols], sem_q.at[which * n_q + i]
                )
            )
    for i in range(n_m):
        cols = pl.ds(i * tile, tile)
        copies.append(pltpu.make_async_copy(wm_hbm.at[:, cols], wm.at[:, cols], sem_m.at[i]))
    for copy in copies:
        copy.start()
    rows[:half] = m0[...]
    rows[half:] = m1[...]

    def normed(y, gain):
        parts = []
        for h in range(tile // head):
            one = y[:, h * head : (h + 1) * head]
            square = jnp.mean(one * one, axis=-1, keepdims=True)
            parts.append((one * lax.rsqrt(square + eps) * gain).astype(bf16))
        return jnp.concatenate(parts, axis=1)

    for which in range(3):
        for i in range(n_q):
            copies[which * n_q + i].wait()
            cols = slice(i * tile, (i + 1) * tile)
            y = jnp.dot(rows[...], wq[which, :, cols], preferred_element_type=f32)
            if which == 0:
                q[:, cols] = normed(y, qg[...])
            elif which == 1:
                k[:, cols] = normed(y, kg[...])
            else:
                v[:, cols] = y.astype(bf16)
    for i in range(n_m):
        copies[3 * n_q + i].wait()
        cols = slice(i * tile, (i + 1) * tile)
        y = jnp.dot(rows[...], wm[:, cols], preferred_element_type=f32)
        act[:, cols] = jax.nn.gelu(y, approximate=True).astype(bf16)


def project_call(m0, m1, q_gain, k_gain, w_qkv, w_mlp_in):
    half, width = m0.shape
    heads = w_qkv.shape[2]
    hidden = w_mlp_in.shape[1]
    tile = min(512, heads)
    rows = 2 * half
    vm = pl.BlockSpec(memory_space=VM)
    hbm = pl.BlockSpec(memory_space=pltpu.HBM)
    return pl.pallas_call(
        functools.partial(project_kernel, tile),
        in_specs=[vm, vm, vm, vm, hbm, hbm],
        out_specs=[vm] * 4,
        out_shape=[jax.ShapeDtypeStruct((rows, heads), bf16)] * 3
        + [jax.ShapeDtypeStruct((rows, hidden), bf16)],
        scratch_shapes=[
            VM((rows, width), bf16),
            VM((3, width, heads), bf16),
            VM((width, hidden), bf16),
            pltpu.SemaphoreType.DMA((3 * heads // tile,)),
            pltpu.SemaphoreType.DMA((hidden // tile,)),
        ],
        compiler_params=params(46),
        cost_estimate=cost(2 * rows * width * (3 * heads + hidden), 0),
        name="project",
    )(m0, m1, q_gain, k_gain, w_qkv, w_mlp_in)


def attend_kernel(pairs, head, *refs):
    q_ref = refs[0]
    k_refs = refs[1 : 1 + pairs]
    v_refs = refs[1 + pairs : 1 + 2 * pairs]
    out = refs[1 + 2 * pairs]
    scale = math.log2(math.e) / math.sqrt(head)
    for h in range(q_ref.shape[1] // head):
        cols = slice(h * head, (h + 1) * head)
        q = q_ref[:, cols]
        scores = [
            lax.dot_general(q, k[:, cols], (((1,), (1,)), ((), ())), preferred_element_type=f32)
            for k in k_refs
        ]
        top = functools.reduce(
            jnp.maximum, [jnp.max(s, axis=-1, keepdims=True) for s in scores]
        )
        weights = [jnp.exp2((s - top) * scale) for s in scores]
        total = sum(jnp.sum(w, axis=-1, keepdims=True) for w in weights)
        inverse = 1.0 / total
        mixed = sum(
            jnp.dot((w * inverse).astype(bf16), v[:, cols], preferred_element_type=f32)
            for w, v in zip(weights, v_refs)
        )
        out[:, cols] = mixed.astype(bf16)


def attend_call(q, ks, vs, head):
    vm = pl.BlockSpec(memory_space=VM)
    return pl.pallas_call(
        functools.partial(attend_kernel, len(ks), head),
        in_specs=[vm] * (1 + 2 * len(ks)),
        out_specs=vm,
        out_shape=jax.ShapeDtypeStruct(q.shape, bf16),
        compiler_params=params(46),
        cost_estimate=cost(4 * len(ks) * q.shape[0] ** 2 * q.shape[1] * 3, 0),
        name="attend",
    )(q, *ks, *vs)


def out_kernel(first, parts, *refs):
    xs, ws, extra = refs[:parts], refs[parts : 2 * parts], refs[2 * parts : -3 - parts]
    keep, send = refs[-3 - parts], refs[-2 - parts]
    held, sem = refs[-1 - parts : -1], refs[-1]
    half, count = keep.shape
    piece = 512
    there = pl.ds(first, count)
    copies = []
    for w, to in zip(ws, held):
        for at in range(0, w.shape[0], piece):
            here = pl.ds(at, min(piece, w.shape[0] - at))
            copies.append(
                pltpu.make_async_copy(w.at[here, there], to.at[here, :], sem.at[len(copies)])
            )
            copies[-1].start()
    turn = 0
    y = None
    for x, to in zip(xs, held):
        for at in range(0, to.shape[0], piece):
            here = slice(at, min(at + piece, to.shape[0]))
            copies[turn].wait()
            turn += 1
            term = jnp.dot(x[:, here], to[here, :], preferred_element_type=f32)
            y = term if y is None else y + term
    low, high = y[:half], y[half:]
    if extra:
        low = low + extra[0][:, first : first + count]
        high = high + extra[1][:, first : first + count]
    keep[...] = low
    send[...] = high.astype(send.dtype)


def out_call(xs, ws, extra, first, count, kind):
    half = xs[0].shape[0] // 2
    depth = sum(x.shape[1] for x in xs)
    vm = pl.BlockSpec(memory_space=VM)
    hbm = pl.BlockSpec(memory_space=pltpu.HBM)
    return pl.pallas_call(
        functools.partial(out_kernel, first, len(xs)),
        in_specs=[vm] * len(xs) + [hbm] * len(ws) + [vm] * len(extra),
        out_specs=[vm, vm],
        out_shape=[
            jax.ShapeDtypeStruct((half, count), f32),
            jax.ShapeDtypeStruct((half, count), kind),
        ],
        scratch_shapes=[VM((x.shape[1], count), bf16) for x in xs]
        + [pltpu.SemaphoreType.DMA((sum(-(-x.shape[1] // 512) for x in xs),))],
        compiler_params=params(46),
        cost_estimate=cost(4 * half * count * depth, 0),
        name="project_out",
    )(*xs, *ws, *extra)


def per_device(
    n_step,
    n_seq,
    trajectory,
    x_start,
    t_idx,
    mod_table,
    step_sizes,
    q_gain,
    k_gain,
    w_qkv,
    w_mlp_in,
    w_out_attn,
    w_out_mlp,
):
    head = q_gain.shape[0]
    rows, width = x_start.shape
    chips = n_seq // 2
    groups = n_step // 2
    chunks = 4
    count = width // chunks
    half = rows // 2
    qg, kg = q_gain[None, :], k_gain[None, :]

    def to_core(x):
        return lax.ppermute(x, "seq", [(i, i ^ 1) for i in range(n_seq)])

    def to_chip(x, offset):
        return lax.ppermute(x, "seq", [(i, (i + 2 * offset) % n_seq) for i in range(n_seq)])

    def to_pair(x):
        return lax.ppermute(x, "step", [(i, i ^ 1) for i in range(n_step)])

    def tied(*values):
        return lax.optimization_barrier(values)

    parity = lax.rem(lax.axis_index("step"), 2)
    even = (parity == 0).astype(f32)
    offsets = range(1, chips)

    mine, sg = norm_call(t_idx, trajectory, mod_table, step_sizes)
    far = [to_chip(mine, j) for j in offsets]
    q0, k0, v0, act0 = project_call(mine, to_core(mine), qg, kg, w_qkv, w_mlp_in)
    low0, high0 = out_call([act0], [w_out_mlp], [], 0, width, f32)
    far, low0, high0 = tied(far, low0, high0)
    qs, ks, vs, acts = [], [k0], [v0], []
    for block in far:
        q, k, v, act = project_call(block, to_core(block), qg, kg, w_qkv, w_mlp_in)
        qs.append(q)
        ks.append(k)
        vs.append(v)
        acts.append(act)
    mixed = [attend_call(q, ks, vs, head) for q in qs]

    firsts = [c * count for c in range(chunks)]
    weights = [w_out_attn, w_out_mlp]
    sums = [[] for _ in offsets]
    ready = [[] for _ in offsets]
    gate = (mixed, acts)
    for c, first in enumerate(firsts):
        for j in range(chips - 1):
            keep, send = out_call([gate[0][j], gate[1][j]], weights, [], first, count, bf16)
            sums[j].append((keep, to_core(send)))
        if c >= 1:
            for j in range(chips - 1):
                keep, send = sums[j][c - 1]
                ready[j].append((keep + send.astype(f32)).astype(bf16))
            recent = [r[-1] for r in ready]
            now = [x[-1][0] for x in sums]
            gate, recent, now = tied(gate, recent, now)
            for j in range(chips - 1):
                ready[j][-1] = recent[j]
                sums[j][-1] = (now[j], sums[j][-1][1])
    for j in range(chips - 1):
        keep, send = sums[j][-1]
        ready[j].append((keep + send.astype(f32)).astype(bf16))
    q0, ready = tied(q0, ready)
    got = [[to_chip(r, chips - 1 - j) for r in ready[j]] for j in range(chips - 1)]
    mixed0 = attend_call(q0, ks, vs, head)
    early = [row[:2] for row in got]
    mixed0, early = tied(mixed0, early)
    got = [e + row[2:] for e, row in zip(early, got)]
    keep0, send0 = out_call([mixed0], [w_out_attn], [low0, high0], 0, width, bf16)
    own = keep0 + to_core(send0).astype(f32)

    def prefix_stages(c):
        first = firsts[c]
        held = {}

        def drift_of(fetched):
            branch = own[:, first : first + count]
            for one in fetched:
                branch = branch + one.astype(f32)
            drift = sg[:, first : first + count] * branch
            held["kept"] = lax.dynamic_slice_in_dim(drift, parity * half, half, 0)
            held["other"] = lax.dynamic_slice_in_dim(drift, (1 - parity) * half, half, 0)
            return held["other"].astype(bf16)

        def pair_sum(fetched):
            held["fetched"] = fetched.astype(f32)
            held["total"] = held["kept"] + held["fetched"]
            held["earlier"] = jnp.zeros_like(held["total"])
            if groups > 1:
                return held["total"].astype(bf16)
            return (even * held["kept"]).astype(bf16)

        def hop(g, fetched):
            held["earlier"] = held["earlier"] + fetched.astype(f32)
            if g < groups - 1:
                return (held["earlier"] + held["total"]).astype(bf16)
            return (held["earlier"] + even * held["kept"]).astype(bf16)

        def finish(fetched):
            mine_half = held["earlier"] + held["kept"] + (1.0 - even) * held["fetched"]
            rest = fetched.astype(f32) + held["other"]
            low = jnp.where(parity == 0, mine_half, rest)
            high = jnp.where(parity == 0, rest, mine_half)
            return x_start[:, first : first + count] + jnp.concatenate([low, high], axis=0)

        def along(g):
            moves = [(2 * (g - 1) + x, 2 * g + x) for x in range(2)]
            return lambda x: lax.ppermute(x, "step", moves)

        stages = [(drift_of, to_pair)]
        stages.append((pair_sum, along(1) if groups > 1 else to_pair))
        for g in range(1, groups):
            stages.append((functools.partial(hop, g), along(g + 1) if g < groups - 1 else to_pair))
        stages.append((finish, None))
        return stages

    plan = [prefix_stages(c) for c in range(chunks)]
    inbox = [[got[j][c] for j in range(chips - 1)] for c in range(chunks)]
    turns = sorted(
        (4 * c + 3 * i, i, c) for c in range(chunks) for i in range(len(plan[c]))
    )
    results = [None] * chunks
    last = None
    for _, i, c in turns:
        compute, move = plan[c][i]
        fetched = inbox[c]
        if last is not None:
            fetched, last = tied(fetched, last)
        out = compute(fetched)
        if move is None:
            results[c] = out
        else:
            inbox[c] = move(out)
            last = out
    return jnp.concatenate(results, axis=1)[None]


def solution(mesh):
    placed = (
        P("step", "seq", None),
        P("seq", None),
        P("step"),
        P(),
        P(),
        P(),
        P(),
        P(None, None, "seq"),
        P(None, "seq"),
        P("seq", None),
        P("seq", None),
    )
    return jax.shard_map(
        functools.partial(per_device, mesh.shape["step"], mesh.shape["seq"]),
        mesh=mesh,
        in_specs=placed,
        out_specs=P("step", "seq", None),
        check_vma=False,
    )
```

time: 140 us -> 121 us (0.86)
  the two profiles are of different devices: /device:TPU:0 before, /device:TPU:24 now
where the time goes in v2:
time: 121 us; the launch traced here: 120 us
  Pallas kernels  45.1 us (37%)
  waiting for transfers between devices  39.1 us (32%)
  starting transfers between devices  29.3 us (24%)
  other arithmetic  4.33 us (4%)
  local copies, waits for them, and re-layouts  1.29 us (1%)
    pallas_call x6, Pallas kernels, out_call(): pl.pallas_call(functools.partial(out_kernel, first, len(xs)), in_specs=[v...  19 us
    pallas_call x2, Pallas kernels, project_call(): pl.pallas_call(functools.partial(project_kernel, tile), in_specs=[vm, vm,...  18.5 us
    ppermute x12, waiting for transfers between devices, along(): return lambda x: lax.ppermute(x, 'step', moves)  13.5 us
    ppermute x8, starting transfers between devices, to_pair(): return lax.ppermute(x, 'step', [(i, i ^ 1) for i in range(n_step)])  11.7 us
    ppermute x12, starting transfers between devices, along(): return lambda x: lax.ppermute(x, 'step', moves)  10.5 us
    ppermute x8, waiting for transfers between devices, to_pair(): return lax.ppermute(x, 'step', [(i, i ^ 1) for i in range(n_step)])  9.63 us
    ppermute x5, waiting for transfers between devices, to_chip(): lax.ppermute(x, 'seq', [(i, (i + 2 * offset) % n_seq) for i in range(n_se...  9.34 us
    ppermute x7, waiting for transfers between devices, to_core(): return lax.ppermute(x, 'seq', [(i, i ^ 1) for i in range(n_seq)])  6.55 us
  transfers between devices with their start and end apart: 32, of which 17 were waited for; matrix products, arithmetic and copies ran while one was open for 1% of the time, Pallas kernels for 20%

profile of v2, /device:TPU:24, one launch (start us, length us, event | category | flops | bytes accessed | tf_op | source)
XLA Modules:
  0.0 120.3 jit_solution(14710964487918744234)
XLA Ops:
  0.7 4.0 %norm.1 = (bf16[128,3072]{1,0:T(8,128)(2,1)}, f32[1,3072]{1,0:T(1,128)}) custom-call(s32[1]{0:T(128)S(6)} %copy.12.t_ref, f32[1,128,3072]{2,1,0:T(8,128)} %x_hbm.1, f32[50,9216]{1,0:T(8,128)} %mod_ref.1, f32[50]{0:T(128)} %size_ref.1), custom_call_target="tpu_custom_call" | custom-call | flops 3932160 | tf_op jit(solution)/shard_map/norm/pallas_call | solution.py:51
  4.8 1.6 %collective-permute-start.1 = (bf16[128,3072]{1,0:T(8,128)(2,1)}, bf16[128,3072]{1,0:T(8,128)(2,1)S(1)}, u32[]{:S(2)}, u32[]{:S(2)}) collective-permute-start(bf16[128,3072]{1,0:T(8,128)(2,1)} %get-tuple-element.69.m0), channel_id=1, source_target_pairs={{0,2},{1,3},{2,0},{3,1},{4,6},{5,7},{6,4},{7,5},{8,10},{9,11},{10,... | collective-permute-start | bytes 2359304 | tf_op jit(solution)/shard_map/ppermute | solution.py:272
  6.3 0.9 collective-permute-done.m1
  7.2 1.1 copy-done.1
  8.4 9.2 %project.2 = (bf16[256,512]{1,0:T(8,128)(2,1)S(1)}, bf16[256,512]{1,0:T(8,128)(2,1)S(1)}, bf16[256,512]{1,0:T(8,128)(2,1)S(1)}, bf16[256,1536]{1,0:T(8,128)(2,1)S(1)}) custom-call(bf16[128,3072]{1,0:T(8,128)(2,1)S(1)} %copy-done.1, bf16[128,3072]{1,0:T(8,128)(2,1)S(1)} %collective-permute-done.m1, f32[1,128]{1,0:T(1,128)S(1)} %bitcast.4, ...), custom_call_target="tpu_custom_call" | custom-call | flops 4831838208 | tf_op jit(solution)/shard_map/project/pallas_call | solution.py:133
  17.6 5.7 %project_out.6 = (f32[128,3072]{1,0:T(8,128)S(1)}, f32[128,3072]{1,0:T(8,128)S(1)}) custom-call(bf16[256,1536]{1,0:T(8,128)(2,1)S(1)} %get-tuple-element.71.refs_0_, bf16[1536,3072]{1,0:T(8,128)(2,1)} %refs_3_.7), custom_call_target="tpu_custom_call" | custom-call | flops 2415919104 | tf_op jit(solution)/shard_map/project_out/pallas_call | solution.py:228
  23.2 1.7 %collective-permute-done.1.m0 = bf16[128,3072]{1,0:T(8,128)(2,1)S(1)} collective-permute-done((bf16[128,3072]{1,0:T(8,128)(2,1)}, bf16[128,3072]{1,0:T(8,128)(2,1)S(1)}, u32[]{:S(2)}, u32[]{:S(2)}) %collective-permute-start.1) | collective-permute-done | bytes 786464 | tf_op jit(solution)/shard_map/ppermute | solution.py:272
  24.9 2.3 %collective-permute-done.2.m1 = bf16[128,3072]{1,0:T(8,128)(2,1)S(1)} collective-permute-done((bf16[128,3072]{1,0:T(8,128)(2,1)S(1)}, bf16[128,3072]{1,0:T(8,128)(2,1)S(1)}, u32[]{:S(2)}, u32[]{:S(2)}) %collective-permute-start.2) | collective-permute-done | bytes 786464 | tf_op jit(solution)/shard_map/ppermute | solution.py:269
  27.2 9.3 %project.3 = (bf16[256,512]{1,0:T(8,128)(2,1)S(1)}, bf16[256,512]{1,0:T(8,128)(2,1)S(1)}, bf16[256,512]{1,0:T(8,128)(2,1)S(1)}, bf16[256,1536]{1,0:T(8,128)(2,1)S(1)}) custom-call(bf16[128,3072]{1,0:T(8,128)(2,1)S(1)} %collective-permute-done.1.m0, bf16[128,3072]{1,0:T(8,128)(2,1)S(1)} %collective-permute-done.2.m1, f32[1,128]{1,0:T(1,128)S(1)} %bitcast.5, ...), custom_call_target="tpu_custom_call" | custom-call | flops 4831838208 | tf_op jit(solution)/shard_map/project/pallas_call | solution.py:133
  36.5 1.9 %attend.2.refs_0_ = bf16[256,512]{1,0:T(8,128)(2,1)S(1)} custom-call(bf16[256,512]{1,0:T(8,128)(2,1)S(1)} %get-tuple-element.75.refs_0_, bf16[256,512]{1,0:T(8,128)(2,1)S(1)} %get-tuple-element.76.refs_1_, bf16[256,512]{1,0:T(8,128)(2,1)S(1)} %get-tuple-element.77.refs_2_, bf16[256,512]{1,0:T(8,128)(2,1)S(1)} %get-tuple-element.78.refs_3_, ...), custom_call_target="tpu_custom_call" | custom-call | flops 805306368 | tf_op jit(solution)/shard_map/attend/pallas_call | solution.py:180
  38.4 2.6 %project_out.7 = (f32[128,768]{1,0:T(8,128)S(1)}, bf16[128,768]{1,0:T(8,128)(2,1)S(1)}) custom-call(bf16[256,512]{1,0:T(8,128)(2,1)S(1)} %attend.2.refs_0_, bf16[256,1536]{1,0:T(8,128)(2,1)S(1)} %get-tuple-element.92.refs_1_, bf16[512,3072]{1,0:T(8,128)(2,1)S(1)} %copy-done, bf16[1536,3072]{1,0:T(8,128)(2,1)} %refs_3_.7), custom_call_target="tpu_custom_call" | custom-call | flops 805306368 | tf_op jit(solution)/shard_map/project_out/pallas_call | solution.py:228
  41.0 0.2 collective-permute-start.3
  41.2 2.6 %project_out.8 = (f32[128,768]{1,0:T(8,128)S(1)}, bf16[128,768]{1,0:T(8,128)(2,1)S(1)}) custom-call(bf16[256,512]{1,0:T(8,128)(2,1)S(1)} %attend.2.refs_0_, bf16[256,1536]{1,0:T(8,128)(2,1)S(1)} %get-tuple-element.92.refs_1_, bf16[512,3072]{1,0:T(8,128)(2,1)S(1)} %copy-done, bf16[1536,3072]{1,0:T(8,128)(2,1)} %refs_3_.7), custom_call_target="tpu_custom_call" | custom-call | flops 805306368 | tf_op jit(solution)/shard_map/project_out/pallas_call | solution.py:228
  43.8 0.5 collective-permute-start.4
  44.3 2.6 %project_out.9 = (f32[128,768]{1,0:T(8,128)S(1)}, bf16[128,768]{1,0:T(8,128)(2,1)S(1)}) custom-call(bf16[256,512]{1,0:T(8,128)(2,1)S(1)} %attend.2.refs_0_, bf16[256,1536]{1,0:T(8,128)(2,1)S(1)} %get-tuple-element.92.refs_1_, bf16[512,3072]{1,0:T(8,128)(2,1)S(1)} %copy-done, bf16[1536,3072]{1,0:T(8,128)(2,1)} %refs_3_.7), custom_call_target="tpu_custom_call" | custom-call | flops 805306368 | tf_op jit(solution)/shard_map/project_out/pallas_call | solution.py:228
  46.9 0.2 collective-permute-start.5
  47.2 2.6 %project_out.10 = (f32[128,768]{1,0:T(8,128)S(1)}, bf16[128,768]{1,0:T(8,128)(2,1)S(1)}) custom-call(bf16[256,512]{1,0:T(8,128)(2,1)S(1)} %attend.2.refs_0_, bf16[256,1536]{1,0:T(8,128)(2,1)S(1)} %get-tuple-element.92.refs_1_, bf16[512,3072]{1,0:T(8,128)(2,1)S(1)} %copy-done, bf16[1536,3072]{1,0:T(8,128)(2,1)} %refs_3_.7), custom_call_target="tpu_custom_call" | custom-call | flops 805306368 | tf_op jit(solution)/shard_map/project_out/pallas_call | solution.py:228
  49.8 0.5 collective-permute-start.6
  50.3 1.0 collective-permute-done.6
  51.4 1.6 %collective-permute-start.7 = (bf16[128,768]{1,0:T(8,128)(2,1)S(1)}, bf16[128,768]{1,0:T(8,128)(2,1)S(1)}, u32[]{:S(2)}, u32[]{:S(2)}) collective-permute-start(bf16[128,768]{1,0:T(8,128)(2,1)S(1)} %add_convert_fusion.3), channel_id=1, source_target_pairs={{0,2},{1,3},{2,0},{3,1},{4,6},{5,7},{6,4},{7,5},{8,10},{9,11},{10,... | collective-permute-start | bytes 589832 | tf_op jit(solution)/shard_map/ppermute | solution.py:272
  53.0 0.5 collective-permute-start.8
  53.5 1.7 %attend.3.refs_0_ = bf16[256,512]{1,0:T(8,128)(2,1)S(1)} custom-call(bf16[256,512]{1,0:T(8,128)(2,1)S(1)} %get-tuple-element.99.refs_0_, bf16[256,512]{1,0:T(8,128)(2,1)S(1)} %get-tuple-element.76.refs_1_, bf16[256,512]{1,0:T(8,128)(2,1)S(1)} %get-tuple-element.77.refs_2_, bf16[256,512]{1,0:T(8,128)(2,1)S(1)} %get-tuple-element.78.refs_3_, ...), custom_call_target="tpu_custom_call" | custom-call | flops 805306368 | tf_op jit(solution)/shard_map/attend/pallas_call | solution.py:180
  55.2 4.0 %collective-permute-done.7 = bf16[128,768]{1,0:T(8,128)(2,1)S(1)} collective-permute-done((bf16[128,768]{1,0:T(8,128)(2,1)S(1)}, bf16[128,768]{1,0:T(8,128)(2,1)S(1)}, u32[]{:S(2)}, u32[]{:S(2)}) %collective-permute-start.7) | collective-permute-done | bytes 196640 | tf_op jit(solution)/shard_map/ppermute | solution.py:272
  59.2 3.7 %collective-permute-done.8 = bf16[128,768]{1,0:T(8,128)(2,1)S(1)} collective-permute-done((bf16[128,768]{1,0:T(8,128)(2,1)S(1)}, bf16[128,768]{1,0:T(8,128)(2,1)S(1)}, u32[]{:S(2)}, u32[]{:S(2)}) %collective-permute-start.8) | collective-permute-done | bytes 196640 | tf_op jit(solution)/shard_map/ppermute | solution.py:272
  62.8 3.0 %project_out.11 = (f32[128,3072]{1,0:T(8,128)S(1)}, bf16[128,3072]{1,0:T(8,128)(2,1)S(1)}) custom-call(bf16[256,512]{1,0:T(8,128)(2,1)S(1)} %attend.3.refs_0_, bf16[512,3072]{1,0:T(8,128)(2,1)} %refs_1_.3, f32[128,3072]{1,0:T(8,128)S(1)} %get-tuple-element.103.refs_2_, f32[128,3072]{1,0:T(8,128)S(1)} %get-tuple-element.104.refs_3_), custom_call_target="tpu_custom_call" | custom-call | flops 805306368 | tf_op jit(solution)/shard_map/project_out/pallas_call | solution.py:228
  65.9 2.3 %collective-permute-done.9 = bf16[128,3072]{1,0:T(8,128)(2,1)} collective-permute-done((bf16[128,3072]{1,0:T(8,128)(2,1)S(1)}, bf16[128,3072]{1,0:T(8,128)(2,1)}, u32[]{:S(2)}, u32[]{:S(2)}) %collective-permute-start.9) | collective-permute-done | bytes 786464 | tf_op jit(solution)/shard_map/ppermute | solution.py:269
  68.3 1.3 %convert_add_fusion = f32[128,3072]{1,0:T(8,128)S(1)} fusion(f32[128,3072]{1,0:T(8,128)S(1)} %get-tuple-element.105, bf16[128,3072]{1,0:T(8,128)(2,1)} %collective-permute-done.9), kind=kLoop, calls=%fused_computation.1 | loop fusion | flops 786432 | bytes 3932160 | tf_op jit(solution)/shard_map/add | solution.py:327
  69.7 1.6 %collective-permute-start.10 = (bf16[64,768]{1,0:T(8,128)(2,1)S(1)}, bf16[64,768]{1,0:T(8,128)(2,1)S(1)}, u32[]{:S(2)}, u32[]{:S(2)}) collective-permute-start(bf16[64,768]{1,0:T(8,128)(2,1)S(1)} %dynamic-slice_convert_fusion.3), channel_id=1, source_target_pairs={{0,4},{4,0},{8,12},{12,8},{16,20},{20,16},{24,28},{28,24},{1,5},{5... | collective-permute-start | bytes 294920 | tf_op jit(solution)/shard_map/ppermute | solution.py:275
  71.3 1.5 %collective-permute-start.13 = (bf16[128,768]{1,0:T(8,128)(2,1)S(1)}, bf16[128,768]{1,0:T(8,128)(2,1)S(1)}, u32[]{:S(2)}, u32[]{:S(2)}) collective-permute-start(bf16[128,768]{1,0:T(8,128)(2,1)S(1)} %add_convert_fusion.1), channel_id=1, source_target_pairs={{0,2},{1,3},{2,0},{3,1},{4,6},{5,7},{6,4},{7,5},{8,10},{9,11},{10,... | collective-permute-start | bytes 589832 | tf_op jit(solution)/shard_map/ppermute | solution.py:272
  72.8 0.5 collective-permute-start.16
  73.3 1.3 %collective-permute-done.10 = bf16[64,768]{1,0:T(8,128)(2,1)S(1)} collective-permute-done((bf16[64,768]{1,0:T(8,128)(2,1)S(1)}, bf16[64,768]{1,0:T(8,128)(2,1)S(1)}, u32[]{:S(2)}, u32[]{:S(2)}) %collective-permute-start.10) | collective-permute-done | bytes 98336 | tf_op jit(solution)/shard_map/ppermute | solution.py:275
  74.7 0.7 collective-permute-start.11
  75.4 1.6 %collective-permute-start.14 = (bf16[64,768]{1,0:T(8,128)(2,1)S(1)}, bf16[64,768]{1,0:T(8,128)(2,1)S(1)}, u32[]{:S(2)}, u32[]{:S(2)}) collective-permute-start(bf16[64,768]{1,0:T(8,128)(2,1)S(1)} %dynamic-slice_convert_fusion.2), channel_id=1, source_target_pairs={{0,4},{4,0},{8,12},{12,8},{16,20},{20,16},{24,28},{28,24},{1,5},{5... | collective-permute-start | bytes 294920 | tf_op jit(solution)/shard_map/ppermute | solution.py:275
  77.0 0.7 collective-permute-start.12
  77.7 2.4 %collective-permute-done.14 = bf16[64,768]{1,0:T(8,128)(2,1)S(1)} collective-permute-done((bf16[64,768]{1,0:T(8,128)(2,1)S(1)}, bf16[64,768]{1,0:T(8,128)(2,1)S(1)}, u32[]{:S(2)}, u32[]{:S(2)}) %collective-permute-start.14) | collective-permute-done | bytes 98336 | tf_op jit(solution)/shard_map/ppermute | solution.py:275
  80.1 0.7 collective-permute-start.18
  80.9 1.6 %collective-permute-start.17 = (bf16[64,768]{1,0:T(8,128)(2,1)S(1)}, bf16[64,768]{1,0:T(8,128)(2,1)S(1)}, u32[]{:S(2)}, u32[]{:S(2)}) collective-permute-start(bf16[64,768]{1,0:T(8,128)(2,1)S(1)} %dynamic-slice_convert_fusion.1), channel_id=1, source_target_pairs={{0,4},{4,0},{8,12},{12,8},{16,20},{20,16},{24,28},{28,24},{1,5},{5... | collective-permute-start | bytes 294920 | tf_op jit(solution)/shard_map/ppermute | solution.py:275
  82.5 1.3 %collective-permute-start.15 = (bf16[64,768]{1,0:T(8,128)(2,1)S(1)}, bf16[64,768]{1,0:T(8,128)(2,1)S(1)}, u32[]{:S(2)}, u32[]{:S(2)}) collective-permute-start(bf16[64,768]{1,0:T(8,128)(2,1)S(1)} %add_convert_fusion.11), channel_id=1, source_target_pairs={{16,24},{20,28},{17,25},{21,29},{18,26},{22,30},{19,27},{23,31}} | collective-permute-start | bytes 294920 | tf_op jit(solution)/shard_map/ppermute | solution.py:365
  83.9 0.7 collective-permute-start.22
  84.5 1.0 collective-permute-done.17
  85.6 0.7 collective-permute-start.21
  86.4 1.6 %collective-permute-start.20 = (bf16[64,768]{1,0:T(8,128)(2,1)S(1)}, bf16[64,768]{1,0:T(8,128)(2,1)S(1)}, u32[]{:S(2)}, u32[]{:S(2)}) collective-permute-start(bf16[64,768]{1,0:T(8,128)(2,1)S(1)} %dynamic-slice_convert_fusion), channel_id=1, source_target_pairs={{0,4},{4,0},{8,12},{12,8},{16,20},{20,16},{24,28},{28,24},{1,5},{5... | collective-permute-start | bytes 294920 | tf_op jit(solution)/shard_map/ppermute | solution.py:275
  87.9 2.0 %collective-permute-done.15 = bf16[64,768]{1,0:T(8,128)(2,1)S(1)} collective-permute-done((bf16[64,768]{1,0:T(8,128)(2,1)S(1)}, bf16[64,768]{1,0:T(8,128)(2,1)S(1)}, u32[]{:S(2)}, u32[]{:S(2)}) %collective-permute-start.15) | collective-permute-done | bytes 98336 | tf_op jit(solution)/shard_map/ppermute | solution.py:365
  89.9 1.5 %collective-permute-start.19 = (bf16[64,768]{1,0:T(8,128)(2,1)S(1)}, bf16[64,768]{1,0:T(8,128)(2,1)S(1)}, u32[]{:S(2)}, u32[]{:S(2)}) collective-permute-start(bf16[64,768]{1,0:T(8,128)(2,1)S(1)} %add_convert_fusion.10), channel_id=1, source_target_pairs={{0,4},{4,0},{8,12},{12,8},{16,20},{20,16},{24,28},{28,24},{1,5},{5... | collective-permute-start | bytes 294920 | tf_op jit(solution)/shard_map/ppermute | solution.py:275
  91.5 1.3 %collective-permute-start.23 = (bf16[64,768]{1,0:T(8,128)(2,1)S(1)}, bf16[64,768]{1,0:T(8,128)(2,1)S(1)}, u32[]{:S(2)}, u32[]{:S(2)}) collective-permute-start(bf16[64,768]{1,0:T(8,128)(2,1)S(1)} %add_convert_fusion.9), channel_id=1, source_target_pairs={{16,24},{20,28},{17,25},{21,29},{18,26},{22,30},{19,27},{23,31}} | collective-permute-start | bytes 294920 | tf_op jit(solution)/shard_map/ppermute | solution.py:365
  92.9 0.7 collective-permute-start.26
  93.6 0.7 collective-permute-start.25
  94.3 0.3 collective-permute-done.19
  94.8 3.3 %collective-permute-done.23 = bf16[64,768]{1,0:T(8,128)(2,1)S(1)} collective-permute-done((bf16[64,768]{1,0:T(8,128)(2,1)S(1)}, bf16[64,768]{1,0:T(8,128)(2,1)S(1)}, u32[]{:S(2)}, u32[]{:S(2)}) %collective-permute-start.23) | collective-permute-done | bytes 98336 | tf_op jit(solution)/shard_map/ppermute | solution.py:365
  98.1 1.3 %collective-permute-start.24 = (bf16[64,768]{1,0:T(8,128)(2,1)S(1)}, bf16[64,768]{1,0:T(8,128)(2,1)S(1)}, u32[]{:S(2)}, u32[]{:S(2)}) collective-permute-start(bf16[64,768]{1,0:T(8,128)(2,1)S(1)} %add_convert_fusion.8), channel_id=1, source_target_pairs={{0,4},{4,0},{8,12},{12,8},{16,20},{20,16},{24,28},{28,24},{1,5},{5... | collective-permute-start | bytes 294920 | tf_op jit(solution)/shard_map/ppermute | solution.py:275
  99.5 1.3 %collective-permute-start.27 = (bf16[64,768]{1,0:T(8,128)(2,1)S(1)}, bf16[64,768]{1,0:T(8,128)(2,1)S(1)}, u32[]{:S(2)}, u32[]{:S(2)}) collective-permute-start(bf16[64,768]{1,0:T(8,128)(2,1)S(1)} %add_convert_fusion.7), channel_id=1, source_target_pairs={{16,24},{20,28},{17,25},{21,29},{18,26},{22,30},{19,27},{23,31}} | collective-permute-start | bytes 294920 | tf_op jit(solution)/shard_map/ppermute | solution.py:365
  100.8 0.7 collective-permute-start.29
  101.5 1.3 %collective-permute-done.24 = bf16[64,768]{1,0:T(8,128)(2,1)S(1)} collective-permute-done((bf16[64,768]{1,0:T(8,128)(2,1)S(1)}, bf16[64,768]{1,0:T(8,128)(2,1)S(1)}, u32[]{:S(2)}, u32[]{:S(2)}) %collective-permute-start.24) | collective-permute-done | bytes 98336 | tf_op jit(solution)/shard_map/ppermute | solution.py:275
  102.8 0.1 fusion.15
  102.9 3.1 %collective-permute-done.27 = bf16[64,768]{1,0:T(8,128)(2,1)S(1)} collective-permute-done((bf16[64,768]{1,0:T(8,128)(2,1)S(1)}, bf16[64,768]{1,0:T(8,128)(2,1)S(1)}, u32[]{:S(2)}, u32[]{:S(2)}) %collective-permute-start.27) | collective-permute-done | bytes 98336 | tf_op jit(solution)/shard_map/ppermute | solution.py:365
  106.0 1.3 %collective-permute-start.28 = (bf16[64,768]{1,0:T(8,128)(2,1)S(1)}, bf16[64,768]{1,0:T(8,128)(2,1)S(1)}, u32[]{:S(2)}, u32[]{:S(2)}) collective-permute-start(bf16[64,768]{1,0:T(8,128)(2,1)S(1)} %add_convert_fusion.6), channel_id=1, source_target_pairs={{0,4},{4,0},{8,12},{12,8},{16,20},{20,16},{24,28},{28,24},{1,5},{5... | collective-permute-start | bytes 294920 | tf_op jit(solution)/shard_map/ppermute | solution.py:275
  107.4 1.3 %collective-permute-start.30 = (bf16[64,768]{1,0:T(8,128)(2,1)S(1)}, bf16[64,768]{1,0:T(8,128)(2,1)S(1)}, u32[]{:S(2)}, u32[]{:S(2)}) collective-permute-start(bf16[64,768]{1,0:T(8,128)(2,1)S(1)} %add_convert_fusion.5), channel_id=1, source_target_pairs={{16,24},{20,28},{17,25},{21,29},{18,26},{22,30},{19,27},{23,31}} | collective-permute-start | bytes 294920 | tf_op jit(solution)/shard_map/ppermute | solution.py:365
  108.7 5.2 %collective-permute-done.30 = bf16[64,768]{1,0:T(8,128)(2,1)S(1)} collective-permute-done((bf16[64,768]{1,0:T(8,128)(2,1)S(1)}, bf16[64,768]{1,0:T(8,128)(2,1)S(1)}, u32[]{:S(2)}, u32[]{:S(2)}) %collective-permute-start.30) | collective-permute-done | bytes 98336 | tf_op jit(solution)/shard_map/ppermute | solution.py:365
  114.0 1.3 %collective-permute-start.31 = (bf16[64,768]{1,0:T(8,128)(2,1)S(1)}, bf16[64,768]{1,0:T(8,128)(2,1)S(1)}, u32[]{:S(2)}, u32[]{:S(2)}) collective-permute-start(bf16[64,768]{1,0:T(8,128)(2,1)S(1)} %add_convert_fusion.4), channel_id=1, source_target_pairs={{0,4},{4,0},{8,12},{12,8},{16,20},{20,16},{24,28},{28,24},{1,5},{5... | collective-permute-start | bytes 294920 | tf_op jit(solution)/shard_map/ppermute | solution.py:275
  115.3 0.1 fusion.17
  115.4 3.2 %collective-permute-done.31 = bf16[64,768]{1,0:T(8,128)(2,1)S(1)} collective-permute-done((bf16[64,768]{1,0:T(8,128)(2,1)S(1)}, bf16[64,768]{1,0:T(8,128)(2,1)S(1)}, u32[]{:S(2)}, u32[]{:S(2)}) %collective-permute-start.31) | collective-permute-done | bytes 98336 | tf_op jit(solution)/shard_map/ppermute | solution.py:275
  118.7 0.1 fusion.19
  118.8 0.2 maximum_add_fusion
  119.0 1.3 %maximum_bitcast_fusion = f32[1,128,3072]{2,1,0:T(8,128)} fusion(f32[128,768]{1,0:T(8,128)S(1)} %get-tuple-element.145, f32[128,768]{1,0:T(8,128)S(1)} %get-tuple-element.146, f32[128,768]{1,0:T(8,128)S(1)} %get-tuple-element.144, f32[128,768]{1,0:T(8,128)S(1)} %get-tuple-element.143), kind=kLoop, calls=%fused_computation | loop fusion | flops 1179648 | bytes 3145728 | tf_op jit(solution)/shard_map/broadcast_in_dim | solution.py:392
  (71 shorter events, 1.6 us)
Async XLA Ops:
  0.7 6.6 %copy-start.2 = (f32[128]{0:T(128)S(1)}, f32[128]{0:T(128)}, u32[]{:S(2)}) copy-start(f32[128]{0:T(128)} %param.16) | copy-start | bytes 1540
  0.7 6.6 %copy-start.3 = (f32[128]{0:T(128)S(1)}, f32[128]{0:T(128)}, u32[]{:S(2)}) copy-start(f32[128]{0:T(128)} %param.17) | copy-start | bytes 1540
  4.7 2.6 %collective-permute-start = (bf16[128,3072]{1,0:T(8,128)(2,1)}, bf16[128,3072]{1,0:T(8,128)(2,1)S(1)}, u32[]{:S(2)}, u32[]{:S(2)}) collective-permute-start(bf16[128,3072]{1,0:T(8,128)(2,1)} %get-tuple-element.69.m0), channel_id=1, source_target_pairs={{0,1},{1,0},{2,3},{3,2},{4,5},{5,4},{6,7},{7,6},{8,9},{9,8},{10,11... | collective-permute-start | bytes 2359304 | tf_op jit(solution)/shard_map/ppermute | solution.py:269
  4.8 20.2 %collective-permute-start.1 = (bf16[128,3072]{1,0:T(8,128)(2,1)}, bf16[128,3072]{1,0:T(8,128)(2,1)S(1)}, u32[]{:S(2)}, u32[]{:S(2)}) collective-permute-start(bf16[128,3072]{1,0:T(8,128)(2,1)} %get-tuple-element.69.m0), channel_id=1, source_target_pairs={{0,2},{1,3},{2,0},{3,1},{4,6},{5,7},{6,4},{7,5},{8,10},{9,11},{10,... | collective-permute-start | bytes 2359304 | tf_op jit(solution)/shard_map/ppermute | solution.py:272
  7.2 1.1 copy-start.1
  24.9 2.3 %collective-permute-start.2 = (bf16[128,3072]{1,0:T(8,128)(2,1)S(1)}, bf16[128,3072]{1,0:T(8,128)(2,1)S(1)}, u32[]{:S(2)}, u32[]{:S(2)}) collective-permute-start(bf16[128,3072]{1,0:T(8,128)(2,1)S(1)} %collective-permute-done.1.m0), channel_id=1, source_target_pairs={{0,1},{1,0},{2,3},{3,2},{4,5},{5,4},{6,7},{7,6},{8,9},{9,8},{10,11... | collective-permute-start | bytes 2359304 | tf_op jit(solution)/shard_map/ppermute | solution.py:269
  27.2 11.2 %copy-start = (bf16[512,3072]{1,0:T(8,128)(2,1)S(1)}, bf16[512,3072]{1,0:T(8,128)(2,1)}, u32[]{:S(2)}) copy-start(bf16[512,3072]{1,0:T(8,128)(2,1)} %refs_1_.3) | copy-start | bytes 9437188
  41.0 3.2 %collective-permute-start.3 = (bf16[128,768]{1,0:T(8,128)(2,1)S(1)}, bf16[128,768]{1,0:T(8,128)(2,1)S(1)}, u32[]{:S(2)}, u32[]{:S(2)}) collective-permute-start(bf16[128,768]{1,0:T(8,128)(2,1)S(1)} %get-tuple-element.82), channel_id=1, source_target_pairs={{0,1},{1,0},{2,3},{3,2},{4,5},{5,4},{6,7},{7,6},{8,9},{9,8},{10,11... | collective-permute-start | bytes 589832 | tf_op jit(solution)/shard_map/ppermute | solution.py:269
  43.8 3.3 %collective-permute-start.4 = (bf16[128,768]{1,0:T(8,128)(2,1)S(1)}, bf16[128,768]{1,0:T(8,128)(2,1)S(1)}, u32[]{:S(2)}, u32[]{:S(2)}) collective-permute-start(bf16[128,768]{1,0:T(8,128)(2,1)S(1)} %get-tuple-element.88), channel_id=1, source_target_pairs={{0,1},{1,0},{2,3},{3,2},{4,5},{5,4},{6,7},{7,6},{8,9},{9,8},{10,11... | collective-permute-start | bytes 589832 | tf_op jit(solution)/shard_map/ppermute | solution.py:269
  46.9 3.3 %collective-permute-start.5 = (bf16[128,768]{1,0:T(8,128)(2,1)S(1)}, bf16[128,768]{1,0:T(8,128)(2,1)S(1)}, u32[]{:S(2)}, u32[]{:S(2)}) collective-permute-start(bf16[128,768]{1,0:T(8,128)(2,1)S(1)} %get-tuple-element.94), channel_id=1, source_target_pairs={{0,1},{1,0},{2,3},{3,2},{4,5},{5,4},{6,7},{7,6},{8,9},{9,8},{10,11... | collective-permute-start | bytes 589832 | tf_op jit(solution)/shard_map/ppermute | solution.py:269
  49.8 1.5 %collective-permute-start.6 = (bf16[128,768]{1,0:T(8,128)(2,1)S(1)}, bf16[128,768]{1,0:T(8,128)(2,1)S(1)}, u32[]{:S(2)}, u32[]{:S(2)}) collective-permute-start(bf16[128,768]{1,0:T(8,128)(2,1)S(1)} %get-tuple-element.98), channel_id=1, source_target_pairs={{0,1},{1,0},{2,3},{3,2},{4,5},{5,4},{6,7},{7,6},{8,9},{9,8},{10,11... | collective-permute-start | bytes 589832 | tf_op jit(solution)/shard_map/ppermute | solution.py:269
  51.4 7.8 %collective-permute-start.7 = (bf16[128,768]{1,0:T(8,128)(2,1)S(1)}, bf16[128,768]{1,0:T(8,128)(2,1)S(1)}, u32[]{:S(2)}, u32[]{:S(2)}) collective-permute-start(bf16[128,768]{1,0:T(8,128)(2,1)S(1)} %add_convert_fusion.3), channel_id=1, source_target_pairs={{0,2},{1,3},{2,0},{3,1},{4,6},{5,7},{6,4},{7,5},{8,10},{9,11},{10,... | collective-permute-start | bytes 589832 | tf_op jit(solution)/shard_map/ppermute | solution.py:272
  53.0 9.9 %collective-permute-start.8 = (bf16[128,768]{1,0:T(8,128)(2,1)S(1)}, bf16[128,768]{1,0:T(8,128)(2,1)S(1)}, u32[]{:S(2)}, u32[]{:S(2)}) collective-permute-start(bf16[128,768]{1,0:T(8,128)(2,1)S(1)} %add_convert_fusion.2), channel_id=1, source_target_pairs={{0,2},{1,3},{2,0},{3,1},{4,6},{5,7},{6,4},{7,5},{8,10},{9,11},{10,... | collective-permute-start | bytes 589832 | tf_op jit(solution)/shard_map/ppermute | solution.py:272
  55.2 10.7 %copy-start.9 = (f32[1,3072]{1,0:T(1,128)S(1)}, f32[1,3072]{1,0:T(1,128)}, u32[]{:S(2)}) copy-start(f32[1,3072]{1,0:T(1,128)} %get-tuple-element.68) | copy-start | bytes 36868
  59.2 6.6 %copy-start.7 = (bf16[128,768]{1,0:T(8,128)(2,1)}, bf16[128,768]{1,0:T(8,128)(2,1)S(1)}, u32[]{:S(2)}) copy-start(bf16[128,768]{1,0:T(8,128)(2,1)S(1)} %collective-permute-done.7) | copy-start | bytes 589828
  62.8 3.0 %copy-start.5 = (bf16[128,768]{1,0:T(8,128)(2,1)}, bf16[128,768]{1,0:T(8,128)(2,1)S(1)}, u32[]{:S(2)}) copy-start(bf16[128,768]{1,0:T(8,128)(2,1)S(1)} %collective-permute-done.8) | copy-start | bytes 589828
  65.8 2.5 %collective-permute-start.9 = (bf16[128,3072]{1,0:T(8,128)(2,1)S(1)}, bf16[128,3072]{1,0:T(8,128)(2,1)}, u32[]{:S(2)}, u32[]{:S(2)}) collective-permute-start(bf16[128,3072]{1,0:T(8,128)(2,1)S(1)} %get-tuple-element.106), channel_id=1, source_target_pairs={{0,1},{1,0},{2,3},{3,2},{4,5},{5,4},{6,7},{7,6},{8,9},{9,8},{10,11... | collective-permute-start | bytes 2359304 | tf_op jit(solution)/shard_map/ppermute | solution.py:269
  68.3 1.4 %copy-start.8 = (bf16[128,768]{1,0:T(8,128)(2,1)S(1)}, bf16[128,768]{1,0:T(8,128)(2,1)}, u32[]{:S(2)}) copy-start(bf16[128,768]{1,0:T(8,128)(2,1)} %copy-done.7) | copy-start | bytes 589828
  69.6 5.7 %copy-start.6 = (bf16[128,768]{1,0:T(8,128)(2,1)S(1)}, bf16[128,768]{1,0:T(8,128)(2,1)}, u32[]{:S(2)}) copy-start(bf16[128,768]{1,0:T(8,128)(2,1)} %copy-done.5) | copy-start | bytes 589828
  69.7 4.9 %collective-permute-start.10 = (bf16[64,768]{1,0:T(8,128)(2,1)S(1)}, bf16[64,768]{1,0:T(8,128)(2,1)S(1)}, u32[]{:S(2)}, u32[]{:S(2)}) collective-permute-start(bf16[64,768]{1,0:T(8,128)(2,1)S(1)} %dynamic-slice_convert_fusion.3), channel_id=1, source_target_pairs={{0,4},{4,0},{8,12},{12,8},{16,20},{20,16},{24,28},{28,24},{1,5},{5... | collective-permute-start | bytes 294920 | tf_op jit(solution)/shard_map/ppermute | solution.py:275
  71.3 9.5 %collective-permute-start.13 = (bf16[128,768]{1,0:T(8,128)(2,1)S(1)}, bf16[128,768]{1,0:T(8,128)(2,1)S(1)}, u32[]{:S(2)}, u32[]{:S(2)}) collective-permute-start(bf16[128,768]{1,0:T(8,128)(2,1)S(1)} %add_convert_fusion.1), channel_id=1, source_target_pairs={{0,2},{1,3},{2,0},{3,1},{4,6},{5,7},{6,4},{7,5},{8,10},{9,11},{10,... | collective-permute-start | bytes 589832 | tf_op jit(solution)/shard_map/ppermute | solution.py:272
  72.8 13.5 %collective-permute-start.16 = (bf16[128,768]{1,0:T(8,128)(2,1)S(1)}, bf16[128,768]{1,0:T(8,128)(2,1)S(1)}, u32[]{:S(2)}, u32[]{:S(2)}) collective-permute-start(bf16[128,768]{1,0:T(8,128)(2,1)S(1)} %add_convert_fusion), channel_id=1, source_target_pairs={{0,2},{1,3},{2,0},{3,1},{4,6},{5,7},{6,4},{7,5},{8,10},{9,11},{10,... | collective-permute-start | bytes 589832 | tf_op jit(solution)/shard_map/ppermute | solution.py:272
  74.7 2.3 %collective-permute-start.11 = (bf16[64,768]{1,0:T(8,128)(2,1)S(1)}, bf16[64,768]{1,0:T(8,128)(2,1)S(1)}, u32[]{:S(2)}, u32[]{:S(2)}) collective-permute-start(bf16[64,768]{1,0:T(8,128)(2,1)S(1)} %fusion.20), channel_id=1, source_target_pairs={{0,8},{4,12},{1,9},{5,13},{2,10},{6,14},{3,11},{7,15}} | collective-permute-start | bytes 294920 | tf_op jit(solution)/shard_map/ppermute | solution.py:365
  75.4 4.7 %collective-permute-start.14 = (bf16[64,768]{1,0:T(8,128)(2,1)S(1)}, bf16[64,768]{1,0:T(8,128)(2,1)S(1)}, u32[]{:S(2)}, u32[]{:S(2)}) collective-permute-start(bf16[64,768]{1,0:T(8,128)(2,1)S(1)} %dynamic-slice_convert_fusion.2), channel_id=1, source_target_pairs={{0,4},{4,0},{8,12},{12,8},{16,20},{20,16},{24,28},{28,24},{1,5},{5... | collective-permute-start | bytes 294920 | tf_op jit(solution)/shard_map/ppermute | solution.py:275
  77.0 5.4 %collective-permute-start.12 = (bf16[64,768]{1,0:T(8,128)(2,1)S(1)}, bf16[64,768]{1,0:T(8,128)(2,1)S(1)}, u32[]{:S(2)}, u32[]{:S(2)}) collective-permute-start(bf16[64,768]{1,0:T(8,128)(2,1)S(1)} %fusion.5), channel_id=1, source_target_pairs={{8,16},{12,20},{9,17},{13,21},{10,18},{14,22},{11,19},{15,23}} | collective-permute-start | bytes 294920 | tf_op jit(solution)/shard_map/ppermute | solution.py:365
  80.1 3.7 %collective-permute-start.18 = (bf16[64,768]{1,0:T(8,128)(2,1)S(1)}, bf16[64,768]{1,0:T(8,128)(2,1)S(1)}, u32[]{:S(2)}, u32[]{:S(2)}) collective-permute-start(bf16[64,768]{1,0:T(8,128)(2,1)S(1)} %fusion.21), channel_id=1, source_target_pairs={{0,8},{4,12},{1,9},{5,13},{2,10},{6,14},{3,11},{7,15}} | collective-permute-start | bytes 294920 | tf_op jit(solution)/shard_map/ppermute | solution.py:365
  80.9 4.7 %collective-permute-start.17 = (bf16[64,768]{1,0:T(8,128)(2,1)S(1)}, bf16[64,768]{1,0:T(8,128)(2,1)S(1)}, u32[]{:S(2)}, u32[]{:S(2)}) collective-permute-start(bf16[64,768]{1,0:T(8,128)(2,1)S(1)} %dynamic-slice_convert_fusion.1), channel_id=1, source_target_pairs={{0,4},{4,0},{8,12},{12,8},{16,20},{20,16},{24,28},{28,24},{1,5},{5... | collective-permute-start | bytes 294920 | tf_op jit(solution)/shard_map/ppermute | solution.py:275
  82.5 7.4 %collective-permute-start.15 = (bf16[64,768]{1,0:T(8,128)(2,1)S(1)}, bf16[64,768]{1,0:T(8,128)(2,1)S(1)}, u32[]{:S(2)}, u32[]{:S(2)}) collective-permute-start(bf16[64,768]{1,0:T(8,128)(2,1)S(1)} %add_convert_fusion.11), channel_id=1, source_target_pairs={{16,24},{20,28},{17,25},{21,29},{18,26},{22,30},{19,27},{23,31}} | collective-permute-start | bytes 294920 | tf_op jit(solution)/shard_map/ppermute | solution.py:365
  83.9 7.6 %collective-permute-start.22 = (bf16[64,768]{1,0:T(8,128)(2,1)S(1)}, bf16[64,768]{1,0:T(8,128)(2,1)S(1)}, u32[]{:S(2)}, u32[]{:S(2)}) collective-permute-start(bf16[64,768]{1,0:T(8,128)(2,1)S(1)} %fusion.7), channel_id=1, source_target_pairs={{8,16},{12,20},{9,17},{13,21},{10,18},{14,22},{11,19},{15,23}} | collective-permute-start | bytes 294920 | tf_op jit(solution)/shard_map/ppermute | solution.py:365
  85.6 7.2 %collective-permute-start.21 = (bf16[64,768]{1,0:T(8,128)(2,1)S(1)}, bf16[64,768]{1,0:T(8,128)(2,1)S(1)}, u32[]{:S(2)}, u32[]{:S(2)}) collective-permute-start(bf16[64,768]{1,0:T(8,128)(2,1)S(1)} %fusion.22), channel_id=1, source_target_pairs={{0,8},{4,12},{1,9},{5,13},{2,10},{6,14},{3,11},{7,15}} | collective-permute-start | bytes 294920 | tf_op jit(solution)/shard_map/ppermute | solution.py:365
  86.4 7.2 %collective-permute-start.20 = (bf16[64,768]{1,0:T(8,128)(2,1)S(1)}, bf16[64,768]{1,0:T(8,128)(2,1)S(1)}, u32[]{:S(2)}, u32[]{:S(2)}) collective-permute-start(bf16[64,768]{1,0:T(8,128)(2,1)S(1)} %dynamic-slice_convert_fusion), channel_id=1, source_target_pairs={{0,4},{4,0},{8,12},{12,8},{16,20},{20,16},{24,28},{28,24},{1,5},{5... | collective-permute-start | bytes 294920 | tf_op jit(solution)/shard_map/ppermute | solution.py:275
  89.9 4.7 %collective-permute-start.19 = (bf16[64,768]{1,0:T(8,128)(2,1)S(1)}, bf16[64,768]{1,0:T(8,128)(2,1)S(1)}, u32[]{:S(2)}, u32[]{:S(2)}) collective-permute-start(bf16[64,768]{1,0:T(8,128)(2,1)S(1)} %add_convert_fusion.10), channel_id=1, source_target_pairs={{0,4},{4,0},{8,12},{12,8},{16,20},{20,16},{24,28},{28,24},{1,5},{5... | collective-permute-start | bytes 294920 | tf_op jit(solution)/shard_map/ppermute | solution.py:275
  91.5 6.5 %collective-permute-start.23 = (bf16[64,768]{1,0:T(8,128)(2,1)S(1)}, bf16[64,768]{1,0:T(8,128)(2,1)S(1)}, u32[]{:S(2)}, u32[]{:S(2)}) collective-permute-start(bf16[64,768]{1,0:T(8,128)(2,1)S(1)} %add_convert_fusion.9), channel_id=1, source_target_pairs={{16,24},{20,28},{17,25},{21,29},{18,26},{22,30},{19,27},{23,31}} | collective-permute-start | bytes 294920 | tf_op jit(solution)/shard_map/ppermute | solution.py:365
  92.9 6.5 %collective-permute-start.26 = (bf16[64,768]{1,0:T(8,128)(2,1)S(1)}, bf16[64,768]{1,0:T(8,128)(2,1)S(1)}, u32[]{:S(2)}, u32[]{:S(2)}) collective-permute-start(bf16[64,768]{1,0:T(8,128)(2,1)S(1)} %fusion.9), channel_id=1, source_target_pairs={{8,16},{12,20},{9,17},{13,21},{10,18},{14,22},{11,19},{15,23}} | collective-permute-start | bytes 294920 | tf_op jit(solution)/shard_map/ppermute | solution.py:365
  93.6 7.2 %collective-permute-start.25 = (bf16[64,768]{1,0:T(8,128)(2,1)S(1)}, bf16[64,768]{1,0:T(8,128)(2,1)S(1)}, u32[]{:S(2)}, u32[]{:S(2)}) collective-permute-start(bf16[64,768]{1,0:T(8,128)(2,1)S(1)} %fusion.23), channel_id=1, source_target_pairs={{0,8},{4,12},{1,9},{5,13},{2,10},{6,14},{3,11},{7,15}} | collective-permute-start | bytes 294920 | tf_op jit(solution)/shard_map/ppermute | solution.py:365
  98.1 4.7 %collective-permute-start.24 = (bf16[64,768]{1,0:T(8,128)(2,1)S(1)}, bf16[64,768]{1,0:T(8,128)(2,1)S(1)}, u32[]{:S(2)}, u32[]{:S(2)}) collective-permute-start(bf16[64,768]{1,0:T(8,128)(2,1)S(1)} %add_convert_fusion.8), channel_id=1, source_target_pairs={{0,4},{4,0},{8,12},{12,8},{16,20},{20,16},{24,28},{28,24},{1,5},{5... | collective-permute-start | bytes 294920 | tf_op jit(solution)/shard_map/ppermute | solution.py:275
  99.5 6.5 %collective-permute-start.27 = (bf16[64,768]{1,0:T(8,128)(2,1)S(1)}, bf16[64,768]{1,0:T(8,128)(2,1)S(1)}, u32[]{:S(2)}, u32[]{:S(2)}) collective-permute-start(bf16[64,768]{1,0:T(8,128)(2,1)S(1)} %add_convert_fusion.7), channel_id=1, source_target_pairs={{16,24},{20,28},{17,25},{21,29},{18,26},{22,30},{19,27},{23,31}} | collective-permute-start | bytes 294920 | tf_op jit(solution)/shard_map/ppermute | solution.py:365
  100.8 6.5 %collective-permute-start.29 = (bf16[64,768]{1,0:T(8,128)(2,1)S(1)}, bf16[64,768]{1,0:T(8,128)(2,1)S(1)}, u32[]{:S(2)}, u32[]{:S(2)}) collective-permute-start(bf16[64,768]{1,0:T(8,128)(2,1)S(1)} %fusion.11), channel_id=1, source_target_pairs={{8,16},{12,20},{9,17},{13,21},{10,18},{14,22},{11,19},{15,23}} | collective-permute-start | bytes 294920 | tf_op jit(solution)/shard_map/ppermute | solution.py:365
  106.0 9.2 %collective-permute-start.28 = (bf16[64,768]{1,0:T(8,128)(2,1)S(1)}, bf16[64,768]{1,0:T(8,128)(2,1)S(1)}, u32[]{:S(2)}, u32[]{:S(2)}) collective-permute-start(bf16[64,768]{1,0:T(8,128)(2,1)S(1)} %add_convert_fusion.6), channel_id=1, source_target_pairs={{0,4},{4,0},{8,12},{12,8},{16,20},{20,16},{24,28},{28,24},{1,5},{5... | collective-permute-start | bytes 294920 | tf_op jit(solution)/shard_map/ppermute | solution.py:275
  107.4 6.5 %collective-permute-start.30 = (bf16[64,768]{1,0:T(8,128)(2,1)S(1)}, bf16[64,768]{1,0:T(8,128)(2,1)S(1)}, u32[]{:S(2)}, u32[]{:S(2)}) collective-permute-start(bf16[64,768]{1,0:T(8,128)(2,1)S(1)} %add_convert_fusion.5), channel_id=1, source_target_pairs={{16,24},{20,28},{17,25},{21,29},{18,26},{22,30},{19,27},{23,31}} | collective-permute-start | bytes 294920 | tf_op jit(solution)/shard_map/ppermute | solution.py:365
  114.0 4.7 %collective-permute-start.31 = (bf16[64,768]{1,0:T(8,128)(2,1)S(1)}, bf16[64,768]{1,0:T(8,128)(2,1)S(1)}, u32[]{:S(2)}, u32[]{:S(2)}) collective-permute-start(bf16[64,768]{1,0:T(8,128)(2,1)S(1)} %add_convert_fusion.4), channel_id=1, source_target_pairs={{0,4},{4,0},{8,12},{12,8},{16,20},{20,16},{24,28},{28,24},{1,5},{5... | collective-permute-start | bytes 294920 | tf_op jit(solution)/shard_map/ppermute | solution.py:275
  115.4 3.4 %copy-start.4 = (f32[128,3072]{1,0:T(8,128)S(1)}, f32[128,3072]{1,0:T(8,128)}, u32[]{:S(2)}) copy-start(f32[128,3072]{1,0:T(8,128)} %param.12) | copy-start | bytes 4718596

commit v3 on v2

--- a/solution.py
+++ b/solution.py
@@ -74,25 +74,25 @@
     )(t_idx, trajectory, mod_table, step_sizes)
 
 
-def project_kernel(tile, m0, m1, qg, kg, wq_hbm, wm_hbm, q, k, v, act, rows, wq, wm, sem_q, sem_m):
+def project_kernel(tile, load, tiles, m0, m1, qg, kg, *refs):
+    if load:
+        wq_hbm, wm_hbm, q, k, v, act = refs[:6]
+        held, rows, sem = refs[6:-2], refs[-2], refs[-1]
+    else:
+        held = refs[:tiles]
+        q, k, v, act, rows = refs[tiles:]
     half = m0.shape[0]
     head = qg.shape[1]
-    n_q = wq.shape[2] // tile
-    n_m = wm.shape[1] // tile
+    n_q = q.shape[1] // tile
     copies = []
-    for which in range(3):
-        for i in range(n_q):
-            cols = pl.ds(i * tile, tile)
-            copies.append(
-                pltpu.make_async_copy(
-                    wq_hbm.at[which, :, cols], wq.at[which, :, cols], sem_q.at[which * n_q + i]
-                )
-            )
-    for i in range(n_m):
-        cols = pl.ds(i * tile, tile)
-        copies.append(pltpu.make_async_copy(wm_hbm.at[:, cols], wm.at[:, cols], sem_m.at[i]))
-    for copy in copies:
-        copy.start()
+    if load:
+        for i in range(tiles):
+            if i < 3 * n_q:
+                source = wq_hbm.at[i // n_q, :, pl.ds(i % n_q * tile, tile)]
+            else:
+                source = wm_hbm.at[:, pl.ds((i - 3 * n_q) * tile, tile)]
+            copies.append(pltpu.make_async_copy(source, held[i], sem.at[i]))
+            copies[i].start()
     rows[:half] = m0[...]
     rows[half:] = m1[...]
 
@@ -104,49 +104,48 @@
             parts.append((one * lax.rsqrt(square + eps) * gain).astype(bf16))
         return jnp.concatenate(parts, axis=1)
 
-    for which in range(3):
-        for i in range(n_q):
-            copies[which * n_q + i].wait()
-            cols = slice(i * tile, (i + 1) * tile)
-            y = jnp.dot(rows[...], wq[which, :, cols], preferred_element_type=f32)
-            if which == 0:
-                q[:, cols] = normed(y, qg[...])
-            elif which == 1:
-                k[:, cols] = normed(y, kg[...])
-            else:
-                v[:, cols] = y.astype(bf16)
-    for i in range(n_m):
-        copies[3 * n_q + i].wait()
-        cols = slice(i * tile, (i + 1) * tile)
-        y = jnp.dot(rows[...], wm[:, cols], preferred_element_type=f32)
-        act[:, cols] = jax.nn.gelu(y, approximate=True).astype(bf16)
-
-
-def project_call(m0, m1, q_gain, k_gain, w_qkv, w_mlp_in):
+    for i in range(tiles):
+        if load:
+            copies[i].wait()
+        y = jnp.dot(rows[...], held[i][...], preferred_element_type=f32)
+        cols = slice(i % n_q * tile, (i % n_q + 1) * tile)
+        if i < n_q:
+            q[:, cols] = normed(y, qg[...])
+        elif i < 2 * n_q:
+            k[:, cols] = normed(y, kg[...])
+        elif i < 3 * n_q:
+            v[:, cols] = y.astype(bf16)
+        else:
+            cols = slice((i - 3 * n_q) * tile, (i - 3 * n_q + 1) * tile)
+            act[:, cols] = jax.nn.gelu(y, approximate=True).astype(bf16)
+
+
+def project_call(m0, m1, q_gain, k_gain, w_qkv, w_mlp_in, held):
     half, width = m0.shape
     heads = w_qkv.shape[2]
     hidden = w_mlp_in.shape[1]
     tile = min(512, heads)
+    tiles = (3 * heads + hidden) // tile
     rows = 2 * half
+    load = held is None
     vm = pl.BlockSpec(memory_space=VM)
     hbm = pl.BlockSpec(memory_space=pltpu.HBM)
+    shapes = [jax.ShapeDtypeStruct((rows, heads), bf16)] * 3
+    shapes.append(jax.ShapeDtypeStruct((rows, hidden), bf16))
+    scratch = [VM((rows, width), bf16)]
+    if load:
+        shapes += [jax.ShapeDtypeStruct((width, tile), bf16)] * tiles
+        scratch.append(pltpu.SemaphoreType.DMA((tiles,)))
     return pl.pallas_call(
-        functools.partial(project_kernel, tile),
-        in_specs=[vm, vm, vm, vm, hbm, hbm],
-        out_specs=[vm] * 4,
-        out_shape=[jax.ShapeDtypeStruct((rows, heads), bf16)] * 3
-        + [jax.ShapeDtypeStruct((rows, hidden), bf16)],
-        scratch_shapes=[
-            VM((rows, width), bf16),
-            VM((3, width, heads), bf16),
-            VM((width, hidden), bf16),
-            pltpu.SemaphoreType.DMA((3 * heads // tile,)),
-            pltpu.SemaphoreType.DMA((hidden // tile,)),
-        ],
-        compiler_params=params(46),
+        functools.partial(project_kernel, tile, load, tiles),
+        in_specs=[vm] * 4 + ([hbm] * 2 if load else [vm] * tiles),
+        out_specs=[vm] * len(shapes),
+        out_shape=shapes,
+        scratch_shapes=scratch,
+        compiler_params=params(26 if load else 9),
         cost_estimate=cost(2 * rows * width * (3 * heads + hidden), 0),
         name="project",
-    )(m0, m1, q_gain, k_gain, w_qkv, w_mlp_in)
+    )(m0, m1, q_gain, k_gain, *([w_qkv, w_mlp_in] if load else held))
 
 
 def attend_kernel(pairs, head, *refs):
@@ -182,63 +181,41 @@
         in_specs=[vm] * (1 + 2 * len(ks)),
         out_specs=vm,
         out_shape=jax.ShapeDtypeStruct(q.shape, bf16),
-        compiler_params=params(46),
+        compiler_params=params(9),
         cost_estimate=cost(4 * len(ks) * q.shape[0] ** 2 * q.shape[1] * 3, 0),
         name="attend",
     )(q, *ks, *vs)
 
 
 def out_kernel(first, parts, *refs):
-    xs, ws, extra = refs[:parts], refs[parts : 2 * parts], refs[2 * parts : -3 - parts]
-    keep, send = refs[-3 - parts], refs[-2 - parts]
-    held, sem = refs[-1 - parts : -1], refs[-1]
+    xs, ws = refs[:parts], refs[parts : 2 * parts]
+    keep, send = refs[-2:]
     half, count = keep.shape
-    piece = 512
-    there = pl.ds(first, count)
-    copies = []
-    for w, to in zip(ws, held):
-        for at in range(0, w.shape[0], piece):
-            here = pl.ds(at, min(piece, w.shape[0] - at))
-            copies.append(
-                pltpu.make_async_copy(w.at[here, there], to.at[here, :], sem.at[len(copies)])
-            )
-            copies[-1].start()
-    turn = 0
-    y = None
-    for x, to in zip(xs, held):
-        for at in range(0, to.shape[0], piece):
-            here = slice(at, min(at + piece, to.shape[0]))
-            copies[turn].wait()
-            turn += 1
-            term = jnp.dot(x[:, here], to[here, :], preferred_element_type=f32)
-            y = term if y is None else y + term
-    low, high = y[:half], y[half:]
-    if extra:
-        low = low + extra[0][:, first : first + count]
-        high = high + extra[1][:, first : first + count]
-    keep[...] = low
-    send[...] = high.astype(send.dtype)
-
-
-def out_call(xs, ws, extra, first, count, kind):
+    cols = slice(first, first + count)
+    terms = [
+        jnp.dot(x[...], w[:, cols], preferred_element_type=f32) for x, w in zip(xs, ws)
+    ]
+    y = functools.reduce(jnp.add, terms)
+    keep[...] = y[:half]
+    send[...] = y[half:].astype(bf16)
+
+
+def out_call(xs, ws, first, count):
     half = xs[0].shape[0] // 2
     depth = sum(x.shape[1] for x in xs)
     vm = pl.BlockSpec(memory_space=VM)
-    hbm = pl.BlockSpec(memory_space=pltpu.HBM)
     return pl.pallas_call(
         functools.partial(out_kernel, first, len(xs)),
-        in_specs=[vm] * len(xs) + [hbm] * len(ws) + [vm] * len(extra),
+        in_specs=[vm] * (2 * len(xs)),
         out_specs=[vm, vm],
         out_shape=[
             jax.ShapeDtypeStruct((half, count), f32),
-            jax.ShapeDtypeStruct((half, count), kind),
+            jax.ShapeDtypeStruct((half, count), bf16),
         ],
-        scratch_shapes=[VM((x.shape[1], count), bf16) for x in xs]
-        + [pltpu.SemaphoreType.DMA((sum(-(-x.shape[1] // 512) for x in xs),))],
-        compiler_params=params(46),
+        compiler_params=params(9),
         cost_estimate=cost(4 * half * count * depth, 0),
         name="project_out",
-    )(*xs, *ws, *extra)
+    )(*xs, *ws)
 
 
 def per_device(
@@ -283,12 +260,13 @@
 
     mine, sg = norm_call(t_idx, trajectory, mod_table, step_sizes)
     far = [to_chip(mine, j) for j in offsets]
-    q0, k0, v0, act0 = project_call(mine, to_core(mine), qg, kg, w_qkv, w_mlp_in)
-    low0, high0 = out_call([act0], [w_out_mlp], [], 0, width, f32)
-    far, low0, high0 = tied(far, low0, high0)
+    q0, k0, v0, act0, *held = project_call(
+        mine, to_core(mine), qg, kg, w_qkv, w_mlp_in, None
+    )
+    far, act0 = tied(far, act0)
     qs, ks, vs, acts = [], [k0], [v0], []
     for block in far:
-        q, k, v, act = project_call(block, to_core(block), qg, kg, w_qkv, w_mlp_in)
+        q, k, v, act = project_call(block, to_core(block), qg, kg, w_qkv, w_mlp_in, held)
         qs.append(q)
         ks.append(k)
         vs.append(v)
@@ -302,7 +280,7 @@
     gate = (mixed, acts)
     for c, first in enumerate(firsts):
         for j in range(chips - 1):
-            keep, send = out_call([gate[0][j], gate[1][j]], weights, [], first, count, bf16)
+            keep, send = out_call([gate[0][j], gate[1][j]], weights, first, count)
             sums[j].append((keep, to_core(send)))
         if c >= 1:
             for j in range(chips - 1):
@@ -323,7 +301,7 @@
     early = [row[:2] for row in got]
     mixed0, early = tied(mixed0, early)
     got = [e + row[2:] for e, row in zip(early, got)]
-    keep0, send0 = out_call([mixed0], [w_out_attn], [low0, high0], 0, width, bf16)
+    keep0, send0 = out_call([mixed0, act0], weights, 0, width)
     own = keep0 + to_core(send0).astype(f32)
 
     def prefix_stages(c):

time: 121 us -> 111 us (0.917)
  Pallas kernels: 45.1 us -> 28.6 us
  waiting for transfers between devices: 39.1 us -> 45.5 us
    pallas_call x6 -> x5, Pallas kernels: 19 us -> 7.55 us  [out_call(): pl.pallas_call(functools.partial(out_kernel, first, len(xs)), in_specs=[v...]
    ppermute x5, waiting for transfers between devices: 9.34 us -> 15.8 us  [to_chip(): lax.ppermute(x, 'seq', [(i, (i + 2 * offset) % n_seq) for i in range(n_se...]
    pallas_call x2, Pallas kernels: 18.5 us -> 13.7 us  [project_call(): pl.pallas_call(functools.partial(project_kernel, tile, load, tiles), in_s...]
    ppermute x8, waiting for transfers between devices: 9.63 us -> 11.1 us  [to_pair(): return lax.ppermute(x, 'step', [(i, i ^ 1) for i in range(n_step)])]
    ppermute x12, waiting for transfers between devices: 13.5 us -> 12.1 us  [along(): return lambda x: lax.ppermute(x, 'step', moves)]
  transfers between devices with their start and end apart: 32 -> 32, of which waited for: 17 -> 16; matrix products, arithmetic and copies ran while one was open for 1% -> 1% of each run, Pallas kernels for 20% -> 12%
where the time goes in v3:
time: 111 us; the launch traced here: 110 us
  waiting for transfers between devices  45.5 us (41%)
  starting transfers between devices  29.2 us (26%)
  Pallas kernels  28.6 us (26%)
  other arithmetic  4.32 us (4%)
  local copies, waits for them, and re-layouts  1.3 us (1%)
  between operations  1.24 us (1%)
    ppermute x5, waiting for transfers between devices, to_chip(): lax.ppermute(x, 'seq', [(i, (i + 2 * offset) % n_seq) for i in range(n_se...  15.8 us
    pallas_call x2, Pallas kernels, project_call(): pl.pallas_call(functools.partial(project_kernel, tile, load, tiles), in_s...  13.7 us
    ppermute x12, waiting for transfers between devices, along(): return lambda x: lax.ppermute(x, 'step', moves)  12.1 us
    ppermute x8, starting transfers between devices, to_pair(): return lax.ppermute(x, 'step', [(i, i ^ 1) for i in range(n_step)])  11.6 us
    ppermute x8, waiting for transfers between devices, to_pair(): return lax.ppermute(x, 'step', [(i, i ^ 1) for i in range(n_step)])  11.1 us
    ppermute x12, starting transfers between devices, along(): return lambda x: lax.ppermute(x, 'step', moves)  10.5 us
    pallas_call x5, Pallas kernels, out_call(): pl.pallas_call(functools.partial(out_kernel, first, len(xs)), in_specs=[v...  7.55 us
    ppermute x7, waiting for transfers between devices, to_core(): return lax.ppermute(x, 'seq', [(i, i ^ 1) for i in range(n_seq)])  6.56 us
  transfers between devices with their start and end apart: 32, of which 16 were waited for; matrix products, arithmetic and copies ran while one was open for 1% of the time, Pallas kernels for 12%

profile of v3, /device:TPU:24, one launch (start us, length us, event | category | flops | bytes accessed | tf_op | source)
XLA Modules:
  0.0 110.3 jit_solution(7001349418719969612)
XLA Ops:
  0.7 4.0 %norm.1 = (bf16[128,3072]{1,0:T(8,128)(2,1)}, f32[1,3072]{1,0:T(1,128)}) custom-call(s32[1]{0:T(128)S(6)} %copy.12.t_ref, f32[1,128,3072]{2,1,0:T(8,128)} %x_hbm.1, f32[50,9216]{1,0:T(8,128)} %mod_ref.1, f32[50]{0:T(128)} %size_ref.1), custom_call_target="tpu_custom_call" | custom-call | flops 3932160 | tf_op jit(solution)/shard_map/norm/pallas_call | solution.py:51
  4.8 1.6 %collective-permute-start.1 = (bf16[128,3072]{1,0:T(8,128)(2,1)}, bf16[128,3072]{1,0:T(8,128)(2,1)S(1)}, u32[]{:S(2)}, u32[]{:S(2)}) collective-permute-start(bf16[128,3072]{1,0:T(8,128)(2,1)} %get-tuple-element.72.m0), channel_id=1, source_target_pairs={{0,2},{1,3},{2,0},{3,1},{4,6},{5,7},{6,4},{7,5},{8,10},{9,11},{10,... | collective-permute-start | bytes 2359304 | tf_op jit(solution)/shard_map/ppermute | solution.py:249
  6.3 0.9 collective-permute-done.m1
  7.2 1.1 %copy-done.1 = bf16[128,3072]{1,0:T(8,128)(2,1)S(1)} copy-done((bf16[128,3072]{1,0:T(8,128)(2,1)S(1)}, bf16[128,3072]{1,0:T(8,128)(2,1)}, u32[]{:S(2)}) %copy-start.1) | copy-done | bytes 786456
  8.4 8.4 %project.2 = (bf16[256,512]{1,0:T(8,128)(2,1)S(1)}, bf16[256,512]{1,0:T(8,128)(2,1)S(1)}, bf16[256,512]{1,0:T(8,128)(2,1)S(1)}, bf16[256,1536]{1,0:T(8,128)(2,1)...) custom-call(bf16[128,3072]{1,0:T(8,128)(2,1)S(1)} %copy-done.1, ...), custom_call_target="tpu_custom_call" | custom-call | flops 4831838208 | tf_op jit(solution)/shard_map/project/pallas_call | solution.py:139
  16.8 8.1 %collective-permute-done.1.m0 = bf16[128,3072]{1,0:T(8,128)(2,1)S(1)} collective-permute-done((bf16[128,3072]{1,0:T(8,128)(2,1)}, bf16[128,3072]{1,0:T(8,128)(2,1)S(1)}, u32[]{:S(2)}, u32[]{:S(2)}) %collective-permute-start.1) | collective-permute-done | bytes 786464 | tf_op jit(solution)/shard_map/ppermute | solution.py:249
  24.9 2.3 %collective-permute-done.2.m1 = bf16[128,3072]{1,0:T(8,128)(2,1)S(1)} collective-permute-done((bf16[128,3072]{1,0:T(8,128)(2,1)S(1)}, bf16[128,3072]{1,0:T(8,128)(2,1)S(1)}, u32[]{:S(2)}, u32[]{:S(2)}) %collective-permute-start.2) | collective-permute-done | bytes 786464 | tf_op jit(solution)/shard_map/ppermute | solution.py:246
  27.2 5.2 %project.3 = (bf16[256,512]{1,0:T(8,128)(2,1)S(1)}, bf16[256,512]{1,0:T(8,128)(2,1)S(1)}, bf16[256,512]{1,0:T(8,128)(2,1)S(1)}, bf16[256,1536]{1,0:T(8,128)(2,1)S(1)}) custom-call(bf16[128,3072]{1,0:T(8,128)(2,1)S(1)} %collective-permute-done.1.m0, bf16[128,3072]{1,0:T(8,128)(2,1)S(1)} %collective-permute-done.2.m1, f32[1,128]{1,0:T(1,128)S(1)} %bitcast.7, ...), custom_call_target="tpu_custom_call" | custom-call | flops 4831838208 | tf_op jit(solution)/shard_map/project/pallas_call | solution.py:139
  32.5 1.7 %attend.2.refs_0_ = bf16[256,512]{1,0:T(8,128)(2,1)S(1)} custom-call(bf16[256,512]{1,0:T(8,128)(2,1)S(1)} %get-tuple-element.82.refs_0_, bf16[256,512]{1,0:T(8,128)(2,1)S(1)} %get-tuple-element.83.refs_1_, bf16[256,512]{1,0:T(8,128)(2,1)S(1)} %get-tuple-element.84.refs_2_, bf16[256,512]{1,0:T(8,128)(2,1)S(1)} %get-tuple-element.85.refs_3_, ...), custom_call_target="tpu_custom_call" | custom-call | flops 805306368 | tf_op jit(solution)/shard_map/attend/pallas_call | solution.py:179
  34.2 1.0 project_out.5
  35.2 0.2 collective-permute-start.3
  35.4 1.0 project_out.6
  36.4 0.5 collective-permute-start.4
  36.9 1.2 %project_out.7 = (f32[128,768]{1,0:T(8,128)S(1)}, bf16[128,768]{1,0:T(8,128)(2,1)S(1)}) custom-call(bf16[256,512]{1,0:T(8,128)(2,1)S(1)} %attend.2.refs_0_, bf16[256,1536]{1,0:T(8,128)(2,1)S(1)} %get-tuple-element.99.refs_1_, bf16[512,3072]{1,0:T(8,128)(2,1)S(1)} %copy-done, bf16[1536,3072]{1,0:T(8,128)(2,1)S(1)} %bitcast.5), custom_call_target="tpu_custom_call" | custom-call | flops 805306368 | tf_op jit(solution)/shard_map/project_out/pallas_call | solution.py:207
  38.1 0.2 collective-permute-start.5
  38.3 1.0 project_out.8
  39.3 0.5 collective-permute-start.6
  39.8 1.0 collective-permute-done.6
  40.9 1.6 %collective-permute-start.7 = (bf16[128,768]{1,0:T(8,128)(2,1)S(1)}, bf16[128,768]{1,0:T(8,128)(2,1)S(1)}, u32[]{:S(2)}, u32[]{:S(2)}) collective-permute-start(bf16[128,768]{1,0:T(8,128)(2,1)S(1)} %add_convert_fusion.3), channel_id=1, source_target_pairs={{0,2},{1,3},{2,0},{3,1},{4,6},{5,7},{6,4},{7,5},{8,10},{9,11},{10,... | collective-permute-start | bytes 589832 | tf_op jit(solution)/shard_map/ppermute | solution.py:249
  42.4 0.5 collective-permute-start.8
  43.0 1.7 %attend.3.refs_0_ = bf16[256,512]{1,0:T(8,128)(2,1)S(1)} custom-call(bf16[256,512]{1,0:T(8,128)(2,1)S(1)} %get-tuple-element.106.refs_0_, bf16[256,512]{1,0:T(8,128)(2,1)S(1)} %get-tuple-element.83.refs_1_, bf16[256,512]{1,0:T(8,128)(2,1)S(1)} %get-tuple-element.84.refs_2_, bf16[256,512]{1,0:T(8,128)(2,1)S(1)} %get-tuple-element.85.refs_3_, ...), custom_call_target="tpu_custom_call" | custom-call | flops 805306368 | tf_op jit(solution)/shard_map/attend/pallas_call | solution.py:179
  44.7 4.0 %collective-permute-done.7 = bf16[128,768]{1,0:T(8,128)(2,1)S(1)} collective-permute-done((bf16[128,768]{1,0:T(8,128)(2,1)S(1)}, bf16[128,768]{1,0:T(8,128)(2,1)S(1)}, u32[]{:S(2)}, u32[]{:S(2)}) %collective-permute-start.7) | collective-permute-done | bytes 196640 | tf_op jit(solution)/shard_map/ppermute | solution.py:249
  48.7 3.7 %collective-permute-done.8 = bf16[128,768]{1,0:T(8,128)(2,1)S(1)} collective-permute-done((bf16[128,768]{1,0:T(8,128)(2,1)S(1)}, bf16[128,768]{1,0:T(8,128)(2,1)S(1)}, u32[]{:S(2)}, u32[]{:S(2)}) %collective-permute-start.8) | collective-permute-done | bytes 196640 | tf_op jit(solution)/shard_map/ppermute | solution.py:249
  52.3 3.4 %project_out.9 = (f32[128,3072]{1,0:T(8,128)S(1)}, bf16[128,3072]{1,0:T(8,128)(2,1)S(1)}) custom-call(bf16[256,512]{1,0:T(8,128)(2,1)S(1)} %attend.3.refs_0_, bf16[256,1536]{1,0:T(8,128)(2,1)S(1)} %get-tuple-element.110.refs_1_, bf16[512,3072]{1,0:T(8,128)(2,1)S(1)} %copy-done, bf16[1536,3072]{1,0:T(8,128)(2,1)S(1)} %bitcast.5), custom_call_target="tpu_custom_call" | custom-call | flops 3221225472 | tf_op jit(solution)/shard_map/project_out/pallas_call | solution.py:207
  55.8 0.1 collective-permute-start.9
  55.9 2.3 %collective-permute-done.9 = bf16[128,3072]{1,0:T(8,128)(2,1)} collective-permute-done((bf16[128,3072]{1,0:T(8,128)(2,1)S(1)}, bf16[128,3072]{1,0:T(8,128)(2,1)}, u32[]{:S(2)}, u32[]{:S(2)}) %collective-permute-start.9) | collective-permute-done | bytes 786464 | tf_op jit(solution)/shard_map/ppermute | solution.py:246
  58.3 1.3 %convert_add_fusion = f32[128,3072]{1,0:T(8,128)S(1)} fusion(f32[128,3072]{1,0:T(8,128)S(1)} %get-tuple-element.111, bf16[128,3072]{1,0:T(8,128)(2,1)} %collective-permute-done.9), kind=kLoop, calls=%fused_computation.1 | loop fusion | flops 786432 | bytes 3932160 | tf_op jit(solution)/shard_map/add | solution.py:305
  59.7 1.5 %collective-permute-start.10 = (bf16[64,768]{1,0:T(8,128)(2,1)S(1)}, bf16[64,768]{1,0:T(8,128)(2,1)S(1)}, u32[]{:S(2)}, u32[]{:S(2)}) collective-permute-start(bf16[64,768]{1,0:T(8,128)(2,1)S(1)} %dynamic-slice_convert_fusion.3), channel_id=1, source_target_pairs={{0,4},{4,0},{8,12},{12,8},{16,20},{20,16},{24,28},{28,24},{1,5},{5... | collective-permute-start | bytes 294920 | tf_op jit(solution)/shard_map/ppermute | solution.py:252
  61.2 1.5 %collective-permute-start.13 = (bf16[128,768]{1,0:T(8,128)(2,1)S(1)}, bf16[128,768]{1,0:T(8,128)(2,1)S(1)}, u32[]{:S(2)}, u32[]{:S(2)}) collective-permute-start(bf16[128,768]{1,0:T(8,128)(2,1)S(1)} %add_convert_fusion.1), channel_id=1, source_target_pairs={{0,2},{1,3},{2,0},{3,1},{4,6},{5,7},{6,4},{7,5},{8,10},{9,11},{10,... | collective-permute-start | bytes 589832 | tf_op jit(solution)/shard_map/ppermute | solution.py:249
  62.8 0.5 collective-permute-start.16
  63.3 1.3 %collective-permute-done.10 = bf16[64,768]{1,0:T(8,128)(2,1)S(1)} collective-permute-done((bf16[64,768]{1,0:T(8,128)(2,1)S(1)}, bf16[64,768]{1,0:T(8,128)(2,1)S(1)}, u32[]{:S(2)}, u32[]{:S(2)}) %collective-permute-start.10) | collective-permute-done | bytes 98336 | tf_op jit(solution)/shard_map/ppermute | solution.py:252
  64.6 0.7 collective-permute-start.11
  65.4 1.5 %collective-permute-start.14 = (bf16[64,768]{1,0:T(8,128)(2,1)S(1)}, bf16[64,768]{1,0:T(8,128)(2,1)S(1)}, u32[]{:S(2)}, u32[]{:S(2)}) collective-permute-start(bf16[64,768]{1,0:T(8,128)(2,1)S(1)} %dynamic-slice_convert_fusion.2), channel_id=1, source_target_pairs={{0,4},{4,0},{8,12},{12,8},{16,20},{20,16},{24,28},{28,24},{1,5},{5... | collective-permute-start | bytes 294920 | tf_op jit(solution)/shard_map/ppermute | solution.py:252
  67.0 0.7 collective-permute-start.12
  67.6 2.4 %collective-permute-done.14 = bf16[64,768]{1,0:T(8,128)(2,1)S(1)} collective-permute-done((bf16[64,768]{1,0:T(8,128)(2,1)S(1)}, bf16[64,768]{1,0:T(8,128)(2,1)S(1)}, u32[]{:S(2)}, u32[]{:S(2)}) %collective-permute-start.14) | collective-permute-done | bytes 98336 | tf_op jit(solution)/shard_map/ppermute | solution.py:252
  70.1 0.7 collective-permute-start.18
  70.9 1.5 %collective-permute-start.17 = (bf16[64,768]{1,0:T(8,128)(2,1)S(1)}, bf16[64,768]{1,0:T(8,128)(2,1)S(1)}, u32[]{:S(2)}, u32[]{:S(2)}) collective-permute-start(bf16[64,768]{1,0:T(8,128)(2,1)S(1)} %dynamic-slice_convert_fusion.1), channel_id=1, source_target_pairs={{0,4},{4,0},{8,12},{12,8},{16,20},{20,16},{24,28},{28,24},{1,5},{5... | collective-permute-start | bytes 294920 | tf_op jit(solution)/shard_map/ppermute | solution.py:252
  72.5 1.3 %collective-permute-start.15 = (bf16[64,768]{1,0:T(8,128)(2,1)S(1)}, bf16[64,768]{1,0:T(8,128)(2,1)S(1)}, u32[]{:S(2)}, u32[]{:S(2)}) collective-permute-start(bf16[64,768]{1,0:T(8,128)(2,1)S(1)} %add_convert_fusion.11), channel_id=1, source_target_pairs={{16,24},{20,28},{17,25},{21,29},{18,26},{22,30},{19,27},{23,31}} | collective-permute-start | bytes 294920 | tf_op jit(solution)/shard_map/ppermute | solution.py:343
  73.8 0.7 collective-permute-start.22
  74.5 1.1 collective-permute-done.17
  75.6 0.7 collective-permute-start.21
  76.3 1.5 %collective-permute-start.20 = (bf16[64,768]{1,0:T(8,128)(2,1)S(1)}, bf16[64,768]{1,0:T(8,128)(2,1)S(1)}, u32[]{:S(2)}, u32[]{:S(2)}) collective-permute-start(bf16[64,768]{1,0:T(8,128)(2,1)S(1)} %dynamic-slice_convert_fusion), channel_id=1, source_target_pairs={{0,4},{4,0},{8,12},{12,8},{16,20},{20,16},{24,28},{28,24},{1,5},{5... | collective-permute-start | bytes 294920 | tf_op jit(solution)/shard_map/ppermute | solution.py:252
  77.9 2.0 %collective-permute-done.15 = bf16[64,768]{1,0:T(8,128)(2,1)S(1)} collective-permute-done((bf16[64,768]{1,0:T(8,128)(2,1)S(1)}, bf16[64,768]{1,0:T(8,128)(2,1)S(1)}, u32[]{:S(2)}, u32[]{:S(2)}) %collective-permute-start.15) | collective-permute-done | bytes 98336 | tf_op jit(solution)/shard_map/ppermute | solution.py:343
  79.9 1.5 %collective-permute-start.19 = (bf16[64,768]{1,0:T(8,128)(2,1)S(1)}, bf16[64,768]{1,0:T(8,128)(2,1)S(1)}, u32[]{:S(2)}, u32[]{:S(2)}) collective-permute-start(bf16[64,768]{1,0:T(8,128)(2,1)S(1)} %add_convert_fusion.10), channel_id=1, source_target_pairs={{0,4},{4,0},{8,12},{12,8},{16,20},{20,16},{24,28},{28,24},{1,5},{5... | collective-permute-start | bytes 294920 | tf_op jit(solution)/shard_map/ppermute | solution.py:252
  81.5 1.3 %collective-permute-start.23 = (bf16[64,768]{1,0:T(8,128)(2,1)S(1)}, bf16[64,768]{1,0:T(8,128)(2,1)S(1)}, u32[]{:S(2)}, u32[]{:S(2)}) collective-permute-start(bf16[64,768]{1,0:T(8,128)(2,1)S(1)} %add_convert_fusion.9), channel_id=1, source_target_pairs={{16,24},{20,28},{17,25},{21,29},{18,26},{22,30},{19,27},{23,31}} | collective-permute-start | bytes 294920 | tf_op jit(solution)/shard_map/ppermute | solution.py:343
  82.9 0.7 collective-permute-start.26
  83.6 0.7 collective-permute-start.25
  84.2 3.8 %collective-permute-done.23 = bf16[64,768]{1,0:T(8,128)(2,1)S(1)} collective-permute-done((bf16[64,768]{1,0:T(8,128)(2,1)S(1)}, bf16[64,768]{1,0:T(8,128)(2,1)S(1)}, u32[]{:S(2)}, u32[]{:S(2)}) %collective-permute-start.23) | collective-permute-done | bytes 98336 | tf_op jit(solution)/shard_map/ppermute | solution.py:343
  88.1 1.3 %collective-permute-start.24 = (bf16[64,768]{1,0:T(8,128)(2,1)S(1)}, bf16[64,768]{1,0:T(8,128)(2,1)S(1)}, u32[]{:S(2)}, u32[]{:S(2)}) collective-permute-start(bf16[64,768]{1,0:T(8,128)(2,1)S(1)} %add_convert_fusion.8), channel_id=1, source_target_pairs={{0,4},{4,0},{8,12},{12,8},{16,20},{20,16},{24,28},{28,24},{1,5},{5... | collective-permute-start | bytes 294920 | tf_op jit(solution)/shard_map/ppermute | solution.py:252
  89.4 1.3 %collective-permute-start.27 = (bf16[64,768]{1,0:T(8,128)(2,1)S(1)}, bf16[64,768]{1,0:T(8,128)(2,1)S(1)}, u32[]{:S(2)}, u32[]{:S(2)}) collective-permute-start(bf16[64,768]{1,0:T(8,128)(2,1)S(1)} %add_convert_fusion.7), channel_id=1, source_target_pairs={{16,24},{20,28},{17,25},{21,29},{18,26},{22,30},{19,27},{23,31}} | collective-permute-start | bytes 294920 | tf_op jit(solution)/shard_map/ppermute | solution.py:343
  90.8 0.7 collective-permute-start.29
  91.5 0.1 fusion.13
  91.6 4.3 %collective-permute-done.27 = bf16[64,768]{1,0:T(8,128)(2,1)S(1)} collective-permute-done((bf16[64,768]{1,0:T(8,128)(2,1)S(1)}, bf16[64,768]{1,0:T(8,128)(2,1)S(1)}, u32[]{:S(2)}, u32[]{:S(2)}) %collective-permute-start.27) | collective-permute-done | bytes 98336 | tf_op jit(solution)/shard_map/ppermute | solution.py:343
  96.0 1.3 %collective-permute-start.28 = (bf16[64,768]{1,0:T(8,128)(2,1)S(1)}, bf16[64,768]{1,0:T(8,128)(2,1)S(1)}, u32[]{:S(2)}, u32[]{:S(2)}) collective-permute-start(bf16[64,768]{1,0:T(8,128)(2,1)S(1)} %add_convert_fusion.6), channel_id=1, source_target_pairs={{0,4},{4,0},{8,12},{12,8},{16,20},{20,16},{24,28},{28,24},{1,5},{5... | collective-permute-start | bytes 294920 | tf_op jit(solution)/shard_map/ppermute | solution.py:252
  97.3 1.3 %collective-permute-start.30 = (bf16[64,768]{1,0:T(8,128)(2,1)S(1)}, bf16[64,768]{1,0:T(8,128)(2,1)S(1)}, u32[]{:S(2)}, u32[]{:S(2)}) collective-permute-start(bf16[64,768]{1,0:T(8,128)(2,1)S(1)} %add_convert_fusion.5), channel_id=1, source_target_pairs={{16,24},{20,28},{17,25},{21,29},{18,26},{22,30},{19,27},{23,31}} | collective-permute-start | bytes 294920 | tf_op jit(solution)/shard_map/ppermute | solution.py:343
  98.7 0.1 fusion.15
  98.8 2.9 %collective-permute-done.28 = bf16[64,768]{1,0:T(8,128)(2,1)S(1)} collective-permute-done((bf16[64,768]{1,0:T(8,128)(2,1)S(1)}, bf16[64,768]{1,0:T(8,128)(2,1)S(1)}, u32[]{:S(2)}, u32[]{:S(2)}) %collective-permute-start.28) | collective-permute-done | bytes 98336 | tf_op jit(solution)/shard_map/ppermute | solution.py:252
  101.7 0.1 fusion.17
  101.8 2.0 %collective-permute-done.30 = bf16[64,768]{1,0:T(8,128)(2,1)S(1)} collective-permute-done((bf16[64,768]{1,0:T(8,128)(2,1)S(1)}, bf16[64,768]{1,0:T(8,128)(2,1)S(1)}, u32[]{:S(2)}, u32[]{:S(2)}) %collective-permute-start.30) | collective-permute-done | bytes 98336 | tf_op jit(solution)/shard_map/ppermute | solution.py:343
  103.9 1.3 %collective-permute-start.31 = (bf16[64,768]{1,0:T(8,128)(2,1)S(1)}, bf16[64,768]{1,0:T(8,128)(2,1)S(1)}, u32[]{:S(2)}, u32[]{:S(2)}) collective-permute-start(bf16[64,768]{1,0:T(8,128)(2,1)S(1)} %add_convert_fusion.4), channel_id=1, source_target_pairs={{0,4},{4,0},{8,12},{12,8},{16,20},{20,16},{24,28},{28,24},{1,5},{5... | collective-permute-start | bytes 294920 | tf_op jit(solution)/shard_map/ppermute | solution.py:252
  105.3 3.3 %collective-permute-done.31 = bf16[64,768]{1,0:T(8,128)(2,1)S(1)} collective-permute-done((bf16[64,768]{1,0:T(8,128)(2,1)S(1)}, bf16[64,768]{1,0:T(8,128)(2,1)S(1)}, u32[]{:S(2)}, u32[]{:S(2)}) %collective-permute-start.31) | collective-permute-done | bytes 98336 | tf_op jit(solution)/shard_map/ppermute | solution.py:252
  108.6 0.1 fusion.19
  108.7 0.2 maximum_add_fusion
  109.0 1.3 %maximum_bitcast_fusion = f32[1,128,3072]{2,1,0:T(8,128)} fusion(f32[128,768]{1,0:T(8,128)S(1)} %get-tuple-element.151, f32[128,768]{1,0:T(8,128)S(1)} %get-tuple-element.152, f32[128,768]{1,0:T(8,128)S(1)} %get-tuple-element.150, f32[128,768]{1,0:T(8,128)S(1)} %get-tuple-element.149), kind=kLoop, calls=%fused_computation | loop fusion | flops 1179648 | bytes 3145728 | tf_op jit(solution)/shard_map/broadcast_in_dim | solution.py:370
  (77 shorter events, 1.4 us)
Async XLA Ops:
  0.7 6.6 %copy-start.2 = (f32[128]{0:T(128)S(1)}, f32[128]{0:T(128)}, u32[]{:S(2)}) copy-start(f32[128]{0:T(128)} %param.16) | copy-start | bytes 1540
  0.7 6.6 %copy-start.3 = (f32[128]{0:T(128)S(1)}, f32[128]{0:T(128)}, u32[]{:S(2)}) copy-start(f32[128]{0:T(128)} %param.17) | copy-start | bytes 1540
  4.7 2.6 %collective-permute-start = (bf16[128,3072]{1,0:T(8,128)(2,1)}, bf16[128,3072]{1,0:T(8,128)(2,1)S(1)}, u32[]{:S(2)}, u32[]{:S(2)}) collective-permute-start(bf16[128,3072]{1,0:T(8,128)(2,1)} %get-tuple-element.72.m0), channel_id=1, source_target_pairs={{0,1},{1,0},{2,3},{3,2},{4,5},{5,4},{6,7},{7,6},{8,9},{9,8},{10,11... | collective-permute-start | bytes 2359304 | tf_op jit(solution)/shard_map/ppermute | solution.py:246
  4.8 20.2 %collective-permute-start.1 = (bf16[128,3072]{1,0:T(8,128)(2,1)}, bf16[128,3072]{1,0:T(8,128)(2,1)S(1)}, u32[]{:S(2)}, u32[]{:S(2)}) collective-permute-start(bf16[128,3072]{1,0:T(8,128)(2,1)} %get-tuple-element.72.m0), channel_id=1, source_target_pairs={{0,2},{1,3},{2,0},{3,1},{4,6},{5,7},{6,4},{7,5},{8,10},{9,11},{10,... | collective-permute-start | bytes 2359304 | tf_op jit(solution)/shard_map/ppermute | solution.py:249
  7.2 1.1 %copy-start.1 = (bf16[128,3072]{1,0:T(8,128)(2,1)S(1)}, bf16[128,3072]{1,0:T(8,128)(2,1)}, u32[]{:S(2)}) copy-start(bf16[128,3072]{1,0:T(8,128)(2,1)} %get-tuple-element.72.m0) | copy-start | bytes 2359300
  24.9 2.3 %collective-permute-start.2 = (bf16[128,3072]{1,0:T(8,128)(2,1)S(1)}, bf16[128,3072]{1,0:T(8,128)(2,1)S(1)}, u32[]{:S(2)}, u32[]{:S(2)}) collective-permute-start(bf16[128,3072]{1,0:T(8,128)(2,1)S(1)} %collective-permute-done.1.m0), channel_id=1, source_target_pairs={{0,1},{1,0},{2,3},{3,2},{4,5},{5,4},{6,7},{7,6},{8,9},{9,8},{10,11... | collective-permute-start | bytes 2359304 | tf_op jit(solution)/shard_map/ppermute | solution.py:246
  27.2 7.0 %slice-start = ((s8[9437184]{0:T(1024)(128)(4,1)}), s8[4194304]{0:T(1024)(128)(4,1)S(1)}, s32[]{:S(2)}) async-start(s8[9437184]{0:T(1024)(128)(4,1)} %bitcast.4), calls=%async_computation | async-start | bytes 8388608
  27.2 7.0 %slice-start.1 = ((s8[9437184]{0:T(1024)(128)(4,1)}), s8[4194304]{0:T(1024)(128)(4,1)S(1)}, s32[]{:S(2)}) async-start(s8[9437184]{0:T(1024)(128)(4,1)} %bitcast.4), calls=%async_computation.1 | async-start | bytes 8388608
  27.2 7.0 %slice-start.2 = ((s8[9437184]{0:T(1024)(128)(4,1)}), s8[1048576]{0:T(1024)(128)(4,1)S(1)}, s32[]{:S(2)}) async-start(s8[9437184]{0:T(1024)(128)(4,1)} %bitcast.4), calls=%async_computation.2 | async-start | bytes 2097152
  27.2 7.0 %copy-start = (bf16[512,3072]{1,0:T(8,128)(2,1)S(1)}, bf16[512,3072]{1,0:T(8,128)(2,1)}, u32[]{:S(2)}) copy-start(bf16[512,3072]{1,0:T(8,128)(2,1)} %refs_2_.9) | copy-start | bytes 9437188
  35.2 1.6 %collective-permute-start.3 = (bf16[128,768]{1,0:T(8,128)(2,1)S(1)}, bf16[128,768]{1,0:T(8,128)(2,1)S(1)}, u32[]{:S(2)}, u32[]{:S(2)}) collective-permute-start(bf16[128,768]{1,0:T(8,128)(2,1)S(1)} %get-tuple-element.89), channel_id=1, source_target_pairs={{0,1},{1,0},{2,3},{3,2},{4,5},{5,4},{6,7},{7,6},{8,9},{9,8},{10,11... | collective-permute-start | bytes 589832 | tf_op jit(solution)/shard_map/ppermute | solution.py:246
  36.4 1.9 %collective-permute-start.4 = (bf16[128,768]{1,0:T(8,128)(2,1)S(1)}, bf16[128,768]{1,0:T(8,128)(2,1)S(1)}, u32[]{:S(2)}, u32[]{:S(2)}) collective-permute-start(bf16[128,768]{1,0:T(8,128)(2,1)S(1)} %get-tuple-element.95), channel_id=1, source_target_pairs={{0,1},{1,0},{2,3},{3,2},{4,5},{5,4},{6,7},{7,6},{8,9},{9,8},{10,11... | collective-permute-start | bytes 589832 | tf_op jit(solution)/shard_map/ppermute | solution.py:246
  38.1 1.7 %collective-permute-start.5 = (bf16[128,768]{1,0:T(8,128)(2,1)S(1)}, bf16[128,768]{1,0:T(8,128)(2,1)S(1)}, u32[]{:S(2)}, u32[]{:S(2)}) collective-permute-start(bf16[128,768]{1,0:T(8,128)(2,1)S(1)} %get-tuple-element.101), channel_id=1, source_target_pairs={{0,1},{1,0},{2,3},{3,2},{4,5},{5,4},{6,7},{7,6},{8,9},{9,8},{10,11... | collective-permute-start | bytes 589832 | tf_op jit(solution)/shard_map/ppermute | solution.py:246
  39.3 1.5 %collective-permute-start.6 = (bf16[128,768]{1,0:T(8,128)(2,1)S(1)}, bf16[128,768]{1,0:T(8,128)(2,1)S(1)}, u32[]{:S(2)}, u32[]{:S(2)}) collective-permute-start(bf16[128,768]{1,0:T(8,128)(2,1)S(1)} %get-tuple-element.105), channel_id=1, source_target_pairs={{0,1},{1,0},{2,3},{3,2},{4,5},{5,4},{6,7},{7,6},{8,9},{9,8},{10,11... | collective-permute-start | bytes 589832 | tf_op jit(solution)/shard_map/ppermute | solution.py:246
  40.9 7.8 %collective-permute-start.7 = (bf16[128,768]{1,0:T(8,128)(2,1)S(1)}, bf16[128,768]{1,0:T(8,128)(2,1)S(1)}, u32[]{:S(2)}, u32[]{:S(2)}) collective-permute-start(bf16[128,768]{1,0:T(8,128)(2,1)S(1)} %add_convert_fusion.3), channel_id=1, source_target_pairs={{0,2},{1,3},{2,0},{3,1},{4,6},{5,7},{6,4},{7,5},{8,10},{9,11},{10,... | collective-permute-start | bytes 589832 | tf_op jit(solution)/shard_map/ppermute | solution.py:249
  42.4 9.9 %collective-permute-start.8 = (bf16[128,768]{1,0:T(8,128)(2,1)S(1)}, bf16[128,768]{1,0:T(8,128)(2,1)S(1)}, u32[]{:S(2)}, u32[]{:S(2)}) collective-permute-start(bf16[128,768]{1,0:T(8,128)(2,1)S(1)} %add_convert_fusion.2), channel_id=1, source_target_pairs={{0,2},{1,3},{2,0},{3,1},{4,6},{5,7},{6,4},{7,5},{8,10},{9,11},{10,... | collective-permute-start | bytes 589832 | tf_op jit(solution)/shard_map/ppermute | solution.py:249
  44.7 11.2 %copy-start.9 = (f32[1,3072]{1,0:T(1,128)S(1)}, f32[1,3072]{1,0:T(1,128)}, u32[]{:S(2)}) copy-start(f32[1,3072]{1,0:T(1,128)} %get-tuple-element.71) | copy-start | bytes 36868
  48.7 7.1 %copy-start.7 = (bf16[128,768]{1,0:T(8,128)(2,1)}, bf16[128,768]{1,0:T(8,128)(2,1)S(1)}, u32[]{:S(2)}) copy-start(bf16[128,768]{1,0:T(8,128)(2,1)S(1)} %collective-permute-done.7) | copy-start | bytes 589828
  52.3 3.4 %copy-start.5 = (bf16[128,768]{1,0:T(8,128)(2,1)}, bf16[128,768]{1,0:T(8,128)(2,1)S(1)}, u32[]{:S(2)}) copy-start(bf16[128,768]{1,0:T(8,128)(2,1)S(1)} %collective-permute-done.8) | copy-start | bytes 589828
  55.8 2.5 %collective-permute-start.9 = (bf16[128,3072]{1,0:T(8,128)(2,1)S(1)}, bf16[128,3072]{1,0:T(8,128)(2,1)}, u32[]{:S(2)}, u32[]{:S(2)}) collective-permute-start(bf16[128,3072]{1,0:T(8,128)(2,1)S(1)} %get-tuple-element.112), channel_id=1, source_target_pairs={{0,1},{1,0},{2,3},{3,2},{4,5},{5,4},{6,7},{7,6},{8,9},{9,8},{10,11... | collective-permute-start | bytes 2359304 | tf_op jit(solution)/shard_map/ppermute | solution.py:246
  58.3 1.4 %copy-start.8 = (bf16[128,768]{1,0:T(8,128)(2,1)S(1)}, bf16[128,768]{1,0:T(8,128)(2,1)}, u32[]{:S(2)}) copy-start(bf16[128,768]{1,0:T(8,128)(2,1)} %copy-done.7) | copy-start | bytes 589828
  59.6 5.7 %copy-start.6 = (bf16[128,768]{1,0:T(8,128)(2,1)S(1)}, bf16[128,768]{1,0:T(8,128)(2,1)}, u32[]{:S(2)}) copy-start(bf16[128,768]{1,0:T(8,128)(2,1)} %copy-done.5) | copy-start | bytes 589828
  59.7 4.9 %collective-permute-start.10 = (bf16[64,768]{1,0:T(8,128)(2,1)S(1)}, bf16[64,768]{1,0:T(8,128)(2,1)S(1)}, u32[]{:S(2)}, u32[]{:S(2)}) collective-permute-start(bf16[64,768]{1,0:T(8,128)(2,1)S(1)} %dynamic-slice_convert_fusion.3), channel_id=1, source_target_pairs={{0,4},{4,0},{8,12},{12,8},{16,20},{20,16},{24,28},{28,24},{1,5},{5... | collective-permute-start | bytes 294920 | tf_op jit(solution)/shard_map/ppermute | solution.py:252
  61.2 9.5 %collective-permute-start.13 = (bf16[128,768]{1,0:T(8,128)(2,1)S(1)}, bf16[128,768]{1,0:T(8,128)(2,1)S(1)}, u32[]{:S(2)}, u32[]{:S(2)}) collective-permute-start(bf16[128,768]{1,0:T(8,128)(2,1)S(1)} %add_convert_fusion.1), channel_id=1, source_target_pairs={{0,2},{1,3},{2,0},{3,1},{4,6},{5,7},{6,4},{7,5},{8,10},{9,11},{10,... | collective-permute-start | bytes 589832 | tf_op jit(solution)/shard_map/ppermute | solution.py:249
  62.8 13.5 %collective-permute-start.16 = (bf16[128,768]{1,0:T(8,128)(2,1)S(1)}, bf16[128,768]{1,0:T(8,128)(2,1)S(1)}, u32[]{:S(2)}, u32[]{:S(2)}) collective-permute-start(bf16[128,768]{1,0:T(8,128)(2,1)S(1)} %add_convert_fusion), channel_id=1, source_target_pairs={{0,2},{1,3},{2,0},{3,1},{4,6},{5,7},{6,4},{7,5},{8,10},{9,11},{10,... | collective-permute-start | bytes 589832 | tf_op jit(solution)/shard_map/ppermute | solution.py:249
  64.6 2.3 %collective-permute-start.11 = (bf16[64,768]{1,0:T(8,128)(2,1)S(1)}, bf16[64,768]{1,0:T(8,128)(2,1)S(1)}, u32[]{:S(2)}, u32[]{:S(2)}) collective-permute-start(bf16[64,768]{1,0:T(8,128)(2,1)S(1)} %fusion.20), channel_id=1, source_target_pairs={{0,8},{4,12},{1,9},{5,13},{2,10},{6,14},{3,11},{7,15}} | collective-permute-start | bytes 294920 | tf_op jit(solution)/shard_map/ppermute | solution.py:343
  65.4 4.7 %collective-permute-start.14 = (bf16[64,768]{1,0:T(8,128)(2,1)S(1)}, bf16[64,768]{1,0:T(8,128)(2,1)S(1)}, u32[]{:S(2)}, u32[]{:S(2)}) collective-permute-start(bf16[64,768]{1,0:T(8,128)(2,1)S(1)} %dynamic-slice_convert_fusion.2), channel_id=1, source_target_pairs={{0,4},{4,0},{8,12},{12,8},{16,20},{20,16},{24,28},{28,24},{1,5},{5... | collective-permute-start | bytes 294920 | tf_op jit(solution)/shard_map/ppermute | solution.py:252
  67.0 5.4 %collective-permute-start.12 = (bf16[64,768]{1,0:T(8,128)(2,1)S(1)}, bf16[64,768]{1,0:T(8,128)(2,1)S(1)}, u32[]{:S(2)}, u32[]{:S(2)}) collective-permute-start(bf16[64,768]{1,0:T(8,128)(2,1)S(1)} %fusion.5), channel_id=1, source_target_pairs={{8,16},{12,20},{9,17},{13,21},{10,18},{14,22},{11,19},{15,23}} | collective-permute-start | bytes 294920 | tf_op jit(solution)/shard_map/ppermute | solution.py:343
  70.1 3.7 %collective-permute-start.18 = (bf16[64,768]{1,0:T(8,128)(2,1)S(1)}, bf16[64,768]{1,0:T(8,128)(2,1)S(1)}, u32[]{:S(2)}, u32[]{:S(2)}) collective-permute-start(bf16[64,768]{1,0:T(8,128)(2,1)S(1)} %fusion.21), channel_id=1, source_target_pairs={{0,8},{4,12},{1,9},{5,13},{2,10},{6,14},{3,11},{7,15}} | collective-permute-start | bytes 294920 | tf_op jit(solution)/shard_map/ppermute | solution.py:343
  70.9 4.7 %collective-permute-start.17 = (bf16[64,768]{1,0:T(8,128)(2,1)S(1)}, bf16[64,768]{1,0:T(8,128)(2,1)S(1)}, u32[]{:S(2)}, u32[]{:S(2)}) collective-permute-start(bf16[64,768]{1,0:T(8,128)(2,1)S(1)} %dynamic-slice_convert_fusion.1), channel_id=1, source_target_pairs={{0,4},{4,0},{8,12},{12,8},{16,20},{20,16},{24,28},{28,24},{1,5},{5... | collective-permute-start | bytes 294920 | tf_op jit(solution)/shard_map/ppermute | solution.py:252
  72.5 7.4 %collective-permute-start.15 = (bf16[64,768]{1,0:T(8,128)(2,1)S(1)}, bf16[64,768]{1,0:T(8,128)(2,1)S(1)}, u32[]{:S(2)}, u32[]{:S(2)}) collective-permute-start(bf16[64,768]{1,0:T(8,128)(2,1)S(1)} %add_convert_fusion.11), channel_id=1, source_target_pairs={{16,24},{20,28},{17,25},{21,29},{18,26},{22,30},{19,27},{23,31}} | collective-permute-start | bytes 294920 | tf_op jit(solution)/shard_map/ppermute | solution.py:343
  73.8 7.6 %collective-permute-start.22 = (bf16[64,768]{1,0:T(8,128)(2,1)S(1)}, bf16[64,768]{1,0:T(8,128)(2,1)S(1)}, u32[]{:S(2)}, u32[]{:S(2)}) collective-permute-start(bf16[64,768]{1,0:T(8,128)(2,1)S(1)} %fusion.7), channel_id=1, source_target_pairs={{8,16},{12,20},{9,17},{13,21},{10,18},{14,22},{11,19},{15,23}} | collective-permute-start | bytes 294920 | tf_op jit(solution)/shard_map/ppermute | solution.py:343
  75.6 7.2 %collective-permute-start.21 = (bf16[64,768]{1,0:T(8,128)(2,1)S(1)}, bf16[64,768]{1,0:T(8,128)(2,1)S(1)}, u32[]{:S(2)}, u32[]{:S(2)}) collective-permute-start(bf16[64,768]{1,0:T(8,128)(2,1)S(1)} %fusion.22), channel_id=1, source_target_pairs={{0,8},{4,12},{1,9},{5,13},{2,10},{6,14},{3,11},{7,15}} | collective-permute-start | bytes 294920 | tf_op jit(solution)/shard_map/ppermute | solution.py:343
  76.3 7.2 %collective-permute-start.20 = (bf16[64,768]{1,0:T(8,128)(2,1)S(1)}, bf16[64,768]{1,0:T(8,128)(2,1)S(1)}, u32[]{:S(2)}, u32[]{:S(2)}) collective-permute-start(bf16[64,768]{1,0:T(8,128)(2,1)S(1)} %dynamic-slice_convert_fusion), channel_id=1, source_target_pairs={{0,4},{4,0},{8,12},{12,8},{16,20},{20,16},{24,28},{28,24},{1,5},{5... | collective-permute-start | bytes 294920 | tf_op jit(solution)/shard_map/ppermute | solution.py:252
  79.9 11.6 %collective-permute-start.19 = (bf16[64,768]{1,0:T(8,128)(2,1)S(1)}, bf16[64,768]{1,0:T(8,128)(2,1)S(1)}, u32[]{:S(2)}, u32[]{:S(2)}) collective-permute-start(bf16[64,768]{1,0:T(8,128)(2,1)S(1)} %add_convert_fusion.10), channel_id=1, source_target_pairs={{0,4},{4,0},{8,12},{12,8},{16,20},{20,16},{24,28},{28,24},{1,5},{5... | collective-permute-start | bytes 294920 | tf_op jit(solution)/shard_map/ppermute | solution.py:252
  81.5 6.5 %collective-permute-start.23 = (bf16[64,768]{1,0:T(8,128)(2,1)S(1)}, bf16[64,768]{1,0:T(8,128)(2,1)S(1)}, u32[]{:S(2)}, u32[]{:S(2)}) collective-permute-start(bf16[64,768]{1,0:T(8,128)(2,1)S(1)} %add_convert_fusion.9), channel_id=1, source_target_pairs={{16,24},{20,28},{17,25},{21,29},{18,26},{22,30},{19,27},{23,31}} | collective-permute-start | bytes 294920 | tf_op jit(solution)/shard_map/ppermute | solution.py:343
  82.9 6.5 %collective-permute-start.26 = (bf16[64,768]{1,0:T(8,128)(2,1)S(1)}, bf16[64,768]{1,0:T(8,128)(2,1)S(1)}, u32[]{:S(2)}, u32[]{:S(2)}) collective-permute-start(bf16[64,768]{1,0:T(8,128)(2,1)S(1)} %fusion.9), channel_id=1, source_target_pairs={{8,16},{12,20},{9,17},{13,21},{10,18},{14,22},{11,19},{15,23}} | collective-permute-start | bytes 294920 | tf_op jit(solution)/shard_map/ppermute | solution.py:343
  83.6 7.2 %collective-permute-start.25 = (bf16[64,768]{1,0:T(8,128)(2,1)S(1)}, bf16[64,768]{1,0:T(8,128)(2,1)S(1)}, u32[]{:S(2)}, u32[]{:S(2)}) collective-permute-start(bf16[64,768]{1,0:T(8,128)(2,1)S(1)} %fusion.23), channel_id=1, source_target_pairs={{0,8},{4,12},{1,9},{5,13},{2,10},{6,14},{3,11},{7,15}} | collective-permute-start | bytes 294920 | tf_op jit(solution)/shard_map/ppermute | solution.py:343
  88.1 10.6 %collective-permute-start.24 = (bf16[64,768]{1,0:T(8,128)(2,1)S(1)}, bf16[64,768]{1,0:T(8,128)(2,1)S(1)}, u32[]{:S(2)}, u32[]{:S(2)}) collective-permute-start(bf16[64,768]{1,0:T(8,128)(2,1)S(1)} %add_convert_fusion.8), channel_id=1, source_target_pairs={{0,4},{4,0},{8,12},{12,8},{16,20},{20,16},{24,28},{28,24},{1,5},{5... | collective-permute-start | bytes 294920 | tf_op jit(solution)/shard_map/ppermute | solution.py:252
  89.4 6.5 %collective-permute-start.27 = (bf16[64,768]{1,0:T(8,128)(2,1)S(1)}, bf16[64,768]{1,0:T(8,128)(2,1)S(1)}, u32[]{:S(2)}, u32[]{:S(2)}) collective-permute-start(bf16[64,768]{1,0:T(8,128)(2,1)S(1)} %add_convert_fusion.7), channel_id=1, source_target_pairs={{16,24},{20,28},{17,25},{21,29},{18,26},{22,30},{19,27},{23,31}} | collective-permute-start | bytes 294920 | tf_op jit(solution)/shard_map/ppermute | solution.py:343
  90.8 6.5 %collective-permute-start.29 = (bf16[64,768]{1,0:T(8,128)(2,1)S(1)}, bf16[64,768]{1,0:T(8,128)(2,1)S(1)}, u32[]{:S(2)}, u32[]{:S(2)}) collective-permute-start(bf16[64,768]{1,0:T(8,128)(2,1)S(1)} %fusion.11), channel_id=1, source_target_pairs={{8,16},{12,20},{9,17},{13,21},{10,18},{14,22},{11,19},{15,23}} | collective-permute-start | bytes 294920 | tf_op jit(solution)/shard_map/ppermute | solution.py:343
  96.0 5.7 %collective-permute-start.28 = (bf16[64,768]{1,0:T(8,128)(2,1)S(1)}, bf16[64,768]{1,0:T(8,128)(2,1)S(1)}, u32[]{:S(2)}, u32[]{:S(2)}) collective-permute-start(bf16[64,768]{1,0:T(8,128)(2,1)S(1)} %add_convert_fusion.6), channel_id=1, source_target_pairs={{0,4},{4,0},{8,12},{12,8},{16,20},{20,16},{24,28},{28,24},{1,5},{5... | collective-permute-start | bytes 294920 | tf_op jit(solution)/shard_map/ppermute | solution.py:252
  97.3 6.5 %collective-permute-start.30 = (bf16[64,768]{1,0:T(8,128)(2,1)S(1)}, bf16[64,768]{1,0:T(8,128)(2,1)S(1)}, u32[]{:S(2)}, u32[]{:S(2)}) collective-permute-start(bf16[64,768]{1,0:T(8,128)(2,1)S(1)} %add_convert_fusion.5), channel_id=1, source_target_pairs={{16,24},{20,28},{17,25},{21,29},{18,26},{22,30},{19,27},{23,31}} | collective-permute-start | bytes 294920 | tf_op jit(solution)/shard_map/ppermute | solution.py:343
  101.8 6.9 %copy-start.4 = (f32[128,3072]{1,0:T(8,128)S(1)}, f32[128,3072]{1,0:T(8,128)}, u32[]{:S(2)}) copy-start(f32[128,3072]{1,0:T(8,128)} %param.12) | copy-start | bytes 4718596
  103.9 4.7 %collective-permute-start.31 = (bf16[64,768]{1,0:T(8,128)(2,1)S(1)}, bf16[64,768]{1,0:T(8,128)(2,1)S(1)}, u32[]{:S(2)}, u32[]{:S(2)}) collective-permute-start(bf16[64,768]{1,0:T(8,128)(2,1)S(1)} %add_convert_fusion.4), channel_id=1, source_target_pairs={{0,4},{4,0},{8,12},{12,8},{16,20},{20,16},{24,28},{28,24},{1,5},{5... | collective-permute-start | bytes 294920 | tf_op jit(solution)/shard_map/ppermute | solution.py:252

commit v4 on v3

--- a/solution.py
+++ b/solution.py
@@ -142,7 +142,7 @@
         out_specs=[vm] * len(shapes),
         out_shape=shapes,
         scratch_shapes=scratch,
-        compiler_params=params(26 if load else 9),
+        compiler_params=params(30 if load else 9),
         cost_estimate=cost(2 * rows * width * (3 * heads + hidden), 0),
         name="project",
     )(m0, m1, q_gain, k_gain, *([w_qkv, w_mlp_in] if load else held))
@@ -188,7 +188,7 @@
 
 
 def out_kernel(first, parts, *refs):
-    xs, ws = refs[:parts], refs[parts : 2 * parts]
+    xs, ws, extra = refs[:parts], refs[parts : 2 * parts], refs[2 * parts : -2]
     keep, send = refs[-2:]
     half, count = keep.shape
     cols = slice(first, first + count)
@@ -196,26 +196,30 @@
         jnp.dot(x[...], w[:, cols], preferred_element_type=f32) for x, w in zip(xs, ws)
     ]
     y = functools.reduce(jnp.add, terms)
-    keep[...] = y[:half]
-    send[...] = y[half:].astype(bf16)
-
-
-def out_call(xs, ws, first, count):
+    low, high = y[:half], y[half:]
+    if extra:
+        low = low + extra[0][:, cols]
+        high = high + extra[1][:, cols]
+    keep[...] = low
+    send[...] = high.astype(send.dtype)
+
+
+def out_call(xs, ws, extra, first, count, kind=bf16):
     half = xs[0].shape[0] // 2
     depth = sum(x.shape[1] for x in xs)
     vm = pl.BlockSpec(memory_space=VM)
     return pl.pallas_call(
         functools.partial(out_kernel, first, len(xs)),
-        in_specs=[vm] * (2 * len(xs)),
+        in_specs=[vm] * (2 * len(xs) + len(extra)),
         out_specs=[vm, vm],
         out_shape=[
             jax.ShapeDtypeStruct((half, count), f32),
-            jax.ShapeDtypeStruct((half, count), bf16),
+            jax.ShapeDtypeStruct((half, count), kind),
         ],
         compiler_params=params(9),
         cost_estimate=cost(4 * half * count * depth, 0),
         name="project_out",
-    )(*xs, *ws)
+    )(*xs, *ws, *extra)
 
 
 def per_device(
@@ -237,9 +241,11 @@
     rows, width = x_start.shape
     chips = n_seq // 2
     groups = n_step // 2
-    chunks = 4
-    count = width // chunks
     half = rows // 2
+    unit = width // 24
+    counts = [4 * unit, 8 * unit, 8 * unit, 4 * unit]
+    chunks = len(counts)
+    firsts = [sum(counts[:c]) for c in range(chunks)]
     qg, kg = q_gain[None, :], k_gain[None, :]
 
     def to_core(x):
@@ -263,7 +269,8 @@
     q0, k0, v0, act0, *held = project_call(
         mine, to_core(mine), qg, kg, w_qkv, w_mlp_in, None
     )
-    far, act0 = tied(far, act0)
+    low0, high0 = out_call([act0], [w_out_mlp], [], 0, width, f32)
+    far, low0, high0 = tied(far, low0, high0)
     qs, ks, vs, acts = [], [k0], [v0], []
     for block in far:
         q, k, v, act = project_call(block, to_core(block), qg, kg, w_qkv, w_mlp_in, held)
@@ -273,14 +280,13 @@
         acts.append(act)
     mixed = [attend_call(q, ks, vs, head) for q in qs]
 
-    firsts = [c * count for c in range(chunks)]
     weights = [w_out_attn, w_out_mlp]
     sums = [[] for _ in offsets]
     ready = [[] for _ in offsets]
     gate = (mixed, acts)
-    for c, first in enumerate(firsts):
+    for c in range(chunks):
         for j in range(chips - 1):
-            keep, send = out_call([gate[0][j], gate[1][j]], weights, first, count)
+            keep, send = out_call([gate[0][j], gate[1][j]], weights, [], firsts[c], counts[c])
             sums[j].append((keep, to_core(send)))
         if c >= 1:
             for j in range(chips - 1):
@@ -298,74 +304,101 @@
     q0, ready = tied(q0, ready)
     got = [[to_chip(r, chips - 1 - j) for r in ready[j]] for j in range(chips - 1)]
     mixed0 = attend_call(q0, ks, vs, head)
-    early = [row[:2] for row in got]
+    early = [row[0] for row in got]
     mixed0, early = tied(mixed0, early)
-    got = [e + row[2:] for e, row in zip(early, got)]
-    keep0, send0 = out_call([mixed0, act0], weights, 0, width)
-    own = keep0 + to_core(send0).astype(f32)
-
-    def prefix_stages(c):
+    got = [[e] + row[1:] for e, row in zip(early, got)]
+    keep, send = out_call([mixed0], [w_out_attn], [low0, high0], 0, width)
+    own = keep + to_core(send).astype(f32)
+
+    def along(pairs):
+        return lambda x: lax.ppermute(x, "step", [(2 * a + i, 2 * b + i) for a, b in pairs for i in (0, 1)])
+
+    rounds = []
+    span = 1
+    while span < groups:
+        moves = []
+        for t in range(span):
+            pairs = [(b + span - 1, b + span + t) for b in range(0, groups, 2 * span)]
+            moves.append(along([p for p in pairs if p[1] < groups]))
+        rounds.append(moves)
+        span *= 2
+
+    def prefix_stages(c, split):
         first = firsts[c]
+        cols = slice(first, first + counts[c])
         held = {}
 
         def drift_of(fetched):
-            branch = own[:, first : first + count]
+            branch = own[:, cols]
             for one in fetched:
                 branch = branch + one.astype(f32)
-            drift = sg[:, first : first + count] * branch
-            held["kept"] = lax.dynamic_slice_in_dim(drift, parity * half, half, 0)
-            held["other"] = lax.dynamic_slice_in_dim(drift, (1 - parity) * half, half, 0)
-            return held["other"].astype(bf16)
+            drift = sg[:, cols] * branch
+            if split:
+                held["kept"] = lax.dynamic_slice_in_dim(drift, parity * half, half, 0)
+                held["other"] = lax.dynamic_slice_in_dim(drift, (1 - parity) * half, half, 0)
+                return held["other"].astype(bf16)
+            held["kept"] = held["total"] = drift
+            return held["total"].astype(bf16)
 
         def pair_sum(fetched):
-            held["fetched"] = fetched.astype(f32)
+            held["fetched"] = fetched[0].astype(f32)
             held["total"] = held["kept"] + held["fetched"]
-            held["earlier"] = jnp.zeros_like(held["total"])
-            if groups > 1:
-                return held["total"].astype(bf16)
-            return (even * held["kept"]).astype(bf16)
-
-        def hop(g, fetched):
-            held["earlier"] = held["earlier"] + fetched.astype(f32)
-            if g < groups - 1:
-                return (held["earlier"] + held["total"]).astype(bf16)
-            return (held["earlier"] + even * held["kept"]).astype(bf16)
+            return held["total"].astype(bf16)
+
+        def collect(final, fetched):
+            for one in fetched:
+                one = one.astype(f32)
+                held["earlier"] = held["earlier"] + one if "earlier" in held else one
+            if final:
+                return (held["earlier"] + even * held["kept"]).astype(bf16)
+            return (held["earlier"] + held["total"]).astype(bf16)
 
         def finish(fetched):
-            mine_half = held["earlier"] + held["kept"] + (1.0 - even) * held["fetched"]
-            rest = fetched.astype(f32) + held["other"]
-            low = jnp.where(parity == 0, mine_half, rest)
-            high = jnp.where(parity == 0, rest, mine_half)
-            return x_start[:, first : first + count] + jnp.concatenate([low, high], axis=0)
-
-        def along(g):
-            moves = [(2 * (g - 1) + x, 2 * g + x) for x in range(2)]
-            return lambda x: lax.ppermute(x, "step", moves)
-
-        stages = [(drift_of, to_pair)]
-        stages.append((pair_sum, along(1) if groups > 1 else to_pair))
-        for g in range(1, groups):
-            stages.append((functools.partial(hop, g), along(g + 1) if g < groups - 1 else to_pair))
+            back = fetched[0].astype(f32)
+            if split:
+                mine_half = held["earlier"] + held["kept"] + (1.0 - even) * held["fetched"]
+                rest = back + held["other"]
+                low = jnp.where(parity == 0, mine_half, rest)
+                high = jnp.where(parity == 0, rest, mine_half)
+                change = jnp.concatenate([low, high], axis=0)
+            else:
+                change = held["earlier"] + held["kept"] + back
+            return x_start[:, cols] + change
+
+        stages = [(drift_of, [to_pair] if split else rounds[0])]
+        if split:
+            stages.append((pair_sum, rounds[0]))
+        for r in range(len(rounds)):
+            final = r == len(rounds) - 1
+            stages.append((functools.partial(collect, final), [to_pair] if final else rounds[r + 1]))
         stages.append((finish, None))
         return stages
 
-    plan = [prefix_stages(c) for c in range(chunks)]
+    plan = [prefix_stages(c, c < chunks - 1) for c in range(chunks)]
     inbox = [[got[j][c] for j in range(chips - 1)] for c in range(chunks)]
-    turns = sorted(
-        (4 * c + 3 * i, i, c) for c in range(chunks) for i in range(len(plan[c]))
-    )
+    turns = []
+    arrival = 2.0
+    for c in range(chunks):
+        share = 16.0 * counts[c] / width
+        arrival += share
+        when = arrival
+        for i, (_, moves) in enumerate(plan[c]):
+            turns.append((when, c, i))
+            if moves is not None:
+                full = 1.0 if c == chunks - 1 else 0.5
+                when += 1.7 + share * full * len(moves)
     results = [None] * chunks
     last = None
-    for _, i, c in turns:
-        compute, move = plan[c][i]
+    for _, c, i in sorted(turns):
+        compute, moves = plan[c][i]
         fetched = inbox[c]
         if last is not None:
             fetched, last = tied(fetched, last)
         out = compute(fetched)
-        if move is None:
+        if moves is None:
             results[c] = out
         else:
-            inbox[c] = move(out)
+            inbox[c] = [move(out) for move in moves]
             last = out
     return jnp.concatenate(results, axis=1)[None]
 

time: 111 us -> 104 us (0.937)
  the two profiles are of different devices: /device:TPU:24 before, /device:TPU:26 now
where the time goes in v4:
time: 104 us; the launch traced here: 103 us
  waiting for transfers between devices  39 us (38%)
  Pallas kernels  29 us (28%)
  starting transfers between devices  26.2 us (25%)
  other arithmetic  6.24 us (6%)
  local copies, waits for them, and re-layouts  1.58 us (2%)
  between operations  1.17 us (1%)
    ppermute x12, waiting for transfers between devices, along(): lax.ppermute(x, 'step', [(2 * a + i, 2 * b + i) for a, b in pairs for i i...  20.7 us
    pallas_call x2, Pallas kernels, project_call(): pl.pallas_call(functools.partial(project_kernel, tile, load, tiles), in_s...  13.8 us
    ppermute x12, starting transfers between devices, along(): lax.ppermute(x, 'step', [(2 * a + i, 2 * b + i) for a, b in pairs for i i...  13 us
    pallas_call x6, Pallas kernels, out_call(): pl.pallas_call(functools.partial(out_kernel, first, len(xs)), in_specs=[v...  7.71 us
    ppermute x5, waiting for transfers between devices, to_chip(): lax.ppermute(x, 'seq', [(i, (i + 2 * offset) % n_seq) for i in range(n_se...  7.54 us
    ppermute x5, starting transfers between devices, to_chip(): lax.ppermute(x, 'seq', [(i, (i + 2 * offset) % n_seq) for i in range(n_se...  6.69 us
    ppermute x7, waiting for transfers between devices, to_pair(): return lax.ppermute(x, 'step', [(i, i ^ 1) for i in range(n_step)])  6.53 us
    ppermute x7, starting transfers between devices, to_pair(): return lax.ppermute(x, 'step', [(i, i ^ 1) for i in range(n_step)])  5.07 us
  transfers between devices with their start and end apart: 31, of which 16 were waited for; matrix products, arithmetic and copies ran while one was open for 4% of the time, Pallas kernels for 16%

profile of v4, /device:TPU:26, one launch (start us, length us, event | category | flops | bytes accessed | tf_op | source)
XLA Modules:
  0.0 103.2 jit_solution(4086997144295293779)
XLA Ops:
  0.7 4.1 %norm.1 = (bf16[128,3072]{1,0:T(8,128)(2,1)}, f32[1,3072]{1,0:T(1,128)}) custom-call(s32[1]{0:T(128)S(6)} %copy.12.t_ref, f32[1,128,3072]{2,1,0:T(8,128)} %x_hbm.1, f32[50,9216]{1,0:T(8,128)} %mod_ref.1, f32[50]{0:T(128)} %size_ref.1), custom_call_target="tpu_custom_call" | custom-call | flops 3932160 | tf_op jit(solution)/shard_map/norm/pallas_call | solution.py:51
  4.8 1.6 %collective-permute-start.1 = (bf16[128,3072]{1,0:T(8,128)(2,1)}, bf16[128,3072]{1,0:T(8,128)(2,1)S(1)}, u32[]{:S(2)}, u32[]{:S(2)}) collective-permute-start(bf16[128,3072]{1,0:T(8,128)(2,1)} %get-tuple-element.74.m0), channel_id=1, source_target_pairs={{0,2},{1,3},{2,0},{3,1},{4,6},{5,7},{6,4},{7,5},{8,10},{9,11},{10,... | collective-permute-start | bytes 2359304 | tf_op jit(solution)/shard_map/ppermute | solution.py:255
  6.4 0.9 collective-permute-done.m1
  7.3 1.1 %copy-done.1 = bf16[128,3072]{1,0:T(8,128)(2,1)S(1)} copy-done((bf16[128,3072]{1,0:T(8,128)(2,1)S(1)}, bf16[128,3072]{1,0:T(8,128)(2,1)}, u32[]{:S(2)}) %copy-start.1) | copy-done | bytes 786456
  8.5 8.6 %project.2 = (bf16[256,512]{1,0:T(8,128)(2,1)S(1)}, bf16[256,512]{1,0:T(8,128)(2,1)S(1)}, bf16[256,512]{1,0:T(8,128)(2,1)S(1)}, bf16[256,1536]{1,0:T(8,128)(2,1)...) custom-call(bf16[128,3072]{1,0:T(8,128)(2,1)S(1)} %copy-done.1, ...), custom_call_target="tpu_custom_call" | custom-call | flops 4831838208 | tf_op jit(solution)/shard_map/project/pallas_call | solution.py:139
  17.1 0.3 slice-done.2
  17.4 2.6 %project_out.6 = (f32[128,3072]{1,0:T(8,128)S(1)}, f32[128,3072]{1,0:T(8,128)S(1)}) custom-call(bf16[256,1536]{1,0:T(8,128)(2,1)S(1)} %get-tuple-element.76.refs_0_, bf16[1536,3072]{1,0:T(8,128)(2,1)S(1)} %bitcast.9), custom_call_target="tpu_custom_call" | custom-call | flops 2415919104 | tf_op jit(solution)/shard_map/project_out/pallas_call | solution.py:211
  20.0 5.0 %collective-permute-done.1.m0 = bf16[128,3072]{1,0:T(8,128)(2,1)S(1)} collective-permute-done((bf16[128,3072]{1,0:T(8,128)(2,1)}, bf16[128,3072]{1,0:T(8,128)(2,1)S(1)}, u32[]{:S(2)}, u32[]{:S(2)}) %collective-permute-start.1) | collective-permute-done | bytes 786464 | tf_op jit(solution)/shard_map/ppermute | solution.py:255
  25.0 2.3 %collective-permute-done.2.m1 = bf16[128,3072]{1,0:T(8,128)(2,1)S(1)} collective-permute-done((bf16[128,3072]{1,0:T(8,128)(2,1)S(1)}, bf16[128,3072]{1,0:T(8,128)(2,1)S(1)}, u32[]{:S(2)}, u32[]{:S(2)}) %collective-permute-start.2) | collective-permute-done | bytes 786464 | tf_op jit(solution)/shard_map/ppermute | solution.py:252
  27.3 5.2 %project.3 = (bf16[256,512]{1,0:T(8,128)(2,1)S(1)}, bf16[256,512]{1,0:T(8,128)(2,1)S(1)}, bf16[256,512]{1,0:T(8,128)(2,1)S(1)}, bf16[256,1536]{1,0:T(8,128)(2,1)S(1)}) custom-call(bf16[128,3072]{1,0:T(8,128)(2,1)S(1)} %collective-permute-done.1.m0, bf16[128,3072]{1,0:T(8,128)(2,1)S(1)} %collective-permute-done.2.m1, f32[1,128]{1,0:T(1,128)S(1)} %bitcast.11, ...), custom_call_target="tpu_custom_call" | custom-call | flops 4831838208 | tf_op jit(solution)/shard_map/project/pallas_call | solution.py:139
  32.6 1.7 %attend.2.refs_0_ = bf16[256,512]{1,0:T(8,128)(2,1)S(1)} custom-call(bf16[256,512]{1,0:T(8,128)(2,1)S(1)} %get-tuple-element.86.refs_0_, bf16[256,512]{1,0:T(8,128)(2,1)S(1)} %get-tuple-element.87.refs_1_, bf16[256,512]{1,0:T(8,128)(2,1)S(1)} %get-tuple-element.88.refs_2_, bf16[256,512]{1,0:T(8,128)(2,1)S(1)} %get-tuple-element.89.refs_3_, ...), custom_call_target="tpu_custom_call" | custom-call | flops 805306368 | tf_op jit(solution)/shard_map/attend/pallas_call | solution.py:179
  34.3 0.9 project_out.7
  35.2 0.2 collective-permute-start.3
  35.4 1.2 %project_out.8 = (f32[128,1024]{1,0:T(8,128)S(1)}, bf16[128,1024]{1,0:T(8,128)(2,1)S(1)}) custom-call(bf16[256,512]{1,0:T(8,128)(2,1)S(1)} %attend.2.refs_0_, bf16[256,1536]{1,0:T(8,128)(2,1)S(1)} %get-tuple-element.103.refs_1_, bf16[512,3072]{1,0:T(8,128)(2,1)S(1)} %copy-done, bf16[1536,3072]{1,0:T(8,128)(2,1)S(1)} %bitcast.9), custom_call_target="tpu_custom_call" | custom-call | flops 1073741824 | tf_op jit(solution)/shard_map/project_out/pallas_call | solution.py:211
  36.6 0.4 collective-permute-start.4
  37.1 1.2 %project_out.9 = (f32[128,1024]{1,0:T(8,128)S(1)}, bf16[128,1024]{1,0:T(8,128)(2,1)S(1)}) custom-call(bf16[256,512]{1,0:T(8,128)(2,1)S(1)} %attend.2.refs_0_, bf16[256,1536]{1,0:T(8,128)(2,1)S(1)} %get-tuple-element.103.refs_1_, bf16[512,3072]{1,0:T(8,128)(2,1)S(1)} %copy-done, bf16[1536,3072]{1,0:T(8,128)(2,1)S(1)} %bitcast.9), custom_call_target="tpu_custom_call" | custom-call | flops 1073741824 | tf_op jit(solution)/shard_map/project_out/pallas_call | solution.py:211
  38.4 0.2 collective-permute-start.5
  38.6 0.8 add_convert_fusion.1
  39.3 0.7 project_out.10
  40.0 0.4 collective-permute-start.6
  40.5 0.8 add_convert_fusion
  41.2 0.2 collective-permute-done.6
  41.5 0.7 add_convert_fusion.5
  42.1 1.5 %collective-permute-start.7 = (bf16[128,512]{1,0:T(8,128)(2,1)S(1)}, bf16[128,512]{1,0:T(8,128)(2,1)S(1)}, u32[]{:S(2)}, u32[]{:S(2)}) collective-permute-start(bf16[128,512]{1,0:T(8,128)(2,1)S(1)} %add_convert_fusion.6), channel_id=1, source_target_pairs={{0,2},{1,3},{2,0},{3,1},{4,6},{5,7},{6,4},{7,5},{8,10},{9,11},{10,... | collective-permute-start | bytes 393224 | tf_op jit(solution)/shard_map/ppermute | solution.py:255
  43.6 1.7 %attend.3.refs_0_ = bf16[256,512]{1,0:T(8,128)(2,1)S(1)} custom-call(bf16[256,512]{1,0:T(8,128)(2,1)S(1)} %get-tuple-element.110.refs_0_, bf16[256,512]{1,0:T(8,128)(2,1)S(1)} %get-tuple-element.87.refs_1_, bf16[256,512]{1,0:T(8,128)(2,1)S(1)} %get-tuple-element.88.refs_2_, bf16[256,512]{1,0:T(8,128)(2,1)S(1)} %get-tuple-element.89.refs_3_, ...), custom_call_target="tpu_custom_call" | custom-call | flops 805306368 | tf_op jit(solution)/shard_map/attend/pallas_call | solution.py:179
  45.4 2.5 %collective-permute-done.7 = bf16[128,512]{1,0:T(8,128)(2,1)S(1)} collective-permute-done((bf16[128,512]{1,0:T(8,128)(2,1)S(1)}, bf16[128,512]{1,0:T(8,128)(2,1)S(1)}, u32[]{:S(2)}, u32[]{:S(2)}) %collective-permute-start.7) | collective-permute-done | bytes 131104 | tf_op jit(solution)/shard_map/ppermute | solution.py:255
  47.9 1.0 project_out.11
  49.0 1.6 %collective-permute-start.11 = (bf16[128,1024]{1,0:T(8,128)(2,1)}, bf16[128,1024]{1,0:T(8,128)(2,1)S(1)}, u32[]{:S(2)}, u32[]{:S(2)}) collective-permute-start(bf16[128,1024]{1,0:T(8,128)(2,1)} %add_convert_fusion.1), channel_id=1, source_target_pairs={{0,2},{1,3},{2,0},{3,1},{4,6},{5,7},{6,4},{7,5},{8,10},{9,11},{10,... | collective-permute-start | bytes 786440 | tf_op jit(solution)/shard_map/ppermute | solution.py:255
  50.6 0.8 collective-permute-done.8
  51.4 1.3 %convert_add_fusion = f32[128,3072]{1,0:T(8,128)S(1)} fusion(f32[128,3072]{1,0:T(8,128)S(1)} %get-tuple-element.115, bf16[128,3072]{1,0:T(8,128)(2,1)} %collective-permute-done.8), kind=kLoop, calls=%fused_computation.1 | loop fusion | flops 786432 | bytes 3932160 | tf_op jit(solution)/shard_map/add | solution.py:311
  52.8 0.6 collective-permute-start.9
  53.4 1.5 %collective-permute-start.17 = (bf16[128,1024]{1,0:T(8,128)(2,1)}, bf16[128,1024]{1,0:T(8,128)(2,1)S(1)}, u32[]{:S(2)}, u32[]{:S(2)}) collective-permute-start(bf16[128,1024]{1,0:T(8,128)(2,1)} %add_convert_fusion), channel_id=1, source_target_pairs={{0,2},{1,3},{2,0},{3,1},{4,6},{5,7},{6,4},{7,5},{8,10},{9,11},{10,... | collective-permute-start | bytes 786440 | tf_op jit(solution)/shard_map/ppermute | solution.py:255
  54.9 0.5 collective-permute-start.16
  55.4 1.7 %collective-permute-done.9 = bf16[64,512]{1,0:T(8,128)(2,1)S(1)} collective-permute-done((bf16[64,512]{1,0:T(8,128)(2,1)S(1)}, bf16[64,512]{1,0:T(8,128)(2,1)S(1)}, u32[]{:S(2)}, u32[]{:S(2)}) %collective-permute-start.9) | collective-permute-done | bytes 65568 | tf_op jit(solution)/shard_map/ppermute | solution.py:258
  57.1 1.3 %collective-permute-start.10 = (bf16[64,512]{1,0:T(8,128)(2,1)S(1)}, bf16[64,512]{1,0:T(8,128)(2,1)S(1)}, u32[]{:S(2)}, u32[]{:S(2)}) collective-permute-start(bf16[64,512]{1,0:T(8,128)(2,1)S(1)} %fusion.23), channel_id=1, source_target_pairs={{0,8},{4,12},{16,24},{20,28},{1,9},{5,13},{17,25},{21,29},{2,10},{... | collective-permute-start | bytes 196616 | tf_op jit(solution)/shard_map/ppermute | solution.py:314
  58.5 0.6 collective-permute-start.14
  59.1 4.2 %collective-permute-done.10 = bf16[64,512]{1,0:T(8,128)(2,1)S(1)} collective-permute-done((bf16[64,512]{1,0:T(8,128)(2,1)S(1)}, bf16[64,512]{1,0:T(8,128)(2,1)S(1)}, u32[]{:S(2)}, u32[]{:S(2)}) %collective-permute-start.10) | collective-permute-done | bytes 65568 | tf_op jit(solution)/shard_map/ppermute | solution.py:314
  63.3 0.7 collective-permute-start.12
  64.0 1.3 %collective-permute-start.13 = (bf16[64,512]{1,0:T(8,128)(2,1)S(1)}, bf16[64,512]{1,0:T(8,128)(2,1)S(1)}, u32[]{:S(2)}, u32[]{:S(2)}) collective-permute-start(bf16[64,512]{1,0:T(8,128)(2,1)S(1)} %fusion.19), channel_id=1, source_target_pairs={{8,24},{12,28},{9,25},{13,29},{10,26},{14,30},{11,27},{15,31}} | collective-permute-start | bytes 196616 | tf_op jit(solution)/shard_map/ppermute | solution.py:314
  65.3 1.3 %collective-permute-start.18 = (bf16[64,1024]{1,0:T(8,128)(2,1)S(1)}, bf16[64,1024]{1,0:T(8,128)(2,1)S(1)}, u32[]{:S(2)}, u32[]{:S(2)}) collective-permute-start(bf16[64,1024]{1,0:T(8,128)(2,1)S(1)} %fusion.16), channel_id=1, source_target_pairs={{0,8},{4,12},{16,24},{20,28},{1,9},{5,13},{17,25},{21,29},{2,10},{... | collective-permute-start | bytes 393224 | tf_op jit(solution)/shard_map/ppermute | solution.py:314
  66.6 4.4 %collective-permute-done.13 = bf16[64,512]{1,0:T(8,128)(2,1)S(1)} collective-permute-done((bf16[64,512]{1,0:T(8,128)(2,1)S(1)}, bf16[64,512]{1,0:T(8,128)(2,1)S(1)}, u32[]{:S(2)}, u32[]{:S(2)}) %collective-permute-start.13) | collective-permute-done | bytes 65568 | tf_op jit(solution)/shard_map/ppermute | solution.py:314
  71.1 0.6 collective-permute-start.15
  71.8 1.6 %collective-permute-start.21 = (bf16[64,1024]{1,0:T(8,128)(2,1)S(1)}, bf16[64,1024]{1,0:T(8,128)(2,1)S(1)}, u32[]{:S(2)}, u32[]{:S(2)}) collective-permute-start(bf16[64,1024]{1,0:T(8,128)(2,1)S(1)} %dynamic-slice_convert_fusion), channel_id=1, source_target_pairs={{0,4},{4,0},{8,12},{12,8},{16,20},{20,16},{24,28},{28,24},{1,5},{5... | collective-permute-start | bytes 393224 | tf_op jit(solution)/shard_map/ppermute | solution.py:258
  73.4 1.3 %collective-permute-start.23 = (bf16[128,512]{1,0:T(8,128)(2,1)S(1)}, bf16[128,512]{1,0:T(8,128)(2,1)S(1)}, u32[]{:S(2)}, u32[]{:S(2)}) collective-permute-start(bf16[128,512]{1,0:T(8,128)(2,1)S(1)} %fusion.24), channel_id=1, source_target_pairs={{0,8},{4,12},{16,24},{20,28},{1,9},{5,13},{17,25},{21,29},{2,10},{... | collective-permute-start | bytes 393224 | tf_op jit(solution)/shard_map/ppermute | solution.py:314
  74.7 0.7 collective-permute-done.15
  75.6 0.7 collective-permute-start.19
  76.3 1.3 %collective-permute-start.20 = (bf16[64,1024]{1,0:T(8,128)(2,1)S(1)}, bf16[64,1024]{1,0:T(8,128)(2,1)S(1)}, u32[]{:S(2)}, u32[]{:S(2)}) collective-permute-start(bf16[64,1024]{1,0:T(8,128)(2,1)S(1)} %fusion.3), channel_id=1, source_target_pairs={{8,24},{12,28},{9,25},{13,29},{10,26},{14,30},{11,27},{15,31}} | collective-permute-start | bytes 393224 | tf_op jit(solution)/shard_map/ppermute | solution.py:314
  77.6 1.3 %collective-permute-start.22 = (bf16[64,1024]{1,0:T(8,128)(2,1)S(1)}, bf16[64,1024]{1,0:T(8,128)(2,1)S(1)}, u32[]{:S(2)}, u32[]{:S(2)}) collective-permute-start(bf16[64,1024]{1,0:T(8,128)(2,1)S(1)} %fusion.17), channel_id=1, source_target_pairs={{0,8},{4,12},{16,24},{20,28},{1,9},{5,13},{17,25},{21,29},{2,10},{... | collective-permute-start | bytes 393224 | tf_op jit(solution)/shard_map/ppermute | solution.py:314
  78.9 3.9 %collective-permute-done.23 = bf16[128,512]{1,0:T(8,128)(2,1)S(1)} collective-permute-done((bf16[128,512]{1,0:T(8,128)(2,1)S(1)}, bf16[128,512]{1,0:T(8,128)(2,1)S(1)}, u32[]{:S(2)}, u32[]{:S(2)}) %collective-permute-start.23) | collective-permute-done | bytes 131104 | tf_op jit(solution)/shard_map/ppermute | solution.py:314
  82.9 0.7 collective-permute-start.25
  83.6 1.3 %collective-permute-start.26 = (bf16[128,512]{1,0:T(8,128)(2,1)S(1)}, bf16[128,512]{1,0:T(8,128)(2,1)S(1)}, u32[]{:S(2)}, u32[]{:S(2)}) collective-permute-start(bf16[128,512]{1,0:T(8,128)(2,1)S(1)} %fusion.6), channel_id=1, source_target_pairs={{8,24},{12,28},{9,25},{13,29},{10,26},{14,30},{11,27},{15,31}} | collective-permute-start | bytes 393224 | tf_op jit(solution)/shard_map/ppermute | solution.py:314
  84.9 0.7 collective-permute-start.27
  85.6 1.3 %collective-permute-start.28 = (bf16[64,1024]{1,0:T(8,128)(2,1)S(1)}, bf16[64,1024]{1,0:T(8,128)(2,1)S(1)}, u32[]{:S(2)}, u32[]{:S(2)}) collective-permute-start(bf16[64,1024]{1,0:T(8,128)(2,1)S(1)} %fusion.8), channel_id=1, source_target_pairs={{8,24},{12,28},{9,25},{13,29},{10,26},{14,30},{11,27},{15,31}} | collective-permute-start | bytes 393224 | tf_op jit(solution)/shard_map/ppermute | solution.py:314
  86.9 1.0 %collective-permute-done.20 = bf16[64,1024]{1,0:T(8,128)(2,1)S(1)} collective-permute-done((bf16[64,1024]{1,0:T(8,128)(2,1)S(1)}, bf16[64,1024]{1,0:T(8,128)(2,1)S(1)}, u32[]{:S(2)}, u32[]{:S(2)}) %collective-permute-start.20) | collective-permute-done | bytes 131104 | tf_op jit(solution)/shard_map/ppermute | solution.py:314
  88.0 0.6 collective-permute-start.24
  88.6 4.9 %collective-permute-done.26 = bf16[128,512]{1,0:T(8,128)(2,1)S(1)} collective-permute-done((bf16[128,512]{1,0:T(8,128)(2,1)S(1)}, bf16[128,512]{1,0:T(8,128)(2,1)S(1)}, u32[]{:S(2)}, u32[]{:S(2)}) %collective-permute-start.26) | collective-permute-done | bytes 131104 | tf_op jit(solution)/shard_map/ppermute | solution.py:314
  93.7 0.6 collective-permute-start.30
  94.2 2.2 %collective-permute-done.28 = bf16[64,1024]{1,0:T(8,128)(2,1)S(1)} collective-permute-done((bf16[64,1024]{1,0:T(8,128)(2,1)S(1)}, bf16[64,1024]{1,0:T(8,128)(2,1)S(1)}, u32[]{:S(2)}, u32[]{:S(2)}) %collective-permute-start.28) | collective-permute-done | bytes 131104 | tf_op jit(solution)/shard_map/ppermute | solution.py:314
  96.6 0.6 collective-permute-start.29
  97.3 2.0 %collective-permute-done.30 = bf16[128,512]{1,0:T(8,128)(2,1)S(1)} collective-permute-done((bf16[128,512]{1,0:T(8,128)(2,1)S(1)}, bf16[128,512]{1,0:T(8,128)(2,1)S(1)}, u32[]{:S(2)}, u32[]{:S(2)}) %collective-permute-start.30) | collective-permute-done | bytes 131104 | tf_op jit(solution)/shard_map/ppermute | solution.py:258
  99.2 0.2 maximum_add_fusion.2
  99.5 2.1 %collective-permute-done.29 = bf16[64,1024]{1,0:T(8,128)(2,1)S(1)} collective-permute-done((bf16[64,1024]{1,0:T(8,128)(2,1)S(1)}, bf16[64,1024]{1,0:T(8,128)(2,1)S(1)}, u32[]{:S(2)}, u32[]{:S(2)}) %collective-permute-start.29) | collective-permute-done | bytes 131104 | tf_op jit(solution)/shard_map/ppermute | solution.py:258
  101.8 0.1 maximum_add_fusion
  101.9 1.3 %maximum_bitcast_fusion = f32[1,128,3072]{2,1,0:T(8,128)} fusion(f32[128,512]{1,0:T(8,128)S(1)} %get-tuple-element.148, f32[128,1024]{1,0:T(8,128)S(1)} %get-tuple-element.150, f32[128,1024]{1,0:T(8,128)S(1)} %get-tuple-element.149, f32[128,512]{1,0:T(8,128)S(1)} %get-tuple-element.147), kind=kLoop, calls=%fused_computation | loop fusion | flops 1179648 | bytes 3145728 | tf_op jit(solution)/shard_map/broadcast_in_dim | solution.py:403
  (62 shorter events, 1.5 us)
Async XLA Ops:
  0.7 6.7 %copy-start.2 = (f32[128]{0:T(128)S(1)}, f32[128]{0:T(128)}, u32[]{:S(2)}) copy-start(f32[128]{0:T(128)} %param.16) | copy-start | bytes 1540
  0.7 6.7 %copy-start.3 = (f32[128]{0:T(128)S(1)}, f32[128]{0:T(128)}, u32[]{:S(2)}) copy-start(f32[128]{0:T(128)} %param.17) | copy-start | bytes 1540
  0.7 16.4 %slice-start = ((s8[9437184]{0:T(1024)(128)(4,1)}), s8[1048576]{0:T(1024)(128)(4,1)S(1)}, s32[]{:S(2)}) async-start(s8[9437184]{0:T(1024)(128)(4,1)} %bitcast.8), calls=%async_computation | async-start | bytes 2097152
  4.8 2.6 %collective-permute-start = (bf16[128,3072]{1,0:T(8,128)(2,1)}, bf16[128,3072]{1,0:T(8,128)(2,1)S(1)}, u32[]{:S(2)}, u32[]{:S(2)}) collective-permute-start(bf16[128,3072]{1,0:T(8,128)(2,1)} %get-tuple-element.74.m0), channel_id=1, source_target_pairs={{0,1},{1,0},{2,3},{3,2},{4,5},{5,4},{6,7},{7,6},{8,9},{9,8},{10,11... | collective-permute-start | bytes 2359304 | tf_op jit(solution)/shard_map/ppermute | solution.py:252
  4.8 20.2 %collective-permute-start.1 = (bf16[128,3072]{1,0:T(8,128)(2,1)}, bf16[128,3072]{1,0:T(8,128)(2,1)S(1)}, u32[]{:S(2)}, u32[]{:S(2)}) collective-permute-start(bf16[128,3072]{1,0:T(8,128)(2,1)} %get-tuple-element.74.m0), channel_id=1, source_target_pairs={{0,2},{1,3},{2,0},{3,1},{4,6},{5,7},{6,4},{7,5},{8,10},{9,11},{10,... | collective-permute-start | bytes 2359304 | tf_op jit(solution)/shard_map/ppermute | solution.py:255
  7.3 1.1 %copy-start.1 = (bf16[128,3072]{1,0:T(8,128)(2,1)S(1)}, bf16[128,3072]{1,0:T(8,128)(2,1)}, u32[]{:S(2)}) copy-start(bf16[128,3072]{1,0:T(8,128)(2,1)} %get-tuple-element.74.m0) | copy-start | bytes 2359300
  8.5 8.6 %slice-start.1 = ((s8[9437184]{0:T(1024)(128)(4,1)}), s8[4194304]{0:T(1024)(128)(4,1)S(1)}, s32[]{:S(2)}) async-start(s8[9437184]{0:T(1024)(128)(4,1)} %bitcast.8), calls=%async_computation.1 | async-start | bytes 8388608
  8.5 8.9 %slice-start.2 = ((s8[9437184]{0:T(1024)(128)(4,1)}), s8[4194304]{0:T(1024)(128)(4,1)S(1)}, s32[]{:S(2)}) async-start(s8[9437184]{0:T(1024)(128)(4,1)} %bitcast.8), calls=%async_computation.2 | async-start | bytes 8388608
  25.0 2.3 %collective-permute-start.2 = (bf16[128,3072]{1,0:T(8,128)(2,1)S(1)}, bf16[128,3072]{1,0:T(8,128)(2,1)S(1)}, u32[]{:S(2)}, u32[]{:S(2)}) collective-permute-start(bf16[128,3072]{1,0:T(8,128)(2,1)S(1)} %collective-permute-done.1.m0), channel_id=1, source_target_pairs={{0,1},{1,0},{2,3},{3,2},{4,5},{5,4},{6,7},{7,6},{8,9},{9,8},{10,11... | collective-permute-start | bytes 2359304 | tf_op jit(solution)/shard_map/ppermute | solution.py:252
  27.3 7.0 %copy-start = (bf16[512,3072]{1,0:T(8,128)(2,1)S(1)}, bf16[512,3072]{1,0:T(8,128)(2,1)}, u32[]{:S(2)}) copy-start(bf16[512,3072]{1,0:T(8,128)(2,1)} %refs_1_.5) | copy-start | bytes 9437188
  35.2 1.9 %collective-permute-start.3 = (bf16[128,512]{1,0:T(8,128)(2,1)S(1)}, bf16[128,512]{1,0:T(8,128)(2,1)S(1)}, u32[]{:S(2)}, u32[]{:S(2)}) collective-permute-start(bf16[128,512]{1,0:T(8,128)(2,1)S(1)} %get-tuple-element.93), channel_id=1, source_target_pairs={{0,1},{1,0},{2,3},{3,2},{4,5},{5,4},{6,7},{7,6},{8,9},{9,8},{10,11... | collective-permute-start | bytes 393224 | tf_op jit(solution)/shard_map/ppermute | solution.py:252
  36.6 1.9 %collective-permute-start.4 = (bf16[128,1024]{1,0:T(8,128)(2,1)S(1)}, bf16[128,1024]{1,0:T(8,128)(2,1)S(1)}, u32[]{:S(2)}, u32[]{:S(2)}) collective-permute-start(bf16[128,1024]{1,0:T(8,128)(2,1)S(1)} %get-tuple-element.99), channel_id=1, source_target_pairs={{0,1},{1,0},{2,3},{3,2},{4,5},{5,4},{6,7},{7,6},{8,9},{9,8},{10,11... | collective-permute-start | bytes 786440 | tf_op jit(solution)/shard_map/ppermute | solution.py:252
  38.4 2.1 %collective-permute-start.5 = (bf16[128,1024]{1,0:T(8,128)(2,1)S(1)}, bf16[128,1024]{1,0:T(8,128)(2,1)S(1)}, u32[]{:S(2)}, u32[]{:S(2)}) collective-permute-start(bf16[128,1024]{1,0:T(8,128)(2,1)S(1)} %get-tuple-element.105), channel_id=1, source_target_pairs={{0,1},{1,0},{2,3},{3,2},{4,5},{5,4},{6,7},{7,6},{8,9},{9,8},{10,11... | collective-permute-start | bytes 786440 | tf_op jit(solution)/shard_map/ppermute | solution.py:252
  40.0 1.4 %collective-permute-start.6 = (bf16[128,512]{1,0:T(8,128)(2,1)S(1)}, bf16[128,512]{1,0:T(8,128)(2,1)S(1)}, u32[]{:S(2)}, u32[]{:S(2)}) collective-permute-start(bf16[128,512]{1,0:T(8,128)(2,1)S(1)} %get-tuple-element.109), channel_id=1, source_target_pairs={{0,1},{1,0},{2,3},{3,2},{4,5},{5,4},{6,7},{7,6},{8,9},{9,8},{10,11... | collective-permute-start | bytes 393224 | tf_op jit(solution)/shard_map/ppermute | solution.py:252
  42.1 5.8 %collective-permute-start.7 = (bf16[128,512]{1,0:T(8,128)(2,1)S(1)}, bf16[128,512]{1,0:T(8,128)(2,1)S(1)}, u32[]{:S(2)}, u32[]{:S(2)}) collective-permute-start(bf16[128,512]{1,0:T(8,128)(2,1)S(1)} %add_convert_fusion.6), channel_id=1, source_target_pairs={{0,2},{1,3},{2,0},{3,1},{4,6},{5,7},{6,4},{7,5},{8,10},{9,11},{10,... | collective-permute-start | bytes 393224 | tf_op jit(solution)/shard_map/ppermute | solution.py:255
  45.3 3.7 %copy-start.5 = (f32[1,3072]{1,0:T(1,128)S(1)}, f32[1,3072]{1,0:T(1,128)}, u32[]{:S(2)}) copy-start(f32[1,3072]{1,0:T(1,128)} %get-tuple-element.73) | copy-start | bytes 36868
  48.9 2.5 %collective-permute-start.8 = (bf16[128,3072]{1,0:T(8,128)(2,1)S(1)}, bf16[128,3072]{1,0:T(8,128)(2,1)}, u32[]{:S(2)}, u32[]{:S(2)}) collective-permute-start(bf16[128,3072]{1,0:T(8,128)(2,1)S(1)} %get-tuple-element.116), channel_id=1, source_target_pairs={{0,1},{1,0},{2,3},{3,2},{4,5},{5,4},{6,7},{7,6},{8,9},{9,8},{10,11... | collective-permute-start | bytes 2359304 | tf_op jit(solution)/shard_map/ppermute | solution.py:252
  49.0 9.4 %collective-permute-start.11 = (bf16[128,1024]{1,0:T(8,128)(2,1)}, bf16[128,1024]{1,0:T(8,128)(2,1)S(1)}, u32[]{:S(2)}, u32[]{:S(2)}) collective-permute-start(bf16[128,1024]{1,0:T(8,128)(2,1)} %add_convert_fusion.1), channel_id=1, source_target_pairs={{0,2},{1,3},{2,0},{3,1},{4,6},{5,7},{6,4},{7,5},{8,10},{9,11},{10,... | collective-permute-start | bytes 786440 | tf_op jit(solution)/shard_map/ppermute | solution.py:255
  52.8 4.3 %collective-permute-start.9 = (bf16[64,512]{1,0:T(8,128)(2,1)S(1)}, bf16[64,512]{1,0:T(8,128)(2,1)S(1)}, u32[]{:S(2)}, u32[]{:S(2)}) collective-permute-start(bf16[64,512]{1,0:T(8,128)(2,1)S(1)} %dynamic-slice_convert_fusion.2), channel_id=1, source_target_pairs={{0,4},{4,0},{8,12},{12,8},{16,20},{20,16},{24,28},{28,24},{1,5},{5... | collective-permute-start | bytes 196616 | tf_op jit(solution)/shard_map/ppermute | solution.py:258
  53.4 18.3 %collective-permute-start.17 = (bf16[128,1024]{1,0:T(8,128)(2,1)}, bf16[128,1024]{1,0:T(8,128)(2,1)S(1)}, u32[]{:S(2)}, u32[]{:S(2)}) collective-permute-start(bf16[128,1024]{1,0:T(8,128)(2,1)} %add_convert_fusion), channel_id=1, source_target_pairs={{0,2},{1,3},{2,0},{3,1},{4,6},{5,7},{6,4},{7,5},{8,10},{9,11},{10,... | collective-permute-start | bytes 786440 | tf_op jit(solution)/shard_map/ppermute | solution.py:255
  54.9 18.5 %collective-permute-start.16 = (bf16[128,512]{1,0:T(8,128)(2,1)}, bf16[128,512]{1,0:T(8,128)(2,1)S(1)}, u32[]{:S(2)}, u32[]{:S(2)}) collective-permute-start(bf16[128,512]{1,0:T(8,128)(2,1)} %add_convert_fusion.5), channel_id=1, source_target_pairs={{0,2},{1,3},{2,0},{3,1},{4,6},{5,7},{6,4},{7,5},{8,10},{9,11},{10,... | collective-permute-start | bytes 393224 | tf_op jit(solution)/shard_map/ppermute | solution.py:255
  57.1 6.2 %collective-permute-start.10 = (bf16[64,512]{1,0:T(8,128)(2,1)S(1)}, bf16[64,512]{1,0:T(8,128)(2,1)S(1)}, u32[]{:S(2)}, u32[]{:S(2)}) collective-permute-start(bf16[64,512]{1,0:T(8,128)(2,1)S(1)} %fusion.23), channel_id=1, source_target_pairs={{0,8},{4,12},{16,24},{20,28},{1,9},{5,13},{17,25},{21,29},{2,10},{... | collective-permute-start | bytes 196616 | tf_op jit(solution)/shard_map/ppermute | solution.py:314
  58.5 6.7 %collective-permute-start.14 = (bf16[64,1024]{1,0:T(8,128)(2,1)S(1)}, bf16[64,1024]{1,0:T(8,128)(2,1)S(1)}, u32[]{:S(2)}, u32[]{:S(2)}) collective-permute-start(bf16[64,1024]{1,0:T(8,128)(2,1)S(1)} %dynamic-slice_convert_fusion.1), channel_id=1, source_target_pairs={{0,4},{4,0},{8,12},{12,8},{16,20},{20,16},{24,28},{28,24},{1,5},{5... | collective-permute-start | bytes 393224 | tf_op jit(solution)/shard_map/ppermute | solution.py:258
  63.3 3.3 %collective-permute-start.12 = (bf16[64,512]{1,0:T(8,128)(2,1)S(1)}, bf16[64,512]{1,0:T(8,128)(2,1)S(1)}, u32[]{:S(2)}, u32[]{:S(2)}) collective-permute-start(bf16[64,512]{1,0:T(8,128)(2,1)S(1)} %fusion.19), channel_id=1, source_target_pairs={{8,16},{12,20},{9,17},{13,21},{10,18},{14,22},{11,19},{15,23}} | collective-permute-start | bytes 196616 | tf_op jit(solution)/shard_map/ppermute | solution.py:314
  64.0 7.1 %collective-permute-start.13 = (bf16[64,512]{1,0:T(8,128)(2,1)S(1)}, bf16[64,512]{1,0:T(8,128)(2,1)S(1)}, u32[]{:S(2)}, u32[]{:S(2)}) collective-permute-start(bf16[64,512]{1,0:T(8,128)(2,1)S(1)} %fusion.19), channel_id=1, source_target_pairs={{8,24},{12,28},{9,25},{13,29},{10,26},{14,30},{11,27},{15,31}} | collective-permute-start | bytes 196616 | tf_op jit(solution)/shard_map/ppermute | solution.py:314
  65.3 10.2 %collective-permute-start.18 = (bf16[64,1024]{1,0:T(8,128)(2,1)S(1)}, bf16[64,1024]{1,0:T(8,128)(2,1)S(1)}, u32[]{:S(2)}, u32[]{:S(2)}) collective-permute-start(bf16[64,1024]{1,0:T(8,128)(2,1)S(1)} %fusion.16), channel_id=1, source_target_pairs={{0,8},{4,12},{16,24},{20,28},{1,9},{5,13},{17,25},{21,29},{2,10},{... | collective-permute-start | bytes 393224 | tf_op jit(solution)/shard_map/ppermute | solution.py:314
  71.1 4.3 %collective-permute-start.15 = (bf16[64,512]{1,0:T(8,128)(2,1)S(1)}, bf16[64,512]{1,0:T(8,128)(2,1)S(1)}, u32[]{:S(2)}, u32[]{:S(2)}) collective-permute-start(bf16[64,512]{1,0:T(8,128)(2,1)S(1)} %add_convert_fusion.7), channel_id=1, source_target_pairs={{0,4},{4,0},{8,12},{12,8},{16,20},{20,16},{24,28},{28,24},{1,5},{5... | collective-permute-start | bytes 196616 | tf_op jit(solution)/shard_map/ppermute | solution.py:258
  71.8 5.8 %collective-permute-start.21 = (bf16[64,1024]{1,0:T(8,128)(2,1)S(1)}, bf16[64,1024]{1,0:T(8,128)(2,1)S(1)}, u32[]{:S(2)}, u32[]{:S(2)}) collective-permute-start(bf16[64,1024]{1,0:T(8,128)(2,1)S(1)} %dynamic-slice_convert_fusion), channel_id=1, source_target_pairs={{0,4},{4,0},{8,12},{12,8},{16,20},{20,16},{24,28},{28,24},{1,5},{5... | collective-permute-start | bytes 393224 | tf_op jit(solution)/shard_map/ppermute | solution.py:258
  73.4 9.4 %collective-permute-start.23 = (bf16[128,512]{1,0:T(8,128)(2,1)S(1)}, bf16[128,512]{1,0:T(8,128)(2,1)S(1)}, u32[]{:S(2)}, u32[]{:S(2)}) collective-permute-start(bf16[128,512]{1,0:T(8,128)(2,1)S(1)} %fusion.24), channel_id=1, source_target_pairs={{0,8},{4,12},{16,24},{20,28},{1,9},{5,13},{17,25},{21,29},{2,10},{... | collective-permute-start | bytes 393224 | tf_op jit(solution)/shard_map/ppermute | solution.py:314
  75.6 10.0 %collective-permute-start.19 = (bf16[64,1024]{1,0:T(8,128)(2,1)S(1)}, bf16[64,1024]{1,0:T(8,128)(2,1)S(1)}, u32[]{:S(2)}, u32[]{:S(2)}) collective-permute-start(bf16[64,1024]{1,0:T(8,128)(2,1)S(1)} %fusion.3), channel_id=1, source_target_pairs={{8,16},{12,20},{9,17},{13,21},{10,18},{14,22},{11,19},{15,23}} | collective-permute-start | bytes 393224 | tf_op jit(solution)/shard_map/ppermute | solution.py:314
  76.3 11.7 %collective-permute-start.20 = (bf16[64,1024]{1,0:T(8,128)(2,1)S(1)}, bf16[64,1024]{1,0:T(8,128)(2,1)S(1)}, u32[]{:S(2)}, u32[]{:S(2)}) collective-permute-start(bf16[64,1024]{1,0:T(8,128)(2,1)S(1)} %fusion.3), channel_id=1, source_target_pairs={{8,24},{12,28},{9,25},{13,29},{10,26},{14,30},{11,27},{15,31}} | collective-permute-start | bytes 393224 | tf_op jit(solution)/shard_map/ppermute | solution.py:314
  77.6 7.2 %collective-permute-start.22 = (bf16[64,1024]{1,0:T(8,128)(2,1)S(1)}, bf16[64,1024]{1,0:T(8,128)(2,1)S(1)}, u32[]{:S(2)}, u32[]{:S(2)}) collective-permute-start(bf16[64,1024]{1,0:T(8,128)(2,1)S(1)} %fusion.17), channel_id=1, source_target_pairs={{0,8},{4,12},{16,24},{20,28},{1,9},{5,13},{17,25},{21,29},{2,10},{... | collective-permute-start | bytes 393224 | tf_op jit(solution)/shard_map/ppermute | solution.py:314
  82.9 5.7 %collective-permute-start.25 = (bf16[128,512]{1,0:T(8,128)(2,1)S(1)}, bf16[128,512]{1,0:T(8,128)(2,1)S(1)}, u32[]{:S(2)}, u32[]{:S(2)}) collective-permute-start(bf16[128,512]{1,0:T(8,128)(2,1)S(1)} %fusion.6), channel_id=1, source_target_pairs={{8,16},{12,20},{9,17},{13,21},{10,18},{14,22},{11,19},{15,23}} | collective-permute-start | bytes 393224 | tf_op jit(solution)/shard_map/ppermute | solution.py:314
  83.6 10.0 %collective-permute-start.26 = (bf16[128,512]{1,0:T(8,128)(2,1)S(1)}, bf16[128,512]{1,0:T(8,128)(2,1)S(1)}, u32[]{:S(2)}, u32[]{:S(2)}) collective-permute-start(bf16[128,512]{1,0:T(8,128)(2,1)S(1)} %fusion.6), channel_id=1, source_target_pairs={{8,24},{12,28},{9,25},{13,29},{10,26},{14,30},{11,27},{15,31}} | collective-permute-start | bytes 393224 | tf_op jit(solution)/shard_map/ppermute | solution.py:314
  84.9 9.3 %collective-permute-start.27 = (bf16[64,1024]{1,0:T(8,128)(2,1)S(1)}, bf16[64,1024]{1,0:T(8,128)(2,1)S(1)}, u32[]{:S(2)}, u32[]{:S(2)}) collective-permute-start(bf16[64,1024]{1,0:T(8,128)(2,1)S(1)} %fusion.8), channel_id=1, source_target_pairs={{8,16},{12,20},{9,17},{13,21},{10,18},{14,22},{11,19},{15,23}} | collective-permute-start | bytes 393224 | tf_op jit(solution)/shard_map/ppermute | solution.py:314
  85.6 10.9 %collective-permute-start.28 = (bf16[64,1024]{1,0:T(8,128)(2,1)S(1)}, bf16[64,1024]{1,0:T(8,128)(2,1)S(1)}, u32[]{:S(2)}, u32[]{:S(2)}) collective-permute-start(bf16[64,1024]{1,0:T(8,128)(2,1)S(1)} %fusion.8), channel_id=1, source_target_pairs={{8,24},{12,28},{9,25},{13,29},{10,26},{14,30},{11,27},{15,31}} | collective-permute-start | bytes 393224 | tf_op jit(solution)/shard_map/ppermute | solution.py:314
  88.0 11.2 %copy-start.4 = (f32[128,3072]{1,0:T(8,128)S(1)}, f32[128,3072]{1,0:T(8,128)}, u32[]{:S(2)}) copy-start(f32[128,3072]{1,0:T(8,128)} %param.12) | copy-start | bytes 4718596
  88.0 9.1 %collective-permute-start.24 = (bf16[64,1024]{1,0:T(8,128)(2,1)S(1)}, bf16[64,1024]{1,0:T(8,128)(2,1)S(1)}, u32[]{:S(2)}, u32[]{:S(2)}) collective-permute-start(bf16[64,1024]{1,0:T(8,128)(2,1)S(1)} %add_convert_fusion.4), channel_id=1, source_target_pairs={{0,4},{4,0},{8,12},{12,8},{16,20},{20,16},{24,28},{28,24},{1,5},{5... | collective-permute-start | bytes 393224 | tf_op jit(solution)/shard_map/ppermute | solution.py:258
  93.7 5.6 %collective-permute-start.30 = (bf16[128,512]{1,0:T(8,128)(2,1)S(1)}, bf16[128,512]{1,0:T(8,128)(2,1)S(1)}, u32[]{:S(2)}, u32[]{:S(2)}) collective-permute-start(bf16[128,512]{1,0:T(8,128)(2,1)S(1)} %add_convert_fusion.3), channel_id=1, source_target_pairs={{0,4},{4,0},{8,12},{12,8},{16,20},{20,16},{24,28},{28,24},{1,5},{5... | collective-permute-start | bytes 393224 | tf_op jit(solution)/shard_map/ppermute | solution.py:258
  96.6 5.0 %collective-permute-start.29 = (bf16[64,1024]{1,0:T(8,128)(2,1)S(1)}, bf16[64,1024]{1,0:T(8,128)(2,1)S(1)}, u32[]{:S(2)}, u32[]{:S(2)}) collective-permute-start(bf16[64,1024]{1,0:T(8,128)(2,1)S(1)} %add_convert_fusion.2), channel_id=1, source_target_pairs={{0,4},{4,0},{8,12},{12,8},{16,20},{20,16},{24,28},{28,24},{1,5},{5... | collective-permute-start | bytes 393224 | tf_op jit(solution)/shard_map/ppermute | solution.py:258

commit v5 on v4

--- a/solution.py
+++ b/solution.py
@@ -243,7 +243,7 @@
     groups = n_step // 2
     half = rows // 2
     unit = width // 24
-    counts = [4 * unit, 8 * unit, 8 * unit, 4 * unit]
+    counts = [6 * unit, 10 * unit, 8 * unit]
     chunks = len(counts)
     firsts = [sum(counts[:c]) for c in range(chunks)]
     qg, kg = q_gain[None, :], k_gain[None, :]
@@ -281,51 +281,58 @@
     mixed = [attend_call(q, ks, vs, head) for q in qs]
 
     weights = [w_out_attn, w_out_mlp]
-    sums = [[] for _ in offsets]
-    ready = [[] for _ in offsets]
-    gate = (mixed, acts)
-    for c in range(chunks):
-        for j in range(chips - 1):
-            keep, send = out_call([gate[0][j], gate[1][j]], weights, [], firsts[c], counts[c])
-            sums[j].append((keep, to_core(send)))
-        if c >= 1:
-            for j in range(chips - 1):
-                keep, send = sums[j][c - 1]
-                ready[j].append((keep + send.astype(f32)).astype(bf16))
-            recent = [r[-1] for r in ready]
-            now = [x[-1][0] for x in sums]
-            gate, recent, now = tied(gate, recent, now)
-            for j in range(chips - 1):
-                ready[j][-1] = recent[j]
-                sums[j][-1] = (now[j], sums[j][-1][1])
-    for j in range(chips - 1):
-        keep, send = sums[j][-1]
-        ready[j].append((keep + send.astype(f32)).astype(bf16))
-    q0, ready = tied(q0, ready)
-    got = [[to_chip(r, chips - 1 - j) for r in ready[j]] for j in range(chips - 1)]
+    got = [[] for _ in offsets]
+
+    def rows_out(c):
+        return [
+            out_call([a, b], weights, [], firsts[c], counts[c]) for a, b in zip(mixed, acts)
+        ]
+
+    def joined(parts, sent):
+        return [(keep + s.astype(f32)).astype(bf16) for (keep, _), s in zip(parts, sent)]
+
+    def to_chips(ready):
+        for j, one in enumerate(ready):
+            got[j].append(to_chip(one, chips - 1 - j))
+
+    parts = rows_out(0)
+    sent = [to_core(send) for _, send in parts]
+    q0, parts = tied(q0, parts)
     mixed0 = attend_call(q0, ks, vs, head)
-    early = [row[0] for row in got]
-    mixed0, early = tied(mixed0, early)
-    got = [[e] + row[1:] for e, row in zip(early, got)]
+    mixed0, sent = tied(mixed0, sent)
+    ready = joined(parts, sent)
+    mixed, acts, mixed0, ready = tied(mixed, acts, mixed0, ready)
+    to_chips(ready)
+    waiting = []
+    for c in range(1, chunks):
+        parts = rows_out(c)
+        waiting.append((parts, [to_core(send) for _, send in parts]))
+        mixed, acts, mixed0, parts = tied(mixed, acts, mixed0, parts)
+        waiting[-1] = (parts, waiting[-1][1])
+    mixed0, first = tied(mixed0, [row[0] for row in got])
+    for row, one in zip(got, first):
+        row[0] = one
     keep, send = out_call([mixed0], [w_out_attn], [low0, high0], 0, width)
+    keep, waiting[0] = tied(keep, waiting[0])
+    for parts, sent in waiting:
+        to_chips(joined(parts, sent))
     own = keep + to_core(send).astype(f32)
 
     def along(pairs):
         return lambda x: lax.ppermute(x, "step", [(2 * a + i, 2 * b + i) for a, b in pairs for i in (0, 1)])
 
+    group = lax.div(lax.axis_index("step"), 2)
     rounds = []
     span = 1
     while span < groups:
-        moves = []
-        for t in range(span):
-            pairs = [(b + span - 1, b + span + t) for b in range(0, groups, 2 * span)]
-            moves.append(along([p for p in pairs if p[1] < groups]))
-        rounds.append(moves)
+        pairs = [(b, b ^ span) for b in range(groups) if b ^ span < groups]
+        if 2 * span >= groups:
+            pairs = [p for p in pairs if p[0] < p[1]]
+        rounds.append((span, along(pairs)))
         span *= 2
 
     def prefix_stages(c, split):
-        first = firsts[c]
-        cols = slice(first, first + counts[c])
+        cols = slice(firsts[c], firsts[c] + counts[c])
         held = {}
 
         def drift_of(fetched):
@@ -345,13 +352,14 @@
             held["total"] = held["kept"] + held["fetched"]
             return held["total"].astype(bf16)
 
-        def collect(final, fetched):
-            for one in fetched:
-                one = one.astype(f32)
-                held["earlier"] = held["earlier"] + one if "earlier" in held else one
-            if final:
+        def collect(r, fetched):
+            one = fetched[0].astype(f32)
+            upper = (lax.rem(lax.div(group, rounds[r][0]), 2) == 1).astype(f32)
+            held["earlier"] = held["earlier"] + upper * one if r else upper * one
+            if r == len(rounds) - 1:
                 return (held["earlier"] + even * held["kept"]).astype(bf16)
-            return (held["earlier"] + held["total"]).astype(bf16)
+            held["total"] = held["total"] + one
+            return held["total"].astype(bf16)
 
         def finish(fetched):
             back = fetched[0].astype(f32)
@@ -365,16 +373,16 @@
                 change = held["earlier"] + held["kept"] + back
             return x_start[:, cols] + change
 
-        stages = [(drift_of, [to_pair] if split else rounds[0])]
+        stages = [(drift_of, to_pair if split else rounds[0][1])]
         if split:
-            stages.append((pair_sum, rounds[0]))
+            stages.append((pair_sum, rounds[0][1]))
         for r in range(len(rounds)):
-            final = r == len(rounds) - 1
-            stages.append((functools.partial(collect, final), [to_pair] if final else rounds[r + 1]))
+            move = to_pair if r == len(rounds) - 1 else rounds[r + 1][1]
+            stages.append((functools.partial(collect, r), move))
         stages.append((finish, None))
         return stages
 
-    plan = [prefix_stages(c, c < chunks - 1) for c in range(chunks)]
+    plan = [prefix_stages(c, True) for c in range(chunks)]
     inbox = [[got[j][c] for j in range(chips - 1)] for c in range(chunks)]
     turns = []
     arrival = 2.0
@@ -382,23 +390,21 @@
         share = 16.0 * counts[c] / width
         arrival += share
         when = arrival
-        for i, (_, moves) in enumerate(plan[c]):
+        for i in range(len(plan[c])):
             turns.append((when, c, i))
-            if moves is not None:
-                full = 1.0 if c == chunks - 1 else 0.5
-                when += 1.7 + share * full * len(moves)
+            when += 2.2 + share * (1.0 if i == len(plan[c]) - 3 else 0.5)
     results = [None] * chunks
     last = None
     for _, c, i in sorted(turns):
-        compute, moves = plan[c][i]
+        compute, move = plan[c][i]
         fetched = inbox[c]
         if last is not None:
             fetched, last = tied(fetched, last)
         out = compute(fetched)
-        if moves is None:
+        if move is None:
             results[c] = out
         else:
-            inbox[c] = [move(out) for move in moves]
+            inbox[c] = [move(out)]
             last = out
     return jnp.concatenate(results, axis=1)[None]
 

time: 104 us -> 97.7 us (0.939)
  the two profiles are of different devices: /device:TPU:26 before, /device:TPU:30 now
where the time goes in v5:
time: 97.7 us; the launch traced here: 97.3 us
  waiting for transfers between devices  44.6 us (46%)
  Pallas kernels  29.6 us (30%)
  starting transfers between devices  14 us (14%)
  other arithmetic  5.81 us (6%)
  local copies, waits for them, and re-layouts  2.33 us (2%)
  between operations  1.07 us (1%)
    ppermute x6, waiting for transfers between devices, along(): lax.ppermute(x, 'step', [(2 * a + i, 2 * b + i) for a, b in pairs for i i...  20.2 us
    pallas_call x2, Pallas kernels, project_call(): pl.pallas_call(functools.partial(project_kernel, tile, load, tiles), in_s...  13.8 us
    ppermute x4, waiting for transfers between devices, to_chip(): lax.ppermute(x, 'seq', [(i, (i + 2 * offset) % n_seq) for i in range(n_se...  10.9 us
    ppermute x6, waiting for transfers between devices, to_pair(): return lax.ppermute(x, 'step', [(i, i ^ 1) for i in range(n_step)])  9.09 us
    pallas_call x5, Pallas kernels, out_call(): pl.pallas_call(functools.partial(out_kernel, first, len(xs)), in_specs=[v...  8.28 us
    ppermute x6, starting transfers between devices, along(): lax.ppermute(x, 'step', [(2 * a + i, 2 * b + i) for a, b in pairs for i i...  5.26 us
    ppermute x6, starting transfers between devices, to_pair(): return lax.ppermute(x, 'step', [(i, i ^ 1) for i in range(n_step)])  4.64 us
    ppermute x6, waiting for transfers between devices, to_core(): return lax.ppermute(x, 'seq', [(i, i ^ 1) for i in range(n_seq)])  4.36 us
  transfers between devices with their start and end apart: 22, of which 17 were waited for; matrix products, arithmetic and copies ran while one was open for 4% of the time, Pallas kernels for 18%

profile of v5, /device:TPU:30, one launch (start us, length us, event | category | flops | bytes accessed | tf_op | source)
XLA Modules:
  0.0 97.3 jit_solution(17769084744542534304)
XLA Ops:
  0.7 4.1 %norm.1 = (bf16[128,3072]{1,0:T(8,128)(2,1)}, f32[1,3072]{1,0:T(1,128)}) custom-call(s32[1]{0:T(128)S(6)} %copy.12.t_ref, f32[1,128,3072]{2,1,0:T(8,128)} %x_hbm.1, f32[50,9216]{1,0:T(8,128)} %mod_ref.1, f32[50]{0:T(128)} %size_ref.1), custom_call_target="tpu_custom_call" | custom-call | flops 3932160 | tf_op jit(solution)/shard_map/norm/pallas_call | solution.py:51
  4.8 0.1 collective-permute-start.1
  4.8 0.6 collective-permute-start
  5.4 1.9 %collective-permute-done.1.m1 = bf16[128,3072]{1,0:T(8,128)(2,1)S(1)} collective-permute-done((bf16[128,3072]{1,0:T(8,128)(2,1)}, bf16[128,3072]{1,0:T(8,128)(2,1)S(1)}, u32[]{:S(2)}, u32[]{:S(2)}) %collective-permute-start.1) | collective-permute-done | bytes 786464 | tf_op jit(solution)/shard_map/ppermute | solution.py:252
  7.3 1.1 %copy-done.1 = bf16[128,3072]{1,0:T(8,128)(2,1)S(1)} copy-done((bf16[128,3072]{1,0:T(8,128)(2,1)S(1)}, bf16[128,3072]{1,0:T(8,128)(2,1)}, u32[]{:S(2)}) %copy-start.1) | copy-done | bytes 786456
  8.5 8.6 %project.2 = (bf16[256,512]{1,0:T(8,128)(2,1)S(1)}, bf16[256,512]{1,0:T(8,128)(2,1)S(1)}, bf16[256,512]{1,0:T(8,128)(2,1)S(1)}, bf16[256,1536]{1,0:T(8,128)(2,1)...) custom-call(bf16[128,3072]{1,0:T(8,128)(2,1)S(1)} %copy-done.1, ...), custom_call_target="tpu_custom_call" | custom-call | flops 4831838208 | tf_op jit(solution)/shard_map/project/pallas_call | solution.py:139
  17.1 0.3 slice-done.2
  17.4 2.6 %project_out.5 = (f32[128,3072]{1,0:T(8,128)S(1)}, f32[128,3072]{1,0:T(8,128)S(1)}) custom-call(bf16[256,1536]{1,0:T(8,128)(2,1)S(1)} %get-tuple-element.67.refs_0_, bf16[1536,3072]{1,0:T(8,128)(2,1)S(1)} %bitcast.6), custom_call_target="tpu_custom_call" | custom-call | flops 2415919104 | tf_op jit(solution)/shard_map/project_out/pallas_call | solution.py:211
  20.0 5.0 %collective-permute-done.m0 = bf16[128,3072]{1,0:T(8,128)(2,1)S(1)} collective-permute-done((bf16[128,3072]{1,0:T(8,128)(2,1)}, bf16[128,3072]{1,0:T(8,128)(2,1)S(1)}, u32[]{:S(2)}, u32[]{:S(2)}) %collective-permute-start) | collective-permute-done | bytes 786464 | tf_op jit(solution)/shard_map/ppermute | solution.py:255
  25.0 2.3 %collective-permute-done.2.m1 = bf16[128,3072]{1,0:T(8,128)(2,1)S(1)} collective-permute-done((bf16[128,3072]{1,0:T(8,128)(2,1)S(1)}, bf16[128,3072]{1,0:T(8,128)(2,1)S(1)}, u32[]{:S(2)}, u32[]{:S(2)}) %collective-permute-start.2) | collective-permute-done | bytes 786464 | tf_op jit(solution)/shard_map/ppermute | solution.py:252
  27.3 5.2 %project.3 = (bf16[256,512]{1,0:T(8,128)(2,1)S(1)}, bf16[256,512]{1,0:T(8,128)(2,1)S(1)}, bf16[256,512]{1,0:T(8,128)(2,1)S(1)}, bf16[256,1536]{1,0:T(8,128)(2,1)S(1)}) custom-call(bf16[128,3072]{1,0:T(8,128)(2,1)S(1)} %collective-permute-done.m0, bf16[128,3072]{1,0:T(8,128)(2,1)S(1)} %collective-permute-done.2.m1, f32[1,128]{1,0:T(1,128)S(1)} %bitcast.8, ...), custom_call_target="tpu_custom_call" | custom-call | flops 4831838208 | tf_op jit(solution)/shard_map/project/pallas_call | solution.py:139
  32.5 1.7 %attend.2.refs_0_ = bf16[256,512]{1,0:T(8,128)(2,1)S(1)} custom-call(bf16[256,512]{1,0:T(8,128)(2,1)S(1)} %get-tuple-element.77.refs_0_, bf16[256,512]{1,0:T(8,128)(2,1)S(1)} %get-tuple-element.78.refs_1_, bf16[256,512]{1,0:T(8,128)(2,1)S(1)} %get-tuple-element.79.refs_2_, bf16[256,512]{1,0:T(8,128)(2,1)S(1)} %get-tuple-element.80.refs_3_, ...), custom_call_target="tpu_custom_call" | custom-call | flops 805306368 | tf_op jit(solution)/shard_map/attend/pallas_call | solution.py:179
  34.2 1.2 %project_out.6 = (f32[128,768]{1,0:T(8,128)S(1)}, bf16[128,768]{1,0:T(8,128)(2,1)S(1)}) custom-call(bf16[256,512]{1,0:T(8,128)(2,1)S(1)} %attend.2.refs_0_, bf16[256,1536]{1,0:T(8,128)(2,1)S(1)} %get-tuple-element.96.refs_1_, bf16[512,3072]{1,0:T(8,128)(2,1)S(1)} %copy-done, bf16[1536,3072]{1,0:T(8,128)(2,1)S(1)} %bitcast.6), custom_call_target="tpu_custom_call" | custom-call | flops 805306368 | tf_op jit(solution)/shard_map/project_out/pallas_call | solution.py:211
  35.4 0.2 collective-permute-start.3
  35.6 1.7 %attend.3.refs_0_ = bf16[256,512]{1,0:T(8,128)(2,1)S(1)} custom-call(bf16[256,512]{1,0:T(8,128)(2,1)S(1)} %get-tuple-element.86.refs_0_, bf16[256,512]{1,0:T(8,128)(2,1)S(1)} %get-tuple-element.78.refs_1_, bf16[256,512]{1,0:T(8,128)(2,1)S(1)} %get-tuple-element.79.refs_2_, bf16[256,512]{1,0:T(8,128)(2,1)S(1)} %get-tuple-element.80.refs_3_, ...), custom_call_target="tpu_custom_call" | custom-call | flops 805306368 | tf_op jit(solution)/shard_map/attend/pallas_call | solution.py:179
  37.4 0.6 collective-permute-start.4
  38.0 2.3 %project_out.7 = (f32[128,1280]{1,0:T(8,128)S(1)}, bf16[128,1280]{1,0:T(8,128)(2,1)}) custom-call(bf16[256,512]{1,0:T(8,128)(2,1)S(1)} %attend.2.refs_0_, bf16[256,1536]{1,0:T(8,128)(2,1)S(1)} %get-tuple-element.96.refs_1_, bf16[512,3072]{1,0:T(8,128)(2,1)S(1)} %copy-done, bf16[1536,3072]{1,0:T(8,128)(2,1)S(1)} %bitcast.6), custom_call_target="tpu_custom_call" | custom-call | flops 1342177280 | tf_op jit(solution)/shard_map/project_out/pallas_call | solution.py:211
  40.3 1.2 %project_out.8 = (f32[128,1024]{1,0:T(8,128)S(1)}, bf16[128,1024]{1,0:T(8,128)(2,1)S(1)}) custom-call(bf16[256,512]{1,0:T(8,128)(2,1)S(1)} %attend.2.refs_0_, bf16[256,1536]{1,0:T(8,128)(2,1)S(1)} %get-tuple-element.96.refs_1_, bf16[512,3072]{1,0:T(8,128)(2,1)S(1)} %copy-done, bf16[1536,3072]{1,0:T(8,128)(2,1)S(1)} %bitcast.6), custom_call_target="tpu_custom_call" | custom-call | flops 1073741824 | tf_op jit(solution)/shard_map/project_out/pallas_call | solution.py:211
  41.6 0.7 copy-done.4
  42.3 2.4 %collective-permute-done.4 = bf16[128,768]{1,0:T(8,128)(2,1)} collective-permute-done((bf16[128,768]{1,0:T(8,128)(2,1)S(1)}, bf16[128,768]{1,0:T(8,128)(2,1)}, u32[]{:S(2)}, u32[]{:S(2)}) %collective-permute-start.4) | collective-permute-done | bytes 196640 | tf_op jit(solution)/shard_map/ppermute | solution.py:255
  44.7 1.0 %project_out.9 = (f32[128,3072]{1,0:T(8,128)S(1)}, bf16[128,3072]{1,0:T(8,128)(2,1)S(1)}) custom-call(bf16[256,512]{1,0:T(8,128)(2,1)S(1)} %attend.3.refs_0_, bf16[512,3072]{1,0:T(8,128)(2,1)S(1)} %copy-done, f32[128,3072]{1,0:T(8,128)S(1)} %get-tuple-element.103.refs_2_, f32[128,3072]{1,0:T(8,128)S(1)} %get-tuple-element.104.refs_3_), custom_call_target="tpu_custom_call" | custom-call | flops 805306368 | tf_op jit(solution)/shard_map/project_out/pallas_call | solution.py:211
  45.8 0.1 collective-permute-start.6
  46.0 0.5 collective-permute-start.12
  46.4 1.0 %add_convert_fusion = bf16[128,1280]{1,0:T(8,128)(2,1)S(1)} fusion(f32[128,1280]{1,0:T(8,128)S(1)} %get-tuple-element.111, bf16[128,1280]{1,0:T(8,128)(2,1)} %collective-permute-done.5), kind=kLoop, calls=%fused_computation.5 | loop fusion | flops 491520 | bytes 1310720 | tf_op jit(solution)/shard_map/convert_element_type | solution.py:292
  47.5 0.6 collective-permute-start.9
  48.1 0.2 collective-permute-done.6
  48.2 1.3 %convert_add_fusion = f32[128,3072]{1,0:T(8,128)S(1)} fusion(f32[128,3072]{1,0:T(8,128)S(1)} %get-tuple-element.107, bf16[128,3072]{1,0:T(8,128)(2,1)} %collective-permute-done.6), kind=kLoop, calls=%fused_computation.1 | loop fusion | flops 786432 | bytes 3932160 | tf_op jit(solution)/shard_map/add | solution.py:319
  49.5 1.0 %fusion.2 = f32[128,768]{1,0:T(8,128)S(1)} fusion(f32[128,3072]{1,0:T(8,128)S(1)} %convert_add_fusion, bf16[128,768]{1,0:T(8,128)(2,1)} %collective-permute-done.4, f32[768]{0:T(1024)S(1)} %slice_reduce_fusion.1), kind=kLoop, calls=%fused_computation.15 | loop fusion | flops 294912 | bytes 986112 | tf_op jit(solution)/shard_map/mul | solution.py:342
  50.5 0.6 collective-permute-start.7
  51.2 0.1 add_convert_fusion.1
  51.2 1.4 %collective-permute-start.13 = (bf16[128,1024]{1,0:T(8,128)(2,1)S(1)}, bf16[128,1024]{1,0:T(8,128)(2,1)S(1)}, u32[]{:S(2)}, u32[]{:S(2)}) collective-permute-start(bf16[128,1024]{1,0:T(8,128)(2,1)S(1)} %add_convert_fusion.1), channel_id=1, source_target_pairs={{0,2},{1,3},{2,0},{3,1},{4,6},{5,7},{6,4},{7,5},{8,10},{9,11},{10,... | collective-permute-start | bytes 786440 | tf_op jit(solution)/shard_map/ppermute | solution.py:255
  52.6 2.8 %collective-permute-done.7 = bf16[64,768]{1,0:T(8,128)(2,1)S(1)} collective-permute-done((bf16[64,768]{1,0:T(8,128)(2,1)S(1)}, bf16[64,768]{1,0:T(8,128)(2,1)S(1)}, u32[]{:S(2)}, u32[]{:S(2)}) %collective-permute-start.7) | collective-permute-done | bytes 98336 | tf_op jit(solution)/shard_map/ppermute | solution.py:258
  55.5 0.5 collective-permute-start.8
  56.0 2.1 %collective-permute-done.9 = bf16[128,1280]{1,0:T(8,128)(2,1)S(1)} collective-permute-done((bf16[128,1280]{1,0:T(8,128)(2,1)S(1)}, bf16[128,1280]{1,0:T(8,128)(2,1)S(1)}, u32[]{:S(2)}, u32[]{:S(2)}) %collective-permute-start.9) | collective-permute-done | bytes 327712 | tf_op jit(solution)/shard_map/ppermute | solution.py:255
  58.1 0.1 fusion
  58.2 0.6 collective-permute-start.11
  58.9 1.3 %collective-permute-done.8 = bf16[64,768]{1,0:T(8,128)(2,1)S(1)} collective-permute-done((bf16[64,768]{1,0:T(8,128)(2,1)S(1)}, bf16[64,768]{1,0:T(8,128)(2,1)S(1)}, u32[]{:S(2)}, u32[]{:S(2)}) %collective-permute-start.8) | collective-permute-done | bytes 98336 | tf_op jit(solution)/shard_map/ppermute | solution.py:322
  60.2 1.3 %collective-permute-start.10 = (bf16[64,768]{1,0:T(8,128)(2,1)S(1)}, bf16[64,768]{1,0:T(8,128)(2,1)S(1)}, u32[]{:S(2)}, u32[]{:S(2)}) collective-permute-start(bf16[64,768]{1,0:T(8,128)(2,1)S(1)} %fusion.14), channel_id=1, source_target_pairs={{0,16},{4,20},{8,24},{12,28},{1,17},{5,21},{9,25},{13,29},{2,18},{... | collective-permute-start | bytes 294920 | tf_op jit(solution)/shard_map/ppermute | solution.py:322
  61.5 1.4 %collective-permute-done.13 = bf16[128,1024]{1,0:T(8,128)(2,1)S(1)} collective-permute-done((bf16[128,1024]{1,0:T(8,128)(2,1)S(1)}, bf16[128,1024]{1,0:T(8,128)(2,1)S(1)}, u32[]{:S(2)}, u32[]{:S(2)}) %collective-permute-start.13) | collective-permute-done | bytes 262176 | tf_op jit(solution)/shard_map/ppermute | solution.py:255
  62.9 0.1 fusion.1
  63.0 0.6 collective-permute-start.16
  63.7 0.5 collective-permute-start.15
  64.2 4.5 %collective-permute-done.10 = bf16[64,768]{1,0:T(8,128)(2,1)S(1)} collective-permute-done((bf16[64,768]{1,0:T(8,128)(2,1)S(1)}, bf16[64,768]{1,0:T(8,128)(2,1)S(1)}, u32[]{:S(2)}, u32[]{:S(2)}) %collective-permute-start.10) | collective-permute-done | bytes 98336 | tf_op jit(solution)/shard_map/ppermute | solution.py:322
  68.7 0.6 collective-permute-start.14
  69.4 0.2 collective-permute-start.18
  69.6 2.0 %collective-permute-done.15 = bf16[64,1280]{1,0:T(8,128)(2,1)S(1)} collective-permute-done((bf16[64,1280]{1,0:T(8,128)(2,1)S(1)}, bf16[64,1280]{1,0:T(8,128)(2,1)S(1)}, u32[]{:S(2)}, u32[]{:S(2)}) %collective-permute-start.15) | collective-permute-done | bytes 163872 | tf_op jit(solution)/shard_map/ppermute | solution.py:322
  71.6 1.4 %collective-permute-start.17 = (bf16[64,1280]{1,0:T(8,128)(2,1)S(1)}, bf16[64,1280]{1,0:T(8,128)(2,1)S(1)}, u32[]{:S(2)}, u32[]{:S(2)}) collective-permute-start(bf16[64,1280]{1,0:T(8,128)(2,1)S(1)} %fusion.4), channel_id=1, source_target_pairs={{0,16},{4,20},{8,24},{12,28},{1,17},{5,21},{9,25},{13,29},{2,18},{... | collective-permute-start | bytes 491528 | tf_op jit(solution)/shard_map/ppermute | solution.py:322
  73.0 0.4 collective-permute-done.14
  73.4 0.1 fusion.19
  73.5 0.9 collective-permute-done.18
  74.4 1.3 %collective-permute-start.20 = (bf16[64,1024]{1,0:T(8,128)(2,1)S(1)}, bf16[64,1024]{1,0:T(8,128)(2,1)S(1)}, u32[]{:S(2)}, u32[]{:S(2)}) collective-permute-start(bf16[64,1024]{1,0:T(8,128)(2,1)S(1)} %fusion.7), channel_id=1, source_target_pairs={{0,16},{4,20},{8,24},{12,28},{1,17},{5,21},{9,25},{13,29},{2,18},{... | collective-permute-start | bytes 393224 | tf_op jit(solution)/shard_map/ppermute | solution.py:322
  75.7 9.6 %collective-permute-done.17 = bf16[64,1280]{1,0:T(8,128)(2,1)S(1)} collective-permute-done((bf16[64,1280]{1,0:T(8,128)(2,1)S(1)}, bf16[64,1280]{1,0:T(8,128)(2,1)S(1)}, u32[]{:S(2)}, u32[]{:S(2)}) %collective-permute-start.17) | collective-permute-done | bytes 163872 | tf_op jit(solution)/shard_map/ppermute | solution.py:322
  85.3 0.1 add_convert_fusion.3
  85.4 2.0 %collective-permute-done.20 = bf16[64,1024]{1,0:T(8,128)(2,1)S(1)} collective-permute-done((bf16[64,1024]{1,0:T(8,128)(2,1)S(1)}, bf16[64,1024]{1,0:T(8,128)(2,1)S(1)}, u32[]{:S(2)}, u32[]{:S(2)}) %collective-permute-start.20) | collective-permute-done | bytes 131104 | tf_op jit(solution)/shard_map/ppermute | solution.py:322
  87.4 0.1 add_convert_fusion.4
  87.5 0.5 collective-permute-start.21
  88.0 0.1 maximum_add_fusion.2
  88.1 1.6 %collective-permute-start.19 = (bf16[64,1280]{1,0:T(8,128)(2,1)S(1)}, bf16[64,1280]{1,0:T(8,128)(2,1)S(1)}, u32[]{:S(2)}, u32[]{:S(2)}) collective-permute-start(bf16[64,1280]{1,0:T(8,128)(2,1)S(1)} %add_convert_fusion.3), channel_id=1, source_target_pairs={{0,4},{4,0},{8,12},{12,8},{16,20},{20,16},{24,28},{28,24},{1,5},{5... | collective-permute-start | bytes 491528 | tf_op jit(solution)/shard_map/ppermute | solution.py:258
  89.7 4.3 %collective-permute-done.21 = bf16[64,1024]{1,0:T(8,128)(2,1)S(1)} collective-permute-done((bf16[64,1024]{1,0:T(8,128)(2,1)S(1)}, bf16[64,1024]{1,0:T(8,128)(2,1)S(1)}, u32[]{:S(2)}, u32[]{:S(2)}) %collective-permute-start.21) | collective-permute-done | bytes 131104 | tf_op jit(solution)/shard_map/ppermute | solution.py:258
  94.0 0.1 fusion.16
  94.2 1.6 %collective-permute-done.19 = bf16[64,1280]{1,0:T(8,128)(2,1)S(1)} collective-permute-done((bf16[64,1280]{1,0:T(8,128)(2,1)S(1)}, bf16[64,1280]{1,0:T(8,128)(2,1)S(1)}, u32[]{:S(2)}, u32[]{:S(2)}) %collective-permute-start.19) | collective-permute-done | bytes 163872 | tf_op jit(solution)/shard_map/ppermute | solution.py:258
  95.8 0.1 fusion.10
  96.0 0.1 maximum_add_fusion
  96.0 1.3 %maximum_bitcast_fusion = f32[1,128,3072]{2,1,0:T(8,128)} fusion(f32[128,1024]{1,0:T(8,128)S(1)} %maximum_add_fusion.1, f32[128,1280]{1,0:T(8,128)S(1)} %maximum_add_fusion, f32[128,768]{1,0:T(8,128)S(1)} %maximum_add_fusion.2), kind=kLoop, calls=%fused_computation | loop fusion | flops 786432 | bytes 3145728 | tf_op jit(solution)/shard_map/broadcast_in_dim | solution.py:409
  (40 shorter events, 0.6 us)
Async XLA Ops:
  0.7 6.7 %copy-start.2 = (f32[128]{0:T(128)S(1)}, f32[128]{0:T(128)}, u32[]{:S(2)}) copy-start(f32[128]{0:T(128)} %param.16) | copy-start | bytes 1540
  0.7 6.7 %copy-start.3 = (f32[128]{0:T(128)S(1)}, f32[128]{0:T(128)}, u32[]{:S(2)}) copy-start(f32[128]{0:T(128)} %param.17) | copy-start | bytes 1540
  0.7 16.4 %slice-start = ((s8[9437184]{0:T(1024)(128)(4,1)}), s8[1048576]{0:T(1024)(128)(4,1)S(1)}, s32[]{:S(2)}) async-start(s8[9437184]{0:T(1024)(128)(4,1)} %bitcast.5), calls=%async_computation | async-start | bytes 2097152
  4.8 2.6 %collective-permute-start.1 = (bf16[128,3072]{1,0:T(8,128)(2,1)}, bf16[128,3072]{1,0:T(8,128)(2,1)S(1)}, u32[]{:S(2)}, u32[]{:S(2)}) collective-permute-start(bf16[128,3072]{1,0:T(8,128)(2,1)} %get-tuple-element.66.m0), channel_id=1, source_target_pairs={{0,1},{1,0},{2,3},{3,2},{4,5},{5,4},{6,7},{7,6},{8,9},{9,8},{10,11... | collective-permute-start | bytes 2359304 | tf_op jit(solution)/shard_map/ppermute | solution.py:252
  4.8 20.2 %collective-permute-start = (bf16[128,3072]{1,0:T(8,128)(2,1)}, bf16[128,3072]{1,0:T(8,128)(2,1)S(1)}, u32[]{:S(2)}, u32[]{:S(2)}) collective-permute-start(bf16[128,3072]{1,0:T(8,128)(2,1)} %get-tuple-element.66.m0), channel_id=1, source_target_pairs={{0,2},{1,3},{2,0},{3,1},{4,6},{5,7},{6,4},{7,5},{8,10},{9,11},{10,... | collective-permute-start | bytes 2359304 | tf_op jit(solution)/shard_map/ppermute | solution.py:255
  7.3 1.1 %copy-start.1 = (bf16[128,3072]{1,0:T(8,128)(2,1)S(1)}, bf16[128,3072]{1,0:T(8,128)(2,1)}, u32[]{:S(2)}) copy-start(bf16[128,3072]{1,0:T(8,128)(2,1)} %get-tuple-element.66.m0) | copy-start | bytes 2359300
  8.5 8.6 %slice-start.1 = ((s8[9437184]{0:T(1024)(128)(4,1)}), s8[4194304]{0:T(1024)(128)(4,1)S(1)}, s32[]{:S(2)}) async-start(s8[9437184]{0:T(1024)(128)(4,1)} %bitcast.5), calls=%async_computation.1 | async-start | bytes 8388608
  8.5 8.9 %slice-start.2 = ((s8[9437184]{0:T(1024)(128)(4,1)}), s8[4194304]{0:T(1024)(128)(4,1)S(1)}, s32[]{:S(2)}) async-start(s8[9437184]{0:T(1024)(128)(4,1)} %bitcast.5), calls=%async_computation.2 | async-start | bytes 8388608
  25.0 2.3 %collective-permute-start.2 = (bf16[128,3072]{1,0:T(8,128)(2,1)S(1)}, bf16[128,3072]{1,0:T(8,128)(2,1)S(1)}, u32[]{:S(2)}, u32[]{:S(2)}) collective-permute-start(bf16[128,3072]{1,0:T(8,128)(2,1)S(1)} %collective-permute-done.m0), channel_id=1, source_target_pairs={{0,1},{1,0},{2,3},{3,2},{4,5},{5,4},{6,7},{7,6},{8,9},{9,8},{10,11... | collective-permute-start | bytes 2359304 | tf_op jit(solution)/shard_map/ppermute | solution.py:252
  27.3 6.9 %copy-start = (bf16[512,3072]{1,0:T(8,128)(2,1)S(1)}, bf16[512,3072]{1,0:T(8,128)(2,1)}, u32[]{:S(2)}) copy-start(bf16[512,3072]{1,0:T(8,128)(2,1)} %refs_1_.5) | copy-start | bytes 9437188
  35.4 1.9 %collective-permute-start.3 = (bf16[128,768]{1,0:T(8,128)(2,1)S(1)}, bf16[128,768]{1,0:T(8,128)(2,1)S(1)}, u32[]{:S(2)}, u32[]{:S(2)}) collective-permute-start(bf16[128,768]{1,0:T(8,128)(2,1)S(1)} %get-tuple-element.85), channel_id=1, source_target_pairs={{0,1},{1,0},{2,3},{3,2},{4,5},{5,4},{6,7},{7,6},{8,9},{9,8},{10,11... | collective-permute-start | bytes 589832 | tf_op jit(solution)/shard_map/ppermute | solution.py:252
  37.4 7.3 %collective-permute-start.4 = (bf16[128,768]{1,0:T(8,128)(2,1)S(1)}, bf16[128,768]{1,0:T(8,128)(2,1)}, u32[]{:S(2)}, u32[]{:S(2)}) collective-permute-start(bf16[128,768]{1,0:T(8,128)(2,1)S(1)} %add_convert_fusion.2), channel_id=1, source_target_pairs={{0,2},{1,3},{2,0},{3,1},{4,6},{5,7},{6,4},{7,5},{8,10},{9,11},{10,... | collective-permute-start | bytes 589832 | tf_op jit(solution)/shard_map/ppermute | solution.py:255
  40.3 6.2 %collective-permute-start.5 = (bf16[128,1280]{1,0:T(8,128)(2,1)}, bf16[128,1280]{1,0:T(8,128)(2,1)}, u32[]{:S(2)}, u32[]{:S(2)}) collective-permute-start(bf16[128,1280]{1,0:T(8,128)(2,1)} %get-tuple-element.94), channel_id=1, source_target_pairs={{0,1},{1,0},{2,3},{3,2},{4,5},{5,4},{6,7},{7,6},{8,9},{9,8},{10,11... | collective-permute-start | bytes 983048 | tf_op jit(solution)/shard_map/ppermute | solution.py:252
  41.6 0.7 copy-start.4
  42.3 3.6 %copy-start.6 = (f32[1,3072]{1,0:T(1,128)S(1)}, f32[1,3072]{1,0:T(1,128)}, u32[]{:S(2)}) copy-start(f32[1,3072]{1,0:T(1,128)} %get-tuple-element.65) | copy-start | bytes 36868
  45.8 2.5 %collective-permute-start.6 = (bf16[128,3072]{1,0:T(8,128)(2,1)S(1)}, bf16[128,3072]{1,0:T(8,128)(2,1)}, u32[]{:S(2)}, u32[]{:S(2)}) collective-permute-start(bf16[128,3072]{1,0:T(8,128)(2,1)S(1)} %get-tuple-element.108), channel_id=1, source_target_pairs={{0,1},{1,0},{2,3},{3,2},{4,5},{5,4},{6,7},{7,6},{8,9},{9,8},{10,11... | collective-permute-start | bytes 2359304 | tf_op jit(solution)/shard_map/ppermute | solution.py:252
  46.0 5.2 %collective-permute-start.12 = (bf16[128,1024]{1,0:T(8,128)(2,1)}, bf16[128,1024]{1,0:T(8,128)(2,1)S(1)}, u32[]{:S(2)}, u32[]{:S(2)}) collective-permute-start(bf16[128,1024]{1,0:T(8,128)(2,1)} %copy-done.4), channel_id=1, source_target_pairs={{0,1},{1,0},{2,3},{3,2},{4,5},{5,4},{6,7},{7,6},{8,9},{9,8},{10,11... | collective-permute-start | bytes 786440 | tf_op jit(solution)/shard_map/ppermute | solution.py:252
  47.5 10.6 %collective-permute-start.9 = (bf16[128,1280]{1,0:T(8,128)(2,1)S(1)}, bf16[128,1280]{1,0:T(8,128)(2,1)S(1)}, u32[]{:S(2)}, u32[]{:S(2)}) collective-permute-start(bf16[128,1280]{1,0:T(8,128)(2,1)S(1)} %add_convert_fusion), channel_id=1, source_target_pairs={{0,2},{1,3},{2,0},{3,1},{4,6},{5,7},{6,4},{7,5},{8,10},{9,11},{10,... | collective-permute-start | bytes 983048 | tf_op jit(solution)/shard_map/ppermute | solution.py:255
  50.5 4.9 %collective-permute-start.7 = (bf16[64,768]{1,0:T(8,128)(2,1)S(1)}, bf16[64,768]{1,0:T(8,128)(2,1)S(1)}, u32[]{:S(2)}, u32[]{:S(2)}) collective-permute-start(bf16[64,768]{1,0:T(8,128)(2,1)S(1)} %dynamic-slice_convert_fusion.2), channel_id=1, source_target_pairs={{0,4},{4,0},{8,12},{12,8},{16,20},{20,16},{24,28},{28,24},{1,5},{5... | collective-permute-start | bytes 294920 | tf_op jit(solution)/shard_map/ppermute | solution.py:258
  51.2 11.6 %collective-permute-start.13 = (bf16[128,1024]{1,0:T(8,128)(2,1)S(1)}, bf16[128,1024]{1,0:T(8,128)(2,1)S(1)}, u32[]{:S(2)}, u32[]{:S(2)}) collective-permute-start(bf16[128,1024]{1,0:T(8,128)(2,1)S(1)} %add_convert_fusion.1), channel_id=1, source_target_pairs={{0,2},{1,3},{2,0},{3,1},{4,6},{5,7},{6,4},{7,5},{8,10},{9,11},{10,... | collective-permute-start | bytes 786440 | tf_op jit(solution)/shard_map/ppermute | solution.py:255
  55.5 4.7 %collective-permute-start.8 = (bf16[64,768]{1,0:T(8,128)(2,1)S(1)}, bf16[64,768]{1,0:T(8,128)(2,1)S(1)}, u32[]{:S(2)}, u32[]{:S(2)}) collective-permute-start(bf16[64,768]{1,0:T(8,128)(2,1)S(1)} %fusion.20), channel_id=1, source_target_pairs={{0,8},{4,12},{8,0},{12,4},{16,24},{20,28},{24,16},{28,20},{1,9},{5... | collective-permute-start | bytes 294920 | tf_op jit(solution)/shard_map/ppermute | solution.py:322
  58.2 5.4 %collective-permute-start.11 = (bf16[64,1280]{1,0:T(8,128)(2,1)S(1)}, bf16[64,1280]{1,0:T(8,128)(2,1)S(1)}, u32[]{:S(2)}, u32[]{:S(2)}) collective-permute-start(bf16[64,1280]{1,0:T(8,128)(2,1)S(1)} %dynamic-slice_convert_fusion), channel_id=1, source_target_pairs={{0,4},{4,0},{8,12},{12,8},{16,20},{20,16},{24,28},{28,24},{1,5},{5... | collective-permute-start | bytes 491528 | tf_op jit(solution)/shard_map/ppermute | solution.py:258
  60.2 8.5 %collective-permute-start.10 = (bf16[64,768]{1,0:T(8,128)(2,1)S(1)}, bf16[64,768]{1,0:T(8,128)(2,1)S(1)}, u32[]{:S(2)}, u32[]{:S(2)}) collective-permute-start(bf16[64,768]{1,0:T(8,128)(2,1)S(1)} %fusion.14), channel_id=1, source_target_pairs={{0,16},{4,20},{8,24},{12,28},{1,17},{5,21},{9,25},{13,29},{2,18},{... | collective-permute-start | bytes 294920 | tf_op jit(solution)/shard_map/ppermute | solution.py:322
  63.0 6.3 %collective-permute-start.16 = (bf16[64,1024]{1,0:T(8,128)(2,1)S(1)}, bf16[64,1024]{1,0:T(8,128)(2,1)S(1)}, u32[]{:S(2)}, u32[]{:S(2)}) collective-permute-start(bf16[64,1024]{1,0:T(8,128)(2,1)S(1)} %dynamic-slice_convert_fusion.1), channel_id=1, source_target_pairs={{0,4},{4,0},{8,12},{12,8},{16,20},{20,16},{24,28},{28,24},{1,5},{5... | collective-permute-start | bytes 393224 | tf_op jit(solution)/shard_map/ppermute | solution.py:258
  63.7 7.9 %collective-permute-start.15 = (bf16[64,1280]{1,0:T(8,128)(2,1)S(1)}, bf16[64,1280]{1,0:T(8,128)(2,1)S(1)}, u32[]{:S(2)}, u32[]{:S(2)}) collective-permute-start(bf16[64,1280]{1,0:T(8,128)(2,1)S(1)} %fusion.11), channel_id=1, source_target_pairs={{0,8},{4,12},{8,0},{12,4},{16,24},{20,28},{24,16},{28,20},{1,9},{5... | collective-permute-start | bytes 491528 | tf_op jit(solution)/shard_map/ppermute | solution.py:322
  68.7 4.7 %collective-permute-start.14 = (bf16[64,768]{1,0:T(8,128)(2,1)S(1)}, bf16[64,768]{1,0:T(8,128)(2,1)S(1)}, u32[]{:S(2)}, u32[]{:S(2)}) collective-permute-start(bf16[64,768]{1,0:T(8,128)(2,1)S(1)} %add_convert_fusion.5), channel_id=1, source_target_pairs={{0,4},{4,0},{8,12},{12,8},{16,20},{20,16},{24,28},{28,24},{1,5},{5... | collective-permute-start | bytes 294920 | tf_op jit(solution)/shard_map/ppermute | solution.py:258
  69.4 5.0 %collective-permute-start.18 = (bf16[64,1024]{1,0:T(8,128)(2,1)S(1)}, bf16[64,1024]{1,0:T(8,128)(2,1)S(1)}, u32[]{:S(2)}, u32[]{:S(2)}) collective-permute-start(bf16[64,1024]{1,0:T(8,128)(2,1)S(1)} %fusion.17), channel_id=1, source_target_pairs={{0,8},{4,12},{8,0},{12,4},{16,24},{20,28},{24,16},{28,20},{1,9},{5... | collective-permute-start | bytes 393224 | tf_op jit(solution)/shard_map/ppermute | solution.py:322
  71.6 16.4 %copy-start.5 = (f32[128,3072]{1,0:T(8,128)S(1)}, f32[128,3072]{1,0:T(8,128)}, u32[]{:S(2)}) copy-start(f32[128,3072]{1,0:T(8,128)} %param.12) | copy-start | bytes 4718596
  71.6 13.7 %collective-permute-start.17 = (bf16[64,1280]{1,0:T(8,128)(2,1)S(1)}, bf16[64,1280]{1,0:T(8,128)(2,1)S(1)}, u32[]{:S(2)}, u32[]{:S(2)}) collective-permute-start(bf16[64,1280]{1,0:T(8,128)(2,1)S(1)} %fusion.4), channel_id=1, source_target_pairs={{0,16},{4,20},{8,24},{12,28},{1,17},{5,21},{9,25},{13,29},{2,18},{... | collective-permute-start | bytes 491528 | tf_op jit(solution)/shard_map/ppermute | solution.py:322
  74.4 13.0 %collective-permute-start.20 = (bf16[64,1024]{1,0:T(8,128)(2,1)S(1)}, bf16[64,1024]{1,0:T(8,128)(2,1)S(1)}, u32[]{:S(2)}, u32[]{:S(2)}) collective-permute-start(bf16[64,1024]{1,0:T(8,128)(2,1)S(1)} %fusion.7), channel_id=1, source_target_pairs={{0,16},{4,20},{8,24},{12,28},{1,17},{5,21},{9,25},{13,29},{2,18},{... | collective-permute-start | bytes 393224 | tf_op jit(solution)/shard_map/ppermute | solution.py:322
  87.5 6.5 %collective-permute-start.21 = (bf16[64,1024]{1,0:T(8,128)(2,1)S(1)}, bf16[64,1024]{1,0:T(8,128)(2,1)S(1)}, u32[]{:S(2)}, u32[]{:S(2)}) collective-permute-start(bf16[64,1024]{1,0:T(8,128)(2,1)S(1)} %add_convert_fusion.4), channel_id=1, source_target_pairs={{0,4},{4,0},{8,12},{12,8},{16,20},{20,16},{24,28},{28,24},{1,5},{5... | collective-permute-start | bytes 393224 | tf_op jit(solution)/shard_map/ppermute | solution.py:258
  88.1 7.8 %collective-permute-start.19 = (bf16[64,1280]{1,0:T(8,128)(2,1)S(1)}, bf16[64,1280]{1,0:T(8,128)(2,1)S(1)}, u32[]{:S(2)}, u32[]{:S(2)}) collective-permute-start(bf16[64,1280]{1,0:T(8,128)(2,1)S(1)} %add_convert_fusion.3), channel_id=1, source_target_pairs={{0,4},{4,0},{8,12},{12,8},{16,20},{20,16},{24,28},{28,24},{1,5},{5... | collective-permute-start | bytes 491528 | tf_op jit(solution)/shard_map/ppermute | solution.py:258

commit v6 on v5

v6 whole, which is shorter than its diff:
```python
import functools
import math

import jax
import jax.numpy as jnp
from jax import lax
from jax.experimental import pallas as pl
from jax.experimental.pallas import tpu as pltpu
from jax.sharding import PartitionSpec as P

eps = 1e-06
f32 = jnp.float32
bf16 = jnp.bfloat16
VM = pltpu.VMEM
MIB = 1024 * 1024


def params(mib):
    return pltpu.CompilerParams(vmem_limit_bytes=mib * MIB)


def cost(flops, moved):
    return pl.CostEstimate(flops=flops, transcendentals=0, bytes_accessed=moved)


def norm_kernel(t_ref, size_ref, x_hbm, mod_hbm, m_ref, sg_ref, x_ref, mod_ref, sem):
    width = x_hbm.shape[-1]
    pieces = sem.shape[0] - 1
    block = x_hbm.shape[1] // pieces
    t = t_ref[0]
    mod_copy = pltpu.make_async_copy(mod_hbm.at[pl.ds(t, 1), :], mod_ref, sem.at[pieces])
    mod_copy.start()
    copies = []
    for i in range(pieces):
        here = pl.ds(i * block, block)
        copies.append(pltpu.make_async_copy(x_hbm.at[0, here, :], x_ref.at[here, :], sem.at[i]))
        copies[i].start()
    mod_copy.wait()
    shift = mod_ref[:, :width]
    scale = 1.0 + mod_ref[:, width : 2 * width]
    sg_ref[...] = size_ref[t] * mod_ref[:, 2 * width :]
    for i in range(pieces):
        copies[i].wait()
        here = slice(i * block, (i + 1) * block)
        x = x_ref[here, :]
        center = x - jnp.mean(x, axis=-1, keepdims=True)
        spread = jnp.mean(center * center, axis=-1, keepdims=True)
        m_ref[here, :] = (center * lax.rsqrt(spread + eps) * scale + shift).astype(bf16)


def norm_call(t_idx, trajectory, mod_table, step_sizes):
    _, rows, width = trajectory.shape
    smem = pl.BlockSpec(memory_space=pltpu.SMEM)
    hbm = pl.BlockSpec(memory_space=pltpu.HBM)
    vm = pl.BlockSpec(memory_space=VM)
    return pl.pallas_call(
        norm_kernel,
        in_specs=[smem, smem, hbm, hbm],
        out_specs=[vm, vm],
        out_shape=[
            jax.ShapeDtypeStruct((rows, width), bf16),
            jax.ShapeDtypeStruct((1, width), f32),
        ],
        scratch_shapes=[
            VM((rows, width), f32),
            VM((1, 3 * width), f32),
            pltpu.SemaphoreType.DMA((5,)),
        ],
        compiler_params=params(60),
        cost_estimate=cost(10 * rows * width, 0),
        name="norm",
    )(t_idx, step_sizes, trajectory, mod_table)


def project_kernel(tile, load, tiles, m0, m1, qg, kg, *refs):
    if load:
        wq_hbm, wm_hbm, wb_hbm, q, k, v, act, low, high = refs[:9]
        held, rows, wb, sem = refs[9:-3], refs[-3], refs[-2], refs[-1]
    else:
        held = refs[:tiles]
        q, k, v, act, rows = refs[tiles:]
    half = m0.shape[0]
    head = qg.shape[1]
    n_q = q.shape[1] // tile
    copies = []
    if load:
        for i in range(tiles):
            if i < 3 * n_q:
                source = wq_hbm.at[i // n_q, :, pl.ds(i % n_q * tile, tile)]
            else:
                source = wm_hbm.at[:, pl.ds((i - 3 * n_q) * tile, tile)]
            copies.append(pltpu.make_async_copy(source, held[i], sem.at[i]))
            copies[i].start()
        span = low.shape[1] // (sem.shape[0] - tiles)
        for at in range(0, low.shape[1], span):
            here = (slice(None), pl.ds(at, span))
            copies.append(pltpu.make_async_copy(wb_hbm.at[here], wb.at[here], sem.at[len(copies)]))
            copies[-1].start()
    rows[:half] = m0[...]
    rows[half:] = m1[...]

    def normed(y, gain):
        parts = []
        for h in range(tile // head):
            one = y[:, h * head : (h + 1) * head]
            square = jnp.mean(one * one, axis=-1, keepdims=True)
            parts.append((one * lax.rsqrt(square + eps) * gain).astype(bf16))
        return jnp.concatenate(parts, axis=1)

    for i in range(tiles):
        if load:
            copies[i].wait()
        y = jnp.dot(rows[...], held[i][...], preferred_element_type=f32)
        cols = slice(i % n_q * tile, (i % n_q + 1) * tile)
        if i < n_q:
            q[:, cols] = normed(y, qg[...])
        elif i < 2 * n_q:
            k[:, cols] = normed(y, kg[...])
        elif i < 3 * n_q:
            v[:, cols] = y.astype(bf16)
        else:
            cols = slice((i - 3 * n_q) * tile, (i - 3 * n_q + 1) * tile)
            act[:, cols] = jax.nn.gelu(y, approximate=True).astype(bf16)
    if load:
        for i, copy in enumerate(copies[tiles:]):
            copy.wait()
            cols = slice(i * span, (i + 1) * span)
            y = jnp.dot(act[...], wb[:, cols], preferred_element_type=f32)
            low[:, cols] = y[:half]
            high[:, cols] = y[half:]


def project_call(m0, m1, q_gain, k_gain, w_qkv, w_mlp_in, w_out_mlp, held):
    half, width = m0.shape
    heads = w_qkv.shape[2]
    hidden = w_mlp_in.shape[1]
    tile = min(512, heads)
    tiles = (3 * heads + hidden) // tile
    rows = 2 * half
    load = held is None
    vm = pl.BlockSpec(memory_space=VM)
    hbm = pl.BlockSpec(memory_space=pltpu.HBM)
    shapes = [jax.ShapeDtypeStruct((rows, heads), bf16)] * 3
    shapes.append(jax.ShapeDtypeStruct((rows, hidden), bf16))
    scratch = [VM((rows, width), bf16)]
    if load:
        shapes += [jax.ShapeDtypeStruct((half, width), f32)] * 2
        shapes += [jax.ShapeDtypeStruct((width, tile), bf16)] * tiles
        scratch.append(VM(w_out_mlp.shape, bf16))
        scratch.append(pltpu.SemaphoreType.DMA((tiles + 4,)))
    return pl.pallas_call(
        functools.partial(project_kernel, tile, load, tiles),
        in_specs=[vm] * 4 + ([hbm] * 3 if load else [vm] * tiles),
        out_specs=[vm] * len(shapes),
        out_shape=shapes,
        scratch_shapes=scratch,
        compiler_params=params(27 if load else 9),
        cost_estimate=cost(2 * rows * width * (3 * heads + hidden), 0),
        name="project",
    )(m0, m1, q_gain, k_gain, *([w_qkv, w_mlp_in, w_out_mlp] if load else held))


def attend_kernel(pairs, head, *refs):
    q_ref = refs[0]
    k_refs = refs[1 : 1 + pairs]
    v_refs = refs[1 + pairs : 1 + 2 * pairs]
    out = refs[1 + 2 * pairs]
    scale = math.log2(math.e) / math.sqrt(head)
    for h in range(q_ref.shape[1] // head):
        cols = slice(h * head, (h + 1) * head)
        q = q_ref[:, cols]
        scores = [
            lax.dot_general(q, k[:, cols], (((1,), (1,)), ((), ())), preferred_element_type=f32)
            for k in k_refs
        ]
        top = functools.reduce(
            jnp.maximum, [jnp.max(s, axis=-1, keepdims=True) for s in scores]
        )
        weights = [jnp.exp2((s - top) * scale) for s in scores]
        total = sum(jnp.sum(w, axis=-1, keepdims=True) for w in weights)
        inverse = 1.0 / total
        mixed = sum(
            jnp.dot((w * inverse).astype(bf16), v[:, cols], preferred_element_type=f32)
            for w, v in zip(weights, v_refs)
        )
        out[:, cols] = mixed.astype(bf16)


def attend_call(q, ks, vs, head):
    vm = pl.BlockSpec(memory_space=VM)
    return pl.pallas_call(
        functools.partial(attend_kernel, len(ks), head),
        in_specs=[vm] * (1 + 2 * len(ks)),
        out_specs=vm,
        out_shape=jax.ShapeDtypeStruct(q.shape, bf16),
        compiler_params=params(9),
        cost_estimate=cost(4 * len(ks) * q.shape[0] ** 2 * q.shape[1] * 3, 0),
        name="attend",
    )(q, *ks, *vs)


def out_kernel(jobs, *refs):
    outs = refs[len(refs) - 2 * len(jobs) :]
    at = 0
    for turn, (parts, extras, first, count) in enumerate(jobs):
        xs = refs[at : at + parts]
        ws = refs[at + parts : at + 2 * parts]
        extra = refs[at + 2 * parts : at + 2 * parts + extras]
        at += 2 * parts + extras
        keep, send = outs[2 * turn : 2 * turn + 2]
        half = keep.shape[0]
        cols = slice(first, first + count)
        terms = [
            jnp.dot(x[...], w[:, cols], preferred_element_type=f32) for x, w in zip(xs, ws)
        ]
        y = functools.reduce(jnp.add, terms)
        low, high = y[:half], y[half:]
        if extra:
            low = low + extra[0][:, cols]
            high = high + extra[1][:, cols]
        keep[...] = low
        send[...] = high.astype(bf16)


def out_call(jobs):
    vm = pl.BlockSpec(memory_space=VM)
    given, plan, shapes, flops = [], [], [], 0
    for xs, ws, extra, first, count in jobs:
        given += [*xs, *ws, *extra]
        plan.append((len(xs), len(extra), first, count))
        half = xs[0].shape[0] // 2
        shapes.append(jax.ShapeDtypeStruct((half, count), f32))
        shapes.append(jax.ShapeDtypeStruct((half, count), bf16))
        flops += 4 * half * count * sum(x.shape[1] for x in xs)
    outs = pl.pallas_call(
        functools.partial(out_kernel, plan),
        in_specs=[vm] * len(given),
        out_specs=[vm] * len(shapes),
        out_shape=shapes,
        compiler_params=params(9),
        cost_estimate=cost(flops, 0),
        name="project_out",
    )(*given)
    return [tuple(outs[i : i + 2]) for i in range(0, len(outs), 2)]


def join_kernel(keep, sent, out):
    out[...] = (keep[...] + sent[...].astype(f32)).astype(bf16)


def join_call(keep, sent):
    vm = pl.BlockSpec(memory_space=VM)
    return pl.pallas_call(
        join_kernel,
        in_specs=[vm, vm],
        out_specs=vm,
        out_shape=jax.ShapeDtypeStruct(keep.shape, bf16),
        compiler_params=params(6),
        name="join",
    )(keep, sent)


def drift_kernel(first, parity, keep, sent, sg, *refs):
    fetched, (kept, other, send) = refs[:-3], refs[-3:]
    half, count = kept.shape
    p = parity[0]

    def part(which):
        rows = pl.ds(pl.multiple_of(which * half, half), half)
        branch = keep[rows, :] + sent[rows, :].astype(f32)
        for one in fetched:
            branch = branch + one[rows, :].astype(f32)
        return sg[:, first : first + count] * branch

    kept[...] = part(p)
    passed = part(1 - p)
    other[...] = passed
    send[...] = passed.astype(bf16)


def drift_call(parity, keep, sent, sg, fetched, first):
    rows, count = fetched[0].shape
    vm = pl.BlockSpec(memory_space=VM)
    smem = pl.BlockSpec(memory_space=pltpu.SMEM)
    shape = (rows // 2, count)
    return pl.pallas_call(
        functools.partial(drift_kernel, first),
        in_specs=[smem] + [vm] * (3 + len(fetched)),
        out_specs=[vm] * 3,
        out_shape=[
            jax.ShapeDtypeStruct(shape, f32),
            jax.ShapeDtypeStruct(shape, f32),
            jax.ShapeDtypeStruct(shape, bf16),
        ],
        compiler_params=params(6),
        name="drift",
    )(parity, keep, sent, sg, *fetched)


def finish_kernel(first, parity, x_start, earlier, kept, fetched, other, back, *refs):
    out, result, sem = refs[-3:]
    half, count = kept.shape
    cols = slice(first, first + count)
    p = parity[0]
    mine = pl.ds(pl.multiple_of(p * half, half), half)
    rest = pl.ds(pl.multiple_of((1 - p) * half, half), half)
    odd = p.astype(f32)
    result[mine, :] = x_start[mine, cols] + earlier[...] + kept[...] + odd * fetched[...].astype(f32)
    result[rest, :] = x_start[rest, cols] + other[...] + back[...].astype(f32)
    copy = pltpu.make_async_copy(result, out.at[0, :, pl.ds(first, count)], sem)
    copy.start()
    copy.wait()


def finish_call(parity, x_start, earlier, kept, fetched, other, back, into, first):
    rows, width = x_start.shape
    vm = pl.BlockSpec(memory_space=VM)
    smem = pl.BlockSpec(memory_space=pltpu.SMEM)
    hbm = pl.BlockSpec(memory_space=pltpu.HBM)
    given = [parity, x_start, earlier, kept, fetched, other, back]
    return pl.pallas_call(
        functools.partial(finish_kernel, first),
        in_specs=[smem] + [vm] * 6 + [hbm] * len(into),
        out_specs=hbm,
        out_shape=jax.ShapeDtypeStruct((1, rows, width), f32),
        scratch_shapes=[VM((rows, kept.shape[1]), f32), pltpu.SemaphoreType.DMA],
        input_output_aliases={len(given): 0} if into else {},
        compiler_params=params(6),
        name="finish",
    )(*given, *into)


def per_device(
    n_step,
    n_seq,
    trajectory,
    x_start,
    t_idx,
    mod_table,
    step_sizes,
    q_gain,
    k_gain,
    w_qkv,
    w_mlp_in,
    w_out_attn,
    w_out_mlp,
):
    head = q_gain.shape[0]
    rows, width = x_start.shape
    chips = n_seq // 2
    groups = n_step // 2
    half = rows // 2
    unit = width // 24
    counts = [10 * unit, 8 * unit, 6 * unit]
    chunks = len(counts)
    firsts = [sum(counts[:c]) for c in range(chunks)]
    qg, kg = q_gain[None, :], k_gain[None, :]

    def to_core(x):
        return lax.ppermute(x, "seq", [(i, i ^ 1) for i in range(n_seq)])

    def to_chip(x, offset):
        return lax.ppermute(x, "seq", [(i, (i + 2 * offset) % n_seq) for i in range(n_seq)])

    def to_pair(x):
        return lax.ppermute(x, "step", [(i, i ^ 1) for i in range(n_step)])

    def tied(*values):
        return lax.optimization_barrier(values)

    parity = lax.rem(lax.axis_index("step"), 2)
    even = (parity == 0).astype(f32)
    which = parity[None]
    offsets = range(1, chips)

    mine, sg = norm_call(t_idx, trajectory, mod_table, step_sizes)
    far = [to_chip(mine, j) for j in offsets]
    q0, k0, v0, act0, low0, high0, *held = project_call(
        mine, to_core(mine), qg, kg, w_qkv, w_mlp_in, w_out_mlp, None
    )
    far, low0, high0 = tied(far, low0, high0)
    qs, ks, vs, acts = [], [k0], [v0], []
    for block in far:
        q, k, v, act = project_call(block, to_core(block), qg, kg, w_qkv, w_mlp_in, w_out_mlp, held)
        qs.append(q)
        ks.append(k)
        vs.append(v)
        acts.append(act)
    mixed = [attend_call(q, ks, vs, head) for q in qs]

    weights = [w_out_attn, w_out_mlp]
    got = [[] for _ in offsets]

    def jobs_of(c):
        return [([a, b], weights, [], firsts[c], counts[c]) for a, b in zip(mixed, acts)]

    def joined(parts, sent):
        return [join_call(keep, s) for (keep, _), s in zip(parts, sent)]

    def to_chips(ready):
        for j, one in enumerate(ready):
            got[j].append(to_chip(one, chips - 1 - j))

    parts = out_call(jobs_of(0))
    sent = [to_core(send) for _, send in parts]
    q0, parts = tied(q0, parts)
    mixed0 = attend_call(q0, ks, vs, head)
    mixed0, sent = tied(mixed0, sent)
    ready = joined(parts, sent)
    mixed, acts, mixed0, ready = tied(mixed, acts, mixed0, ready)
    to_chips(ready)
    jobs = [job for c in range(1, chunks) for job in jobs_of(c)]
    for c in range(chunks):
        jobs.append(([mixed0], [w_out_attn], [low0, high0], firsts[c], counts[c]))
    parts = out_call(jobs)
    sent = [to_core(send) for _, send in parts]
    keep = [part[0] for part in parts[-chunks:]]
    sent0 = sent[-chunks:]
    others = chips - 1
    first, keep, sent[:others] = tied([row[0] for row in got], keep, sent[:others])
    for row, one in zip(got, first):
        row[0] = one
    ready = joined(parts[:others], sent[:others])
    keep, ready = tied(keep, ready)
    to_chips(ready)
    for c in range(2, chunks):
        here = slice((c - 1) * others, c * others)
        to_chips(joined(parts[here], sent[here]))

    def along(pairs):
        return lambda x: lax.ppermute(x, "step", [(2 * a + i, 2 * b + i) for a, b in pairs for i in (0, 1)])

    group = lax.div(lax.axis_index("step"), 2)
    rounds = []
    span = 1
    while span < groups:
        pairs = [(b, b ^ span) for b in range(groups) if b ^ span < groups]
        rounds.append((span, along(pairs)))
        span *= 2

    def prefix_stages(c):
        held = {}

        def drift_of(fetched):
            drift = drift_call(which, keep[c], sent0[c], sg, fetched, firsts[c])
            held["kept"], held["other"], send = drift
            return send

        def pair_sum(fetched):
            held["fetched"] = fetched[0]
            held["total"] = held["kept"] + fetched[0].astype(f32)
            return held["total"].astype(bf16)

        def collect(r, fetched):
            one = fetched[0].astype(f32)
            upper = (lax.rem(lax.div(group, rounds[r][0]), 2) == 1).astype(f32)
            held["earlier"] = held["earlier"] + upper * one if r else upper * one
            if r == len(rounds) - 1:
                return (held["earlier"] + even * held["kept"]).astype(bf16)
            held["total"] = held["total"] + one
            return held["total"].astype(bf16)

        def finish(fetched):
            given = [held[name] for name in ("earlier", "kept", "fetched", "other")]
            into = list(written)
            written[:] = [finish_call(which, x_start, *given, fetched[0], into, firsts[c])]

        stages = [(drift_of, to_pair), (pair_sum, rounds[0][1])]
        for r in range(len(rounds)):
            move = to_pair if r == len(rounds) - 1 else rounds[r + 1][1]
            stages.append((functools.partial(collect, r), move))
        stages.append((finish, None))
        return stages

    plan = [prefix_stages(c) for c in range(chunks)]
    inbox = [[got[j][c] for j in range(chips - 1)] for c in range(chunks)]
    turns = []
    arrival = 2.0
    for c in range(chunks):
        share = 16.0 * counts[c] / width
        arrival += share
        when = arrival
        for i in range(len(plan[c])):
            turns.append((when, c, i))
            when += 2.2 + share * (1.0 if i == len(plan[c]) - 3 else 0.5)
    written = []
    last = None
    for _, c, i in sorted(turns):
        compute, move = plan[c][i]
        fetched = inbox[c]
        if last is not None:
            fetched, last = tied(fetched, last)
        out = compute(fetched)
        if move is not None:
            inbox[c] = [move(out)]
            last = out
    return written[0]


def solution(mesh):
    placed = (
        P("step", "seq", None),
        P("seq", None),
        P("step"),
        P(),
        P(),
        P(),
        P(),
        P(None, None, "seq"),
        P(None, "seq"),
        P("seq", None),
        P("seq", None),
    )
    return jax.shard_map(
        functools.partial(per_device, mesh.shape["step"], mesh.shape["seq"]),
        mesh=mesh,
        in_specs=placed,
        out_specs=P("step", "seq", None),
        check_vma=False,
    )
```

time: 97.7 us -> 93.4 us (0.956)
  the two profiles are of different devices: /device:TPU:30 before, /device:TPU:0 now
where the time goes in v6:
time: 93.4 us; the launch traced here: 93.1 us
  Pallas kernels  36.2 us (39%)
  starting transfers between devices  28 us (30%)
  waiting for transfers between devices  26.2 us (28%)
  local copies, waits for them, and re-layouts  1.18 us (1%)
  between operations  1.07 us (1%)
    pallas_call x2, Pallas kernels, project_call(): pl.pallas_call(functools.partial(project_kernel, tile, load, tiles), in_s...  17.6 us
    ppermute x6, starting transfers between devices, along(): lax.ppermute(x, 'step', [(2 * a + i, 2 * b + i) for a, b in pairs for i i...  13.4 us
    ppermute x4, waiting for transfers between devices, to_chip(): lax.ppermute(x, 'seq', [(i, (i + 2 * offset) % n_seq) for i in range(n_se...  9.96 us
    ppermute x6, waiting for transfers between devices, along(): lax.ppermute(x, 'step', [(2 * a + i, 2 * b + i) for a, b in pairs for i i...  9.72 us
    ppermute x4, starting transfers between devices, to_chip(): lax.ppermute(x, 'seq', [(i, (i + 2 * offset) % n_seq) for i in range(n_se...  6.76 us
    ppermute x6, starting transfers between devices, to_pair(): return lax.ppermute(x, 'step', [(i, i ^ 1) for i in range(n_step)])  6.05 us
    pallas_call x2, Pallas kernels, out_call(): pl.pallas_call(functools.partial(out_kernel, plan), in_specs=[vm] * len(g...  5.02 us
    pallas_call x1, Pallas kernels, norm_call(): pl.pallas_call(norm_kernel, in_specs=[smem, smem, hbm, hbm], out_specs=[v...  3.71 us
  transfers between devices with their start and end apart: 24, of which 13 were waited for; matrix products, arithmetic and copies ran while one was open for 0% of the time, Pallas kernels for 24%

profile of v6, /device:TPU:0, one launch (start us, length us, event | category | flops | bytes accessed | tf_op | source)
XLA Modules:
  0.0 93.1 jit_solution(18118631479347808775)
XLA Ops:
  0.7 3.7 %norm.1 = (bf16[128,3072]{1,0:T(8,128)(2,1)}, f32[1,3072]{1,0:T(1,128)}) custom-call(s32[1]{0:T(128)S(6)} %copy.16.t_ref, f32[50]{0:T(128)} %size_ref.1, f32[1,128,3072]{2,1,0:T(8,128)} %x_hbm.1, f32[50,9216]{1,0:T(8,128)} %mod_hbm.1), custom_call_target="tpu_custom_call" | custom-call | flops 3932160 | tf_op jit(solution)/shard_map/norm/pallas_call | solution.py:56
  4.4 0.5 collective-permute-start.1
  4.9 2.6 %collective-permute-start = (bf16[128,3072]{1,0:T(8,128)(2,1)}, bf16[128,3072]{1,0:T(8,128)(2,1)S(1)}, u32[]{:S(2)}, u32[]{:S(2)}) collective-permute-start(bf16[128,3072]{1,0:T(8,128)(2,1)} %get-tuple-element.75.m0), channel_id=1, source_target_pairs={{0,2},{1,3},{2,0},{3,1},{4,6},{5,7},{6,4},{7,5},{8,10},{9,11},{10,... | collective-permute-start | bytes 2359304 | tf_op jit(solution)/shard_map/ppermute | solution.py:363
  7.5 0.0 collective-permute-done.1.m1
  7.5 0.0 copy-start.2
  7.5 1.1 %copy-done.2 = bf16[128,3072]{1,0:T(8,128)(2,1)S(1)} copy-done((bf16[128,3072]{1,0:T(8,128)(2,1)S(1)}, bf16[128,3072]{1,0:T(8,128)(2,1)}, u32[]{:S(2)}) %copy-start.2) | copy-done | bytes 786456
  8.7 12.4 %project.2 = (bf16[256,512]{1,0:T(8,128)(2,1)S(1)}, bf16[256,512]{1,0:T(8,128)(2,1)S(1)}, bf16[256,512]{1,0:T(8,128)(2,1)S(1)}, bf16[256,1536]{1,0:T(8,128)(2,1)...) custom-call(bf16[128,3072]{1,0:T(8,128)(2,1)S(1)} %copy-done.2, ...), custom_call_target="tpu_custom_call" | custom-call | flops 4831838208 | tf_op jit(solution)/shard_map/project/pallas_call | solution.py:151
  21.1 4.8 %collective-permute-done.m0 = bf16[128,3072]{1,0:T(8,128)(2,1)S(1)} collective-permute-done((bf16[128,3072]{1,0:T(8,128)(2,1)}, bf16[128,3072]{1,0:T(8,128)(2,1)S(1)}, u32[]{:S(2)}, u32[]{:S(2)}) %collective-permute-start) | collective-permute-done | bytes 786464 | tf_op jit(solution)/shard_map/ppermute | solution.py:363
  25.9 2.3 %collective-permute-done.2.m1 = bf16[128,3072]{1,0:T(8,128)(2,1)S(1)} collective-permute-done((bf16[128,3072]{1,0:T(8,128)(2,1)S(1)}, bf16[128,3072]{1,0:T(8,128)(2,1)S(1)}, u32[]{:S(2)}, u32[]{:S(2)}) %collective-permute-start.2) | collective-permute-done | bytes 786464 | tf_op jit(solution)/shard_map/ppermute | solution.py:360
  28.2 5.2 %project.3 = (bf16[256,512]{1,0:T(8,128)(2,1)S(1)}, bf16[256,512]{1,0:T(8,128)(2,1)S(1)}, bf16[256,512]{1,0:T(8,128)(2,1)S(1)}, bf16[256,1536]{1,0:T(8,128)(2,1)S(1)}) custom-call(bf16[128,3072]{1,0:T(8,128)(2,1)S(1)} %collective-permute-done.m0, bf16[128,3072]{1,0:T(8,128)(2,1)S(1)} %collective-permute-done.2.m1, f32[1,128]{1,0:T(1,128)S(1)} %bitcast.6, ...), custom_call_target="tpu_custom_call" | custom-call | flops 4831838208 | tf_op jit(solution)/shard_map/project/pallas_call | solution.py:151
  33.4 1.9 %attend.2.refs_0_.refs_4_ = bf16[256,512]{1,0:T(8,128)(2,1)S(1)} custom-call(bf16[256,512]{1,0:T(8,128)(2,1)S(1)} %get-tuple-element.85.refs_0_, bf16[256,512]{1,0:T(8,128)(2,1)S(1)} %get-tuple-element.86.refs_1_, bf16[256,512]{1,0:T(8,128)(2,1)S(1)} %get-tuple-element.87.refs_2_, bf16[256,512]{1,0:T(8,128)(2,1)S(1)} %get-tuple-element.88.refs_3_, ...), custom_call_target="tpu_custom_call" | custom-call | flops 805306368 | tf_op jit(solution)/shard_map/attend/pallas_call | solution.py:191
  35.3 1.5 %project_out.2 = (f32[128,1280]{1,0:T(8,128)S(1)}, bf16[128,1280]{1,0:T(8,128)(2,1)S(1)}) custom-call(bf16[256,512]{1,0:T(8,128)(2,1)S(1)} %attend.2.refs_0_.refs_4_, bf16[256,1536]{1,0:T(8,128)(2,1)S(1)} %get-tuple-element.100.refs_1_.refs_5_, bf16[512,3072]{1,0:T(8,128)(2,1)S(1)} %copy-done, bf16[1536,3072]{1,0:T(8,128)(2,1)S(1)} %bitcast.4), custom_call_target="tpu_custom_call" | custom-call | flops 1342177280 | tf_op jit(solution)/shard_map/project_out/pallas_call | solution.py:235
  36.9 0.2 collective-permute-start.3
  37.1 1.7 %attend.3.refs_8_.refs_12_.refs_16_ = bf16[256,512]{1,0:T(8,128)(2,1)S(1)} custom-call(bf16[256,512]{1,0:T(8,128)(2,1)S(1)} %get-tuple-element.94.refs_0_, bf16[256,512]{1,0:T(8,128)(2,1)S(1)} %get-tuple-element.86.refs_1_, bf16[256,512]{1,0:T(8,128)(2,1)S(1)} %get-tuple-element.87.refs_2_, bf16[256,512]{1,0:T(8,128)(2,1)S(1)} %get-tuple-element.88.refs_3_, ...), custom_call_target="tpu_custom_call" | custom-call | flops 805306368 | tf_op jit(solution)/shard_map/attend/pallas_call | solution.py:191
  38.8 0.1 join.3
  38.8 1.9 %collective-permute-start.4 = (bf16[128,1280]{1,0:T(8,128)(2,1)S(1)}, bf16[128,1280]{1,0:T(8,128)(2,1)S(1)}, u32[]{:S(2)}, u32[]{:S(2)}) collective-permute-start(bf16[128,1280]{1,0:T(8,128)(2,1)S(1)} %join.3), channel_id=1, source_target_pairs={{0,2},{1,3},{2,0},{3,1},{4,6},{5,7},{6,4},{7,5},{8,10},{9,11},{10,... | collective-permute-start | bytes 983048 | tf_op jit(solution)/shard_map/ppermute | solution.py:363
  40.7 3.5 %project_out.3 = (f32[128,1024]{1,0:T(8,128)S(1)}, bf16[128,1024]{1,0:T(8,128)(2,1)S(1)}, f32[128,768]{1,0:T(8,128)S(1)}, bf16[128,768]{1,0:T(8,128)(2,1)}, f32[...) custom-call(bf16[256,512]{1,0:T(8,128)(2,1)S(1)} %attend.2.refs_0_.r, ...), custom_call_target="tpu_custom_call" | custom-call | flops 2684354560 | tf_op jit(solution)/shard_map/project_out/pallas_call | solution.py:235
  44.2 0.1 collective-permute-start.5
  44.3 0.4 collective-permute-start.9
  44.7 1.0 %collective-permute-done.5.sent = bf16[128,1024]{1,0:T(8,128)(2,1)S(1)} collective-permute-done((bf16[128,1024]{1,0:T(8,128)(2,1)S(1)}, bf16[128,1024]{1,0:T(8,128)(2,1)S(1)}, u32[]{:S(2)}, u32[]{:S(2)}) %collective-permute-start.5) | collective-permute-done | bytes 262176 | tf_op jit(solution)/shard_map/ppermute | solution.py:360
  45.7 3.2 %collective-permute-done.4.refs_0_ = bf16[128,1280]{1,0:T(8,128)(2,1)S(1)} collective-permute-done((bf16[128,1280]{1,0:T(8,128)(2,1)S(1)}, bf16[128,1280]{1,0:T(8,128)(2,1)S(1)}, u32[]{:S(2)}, u32[]{:S(2)}) %collective-permute-start.4) | collective-permute-done | bytes 327712 | tf_op jit(solution)/shard_map/ppermute | solution.py:363
  48.9 0.8 join.4
  49.7 1.7 %collective-permute-start.12 = (bf16[128,1024]{1,0:T(8,128)(2,1)}, bf16[128,1024]{1,0:T(8,128)(2,1)S(1)}, u32[]{:S(2)}, u32[]{:S(2)}) collective-permute-start(bf16[128,1024]{1,0:T(8,128)(2,1)} %join.4), channel_id=1, source_target_pairs={{0,2},{1,3},{2,0},{3,1},{4,6},{5,7},{6,4},{7,5},{8,10},{9,11},{10,... | collective-permute-start | bytes 786440 | tf_op jit(solution)/shard_map/ppermute | solution.py:363
  51.4 0.5 collective-permute-start.7
  51.9 0.0 collective-permute-done.9.sent
  52.0 0.7 drift.3
  52.7 1.5 %collective-permute-start.10 = (bf16[64,1280]{1,0:T(8,128)(2,1)}, bf16[64,1280]{1,0:T(8,128)(2,1)S(1)}, u32[]{:S(2)}, u32[]{:S(2)}) collective-permute-start(bf16[64,1280]{1,0:T(8,128)(2,1)} %get-tuple-element.122), channel_id=1, source_target_pairs={{0,4},{4,0},{8,12},{12,8},{16,20},{20,16},{24,28},{28,24},{1,5},{5... | collective-permute-start | bytes 491528 | tf_op jit(solution)/shard_map/ppermute | solution.py:366
  54.2 0.0 collective-permute-done.7.sent
  54.2 1.0 %join.5 = bf16[128,768]{1,0:T(8,128)(2,1)S(1)} custom-call(f32[128,768]{1,0:T(8,128)S(1)} %get-tuple-element.116.keep, bf16[128,768]{1,0:T(8,128)(2,1)} %collective-permute-done.7.sent), custom_call_target="tpu_custom_call" | custom-call | tf_op jit(solution)/shard_map/join/pallas_call | solution.py:253
  55.2 0.6 collective-permute-start.8
  55.7 2.0 %collective-permute-done.12.refs_0_ = bf16[128,1024]{1,0:T(8,128)(2,1)S(1)} collective-permute-done((bf16[128,1024]{1,0:T(8,128)(2,1)}, bf16[128,1024]{1,0:T(8,128)(2,1)S(1)}, u32[]{:S(2)}, u32[]{:S(2)}) %collective-permute-start.12) | collective-permute-done | bytes 262176 | tf_op jit(solution)/shard_map/ppermute | solution.py:363
  57.7 0.0 collective-permute-done.11.sent
  57.7 1.0 %drift.4 = (f32[64,1024]{1,0:T(8,128)S(1)}, f32[64,1024]{1,0:T(8,128)S(1)}, bf16[64,1024]{1,0:T(8,128)(2,1)S(1)}) custom-call(s32[1]{0:T(128)} %bitcast.parity, f32[128,1024]{1,0:T(8,128)S(1)} %get-tuple-element.123.keep, bf16[128,1024]{1,0:T(8,128)(2,1)} %collective-permute-done.11.sent, f32[1,3072]{1,0:T(1,128)S(1)} %copy-done.3, ...), custom_call_target="tpu_custom_call" | custom-call | tf_op jit(solution)/shard_map/drift/pallas_call | solution.py:286
  58.7 2.4 %collective-permute-start.15 = (bf16[64,1024]{1,0:T(8,128)(2,1)S(1)}, bf16[64,1024]{1,0:T(8,128)(2,1)S(1)}, u32[]{:S(2)}, u32[]{:S(2)}) collective-permute-start(bf16[64,1024]{1,0:T(8,128)(2,1)S(1)} %get-tuple-element.127), channel_id=1, source_target_pairs={{0,4},{4,0},{8,12},{12,8},{16,20},{20,16},{24,28},{28,24},{1,5},{5... | collective-permute-start | bytes 393224 | tf_op jit(solution)/shard_map/ppermute | solution.py:366
  61.2 0.0 copy-start.1
  61.2 1.7 %collective-permute-start.14 = (bf16[64,1280]{1,0:T(8,128)(2,1)S(1)}, bf16[64,1280]{1,0:T(8,128)(2,1)S(1)}, u32[]{:S(2)}, u32[]{:S(2)}) collective-permute-start(bf16[64,1280]{1,0:T(8,128)(2,1)S(1)} %fusion.4), channel_id=1, source_target_pairs={{0,8},{4,12},{8,0},{12,4},{16,24},{20,28},{24,16},{28,20},{1,9},{5... | collective-permute-start | bytes 491528 | tf_op jit(solution)/shard_map/ppermute | solution.py:431
  62.8 0.1 drift.5
  62.9 0.9 collective-permute-start.13
  63.8 0.3 collective-permute-done.15.fetched
  64.1 1.7 %collective-permute-start.17 = (bf16[64,1024]{1,0:T(8,128)(2,1)S(1)}, bf16[64,1024]{1,0:T(8,128)(2,1)S(1)}, u32[]{:S(2)}, u32[]{:S(2)}) collective-permute-start(bf16[64,1024]{1,0:T(8,128)(2,1)S(1)} %fusion.7), channel_id=1, source_target_pairs={{0,8},{4,12},{8,0},{12,4},{16,24},{20,28},{24,16},{28,20},{1,9},{5... | collective-permute-start | bytes 393224 | tf_op jit(solution)/shard_map/ppermute | solution.py:431
  65.7 1.5 %collective-permute-done.14 = bf16[64,1280]{1,0:T(8,128)(2,1)S(1)} collective-permute-done((bf16[64,1280]{1,0:T(8,128)(2,1)S(1)}, bf16[64,1280]{1,0:T(8,128)(2,1)S(1)}, u32[]{:S(2)}, u32[]{:S(2)}) %collective-permute-start.14) | collective-permute-done | bytes 163872 | tf_op jit(solution)/shard_map/ppermute | solution.py:431
  67.3 0.1 fusion
  67.4 2.6 %collective-permute-start.20 = (bf16[64,1280]{1,0:T(8,128)(2,1)S(1)}, bf16[64,1280]{1,0:T(8,128)(2,1)S(1)}, u32[]{:S(2)}, u32[]{:S(2)}) collective-permute-start(bf16[64,1280]{1,0:T(8,128)(2,1)S(1)} %fusion), channel_id=1, source_target_pairs={{0,16},{4,20},{8,24},{12,28},{16,0},{20,4},{24,8},{28,12},{1,17},{... | collective-permute-start | bytes 491528 | tf_op jit(solution)/shard_map/ppermute | solution.py:431
  70.0 2.8 %collective-permute-start.16 = (bf16[64,768]{1,0:T(8,128)(2,1)S(1)}, bf16[64,768]{1,0:T(8,128)(2,1)S(1)}, u32[]{:S(2)}, u32[]{:S(2)}) collective-permute-start(bf16[64,768]{1,0:T(8,128)(2,1)S(1)} %fusion.8), channel_id=1, source_target_pairs={{0,8},{4,12},{8,0},{12,4},{16,24},{20,28},{24,16},{28,20},{1,9},{5... | collective-permute-start | bytes 294920 | tf_op jit(solution)/shard_map/ppermute | solution.py:431
  72.8 0.0 collective-permute-done.17
  72.8 0.1 fusion.2
  72.8 0.8 collective-permute-start.19
  73.7 2.0 %collective-permute-done.16 = bf16[64,768]{1,0:T(8,128)(2,1)S(1)} collective-permute-done((bf16[64,768]{1,0:T(8,128)(2,1)S(1)}, bf16[64,768]{1,0:T(8,128)(2,1)S(1)}, u32[]{:S(2)}, u32[]{:S(2)}) %collective-permute-start.16) | collective-permute-done | bytes 98336 | tf_op jit(solution)/shard_map/ppermute | solution.py:431
  75.7 3.9 %collective-permute-start.18 = (bf16[64,768]{1,0:T(8,128)(2,1)S(1)}, bf16[64,768]{1,0:T(8,128)(2,1)S(1)}, u32[]{:S(2)}, u32[]{:S(2)}) collective-permute-start(bf16[64,768]{1,0:T(8,128)(2,1)S(1)} %fusion.6), channel_id=1, source_target_pairs={{0,16},{4,20},{8,24},{12,28},{16,0},{20,4},{24,8},{28,12},{1,17},{... | collective-permute-start | bytes 294920 | tf_op jit(solution)/shard_map/ppermute | solution.py:431
  79.6 1.8 %collective-permute-done.20 = bf16[64,1280]{1,0:T(8,128)(2,1)S(1)} collective-permute-done((bf16[64,1280]{1,0:T(8,128)(2,1)S(1)}, bf16[64,1280]{1,0:T(8,128)(2,1)S(1)}, u32[]{:S(2)}, u32[]{:S(2)}) %collective-permute-start.20) | collective-permute-done | bytes 163872 | tf_op jit(solution)/shard_map/ppermute | solution.py:431
  81.4 0.1 add_convert_fusion
  81.5 0.1 collective-permute-start.23
  81.6 3.5 %collective-permute-done.19 = bf16[64,1024]{1,0:T(8,128)(2,1)S(1)} collective-permute-done((bf16[64,1024]{1,0:T(8,128)(2,1)S(1)}, bf16[64,1024]{1,0:T(8,128)(2,1)S(1)}, u32[]{:S(2)}, u32[]{:S(2)}) %collective-permute-start.19) | collective-permute-done | bytes 131104 | tf_op jit(solution)/shard_map/ppermute | solution.py:431
  85.1 0.1 add_convert_fusion.1
  85.1 0.1 collective-permute-start.22
  85.2 0.9 collective-permute-done.18
  86.1 0.1 add_convert_fusion.2
  86.2 1.2 %collective-permute-start.21 = (bf16[64,768]{1,0:T(8,128)(2,1)S(1)}, bf16[64,768]{1,0:T(8,128)(2,1)S(1)}, u32[]{:S(2)}, u32[]{:S(2)}) collective-permute-start(bf16[64,768]{1,0:T(8,128)(2,1)S(1)} %get-tuple-element.145), channel_id=1, source_target_pairs={{0,4},{4,0},{8,12},{12,8},{16,20},{20,16},{24,28},{28,24},{1,5},{5... | collective-permute-start | bytes 294920 | tf_op jit(solution)/shard_map/ppermute | solution.py:366
  87.4 0.3 collective-permute-done.23.back
  87.7 1.0 %finish.3.refs_0_ = f32[1,128,3072]{2,1,0:T(8,128)} custom-call(s32[1]{0:T(128)} %bitcast.parity, f32[128,3072]{1,0:T(8,128)S(1)} %copy-done.1, f32[64,1280]{1,0:T(8,128)S(1)} %get-tuple-element.150.earlier, f32[64,1280]{1,0:T(8,128)S(1)} %get-tuple-element.121.kept, bf16[64,1280]{1,0:T(8,128)(2,1)S(1)} %collective-permute-done.10.fetched, ...), custom_call_target="tpu_custom_call" | custom-call | tf_op jit(solution)/shard_map/finish/pallas_call | solution.py:321
  88.7 2.6 %collective-permute-done.21.back = bf16[64,768]{1,0:T(8,128)(2,1)S(1)} collective-permute-done((bf16[64,768]{1,0:T(8,128)(2,1)S(1)}, bf16[64,768]{1,0:T(8,128)(2,1)S(1)}, u32[]{:S(2)}, u32[]{:S(2)}) %collective-permute-start.21) | collective-permute-done | bytes 98336 | tf_op jit(solution)/shard_map/ppermute | solution.py:366
  91.2 0.0 collective-permute-done.22.back
  91.2 0.9 finish.4.refs_0_
  92.1 0.8 finish.5
  (30 shorter events, 0.2 us)
Async XLA Ops:
  0.0 7.5 %copy-start.4 = (f32[128]{0:T(128)S(1)}, f32[128]{0:T(128)}, u32[]{:S(2)}) copy-start(f32[128]{0:T(128)} %param.16) | copy-start | bytes 1540
  0.0 7.5 %copy-start.5 = (f32[128]{0:T(128)S(1)}, f32[128]{0:T(128)}, u32[]{:S(2)}) copy-start(f32[128]{0:T(128)} %param.17) | copy-start | bytes 1540
  4.4 3.1 %collective-permute-start.1 = (bf16[128,3072]{1,0:T(8,128)(2,1)}, bf16[128,3072]{1,0:T(8,128)(2,1)S(1)}, u32[]{:S(2)}, u32[]{:S(2)}) collective-permute-start(bf16[128,3072]{1,0:T(8,128)(2,1)} %get-tuple-element.75.m0), channel_id=1, source_target_pairs={{0,1},{1,0},{2,3},{3,2},{4,5},{5,4},{6,7},{7,6},{8,9},{9,8},{10,11... | collective-permute-start | bytes 2359304 | tf_op jit(solution)/shard_map/ppermute | solution.py:360
  4.9 20.9 %collective-permute-start = (bf16[128,3072]{1,0:T(8,128)(2,1)}, bf16[128,3072]{1,0:T(8,128)(2,1)S(1)}, u32[]{:S(2)}, u32[]{:S(2)}) collective-permute-start(bf16[128,3072]{1,0:T(8,128)(2,1)} %get-tuple-element.75.m0), channel_id=1, source_target_pairs={{0,2},{1,3},{2,0},{3,1},{4,6},{5,7},{6,4},{7,5},{8,10},{9,11},{10,... | collective-permute-start | bytes 2359304 | tf_op jit(solution)/shard_map/ppermute | solution.py:363
  7.5 1.2 %copy-start.2 = (bf16[128,3072]{1,0:T(8,128)(2,1)S(1)}, bf16[128,3072]{1,0:T(8,128)(2,1)}, u32[]{:S(2)}) copy-start(bf16[128,3072]{1,0:T(8,128)(2,1)} %get-tuple-element.75.m0) | copy-start | bytes 2359300
  25.9 2.3 %collective-permute-start.2 = (bf16[128,3072]{1,0:T(8,128)(2,1)S(1)}, bf16[128,3072]{1,0:T(8,128)(2,1)S(1)}, u32[]{:S(2)}, u32[]{:S(2)}) collective-permute-start(bf16[128,3072]{1,0:T(8,128)(2,1)S(1)} %collective-permute-done.m0), channel_id=1, source_target_pairs={{0,1},{1,0},{2,3},{3,2},{4,5},{5,4},{6,7},{7,6},{8,9},{9,8},{10,11... | collective-permute-start | bytes 2359304 | tf_op jit(solution)/shard_map/ppermute | solution.py:360
  28.1 7.1 %slice-start = ((s8[9437184]{0:T(1024)(128)(4,1)}), s8[4194304]{0:T(1024)(128)(4,1)S(1)}, s32[]{:S(2)}) async-start(s8[9437184]{0:T(1024)(128)(4,1)} %bitcast.3), calls=%async_computation | async-start | bytes 8388608
  28.1 7.1 %slice-start.1 = ((s8[9437184]{0:T(1024)(128)(4,1)}), s8[4194304]{0:T(1024)(128)(4,1)S(1)}, s32[]{:S(2)}) async-start(s8[9437184]{0:T(1024)(128)(4,1)} %bitcast.3), calls=%async_computation.1 | async-start | bytes 8388608
  28.1 7.1 %slice-start.2 = ((s8[9437184]{0:T(1024)(128)(4,1)}), s8[1048576]{0:T(1024)(128)(4,1)S(1)}, s32[]{:S(2)}) async-start(s8[9437184]{0:T(1024)(128)(4,1)} %bitcast.3), calls=%async_computation.2 | async-start | bytes 2097152
  28.1 7.2 %copy-start = (bf16[512,3072]{1,0:T(8,128)(2,1)S(1)}, bf16[512,3072]{1,0:T(8,128)(2,1)}, u32[]{:S(2)}) copy-start(bf16[512,3072]{1,0:T(8,128)(2,1)} %refs_17_.1) | copy-start | bytes 9437188
  36.9 1.9 %collective-permute-start.3 = (bf16[128,1280]{1,0:T(8,128)(2,1)S(1)}, bf16[128,1280]{1,0:T(8,128)(2,1)S(1)}, u32[]{:S(2)}, u32[]{:S(2)}) collective-permute-start(bf16[128,1280]{1,0:T(8,128)(2,1)S(1)} %get-tuple-element.93), channel_id=1, source_target_pairs={{0,1},{1,0},{2,3},{3,2},{4,5},{5,4},{6,7},{7,6},{8,9},{9,8},{10,11... | collective-permute-start | bytes 983048 | tf_op jit(solution)/shard_map/ppermute | solution.py:360
  38.8 13.1 %copy-start.3 = (f32[1,3072]{1,0:T(1,128)S(1)}, f32[1,3072]{1,0:T(1,128)}, u32[]{:S(2)}) copy-start(f32[1,3072]{1,0:T(1,128)} %get-tuple-element.115.sg) | copy-start | bytes 36868
  38.8 10.1 %collective-permute-start.4 = (bf16[128,1280]{1,0:T(8,128)(2,1)S(1)}, bf16[128,1280]{1,0:T(8,128)(2,1)S(1)}, u32[]{:S(2)}, u32[]{:S(2)}) collective-permute-start(bf16[128,1280]{1,0:T(8,128)(2,1)S(1)} %join.3), channel_id=1, source_target_pairs={{0,2},{1,3},{2,0},{3,1},{4,6},{5,7},{6,4},{7,5},{8,10},{9,11},{10,... | collective-permute-start | bytes 983048 | tf_op jit(solution)/shard_map/ppermute | solution.py:363
  44.2 5.5 %copy-start.6 = (bf16[128,768]{1,0:T(8,128)(2,1)}, bf16[128,768]{1,0:T(8,128)(2,1)S(1)}, u32[]{:S(2)}) copy-start(bf16[128,768]{1,0:T(8,128)(2,1)S(1)} %get-tuple-element.114) | copy-start | bytes 589828
  44.2 1.5 %collective-permute-start.5 = (bf16[128,1024]{1,0:T(8,128)(2,1)S(1)}, bf16[128,1024]{1,0:T(8,128)(2,1)S(1)}, u32[]{:S(2)}, u32[]{:S(2)}) collective-permute-start(bf16[128,1024]{1,0:T(8,128)(2,1)S(1)} %get-tuple-element.107), channel_id=1, source_target_pairs={{0,1},{1,0},{2,3},{3,2},{4,5},{5,4},{6,7},{7,6},{8,9},{9,8},{10,11... | collective-permute-start | bytes 786440 | tf_op jit(solution)/shard_map/ppermute | solution.py:360
  44.3 7.7 %collective-permute-start.9 = (bf16[128,1280]{1,0:T(8,128)(2,1)S(1)}, bf16[128,1280]{1,0:T(8,128)(2,1)S(1)}, u32[]{:S(2)}, u32[]{:S(2)}) collective-permute-start(bf16[128,1280]{1,0:T(8,128)(2,1)S(1)} %get-tuple-element.119), channel_id=1, source_target_pairs={{0,1},{1,0},{2,3},{3,2},{4,5},{5,4},{6,7},{7,6},{8,9},{9,8},{10,11... | collective-permute-start | bytes 983048 | tf_op jit(solution)/shard_map/ppermute | solution.py:360
  49.7 8.0 %collective-permute-start.12 = (bf16[128,1024]{1,0:T(8,128)(2,1)}, bf16[128,1024]{1,0:T(8,128)(2,1)S(1)}, u32[]{:S(2)}, u32[]{:S(2)}) collective-permute-start(bf16[128,1024]{1,0:T(8,128)(2,1)} %join.4), channel_id=1, source_target_pairs={{0,2},{1,3},{2,0},{3,1},{4,6},{5,7},{6,4},{7,5},{8,10},{9,11},{10,... | collective-permute-start | bytes 786440 | tf_op jit(solution)/shard_map/ppermute | solution.py:363
  51.4 6.3 %collective-permute-start.11 = (bf16[128,1024]{1,0:T(8,128)(2,1)}, bf16[128,1024]{1,0:T(8,128)(2,1)}, u32[]{:S(2)}, u32[]{:S(2)}) collective-permute-start(bf16[128,1024]{1,0:T(8,128)(2,1)} %get-tuple-element.124), channel_id=1, source_target_pairs={{0,1},{1,0},{2,3},{3,2},{4,5},{5,4},{6,7},{7,6},{8,9},{9,8},{10,11... | collective-permute-start | bytes 786440 | tf_op jit(solution)/shard_map/ppermute | solution.py:360
  51.4 2.8 %collective-permute-start.7 = (bf16[128,768]{1,0:T(8,128)(2,1)}, bf16[128,768]{1,0:T(8,128)(2,1)}, u32[]{:S(2)}, u32[]{:S(2)}) collective-permute-start(bf16[128,768]{1,0:T(8,128)(2,1)} %get-tuple-element.117), channel_id=1, source_target_pairs={{0,1},{1,0},{2,3},{3,2},{4,5},{5,4},{6,7},{7,6},{8,9},{9,8},{10,11... | collective-permute-start | bytes 589832 | tf_op jit(solution)/shard_map/ppermute | solution.py:360
  52.7 8.4 %collective-permute-start.10 = (bf16[64,1280]{1,0:T(8,128)(2,1)}, bf16[64,1280]{1,0:T(8,128)(2,1)S(1)}, u32[]{:S(2)}, u32[]{:S(2)}) collective-permute-start(bf16[64,1280]{1,0:T(8,128)(2,1)} %get-tuple-element.122), channel_id=1, source_target_pairs={{0,4},{4,0},{8,12},{12,8},{16,20},{20,16},{24,28},{28,24},{1,5},{5... | collective-permute-start | bytes 491528 | tf_op jit(solution)/shard_map/ppermute | solution.py:366
  54.2 8.6 %collective-permute-start.6 = (bf16[128,768]{1,0:T(8,128)(2,1)}, bf16[128,768]{1,0:T(8,128)(2,1)S(1)}, u32[]{:S(2)}, u32[]{:S(2)}) collective-permute-start(bf16[128,768]{1,0:T(8,128)(2,1)} %copy-done.6), channel_id=1, source_target_pairs={{0,1},{1,0},{2,3},{3,2},{4,5},{5,4},{6,7},{7,6},{8,9},{9,8},{10,11... | collective-permute-start | bytes 589832 | tf_op jit(solution)/shard_map/ppermute | solution.py:360
  55.2 7.7 %collective-permute-start.8 = (bf16[128,768]{1,0:T(8,128)(2,1)S(1)}, bf16[128,768]{1,0:T(8,128)(2,1)S(1)}, u32[]{:S(2)}, u32[]{:S(2)}) collective-permute-start(bf16[128,768]{1,0:T(8,128)(2,1)S(1)} %join.5), channel_id=1, source_target_pairs={{0,2},{1,3},{2,0},{3,1},{4,6},{5,7},{6,4},{7,5},{8,10},{9,11},{10,... | collective-permute-start | bytes 589832 | tf_op jit(solution)/shard_map/ppermute | solution.py:363
  58.7 5.3 %collective-permute-start.15 = (bf16[64,1024]{1,0:T(8,128)(2,1)S(1)}, bf16[64,1024]{1,0:T(8,128)(2,1)S(1)}, u32[]{:S(2)}, u32[]{:S(2)}) collective-permute-start(bf16[64,1024]{1,0:T(8,128)(2,1)S(1)} %get-tuple-element.127), channel_id=1, source_target_pairs={{0,4},{4,0},{8,12},{12,8},{16,20},{20,16},{24,28},{28,24},{1,5},{5... | collective-permute-start | bytes 393224 | tf_op jit(solution)/shard_map/ppermute | solution.py:366
  61.2 26.5 %copy-start.1 = (f32[128,3072]{1,0:T(8,128)S(1)}, f32[128,3072]{1,0:T(8,128)}, u32[]{:S(2)}) copy-start(f32[128,3072]{1,0:T(8,128)} %x_start.5) | copy-start | bytes 4718596
  61.2 6.1 %collective-permute-start.14 = (bf16[64,1280]{1,0:T(8,128)(2,1)S(1)}, bf16[64,1280]{1,0:T(8,128)(2,1)S(1)}, u32[]{:S(2)}, u32[]{:S(2)}) collective-permute-start(bf16[64,1280]{1,0:T(8,128)(2,1)S(1)} %fusion.4), channel_id=1, source_target_pairs={{0,8},{4,12},{8,0},{12,4},{16,24},{20,28},{24,16},{28,20},{1,9},{5... | collective-permute-start | bytes 491528 | tf_op jit(solution)/shard_map/ppermute | solution.py:431
  62.9 7.1 %collective-permute-start.13 = (bf16[64,768]{1,0:T(8,128)(2,1)S(1)}, bf16[64,768]{1,0:T(8,128)(2,1)S(1)}, u32[]{:S(2)}, u32[]{:S(2)}) collective-permute-start(bf16[64,768]{1,0:T(8,128)(2,1)S(1)} %get-tuple-element.131), channel_id=1, source_target_pairs={{0,4},{4,0},{8,12},{12,8},{16,20},{20,16},{24,28},{28,24},{1,5},{5... | collective-permute-start | bytes 294920 | tf_op jit(solution)/shard_map/ppermute | solution.py:366
  64.1 8.7 %collective-permute-start.17 = (bf16[64,1024]{1,0:T(8,128)(2,1)S(1)}, bf16[64,1024]{1,0:T(8,128)(2,1)S(1)}, u32[]{:S(2)}, u32[]{:S(2)}) collective-permute-start(bf16[64,1024]{1,0:T(8,128)(2,1)S(1)} %fusion.7), channel_id=1, source_target_pairs={{0,8},{4,12},{8,0},{12,4},{16,24},{20,28},{24,16},{28,20},{1,9},{5... | collective-permute-start | bytes 393224 | tf_op jit(solution)/shard_map/ppermute | solution.py:431
  67.4 14.1 %collective-permute-start.20 = (bf16[64,1280]{1,0:T(8,128)(2,1)S(1)}, bf16[64,1280]{1,0:T(8,128)(2,1)S(1)}, u32[]{:S(2)}, u32[]{:S(2)}) collective-permute-start(bf16[64,1280]{1,0:T(8,128)(2,1)S(1)} %fusion), channel_id=1, source_target_pairs={{0,16},{4,20},{8,24},{12,28},{16,0},{20,4},{24,8},{28,12},{1,17},{... | collective-permute-start | bytes 491528 | tf_op jit(solution)/shard_map/ppermute | solution.py:431
  70.0 5.6 %collective-permute-start.16 = (bf16[64,768]{1,0:T(8,128)(2,1)S(1)}, bf16[64,768]{1,0:T(8,128)(2,1)S(1)}, u32[]{:S(2)}, u32[]{:S(2)}) collective-permute-start(bf16[64,768]{1,0:T(8,128)(2,1)S(1)} %fusion.8), channel_id=1, source_target_pairs={{0,8},{4,12},{8,0},{12,4},{16,24},{20,28},{24,16},{28,20},{1,9},{5... | collective-permute-start | bytes 294920 | tf_op jit(solution)/shard_map/ppermute | solution.py:431
  72.8 12.2 %collective-permute-start.19 = (bf16[64,1024]{1,0:T(8,128)(2,1)S(1)}, bf16[64,1024]{1,0:T(8,128)(2,1)S(1)}, u32[]{:S(2)}, u32[]{:S(2)}) collective-permute-start(bf16[64,1024]{1,0:T(8,128)(2,1)S(1)} %fusion.2), channel_id=1, source_target_pairs={{0,16},{4,20},{8,24},{12,28},{16,0},{20,4},{24,8},{28,12},{1,17},{... | collective-permute-start | bytes 393224 | tf_op jit(solution)/shard_map/ppermute | solution.py:431
  75.7 10.4 %collective-permute-start.18 = (bf16[64,768]{1,0:T(8,128)(2,1)S(1)}, bf16[64,768]{1,0:T(8,128)(2,1)S(1)}, u32[]{:S(2)}, u32[]{:S(2)}) collective-permute-start(bf16[64,768]{1,0:T(8,128)(2,1)S(1)} %fusion.6), channel_id=1, source_target_pairs={{0,16},{4,20},{8,24},{12,28},{16,0},{20,4},{24,8},{28,12},{1,17},{... | collective-permute-start | bytes 294920 | tf_op jit(solution)/shard_map/ppermute | solution.py:431
  81.5 6.2 %collective-permute-start.23 = (bf16[64,1280]{1,0:T(8,128)(2,1)S(1)}, bf16[64,1280]{1,0:T(8,128)(2,1)S(1)}, u32[]{:S(2)}, u32[]{:S(2)}) collective-permute-start(bf16[64,1280]{1,0:T(8,128)(2,1)S(1)} %get-tuple-element.149), channel_id=1, source_target_pairs={{0,4},{4,0},{8,12},{12,8},{16,20},{20,16},{24,28},{28,24},{1,5},{5... | collective-permute-start | bytes 491528 | tf_op jit(solution)/shard_map/ppermute | solution.py:366
  85.1 6.1 %collective-permute-start.22 = (bf16[64,1024]{1,0:T(8,128)(2,1)S(1)}, bf16[64,1024]{1,0:T(8,128)(2,1)S(1)}, u32[]{:S(2)}, u32[]{:S(2)}) collective-permute-start(bf16[64,1024]{1,0:T(8,128)(2,1)S(1)} %get-tuple-element.147), channel_id=1, source_target_pairs={{0,4},{4,0},{8,12},{12,8},{16,20},{20,16},{24,28},{28,24},{1,5},{5... | collective-permute-start | bytes 393224 | tf_op jit(solution)/shard_map/ppermute | solution.py:366
  86.2 5.1 %collective-permute-start.21 = (bf16[64,768]{1,0:T(8,128)(2,1)S(1)}, bf16[64,768]{1,0:T(8,128)(2,1)S(1)}, u32[]{:S(2)}, u32[]{:S(2)}) collective-permute-start(bf16[64,768]{1,0:T(8,128)(2,1)S(1)} %get-tuple-element.145), channel_id=1, source_target_pairs={{0,4},{4,0},{8,12},{12,8},{16,20},{20,16},{24,28},{28,24},{1,5},{5... | collective-permute-start | bytes 294920 | tf_op jit(solution)/shard_map/ppermute | solution.py:366

commit v7 on v6

--- a/solution.py
+++ b/solution.py
@@ -431,15 +431,17 @@
         return lambda x: lax.ppermute(x, "step", [(2 * a + i, 2 * b + i) for a, b in pairs for i in (0, 1)])
 
     group = lax.div(lax.axis_index("step"), 2)
-    rounds = []
-    span = 1
-    while span < groups:
-        pairs = [(b, b ^ span) for b in range(groups) if b ^ span < groups]
-        rounds.append((span, along(pairs)))
-        span *= 2
-
-    def prefix_stages(c):
+    spans = []
+    while 2 ** len(spans) < groups:
+        spans.append(2 ** len(spans))
+
+    def swap(span):
+        return along([(b, b ^ span) for b in range(groups) if b ^ span < groups])
+
+    def prefix_stages(c, halves):
         held = {}
+        quarter = half // 2
+        bit = lax.rem(group, 2)
 
         def drift_of(fetched):
             drift = drift_call(which, keep[c], sent0[c], sg, fetched, firsts[c])
@@ -452,41 +454,65 @@
             return held["total"].astype(bf16)
 
         def collect(r, fetched):
-            one = fetched[0].astype(f32)
-            upper = (lax.rem(lax.div(group, rounds[r][0]), 2) == 1).astype(f32)
+            one = fetched[0]
+            if halves and spans[r] == 2:
+                both = [held["piece"], one]
+                one = jnp.where(
+                    bit == 0, jnp.concatenate(both, axis=0), jnp.concatenate(both[::-1], axis=0)
+                )
+            one = one.astype(f32)
+            upper = (lax.rem(lax.div(group, spans[r]), 2) == 1).astype(f32)
             held["earlier"] = held["earlier"] + upper * one if r else upper * one
-            if r == len(rounds) - 1:
+            if r == len(spans) - 1:
                 return (held["earlier"] + even * held["kept"]).astype(bf16)
             held["total"] = held["total"] + one
-            return held["total"].astype(bf16)
+            total = held["total"].astype(bf16)
+            if halves and spans[r + 1] == 2:
+                return lax.dynamic_slice_in_dim(total, bit * quarter, quarter, 0)
+            return total
+
+        def pass_on(fetched):
+            held["piece"] = fetched[0]
+            return fetched[0]
 
         def finish(fetched):
             given = [held[name] for name in ("earlier", "kept", "fetched", "other")]
             into = list(written)
             written[:] = [finish_call(which, x_start, *given, fetched[0], into, firsts[c])]
 
-        stages = [(drift_of, to_pair), (pair_sum, rounds[0][1])]
-        for r in range(len(rounds)):
-            move = to_pair if r == len(rounds) - 1 else rounds[r + 1][1]
-            stages.append((functools.partial(collect, r), move))
-        stages.append((finish, None))
+        stages = [(drift_of, to_pair, "x", 0.5), (pair_sum, swap(1), "z1", 0.5)]
+        for r in range(len(spans)):
+            take = functools.partial(collect, r)
+            if r == len(spans) - 1:
+                stages.append((take, to_pair, "x", 0.5))
+            elif halves and spans[r + 1] == 2:
+                stages.append((take, swap(2), "z2", 0.5))
+                stages.append((pass_on, swap(1), "z1", 0.25))
+            else:
+                stages.append((take, swap(spans[r + 1]), "z2", 1.0))
+        stages.append((finish, None, "", 0.0))
         return stages
 
-    plan = [prefix_stages(c) for c in range(chunks)]
+    plan = [prefix_stages(c, c < chunks - 1) for c in range(chunks)]
     inbox = [[got[j][c] for j in range(chips - 1)] for c in range(chunks)]
+    shares = [18.5 * n / width for n in counts]
+    ends = [2.0 + sum(shares[: c + 1]) for c in range(chunks)]
+    waits = [(end, c, 0) for c, end in enumerate(ends)]
+    free = {"x": 0.0, "z1": 0.0, "z2": 0.0, "": 0.0}
     turns = []
-    arrival = 2.0
-    for c in range(chunks):
-        share = 16.0 * counts[c] / width
-        arrival += share
-        when = arrival
-        for i in range(len(plan[c])):
-            turns.append((when, c, i))
-            when += 2.2 + share * (1.0 if i == len(plan[c]) - 3 else 0.5)
+    while waits:
+        when, c, i = min(waits)
+        waits.remove((when, c, i))
+        turns.append((c, i))
+        if i + 1 < len(plan[c]):
+            link, load = plan[c][i][2:]
+            begin = max(when + 2.0, free[link])
+            free[link] = begin + load * shares[c]
+            waits.append((free[link] + 0.7, c, i + 1))
     written = []
     last = None
-    for _, c, i in sorted(turns):
-        compute, move = plan[c][i]
+    for c, i in turns:
+        compute, move = plan[c][i][:2]
         fetched = inbox[c]
         if last is not None:
             fetched, last = tied(fetched, last)

time: 93.4 us -> 93.6 us (level)
  starting transfers between devices: 28 us -> 32.2 us
  waiting for transfers between devices: 26.2 us -> 22.2 us
    ppermute x6 -> x8, waiting for transfers between devices: 9.72 us -> 4.75 us  [along(): lax.ppermute(x, 'step', [(2 * a + i, 2 * b + i) for a, b in pairs for i i...]
    ppermute x6 -> x8, starting transfers between devices: 13.4 us -> 16.1 us  [along(): lax.ppermute(x, 'step', [(2 * a + i, 2 * b + i) for a, b in pairs for i i...]
    ppermute x6, starting transfers between devices: 6.05 us -> 7.59 us  [to_pair(): return lax.ppermute(x, 'step', [(i, i ^ 1) for i in range(n_step)])]
    ppermute x6, waiting for transfers between devices: 3.19 us -> 4.16 us  [to_pair(): return lax.ppermute(x, 'step', [(i, i ^ 1) for i in range(n_step)])]
  transfers between devices with their start and end apart: 24 -> 26, of which waited for: 13 -> 10; matrix products, arithmetic and copies ran while one was open for 0% -> 0% of each run, Pallas kernels for 24% -> 24%
where the time goes in v7:
time: 93.6 us; the launch traced here: 93.3 us
  Pallas kernels  36.2 us (39%)
  starting transfers between devices  32.2 us (34%)
  waiting for transfers between devices  22.2 us (24%)
  local copies, waits for them, and re-layouts  1.18 us (1%)
  between operations  1.07 us (1%)
    pallas_call x2, Pallas kernels, project_call(): pl.pallas_call(functools.partial(project_kernel, tile, load, tiles), in_s...  17.6 us
    ppermute x8, starting transfers between devices, along(): lax.ppermute(x, 'step', [(2 * a + i, 2 * b + i) for a, b in pairs for i i...  16.1 us
    ppermute x4, waiting for transfers between devices, to_chip(): lax.ppermute(x, 'seq', [(i, (i + 2 * offset) % n_seq) for i in range(n_se...  9.97 us
    ppermute x6, starting transfers between devices, to_pair(): return lax.ppermute(x, 'step', [(i, i ^ 1) for i in range(n_step)])  7.59 us
    ppermute x4, starting transfers between devices, to_chip(): lax.ppermute(x, 'seq', [(i, (i + 2 * offset) % n_seq) for i in range(n_se...  6.76 us
    pallas_call x2, Pallas kernels, out_call(): pl.pallas_call(functools.partial(out_kernel, plan), in_specs=[vm] * len(g...  5.02 us
    ppermute x8, waiting for transfers between devices, along(): lax.ppermute(x, 'step', [(2 * a + i, 2 * b + i) for a, b in pairs for i i...  4.75 us
    ppermute x6, waiting for transfers between devices, to_pair(): return lax.ppermute(x, 'step', [(i, i ^ 1) for i in range(n_step)])  4.16 us
  transfers between devices with their start and end apart: 26, of which 10 were waited for; matrix products, arithmetic and copies ran while one was open for 0% of the time, Pallas kernels for 24%

profile of v7, /device:TPU:0, one launch (start us, length us, event | category | flops | bytes accessed | tf_op | source)
XLA Modules:
  0.0 93.3 jit_solution(3967391863400745756)
XLA Ops:
  0.7 3.7 %norm.1 = (bf16[128,3072]{1,0:T(8,128)(2,1)}, f32[1,3072]{1,0:T(1,128)}) custom-call(s32[1]{0:T(128)S(6)} %copy.16.t_ref, f32[50]{0:T(128)} %size_ref.1, f32[1,128,3072]{2,1,0:T(8,128)} %x_hbm.1, f32[50,9216]{1,0:T(8,128)} %mod_hbm.1), custom_call_target="tpu_custom_call" | custom-call | flops 3932160 | tf_op jit(solution)/shard_map/norm/pallas_call | solution.py:56
  4.4 0.5 collective-permute-start.1
  4.9 2.6 %collective-permute-start = (bf16[128,3072]{1,0:T(8,128)(2,1)}, bf16[128,3072]{1,0:T(8,128)(2,1)S(1)}, u32[]{:S(2)}, u32[]{:S(2)}) collective-permute-start(bf16[128,3072]{1,0:T(8,128)(2,1)} %get-tuple-element.77.m0), channel_id=1, source_target_pairs={{0,2},{1,3},{2,0},{3,1},{4,6},{5,7},{6,4},{7,5},{8,10},{9,11},{10,... | collective-permute-start | bytes 2359304 | tf_op jit(solution)/shard_map/ppermute | solution.py:363
  7.5 0.0 collective-permute-done.1.m1
  7.5 0.0 copy-start.2
  7.5 1.1 %copy-done.2 = bf16[128,3072]{1,0:T(8,128)(2,1)S(1)} copy-done((bf16[128,3072]{1,0:T(8,128)(2,1)S(1)}, bf16[128,3072]{1,0:T(8,128)(2,1)}, u32[]{:S(2)}) %copy-start.2) | copy-done | bytes 786456
  8.7 12.4 %project.2 = (bf16[256,512]{1,0:T(8,128)(2,1)S(1)}, bf16[256,512]{1,0:T(8,128)(2,1)S(1)}, bf16[256,512]{1,0:T(8,128)(2,1)S(1)}, bf16[256,1536]{1,0:T(8,128)(2,1)...) custom-call(bf16[128,3072]{1,0:T(8,128)(2,1)S(1)} %copy-done.2, ...), custom_call_target="tpu_custom_call" | custom-call | flops 4831838208 | tf_op jit(solution)/shard_map/project/pallas_call | solution.py:151
  21.1 4.8 %collective-permute-done.m0 = bf16[128,3072]{1,0:T(8,128)(2,1)S(1)} collective-permute-done((bf16[128,3072]{1,0:T(8,128)(2,1)}, bf16[128,3072]{1,0:T(8,128)(2,1)S(1)}, u32[]{:S(2)}, u32[]{:S(2)}) %collective-permute-start) | collective-permute-done | bytes 786464 | tf_op jit(solution)/shard_map/ppermute | solution.py:363
  25.9 2.3 %collective-permute-done.2.m1 = bf16[128,3072]{1,0:T(8,128)(2,1)S(1)} collective-permute-done((bf16[128,3072]{1,0:T(8,128)(2,1)S(1)}, bf16[128,3072]{1,0:T(8,128)(2,1)S(1)}, u32[]{:S(2)}, u32[]{:S(2)}) %collective-permute-start.2) | collective-permute-done | bytes 786464 | tf_op jit(solution)/shard_map/ppermute | solution.py:360
  28.2 5.2 %project.3 = (bf16[256,512]{1,0:T(8,128)(2,1)S(1)}, bf16[256,512]{1,0:T(8,128)(2,1)S(1)}, bf16[256,512]{1,0:T(8,128)(2,1)S(1)}, bf16[256,1536]{1,0:T(8,128)(2,1)S(1)}) custom-call(bf16[128,3072]{1,0:T(8,128)(2,1)S(1)} %collective-permute-done.m0, bf16[128,3072]{1,0:T(8,128)(2,1)S(1)} %collective-permute-done.2.m1, f32[1,128]{1,0:T(1,128)S(1)} %bitcast.6, ...), custom_call_target="tpu_custom_call" | custom-call | flops 4831838208 | tf_op jit(solution)/shard_map/project/pallas_call | solution.py:151
  33.4 1.9 %attend.2.refs_0_.refs_4_ = bf16[256,512]{1,0:T(8,128)(2,1)S(1)} custom-call(bf16[256,512]{1,0:T(8,128)(2,1)S(1)} %get-tuple-element.87.refs_0_, bf16[256,512]{1,0:T(8,128)(2,1)S(1)} %get-tuple-element.88.refs_1_, bf16[256,512]{1,0:T(8,128)(2,1)S(1)} %get-tuple-element.89.refs_2_, bf16[256,512]{1,0:T(8,128)(2,1)S(1)} %get-tuple-element.90.refs_3_, ...), custom_call_target="tpu_custom_call" | custom-call | flops 805306368 | tf_op jit(solution)/shard_map/attend/pallas_call | solution.py:191
  35.3 1.5 %project_out.2 = (f32[128,1280]{1,0:T(8,128)S(1)}, bf16[128,1280]{1,0:T(8,128)(2,1)S(1)}) custom-call(bf16[256,512]{1,0:T(8,128)(2,1)S(1)} %attend.2.refs_0_.refs_4_, bf16[256,1536]{1,0:T(8,128)(2,1)S(1)} %get-tuple-element.102.refs_1_.refs_5_, bf16[512,3072]{1,0:T(8,128)(2,1)S(1)} %copy-done, bf16[1536,3072]{1,0:T(8,128)(2,1)S(1)} %bitcast.4), custom_call_target="tpu_custom_call" | custom-call | flops 1342177280 | tf_op jit(solution)/shard_map/project_out/pallas_call | solution.py:235
  36.9 0.2 collective-permute-start.3
  37.1 1.7 %attend.3.refs_8_.refs_12_.refs_16_ = bf16[256,512]{1,0:T(8,128)(2,1)S(1)} custom-call(bf16[256,512]{1,0:T(8,128)(2,1)S(1)} %get-tuple-element.96.refs_0_, bf16[256,512]{1,0:T(8,128)(2,1)S(1)} %get-tuple-element.88.refs_1_, bf16[256,512]{1,0:T(8,128)(2,1)S(1)} %get-tuple-element.89.refs_2_, bf16[256,512]{1,0:T(8,128)(2,1)S(1)} %get-tuple-element.90.refs_3_, ...), custom_call_target="tpu_custom_call" | custom-call | flops 805306368 | tf_op jit(solution)/shard_map/attend/pallas_call | solution.py:191
  38.8 0.0 collective-permute-done.3.sent
  38.8 0.1 join.3
  38.8 1.9 %collective-permute-start.4 = (bf16[128,1280]{1,0:T(8,128)(2,1)S(1)}, bf16[128,1280]{1,0:T(8,128)(2,1)S(1)}, u32[]{:S(2)}, u32[]{:S(2)}) collective-permute-start(bf16[128,1280]{1,0:T(8,128)(2,1)S(1)} %join.3), channel_id=1, source_target_pairs={{0,2},{1,3},{2,0},{3,1},{4,6},{5,7},{6,4},{7,5},{8,10},{9,11},{10,... | collective-permute-start | bytes 983048 | tf_op jit(solution)/shard_map/ppermute | solution.py:363
  40.7 3.5 %project_out.3 = (f32[128,1024]{1,0:T(8,128)S(1)}, bf16[128,1024]{1,0:T(8,128)(2,1)S(1)}, f32[128,768]{1,0:T(8,128)S(1)}, bf16[128,768]{1,0:T(8,128)(2,1)}, f32[...) custom-call(bf16[256,512]{1,0:T(8,128)(2,1)S(1)} %attend.2.refs_0_.r, ...), custom_call_target="tpu_custom_call" | custom-call | flops 2684354560 | tf_op jit(solution)/shard_map/project_out/pallas_call | solution.py:235
  44.2 0.1 collective-permute-start.5
  44.3 0.4 collective-permute-start.9
  44.7 1.0 %collective-permute-done.5.sent = bf16[128,1024]{1,0:T(8,128)(2,1)S(1)} collective-permute-done((bf16[128,1024]{1,0:T(8,128)(2,1)S(1)}, bf16[128,1024]{1,0:T(8,128)(2,1)S(1)}, u32[]{:S(2)}, u32[]{:S(2)}) %collective-permute-start.5) | collective-permute-done | bytes 262176 | tf_op jit(solution)/shard_map/ppermute | solution.py:360
  45.7 3.2 %collective-permute-done.4.refs_0_ = bf16[128,1280]{1,0:T(8,128)(2,1)S(1)} collective-permute-done((bf16[128,1280]{1,0:T(8,128)(2,1)S(1)}, bf16[128,1280]{1,0:T(8,128)(2,1)S(1)}, u32[]{:S(2)}, u32[]{:S(2)}) %collective-permute-start.4) | collective-permute-done | bytes 327712 | tf_op jit(solution)/shard_map/ppermute | solution.py:363
  48.9 0.7 join.4
  49.7 1.7 %collective-permute-start.12 = (bf16[128,1024]{1,0:T(8,128)(2,1)}, bf16[128,1024]{1,0:T(8,128)(2,1)S(1)}, u32[]{:S(2)}, u32[]{:S(2)}) collective-permute-start(bf16[128,1024]{1,0:T(8,128)(2,1)} %join.4), channel_id=1, source_target_pairs={{0,2},{1,3},{2,0},{3,1},{4,6},{5,7},{6,4},{7,5},{8,10},{9,11},{10,... | collective-permute-start | bytes 786440 | tf_op jit(solution)/shard_map/ppermute | solution.py:363
  51.4 0.0 collective-permute-start.11
  51.4 0.5 collective-permute-start.7
  51.9 0.7 drift.3
  52.7 1.5 %collective-permute-start.10 = (bf16[64,1280]{1,0:T(8,128)(2,1)}, bf16[64,1280]{1,0:T(8,128)(2,1)S(1)}, u32[]{:S(2)}, u32[]{:S(2)}) collective-permute-start(bf16[64,1280]{1,0:T(8,128)(2,1)} %get-tuple-element.124), channel_id=1, source_target_pairs={{0,4},{4,0},{8,12},{12,8},{16,20},{20,16},{24,28},{28,24},{1,5},{5... | collective-permute-start | bytes 491528 | tf_op jit(solution)/shard_map/ppermute | solution.py:366
  54.2 1.0 %join.5 = bf16[128,768]{1,0:T(8,128)(2,1)S(1)} custom-call(f32[128,768]{1,0:T(8,128)S(1)} %get-tuple-element.118.keep, bf16[128,768]{1,0:T(8,128)(2,1)} %collective-permute-done.7.sent), custom_call_target="tpu_custom_call" | custom-call | tf_op jit(solution)/shard_map/join/pallas_call | solution.py:253
  55.1 0.6 collective-permute-start.8
  55.7 2.0 %collective-permute-done.12.refs_0_ = bf16[128,1024]{1,0:T(8,128)(2,1)S(1)} collective-permute-done((bf16[128,1024]{1,0:T(8,128)(2,1)}, bf16[128,1024]{1,0:T(8,128)(2,1)S(1)}, u32[]{:S(2)}, u32[]{:S(2)}) %collective-permute-start.12) | collective-permute-done | bytes 262176 | tf_op jit(solution)/shard_map/ppermute | solution.py:363
  57.7 0.0 collective-permute-done.11.sent
  57.7 1.0 %drift.4 = (f32[64,1024]{1,0:T(8,128)S(1)}, f32[64,1024]{1,0:T(8,128)S(1)}, bf16[64,1024]{1,0:T(8,128)(2,1)S(1)}) custom-call(s32[1]{0:T(128)} %bitcast.parity, f32[128,1024]{1,0:T(8,128)S(1)} %get-tuple-element.125.keep, bf16[128,1024]{1,0:T(8,128)(2,1)} %collective-permute-done.11.sent, f32[1,3072]{1,0:T(1,128)S(1)} %copy-done.3, ...), custom_call_target="tpu_custom_call" | custom-call | tf_op jit(solution)/shard_map/drift/pallas_call | solution.py:286
  58.7 2.4 %collective-permute-start.15 = (bf16[64,1024]{1,0:T(8,128)(2,1)S(1)}, bf16[64,1024]{1,0:T(8,128)(2,1)S(1)}, u32[]{:S(2)}, u32[]{:S(2)}) collective-permute-start(bf16[64,1024]{1,0:T(8,128)(2,1)S(1)} %get-tuple-element.129), channel_id=1, source_target_pairs={{0,4},{4,0},{8,12},{12,8},{16,20},{20,16},{24,28},{28,24},{1,5},{5... | collective-permute-start | bytes 393224 | tf_op jit(solution)/shard_map/ppermute | solution.py:366
  61.1 0.0 collective-permute-done.10.fetched
  61.1 1.7 %collective-permute-start.14 = (bf16[64,1280]{1,0:T(8,128)(2,1)S(1)}, bf16[64,1280]{1,0:T(8,128)(2,1)S(1)}, u32[]{:S(2)}, u32[]{:S(2)}) collective-permute-start(bf16[64,1280]{1,0:T(8,128)(2,1)S(1)} %get-tuple-element.157), channel_id=1, source_target_pairs={{0,8},{4,12},{8,0},{12,4},{16,24},{20,28},{24,16},{28,20},{1,9},{5... | collective-permute-start | bytes 491528 | tf_op jit(solution)/shard_map/ppermute | solution.py:431
  62.8 0.0 collective-permute-done.8.refs_0_
  62.8 0.0 collective-permute-done.6.sent
  62.8 0.1 drift.5
  62.9 0.0 copy-start.1
  62.9 0.9 collective-permute-start.13
  63.8 0.3 collective-permute-done.15.fetched
  64.1 1.7 %collective-permute-start.18 = (bf16[64,1024]{1,0:T(8,128)(2,1)S(1)}, bf16[64,1024]{1,0:T(8,128)(2,1)S(1)}, u32[]{:S(2)}, u32[]{:S(2)}) collective-permute-start(bf16[64,1024]{1,0:T(8,128)(2,1)S(1)} %get-tuple-element.155), channel_id=1, source_target_pairs={{0,8},{4,12},{8,0},{12,4},{16,24},{20,28},{24,16},{28,20},{1,9},{5... | collective-permute-start | bytes 393224 | tf_op jit(solution)/shard_map/ppermute | solution.py:431
  65.7 1.5 %collective-permute-done.14 = bf16[64,1280]{1,0:T(8,128)(2,1)S(1)} collective-permute-done((bf16[64,1280]{1,0:T(8,128)(2,1)S(1)}, bf16[64,1280]{1,0:T(8,128)(2,1)S(1)}, u32[]{:S(2)}, u32[]{:S(2)}) %collective-permute-start.14) | collective-permute-done | bytes 163872 | tf_op jit(solution)/shard_map/ppermute | solution.py:431
  67.3 2.7 %collective-permute-start.17 = (bf16[32,1280]{1,0:T(8,128)(2,1)S(1)}, bf16[32,1280]{1,0:T(8,128)(2,1)S(1)}, u32[]{:S(2)}, u32[]{:S(2)}) collective-permute-start(bf16[32,1280]{1,0:T(8,128)(2,1)S(1)} %fusion.2), channel_id=1, source_target_pairs={{0,16},{4,20},{8,24},{12,28},{16,0},{20,4},{24,8},{28,12},{1,17},{... | collective-permute-start | bytes 245768 | tf_op jit(solution)/shard_map/ppermute | solution.py:431
  70.0 0.0 collective-permute-done.13.fetched
  70.0 2.5 %collective-permute-start.16 = (bf16[64,768]{1,0:T(8,128)(2,1)S(1)}, bf16[64,768]{1,0:T(8,128)(2,1)S(1)}, u32[]{:S(2)}, u32[]{:S(2)}) collective-permute-start(bf16[64,768]{1,0:T(8,128)(2,1)S(1)} %fusion.3), channel_id=1, source_target_pairs={{0,8},{4,12},{8,0},{12,4},{16,24},{20,28},{24,16},{28,20},{1,9},{5... | collective-permute-start | bytes 294920 | tf_op jit(solution)/shard_map/ppermute | solution.py:431
  72.5 0.0 collective-permute-done.18
  72.6 0.7 collective-permute-start.20
  73.3 2.6 %collective-permute-start.22 = (bf16[32,1280]{1,0:T(8,128)(2,1)S(1)}, bf16[32,1280]{1,0:T(8,128)(2,1)S(1)}, u32[]{:S(2)}, u32[]{:S(2)}) collective-permute-start(bf16[32,1280]{1,0:T(8,128)(2,1)S(1)} %collective-permute-done.17), channel_id=1, source_target_pairs={{0,8},{4,12},{8,0},{12,4},{16,24},{20,28},{24,16},{28,20},{1,9},{5... | collective-permute-start | bytes 245768 | tf_op jit(solution)/shard_map/ppermute | solution.py:431
  75.9 3.5 %collective-permute-start.19 = (bf16[64,768]{1,0:T(8,128)(2,1)S(1)}, bf16[64,768]{1,0:T(8,128)(2,1)S(1)}, u32[]{:S(2)}, u32[]{:S(2)}) collective-permute-start(bf16[64,768]{1,0:T(8,128)(2,1)S(1)} %fusion.1), channel_id=1, source_target_pairs={{0,16},{4,20},{8,24},{12,28},{16,0},{20,4},{24,8},{28,12},{1,17},{... | collective-permute-start | bytes 294920 | tf_op jit(solution)/shard_map/ppermute | solution.py:431
  79.4 0.6 collective-permute-done.20
  80.0 0.9 collective-permute-start.21
  80.9 0.1 add_convert_fusion
  81.0 0.7 collective-permute-start.25
  81.7 2.6 %collective-permute-done.21 = bf16[32,1024]{1,0:T(8,128)(2,1)S(1)} collective-permute-done((bf16[32,1024]{1,0:T(8,128)(2,1)S(1)}, bf16[32,1024]{1,0:T(8,128)(2,1)S(1)}, u32[]{:S(2)}, u32[]{:S(2)}) %collective-permute-start.21) | collective-permute-done | bytes 65568 | tf_op jit(solution)/shard_map/ppermute | solution.py:431
  84.3 0.1 add_convert_fusion.1
  84.4 1.0 %collective-permute-start.24 = (bf16[64,1024]{1,0:T(8,128)(2,1)S(1)}, bf16[64,1024]{1,0:T(8,128)(2,1)S(1)}, u32[]{:S(2)}, u32[]{:S(2)}) collective-permute-start(bf16[64,1024]{1,0:T(8,128)(2,1)S(1)} %get-tuple-element.151), channel_id=1, source_target_pairs={{0,4},{4,0},{8,12},{12,8},{16,20},{20,16},{24,28},{28,24},{1,5},{5... | collective-permute-start | bytes 393224 | tf_op jit(solution)/shard_map/ppermute | solution.py:366
  85.4 0.1 add_convert_fusion.2
  85.4 1.1 %collective-permute-start.23 = (bf16[64,768]{1,0:T(8,128)(2,1)S(1)}, bf16[64,768]{1,0:T(8,128)(2,1)S(1)}, u32[]{:S(2)}, u32[]{:S(2)}) collective-permute-start(bf16[64,768]{1,0:T(8,128)(2,1)S(1)} %get-tuple-element.149), channel_id=1, source_target_pairs={{0,4},{4,0},{8,12},{12,8},{16,20},{20,16},{24,28},{28,24},{1,5},{5... | collective-permute-start | bytes 294920 | tf_op jit(solution)/shard_map/ppermute | solution.py:366
  86.6 3.9 %collective-permute-done.23.back = bf16[64,768]{1,0:T(8,128)(2,1)S(1)} collective-permute-done((bf16[64,768]{1,0:T(8,128)(2,1)S(1)}, bf16[64,768]{1,0:T(8,128)(2,1)S(1)}, u32[]{:S(2)}, u32[]{:S(2)}) %collective-permute-start.23) | collective-permute-done | bytes 98336 | tf_op jit(solution)/shard_map/ppermute | solution.py:366
  90.5 1.0 %finish.3.refs_0_ = f32[1,128,3072]{2,1,0:T(8,128)} custom-call(s32[1]{0:T(128)} %bitcast.parity, f32[128,3072]{1,0:T(8,128)S(1)} %copy-done.1, f32[64,1280]{1,0:T(8,128)S(1)} %get-tuple-element.154.earlier, f32[64,1280]{1,0:T(8,128)S(1)} %get-tuple-element.123.kept, bf16[64,1280]{1,0:T(8,128)(2,1)S(1)} %collective-permute-done.10.fetched, ...), custom_call_target="tpu_custom_call" | custom-call | tf_op jit(solution)/shard_map/finish/pallas_call | solution.py:321
  91.4 0.9 finish.4.refs_0_
  92.3 0.8 finish.5
  (36 shorter events, 0.3 us)
Async XLA Ops:
  0.0 7.5 %copy-start.4 = (f32[128]{0:T(128)S(1)}, f32[128]{0:T(128)}, u32[]{:S(2)}) copy-start(f32[128]{0:T(128)} %param.16) | copy-start | bytes 1540
  0.0 7.5 %copy-start.5 = (f32[128]{0:T(128)S(1)}, f32[128]{0:T(128)}, u32[]{:S(2)}) copy-start(f32[128]{0:T(128)} %param.17) | copy-start | bytes 1540
  4.4 3.1 %collective-permute-start.1 = (bf16[128,3072]{1,0:T(8,128)(2,1)}, bf16[128,3072]{1,0:T(8,128)(2,1)S(1)}, u32[]{:S(2)}, u32[]{:S(2)}) collective-permute-start(bf16[128,3072]{1,0:T(8,128)(2,1)} %get-tuple-element.77.m0), channel_id=1, source_target_pairs={{0,1},{1,0},{2,3},{3,2},{4,5},{5,4},{6,7},{7,6},{8,9},{9,8},{10,11... | collective-permute-start | bytes 2359304 | tf_op jit(solution)/shard_map/ppermute | solution.py:360
  4.9 20.9 %collective-permute-start = (bf16[128,3072]{1,0:T(8,128)(2,1)}, bf16[128,3072]{1,0:T(8,128)(2,1)S(1)}, u32[]{:S(2)}, u32[]{:S(2)}) collective-permute-start(bf16[128,3072]{1,0:T(8,128)(2,1)} %get-tuple-element.77.m0), channel_id=1, source_target_pairs={{0,2},{1,3},{2,0},{3,1},{4,6},{5,7},{6,4},{7,5},{8,10},{9,11},{10,... | collective-permute-start | bytes 2359304 | tf_op jit(solution)/shard_map/ppermute | solution.py:363
  7.5 1.2 %copy-start.2 = (bf16[128,3072]{1,0:T(8,128)(2,1)S(1)}, bf16[128,3072]{1,0:T(8,128)(2,1)}, u32[]{:S(2)}) copy-start(bf16[128,3072]{1,0:T(8,128)(2,1)} %get-tuple-element.77.m0) | copy-start | bytes 2359300
  25.9 2.3 %collective-permute-start.2 = (bf16[128,3072]{1,0:T(8,128)(2,1)S(1)}, bf16[128,3072]{1,0:T(8,128)(2,1)S(1)}, u32[]{:S(2)}, u32[]{:S(2)}) collective-permute-start(bf16[128,3072]{1,0:T(8,128)(2,1)S(1)} %collective-permute-done.m0), channel_id=1, source_target_pairs={{0,1},{1,0},{2,3},{3,2},{4,5},{5,4},{6,7},{7,6},{8,9},{9,8},{10,11... | collective-permute-start | bytes 2359304 | tf_op jit(solution)/shard_map/ppermute | solution.py:360
  28.1 7.1 %slice-start = ((s8[9437184]{0:T(1024)(128)(4,1)}), s8[4194304]{0:T(1024)(128)(4,1)S(1)}, s32[]{:S(2)}) async-start(s8[9437184]{0:T(1024)(128)(4,1)} %bitcast.3), calls=%async_computation | async-start | bytes 8388608
  28.1 7.1 %slice-start.1 = ((s8[9437184]{0:T(1024)(128)(4,1)}), s8[4194304]{0:T(1024)(128)(4,1)S(1)}, s32[]{:S(2)}) async-start(s8[9437184]{0:T(1024)(128)(4,1)} %bitcast.3), calls=%async_computation.1 | async-start | bytes 8388608
  28.1 7.1 %slice-start.2 = ((s8[9437184]{0:T(1024)(128)(4,1)}), s8[1048576]{0:T(1024)(128)(4,1)S(1)}, s32[]{:S(2)}) async-start(s8[9437184]{0:T(1024)(128)(4,1)} %bitcast.3), calls=%async_computation.2 | async-start | bytes 2097152
  28.1 7.2 %copy-start = (bf16[512,3072]{1,0:T(8,128)(2,1)S(1)}, bf16[512,3072]{1,0:T(8,128)(2,1)}, u32[]{:S(2)}) copy-start(bf16[512,3072]{1,0:T(8,128)(2,1)} %refs_17_.1) | copy-start | bytes 9437188
  36.9 1.9 %collective-permute-start.3 = (bf16[128,1280]{1,0:T(8,128)(2,1)S(1)}, bf16[128,1280]{1,0:T(8,128)(2,1)S(1)}, u32[]{:S(2)}, u32[]{:S(2)}) collective-permute-start(bf16[128,1280]{1,0:T(8,128)(2,1)S(1)} %get-tuple-element.95), channel_id=1, source_target_pairs={{0,1},{1,0},{2,3},{3,2},{4,5},{5,4},{6,7},{7,6},{8,9},{9,8},{10,11... | collective-permute-start | bytes 983048 | tf_op jit(solution)/shard_map/ppermute | solution.py:360
  38.8 13.1 %copy-start.3 = (f32[1,3072]{1,0:T(1,128)S(1)}, f32[1,3072]{1,0:T(1,128)}, u32[]{:S(2)}) copy-start(f32[1,3072]{1,0:T(1,128)} %get-tuple-element.117.sg) | copy-start | bytes 36868
  38.8 10.1 %collective-permute-start.4 = (bf16[128,1280]{1,0:T(8,128)(2,1)S(1)}, bf16[128,1280]{1,0:T(8,128)(2,1)S(1)}, u32[]{:S(2)}, u32[]{:S(2)}) collective-permute-start(bf16[128,1280]{1,0:T(8,128)(2,1)S(1)} %join.3), channel_id=1, source_target_pairs={{0,2},{1,3},{2,0},{3,1},{4,6},{5,7},{6,4},{7,5},{8,10},{9,11},{10,... | collective-permute-start | bytes 983048 | tf_op jit(solution)/shard_map/ppermute | solution.py:363
  44.2 5.5 %copy-start.6 = (bf16[128,768]{1,0:T(8,128)(2,1)}, bf16[128,768]{1,0:T(8,128)(2,1)S(1)}, u32[]{:S(2)}) copy-start(bf16[128,768]{1,0:T(8,128)(2,1)S(1)} %get-tuple-element.116) | copy-start | bytes 589828
  44.2 1.5 %collective-permute-start.5 = (bf16[128,1024]{1,0:T(8,128)(2,1)S(1)}, bf16[128,1024]{1,0:T(8,128)(2,1)S(1)}, u32[]{:S(2)}, u32[]{:S(2)}) collective-permute-start(bf16[128,1024]{1,0:T(8,128)(2,1)S(1)} %get-tuple-element.109), channel_id=1, source_target_pairs={{0,1},{1,0},{2,3},{3,2},{4,5},{5,4},{6,7},{7,6},{8,9},{9,8},{10,11... | collective-permute-start | bytes 786440 | tf_op jit(solution)/shard_map/ppermute | solution.py:360
  44.3 7.7 %collective-permute-start.9 = (bf16[128,1280]{1,0:T(8,128)(2,1)S(1)}, bf16[128,1280]{1,0:T(8,128)(2,1)S(1)}, u32[]{:S(2)}, u32[]{:S(2)}) collective-permute-start(bf16[128,1280]{1,0:T(8,128)(2,1)S(1)} %get-tuple-element.121), channel_id=1, source_target_pairs={{0,1},{1,0},{2,3},{3,2},{4,5},{5,4},{6,7},{7,6},{8,9},{9,8},{10,11... | collective-permute-start | bytes 983048 | tf_op jit(solution)/shard_map/ppermute | solution.py:360
  49.7 8.0 %collective-permute-start.12 = (bf16[128,1024]{1,0:T(8,128)(2,1)}, bf16[128,1024]{1,0:T(8,128)(2,1)S(1)}, u32[]{:S(2)}, u32[]{:S(2)}) collective-permute-start(bf16[128,1024]{1,0:T(8,128)(2,1)} %join.4), channel_id=1, source_target_pairs={{0,2},{1,3},{2,0},{3,1},{4,6},{5,7},{6,4},{7,5},{8,10},{9,11},{10,... | collective-permute-start | bytes 786440 | tf_op jit(solution)/shard_map/ppermute | solution.py:363
  51.4 6.3 %collective-permute-start.11 = (bf16[128,1024]{1,0:T(8,128)(2,1)}, bf16[128,1024]{1,0:T(8,128)(2,1)}, u32[]{:S(2)}, u32[]{:S(2)}) collective-permute-start(bf16[128,1024]{1,0:T(8,128)(2,1)} %get-tuple-element.126), channel_id=1, source_target_pairs={{0,1},{1,0},{2,3},{3,2},{4,5},{5,4},{6,7},{7,6},{8,9},{9,8},{10,11... | collective-permute-start | bytes 786440 | tf_op jit(solution)/shard_map/ppermute | solution.py:360
  51.4 2.7 %collective-permute-start.7 = (bf16[128,768]{1,0:T(8,128)(2,1)}, bf16[128,768]{1,0:T(8,128)(2,1)}, u32[]{:S(2)}, u32[]{:S(2)}) collective-permute-start(bf16[128,768]{1,0:T(8,128)(2,1)} %get-tuple-element.119), channel_id=1, source_target_pairs={{0,1},{1,0},{2,3},{3,2},{4,5},{5,4},{6,7},{7,6},{8,9},{9,8},{10,11... | collective-permute-start | bytes 589832 | tf_op jit(solution)/shard_map/ppermute | solution.py:360
  52.7 8.4 %collective-permute-start.10 = (bf16[64,1280]{1,0:T(8,128)(2,1)}, bf16[64,1280]{1,0:T(8,128)(2,1)S(1)}, u32[]{:S(2)}, u32[]{:S(2)}) collective-permute-start(bf16[64,1280]{1,0:T(8,128)(2,1)} %get-tuple-element.124), channel_id=1, source_target_pairs={{0,4},{4,0},{8,12},{12,8},{16,20},{20,16},{24,28},{28,24},{1,5},{5... | collective-permute-start | bytes 491528 | tf_op jit(solution)/shard_map/ppermute | solution.py:366
  54.2 8.6 %collective-permute-start.6 = (bf16[128,768]{1,0:T(8,128)(2,1)}, bf16[128,768]{1,0:T(8,128)(2,1)S(1)}, u32[]{:S(2)}, u32[]{:S(2)}) collective-permute-start(bf16[128,768]{1,0:T(8,128)(2,1)} %copy-done.6), channel_id=1, source_target_pairs={{0,1},{1,0},{2,3},{3,2},{4,5},{5,4},{6,7},{7,6},{8,9},{9,8},{10,11... | collective-permute-start | bytes 589832 | tf_op jit(solution)/shard_map/ppermute | solution.py:360
  55.1 7.7 %collective-permute-start.8 = (bf16[128,768]{1,0:T(8,128)(2,1)S(1)}, bf16[128,768]{1,0:T(8,128)(2,1)S(1)}, u32[]{:S(2)}, u32[]{:S(2)}) collective-permute-start(bf16[128,768]{1,0:T(8,128)(2,1)S(1)} %join.5), channel_id=1, source_target_pairs={{0,2},{1,3},{2,0},{3,1},{4,6},{5,7},{6,4},{7,5},{8,10},{9,11},{10,... | collective-permute-start | bytes 589832 | tf_op jit(solution)/shard_map/ppermute | solution.py:363
  58.7 5.3 %collective-permute-start.15 = (bf16[64,1024]{1,0:T(8,128)(2,1)S(1)}, bf16[64,1024]{1,0:T(8,128)(2,1)S(1)}, u32[]{:S(2)}, u32[]{:S(2)}) collective-permute-start(bf16[64,1024]{1,0:T(8,128)(2,1)S(1)} %get-tuple-element.129), channel_id=1, source_target_pairs={{0,4},{4,0},{8,12},{12,8},{16,20},{20,16},{24,28},{28,24},{1,5},{5... | collective-permute-start | bytes 393224 | tf_op jit(solution)/shard_map/ppermute | solution.py:366
  61.1 6.1 %collective-permute-start.14 = (bf16[64,1280]{1,0:T(8,128)(2,1)S(1)}, bf16[64,1280]{1,0:T(8,128)(2,1)S(1)}, u32[]{:S(2)}, u32[]{:S(2)}) collective-permute-start(bf16[64,1280]{1,0:T(8,128)(2,1)S(1)} %get-tuple-element.157), channel_id=1, source_target_pairs={{0,8},{4,12},{8,0},{12,4},{16,24},{20,28},{24,16},{28,20},{1,9},{5... | collective-permute-start | bytes 491528 | tf_op jit(solution)/shard_map/ppermute | solution.py:431
  62.9 27.6 %copy-start.1 = (f32[128,3072]{1,0:T(8,128)S(1)}, f32[128,3072]{1,0:T(8,128)}, u32[]{:S(2)}) copy-start(f32[128,3072]{1,0:T(8,128)} %x_start.5) | copy-start | bytes 4718596
  62.9 7.1 %collective-permute-start.13 = (bf16[64,768]{1,0:T(8,128)(2,1)S(1)}, bf16[64,768]{1,0:T(8,128)(2,1)S(1)}, u32[]{:S(2)}, u32[]{:S(2)}) collective-permute-start(bf16[64,768]{1,0:T(8,128)(2,1)S(1)} %get-tuple-element.133), channel_id=1, source_target_pairs={{0,4},{4,0},{8,12},{12,8},{16,20},{20,16},{24,28},{28,24},{1,5},{5... | collective-permute-start | bytes 294920 | tf_op jit(solution)/shard_map/ppermute | solution.py:366
  64.1 8.4 %collective-permute-start.18 = (bf16[64,1024]{1,0:T(8,128)(2,1)S(1)}, bf16[64,1024]{1,0:T(8,128)(2,1)S(1)}, u32[]{:S(2)}, u32[]{:S(2)}) collective-permute-start(bf16[64,1024]{1,0:T(8,128)(2,1)S(1)} %get-tuple-element.155), channel_id=1, source_target_pairs={{0,8},{4,12},{8,0},{12,4},{16,24},{20,28},{24,16},{28,20},{1,9},{5... | collective-permute-start | bytes 393224 | tf_op jit(solution)/shard_map/ppermute | solution.py:431
  67.3 6.0 %collective-permute-start.17 = (bf16[32,1280]{1,0:T(8,128)(2,1)S(1)}, bf16[32,1280]{1,0:T(8,128)(2,1)S(1)}, u32[]{:S(2)}, u32[]{:S(2)}) collective-permute-start(bf16[32,1280]{1,0:T(8,128)(2,1)S(1)} %fusion.2), channel_id=1, source_target_pairs={{0,16},{4,20},{8,24},{12,28},{16,0},{20,4},{24,8},{28,12},{1,17},{... | collective-permute-start | bytes 245768 | tf_op jit(solution)/shard_map/ppermute | solution.py:431
  70.0 5.9 %collective-permute-start.16 = (bf16[64,768]{1,0:T(8,128)(2,1)S(1)}, bf16[64,768]{1,0:T(8,128)(2,1)S(1)}, u32[]{:S(2)}, u32[]{:S(2)}) collective-permute-start(bf16[64,768]{1,0:T(8,128)(2,1)S(1)} %fusion.3), channel_id=1, source_target_pairs={{0,8},{4,12},{8,0},{12,4},{16,24},{20,28},{24,16},{28,20},{1,9},{5... | collective-permute-start | bytes 294920 | tf_op jit(solution)/shard_map/ppermute | solution.py:431
  72.6 7.5 %collective-permute-start.20 = (bf16[32,1024]{1,0:T(8,128)(2,1)S(1)}, bf16[32,1024]{1,0:T(8,128)(2,1)S(1)}, u32[]{:S(2)}, u32[]{:S(2)}) collective-permute-start(bf16[32,1024]{1,0:T(8,128)(2,1)S(1)} %fusion.4), channel_id=1, source_target_pairs={{0,16},{4,20},{8,24},{12,28},{16,0},{20,4},{24,8},{28,12},{1,17},{... | collective-permute-start | bytes 196616 | tf_op jit(solution)/shard_map/ppermute | solution.py:431
  73.3 7.6 %collective-permute-start.22 = (bf16[32,1280]{1,0:T(8,128)(2,1)S(1)}, bf16[32,1280]{1,0:T(8,128)(2,1)S(1)}, u32[]{:S(2)}, u32[]{:S(2)}) collective-permute-start(bf16[32,1280]{1,0:T(8,128)(2,1)S(1)} %collective-permute-done.17), channel_id=1, source_target_pairs={{0,8},{4,12},{8,0},{12,4},{16,24},{20,28},{24,16},{28,20},{1,9},{5... | collective-permute-start | bytes 245768 | tf_op jit(solution)/shard_map/ppermute | solution.py:431
  75.9 9.5 %collective-permute-start.19 = (bf16[64,768]{1,0:T(8,128)(2,1)S(1)}, bf16[64,768]{1,0:T(8,128)(2,1)S(1)}, u32[]{:S(2)}, u32[]{:S(2)}) collective-permute-start(bf16[64,768]{1,0:T(8,128)(2,1)S(1)} %fusion.1), channel_id=1, source_target_pairs={{0,16},{4,20},{8,24},{12,28},{16,0},{20,4},{24,8},{28,12},{1,17},{... | collective-permute-start | bytes 294920 | tf_op jit(solution)/shard_map/ppermute | solution.py:431
  80.0 4.3 %collective-permute-start.21 = (bf16[32,1024]{1,0:T(8,128)(2,1)S(1)}, bf16[32,1024]{1,0:T(8,128)(2,1)S(1)}, u32[]{:S(2)}, u32[]{:S(2)}) collective-permute-start(bf16[32,1024]{1,0:T(8,128)(2,1)S(1)} %collective-permute-done.20), channel_id=1, source_target_pairs={{0,8},{4,12},{8,0},{12,4},{16,24},{20,28},{24,16},{28,20},{1,9},{5... | collective-permute-start | bytes 196616 | tf_op jit(solution)/shard_map/ppermute | solution.py:431
  81.0 9.5 %collective-permute-start.25 = (bf16[64,1280]{1,0:T(8,128)(2,1)S(1)}, bf16[64,1280]{1,0:T(8,128)(2,1)S(1)}, u32[]{:S(2)}, u32[]{:S(2)}) collective-permute-start(bf16[64,1280]{1,0:T(8,128)(2,1)S(1)} %get-tuple-element.153), channel_id=1, source_target_pairs={{0,4},{4,0},{8,12},{12,8},{16,20},{20,16},{24,28},{28,24},{1,5},{5... | collective-permute-start | bytes 491528 | tf_op jit(solution)/shard_map/ppermute | solution.py:366
  84.4 7.1 %collective-permute-start.24 = (bf16[64,1024]{1,0:T(8,128)(2,1)S(1)}, bf16[64,1024]{1,0:T(8,128)(2,1)S(1)}, u32[]{:S(2)}, u32[]{:S(2)}) collective-permute-start(bf16[64,1024]{1,0:T(8,128)(2,1)S(1)} %get-tuple-element.151), channel_id=1, source_target_pairs={{0,4},{4,0},{8,12},{12,8},{16,20},{20,16},{24,28},{28,24},{1,5},{5... | collective-permute-start | bytes 393224 | tf_op jit(solution)/shard_map/ppermute | solution.py:366
  85.4 5.0 %collective-permute-start.23 = (bf16[64,768]{1,0:T(8,128)(2,1)S(1)}, bf16[64,768]{1,0:T(8,128)(2,1)S(1)}, u32[]{:S(2)}, u32[]{:S(2)}) collective-permute-start(bf16[64,768]{1,0:T(8,128)(2,1)S(1)} %get-tuple-element.149), channel_id=1, source_target_pairs={{0,4},{4,0},{8,12},{12,8},{16,20},{20,16},{24,28},{28,24},{1,5},{5... | collective-permute-start | bytes 294920 | tf_op jit(solution)/shard_map/ppermute | solution.py:366

commit v8 on v7

--- a/solution.py
+++ b/solution.py
@@ -417,15 +417,15 @@
     keep = [part[0] for part in parts[-chunks:]]
     sent0 = sent[-chunks:]
     others = chips - 1
-    first, keep, sent[:others] = tied([row[0] for row in got], keep, sent[:others])
+    later = []
+    for c in range(1, chunks):
+        here = slice((c - 1) * others, c * others)
+        later.append(joined(parts[here], sent[here]))
+    first, keep, later = tied([row[0] for row in got], keep, later)
     for row, one in zip(got, first):
         row[0] = one
-    ready = joined(parts[:others], sent[:others])
-    keep, ready = tied(keep, ready)
-    to_chips(ready)
-    for c in range(2, chunks):
-        here = slice((c - 1) * others, c * others)
-        to_chips(joined(parts[here], sent[here]))
+    for ready in later:
+        to_chips(ready)
 
     def along(pairs):
         return lambda x: lax.ppermute(x, "step", [(2 * a + i, 2 * b + i) for a, b in pairs for i in (0, 1)])
@@ -477,7 +477,7 @@
 
         def finish(fetched):
             given = [held[name] for name in ("earlier", "kept", "fetched", "other")]
-            into = list(written)
+            fetched, into = tied(fetched, list(written))
             written[:] = [finish_call(which, x_start, *given, fetched[0], into, firsts[c])]
 
         stages = [(drift_of, to_pair, "x", 0.5), (pair_sum, swap(1), "z1", 0.5)]
@@ -493,10 +493,10 @@
         stages.append((finish, None, "", 0.0))
         return stages
 
-    plan = [prefix_stages(c, c < chunks - 1) for c in range(chunks)]
+    plan = [prefix_stages(c, c == 0) for c in range(chunks)]
     inbox = [[got[j][c] for j in range(chips - 1)] for c in range(chunks)]
     shares = [18.5 * n / width for n in counts]
-    ends = [2.0 + sum(shares[: c + 1]) for c in range(chunks)]
+    ends = [2.0 * c + sum(shares[: c + 1]) for c in range(chunks)]
     waits = [(end, c, 0) for c, end in enumerate(ends)]
     free = {"x": 0.0, "z1": 0.0, "z2": 0.0, "": 0.0}
     turns = []
@@ -506,7 +506,7 @@
         turns.append((c, i))
         if i + 1 < len(plan[c]):
             link, load = plan[c][i][2:]
-            begin = max(when + 2.0, free[link])
+            begin = max(when + 1.5, free[link])
             free[link] = begin + load * shares[c]
             waits.append((free[link] + 0.7, c, i + 1))
     written = []

time: 93.6 us -> 100 us (1.068)
  starting transfers between devices: 32.2 us -> 26.1 us
  other arithmetic: 0.46 us -> 6.29 us
  local copies, waits for them, and re-layouts: 1.18 us -> 6.61 us
  waiting for transfers between devices: 22.2 us -> 23.3 us
    unnamed x20 -> x40, local copies, waits for them, and re-layouts: 1.18 us -> 6.61 us
    ppermute x4, waiting for transfers between devices: 9.97 us -> 5.91 us  [to_chip(): lax.ppermute(x, 'seq', [(i, (i + 2 * offset) % n_seq) for i in range(n_se...]
    ppermute x8 -> x7, starting transfers between devices: 16.1 us -> 12.1 us  [along(): lax.ppermute(x, 'step', [(2 * a + i, 2 * b + i) for a, b in pairs for i i...]
    ppermute x6, waiting for transfers between devices: 4.16 us -> 6.87 us  [to_pair(): return lax.ppermute(x, 'step', [(i, i ^ 1) for i in range(n_step)])]
    convert_element_type x3, other arithmetic: 0.1 us -> 2.69 us  [collect(): total = held['total'].astype(bf16)]
    convert_element_type x3, other arithmetic: 0.23 us -> 2.11 us  [collect(): return (held['earlier'] + even * held['kept']).astype(bf16)]
    ppermute x8 -> x7, waiting for transfers between devices: 4.75 us -> 6.4 us  [along(): lax.ppermute(x, 'step', [(2 * a + i, 2 * b + i) for a, b in pairs for i i...]
    convert_element_type x3, other arithmetic: 0.08 us -> 1.46 us  [pair_sum(): return held['total'].astype(bf16)]
  transfers between devices with their start and end apart: 26 -> 25, of which waited for: 10 -> 12; matrix products, arithmetic and copies ran while one was open for 0% -> 6% of each run, Pallas kernels for 24% -> 22%
where the time goes in v8:
time: 100 us; the launch traced here: 99.7 us
  Pallas kernels  36.2 us (36%)
  starting transfers between devices  26.1 us (26%)
  waiting for transfers between devices  23.3 us (23%)
  local copies, waits for them, and re-layouts  6.61 us (7%)
  other arithmetic  6.29 us (6%)
  between operations  1.15 us (1%)
    pallas_call x2, Pallas kernels, project_call(): pl.pallas_call(functools.partial(project_kernel, tile, load, tiles), in_s...  17.6 us
    ppermute x7, starting transfers between devices, along(): lax.ppermute(x, 'step', [(2 * a + i, 2 * b + i) for a, b in pairs for i i...  12.1 us
    ppermute x6, starting transfers between devices, to_pair(): return lax.ppermute(x, 'step', [(i, i ^ 1) for i in range(n_step)])  7.2 us
    ppermute x6, waiting for transfers between devices, to_pair(): return lax.ppermute(x, 'step', [(i, i ^ 1) for i in range(n_step)])  6.87 us
    unnamed x40, local copies, waits for them, and re-layouts  6.61 us
    ppermute x7, waiting for transfers between devices, along(): lax.ppermute(x, 'step', [(2 * a + i, 2 * b + i) for a, b in pairs for i i...  6.4 us
    ppermute x4, waiting for transfers between devices, to_chip(): lax.ppermute(x, 'seq', [(i, (i + 2 * offset) % n_seq) for i in range(n_se...  5.91 us
    ppermute x4, starting transfers between devices, to_chip(): lax.ppermute(x, 'seq', [(i, (i + 2 * offset) % n_seq) for i in range(n_se...  5.42 us
  transfers between devices with their start and end apart: 25, of which 12 were waited for; matrix products, arithmetic and copies ran while one was open for 6% of the time, Pallas kernels for 22%

profile of v8, /device:TPU:0, one launch (start us, length us, event | category | flops | bytes accessed | tf_op | source)
XLA Modules:
  0.0 99.7 jit_solution(14255773756494190145)
XLA Ops:
  0.7 3.7 %norm.1 = (bf16[128,3072]{1,0:T(8,128)(2,1)}, f32[1,3072]{1,0:T(1,128)}) custom-call(s32[1]{0:T(128)S(6)} %copy.16.t_ref, f32[50]{0:T(128)} %size_ref.1, f32[1,128,3072]{2,1,0:T(8,128)} %x_hbm.1, f32[50,9216]{1,0:T(8,128)} %mod_hbm.1), custom_call_target="tpu_custom_call" | custom-call | flops 3932160 | tf_op jit(solution)/shard_map/norm/pallas_call | solution.py:56
  4.4 0.5 collective-permute-start.1
  4.9 2.6 %collective-permute-start = (bf16[128,3072]{1,0:T(8,128)(2,1)}, bf16[128,3072]{1,0:T(8,128)(2,1)S(1)}, u32[]{:S(2)}, u32[]{:S(2)}) collective-permute-start(bf16[128,3072]{1,0:T(8,128)(2,1)} %get-tuple-element.77.m0), channel_id=1, source_target_pairs={{0,2},{1,3},{2,0},{3,1},{4,6},{5,7},{6,4},{7,5},{8,10},{9,11},{10,... | collective-permute-start | bytes 2359304 | tf_op jit(solution)/shard_map/ppermute | solution.py:363
  7.5 1.1 %copy-done.2 = bf16[128,3072]{1,0:T(8,128)(2,1)S(1)} copy-done((bf16[128,3072]{1,0:T(8,128)(2,1)S(1)}, bf16[128,3072]{1,0:T(8,128)(2,1)}, u32[]{:S(2)}) %copy-start.2) | copy-done | bytes 786456
  8.7 12.4 %project.2 = (bf16[256,512]{1,0:T(8,128)(2,1)S(1)}, bf16[256,512]{1,0:T(8,128)(2,1)S(1)}, bf16[256,512]{1,0:T(8,128)(2,1)S(1)}, bf16[256,1536]{1,0:T(8,128)(2,1)...) custom-call(bf16[128,3072]{1,0:T(8,128)(2,1)S(1)} %copy-done.2, ...), custom_call_target="tpu_custom_call" | custom-call | flops 4831838208 | tf_op jit(solution)/shard_map/project/pallas_call | solution.py:151
  21.1 4.8 %collective-permute-done.m0 = bf16[128,3072]{1,0:T(8,128)(2,1)S(1)} collective-permute-done((bf16[128,3072]{1,0:T(8,128)(2,1)}, bf16[128,3072]{1,0:T(8,128)(2,1)S(1)}, u32[]{:S(2)}, u32[]{:S(2)}) %collective-permute-start) | collective-permute-done | bytes 786464 | tf_op jit(solution)/shard_map/ppermute | solution.py:363
  25.9 2.3 %collective-permute-done.2.m1 = bf16[128,3072]{1,0:T(8,128)(2,1)S(1)} collective-permute-done((bf16[128,3072]{1,0:T(8,128)(2,1)S(1)}, bf16[128,3072]{1,0:T(8,128)(2,1)S(1)}, u32[]{:S(2)}, u32[]{:S(2)}) %collective-permute-start.2) | collective-permute-done | bytes 786464 | tf_op jit(solution)/shard_map/ppermute | solution.py:360
  28.2 5.2 %project.3 = (bf16[256,512]{1,0:T(8,128)(2,1)S(1)}, bf16[256,512]{1,0:T(8,128)(2,1)S(1)}, bf16[256,512]{1,0:T(8,128)(2,1)S(1)}, bf16[256,1536]{1,0:T(8,128)(2,1)S(1)}) custom-call(bf16[128,3072]{1,0:T(8,128)(2,1)S(1)} %collective-permute-done.m0, bf16[128,3072]{1,0:T(8,128)(2,1)S(1)} %collective-permute-done.2.m1, f32[1,128]{1,0:T(1,128)S(1)} %bitcast.6, ...), custom_call_target="tpu_custom_call" | custom-call | flops 4831838208 | tf_op jit(solution)/shard_map/project/pallas_call | solution.py:151
  33.4 1.9 %attend.2.refs_0_.refs_4_ = bf16[256,512]{1,0:T(8,128)(2,1)S(1)} custom-call(bf16[256,512]{1,0:T(8,128)(2,1)S(1)} %get-tuple-element.87.refs_0_, bf16[256,512]{1,0:T(8,128)(2,1)S(1)} %get-tuple-element.88.refs_1_, bf16[256,512]{1,0:T(8,128)(2,1)S(1)} %get-tuple-element.89.refs_2_, bf16[256,512]{1,0:T(8,128)(2,1)S(1)} %get-tuple-element.90.refs_3_, ...), custom_call_target="tpu_custom_call" | custom-call | flops 805306368 | tf_op jit(solution)/shard_map/attend/pallas_call | solution.py:191
  35.3 1.5 %project_out.2 = (f32[128,1280]{1,0:T(8,128)S(1)}, bf16[128,1280]{1,0:T(8,128)(2,1)S(1)}) custom-call(bf16[256,512]{1,0:T(8,128)(2,1)S(1)} %attend.2.refs_0_.refs_4_, bf16[256,1536]{1,0:T(8,128)(2,1)S(1)} %get-tuple-element.102.refs_1_.refs_5_, bf16[512,3072]{1,0:T(8,128)(2,1)S(1)} %copy-done, bf16[1536,3072]{1,0:T(8,128)(2,1)S(1)} %bitcast.4), custom_call_target="tpu_custom_call" | custom-call | flops 1342177280 | tf_op jit(solution)/shard_map/project_out/pallas_call | solution.py:235
  36.9 0.2 collective-permute-start.3
  37.1 1.7 %attend.3.refs_8_.refs_12_.refs_16_ = bf16[256,512]{1,0:T(8,128)(2,1)S(1)} custom-call(bf16[256,512]{1,0:T(8,128)(2,1)S(1)} %get-tuple-element.96.refs_0_, bf16[256,512]{1,0:T(8,128)(2,1)S(1)} %get-tuple-element.88.refs_1_, bf16[256,512]{1,0:T(8,128)(2,1)S(1)} %get-tuple-element.89.refs_2_, bf16[256,512]{1,0:T(8,128)(2,1)S(1)} %get-tuple-element.90.refs_3_, ...), custom_call_target="tpu_custom_call" | custom-call | flops 805306368 | tf_op jit(solution)/shard_map/attend/pallas_call | solution.py:191
  38.8 0.1 join.3
  38.8 1.8 %collective-permute-start.4 = (bf16[128,1280]{1,0:T(8,128)(2,1)S(1)}, bf16[128,1280]{1,0:T(8,128)(2,1)S(1)}, u32[]{:S(2)}, u32[]{:S(2)}) collective-permute-start(bf16[128,1280]{1,0:T(8,128)(2,1)S(1)} %join.3), channel_id=1, source_target_pairs={{0,2},{1,3},{2,0},{3,1},{4,6},{5,7},{6,4},{7,5},{8,10},{9,11},{10,... | collective-permute-start | bytes 983048 | tf_op jit(solution)/shard_map/ppermute | solution.py:363
  40.7 3.5 %project_out.3 = (f32[128,1024]{1,0:T(8,128)S(1)}, bf16[128,1024]{1,0:T(8,128)(2,1)}, f32[128,768]{1,0:T(8,128)S(1)}, bf16[128,768]{1,0:T(8,128)(2,1)}, f32[128,...) custom-call(bf16[256,512]{1,0:T(8,128)(2,1)S(1)} %attend.2.refs_0_.r, ...), custom_call_target="tpu_custom_call" | custom-call | flops 2684354560 | tf_op jit(solution)/shard_map/project_out/pallas_call | solution.py:235
  44.2 0.7 copy-done.15
  44.8 0.1 collective-permute-start.11
  45.0 0.4 collective-permute-start.5
  45.3 0.1 collective-permute-start.6
  45.5 1.8 %collective-permute-done.6.sent = bf16[128,768]{1,0:T(8,128)(2,1)S(1)} collective-permute-done((bf16[128,768]{1,0:T(8,128)(2,1)}, bf16[128,768]{1,0:T(8,128)(2,1)S(1)}, u32[]{:S(2)}, u32[]{:S(2)}) %collective-permute-start.6) | collective-permute-done | bytes 196640 | tf_op jit(solution)/shard_map/ppermute | solution.py:360
  47.3 0.7 copy-done.10
  48.0 0.9 copy-done.11
  49.0 1.1 %join.4 = bf16[128,1024]{1,0:T(8,128)(2,1)S(1)} custom-call(f32[128,1024]{1,0:T(8,128)S(1)} %get-tuple-element.109.keep, bf16[128,1024]{1,0:T(8,128)(2,1)} %collective-permute-done.5.sent), custom_call_target="tpu_custom_call" | custom-call | tf_op jit(solution)/shard_map/join/pallas_call | solution.py:253
  50.1 0.7 copy-done.5
  50.9 1.0 copy-done.6
  51.8 1.1 %drift.3 = (f32[64,1280]{1,0:T(8,128)S(1)}, f32[64,1280]{1,0:T(8,128)S(1)}, bf16[64,1280]{1,0:T(8,128)(2,1)S(1)}) custom-call(s32[1]{0:T(128)} %bitcast.parity, f32[128,1280]{1,0:T(8,128)S(1)} %get-tuple-element.120.keep, bf16[128,1280]{1,0:T(8,128)(2,1)} %collective-permute-done.11.sent, f32[1,3072]{1,0:T(1,128)S(1)} %copy-done.12, ...), custom_call_target="tpu_custom_call" | custom-call | tf_op jit(solution)/shard_map/drift/pallas_call | solution.py:286
  53.0 0.7 copy-done.3
  53.7 1.5 %collective-permute-start.12 = (bf16[64,1280]{1,0:T(8,128)(2,1)S(1)}, bf16[64,1280]{1,0:T(8,128)(2,1)S(1)}, u32[]{:S(2)}, u32[]{:S(2)}) collective-permute-start(bf16[64,1280]{1,0:T(8,128)(2,1)S(1)} %get-tuple-element.124), channel_id=1, source_target_pairs={{0,4},{4,0},{8,12},{12,8},{16,20},{20,16},{24,28},{28,24},{1,5},{5... | collective-permute-start | bytes 491528 | tf_op jit(solution)/shard_map/ppermute | solution.py:366
  55.2 0.5 collective-permute-start.10
  55.7 4.2 %collective-permute-done.12.fetched = bf16[64,1280]{1,0:T(8,128)(2,1)S(1)} collective-permute-done((bf16[64,1280]{1,0:T(8,128)(2,1)S(1)}, bf16[64,1280]{1,0:T(8,128)(2,1)S(1)}, u32[]{:S(2)}, u32[]{:S(2)}) %collective-permute-start.12) | collective-permute-done | bytes 163872 | tf_op jit(solution)/shard_map/ppermute | solution.py:366
  60.0 0.8 fusion.9
  60.7 1.6 %collective-permute-start.14 = (bf16[64,1280]{1,0:T(8,128)(2,1)S(1)}, bf16[64,1280]{1,0:T(8,128)(2,1)S(1)}, u32[]{:S(2)}, u32[]{:S(2)}) collective-permute-start(bf16[64,1280]{1,0:T(8,128)(2,1)S(1)} %get-tuple-element.155), channel_id=1, source_target_pairs={{0,8},{4,12},{8,0},{12,4},{16,24},{20,28},{24,16},{28,20},{1,9},{5... | collective-permute-start | bytes 491528 | tf_op jit(solution)/shard_map/ppermute | solution.py:431
  62.3 0.5 collective-permute-start.8
  62.8 1.1 %collective-permute-done.10.refs_0_ = bf16[128,1024]{1,0:T(8,128)(2,1)S(1)} collective-permute-done((bf16[128,1024]{1,0:T(8,128)(2,1)S(1)}, bf16[128,1024]{1,0:T(8,128)(2,1)S(1)}, u32[]{:S(2)}, u32[]{:S(2)}) %collective-permute-start.10) | collective-permute-done | bytes 262176 | tf_op jit(solution)/shard_map/ppermute | solution.py:363
  64.0 0.1 drift.4
  64.1 0.7 copy-done.7
  64.8 0.5 collective-permute-start.13
  65.3 0.9 collective-permute-done.14
  66.2 1.7 %fusion.5 = bf16[32,1280]{1,0:T(8,128)(2,1)} fusion(f32[64,1280]{1,0:T(8,128)S(1)} %convert_element_type.70, s32[]{:T(128)S(6)} %select_n.11, f32[64,1280]{1,0:T(8,128)} %get-tuple-element.156), kind=kLoop, calls=%fused_computation.17 | loop fusion | flops 81920 | bytes 409604 | tf_op jit(solution)/shard_map/convert_element_type | solution.py:469
  67.9 2.0 %collective-permute-done.13.fetched = bf16[64,1024]{1,0:T(8,128)(2,1)S(1)} collective-permute-done((bf16[64,1024]{1,0:T(8,128)(2,1)S(1)}, bf16[64,1024]{1,0:T(8,128)(2,1)S(1)}, u32[]{:S(2)}, u32[]{:S(2)}) %collective-permute-start.13) | collective-permute-done | bytes 131104 | tf_op jit(solution)/shard_map/ppermute | solution.py:366
  69.9 0.7 fusion.4
  70.6 1.6 %collective-permute-start.16 = (bf16[64,1024]{1,0:T(8,128)(2,1)}, bf16[64,1024]{1,0:T(8,128)(2,1)}, u32[]{:S(2)}, u32[]{:S(2)}) collective-permute-start(bf16[64,1024]{1,0:T(8,128)(2,1)} %fusion.4), channel_id=1, source_target_pairs={{0,8},{4,12},{8,0},{12,4},{16,24},{20,28},{24,16},{28,20},{1,9},{5... | collective-permute-start | bytes 393224 | tf_op jit(solution)/shard_map/ppermute | solution.py:431
  72.1 2.6 %collective-permute-start.17 = (bf16[32,1280]{1,0:T(8,128)(2,1)}, bf16[32,1280]{1,0:T(8,128)(2,1)}, u32[]{:S(2)}, u32[]{:S(2)}) collective-permute-start(bf16[32,1280]{1,0:T(8,128)(2,1)} %fusion.5), channel_id=1, source_target_pairs={{0,16},{4,20},{8,24},{12,28},{16,0},{20,4},{24,8},{28,12},{1,17},{... | collective-permute-start | bytes 245768 | tf_op jit(solution)/shard_map/ppermute | solution.py:431
  74.8 1.1 %drift.5 = (f32[64,768]{1,0:T(8,128)S(1)}, f32[64,768]{1,0:T(8,128)S(1)}, bf16[64,768]{1,0:T(8,128)(2,1)S(1)}) custom-call(s32[1]{0:T(128)} %bitcast.parity, f32[128,768]{1,0:T(8,128)S(1)} %get-tuple-element.113.keep, bf16[128,768]{1,0:T(8,128)(2,1)} %collective-permute-done.7.sent, f32[1,3072]{1,0:T(1,128)S(1)} %copy-done.12, ...), custom_call_target="tpu_custom_call" | custom-call | tf_op jit(solution)/shard_map/drift/pallas_call | solution.py:286
  75.9 0.6 collective-permute-start.15
  76.5 1.3 %collective-permute-done.17 = bf16[32,1280]{1,0:T(8,128)(2,1)} collective-permute-done((bf16[32,1280]{1,0:T(8,128)(2,1)}, bf16[32,1280]{1,0:T(8,128)(2,1)}, u32[]{:S(2)}, u32[]{:S(2)}) %collective-permute-start.17) | collective-permute-done | bytes 81952 | tf_op jit(solution)/shard_map/ppermute | solution.py:431
  77.8 1.8 %collective-permute-start.19 = (bf16[32,1280]{1,0:T(8,128)(2,1)}, bf16[32,1280]{1,0:T(8,128)(2,1)S(1)}, u32[]{:S(2)}, u32[]{:S(2)}) collective-permute-start(bf16[32,1280]{1,0:T(8,128)(2,1)} %collective-permute-done.17), channel_id=1, source_target_pairs={{0,8},{4,12},{8,0},{12,4},{16,24},{20,28},{24,16},{28,20},{1,9},{5... | collective-permute-start | bytes 245768 | tf_op jit(solution)/shard_map/ppermute | solution.py:431
  79.6 1.0 fusion
  80.5 1.7 %collective-permute-start.22 = (bf16[64,1024]{1,0:T(8,128)(2,1)S(1)}, bf16[64,1024]{1,0:T(8,128)(2,1)S(1)}, u32[]{:S(2)}, u32[]{:S(2)}) collective-permute-start(bf16[64,1024]{1,0:T(8,128)(2,1)S(1)} %fusion), channel_id=1, source_target_pairs={{0,16},{4,20},{8,24},{12,28},{16,0},{20,4},{24,8},{28,12},{1,17},{... | collective-permute-start | bytes 393224 | tf_op jit(solution)/shard_map/ppermute | solution.py:431
  82.2 1.4 %collective-permute-start.18 = (bf16[64,768]{1,0:T(8,128)(2,1)S(1)}, bf16[64,768]{1,0:T(8,128)(2,1)S(1)}, u32[]{:S(2)}, u32[]{:S(2)}) collective-permute-start(bf16[64,768]{1,0:T(8,128)(2,1)S(1)} %fusion.6), channel_id=1, source_target_pairs={{0,8},{4,12},{8,0},{12,4},{16,24},{20,28},{24,16},{28,20},{1,9},{5... | collective-permute-start | bytes 294920 | tf_op jit(solution)/shard_map/ppermute | solution.py:431
  83.6 0.8 collective-permute-done.19
  84.5 1.1 %add_convert_fusion = (bf16[64,1280]{1,0:T(8,128)(2,1)S(1)}, f32[64,1280]{1,0:T(8,128)S(1)}) fusion(f32[64,1280]{1,0:T(8,128)S(1)} %get-tuple-element.123.kept, f32[]{:T(128)S(6)} %convert_element_type.80, bf16[32,1280]{1,0:T(8,128)(2,1)} %collective-permute-done.17, bf16[32,1280]{1,0:T(8,128)(2,1)S(1)} %collective-permute-done.19, pred[]{:T(512)S(6)} %eq.18, ...), kind=kLoop, calls=%fused_computation.2 | loop fusion | flops 1392640 | bytes 1146893 | tf_op jit(solution)/shard_map/convert_element_type | solution.py:467
  85.5 0.1 collective-permute-start.24
  85.6 1.3 %collective-permute-done.18 = bf16[64,768]{1,0:T(8,128)(2,1)S(1)} collective-permute-done((bf16[64,768]{1,0:T(8,128)(2,1)S(1)}, bf16[64,768]{1,0:T(8,128)(2,1)S(1)}, u32[]{:S(2)}, u32[]{:S(2)}) %collective-permute-start.18) | collective-permute-done | bytes 98336 | tf_op jit(solution)/shard_map/ppermute | solution.py:431
  87.0 1.5 %collective-permute-start.20 = (bf16[64,768]{1,0:T(8,128)(2,1)S(1)}, bf16[64,768]{1,0:T(8,128)(2,1)S(1)}, u32[]{:S(2)}, u32[]{:S(2)}) collective-permute-start(bf16[64,768]{1,0:T(8,128)(2,1)S(1)} %fusion.3), channel_id=1, source_target_pairs={{0,16},{4,20},{8,24},{12,28},{16,0},{20,4},{24,8},{28,12},{1,17},{... | collective-permute-start | bytes 294920 | tf_op jit(solution)/shard_map/ppermute | solution.py:431
  88.5 1.0 add_convert_fusion.1
  89.5 2.1 %collective-permute-start.23 = (bf16[64,1024]{1,0:T(8,128)(2,1)S(1)}, bf16[64,1024]{1,0:T(8,128)(2,1)S(1)}, u32[]{:S(2)}, u32[]{:S(2)}) collective-permute-start(bf16[64,1024]{1,0:T(8,128)(2,1)S(1)} %get-tuple-element.149), channel_id=1, source_target_pairs={{0,4},{4,0},{8,12},{12,8},{16,20},{20,16},{24,28},{28,24},{1,5},{5... | collective-permute-start | bytes 393224 | tf_op jit(solution)/shard_map/ppermute | solution.py:366
  91.5 2.1 %collective-permute-done.20 = bf16[64,768]{1,0:T(8,128)(2,1)S(1)} collective-permute-done((bf16[64,768]{1,0:T(8,128)(2,1)S(1)}, bf16[64,768]{1,0:T(8,128)(2,1)S(1)}, u32[]{:S(2)}, u32[]{:S(2)}) %collective-permute-start.20) | collective-permute-done | bytes 98336 | tf_op jit(solution)/shard_map/ppermute | solution.py:431
  93.6 0.1 add_convert_fusion.2
  93.6 2.4 %collective-permute-start.21 = (bf16[64,768]{1,0:T(8,128)(2,1)S(1)}, bf16[64,768]{1,0:T(8,128)(2,1)S(1)}, u32[]{:S(2)}, u32[]{:S(2)}) collective-permute-start(bf16[64,768]{1,0:T(8,128)(2,1)S(1)} %get-tuple-element.151), channel_id=1, source_target_pairs={{0,4},{4,0},{8,12},{12,8},{16,20},{20,16},{24,28},{28,24},{1,5},{5... | collective-permute-start | bytes 294920 | tf_op jit(solution)/shard_map/ppermute | solution.py:366
  96.1 1.0 finish.3.refs_0_
  97.1 0.9 finish.4.refs_0_
  98.0 0.6 collective-permute-done.21.back
  98.7 0.8 finish.5
  (53 shorter events, 0.2 us)
Async XLA Ops:
  0.0 7.5 %copy-start.13 = (f32[128]{0:T(128)S(1)}, f32[128]{0:T(128)}, u32[]{:S(2)}) copy-start(f32[128]{0:T(128)} %param.16) | copy-start | bytes 1540
  0.0 7.5 %copy-start.14 = (f32[128]{0:T(128)S(1)}, f32[128]{0:T(128)}, u32[]{:S(2)}) copy-start(f32[128]{0:T(128)} %param.17) | copy-start | bytes 1540
  4.4 3.1 %collective-permute-start.1 = (bf16[128,3072]{1,0:T(8,128)(2,1)}, bf16[128,3072]{1,0:T(8,128)(2,1)S(1)}, u32[]{:S(2)}, u32[]{:S(2)}) collective-permute-start(bf16[128,3072]{1,0:T(8,128)(2,1)} %get-tuple-element.77.m0), channel_id=1, source_target_pairs={{0,1},{1,0},{2,3},{3,2},{4,5},{5,4},{6,7},{7,6},{8,9},{9,8},{10,11... | collective-permute-start | bytes 2359304 | tf_op jit(solution)/shard_map/ppermute | solution.py:360
  4.9 20.9 %collective-permute-start = (bf16[128,3072]{1,0:T(8,128)(2,1)}, bf16[128,3072]{1,0:T(8,128)(2,1)S(1)}, u32[]{:S(2)}, u32[]{:S(2)}) collective-permute-start(bf16[128,3072]{1,0:T(8,128)(2,1)} %get-tuple-element.77.m0), channel_id=1, source_target_pairs={{0,2},{1,3},{2,0},{3,1},{4,6},{5,7},{6,4},{7,5},{8,10},{9,11},{10,... | collective-permute-start | bytes 2359304 | tf_op jit(solution)/shard_map/ppermute | solution.py:363
  7.5 1.2 %copy-start.2 = (bf16[128,3072]{1,0:T(8,128)(2,1)S(1)}, bf16[128,3072]{1,0:T(8,128)(2,1)}, u32[]{:S(2)}) copy-start(bf16[128,3072]{1,0:T(8,128)(2,1)} %get-tuple-element.77.m0) | copy-start | bytes 2359300
  25.9 2.3 %collective-permute-start.2 = (bf16[128,3072]{1,0:T(8,128)(2,1)S(1)}, bf16[128,3072]{1,0:T(8,128)(2,1)S(1)}, u32[]{:S(2)}, u32[]{:S(2)}) collective-permute-start(bf16[128,3072]{1,0:T(8,128)(2,1)S(1)} %collective-permute-done.m0), channel_id=1, source_target_pairs={{0,1},{1,0},{2,3},{3,2},{4,5},{5,4},{6,7},{7,6},{8,9},{9,8},{10,11... | collective-permute-start | bytes 2359304 | tf_op jit(solution)/shard_map/ppermute | solution.py:360
  28.1 7.1 %slice-start = ((s8[9437184]{0:T(1024)(128)(4,1)}), s8[4194304]{0:T(1024)(128)(4,1)S(1)}, s32[]{:S(2)}) async-start(s8[9437184]{0:T(1024)(128)(4,1)} %bitcast.3), calls=%async_computation | async-start | bytes 8388608
  28.1 7.1 %slice-start.1 = ((s8[9437184]{0:T(1024)(128)(4,1)}), s8[4194304]{0:T(1024)(128)(4,1)S(1)}, s32[]{:S(2)}) async-start(s8[9437184]{0:T(1024)(128)(4,1)} %bitcast.3), calls=%async_computation.1 | async-start | bytes 8388608
  28.1 7.1 %slice-start.2 = ((s8[9437184]{0:T(1024)(128)(4,1)}), s8[1048576]{0:T(1024)(128)(4,1)S(1)}, s32[]{:S(2)}) async-start(s8[9437184]{0:T(1024)(128)(4,1)} %bitcast.3), calls=%async_computation.2 | async-start | bytes 2097152
  28.1 7.2 %copy-start = (bf16[512,3072]{1,0:T(8,128)(2,1)S(1)}, bf16[512,3072]{1,0:T(8,128)(2,1)}, u32[]{:S(2)}) copy-start(bf16[512,3072]{1,0:T(8,128)(2,1)} %refs_17_.1) | copy-start | bytes 9437188
  36.9 1.9 %collective-permute-start.3 = (bf16[128,1280]{1,0:T(8,128)(2,1)S(1)}, bf16[128,1280]{1,0:T(8,128)(2,1)S(1)}, u32[]{:S(2)}, u32[]{:S(2)}) collective-permute-start(bf16[128,1280]{1,0:T(8,128)(2,1)S(1)} %get-tuple-element.95), channel_id=1, source_target_pairs={{0,1},{1,0},{2,3},{3,2},{4,5},{5,4},{6,7},{7,6},{8,9},{9,8},{10,11... | collective-permute-start | bytes 983048 | tf_op jit(solution)/shard_map/ppermute | solution.py:360
  38.8 12.0 %copy-start.12 = (f32[1,3072]{1,0:T(1,128)S(1)}, f32[1,3072]{1,0:T(1,128)}, u32[]{:S(2)}) copy-start(f32[1,3072]{1,0:T(1,128)} %get-tuple-element.115.sg) | copy-start | bytes 36868
  38.8 11.3 %collective-permute-start.4 = (bf16[128,1280]{1,0:T(8,128)(2,1)S(1)}, bf16[128,1280]{1,0:T(8,128)(2,1)S(1)}, u32[]{:S(2)}, u32[]{:S(2)}) collective-permute-start(bf16[128,1280]{1,0:T(8,128)(2,1)S(1)} %join.3), channel_id=1, source_target_pairs={{0,2},{1,3},{2,0},{3,1},{4,6},{5,7},{6,4},{7,5},{8,10},{9,11},{10,... | collective-permute-start | bytes 983048 | tf_op jit(solution)/shard_map/ppermute | solution.py:363
  44.2 0.7 copy-start.15
  44.8 6.0 %collective-permute-start.11 = (bf16[128,1280]{1,0:T(8,128)(2,1)}, bf16[128,1280]{1,0:T(8,128)(2,1)}, u32[]{:S(2)}, u32[]{:S(2)}) collective-permute-start(bf16[128,1280]{1,0:T(8,128)(2,1)} %get-tuple-element.121), channel_id=1, source_target_pairs={{0,1},{1,0},{2,3},{3,2},{4,5},{5,4},{6,7},{7,6},{8,9},{9,8},{10,11... | collective-permute-start | bytes 983048 | tf_op jit(solution)/shard_map/ppermute | solution.py:360
  45.0 4.0 %collective-permute-start.5 = (bf16[128,1024]{1,0:T(8,128)(2,1)}, bf16[128,1024]{1,0:T(8,128)(2,1)}, u32[]{:S(2)}, u32[]{:S(2)}) collective-permute-start(bf16[128,1024]{1,0:T(8,128)(2,1)} %get-tuple-element.110), channel_id=1, source_target_pairs={{0,1},{1,0},{2,3},{3,2},{4,5},{5,4},{6,7},{7,6},{8,9},{9,8},{10,11... | collective-permute-start | bytes 786440 | tf_op jit(solution)/shard_map/ppermute | solution.py:360
  45.3 2.0 %collective-permute-start.6 = (bf16[128,768]{1,0:T(8,128)(2,1)}, bf16[128,768]{1,0:T(8,128)(2,1)S(1)}, u32[]{:S(2)}, u32[]{:S(2)}) collective-permute-start(bf16[128,768]{1,0:T(8,128)(2,1)} %get-tuple-element.112), channel_id=1, source_target_pairs={{0,1},{1,0},{2,3},{3,2},{4,5},{5,4},{6,7},{7,6},{8,9},{9,8},{10,11... | collective-permute-start | bytes 589832 | tf_op jit(solution)/shard_map/ppermute | solution.py:360
  47.3 0.7 copy-start.10
  48.0 0.9 copy-start.11
  48.9 13.4 %copy-start.16 = (bf16[128,768]{1,0:T(8,128)(2,1)S(1)}, bf16[128,768]{1,0:T(8,128)(2,1)}, u32[]{:S(2)}) copy-start(bf16[128,768]{1,0:T(8,128)(2,1)} %copy-done.15) | copy-start | bytes 589828
  49.0 4.0 %copy-start.9 = (bf16[128,768]{1,0:T(8,128)(2,1)}, bf16[128,768]{1,0:T(8,128)(2,1)S(1)}, u32[]{:S(2)}) copy-start(bf16[128,768]{1,0:T(8,128)(2,1)S(1)} %join.5) | copy-start | bytes 589828
  50.1 0.7 copy-start.5
  50.9 1.0 copy-start.6
  53.0 0.7 copy-start.3
  53.7 6.3 %collective-permute-start.12 = (bf16[64,1280]{1,0:T(8,128)(2,1)S(1)}, bf16[64,1280]{1,0:T(8,128)(2,1)S(1)}, u32[]{:S(2)}, u32[]{:S(2)}) collective-permute-start(bf16[64,1280]{1,0:T(8,128)(2,1)S(1)} %get-tuple-element.124), channel_id=1, source_target_pairs={{0,4},{4,0},{8,12},{12,8},{16,20},{20,16},{24,28},{28,24},{1,5},{5... | collective-permute-start | bytes 491528 | tf_op jit(solution)/shard_map/ppermute | solution.py:366
  55.2 8.7 %collective-permute-start.9 = (bf16[128,1024]{1,0:T(8,128)(2,1)}, bf16[128,1024]{1,0:T(8,128)(2,1)S(1)}, u32[]{:S(2)}, u32[]{:S(2)}) collective-permute-start(bf16[128,1024]{1,0:T(8,128)(2,1)} %get-tuple-element.118), channel_id=1, source_target_pairs={{0,1},{1,0},{2,3},{3,2},{4,5},{5,4},{6,7},{7,6},{8,9},{9,8},{10,11... | collective-permute-start | bytes 786440 | tf_op jit(solution)/shard_map/ppermute | solution.py:360
  55.2 8.7 %collective-permute-start.10 = (bf16[128,1024]{1,0:T(8,128)(2,1)S(1)}, bf16[128,1024]{1,0:T(8,128)(2,1)S(1)}, u32[]{:S(2)}, u32[]{:S(2)}) collective-permute-start(bf16[128,1024]{1,0:T(8,128)(2,1)S(1)} %join.4), channel_id=1, source_target_pairs={{0,2},{1,3},{2,0},{3,1},{4,6},{5,7},{6,4},{7,5},{8,10},{9,11},{10,... | collective-permute-start | bytes 786440 | tf_op jit(solution)/shard_map/ppermute | solution.py:363
  60.7 5.4 %collective-permute-start.14 = (bf16[64,1280]{1,0:T(8,128)(2,1)S(1)}, bf16[64,1280]{1,0:T(8,128)(2,1)S(1)}, u32[]{:S(2)}, u32[]{:S(2)}) collective-permute-start(bf16[64,1280]{1,0:T(8,128)(2,1)S(1)} %get-tuple-element.155), channel_id=1, source_target_pairs={{0,8},{4,12},{8,0},{12,4},{16,24},{20,28},{24,16},{28,20},{1,9},{5... | collective-permute-start | bytes 491528 | tf_op jit(solution)/shard_map/ppermute | solution.py:431
  62.3 12.4 %collective-permute-start.7 = (bf16[128,768]{1,0:T(8,128)(2,1)S(1)}, bf16[128,768]{1,0:T(8,128)(2,1)}, u32[]{:S(2)}, u32[]{:S(2)}) collective-permute-start(bf16[128,768]{1,0:T(8,128)(2,1)S(1)} %copy-done.16), channel_id=1, source_target_pairs={{0,1},{1,0},{2,3},{3,2},{4,5},{5,4},{6,7},{7,6},{8,9},{9,8},{10,11... | collective-permute-start | bytes 589832 | tf_op jit(solution)/shard_map/ppermute | solution.py:360
  62.3 12.4 %collective-permute-start.8 = (bf16[128,768]{1,0:T(8,128)(2,1)}, bf16[128,768]{1,0:T(8,128)(2,1)}, u32[]{:S(2)}, u32[]{:S(2)}) collective-permute-start(bf16[128,768]{1,0:T(8,128)(2,1)} %copy-done.9), channel_id=1, source_target_pairs={{0,2},{1,3},{2,0},{3,1},{4,6},{5,7},{6,4},{7,5},{8,10},{9,11},{10,... | collective-permute-start | bytes 589832 | tf_op jit(solution)/shard_map/ppermute | solution.py:363
  64.1 0.7 copy-start.7
  64.8 5.1 %collective-permute-start.13 = (bf16[64,1024]{1,0:T(8,128)(2,1)S(1)}, bf16[64,1024]{1,0:T(8,128)(2,1)S(1)}, u32[]{:S(2)}, u32[]{:S(2)}) collective-permute-start(bf16[64,1024]{1,0:T(8,128)(2,1)S(1)} %get-tuple-element.128), channel_id=1, source_target_pairs={{0,4},{4,0},{8,12},{12,8},{16,20},{20,16},{24,28},{28,24},{1,5},{5... | collective-permute-start | bytes 393224 | tf_op jit(solution)/shard_map/ppermute | solution.py:366
  66.2 29.9 %copy-start.1 = (f32[128,3072]{1,0:T(8,128)S(1)}, f32[128,3072]{1,0:T(8,128)}, u32[]{:S(2)}) copy-start(f32[128,3072]{1,0:T(8,128)} %x_start.5) | copy-start | bytes 4718596
  66.2 29.9 %copy-start.4 = (f32[64,1280]{1,0:T(8,128)S(1)}, f32[64,1280]{1,0:T(8,128)}, u32[]{:S(2)}) copy-start(f32[64,1280]{1,0:T(8,128)} %copy-done.3) | copy-start | bytes 983044
  70.6 9.0 %collective-permute-start.16 = (bf16[64,1024]{1,0:T(8,128)(2,1)}, bf16[64,1024]{1,0:T(8,128)(2,1)}, u32[]{:S(2)}, u32[]{:S(2)}) collective-permute-start(bf16[64,1024]{1,0:T(8,128)(2,1)} %fusion.4), channel_id=1, source_target_pairs={{0,8},{4,12},{8,0},{12,4},{16,24},{20,28},{24,16},{28,20},{1,9},{5... | collective-permute-start | bytes 393224 | tf_op jit(solution)/shard_map/ppermute | solution.py:431
  72.1 5.7 %collective-permute-start.17 = (bf16[32,1280]{1,0:T(8,128)(2,1)}, bf16[32,1280]{1,0:T(8,128)(2,1)}, u32[]{:S(2)}, u32[]{:S(2)}) collective-permute-start(bf16[32,1280]{1,0:T(8,128)(2,1)} %fusion.5), channel_id=1, source_target_pairs={{0,16},{4,20},{8,24},{12,28},{16,0},{20,4},{24,8},{28,12},{1,17},{... | collective-permute-start | bytes 245768 | tf_op jit(solution)/shard_map/ppermute | solution.py:431
  75.9 6.3 %collective-permute-start.15 = (bf16[64,768]{1,0:T(8,128)(2,1)S(1)}, bf16[64,768]{1,0:T(8,128)(2,1)S(1)}, u32[]{:S(2)}, u32[]{:S(2)}) collective-permute-start(bf16[64,768]{1,0:T(8,128)(2,1)S(1)} %get-tuple-element.133), channel_id=1, source_target_pairs={{0,4},{4,0},{8,12},{12,8},{16,20},{20,16},{24,28},{28,24},{1,5},{5... | collective-permute-start | bytes 294920 | tf_op jit(solution)/shard_map/ppermute | solution.py:366
  77.8 6.7 %collective-permute-start.19 = (bf16[32,1280]{1,0:T(8,128)(2,1)}, bf16[32,1280]{1,0:T(8,128)(2,1)S(1)}, u32[]{:S(2)}, u32[]{:S(2)}) collective-permute-start(bf16[32,1280]{1,0:T(8,128)(2,1)} %collective-permute-done.17), channel_id=1, source_target_pairs={{0,8},{4,12},{8,0},{12,4},{16,24},{20,28},{24,16},{28,20},{1,9},{5... | collective-permute-start | bytes 245768 | tf_op jit(solution)/shard_map/ppermute | solution.py:431
  80.5 8.0 %collective-permute-start.22 = (bf16[64,1024]{1,0:T(8,128)(2,1)S(1)}, bf16[64,1024]{1,0:T(8,128)(2,1)S(1)}, u32[]{:S(2)}, u32[]{:S(2)}) collective-permute-start(bf16[64,1024]{1,0:T(8,128)(2,1)S(1)} %fusion), channel_id=1, source_target_pairs={{0,16},{4,20},{8,24},{12,28},{16,0},{20,4},{24,8},{28,12},{1,17},{... | collective-permute-start | bytes 393224 | tf_op jit(solution)/shard_map/ppermute | solution.py:431
  82.2 4.7 %collective-permute-start.18 = (bf16[64,768]{1,0:T(8,128)(2,1)S(1)}, bf16[64,768]{1,0:T(8,128)(2,1)S(1)}, u32[]{:S(2)}, u32[]{:S(2)}) collective-permute-start(bf16[64,768]{1,0:T(8,128)(2,1)S(1)} %fusion.6), channel_id=1, source_target_pairs={{0,8},{4,12},{8,0},{12,4},{16,24},{20,28},{24,16},{28,20},{1,9},{5... | collective-permute-start | bytes 294920 | tf_op jit(solution)/shard_map/ppermute | solution.py:431
  85.5 10.6 %collective-permute-start.24 = (bf16[64,1280]{1,0:T(8,128)(2,1)S(1)}, bf16[64,1280]{1,0:T(8,128)(2,1)S(1)}, u32[]{:S(2)}, u32[]{:S(2)}) collective-permute-start(bf16[64,1280]{1,0:T(8,128)(2,1)S(1)} %get-tuple-element.153), channel_id=1, source_target_pairs={{0,4},{4,0},{8,12},{12,8},{16,20},{20,16},{24,28},{28,24},{1,5},{5... | collective-permute-start | bytes 491528 | tf_op jit(solution)/shard_map/ppermute | solution.py:366
  86.9 10.2 %copy-start.8 = (f32[64,1024]{1,0:T(8,128)S(1)}, f32[64,1024]{1,0:T(8,128)}, u32[]{:S(2)}) copy-start(f32[64,1024]{1,0:T(8,128)} %copy-done.7) | copy-start | bytes 786436
  87.0 6.6 %collective-permute-start.20 = (bf16[64,768]{1,0:T(8,128)(2,1)S(1)}, bf16[64,768]{1,0:T(8,128)(2,1)S(1)}, u32[]{:S(2)}, u32[]{:S(2)}) collective-permute-start(bf16[64,768]{1,0:T(8,128)(2,1)S(1)} %fusion.3), channel_id=1, source_target_pairs={{0,16},{4,20},{8,24},{12,28},{16,0},{20,4},{24,8},{28,12},{1,17},{... | collective-permute-start | bytes 294920 | tf_op jit(solution)/shard_map/ppermute | solution.py:431
  89.5 7.6 %collective-permute-start.23 = (bf16[64,1024]{1,0:T(8,128)(2,1)S(1)}, bf16[64,1024]{1,0:T(8,128)(2,1)S(1)}, u32[]{:S(2)}, u32[]{:S(2)}) collective-permute-start(bf16[64,1024]{1,0:T(8,128)(2,1)S(1)} %get-tuple-element.149), channel_id=1, source_target_pairs={{0,4},{4,0},{8,12},{12,8},{16,20},{20,16},{24,28},{28,24},{1,5},{5... | collective-permute-start | bytes 393224 | tf_op jit(solution)/shard_map/ppermute | solution.py:366
  93.6 5.0 %collective-permute-start.21 = (bf16[64,768]{1,0:T(8,128)(2,1)S(1)}, bf16[64,768]{1,0:T(8,128)(2,1)S(1)}, u32[]{:S(2)}, u32[]{:S(2)}) collective-permute-start(bf16[64,768]{1,0:T(8,128)(2,1)S(1)} %get-tuple-element.151), channel_id=1, source_target_pairs={{0,4},{4,0},{8,12},{12,8},{16,20},{20,16},{24,28},{28,24},{1,5},{5... | collective-permute-start | bytes 294920 | tf_op jit(solution)/shard_map/ppermute | solution.py:366

commit v9 on v8

--- a/solution.py
+++ b/solution.py
@@ -421,7 +421,7 @@
     for c in range(1, chunks):
         here = slice((c - 1) * others, c * others)
         later.append(joined(parts[here], sent[here]))
-    first, keep, later = tied([row[0] for row in got], keep, later)
+    first, later = tied([row[0] for row in got], later)
     for row, one in zip(got, first):
         row[0] = one
     for ready in later:
@@ -477,7 +477,7 @@
 
         def finish(fetched):
             given = [held[name] for name in ("earlier", "kept", "fetched", "other")]
-            fetched, into = tied(fetched, list(written))
+            into = list(written)
             written[:] = [finish_call(which, x_start, *given, fetched[0], into, firsts[c])]
 
         stages = [(drift_of, to_pair, "x", 0.5), (pair_sum, swap(1), "z1", 0.5)]

time: 100 us -> 100 us (level)
  no operation moved by 1% of the time
where the time goes in v9:
time: 100 us; the launch traced here: 99.7 us
  Pallas kernels  36.2 us (36%)
  starting transfers between devices  26.1 us (26%)
  waiting for transfers between devices  23.3 us (23%)
  local copies, waits for them, and re-layouts  6.61 us (7%)
  other arithmetic  6.3 us (6%)
  between operations  1.15 us (1%)
    pallas_call x2, Pallas kernels, project_call(): pl.pallas_call(functools.partial(project_kernel, tile, load, tiles), in_s...  17.6 us
    ppermute x7, starting transfers between devices, along(): lax.ppermute(x, 'step', [(2 * a + i, 2 * b + i) for a, b in pairs for i i...  12.1 us
    ppermute x6, starting transfers between devices, to_pair(): return lax.ppermute(x, 'step', [(i, i ^ 1) for i in range(n_step)])  7.22 us
    ppermute x6, waiting for transfers between devices, to_pair(): return lax.ppermute(x, 'step', [(i, i ^ 1) for i in range(n_step)])  6.87 us
    unnamed x40, local copies, waits for them, and re-layouts  6.61 us
    ppermute x7, waiting for transfers between devices, along(): lax.ppermute(x, 'step', [(2 * a + i, 2 * b + i) for a, b in pairs for i i...  6.4 us
    ppermute x4, waiting for transfers between devices, to_chip(): lax.ppermute(x, 'seq', [(i, (i + 2 * offset) % n_seq) for i in range(n_se...  5.91 us
    ppermute x4, starting transfers between devices, to_chip(): lax.ppermute(x, 'seq', [(i, (i + 2 * offset) % n_seq) for i in range(n_se...  5.42 us
  transfers between devices with their start and end apart: 25, of which 12 were waited for; matrix products, arithmetic and copies ran while one was open for 6% of the time, Pallas kernels for 22%

profile of v9, /device:TPU:0, one launch (start us, length us, event | category | flops | bytes accessed | tf_op | source)
XLA Modules:
  0.0 99.7 jit_solution(12680133927506133003)
XLA Ops:
  0.7 3.7 %norm.1 = (bf16[128,3072]{1,0:T(8,128)(2,1)}, f32[1,3072]{1,0:T(1,128)}) custom-call(s32[1]{0:T(128)S(6)} %copy.16.t_ref, f32[50]{0:T(128)} %size_ref.1, f32[1,128,3072]{2,1,0:T(8,128)} %x_hbm.1, f32[50,9216]{1,0:T(8,128)} %mod_hbm.1), custom_call_target="tpu_custom_call" | custom-call | flops 3932160 | tf_op jit(solution)/shard_map/norm/pallas_call | solution.py:56
  4.4 0.5 collective-permute-start.1
  4.9 2.6 %collective-permute-start = (bf16[128,3072]{1,0:T(8,128)(2,1)}, bf16[128,3072]{1,0:T(8,128)(2,1)S(1)}, u32[]{:S(2)}, u32[]{:S(2)}) collective-permute-start(bf16[128,3072]{1,0:T(8,128)(2,1)} %get-tuple-element.70.m0), channel_id=1, source_target_pairs={{0,2},{1,3},{2,0},{3,1},{4,6},{5,7},{6,4},{7,5},{8,10},{9,11},{10,... | collective-permute-start | bytes 2359304 | tf_op jit(solution)/shard_map/ppermute | solution.py:363
  7.5 1.1 %copy-done.2 = bf16[128,3072]{1,0:T(8,128)(2,1)S(1)} copy-done((bf16[128,3072]{1,0:T(8,128)(2,1)S(1)}, bf16[128,3072]{1,0:T(8,128)(2,1)}, u32[]{:S(2)}) %copy-start.2) | copy-done | bytes 786456
  8.7 12.4 %project.2 = (bf16[256,512]{1,0:T(8,128)(2,1)S(1)}, bf16[256,512]{1,0:T(8,128)(2,1)S(1)}, bf16[256,512]{1,0:T(8,128)(2,1)S(1)}, bf16[256,1536]{1,0:T(8,128)(2,1)...) custom-call(bf16[128,3072]{1,0:T(8,128)(2,1)S(1)} %copy-done.2, ...), custom_call_target="tpu_custom_call" | custom-call | flops 4831838208 | tf_op jit(solution)/shard_map/project/pallas_call | solution.py:151
  21.1 4.8 %collective-permute-done.m0 = bf16[128,3072]{1,0:T(8,128)(2,1)S(1)} collective-permute-done((bf16[128,3072]{1,0:T(8,128)(2,1)}, bf16[128,3072]{1,0:T(8,128)(2,1)S(1)}, u32[]{:S(2)}, u32[]{:S(2)}) %collective-permute-start) | collective-permute-done | bytes 786464 | tf_op jit(solution)/shard_map/ppermute | solution.py:363
  25.9 2.3 %collective-permute-done.2.m1 = bf16[128,3072]{1,0:T(8,128)(2,1)S(1)} collective-permute-done((bf16[128,3072]{1,0:T(8,128)(2,1)S(1)}, bf16[128,3072]{1,0:T(8,128)(2,1)S(1)}, u32[]{:S(2)}, u32[]{:S(2)}) %collective-permute-start.2) | collective-permute-done | bytes 786464 | tf_op jit(solution)/shard_map/ppermute | solution.py:360
  28.2 5.2 %project.3 = (bf16[256,512]{1,0:T(8,128)(2,1)S(1)}, bf16[256,512]{1,0:T(8,128)(2,1)S(1)}, bf16[256,512]{1,0:T(8,128)(2,1)S(1)}, bf16[256,1536]{1,0:T(8,128)(2,1)S(1)}) custom-call(bf16[128,3072]{1,0:T(8,128)(2,1)S(1)} %collective-permute-done.m0, bf16[128,3072]{1,0:T(8,128)(2,1)S(1)} %collective-permute-done.2.m1, f32[1,128]{1,0:T(1,128)S(1)} %bitcast.6, ...), custom_call_target="tpu_custom_call" | custom-call | flops 4831838208 | tf_op jit(solution)/shard_map/project/pallas_call | solution.py:151
  33.4 1.9 %attend.2.refs_0_.refs_4_ = bf16[256,512]{1,0:T(8,128)(2,1)S(1)} custom-call(bf16[256,512]{1,0:T(8,128)(2,1)S(1)} %get-tuple-element.80.refs_0_, bf16[256,512]{1,0:T(8,128)(2,1)S(1)} %get-tuple-element.81.refs_1_, bf16[256,512]{1,0:T(8,128)(2,1)S(1)} %get-tuple-element.82.refs_2_, bf16[256,512]{1,0:T(8,128)(2,1)S(1)} %get-tuple-element.83.refs_3_, ...), custom_call_target="tpu_custom_call" | custom-call | flops 805306368 | tf_op jit(solution)/shard_map/attend/pallas_call | solution.py:191
  35.3 1.5 %project_out.2 = (f32[128,1280]{1,0:T(8,128)S(1)}, bf16[128,1280]{1,0:T(8,128)(2,1)S(1)}) custom-call(bf16[256,512]{1,0:T(8,128)(2,1)S(1)} %attend.2.refs_0_.refs_4_, bf16[256,1536]{1,0:T(8,128)(2,1)S(1)} %get-tuple-element.94.refs_1_.refs_5_, bf16[512,3072]{1,0:T(8,128)(2,1)S(1)} %copy-done, bf16[1536,3072]{1,0:T(8,128)(2,1)S(1)} %bitcast.4), custom_call_target="tpu_custom_call" | custom-call | flops 1342177280 | tf_op jit(solution)/shard_map/project_out/pallas_call | solution.py:235
  36.9 0.2 collective-permute-start.3
  37.1 1.7 %attend.3.refs_8_.refs_12_.refs_16_ = bf16[256,512]{1,0:T(8,128)(2,1)S(1)} custom-call(bf16[256,512]{1,0:T(8,128)(2,1)S(1)} %get-tuple-element.89.refs_0_, bf16[256,512]{1,0:T(8,128)(2,1)S(1)} %get-tuple-element.81.refs_1_, bf16[256,512]{1,0:T(8,128)(2,1)S(1)} %get-tuple-element.82.refs_2_, bf16[256,512]{1,0:T(8,128)(2,1)S(1)} %get-tuple-element.83.refs_3_, ...), custom_call_target="tpu_custom_call" | custom-call | flops 805306368 | tf_op jit(solution)/shard_map/attend/pallas_call | solution.py:191
  38.8 0.1 join.3
  38.8 1.8 %collective-permute-start.5 = (bf16[128,1280]{1,0:T(8,128)(2,1)S(1)}, bf16[128,1280]{1,0:T(8,128)(2,1)S(1)}, u32[]{:S(2)}, u32[]{:S(2)}) collective-permute-start(bf16[128,1280]{1,0:T(8,128)(2,1)S(1)} %join.3), channel_id=1, source_target_pairs={{0,2},{1,3},{2,0},{3,1},{4,6},{5,7},{6,4},{7,5},{8,10},{9,11},{10,... | collective-permute-start | bytes 983048 | tf_op jit(solution)/shard_map/ppermute | solution.py:363
  40.7 3.5 %project_out.3 = (f32[128,1024]{1,0:T(8,128)S(1)}, bf16[128,1024]{1,0:T(8,128)(2,1)}, f32[128,768]{1,0:T(8,128)S(1)}, bf16[128,768]{1,0:T(8,128)(2,1)}, f32[128,...) custom-call(bf16[256,512]{1,0:T(8,128)(2,1)S(1)} %attend.2.refs_0_.r, ...), custom_call_target="tpu_custom_call" | custom-call | flops 2684354560 | tf_op jit(solution)/shard_map/project_out/pallas_call | solution.py:235
  44.2 0.7 copy-done.15
  44.8 0.1 collective-permute-start.11
  45.0 0.4 collective-permute-start.6
  45.3 0.1 collective-permute-start.7
  45.5 1.8 %collective-permute-done.7.sent = bf16[128,768]{1,0:T(8,128)(2,1)S(1)} collective-permute-done((bf16[128,768]{1,0:T(8,128)(2,1)}, bf16[128,768]{1,0:T(8,128)(2,1)S(1)}, u32[]{:S(2)}, u32[]{:S(2)}) %collective-permute-start.7) | collective-permute-done | bytes 196640 | tf_op jit(solution)/shard_map/ppermute | solution.py:360
  47.3 0.7 copy-done.10
  48.0 0.9 copy-done.11
  49.0 1.1 %join.4 = bf16[128,1024]{1,0:T(8,128)(2,1)S(1)} custom-call(f32[128,1024]{1,0:T(8,128)S(1)} %get-tuple-element.102.keep, bf16[128,1024]{1,0:T(8,128)(2,1)} %collective-permute-done.6.sent), custom_call_target="tpu_custom_call" | custom-call | tf_op jit(solution)/shard_map/join/pallas_call | solution.py:253
  50.1 0.7 copy-done.5
  50.9 1.0 copy-done.6
  51.8 1.1 %drift.3 = (f32[64,1280]{1,0:T(8,128)S(1)}, f32[64,1280]{1,0:T(8,128)S(1)}, bf16[64,1280]{1,0:T(8,128)(2,1)S(1)}) custom-call(s32[1]{0:T(128)} %bitcast.parity, f32[128,1280]{1,0:T(8,128)S(1)} %get-tuple-element.110.keep, bf16[128,1280]{1,0:T(8,128)(2,1)} %collective-permute-done.11.sent, f32[1,3072]{1,0:T(1,128)S(1)} %copy-done.12, ...), custom_call_target="tpu_custom_call" | custom-call | tf_op jit(solution)/shard_map/drift/pallas_call | solution.py:286
  53.0 0.7 copy-done.3
  53.7 1.5 %collective-permute-start.12 = (bf16[64,1280]{1,0:T(8,128)(2,1)S(1)}, bf16[64,1280]{1,0:T(8,128)(2,1)S(1)}, u32[]{:S(2)}, u32[]{:S(2)}) collective-permute-start(bf16[64,1280]{1,0:T(8,128)(2,1)S(1)} %get-tuple-element.114), channel_id=1, source_target_pairs={{0,4},{4,0},{8,12},{12,8},{16,20},{20,16},{24,28},{28,24},{1,5},{5... | collective-permute-start | bytes 491528 | tf_op jit(solution)/shard_map/ppermute | solution.py:366
  55.2 0.5 collective-permute-start.10
  55.7 4.2 %collective-permute-done.12.fetched = bf16[64,1280]{1,0:T(8,128)(2,1)S(1)} collective-permute-done((bf16[64,1280]{1,0:T(8,128)(2,1)S(1)}, bf16[64,1280]{1,0:T(8,128)(2,1)S(1)}, u32[]{:S(2)}, u32[]{:S(2)}) %collective-permute-start.12) | collective-permute-done | bytes 163872 | tf_op jit(solution)/shard_map/ppermute | solution.py:366
  60.0 0.8 fusion.9
  60.7 1.6 %collective-permute-start.14 = (bf16[64,1280]{1,0:T(8,128)(2,1)S(1)}, bf16[64,1280]{1,0:T(8,128)(2,1)S(1)}, u32[]{:S(2)}, u32[]{:S(2)}) collective-permute-start(bf16[64,1280]{1,0:T(8,128)(2,1)S(1)} %get-tuple-element.141), channel_id=1, source_target_pairs={{0,8},{4,12},{8,0},{12,4},{16,24},{20,28},{24,16},{28,20},{1,9},{5... | collective-permute-start | bytes 491528 | tf_op jit(solution)/shard_map/ppermute | solution.py:431
  62.3 0.5 collective-permute-start.8
  62.8 1.1 %collective-permute-done.10.refs_0_ = bf16[128,1024]{1,0:T(8,128)(2,1)S(1)} collective-permute-done((bf16[128,1024]{1,0:T(8,128)(2,1)S(1)}, bf16[128,1024]{1,0:T(8,128)(2,1)S(1)}, u32[]{:S(2)}, u32[]{:S(2)}) %collective-permute-start.10) | collective-permute-done | bytes 262176 | tf_op jit(solution)/shard_map/ppermute | solution.py:363
  64.0 0.1 drift.4
  64.1 0.7 copy-done.7
  64.8 0.5 collective-permute-start.13
  65.3 0.9 collective-permute-done.14
  66.2 1.7 %fusion.5 = bf16[32,1280]{1,0:T(8,128)(2,1)} fusion(f32[64,1280]{1,0:T(8,128)S(1)} %convert_element_type.70, s32[]{:T(128)S(6)} %select_n.11, f32[64,1280]{1,0:T(8,128)} %get-tuple-element.142), kind=kLoop, calls=%fused_computation.17 | loop fusion | flops 81920 | bytes 409604 | tf_op jit(solution)/shard_map/convert_element_type | solution.py:469
  67.9 2.0 %collective-permute-done.13.fetched = bf16[64,1024]{1,0:T(8,128)(2,1)S(1)} collective-permute-done((bf16[64,1024]{1,0:T(8,128)(2,1)S(1)}, bf16[64,1024]{1,0:T(8,128)(2,1)S(1)}, u32[]{:S(2)}, u32[]{:S(2)}) %collective-permute-start.13) | collective-permute-done | bytes 131104 | tf_op jit(solution)/shard_map/ppermute | solution.py:366
  69.9 0.7 fusion.4
  70.6 1.6 %collective-permute-start.16 = (bf16[64,1024]{1,0:T(8,128)(2,1)}, bf16[64,1024]{1,0:T(8,128)(2,1)}, u32[]{:S(2)}, u32[]{:S(2)}) collective-permute-start(bf16[64,1024]{1,0:T(8,128)(2,1)} %fusion.4), channel_id=1, source_target_pairs={{0,8},{4,12},{8,0},{12,4},{16,24},{20,28},{24,16},{28,20},{1,9},{5... | collective-permute-start | bytes 393224 | tf_op jit(solution)/shard_map/ppermute | solution.py:431
  72.1 2.6 %collective-permute-start.17 = (bf16[32,1280]{1,0:T(8,128)(2,1)}, bf16[32,1280]{1,0:T(8,128)(2,1)}, u32[]{:S(2)}, u32[]{:S(2)}) collective-permute-start(bf16[32,1280]{1,0:T(8,128)(2,1)} %fusion.5), channel_id=1, source_target_pairs={{0,16},{4,20},{8,24},{12,28},{16,0},{20,4},{24,8},{28,12},{1,17},{... | collective-permute-start | bytes 245768 | tf_op jit(solution)/shard_map/ppermute | solution.py:431
  74.8 1.1 %drift.5 = (f32[64,768]{1,0:T(8,128)S(1)}, f32[64,768]{1,0:T(8,128)S(1)}, bf16[64,768]{1,0:T(8,128)(2,1)S(1)}) custom-call(s32[1]{0:T(128)} %bitcast.parity, f32[128,768]{1,0:T(8,128)S(1)} %get-tuple-element.98.keep, bf16[128,768]{1,0:T(8,128)(2,1)} %collective-permute-done.4.sent, f32[1,3072]{1,0:T(1,128)S(1)} %copy-done.12, ...), custom_call_target="tpu_custom_call" | custom-call | tf_op jit(solution)/shard_map/drift/pallas_call | solution.py:286
  75.9 0.6 collective-permute-start.15
  76.5 1.3 %collective-permute-done.17 = bf16[32,1280]{1,0:T(8,128)(2,1)} collective-permute-done((bf16[32,1280]{1,0:T(8,128)(2,1)}, bf16[32,1280]{1,0:T(8,128)(2,1)}, u32[]{:S(2)}, u32[]{:S(2)}) %collective-permute-start.17) | collective-permute-done | bytes 81952 | tf_op jit(solution)/shard_map/ppermute | solution.py:431
  77.8 1.8 %collective-permute-start.19 = (bf16[32,1280]{1,0:T(8,128)(2,1)}, bf16[32,1280]{1,0:T(8,128)(2,1)S(1)}, u32[]{:S(2)}, u32[]{:S(2)}) collective-permute-start(bf16[32,1280]{1,0:T(8,128)(2,1)} %collective-permute-done.17), channel_id=1, source_target_pairs={{0,8},{4,12},{8,0},{12,4},{16,24},{20,28},{24,16},{28,20},{1,9},{5... | collective-permute-start | bytes 245768 | tf_op jit(solution)/shard_map/ppermute | solution.py:431
  79.6 1.0 fusion
  80.5 1.7 %collective-permute-start.22 = (bf16[64,1024]{1,0:T(8,128)(2,1)S(1)}, bf16[64,1024]{1,0:T(8,128)(2,1)S(1)}, u32[]{:S(2)}, u32[]{:S(2)}) collective-permute-start(bf16[64,1024]{1,0:T(8,128)(2,1)S(1)} %fusion), channel_id=1, source_target_pairs={{0,16},{4,20},{8,24},{12,28},{16,0},{20,4},{24,8},{28,12},{1,17},{... | collective-permute-start | bytes 393224 | tf_op jit(solution)/shard_map/ppermute | solution.py:431
  82.2 1.4 %collective-permute-start.18 = (bf16[64,768]{1,0:T(8,128)(2,1)S(1)}, bf16[64,768]{1,0:T(8,128)(2,1)S(1)}, u32[]{:S(2)}, u32[]{:S(2)}) collective-permute-start(bf16[64,768]{1,0:T(8,128)(2,1)S(1)} %fusion.6), channel_id=1, source_target_pairs={{0,8},{4,12},{8,0},{12,4},{16,24},{20,28},{24,16},{28,20},{1,9},{5... | collective-permute-start | bytes 294920 | tf_op jit(solution)/shard_map/ppermute | solution.py:431
  83.6 0.8 collective-permute-done.19
  84.5 1.1 %add_convert_fusion = (bf16[64,1280]{1,0:T(8,128)(2,1)S(1)}, f32[64,1280]{1,0:T(8,128)S(1)}) fusion(f32[64,1280]{1,0:T(8,128)S(1)} %get-tuple-element.113.kept, f32[]{:T(128)S(6)} %convert_element_type.80, bf16[32,1280]{1,0:T(8,128)(2,1)} %collective-permute-done.17, bf16[32,1280]{1,0:T(8,128)(2,1)S(1)} %collective-permute-done.19, pred[]{:T(512)S(6)} %eq.18, ...), kind=kLoop, calls=%fused_computation.2 | loop fusion | flops 1392640 | bytes 1146893 | tf_op jit(solution)/shard_map/convert_element_type | solution.py:467
  85.5 0.1 collective-permute-start.24
  85.6 1.3 %collective-permute-done.18 = bf16[64,768]{1,0:T(8,128)(2,1)S(1)} collective-permute-done((bf16[64,768]{1,0:T(8,128)(2,1)S(1)}, bf16[64,768]{1,0:T(8,128)(2,1)S(1)}, u32[]{:S(2)}, u32[]{:S(2)}) %collective-permute-start.18) | collective-permute-done | bytes 98336 | tf_op jit(solution)/shard_map/ppermute | solution.py:431
  87.0 1.5 %collective-permute-start.20 = (bf16[64,768]{1,0:T(8,128)(2,1)S(1)}, bf16[64,768]{1,0:T(8,128)(2,1)S(1)}, u32[]{:S(2)}, u32[]{:S(2)}) collective-permute-start(bf16[64,768]{1,0:T(8,128)(2,1)S(1)} %fusion.3), channel_id=1, source_target_pairs={{0,16},{4,20},{8,24},{12,28},{16,0},{20,4},{24,8},{28,12},{1,17},{... | collective-permute-start | bytes 294920 | tf_op jit(solution)/shard_map/ppermute | solution.py:431
  88.5 1.0 add_convert_fusion.1
  89.5 2.1 %collective-permute-start.23 = (bf16[64,1024]{1,0:T(8,128)(2,1)S(1)}, bf16[64,1024]{1,0:T(8,128)(2,1)S(1)}, u32[]{:S(2)}, u32[]{:S(2)}) collective-permute-start(bf16[64,1024]{1,0:T(8,128)(2,1)S(1)} %get-tuple-element.135), channel_id=1, source_target_pairs={{0,4},{4,0},{8,12},{12,8},{16,20},{20,16},{24,28},{28,24},{1,5},{5... | collective-permute-start | bytes 393224 | tf_op jit(solution)/shard_map/ppermute | solution.py:366
  91.5 2.1 %collective-permute-done.20 = bf16[64,768]{1,0:T(8,128)(2,1)S(1)} collective-permute-done((bf16[64,768]{1,0:T(8,128)(2,1)S(1)}, bf16[64,768]{1,0:T(8,128)(2,1)S(1)}, u32[]{:S(2)}, u32[]{:S(2)}) %collective-permute-start.20) | collective-permute-done | bytes 98336 | tf_op jit(solution)/shard_map/ppermute | solution.py:431
  93.6 0.1 add_convert_fusion.2
  93.7 2.4 %collective-permute-start.21 = (bf16[64,768]{1,0:T(8,128)(2,1)S(1)}, bf16[64,768]{1,0:T(8,128)(2,1)S(1)}, u32[]{:S(2)}, u32[]{:S(2)}) collective-permute-start(bf16[64,768]{1,0:T(8,128)(2,1)S(1)} %get-tuple-element.137), channel_id=1, source_target_pairs={{0,4},{4,0},{8,12},{12,8},{16,20},{20,16},{24,28},{28,24},{1,5},{5... | collective-permute-start | bytes 294920 | tf_op jit(solution)/shard_map/ppermute | solution.py:366
  96.1 1.0 finish.3.refs_0_
  97.1 0.9 finish.4.refs_0_
  98.1 0.7 collective-permute-done.21.back
  98.7 0.8 finish.5
  (53 shorter events, 0.2 us)
Async XLA Ops:
  0.0 7.5 %copy-start.13 = (f32[128]{0:T(128)S(1)}, f32[128]{0:T(128)}, u32[]{:S(2)}) copy-start(f32[128]{0:T(128)} %param.16) | copy-start | bytes 1540
  0.0 7.5 %copy-start.14 = (f32[128]{0:T(128)S(1)}, f32[128]{0:T(128)}, u32[]{:S(2)}) copy-start(f32[128]{0:T(128)} %param.17) | copy-start | bytes 1540
  4.4 3.1 %collective-permute-start.1 = (bf16[128,3072]{1,0:T(8,128)(2,1)}, bf16[128,3072]{1,0:T(8,128)(2,1)S(1)}, u32[]{:S(2)}, u32[]{:S(2)}) collective-permute-start(bf16[128,3072]{1,0:T(8,128)(2,1)} %get-tuple-element.70.m0), channel_id=1, source_target_pairs={{0,1},{1,0},{2,3},{3,2},{4,5},{5,4},{6,7},{7,6},{8,9},{9,8},{10,11... | collective-permute-start | bytes 2359304 | tf_op jit(solution)/shard_map/ppermute | solution.py:360
  4.9 20.9 %collective-permute-start = (bf16[128,3072]{1,0:T(8,128)(2,1)}, bf16[128,3072]{1,0:T(8,128)(2,1)S(1)}, u32[]{:S(2)}, u32[]{:S(2)}) collective-permute-start(bf16[128,3072]{1,0:T(8,128)(2,1)} %get-tuple-element.70.m0), channel_id=1, source_target_pairs={{0,2},{1,3},{2,0},{3,1},{4,6},{5,7},{6,4},{7,5},{8,10},{9,11},{10,... | collective-permute-start | bytes 2359304 | tf_op jit(solution)/shard_map/ppermute | solution.py:363
  7.5 1.2 %copy-start.2 = (bf16[128,3072]{1,0:T(8,128)(2,1)S(1)}, bf16[128,3072]{1,0:T(8,128)(2,1)}, u32[]{:S(2)}) copy-start(bf16[128,3072]{1,0:T(8,128)(2,1)} %get-tuple-element.70.m0) | copy-start | bytes 2359300
  25.9 2.3 %collective-permute-start.2 = (bf16[128,3072]{1,0:T(8,128)(2,1)S(1)}, bf16[128,3072]{1,0:T(8,128)(2,1)S(1)}, u32[]{:S(2)}, u32[]{:S(2)}) collective-permute-start(bf16[128,3072]{1,0:T(8,128)(2,1)S(1)} %collective-permute-done.m0), channel_id=1, source_target_pairs={{0,1},{1,0},{2,3},{3,2},{4,5},{5,4},{6,7},{7,6},{8,9},{9,8},{10,11... | collective-permute-start | bytes 2359304 | tf_op jit(solution)/shard_map/ppermute | solution.py:360
  28.1 7.1 %slice-start = ((s8[9437184]{0:T(1024)(128)(4,1)}), s8[4194304]{0:T(1024)(128)(4,1)S(1)}, s32[]{:S(2)}) async-start(s8[9437184]{0:T(1024)(128)(4,1)} %bitcast.3), calls=%async_computation | async-start | bytes 8388608
  28.1 7.1 %slice-start.1 = ((s8[9437184]{0:T(1024)(128)(4,1)}), s8[4194304]{0:T(1024)(128)(4,1)S(1)}, s32[]{:S(2)}) async-start(s8[9437184]{0:T(1024)(128)(4,1)} %bitcast.3), calls=%async_computation.1 | async-start | bytes 8388608
  28.1 7.1 %slice-start.2 = ((s8[9437184]{0:T(1024)(128)(4,1)}), s8[1048576]{0:T(1024)(128)(4,1)S(1)}, s32[]{:S(2)}) async-start(s8[9437184]{0:T(1024)(128)(4,1)} %bitcast.3), calls=%async_computation.2 | async-start | bytes 2097152
  28.1 7.2 %copy-start = (bf16[512,3072]{1,0:T(8,128)(2,1)S(1)}, bf16[512,3072]{1,0:T(8,128)(2,1)}, u32[]{:S(2)}) copy-start(bf16[512,3072]{1,0:T(8,128)(2,1)} %refs_17_.1) | copy-start | bytes 9437188
  36.9 1.9 %collective-permute-start.3 = (bf16[128,1280]{1,0:T(8,128)(2,1)S(1)}, bf16[128,1280]{1,0:T(8,128)(2,1)S(1)}, u32[]{:S(2)}, u32[]{:S(2)}) collective-permute-start(bf16[128,1280]{1,0:T(8,128)(2,1)S(1)} %get-tuple-element.88), channel_id=1, source_target_pairs={{0,1},{1,0},{2,3},{3,2},{4,5},{5,4},{6,7},{7,6},{8,9},{9,8},{10,11... | collective-permute-start | bytes 983048 | tf_op jit(solution)/shard_map/ppermute | solution.py:360
  38.8 12.0 %copy-start.12 = (f32[1,3072]{1,0:T(1,128)S(1)}, f32[1,3072]{1,0:T(1,128)}, u32[]{:S(2)}) copy-start(f32[1,3072]{1,0:T(1,128)} %get-tuple-element.100.sg) | copy-start | bytes 36868
  38.8 11.3 %collective-permute-start.5 = (bf16[128,1280]{1,0:T(8,128)(2,1)S(1)}, bf16[128,1280]{1,0:T(8,128)(2,1)S(1)}, u32[]{:S(2)}, u32[]{:S(2)}) collective-permute-start(bf16[128,1280]{1,0:T(8,128)(2,1)S(1)} %join.3), channel_id=1, source_target_pairs={{0,2},{1,3},{2,0},{3,1},{4,6},{5,7},{6,4},{7,5},{8,10},{9,11},{10,... | collective-permute-start | bytes 983048 | tf_op jit(solution)/shard_map/ppermute | solution.py:363
  44.2 0.7 copy-start.15
  44.8 6.0 %collective-permute-start.11 = (bf16[128,1280]{1,0:T(8,128)(2,1)}, bf16[128,1280]{1,0:T(8,128)(2,1)}, u32[]{:S(2)}, u32[]{:S(2)}) collective-permute-start(bf16[128,1280]{1,0:T(8,128)(2,1)} %get-tuple-element.111), channel_id=1, source_target_pairs={{0,1},{1,0},{2,3},{3,2},{4,5},{5,4},{6,7},{7,6},{8,9},{9,8},{10,11... | collective-permute-start | bytes 983048 | tf_op jit(solution)/shard_map/ppermute | solution.py:360
  45.0 4.0 %collective-permute-start.6 = (bf16[128,1024]{1,0:T(8,128)(2,1)}, bf16[128,1024]{1,0:T(8,128)(2,1)}, u32[]{:S(2)}, u32[]{:S(2)}) collective-permute-start(bf16[128,1024]{1,0:T(8,128)(2,1)} %get-tuple-element.103), channel_id=1, source_target_pairs={{0,1},{1,0},{2,3},{3,2},{4,5},{5,4},{6,7},{7,6},{8,9},{9,8},{10,11... | collective-permute-start | bytes 786440 | tf_op jit(solution)/shard_map/ppermute | solution.py:360
  45.3 2.0 %collective-permute-start.7 = (bf16[128,768]{1,0:T(8,128)(2,1)}, bf16[128,768]{1,0:T(8,128)(2,1)S(1)}, u32[]{:S(2)}, u32[]{:S(2)}) collective-permute-start(bf16[128,768]{1,0:T(8,128)(2,1)} %get-tuple-element.105), channel_id=1, source_target_pairs={{0,1},{1,0},{2,3},{3,2},{4,5},{5,4},{6,7},{7,6},{8,9},{9,8},{10,11... | collective-permute-start | bytes 589832 | tf_op jit(solution)/shard_map/ppermute | solution.py:360
  47.3 0.7 copy-start.10
  48.0 0.9 copy-start.11
  48.9 13.4 %copy-start.16 = (bf16[128,768]{1,0:T(8,128)(2,1)S(1)}, bf16[128,768]{1,0:T(8,128)(2,1)}, u32[]{:S(2)}) copy-start(bf16[128,768]{1,0:T(8,128)(2,1)} %copy-done.15) | copy-start | bytes 589828
  49.0 4.0 %copy-start.9 = (bf16[128,768]{1,0:T(8,128)(2,1)}, bf16[128,768]{1,0:T(8,128)(2,1)S(1)}, u32[]{:S(2)}) copy-start(bf16[128,768]{1,0:T(8,128)(2,1)S(1)} %join.5) | copy-start | bytes 589828
  50.1 0.7 copy-start.5
  50.9 1.0 copy-start.6
  53.0 0.7 copy-start.3
  53.7 6.3 %collective-permute-start.12 = (bf16[64,1280]{1,0:T(8,128)(2,1)S(1)}, bf16[64,1280]{1,0:T(8,128)(2,1)S(1)}, u32[]{:S(2)}, u32[]{:S(2)}) collective-permute-start(bf16[64,1280]{1,0:T(8,128)(2,1)S(1)} %get-tuple-element.114), channel_id=1, source_target_pairs={{0,4},{4,0},{8,12},{12,8},{16,20},{20,16},{24,28},{28,24},{1,5},{5... | collective-permute-start | bytes 491528 | tf_op jit(solution)/shard_map/ppermute | solution.py:366
  55.2 8.7 %collective-permute-start.9 = (bf16[128,1024]{1,0:T(8,128)(2,1)}, bf16[128,1024]{1,0:T(8,128)(2,1)S(1)}, u32[]{:S(2)}, u32[]{:S(2)}) collective-permute-start(bf16[128,1024]{1,0:T(8,128)(2,1)} %get-tuple-element.108), channel_id=1, source_target_pairs={{0,1},{1,0},{2,3},{3,2},{4,5},{5,4},{6,7},{7,6},{8,9},{9,8},{10,11... | collective-permute-start | bytes 786440 | tf_op jit(solution)/shard_map/ppermute | solution.py:360
  55.2 8.7 %collective-permute-start.10 = (bf16[128,1024]{1,0:T(8,128)(2,1)S(1)}, bf16[128,1024]{1,0:T(8,128)(2,1)S(1)}, u32[]{:S(2)}, u32[]{:S(2)}) collective-permute-start(bf16[128,1024]{1,0:T(8,128)(2,1)S(1)} %join.4), channel_id=1, source_target_pairs={{0,2},{1,3},{2,0},{3,1},{4,6},{5,7},{6,4},{7,5},{8,10},{9,11},{10,... | collective-permute-start | bytes 786440 | tf_op jit(solution)/shard_map/ppermute | solution.py:363
  60.7 5.4 %collective-permute-start.14 = (bf16[64,1280]{1,0:T(8,128)(2,1)S(1)}, bf16[64,1280]{1,0:T(8,128)(2,1)S(1)}, u32[]{:S(2)}, u32[]{:S(2)}) collective-permute-start(bf16[64,1280]{1,0:T(8,128)(2,1)S(1)} %get-tuple-element.141), channel_id=1, source_target_pairs={{0,8},{4,12},{8,0},{12,4},{16,24},{20,28},{24,16},{28,20},{1,9},{5... | collective-permute-start | bytes 491528 | tf_op jit(solution)/shard_map/ppermute | solution.py:431
  62.3 12.4 %collective-permute-start.4 = (bf16[128,768]{1,0:T(8,128)(2,1)S(1)}, bf16[128,768]{1,0:T(8,128)(2,1)}, u32[]{:S(2)}, u32[]{:S(2)}) collective-permute-start(bf16[128,768]{1,0:T(8,128)(2,1)S(1)} %copy-done.16), channel_id=1, source_target_pairs={{0,1},{1,0},{2,3},{3,2},{4,5},{5,4},{6,7},{7,6},{8,9},{9,8},{10,11... | collective-permute-start | bytes 589832 | tf_op jit(solution)/shard_map/ppermute | solution.py:360
  62.3 12.4 %collective-permute-start.8 = (bf16[128,768]{1,0:T(8,128)(2,1)}, bf16[128,768]{1,0:T(8,128)(2,1)}, u32[]{:S(2)}, u32[]{:S(2)}) collective-permute-start(bf16[128,768]{1,0:T(8,128)(2,1)} %copy-done.9), channel_id=1, source_target_pairs={{0,2},{1,3},{2,0},{3,1},{4,6},{5,7},{6,4},{7,5},{8,10},{9,11},{10,... | collective-permute-start | bytes 589832 | tf_op jit(solution)/shard_map/ppermute | solution.py:363
  64.1 0.7 copy-start.7
  64.8 5.1 %collective-permute-start.13 = (bf16[64,1024]{1,0:T(8,128)(2,1)S(1)}, bf16[64,1024]{1,0:T(8,128)(2,1)S(1)}, u32[]{:S(2)}, u32[]{:S(2)}) collective-permute-start(bf16[64,1024]{1,0:T(8,128)(2,1)S(1)} %get-tuple-element.118), channel_id=1, source_target_pairs={{0,4},{4,0},{8,12},{12,8},{16,20},{20,16},{24,28},{28,24},{1,5},{5... | collective-permute-start | bytes 393224 | tf_op jit(solution)/shard_map/ppermute | solution.py:366
  66.2 29.9 %copy-start.1 = (f32[128,3072]{1,0:T(8,128)S(1)}, f32[128,3072]{1,0:T(8,128)}, u32[]{:S(2)}) copy-start(f32[128,3072]{1,0:T(8,128)} %x_start.5) | copy-start | bytes 4718596
  66.2 29.9 %copy-start.4 = (f32[64,1280]{1,0:T(8,128)S(1)}, f32[64,1280]{1,0:T(8,128)}, u32[]{:S(2)}) copy-start(f32[64,1280]{1,0:T(8,128)} %copy-done.3) | copy-start | bytes 983044
  70.6 9.0 %collective-permute-start.16 = (bf16[64,1024]{1,0:T(8,128)(2,1)}, bf16[64,1024]{1,0:T(8,128)(2,1)}, u32[]{:S(2)}, u32[]{:S(2)}) collective-permute-start(bf16[64,1024]{1,0:T(8,128)(2,1)} %fusion.4), channel_id=1, source_target_pairs={{0,8},{4,12},{8,0},{12,4},{16,24},{20,28},{24,16},{28,20},{1,9},{5... | collective-permute-start | bytes 393224 | tf_op jit(solution)/shard_map/ppermute | solution.py:431
  72.1 5.7 %collective-permute-start.17 = (bf16[32,1280]{1,0:T(8,128)(2,1)}, bf16[32,1280]{1,0:T(8,128)(2,1)}, u32[]{:S(2)}, u32[]{:S(2)}) collective-permute-start(bf16[32,1280]{1,0:T(8,128)(2,1)} %fusion.5), channel_id=1, source_target_pairs={{0,16},{4,20},{8,24},{12,28},{16,0},{20,4},{24,8},{28,12},{1,17},{... | collective-permute-start | bytes 245768 | tf_op jit(solution)/shard_map/ppermute | solution.py:431
  75.9 6.3 %collective-permute-start.15 = (bf16[64,768]{1,0:T(8,128)(2,1)S(1)}, bf16[64,768]{1,0:T(8,128)(2,1)S(1)}, u32[]{:S(2)}, u32[]{:S(2)}) collective-permute-start(bf16[64,768]{1,0:T(8,128)(2,1)S(1)} %get-tuple-element.123), channel_id=1, source_target_pairs={{0,4},{4,0},{8,12},{12,8},{16,20},{20,16},{24,28},{28,24},{1,5},{5... | collective-permute-start | bytes 294920 | tf_op jit(solution)/shard_map/ppermute | solution.py:366
  77.8 6.7 %collective-permute-start.19 = (bf16[32,1280]{1,0:T(8,128)(2,1)}, bf16[32,1280]{1,0:T(8,128)(2,1)S(1)}, u32[]{:S(2)}, u32[]{:S(2)}) collective-permute-start(bf16[32,1280]{1,0:T(8,128)(2,1)} %collective-permute-done.17), channel_id=1, source_target_pairs={{0,8},{4,12},{8,0},{12,4},{16,24},{20,28},{24,16},{28,20},{1,9},{5... | collective-permute-start | bytes 245768 | tf_op jit(solution)/shard_map/ppermute | solution.py:431
  80.5 8.0 %collective-permute-start.22 = (bf16[64,1024]{1,0:T(8,128)(2,1)S(1)}, bf16[64,1024]{1,0:T(8,128)(2,1)S(1)}, u32[]{:S(2)}, u32[]{:S(2)}) collective-permute-start(bf16[64,1024]{1,0:T(8,128)(2,1)S(1)} %fusion), channel_id=1, source_target_pairs={{0,16},{4,20},{8,24},{12,28},{16,0},{20,4},{24,8},{28,12},{1,17},{... | collective-permute-start | bytes 393224 | tf_op jit(solution)/shard_map/ppermute | solution.py:431
  82.2 4.7 %collective-permute-start.18 = (bf16[64,768]{1,0:T(8,128)(2,1)S(1)}, bf16[64,768]{1,0:T(8,128)(2,1)S(1)}, u32[]{:S(2)}, u32[]{:S(2)}) collective-permute-start(bf16[64,768]{1,0:T(8,128)(2,1)S(1)} %fusion.6), channel_id=1, source_target_pairs={{0,8},{4,12},{8,0},{12,4},{16,24},{20,28},{24,16},{28,20},{1,9},{5... | collective-permute-start | bytes 294920 | tf_op jit(solution)/shard_map/ppermute | solution.py:431
  85.5 10.6 %collective-permute-start.24 = (bf16[64,1280]{1,0:T(8,128)(2,1)S(1)}, bf16[64,1280]{1,0:T(8,128)(2,1)S(1)}, u32[]{:S(2)}, u32[]{:S(2)}) collective-permute-start(bf16[64,1280]{1,0:T(8,128)(2,1)S(1)} %get-tuple-element.139), channel_id=1, source_target_pairs={{0,4},{4,0},{8,12},{12,8},{16,20},{20,16},{24,28},{28,24},{1,5},{5... | collective-permute-start | bytes 491528 | tf_op jit(solution)/shard_map/ppermute | solution.py:366
  87.0 10.2 %copy-start.8 = (f32[64,1024]{1,0:T(8,128)S(1)}, f32[64,1024]{1,0:T(8,128)}, u32[]{:S(2)}) copy-start(f32[64,1024]{1,0:T(8,128)} %copy-done.7) | copy-start | bytes 786436
  87.0 6.6 %collective-permute-start.20 = (bf16[64,768]{1,0:T(8,128)(2,1)S(1)}, bf16[64,768]{1,0:T(8,128)(2,1)S(1)}, u32[]{:S(2)}, u32[]{:S(2)}) collective-permute-start(bf16[64,768]{1,0:T(8,128)(2,1)S(1)} %fusion.3), channel_id=1, source_target_pairs={{0,16},{4,20},{8,24},{12,28},{16,0},{20,4},{24,8},{28,12},{1,17},{... | collective-permute-start | bytes 294920 | tf_op jit(solution)/shard_map/ppermute | solution.py:431
  89.5 7.6 %collective-permute-start.23 = (bf16[64,1024]{1,0:T(8,128)(2,1)S(1)}, bf16[64,1024]{1,0:T(8,128)(2,1)S(1)}, u32[]{:S(2)}, u32[]{:S(2)}) collective-permute-start(bf16[64,1024]{1,0:T(8,128)(2,1)S(1)} %get-tuple-element.135), channel_id=1, source_target_pairs={{0,4},{4,0},{8,12},{12,8},{16,20},{20,16},{24,28},{28,24},{1,5},{5... | collective-permute-start | bytes 393224 | tf_op jit(solution)/shard_map/ppermute | solution.py:366
  93.7 5.0 %collective-permute-start.21 = (bf16[64,768]{1,0:T(8,128)(2,1)S(1)}, bf16[64,768]{1,0:T(8,128)(2,1)S(1)}, u32[]{:S(2)}, u32[]{:S(2)}) collective-permute-start(bf16[64,768]{1,0:T(8,128)(2,1)S(1)} %get-tuple-element.137), channel_id=1, source_target_pairs={{0,4},{4,0},{8,12},{12,8},{16,20},{20,16},{24,28},{28,24},{1,5},{5... | collective-permute-start | bytes 294920 | tf_op jit(solution)/shard_map/ppermute | solution.py:366

commit v10 on v9

--- a/solution.py
+++ b/solution.py
@@ -74,8 +74,8 @@
 
 def project_kernel(tile, load, tiles, m0, m1, qg, kg, *refs):
     if load:
-        wq_hbm, wm_hbm, wb_hbm, q, k, v, act, low, high = refs[:9]
-        held, rows, wb, sem = refs[9:-3], refs[-3], refs[-2], refs[-1]
+        wq_hbm, wm_hbm, q, k, v, act = refs[:6]
+        held, rows, sem = refs[6:-2], refs[-2], refs[-1]
     else:
         held = refs[:tiles]
         q, k, v, act, rows = refs[tiles:]
@@ -91,11 +91,6 @@
                 source = wm_hbm.at[:, pl.ds((i - 3 * n_q) * tile, tile)]
             copies.append(pltpu.make_async_copy(source, held[i], sem.at[i]))
             copies[i].start()
-        span = low.shape[1] // (sem.shape[0] - tiles)
-        for at in range(0, low.shape[1], span):
-            here = (slice(None), pl.ds(at, span))
-            copies.append(pltpu.make_async_copy(wb_hbm.at[here], wb.at[here], sem.at[len(copies)]))
-            copies[-1].start()
     rows[:half] = m0[...]
     rows[half:] = m1[...]
 
@@ -121,16 +116,9 @@
         else:
             cols = slice((i - 3 * n_q) * tile, (i - 3 * n_q + 1) * tile)
             act[:, cols] = jax.nn.gelu(y, approximate=True).astype(bf16)
-    if load:
-        for i, copy in enumerate(copies[tiles:]):
-            copy.wait()
-            cols = slice(i * span, (i + 1) * span)
-            y = jnp.dot(act[...], wb[:, cols], preferred_element_type=f32)
-            low[:, cols] = y[:half]
-            high[:, cols] = y[half:]
-
-
-def project_call(m0, m1, q_gain, k_gain, w_qkv, w_mlp_in, w_out_mlp, held):
+
+
+def project_call(m0, m1, q_gain, k_gain, w_qkv, w_mlp_in, held):
     half, width = m0.shape
     heads = w_qkv.shape[2]
     hidden = w_mlp_in.shape[1]
@@ -144,27 +132,21 @@
     shapes.append(jax.ShapeDtypeStruct((rows, hidden), bf16))
     scratch = [VM((rows, width), bf16)]
     if load:
-        shapes += [jax.ShapeDtypeStruct((half, width), f32)] * 2
         shapes += [jax.ShapeDtypeStruct((width, tile), bf16)] * tiles
-        scratch.append(VM(w_out_mlp.shape, bf16))
-        scratch.append(pltpu.SemaphoreType.DMA((tiles + 4,)))
+        scratch.append(pltpu.SemaphoreType.DMA((tiles,)))
     return pl.pallas_call(
         functools.partial(project_kernel, tile, load, tiles),
-        in_specs=[vm] * 4 + ([hbm] * 3 if load else [vm] * tiles),
+        in_specs=[vm] * 4 + ([hbm] * 2 if load else [vm] * tiles),
         out_specs=[vm] * len(shapes),
         out_shape=shapes,
         scratch_shapes=scratch,
         compiler_params=params(27 if load else 9),
         cost_estimate=cost(2 * rows * width * (3 * heads + hidden), 0),
         name="project",
-    )(m0, m1, q_gain, k_gain, *([w_qkv, w_mlp_in, w_out_mlp] if load else held))
-
-
-def attend_kernel(pairs, head, *refs):
-    q_ref = refs[0]
-    k_refs = refs[1 : 1 + pairs]
-    v_refs = refs[1 + pairs : 1 + 2 * pairs]
-    out = refs[1 + 2 * pairs]
+    )(m0, m1, q_gain, k_gain, *([w_qkv, w_mlp_in] if load else held))
+
+
+def attend(head, q_ref, k_refs, v_refs, out):
     scale = math.log2(math.e) / math.sqrt(head)
     for h in range(q_ref.shape[1] // head):
         cols = slice(h * head, (h + 1) * head)
@@ -186,27 +168,22 @@
         out[:, cols] = mixed.astype(bf16)
 
 
-def attend_call(q, ks, vs, head):
-    vm = pl.BlockSpec(memory_space=VM)
-    return pl.pallas_call(
-        functools.partial(attend_kernel, len(ks), head),
-        in_specs=[vm] * (1 + 2 * len(ks)),
-        out_specs=vm,
-        out_shape=jax.ShapeDtypeStruct(q.shape, bf16),
-        compiler_params=params(9),
-        cost_estimate=cost(4 * len(ks) * q.shape[0] ** 2 * q.shape[1] * 3, 0),
-        name="attend",
-    )(q, *ks, *vs)
-
-
-def out_kernel(jobs, *refs):
-    outs = refs[len(refs) - 2 * len(jobs) :]
-    at = 0
-    for turn, (parts, extras, first, count) in enumerate(jobs):
-        xs = refs[at : at + parts]
-        ws = refs[at + parts : at + 2 * parts]
-        extra = refs[at + 2 * parts : at + 2 * parts + extras]
-        at += 2 * parts + extras
+def out_kernel(head, pairs, n_q, shown, jobs, *refs):
+    queries, k_refs = refs[:n_q], refs[n_q : n_q + pairs]
+    v_refs = refs[n_q + pairs : n_q + 2 * pairs]
+    at = n_q + 2 * pairs
+    outs = refs[at + sum(job[0] for job in jobs) :]
+    if shown:
+        mixed, outs = outs[:n_q], outs[n_q:]
+    else:
+        mixed = outs[len(outs) - n_q :]
+    for q, out in zip(queries, mixed):
+        attend(head, q, k_refs, v_refs, out)
+    for turn, (given, which, parts, first, count) in enumerate(jobs):
+        refs_in = list(refs[at : at + given])
+        at += given
+        xs = ([] if which is None else [mixed[which]]) + refs_in[: given - parts]
+        ws = refs_in[given - parts :]
         keep, send = outs[2 * turn : 2 * turn + 2]
         half = keep.shape[0]
         cols = slice(first, first + count)
@@ -214,34 +191,37 @@
             jnp.dot(x[...], w[:, cols], preferred_element_type=f32) for x, w in zip(xs, ws)
         ]
         y = functools.reduce(jnp.add, terms)
-        low, high = y[:half], y[half:]
-        if extra:
-            low = low + extra[0][:, cols]
-            high = high + extra[1][:, cols]
-        keep[...] = low
-        send[...] = high.astype(bf16)
-
-
-def out_call(jobs):
+        keep[...] = y[:half]
+        send[...] = y[half:].astype(bf16)
+
+
+def out_call(head, queries, ks, vs, shown, jobs):
     vm = pl.BlockSpec(memory_space=VM)
-    given, plan, shapes, flops = [], [], [], 0
-    for xs, ws, extra, first, count in jobs:
-        given += [*xs, *ws, *extra]
-        plan.append((len(xs), len(extra), first, count))
-        half = xs[0].shape[0] // 2
+    given, plan, shapes, flops, moved = [*queries, *ks, *vs], [], [], 0, 0
+    mixed = [jax.ShapeDtypeStruct(q.shape, bf16) for q in queries]
+    if shown:
+        shapes += mixed
+    for which, xs, ws, first, count in jobs:
+        plan.append((len(xs) + len(ws), which, len(ws), first, count))
+        given += [*xs, *ws]
+        half = queries[0].shape[0] // 2
         shapes.append(jax.ShapeDtypeStruct((half, count), f32))
         shapes.append(jax.ShapeDtypeStruct((half, count), bf16))
-        flops += 4 * half * count * sum(x.shape[1] for x in xs)
+        depth = sum(w.shape[0] for w in ws)
+        flops += 4 * half * count * depth
+        moved += 2 * count * depth + 6 * half * count + 4 * half * depth
     outs = pl.pallas_call(
-        functools.partial(out_kernel, plan),
+        functools.partial(out_kernel, head, len(ks), len(queries), shown, plan),
         in_specs=[vm] * len(given),
         out_specs=[vm] * len(shapes),
         out_shape=shapes,
+        scratch_shapes=[] if shown else [VM(m.shape, bf16) for m in mixed],
         compiler_params=params(9),
-        cost_estimate=cost(flops, 0),
-        name="project_out",
+        cost_estimate=cost(flops, moved),
+        name="attend_out",
     )(*given)
-    return [tuple(outs[i : i + 2]) for i in range(0, len(outs), 2)]
+    skip = len(queries) if shown else 0
+    return list(outs[:skip]), [tuple(outs[i : i + 2]) for i in range(skip, len(outs), 2)]
 
 
 def join_kernel(keep, sent, out):
@@ -256,6 +236,7 @@
         out_specs=vm,
         out_shape=jax.ShapeDtypeStruct(keep.shape, bf16),
         compiler_params=params(6),
+        cost_estimate=cost(keep.size, 8 * keep.size),
         name="join",
     )(keep, sent)
 
@@ -293,6 +274,7 @@
             jax.ShapeDtypeStruct(shape, bf16),
         ],
         compiler_params=params(6),
+        cost_estimate=cost(4 * rows * count, 13 * rows * count),
         name="drift",
     )(parity, keep, sent, sg, *fetched)
 
@@ -326,6 +308,7 @@
         scratch_shapes=[VM((rows, kept.shape[1]), f32), pltpu.SemaphoreType.DMA],
         input_output_aliases={len(given): 0} if into else {},
         compiler_params=params(6),
+        cost_estimate=cost(5 * kept.size, 24 * kept.size),
         name="finish",
     )(*given, *into)
 
@@ -375,24 +358,19 @@
 
     mine, sg = norm_call(t_idx, trajectory, mod_table, step_sizes)
     far = [to_chip(mine, j) for j in offsets]
-    q0, k0, v0, act0, low0, high0, *held = project_call(
-        mine, to_core(mine), qg, kg, w_qkv, w_mlp_in, w_out_mlp, None
+    q0, k0, v0, act0, *held = project_call(
+        mine, to_core(mine), qg, kg, w_qkv, w_mlp_in, None
     )
-    far, low0, high0 = tied(far, low0, high0)
+    far, q0 = tied(far, q0)
     qs, ks, vs, acts = [], [k0], [v0], []
     for block in far:
-        q, k, v, act = project_call(block, to_core(block), qg, kg, w_qkv, w_mlp_in, w_out_mlp, held)
+        q, k, v, act = project_call(block, to_core(block), qg, kg, w_qkv, w_mlp_in, held)
         qs.append(q)
         ks.append(k)
         vs.append(v)
         acts.append(act)
-    mixed = [attend_call(q, ks, vs, head) for q in qs]
-
     weights = [w_out_attn, w_out_mlp]
     got = [[] for _ in offsets]
-
-    def jobs_of(c):
-        return [([a, b], weights, [], firsts[c], counts[c]) for a, b in zip(mixed, acts)]
 
     def joined(parts, sent):
         return [join_call(keep, s) for (keep, _), s in zip(parts, sent)]
@@ -401,22 +379,23 @@
         for j, one in enumerate(ready):
             got[j].append(to_chip(one, chips - 1 - j))
 
-    parts = out_call(jobs_of(0))
+    others = chips - 1
+    jobs = [(j, [acts[j]], weights, firsts[0], counts[0]) for j in range(others)]
+    mixed, parts = out_call(head, qs, ks, vs, True, jobs)
     sent = [to_core(send) for _, send in parts]
-    q0, parts = tied(q0, parts)
-    mixed0 = attend_call(q0, ks, vs, head)
-    mixed0, sent = tied(mixed0, sent)
     ready = joined(parts, sent)
-    mixed, acts, mixed0, ready = tied(mixed, acts, mixed0, ready)
+    q0, ready = tied(q0, ready)
     to_chips(ready)
-    jobs = [job for c in range(1, chunks) for job in jobs_of(c)]
+    jobs = []
+    for c in range(1, chunks):
+        for j in range(others):
+            jobs.append((None, [mixed[j], acts[j]], weights, firsts[c], counts[c]))
     for c in range(chunks):
-        jobs.append(([mixed0], [w_out_attn], [low0, high0], firsts[c], counts[c]))
-    parts = out_call(jobs)
+        jobs.append((0, [act0], weights, firsts[c], counts[c]))
+    _, parts = out_call(head, [q0], ks, vs, False, jobs)
     sent = [to_core(send) for _, send in parts]
     keep = [part[0] for part in parts[-chunks:]]
     sent0 = sent[-chunks:]
-    others = chips - 1
     later = []
     for c in range(1, chunks):
         here = slice((c - 1) * others, c * others)

time: 100 us -> 102 us (1.020)
  waiting for transfers between devices: 23.3 us -> 29.3 us
  local copies, waits for them, and re-layouts: 6.61 us -> 4.21 us
  Pallas kernels: 36.2 us -> 35.1 us
    pallas_call x2, Pallas kernels: 17.6 us -> 13.7 us  [project_call(): pl.pallas_call(functools.partial(project_kernel, tile, load, tiles), in_s...]
    ppermute x4, waiting for transfers between devices: 5.91 us -> 9.82 us  [to_chip(): lax.ppermute(x, 'seq', [(i, (i + 2 * offset) % n_seq) for i in range(n_se...]
    unnamed x40 -> x34, local copies, waits for them, and re-layouts: 6.61 us -> 4.21 us
    pallas_call x4 -> x2, Pallas kernels: 8.61 us -> 10.9 us  [out_call(): pl.pallas_call(functools.partial(out_kernel, head, len(ks), len(queries),...]
    ppermute x8, waiting for transfers between devices: 4.13 us -> 5.37 us  [to_core(): return lax.ppermute(x, 'seq', [(i, i ^ 1) for i in range(n_seq)])]
    ppermute x6, starting transfers between devices: 7.22 us -> 5.99 us  [to_pair(): return lax.ppermute(x, 'step', [(i, i ^ 1) for i in range(n_step)])]
  transfers between devices with their start and end apart: 25 -> 25, of which waited for: 12 -> 13; matrix products, arithmetic and copies ran while one was open for 6% -> 6% of each run, Pallas kernels for 22% -> 20%
where the time goes in v10:
time: 102 us; the launch traced here: 101 us
  Pallas kernels  35.1 us (34%)
  waiting for transfers between devices  29.3 us (29%)
  starting transfers between devices  25.3 us (25%)
  other arithmetic  6.28 us (6%)
  local copies, waits for them, and re-layouts  4.21 us (4%)
  between operations  1.15 us (1%)
    pallas_call x2, Pallas kernels, project_call(): pl.pallas_call(functools.partial(project_kernel, tile, load, tiles), in_s...  13.7 us
    ppermute x7, starting transfers between devices, along(): lax.ppermute(x, 'step', [(2 * a + i, 2 * b + i) for a, b in pairs for i i...  12.6 us
    pallas_call x2, Pallas kernels, out_call(): pl.pallas_call(functools.partial(out_kernel, head, len(ks), len(queries),...  10.9 us
    ppermute x4, waiting for transfers between devices, to_chip(): lax.ppermute(x, 'seq', [(i, (i + 2 * offset) % n_seq) for i in range(n_se...  9.82 us
    ppermute x7, waiting for transfers between devices, along(): lax.ppermute(x, 'step', [(2 * a + i, 2 * b + i) for a, b in pairs for i i...  7.21 us
    ppermute x6, waiting for transfers between devices, to_pair(): return lax.ppermute(x, 'step', [(i, i ^ 1) for i in range(n_step)])  6.89 us
    ppermute x6, starting transfers between devices, to_pair(): return lax.ppermute(x, 'step', [(i, i ^ 1) for i in range(n_step)])  5.99 us
    ppermute x8, waiting for transfers between devices, to_core(): return lax.ppermute(x, 'seq', [(i, i ^ 1) for i in range(n_seq)])  5.37 us
  transfers between devices with their start and end apart: 25, of which 13 were waited for; matrix products, arithmetic and copies ran while one was open for 6% of the time, Pallas kernels for 20%

profile of v10, /device:TPU:0, one launch (start us, length us, event | category | flops | bytes accessed | tf_op | source)
XLA Modules:
  0.0 101.3 jit_solution(8851216616968931888)
XLA Ops:
  0.7 3.7 %norm.1 = (bf16[128,3072]{1,0:T(8,128)(2,1)}, f32[1,3072]{1,0:T(1,128)}) custom-call(s32[1]{0:T(128)S(6)} %copy.16.t_ref, f32[50]{0:T(128)} %size_ref.1, f32[1,128,3072]{2,1,0:T(8,128)} %x_hbm.1, f32[50,9216]{1,0:T(8,128)} %mod_hbm.1), custom_call_target="tpu_custom_call" | custom-call | flops 3932160 | tf_op jit(solution)/shard_map/norm/pallas_call | solution.py:56
  4.4 0.5 collective-permute-start.1
  4.9 2.6 %collective-permute-start = (bf16[128,3072]{1,0:T(8,128)(2,1)}, bf16[128,3072]{1,0:T(8,128)(2,1)S(1)}, u32[]{:S(2)}, u32[]{:S(2)}) collective-permute-start(bf16[128,3072]{1,0:T(8,128)(2,1)} %get-tuple-element.63.m0), channel_id=1, source_target_pairs={{0,2},{1,3},{2,0},{3,1},{4,6},{5,7},{6,4},{7,5},{8,10},{9,11},{10,... | collective-permute-start | bytes 2359304 | tf_op jit(solution)/shard_map/ppermute | solution.py:346
  7.5 0.0 collective-permute-done.1.m1
  7.5 1.1 %copy-done.2 = bf16[128,3072]{1,0:T(8,128)(2,1)S(1)} copy-done((bf16[128,3072]{1,0:T(8,128)(2,1)S(1)}, bf16[128,3072]{1,0:T(8,128)(2,1)}, u32[]{:S(2)}) %copy-start.2) | copy-done | bytes 786456
  8.7 8.4 %project.2 = (bf16[256,512]{1,0:T(8,128)(2,1)S(1)}, bf16[256,512]{1,0:T(8,128)(2,1)S(1)}, bf16[256,512]{1,0:T(8,128)(2,1)S(1)}, bf16[256,1536]{1,0:T(8,128)(2,1)...) custom-call(bf16[128,3072]{1,0:T(8,128)(2,1)S(1)} %copy-done.2, ...), custom_call_target="tpu_custom_call" | custom-call | flops 4831838208 | tf_op jit(solution)/shard_map/project/pallas_call | solution.py:137
  17.1 8.7 %collective-permute-done.m0 = bf16[128,3072]{1,0:T(8,128)(2,1)S(1)} collective-permute-done((bf16[128,3072]{1,0:T(8,128)(2,1)}, bf16[128,3072]{1,0:T(8,128)(2,1)S(1)}, u32[]{:S(2)}, u32[]{:S(2)}) %collective-permute-start) | collective-permute-done | bytes 786464 | tf_op jit(solution)/shard_map/ppermute | solution.py:346
  25.9 0.0 collective-permute-start.2
  25.9 2.3 %collective-permute-done.2.m1 = bf16[128,3072]{1,0:T(8,128)(2,1)S(1)} collective-permute-done((bf16[128,3072]{1,0:T(8,128)(2,1)S(1)}, bf16[128,3072]{1,0:T(8,128)(2,1)S(1)}, u32[]{:S(2)}, u32[]{:S(2)}) %collective-permute-start.2) | collective-permute-done | bytes 786464 | tf_op jit(solution)/shard_map/ppermute | solution.py:343
  28.2 5.2 %project.3 = (bf16[256,512]{1,0:T(8,128)(2,1)S(1)}, bf16[256,512]{1,0:T(8,128)(2,1)S(1)}, bf16[256,512]{1,0:T(8,128)(2,1)S(1)}, bf16[256,1536]{1,0:T(8,128)(2,1)S(1)}) custom-call(bf16[128,3072]{1,0:T(8,128)(2,1)S(1)} %collective-permute-done.m0, bf16[128,3072]{1,0:T(8,128)(2,1)S(1)} %collective-permute-done.2.m1, f32[1,128]{1,0:T(1,128)S(1)} %bitcast.6, ...), custom_call_target="tpu_custom_call" | custom-call | flops 4831838208 | tf_op jit(solution)/shard_map/project/pallas_call | solution.py:137
  33.4 3.5 %attend_out.2 = (bf16[256,512]{1,0:T(8,128)(2,1)S(1)}, f32[128,1280]{1,0:T(8,128)S(1)}, bf16[128,1280]{1,0:T(8,128)(2,1)S(1)}) custom-call(bf16[256,512]{1,0:T(8,128)(2,1)S(1)} %get-tuple-element.73.refs_0_, bf16[256,512]{1,0:T(8,128)(2,1)S(1)} %get-tuple-element.74.refs_1_, bf16[256,512]{1,0:T(8,128)(2,1)S(1)} %get-tuple-element.75.refs_2_, ...), custom_call_target="tpu_custom_call" | custom-call | flops 1342177280 | bytes 7274496 | tf_op jit(solution)/shard_map/attend_out/pallas_call | solution.py:213
  36.9 0.2 collective-permute-start.3
  37.1 1.5 %collective-permute-done.3.sent = bf16[128,1280]{1,0:T(8,128)(2,1)S(1)} collective-permute-done((bf16[128,1280]{1,0:T(8,128)(2,1)S(1)}, bf16[128,1280]{1,0:T(8,128)(2,1)S(1)}, u32[]{:S(2)}, u32[]{:S(2)}) %collective-permute-start.3) | collective-permute-done | bytes 327712 | tf_op jit(solution)/shard_map/ppermute | solution.py:343
  38.6 0.8 join.3
  39.4 1.8 %collective-permute-start.5 = (bf16[128,1280]{1,0:T(8,128)(2,1)}, bf16[128,1280]{1,0:T(8,128)(2,1)}, u32[]{:S(2)}, u32[]{:S(2)}) collective-permute-start(bf16[128,1280]{1,0:T(8,128)(2,1)} %join.3), channel_id=1, source_target_pairs={{0,2},{1,3},{2,0},{3,1},{4,6},{5,7},{6,4},{7,5},{8,10},{9,11},{10,... | collective-permute-start | bytes 983048 | tf_op jit(solution)/shard_map/ppermute | solution.py:346
  41.2 7.4 %attend_out.3 = (f32[128,1024]{1,0:T(8,128)S(1)}, bf16[128,1024]{1,0:T(8,128)(2,1)}, f32[128,768]{1,0:T(8,128)S(1)}, bf16[128,768]{1,0:T(8,128)(2,1)}, f32[128,1...) custom-call(bf16[256,512]{1,0:T(8,128)(2,1)S(1)} %get-tuple-element., ...), custom_call_target="tpu_custom_call" | custom-call | flops 5100273664 | bytes 28901376 | tf_op jit(solution)/shard_map/attend_out/pallas_call | solution.py:213
  48.6 0.1 collective-permute-start.11
  48.7 0.6 copy-done.13
  49.3 0.0 collective-permute-start.6
  49.3 0.5 collective-permute-start.7
  49.8 1.6 %collective-permute-done.7.sent = bf16[128,768]{1,0:T(8,128)(2,1)} collective-permute-done((bf16[128,768]{1,0:T(8,128)(2,1)}, bf16[128,768]{1,0:T(8,128)(2,1)}, u32[]{:S(2)}, u32[]{:S(2)}) %collective-permute-start.7) | collective-permute-done | bytes 196640 | tf_op jit(solution)/shard_map/ppermute | solution.py:343
  51.4 1.0 join.5
  52.4 0.0 collective-permute-done.6.sent
  52.4 0.7 copy-done.7
  53.2 0.9 copy-done.8
  54.2 1.1 %drift.3 = (f32[64,1280]{1,0:T(8,128)S(1)}, f32[64,1280]{1,0:T(8,128)S(1)}, bf16[64,1280]{1,0:T(8,128)(2,1)S(1)}) custom-call(s32[1]{0:T(128)} %bitcast.parity, f32[128,1280]{1,0:T(8,128)S(1)} %get-tuple-element.96.keep, bf16[128,1280]{1,0:T(8,128)(2,1)S(1)} %collective-permute-done.11.sent, f32[1,3072]{1,0:T(1,128)S(1)} %copy-done.10, ...), custom_call_target="tpu_custom_call" | custom-call | flops 655360 | bytes 2129920 | tf_op jit(solution)/shard_map/drift/pallas_call | solution.py:267
  55.3 1.6 %collective-permute-start.12 = (bf16[64,1280]{1,0:T(8,128)(2,1)S(1)}, bf16[64,1280]{1,0:T(8,128)(2,1)S(1)}, u32[]{:S(2)}, u32[]{:S(2)}) collective-permute-start(bf16[64,1280]{1,0:T(8,128)(2,1)S(1)} %get-tuple-element.100), channel_id=1, source_target_pairs={{0,4},{4,0},{8,12},{12,8},{16,20},{20,16},{24,28},{28,24},{1,5},{5... | collective-permute-start | bytes 491528 | tf_op jit(solution)/shard_map/ppermute | solution.py:349
  56.9 0.5 collective-permute-start.10
  57.4 4.3 %collective-permute-done.12.fetched = bf16[64,1280]{1,0:T(8,128)(2,1)S(1)} collective-permute-done((bf16[64,1280]{1,0:T(8,128)(2,1)S(1)}, bf16[64,1280]{1,0:T(8,128)(2,1)S(1)}, u32[]{:S(2)}, u32[]{:S(2)}) %collective-permute-start.12) | collective-permute-done | bytes 163872 | tf_op jit(solution)/shard_map/ppermute | solution.py:349
  61.7 0.8 fusion.9
  62.4 1.6 %collective-permute-start.14 = (bf16[64,1280]{1,0:T(8,128)(2,1)S(1)}, bf16[64,1280]{1,0:T(8,128)(2,1)S(1)}, u32[]{:S(2)}, u32[]{:S(2)}) collective-permute-start(bf16[64,1280]{1,0:T(8,128)(2,1)S(1)} %get-tuple-element.127), channel_id=1, source_target_pairs={{0,8},{4,12},{8,0},{12,4},{16,24},{20,28},{24,16},{28,20},{1,9},{5... | collective-permute-start | bytes 491528 | tf_op jit(solution)/shard_map/ppermute | solution.py:410
  64.0 0.5 collective-permute-start.8
  64.5 1.1 %collective-permute-done.10.refs_0_ = bf16[128,1024]{1,0:T(8,128)(2,1)S(1)} collective-permute-done((bf16[128,1024]{1,0:T(8,128)(2,1)S(1)}, bf16[128,1024]{1,0:T(8,128)(2,1)S(1)}, u32[]{:S(2)}, u32[]{:S(2)}) %collective-permute-start.10) | collective-permute-done | bytes 262176 | tf_op jit(solution)/shard_map/ppermute | solution.py:346
  65.6 0.1 drift.4
  65.7 0.7 copy-done.5
  66.4 0.5 collective-permute-start.13
  67.0 1.0 collective-permute-done.14
  68.0 0.0 copy-start.1
  68.0 1.7 %fusion.5 = bf16[32,1280]{1,0:T(8,128)(2,1)} fusion(f32[64,1280]{1,0:T(8,128)S(1)} %convert_element_type.70, s32[]{:T(128)S(6)} %select_n.11, f32[64,1280]{1,0:T(8,128)} %get-tuple-element.128), kind=kLoop, calls=%fused_computation.17 | loop fusion | flops 81920 | bytes 409604 | tf_op jit(solution)/shard_map/convert_element_type | solution.py:448
  69.7 1.9 %collective-permute-done.13.fetched = bf16[64,1024]{1,0:T(8,128)(2,1)S(1)} collective-permute-done((bf16[64,1024]{1,0:T(8,128)(2,1)S(1)}, bf16[64,1024]{1,0:T(8,128)(2,1)S(1)}, u32[]{:S(2)}, u32[]{:S(2)}) %collective-permute-start.13) | collective-permute-done | bytes 131104 | tf_op jit(solution)/shard_map/ppermute | solution.py:349
  71.6 0.7 fusion.4
  72.2 1.6 %collective-permute-start.16 = (bf16[64,1024]{1,0:T(8,128)(2,1)}, bf16[64,1024]{1,0:T(8,128)(2,1)}, u32[]{:S(2)}, u32[]{:S(2)}) collective-permute-start(bf16[64,1024]{1,0:T(8,128)(2,1)} %fusion.4), channel_id=1, source_target_pairs={{0,8},{4,12},{8,0},{12,4},{16,24},{20,28},{24,16},{28,20},{1,9},{5... | collective-permute-start | bytes 393224 | tf_op jit(solution)/shard_map/ppermute | solution.py:410
  73.8 2.6 %collective-permute-start.17 = (bf16[32,1280]{1,0:T(8,128)(2,1)}, bf16[32,1280]{1,0:T(8,128)(2,1)}, u32[]{:S(2)}, u32[]{:S(2)}) collective-permute-start(bf16[32,1280]{1,0:T(8,128)(2,1)} %fusion.5), channel_id=1, source_target_pairs={{0,16},{4,20},{8,24},{12,28},{16,0},{20,4},{24,8},{28,12},{1,17},{... | collective-permute-start | bytes 245768 | tf_op jit(solution)/shard_map/ppermute | solution.py:410
  76.4 1.1 %drift.5 = (f32[64,768]{1,0:T(8,128)S(1)}, f32[64,768]{1,0:T(8,128)S(1)}, bf16[64,768]{1,0:T(8,128)(2,1)S(1)}) custom-call(s32[1]{0:T(128)} %bitcast.parity, f32[128,768]{1,0:T(8,128)S(1)} %get-tuple-element.84.keep, bf16[128,768]{1,0:T(8,128)(2,1)} %collective-permute-done.4.sent, f32[1,3072]{1,0:T(1,128)S(1)} %copy-done.10, ...), custom_call_target="tpu_custom_call" | custom-call | flops 393216 | bytes 1277952 | tf_op jit(solution)/shard_map/drift/pallas_call | solution.py:267
  77.5 0.6 collective-permute-start.15
  78.1 1.4 %collective-permute-done.17 = bf16[32,1280]{1,0:T(8,128)(2,1)} collective-permute-done((bf16[32,1280]{1,0:T(8,128)(2,1)}, bf16[32,1280]{1,0:T(8,128)(2,1)}, u32[]{:S(2)}, u32[]{:S(2)}) %collective-permute-start.17) | collective-permute-done | bytes 81952 | tf_op jit(solution)/shard_map/ppermute | solution.py:410
  79.5 1.8 %collective-permute-start.19 = (bf16[32,1280]{1,0:T(8,128)(2,1)}, bf16[32,1280]{1,0:T(8,128)(2,1)S(1)}, u32[]{:S(2)}, u32[]{:S(2)}) collective-permute-start(bf16[32,1280]{1,0:T(8,128)(2,1)} %collective-permute-done.17), channel_id=1, source_target_pairs={{0,8},{4,12},{8,0},{12,4},{16,24},{20,28},{24,16},{28,20},{1,9},{5... | collective-permute-start | bytes 245768 | tf_op jit(solution)/shard_map/ppermute | solution.py:410
  81.2 0.9 fusion
  82.2 1.6 %collective-permute-start.22 = (bf16[64,1024]{1,0:T(8,128)(2,1)S(1)}, bf16[64,1024]{1,0:T(8,128)(2,1)S(1)}, u32[]{:S(2)}, u32[]{:S(2)}) collective-permute-start(bf16[64,1024]{1,0:T(8,128)(2,1)S(1)} %fusion), channel_id=1, source_target_pairs={{0,16},{4,20},{8,24},{12,28},{16,0},{20,4},{24,8},{28,12},{1,17},{... | collective-permute-start | bytes 393224 | tf_op jit(solution)/shard_map/ppermute | solution.py:410
  83.9 1.4 %collective-permute-start.18 = (bf16[64,768]{1,0:T(8,128)(2,1)S(1)}, bf16[64,768]{1,0:T(8,128)(2,1)S(1)}, u32[]{:S(2)}, u32[]{:S(2)}) collective-permute-start(bf16[64,768]{1,0:T(8,128)(2,1)S(1)} %fusion.6), channel_id=1, source_target_pairs={{0,8},{4,12},{8,0},{12,4},{16,24},{20,28},{24,16},{28,20},{1,9},{5... | collective-permute-start | bytes 294920 | tf_op jit(solution)/shard_map/ppermute | solution.py:410
  85.3 0.9 collective-permute-done.19
  86.1 1.1 %add_convert_fusion = (bf16[64,1280]{1,0:T(8,128)(2,1)S(1)}, f32[64,1280]{1,0:T(8,128)S(1)}) fusion(f32[64,1280]{1,0:T(8,128)S(1)} %get-tuple-element.99.kept, f32[]{:T(128)S(6)} %convert_element_type.80, bf16[32,1280]{1,0:T(8,128)(2,1)} %collective-permute-done.17, bf16[32,1280]{1,0:T(8,128)(2,1)S(1)} %collective-permute-done.19, pred[]{:T(512)S(6)} %eq.18, ...), kind=kLoop, calls=%fused_computation.2 | loop fusion | flops 1392640 | bytes 1146893 | tf_op jit(solution)/shard_map/convert_element_type | solution.py:446
  87.2 0.1 collective-permute-start.24
  87.3 1.3 %collective-permute-done.18 = bf16[64,768]{1,0:T(8,128)(2,1)S(1)} collective-permute-done((bf16[64,768]{1,0:T(8,128)(2,1)S(1)}, bf16[64,768]{1,0:T(8,128)(2,1)S(1)}, u32[]{:S(2)}, u32[]{:S(2)}) %collective-permute-start.18) | collective-permute-done | bytes 98336 | tf_op jit(solution)/shard_map/ppermute | solution.py:410
  88.6 2.0 %collective-permute-start.20 = (bf16[64,768]{1,0:T(8,128)(2,1)S(1)}, bf16[64,768]{1,0:T(8,128)(2,1)S(1)}, u32[]{:S(2)}, u32[]{:S(2)}) collective-permute-start(bf16[64,768]{1,0:T(8,128)(2,1)S(1)} %fusion.3), channel_id=1, source_target_pairs={{0,16},{4,20},{8,24},{12,28},{16,0},{20,4},{24,8},{28,12},{1,17},{... | collective-permute-start | bytes 294920 | tf_op jit(solution)/shard_map/ppermute | solution.py:410
  90.6 1.0 add_convert_fusion.1
  91.6 0.8 collective-permute-start.23
  92.5 2.8 %collective-permute-done.20 = bf16[64,768]{1,0:T(8,128)(2,1)S(1)} collective-permute-done((bf16[64,768]{1,0:T(8,128)(2,1)S(1)}, bf16[64,768]{1,0:T(8,128)(2,1)S(1)}, u32[]{:S(2)}, u32[]{:S(2)}) %collective-permute-start.20) | collective-permute-done | bytes 98336 | tf_op jit(solution)/shard_map/ppermute | solution.py:410
  95.2 0.1 add_convert_fusion.2
  95.3 2.4 %collective-permute-start.21 = (bf16[64,768]{1,0:T(8,128)(2,1)S(1)}, bf16[64,768]{1,0:T(8,128)(2,1)S(1)}, u32[]{:S(2)}, u32[]{:S(2)}) collective-permute-start(bf16[64,768]{1,0:T(8,128)(2,1)S(1)} %get-tuple-element.123), channel_id=1, source_target_pairs={{0,4},{4,0},{8,12},{12,8},{16,20},{20,16},{24,28},{28,24},{1,5},{5... | collective-permute-start | bytes 294920 | tf_op jit(solution)/shard_map/ppermute | solution.py:349
  97.7 1.0 finish.3.refs_0_
  98.7 0.9 finish.4.refs_0_
  99.6 0.7 collective-permute-done.21.back
  100.3 0.8 finish.5
  (45 shorter events, 0.2 us)
Async XLA Ops:
  0.0 7.5 %copy-start.11 = (f32[128]{0:T(128)S(1)}, f32[128]{0:T(128)}, u32[]{:S(2)}) copy-start(f32[128]{0:T(128)} %param.16) | copy-start | bytes 1540
  0.0 7.5 %copy-start.12 = (f32[128]{0:T(128)S(1)}, f32[128]{0:T(128)}, u32[]{:S(2)}) copy-start(f32[128]{0:T(128)} %param.17) | copy-start | bytes 1540
  4.4 3.1 %collective-permute-start.1 = (bf16[128,3072]{1,0:T(8,128)(2,1)}, bf16[128,3072]{1,0:T(8,128)(2,1)S(1)}, u32[]{:S(2)}, u32[]{:S(2)}) collective-permute-start(bf16[128,3072]{1,0:T(8,128)(2,1)} %get-tuple-element.63.m0), channel_id=1, source_target_pairs={{0,1},{1,0},{2,3},{3,2},{4,5},{5,4},{6,7},{7,6},{8,9},{9,8},{10,11... | collective-permute-start | bytes 2359304 | tf_op jit(solution)/shard_map/ppermute | solution.py:343
  4.9 20.9 %collective-permute-start = (bf16[128,3072]{1,0:T(8,128)(2,1)}, bf16[128,3072]{1,0:T(8,128)(2,1)S(1)}, u32[]{:S(2)}, u32[]{:S(2)}) collective-permute-start(bf16[128,3072]{1,0:T(8,128)(2,1)} %get-tuple-element.63.m0), channel_id=1, source_target_pairs={{0,2},{1,3},{2,0},{3,1},{4,6},{5,7},{6,4},{7,5},{8,10},{9,11},{10,... | collective-permute-start | bytes 2359304 | tf_op jit(solution)/shard_map/ppermute | solution.py:346
  7.5 1.2 %copy-start.2 = (bf16[128,3072]{1,0:T(8,128)(2,1)S(1)}, bf16[128,3072]{1,0:T(8,128)(2,1)}, u32[]{:S(2)}) copy-start(bf16[128,3072]{1,0:T(8,128)(2,1)} %get-tuple-element.63.m0) | copy-start | bytes 2359300
  25.9 2.3 %collective-permute-start.2 = (bf16[128,3072]{1,0:T(8,128)(2,1)S(1)}, bf16[128,3072]{1,0:T(8,128)(2,1)S(1)}, u32[]{:S(2)}, u32[]{:S(2)}) collective-permute-start(bf16[128,3072]{1,0:T(8,128)(2,1)S(1)} %collective-permute-done.m0), channel_id=1, source_target_pairs={{0,1},{1,0},{2,3},{3,2},{4,5},{5,4},{6,7},{7,6},{8,9},{9,8},{10,11... | collective-permute-start | bytes 2359304 | tf_op jit(solution)/shard_map/ppermute | solution.py:343
  28.1 5.3 %slice-start = ((s8[9437184]{0:T(1024)(128)(4,1)}), s8[4194304]{0:T(1024)(128)(4,1)S(1)}, s32[]{:S(2)}) async-start(s8[9437184]{0:T(1024)(128)(4,1)} %bitcast.3), calls=%async_computation | async-start | bytes 8388608
  28.1 5.3 %slice-start.1 = ((s8[9437184]{0:T(1024)(128)(4,1)}), s8[4194304]{0:T(1024)(128)(4,1)S(1)}, s32[]{:S(2)}) async-start(s8[9437184]{0:T(1024)(128)(4,1)} %bitcast.3), calls=%async_computation.1 | async-start | bytes 8388608
  28.1 5.3 %slice-start.2 = ((s8[9437184]{0:T(1024)(128)(4,1)}), s8[1048576]{0:T(1024)(128)(4,1)S(1)}, s32[]{:S(2)}) async-start(s8[9437184]{0:T(1024)(128)(4,1)} %bitcast.3), calls=%async_computation.2 | async-start | bytes 2097152
  28.1 5.3 %copy-start = (bf16[512,3072]{1,0:T(8,128)(2,1)S(1)}, bf16[512,3072]{1,0:T(8,128)(2,1)}, u32[]{:S(2)}) copy-start(bf16[512,3072]{1,0:T(8,128)(2,1)} %refs_20_.1) | copy-start | bytes 9437188
  36.9 1.7 %collective-permute-start.3 = (bf16[128,1280]{1,0:T(8,128)(2,1)S(1)}, bf16[128,1280]{1,0:T(8,128)(2,1)S(1)}, u32[]{:S(2)}, u32[]{:S(2)}) collective-permute-start(bf16[128,1280]{1,0:T(8,128)(2,1)S(1)} %get-tuple-element.80), channel_id=1, source_target_pairs={{0,1},{1,0},{2,3},{3,2},{4,5},{5,4},{6,7},{7,6},{8,9},{9,8},{10,11... | collective-permute-start | bytes 983048 | tf_op jit(solution)/shard_map/ppermute | solution.py:343
  39.4 14.7 %collective-permute-start.5 = (bf16[128,1280]{1,0:T(8,128)(2,1)}, bf16[128,1280]{1,0:T(8,128)(2,1)}, u32[]{:S(2)}, u32[]{:S(2)}) collective-permute-start(bf16[128,1280]{1,0:T(8,128)(2,1)} %join.3), channel_id=1, source_target_pairs={{0,2},{1,3},{2,0},{3,1},{4,6},{5,7},{6,4},{7,5},{8,10},{9,11},{10,... | collective-permute-start | bytes 983048 | tf_op jit(solution)/shard_map/ppermute | solution.py:346
  41.2 13.0 %copy-start.10 = (f32[1,3072]{1,0:T(1,128)S(1)}, f32[1,3072]{1,0:T(1,128)}, u32[]{:S(2)}) copy-start(f32[1,3072]{1,0:T(1,128)} %get-tuple-element.86.sg) | copy-start | bytes 36868
  48.6 0.7 copy-start.13
  48.6 5.5 %collective-permute-start.11 = (bf16[128,1280]{1,0:T(8,128)(2,1)}, bf16[128,1280]{1,0:T(8,128)(2,1)S(1)}, u32[]{:S(2)}, u32[]{:S(2)}) collective-permute-start(bf16[128,1280]{1,0:T(8,128)(2,1)} %get-tuple-element.97), channel_id=1, source_target_pairs={{0,1},{1,0},{2,3},{3,2},{4,5},{5,4},{6,7},{7,6},{8,9},{9,8},{10,11... | collective-permute-start | bytes 983048 | tf_op jit(solution)/shard_map/ppermute | solution.py:343
  49.3 3.1 %collective-permute-start.6 = (bf16[128,1024]{1,0:T(8,128)(2,1)}, bf16[128,1024]{1,0:T(8,128)(2,1)S(1)}, u32[]{:S(2)}, u32[]{:S(2)}) collective-permute-start(bf16[128,1024]{1,0:T(8,128)(2,1)} %get-tuple-element.89), channel_id=1, source_target_pairs={{0,1},{1,0},{2,3},{3,2},{4,5},{5,4},{6,7},{7,6},{8,9},{9,8},{10,11... | collective-permute-start | bytes 786440 | tf_op jit(solution)/shard_map/ppermute | solution.py:343
  49.3 2.1 %collective-permute-start.7 = (bf16[128,768]{1,0:T(8,128)(2,1)}, bf16[128,768]{1,0:T(8,128)(2,1)}, u32[]{:S(2)}, u32[]{:S(2)}) collective-permute-start(bf16[128,768]{1,0:T(8,128)(2,1)} %get-tuple-element.91), channel_id=1, source_target_pairs={{0,1},{1,0},{2,3},{3,2},{4,5},{5,4},{6,7},{7,6},{8,9},{9,8},{10,11... | collective-permute-start | bytes 589832 | tf_op jit(solution)/shard_map/ppermute | solution.py:343
  52.4 1.8 %copy-start.9 = (bf16[128,768]{1,0:T(8,128)(2,1)}, bf16[128,768]{1,0:T(8,128)(2,1)S(1)}, u32[]{:S(2)}) copy-start(bf16[128,768]{1,0:T(8,128)(2,1)S(1)} %join.5) | copy-start | bytes 589828
  52.4 0.7 copy-start.7
  53.2 0.9 copy-start.8
  55.3 10.3 %copy-start.3 = (f32[64,1280]{1,0:T(8,128)}, f32[64,1280]{1,0:T(8,128)S(1)}, u32[]{:S(2)}) copy-start(f32[64,1280]{1,0:T(8,128)S(1)} %get-tuple-element.119.other) | copy-start | bytes 983044
  55.3 6.4 %collective-permute-start.12 = (bf16[64,1280]{1,0:T(8,128)(2,1)S(1)}, bf16[64,1280]{1,0:T(8,128)(2,1)S(1)}, u32[]{:S(2)}, u32[]{:S(2)}) collective-permute-start(bf16[64,1280]{1,0:T(8,128)(2,1)S(1)} %get-tuple-element.100), channel_id=1, source_target_pairs={{0,4},{4,0},{8,12},{12,8},{16,20},{20,16},{24,28},{28,24},{1,5},{5... | collective-permute-start | bytes 491528 | tf_op jit(solution)/shard_map/ppermute | solution.py:349
  56.9 8.7 %collective-permute-start.9 = (bf16[128,1024]{1,0:T(8,128)(2,1)}, bf16[128,1024]{1,0:T(8,128)(2,1)S(1)}, u32[]{:S(2)}, u32[]{:S(2)}) collective-permute-start(bf16[128,1024]{1,0:T(8,128)(2,1)} %get-tuple-element.94), channel_id=1, source_target_pairs={{0,1},{1,0},{2,3},{3,2},{4,5},{5,4},{6,7},{7,6},{8,9},{9,8},{10,11... | collective-permute-start | bytes 786440 | tf_op jit(solution)/shard_map/ppermute | solution.py:343
  56.9 8.7 %collective-permute-start.10 = (bf16[128,1024]{1,0:T(8,128)(2,1)S(1)}, bf16[128,1024]{1,0:T(8,128)(2,1)S(1)}, u32[]{:S(2)}, u32[]{:S(2)}) collective-permute-start(bf16[128,1024]{1,0:T(8,128)(2,1)S(1)} %join.4), channel_id=1, source_target_pairs={{0,2},{1,3},{2,0},{3,1},{4,6},{5,7},{6,4},{7,5},{8,10},{9,11},{10,... | collective-permute-start | bytes 786440 | tf_op jit(solution)/shard_map/ppermute | solution.py:346
  62.4 5.5 %collective-permute-start.14 = (bf16[64,1280]{1,0:T(8,128)(2,1)S(1)}, bf16[64,1280]{1,0:T(8,128)(2,1)S(1)}, u32[]{:S(2)}, u32[]{:S(2)}) collective-permute-start(bf16[64,1280]{1,0:T(8,128)(2,1)S(1)} %get-tuple-element.127), channel_id=1, source_target_pairs={{0,8},{4,12},{8,0},{12,4},{16,24},{20,28},{24,16},{28,20},{1,9},{5... | collective-permute-start | bytes 491528 | tf_op jit(solution)/shard_map/ppermute | solution.py:410
  64.0 12.4 %collective-permute-start.4 = (bf16[128,768]{1,0:T(8,128)(2,1)}, bf16[128,768]{1,0:T(8,128)(2,1)}, u32[]{:S(2)}, u32[]{:S(2)}) collective-permute-start(bf16[128,768]{1,0:T(8,128)(2,1)} %copy-done.13), channel_id=1, source_target_pairs={{0,1},{1,0},{2,3},{3,2},{4,5},{5,4},{6,7},{7,6},{8,9},{9,8},{10,11... | collective-permute-start | bytes 589832 | tf_op jit(solution)/shard_map/ppermute | solution.py:343
  64.0 12.4 %collective-permute-start.8 = (bf16[128,768]{1,0:T(8,128)(2,1)}, bf16[128,768]{1,0:T(8,128)(2,1)}, u32[]{:S(2)}, u32[]{:S(2)}) collective-permute-start(bf16[128,768]{1,0:T(8,128)(2,1)} %copy-done.9), channel_id=1, source_target_pairs={{0,2},{1,3},{2,0},{3,1},{4,6},{5,7},{6,4},{7,5},{8,10},{9,11},{10,... | collective-permute-start | bytes 589832 | tf_op jit(solution)/shard_map/ppermute | solution.py:346
  65.7 0.7 copy-start.5
  66.4 5.1 %collective-permute-start.13 = (bf16[64,1024]{1,0:T(8,128)(2,1)S(1)}, bf16[64,1024]{1,0:T(8,128)(2,1)S(1)}, u32[]{:S(2)}, u32[]{:S(2)}) collective-permute-start(bf16[64,1024]{1,0:T(8,128)(2,1)S(1)} %get-tuple-element.104), channel_id=1, source_target_pairs={{0,4},{4,0},{8,12},{12,8},{16,20},{20,16},{24,28},{28,24},{1,5},{5... | collective-permute-start | bytes 393224 | tf_op jit(solution)/shard_map/ppermute | solution.py:349
  68.0 29.7 %copy-start.1 = (f32[128,3072]{1,0:T(8,128)S(1)}, f32[128,3072]{1,0:T(8,128)}, u32[]{:S(2)}) copy-start(f32[128,3072]{1,0:T(8,128)} %x_start.5) | copy-start | bytes 4718596
  68.0 29.7 %copy-start.4 = (f32[64,1280]{1,0:T(8,128)S(1)}, f32[64,1280]{1,0:T(8,128)}, u32[]{:S(2)}) copy-start(f32[64,1280]{1,0:T(8,128)} %copy-done.3) | copy-start | bytes 983044
  72.2 9.0 %collective-permute-start.16 = (bf16[64,1024]{1,0:T(8,128)(2,1)}, bf16[64,1024]{1,0:T(8,128)(2,1)}, u32[]{:S(2)}, u32[]{:S(2)}) collective-permute-start(bf16[64,1024]{1,0:T(8,128)(2,1)} %fusion.4), channel_id=1, source_target_pairs={{0,8},{4,12},{8,0},{12,4},{16,24},{20,28},{24,16},{28,20},{1,9},{5... | collective-permute-start | bytes 393224 | tf_op jit(solution)/shard_map/ppermute | solution.py:410
  73.8 5.7 %collective-permute-start.17 = (bf16[32,1280]{1,0:T(8,128)(2,1)}, bf16[32,1280]{1,0:T(8,128)(2,1)}, u32[]{:S(2)}, u32[]{:S(2)}) collective-permute-start(bf16[32,1280]{1,0:T(8,128)(2,1)} %fusion.5), channel_id=1, source_target_pairs={{0,16},{4,20},{8,24},{12,28},{16,0},{20,4},{24,8},{28,12},{1,17},{... | collective-permute-start | bytes 245768 | tf_op jit(solution)/shard_map/ppermute | solution.py:410
  77.5 6.3 %collective-permute-start.15 = (bf16[64,768]{1,0:T(8,128)(2,1)S(1)}, bf16[64,768]{1,0:T(8,128)(2,1)S(1)}, u32[]{:S(2)}, u32[]{:S(2)}) collective-permute-start(bf16[64,768]{1,0:T(8,128)(2,1)S(1)} %get-tuple-element.109), channel_id=1, source_target_pairs={{0,4},{4,0},{8,12},{12,8},{16,20},{20,16},{24,28},{28,24},{1,5},{5... | collective-permute-start | bytes 294920 | tf_op jit(solution)/shard_map/ppermute | solution.py:349
  79.5 6.7 %collective-permute-start.19 = (bf16[32,1280]{1,0:T(8,128)(2,1)}, bf16[32,1280]{1,0:T(8,128)(2,1)S(1)}, u32[]{:S(2)}, u32[]{:S(2)}) collective-permute-start(bf16[32,1280]{1,0:T(8,128)(2,1)} %collective-permute-done.17), channel_id=1, source_target_pairs={{0,8},{4,12},{8,0},{12,4},{16,24},{20,28},{24,16},{28,20},{1,9},{5... | collective-permute-start | bytes 245768 | tf_op jit(solution)/shard_map/ppermute | solution.py:410
  82.2 8.4 %collective-permute-start.22 = (bf16[64,1024]{1,0:T(8,128)(2,1)S(1)}, bf16[64,1024]{1,0:T(8,128)(2,1)S(1)}, u32[]{:S(2)}, u32[]{:S(2)}) collective-permute-start(bf16[64,1024]{1,0:T(8,128)(2,1)S(1)} %fusion), channel_id=1, source_target_pairs={{0,16},{4,20},{8,24},{12,28},{16,0},{20,4},{24,8},{28,12},{1,17},{... | collective-permute-start | bytes 393224 | tf_op jit(solution)/shard_map/ppermute | solution.py:410
  83.9 4.7 %collective-permute-start.18 = (bf16[64,768]{1,0:T(8,128)(2,1)S(1)}, bf16[64,768]{1,0:T(8,128)(2,1)S(1)}, u32[]{:S(2)}, u32[]{:S(2)}) collective-permute-start(bf16[64,768]{1,0:T(8,128)(2,1)S(1)} %fusion.6), channel_id=1, source_target_pairs={{0,8},{4,12},{8,0},{12,4},{16,24},{20,28},{24,16},{28,20},{1,9},{5... | collective-permute-start | bytes 294920 | tf_op jit(solution)/shard_map/ppermute | solution.py:410
  87.2 10.5 %collective-permute-start.24 = (bf16[64,1280]{1,0:T(8,128)(2,1)S(1)}, bf16[64,1280]{1,0:T(8,128)(2,1)S(1)}, u32[]{:S(2)}, u32[]{:S(2)}) collective-permute-start(bf16[64,1280]{1,0:T(8,128)(2,1)S(1)} %get-tuple-element.125), channel_id=1, source_target_pairs={{0,4},{4,0},{8,12},{12,8},{16,20},{20,16},{24,28},{28,24},{1,5},{5... | collective-permute-start | bytes 491528 | tf_op jit(solution)/shard_map/ppermute | solution.py:349
  88.6 10.1 %copy-start.6 = (f32[64,1024]{1,0:T(8,128)S(1)}, f32[64,1024]{1,0:T(8,128)}, u32[]{:S(2)}) copy-start(f32[64,1024]{1,0:T(8,128)} %copy-done.5) | copy-start | bytes 786436
  88.6 6.6 %collective-permute-start.20 = (bf16[64,768]{1,0:T(8,128)(2,1)S(1)}, bf16[64,768]{1,0:T(8,128)(2,1)S(1)}, u32[]{:S(2)}, u32[]{:S(2)}) collective-permute-start(bf16[64,768]{1,0:T(8,128)(2,1)S(1)} %fusion.3), channel_id=1, source_target_pairs={{0,16},{4,20},{8,24},{12,28},{16,0},{20,4},{24,8},{28,12},{1,17},{... | collective-permute-start | bytes 294920 | tf_op jit(solution)/shard_map/ppermute | solution.py:410
  91.6 7.0 %collective-permute-start.23 = (bf16[64,1024]{1,0:T(8,128)(2,1)S(1)}, bf16[64,1024]{1,0:T(8,128)(2,1)S(1)}, u32[]{:S(2)}, u32[]{:S(2)}) collective-permute-start(bf16[64,1024]{1,0:T(8,128)(2,1)S(1)} %get-tuple-element.121), channel_id=1, source_target_pairs={{0,4},{4,0},{8,12},{12,8},{16,20},{20,16},{24,28},{28,24},{1,5},{5... | collective-permute-start | bytes 393224 | tf_op jit(solution)/shard_map/ppermute | solution.py:349
  95.3 5.0 %collective-permute-start.21 = (bf16[64,768]{1,0:T(8,128)(2,1)S(1)}, bf16[64,768]{1,0:T(8,128)(2,1)S(1)}, u32[]{:S(2)}, u32[]{:S(2)}) collective-permute-start(bf16[64,768]{1,0:T(8,128)(2,1)S(1)} %get-tuple-element.123), channel_id=1, source_target_pairs={{0,4},{4,0},{8,12},{12,8},{16,20},{20,16},{24,28},{28,24},{1,5},{5... | collective-permute-start | bytes 294920 | tf_op jit(solution)/shard_map/ppermute | solution.py:349

commit v11 on v7

--- a/solution.py
+++ b/solution.py
@@ -297,33 +297,44 @@
     )(parity, keep, sent, sg, *fetched)
 
 
-def finish_kernel(first, parity, x_start, earlier, kept, fetched, other, back, *refs):
-    out, result, sem = refs[-3:]
-    half, count = kept.shape
-    cols = slice(first, first + count)
+def finish_kernel(firsts, parity, x_start, *refs):
+    n = len(firsts)
+    given, rest = refs[: 5 * n], refs[-2 - n :]
+    out, results, sem = rest[0], rest[1 : 1 + n], rest[1 + n]
     p = parity[0]
-    mine = pl.ds(pl.multiple_of(p * half, half), half)
-    rest = pl.ds(pl.multiple_of((1 - p) * half, half), half)
     odd = p.astype(f32)
-    result[mine, :] = x_start[mine, cols] + earlier[...] + kept[...] + odd * fetched[...].astype(f32)
-    result[rest, :] = x_start[rest, cols] + other[...] + back[...].astype(f32)
-    copy = pltpu.make_async_copy(result, out.at[0, :, pl.ds(first, count)], sem)
-    copy.start()
-    copy.wait()
-
-
-def finish_call(parity, x_start, earlier, kept, fetched, other, back, into, first):
+    copies = []
+    for i, first in enumerate(firsts):
+        earlier, kept, fetched, other, back = given[5 * i : 5 * i + 5]
+        half, count = kept.shape
+        cols = slice(first, first + count)
+        mine = pl.ds(pl.multiple_of(p * half, half), half)
+        rest = pl.ds(pl.multiple_of((1 - p) * half, half), half)
+        results[i][mine, :] = (
+            x_start[mine, cols] + earlier[...] + kept[...] + odd * fetched[...].astype(f32)
+        )
+        results[i][rest, :] = x_start[rest, cols] + other[...] + back[...].astype(f32)
+        copies.append(
+            pltpu.make_async_copy(results[i], out.at[0, :, pl.ds(first, count)], sem.at[i])
+        )
+        copies[i].start()
+    for copy in copies:
+        copy.wait()
+
+
+def finish_call(parity, x_start, groups, firsts, into):
     rows, width = x_start.shape
     vm = pl.BlockSpec(memory_space=VM)
     smem = pl.BlockSpec(memory_space=pltpu.SMEM)
     hbm = pl.BlockSpec(memory_space=pltpu.HBM)
-    given = [parity, x_start, earlier, kept, fetched, other, back]
+    given = [parity, x_start] + [one for group in groups for one in group]
     return pl.pallas_call(
-        functools.partial(finish_kernel, first),
-        in_specs=[smem] + [vm] * 6 + [hbm] * len(into),
+        functools.partial(finish_kernel, firsts),
+        in_specs=[smem] + [vm] * (len(given) - 1) + [hbm] * len(into),
         out_specs=hbm,
         out_shape=jax.ShapeDtypeStruct((1, rows, width), f32),
-        scratch_shapes=[VM((rows, kept.shape[1]), f32), pltpu.SemaphoreType.DMA],
+        scratch_shapes=[VM((rows, group[1].shape[1]), f32) for group in groups]
+        + [pltpu.SemaphoreType.DMA((len(groups),))],
         input_output_aliases={len(given): 0} if into else {},
         compiler_params=params(6),
         name="finish",
@@ -477,8 +488,13 @@
 
         def finish(fetched):
             given = [held[name] for name in ("earlier", "kept", "fetched", "other")]
-            into = list(written)
-            written[:] = [finish_call(which, x_start, *given, fetched[0], into, firsts[c])]
+            stash.append((firsts[c], given + [fetched[0]]))
+            if len(stash) in (1, chunks):
+                mine = stash[len(stash) - 1 :] if len(stash) == 1 else stash[1:]
+                places = [place for place, _ in mine]
+                groups_in = [group for _, group in mine]
+                into = list(written)
+                written[:] = [finish_call(which, x_start, groups_in, places, into)]
 
         stages = [(drift_of, to_pair, "x", 0.5), (pair_sum, swap(1), "z1", 0.5)]
         for r in range(len(spans)):
@@ -493,10 +509,10 @@
         stages.append((finish, None, "", 0.0))
         return stages
 
-    plan = [prefix_stages(c, c < chunks - 1) for c in range(chunks)]
+    plan = [prefix_stages(c, False) for c in range(chunks)]
     inbox = [[got[j][c] for j in range(chips - 1)] for c in range(chunks)]
     shares = [18.5 * n / width for n in counts]
-    ends = [2.0 + sum(shares[: c + 1]) for c in range(chunks)]
+    ends = [2.0 * (c + 1) + sum(shares[: c + 1]) for c in range(chunks)]
     waits = [(end, c, 0) for c, end in enumerate(ends)]
     free = {"x": 0.0, "z1": 0.0, "z2": 0.0, "": 0.0}
     turns = []
@@ -506,10 +522,10 @@
         turns.append((c, i))
         if i + 1 < len(plan[c]):
             link, load = plan[c][i][2:]
-            begin = max(when + 2.0, free[link])
+            begin = max(when + 1.5, free[link])
             free[link] = begin + load * shares[c]
             waits.append((free[link] + 0.7, c, i + 1))
-    written = []
+    written, stash = [], []
     last = None
     for c, i in turns:
         compute, move = plan[c][i][:2]

time: 93.6 us -> 95.8 us (1.024)
  other arithmetic: 0.46 us -> 4.51 us
  starting transfers between devices: 32.2 us -> 28.6 us
  local copies, waits for them, and re-layouts: 1.18 us -> 4.27 us
  Pallas kernels: 36.2 us -> 35 us
    ppermute x8 -> x6, starting transfers between devices: 16.1 us -> 11.6 us  [along(): lax.ppermute(x, 'step', [(2 * a + i, 2 * b + i) for a, b in pairs for i i...]
    unnamed x20 -> x34, local copies, waits for them, and re-layouts: 1.18 us -> 4.27 us
    ppermute x6, waiting for transfers between devices: 4.16 us -> 7.07 us  [to_pair(): return lax.ppermute(x, 'step', [(i, i ^ 1) for i in range(n_step)])]
    ppermute x4, waiting for transfers between devices: 9.97 us -> 7.66 us  [to_chip(): lax.ppermute(x, 'seq', [(i, (i + 2 * offset) % n_seq) for i in range(n_se...]
    convert_element_type x3, other arithmetic: 0.23 us -> 2.04 us  [collect(): return (held['earlier'] + even * held['kept']).astype(bf16)]
    ppermute x8 -> x6, waiting for transfers between devices: 4.75 us -> 3.01 us  [along(): lax.ppermute(x, 'step', [(2 * a + i, 2 * b + i) for a, b in pairs for i i...]
    convert_element_type x3, other arithmetic: 0.1 us -> 1.73 us  [collect(): total = held['total'].astype(bf16)]
    pallas_call x3 -> x2, Pallas kernels: 2.69 us -> 2 us  [finish_call(): pl.pallas_call(functools.partial(finish_kernel, firsts), in_specs=[smem]...]
  transfers between devices with their start and end apart: 26 -> 24, of which waited for: 10 -> 12; matrix products, arithmetic and copies ran while one was open for 0% -> 5% of each run, Pallas kernels for 24% -> 22%
where the time goes in v11:
time: 95.8 us; the launch traced here: 95.2 us
  Pallas kernels  35 us (37%)
  starting transfers between devices  28.6 us (30%)
  waiting for transfers between devices  21.7 us (23%)
  other arithmetic  4.51 us (5%)
  local copies, waits for them, and re-layouts  4.27 us (4%)
  between operations  1.09 us (1%)
    pallas_call x2, Pallas kernels, project_call(): pl.pallas_call(functools.partial(project_kernel, tile, load, tiles), in_s...  17.6 us
    ppermute x6, starting transfers between devices, along(): lax.ppermute(x, 'step', [(2 * a + i, 2 * b + i) for a, b in pairs for i i...  11.6 us
    ppermute x6, starting transfers between devices, to_pair(): return lax.ppermute(x, 'step', [(i, i ^ 1) for i in range(n_step)])  8.19 us
    ppermute x4, waiting for transfers between devices, to_chip(): lax.ppermute(x, 'seq', [(i, (i + 2 * offset) % n_seq) for i in range(n_se...  7.66 us
    ppermute x4, starting transfers between devices, to_chip(): lax.ppermute(x, 'seq', [(i, (i + 2 * offset) % n_seq) for i in range(n_se...  7.47 us
    ppermute x6, waiting for transfers between devices, to_pair(): return lax.ppermute(x, 'step', [(i, i ^ 1) for i in range(n_step)])  7.07 us
    pallas_call x2, Pallas kernels, out_call(): pl.pallas_call(functools.partial(out_kernel, plan), in_specs=[vm] * len(g...  5.01 us
    unnamed x34, local copies, waits for them, and re-layouts  4.27 us
  transfers between devices with their start and end apart: 24, of which 12 were waited for; matrix products, arithmetic and copies ran while one was open for 5% of the time, Pallas kernels for 22%

profile of v11, /device:TPU:0, one launch (start us, length us, event | category | flops | bytes accessed | tf_op | source)
XLA Modules:
  0.0 95.2 jit_solution(17018904848916764445)
XLA Ops:
  0.7 3.7 %norm.1 = (bf16[128,3072]{1,0:T(8,128)(2,1)}, f32[1,3072]{1,0:T(1,128)}) custom-call(s32[1]{0:T(128)S(6)} %copy.14.t_ref, f32[50]{0:T(128)} %size_ref.1, f32[1,128,3072]{2,1,0:T(8,128)} %x_hbm.1, f32[50,9216]{1,0:T(8,128)} %mod_hbm.1), custom_call_target="tpu_custom_call" | custom-call | flops 3932160 | tf_op jit(solution)/shard_map/norm/pallas_call | solution.py:56
  4.4 0.5 collective-permute-start.1
  4.9 2.6 %collective-permute-start = (bf16[128,3072]{1,0:T(8,128)(2,1)}, bf16[128,3072]{1,0:T(8,128)(2,1)S(1)}, u32[]{:S(2)}, u32[]{:S(2)}) collective-permute-start(bf16[128,3072]{1,0:T(8,128)(2,1)} %get-tuple-element.75.m0), channel_id=1, source_target_pairs={{0,2},{1,3},{2,0},{3,1},{4,6},{5,7},{6,4},{7,5},{8,10},{9,11},{10,... | collective-permute-start | bytes 2359304 | tf_op jit(solution)/shard_map/ppermute | solution.py:374
  7.5 0.0 copy-start.2
  7.5 1.1 %copy-done.2 = bf16[128,3072]{1,0:T(8,128)(2,1)S(1)} copy-done((bf16[128,3072]{1,0:T(8,128)(2,1)S(1)}, bf16[128,3072]{1,0:T(8,128)(2,1)}, u32[]{:S(2)}) %copy-start.2) | copy-done | bytes 786456
  8.7 12.4 %project.2 = (bf16[256,512]{1,0:T(8,128)(2,1)S(1)}, bf16[256,512]{1,0:T(8,128)(2,1)S(1)}, bf16[256,512]{1,0:T(8,128)(2,1)S(1)}, bf16[256,1536]{1,0:T(8,128)(2,1)...) custom-call(bf16[128,3072]{1,0:T(8,128)(2,1)S(1)} %copy-done.2, ...), custom_call_target="tpu_custom_call" | custom-call | flops 4831838208 | tf_op jit(solution)/shard_map/project/pallas_call | solution.py:151
  21.1 4.8 %collective-permute-done.m0 = bf16[128,3072]{1,0:T(8,128)(2,1)S(1)} collective-permute-done((bf16[128,3072]{1,0:T(8,128)(2,1)}, bf16[128,3072]{1,0:T(8,128)(2,1)S(1)}, u32[]{:S(2)}, u32[]{:S(2)}) %collective-permute-start) | collective-permute-done | bytes 786464 | tf_op jit(solution)/shard_map/ppermute | solution.py:374
  25.9 2.3 %collective-permute-done.2.m1 = bf16[128,3072]{1,0:T(8,128)(2,1)S(1)} collective-permute-done((bf16[128,3072]{1,0:T(8,128)(2,1)S(1)}, bf16[128,3072]{1,0:T(8,128)(2,1)S(1)}, u32[]{:S(2)}, u32[]{:S(2)}) %collective-permute-start.2) | collective-permute-done | bytes 786464 | tf_op jit(solution)/shard_map/ppermute | solution.py:371
  28.2 5.2 %project.3 = (bf16[256,512]{1,0:T(8,128)(2,1)S(1)}, bf16[256,512]{1,0:T(8,128)(2,1)S(1)}, bf16[256,512]{1,0:T(8,128)(2,1)S(1)}, bf16[256,1536]{1,0:T(8,128)(2,1)S(1)}) custom-call(bf16[128,3072]{1,0:T(8,128)(2,1)S(1)} %collective-permute-done.m0, bf16[128,3072]{1,0:T(8,128)(2,1)S(1)} %collective-permute-done.2.m1, f32[1,128]{1,0:T(1,128)S(1)} %bitcast.6, ...), custom_call_target="tpu_custom_call" | custom-call | flops 4831838208 | tf_op jit(solution)/shard_map/project/pallas_call | solution.py:151
  33.4 1.9 %attend.2.refs_0_.refs_4_ = bf16[256,512]{1,0:T(8,128)(2,1)S(1)} custom-call(bf16[256,512]{1,0:T(8,128)(2,1)S(1)} %get-tuple-element.85.refs_0_, bf16[256,512]{1,0:T(8,128)(2,1)S(1)} %get-tuple-element.86.refs_1_, bf16[256,512]{1,0:T(8,128)(2,1)S(1)} %get-tuple-element.87.refs_2_, bf16[256,512]{1,0:T(8,128)(2,1)S(1)} %get-tuple-element.88.refs_3_, ...), custom_call_target="tpu_custom_call" | custom-call | flops 805306368 | tf_op jit(solution)/shard_map/attend/pallas_call | solution.py:191
  35.3 1.5 %project_out.2 = (f32[128,1280]{1,0:T(8,128)S(1)}, bf16[128,1280]{1,0:T(8,128)(2,1)S(1)}) custom-call(bf16[256,512]{1,0:T(8,128)(2,1)S(1)} %attend.2.refs_0_.refs_4_, bf16[256,1536]{1,0:T(8,128)(2,1)S(1)} %get-tuple-element.100.refs_1_.refs_5_, bf16[512,3072]{1,0:T(8,128)(2,1)S(1)} %copy-done, bf16[1536,3072]{1,0:T(8,128)(2,1)S(1)} %bitcast.4), custom_call_target="tpu_custom_call" | custom-call | flops 1342177280 | tf_op jit(solution)/shard_map/project_out/pallas_call | solution.py:235
  36.9 0.2 collective-permute-start.3
  37.1 1.7 %attend.3.refs_8_.refs_12_.refs_16_ = bf16[256,512]{1,0:T(8,128)(2,1)S(1)} custom-call(bf16[256,512]{1,0:T(8,128)(2,1)S(1)} %get-tuple-element.94.refs_0_, bf16[256,512]{1,0:T(8,128)(2,1)S(1)} %get-tuple-element.86.refs_1_, bf16[256,512]{1,0:T(8,128)(2,1)S(1)} %get-tuple-element.87.refs_2_, bf16[256,512]{1,0:T(8,128)(2,1)S(1)} %get-tuple-element.88.refs_3_, ...), custom_call_target="tpu_custom_call" | custom-call | flops 805306368 | tf_op jit(solution)/shard_map/attend/pallas_call | solution.py:191
  38.8 0.1 join.3
  38.8 1.9 %collective-permute-start.4 = (bf16[128,1280]{1,0:T(8,128)(2,1)S(1)}, bf16[128,1280]{1,0:T(8,128)(2,1)S(1)}, u32[]{:S(2)}, u32[]{:S(2)}) collective-permute-start(bf16[128,1280]{1,0:T(8,128)(2,1)S(1)} %join.3), channel_id=1, source_target_pairs={{0,2},{1,3},{2,0},{3,1},{4,6},{5,7},{6,4},{7,5},{8,10},{9,11},{10,... | collective-permute-start | bytes 983048 | tf_op jit(solution)/shard_map/ppermute | solution.py:374
  40.7 3.5 %project_out.3 = (f32[128,1024]{1,0:T(8,128)S(1)}, bf16[128,1024]{1,0:T(8,128)(2,1)}, f32[128,768]{1,0:T(8,128)S(1)}, bf16[128,768]{1,0:T(8,128)(2,1)S(1)}, f32[...) custom-call(bf16[256,512]{1,0:T(8,128)(2,1)S(1)} %attend.2.refs_0_.r, ...), custom_call_target="tpu_custom_call" | custom-call | flops 2684354560 | tf_op jit(solution)/shard_map/project_out/pallas_call | solution.py:235
  44.2 0.1 collective-permute-start.8
  44.3 0.6 copy-done.10
  44.9 0.1 copy-done.11
  44.9 0.1 collective-permute-start.5
  45.0 1.7 %collective-permute-done.5.sent = bf16[128,1024]{1,0:T(8,128)(2,1)S(1)} collective-permute-done((bf16[128,1024]{1,0:T(8,128)(2,1)}, bf16[128,1024]{1,0:T(8,128)(2,1)S(1)}, u32[]{:S(2)}, u32[]{:S(2)}) %collective-permute-start.5) | collective-permute-done | bytes 262176 | tf_op jit(solution)/shard_map/ppermute | solution.py:371
  46.7 2.2 %collective-permute-done.4.refs_0_ = bf16[128,1280]{1,0:T(8,128)(2,1)S(1)} collective-permute-done((bf16[128,1280]{1,0:T(8,128)(2,1)S(1)}, bf16[128,1280]{1,0:T(8,128)(2,1)S(1)}, u32[]{:S(2)}, u32[]{:S(2)}) %collective-permute-start.4) | collective-permute-done | bytes 327712 | tf_op jit(solution)/shard_map/ppermute | solution.py:374
  49.0 0.7 copy-done.5
  49.7 1.0 %copy-done.6 = bf16[128,1280]{1,0:T(8,128)(2,1)S(1)} copy-done((bf16[128,1280]{1,0:T(8,128)(2,1)S(1)}, bf16[128,1280]{1,0:T(8,128)(2,1)}, u32[]{:S(2)}) %copy-start.6) | copy-done | bytes 327704
  50.6 1.1 %drift.3 = (f32[64,1280]{1,0:T(8,128)S(1)}, f32[64,1280]{1,0:T(8,128)S(1)}, bf16[64,1280]{1,0:T(8,128)(2,1)S(1)}) custom-call(s32[1]{0:T(128)} %bitcast.parity, f32[128,1280]{1,0:T(8,128)S(1)} %get-tuple-element.117.keep, bf16[128,1280]{1,0:T(8,128)(2,1)} %collective-permute-done.8.sent, f32[1,3072]{1,0:T(1,128)S(1)} %copy-done.7, ...), custom_call_target="tpu_custom_call" | custom-call | tf_op jit(solution)/shard_map/drift/pallas_call | solution.py:286
  51.7 0.0 copy-start.3
  51.8 0.7 copy-done.3
  52.5 1.7 %collective-permute-start.9 = (bf16[64,1280]{1,0:T(8,128)(2,1)S(1)}, bf16[64,1280]{1,0:T(8,128)(2,1)S(1)}, u32[]{:S(2)}, u32[]{:S(2)}) collective-permute-start(bf16[64,1280]{1,0:T(8,128)(2,1)S(1)} %get-tuple-element.121), channel_id=1, source_target_pairs={{0,4},{4,0},{8,12},{12,8},{16,20},{20,16},{24,28},{28,24},{1,5},{5... | collective-permute-start | bytes 491528 | tf_op jit(solution)/shard_map/ppermute | solution.py:377
  54.2 0.5 collective-permute-start.6
  54.7 1.5 %collective-permute-start.7 = (bf16[128,1024]{1,0:T(8,128)(2,1)S(1)}, bf16[128,1024]{1,0:T(8,128)(2,1)S(1)}, u32[]{:S(2)}, u32[]{:S(2)}) collective-permute-start(bf16[128,1024]{1,0:T(8,128)(2,1)S(1)} %join.4), channel_id=1, source_target_pairs={{0,2},{1,3},{2,0},{3,1},{4,6},{5,7},{6,4},{7,5},{8,10},{9,11},{10,... | collective-permute-start | bytes 786440 | tf_op jit(solution)/shard_map/ppermute | solution.py:374
  56.2 1.9 %collective-permute-done.9.refs_2_ = bf16[64,1280]{1,0:T(8,128)(2,1)S(1)} collective-permute-done((bf16[64,1280]{1,0:T(8,128)(2,1)S(1)}, bf16[64,1280]{1,0:T(8,128)(2,1)S(1)}, u32[]{:S(2)}, u32[]{:S(2)}) %collective-permute-start.9) | collective-permute-done | bytes 163872 | tf_op jit(solution)/shard_map/ppermute | solution.py:377
  58.2 1.8 %collective-permute-start.11 = (bf16[64,1280]{1,0:T(8,128)(2,1)S(1)}, bf16[64,1280]{1,0:T(8,128)(2,1)S(1)}, u32[]{:S(2)}, u32[]{:S(2)}) collective-permute-start(bf16[64,1280]{1,0:T(8,128)(2,1)S(1)} %fusion.4), channel_id=1, source_target_pairs={{0,8},{4,12},{8,0},{12,4},{16,24},{20,28},{24,16},{28,20},{1,9},{5... | collective-permute-start | bytes 491528 | tf_op jit(solution)/shard_map/ppermute | solution.py:442
  60.0 0.7 join.5
  60.8 1.5 %collective-permute-start.15 = (bf16[128,768]{1,0:T(8,128)(2,1)}, bf16[128,768]{1,0:T(8,128)(2,1)}, u32[]{:S(2)}, u32[]{:S(2)}) collective-permute-start(bf16[128,768]{1,0:T(8,128)(2,1)} %join.5), channel_id=1, source_target_pairs={{0,2},{1,3},{2,0},{3,1},{4,6},{5,7},{6,4},{7,5},{8,10},{9,11},{10,... | collective-permute-start | bytes 589832 | tf_op jit(solution)/shard_map/ppermute | solution.py:374
  62.3 0.6 collective-permute-done.7.refs_0_
  62.9 0.1 drift.4
  63.0 0.0 copy-start.1
  63.1 0.0 copy-start.4
  63.1 0.9 collective-permute-start.10
  64.0 0.7 fusion
  64.7 3.4 %collective-permute-done.10.refs_2_ = bf16[64,1024]{1,0:T(8,128)(2,1)S(1)} collective-permute-done((bf16[64,1024]{1,0:T(8,128)(2,1)S(1)}, bf16[64,1024]{1,0:T(8,128)(2,1)S(1)}, u32[]{:S(2)}, u32[]{:S(2)}) %collective-permute-start.10) | collective-permute-done | bytes 131104 | tf_op jit(solution)/shard_map/ppermute | solution.py:377
  68.1 0.7 fusion.7
  68.8 1.6 %collective-permute-start.12 = (bf16[64,1024]{1,0:T(8,128)(2,1)}, bf16[64,1024]{1,0:T(8,128)(2,1)}, u32[]{:S(2)}, u32[]{:S(2)}) collective-permute-start(bf16[64,1024]{1,0:T(8,128)(2,1)} %fusion.7), channel_id=1, source_target_pairs={{0,8},{4,12},{8,0},{12,4},{16,24},{20,28},{24,16},{28,20},{1,9},{5... | collective-permute-start | bytes 393224 | tf_op jit(solution)/shard_map/ppermute | solution.py:442
  70.5 2.5 %collective-permute-start.20 = (bf16[64,1280]{1,0:T(8,128)(2,1)}, bf16[64,1280]{1,0:T(8,128)(2,1)S(1)}, u32[]{:S(2)}, u32[]{:S(2)}) collective-permute-start(bf16[64,1280]{1,0:T(8,128)(2,1)} %fusion), channel_id=1, source_target_pairs={{0,16},{4,20},{8,24},{12,28},{16,0},{20,4},{24,8},{28,12},{1,17},{... | collective-permute-start | bytes 491528 | tf_op jit(solution)/shard_map/ppermute | solution.py:442
  73.0 1.1 %drift.5 = (f32[64,768]{1,0:T(8,128)S(1)}, f32[64,768]{1,0:T(8,128)S(1)}, bf16[64,768]{1,0:T(8,128)(2,1)S(1)}) custom-call(s32[1]{0:T(128)} %bitcast.parity, f32[128,768]{1,0:T(8,128)S(1)} %get-tuple-element.128.keep, bf16[128,768]{1,0:T(8,128)(2,1)} %collective-permute-done.13.sent, f32[1,3072]{1,0:T(1,128)S(1)} %copy-done.7, ...), custom_call_target="tpu_custom_call" | custom-call | tf_op jit(solution)/shard_map/drift/pallas_call | solution.py:286
  74.1 0.6 collective-permute-start.18
  74.7 1.0 %collective-permute-done.12 = bf16[64,1024]{1,0:T(8,128)(2,1)} collective-permute-done((bf16[64,1024]{1,0:T(8,128)(2,1)}, bf16[64,1024]{1,0:T(8,128)(2,1)}, u32[]{:S(2)}, u32[]{:S(2)}) %collective-permute-start.12) | collective-permute-done | bytes 131104 | tf_op jit(solution)/shard_map/ppermute | solution.py:442
  75.7 0.9 fusion.3
  76.6 2.1 %collective-permute-start.16 = (bf16[64,1024]{1,0:T(8,128)(2,1)S(1)}, bf16[64,1024]{1,0:T(8,128)(2,1)S(1)}, u32[]{:S(2)}, u32[]{:S(2)}) collective-permute-start(bf16[64,1024]{1,0:T(8,128)(2,1)S(1)} %fusion.3), channel_id=1, source_target_pairs={{0,16},{4,20},{8,24},{12,28},{16,0},{20,4},{24,8},{28,12},{1,17},{... | collective-permute-start | bytes 393224 | tf_op jit(solution)/shard_map/ppermute | solution.py:442
  78.7 0.0 collective-permute-done.18.refs_7_
  78.8 1.9 %collective-permute-start.19 = (bf16[64,768]{1,0:T(8,128)(2,1)S(1)}, bf16[64,768]{1,0:T(8,128)(2,1)S(1)}, u32[]{:S(2)}, u32[]{:S(2)}) collective-permute-start(bf16[64,768]{1,0:T(8,128)(2,1)S(1)} %fusion.8), channel_id=1, source_target_pairs={{0,8},{4,12},{8,0},{12,4},{16,24},{20,28},{24,16},{28,20},{1,9},{5... | collective-permute-start | bytes 294920 | tf_op jit(solution)/shard_map/ppermute | solution.py:442
  80.6 0.5 collective-permute-done.20
  81.2 1.0 %add_convert_fusion = (bf16[64,1280]{1,0:T(8,128)(2,1)S(1)}, f32[64,1280]{1,0:T(8,128)S(1)}) fusion(f32[64,1280]{1,0:T(8,128)S(1)} %get-tuple-element.120.refs_1_, f32[]{:T(128)S(6)} %convert_element_type.78, bf16[64,1280]{1,0:T(8,128)(2,1)S(1)} %collective-permute-done.20, f32[]{:T(128)S(6)} %convert_element_type.75, bf16[64,1280]{1,0:T(8,128)(2,1)} %copy-done.13, ...), kind=kLoop, calls=%fused_computation.6 | loop fusion | flops 655360 | bytes 1146892 | tf_op jit(solution)/shard_map/convert_element_type | solution.py:478
  82.2 0.1 collective-permute-start.23
  82.3 1.3 %collective-permute-done.19 = bf16[64,768]{1,0:T(8,128)(2,1)S(1)} collective-permute-done((bf16[64,768]{1,0:T(8,128)(2,1)S(1)}, bf16[64,768]{1,0:T(8,128)(2,1)S(1)}, u32[]{:S(2)}, u32[]{:S(2)}) %collective-permute-start.19) | collective-permute-done | bytes 98336 | tf_op jit(solution)/shard_map/ppermute | solution.py:442
  83.6 1.6 %collective-permute-start.21 = (bf16[64,768]{1,0:T(8,128)(2,1)S(1)}, bf16[64,768]{1,0:T(8,128)(2,1)S(1)}, u32[]{:S(2)}, u32[]{:S(2)}) collective-permute-start(bf16[64,768]{1,0:T(8,128)(2,1)S(1)} %fusion.6), channel_id=1, source_target_pairs={{0,16},{4,20},{8,24},{12,28},{16,0},{20,4},{24,8},{28,12},{1,17},{... | collective-permute-start | bytes 294920 | tf_op jit(solution)/shard_map/ppermute | solution.py:442
  85.1 0.2 collective-permute-done.16
  85.4 1.0 %add_convert_fusion.1 = (bf16[64,1024]{1,0:T(8,128)(2,1)S(1)}, f32[64,1024]{1,0:T(8,128)S(1)}) fusion(f32[64,1024]{1,0:T(8,128)S(1)} %get-tuple-element.124.refs_1_, f32[]{:T(128)S(6)} %convert_element_type.78, bf16[64,1024]{1,0:T(8,128)(2,1)S(1)} %collective-permute-done.16, f32[]{:T(128)S(6)} %convert_element_type.75, ...), kind=kLoop, calls=%fused_computation.10 | loop fusion | flops 524288 | bytes 917516 | tf_op jit(solution)/shard_map/convert_element_type | solution.py:478
  86.4 2.9 %collective-permute-start.17 = (bf16[64,1024]{1,0:T(8,128)(2,1)S(1)}, bf16[64,1024]{1,0:T(8,128)(2,1)S(1)}, u32[]{:S(2)}, u32[]{:S(2)}) collective-permute-start(bf16[64,1024]{1,0:T(8,128)(2,1)S(1)} %get-tuple-element.149), channel_id=1, source_target_pairs={{0,4},{4,0},{8,12},{12,8},{16,20},{20,16},{24,28},{28,24},{1,5},{5... | collective-permute-start | bytes 393224 | tf_op jit(solution)/shard_map/ppermute | solution.py:377
  89.2 0.1 add_convert_fusion.2
  89.3 2.0 %collective-permute-start.22 = (bf16[64,768]{1,0:T(8,128)(2,1)S(1)}, bf16[64,768]{1,0:T(8,128)(2,1)S(1)}, u32[]{:S(2)}, u32[]{:S(2)}) collective-permute-start(bf16[64,768]{1,0:T(8,128)(2,1)S(1)} %get-tuple-element.145), channel_id=1, source_target_pairs={{0,4},{4,0},{8,12},{12,8},{16,20},{20,16},{24,28},{28,24},{1,5},{5... | collective-permute-start | bytes 294920 | tf_op jit(solution)/shard_map/ppermute | solution.py:377
  91.3 0.9 finish.2.refs_10_
  92.2 1.7 %collective-permute-done.22.refs_9_ = bf16[64,768]{1,0:T(8,128)(2,1)S(1)} collective-permute-done((bf16[64,768]{1,0:T(8,128)(2,1)S(1)}, bf16[64,768]{1,0:T(8,128)(2,1)S(1)}, u32[]{:S(2)}, u32[]{:S(2)}) %collective-permute-start.22) | collective-permute-done | bytes 98336 | tf_op jit(solution)/shard_map/ppermute | solution.py:377
  94.0 1.1 %finish.3 = f32[1,128,3072]{2,1,0:T(8,128)} custom-call(s32[1]{0:T(128)} %bitcast.parity, f32[128,3072]{1,0:T(8,128)S(1)} %copy-done.1, f32[64,1024]{1,0:T(8,128)S(1)} %get-tuple-element.150.refs_0_, f32[64,1024]{1,0:T(8,128)S(1)} %get-tuple-element.124.refs_1_, ...), custom_call_target="tpu_custom_call", output_to_operand_aliasing={{}: (12, {})} | custom-call | tf_op jit(solution)/shard_map/finish/pallas_call | solution.py:331
  (43 shorter events, 0.2 us)
Async XLA Ops:
  0.0 7.5 %copy-start.8 = (f32[128]{0:T(128)S(1)}, f32[128]{0:T(128)}, u32[]{:S(2)}) copy-start(f32[128]{0:T(128)} %param.16) | copy-start | bytes 1540
  0.0 7.5 %copy-start.9 = (f32[128]{0:T(128)S(1)}, f32[128]{0:T(128)}, u32[]{:S(2)}) copy-start(f32[128]{0:T(128)} %param.17) | copy-start | bytes 1540
  4.4 3.1 %collective-permute-start.1 = (bf16[128,3072]{1,0:T(8,128)(2,1)}, bf16[128,3072]{1,0:T(8,128)(2,1)S(1)}, u32[]{:S(2)}, u32[]{:S(2)}) collective-permute-start(bf16[128,3072]{1,0:T(8,128)(2,1)} %get-tuple-element.75.m0), channel_id=1, source_target_pairs={{0,1},{1,0},{2,3},{3,2},{4,5},{5,4},{6,7},{7,6},{8,9},{9,8},{10,11... | collective-permute-start | bytes 2359304 | tf_op jit(solution)/shard_map/ppermute | solution.py:371
  4.9 20.9 %collective-permute-start = (bf16[128,3072]{1,0:T(8,128)(2,1)}, bf16[128,3072]{1,0:T(8,128)(2,1)S(1)}, u32[]{:S(2)}, u32[]{:S(2)}) collective-permute-start(bf16[128,3072]{1,0:T(8,128)(2,1)} %get-tuple-element.75.m0), channel_id=1, source_target_pairs={{0,2},{1,3},{2,0},{3,1},{4,6},{5,7},{6,4},{7,5},{8,10},{9,11},{10,... | collective-permute-start | bytes 2359304 | tf_op jit(solution)/shard_map/ppermute | solution.py:374
  7.5 1.2 %copy-start.2 = (bf16[128,3072]{1,0:T(8,128)(2,1)S(1)}, bf16[128,3072]{1,0:T(8,128)(2,1)}, u32[]{:S(2)}) copy-start(bf16[128,3072]{1,0:T(8,128)(2,1)} %get-tuple-element.75.m0) | copy-start | bytes 2359300
  25.9 2.3 %collective-permute-start.2 = (bf16[128,3072]{1,0:T(8,128)(2,1)S(1)}, bf16[128,3072]{1,0:T(8,128)(2,1)S(1)}, u32[]{:S(2)}, u32[]{:S(2)}) collective-permute-start(bf16[128,3072]{1,0:T(8,128)(2,1)S(1)} %collective-permute-done.m0), channel_id=1, source_target_pairs={{0,1},{1,0},{2,3},{3,2},{4,5},{5,4},{6,7},{7,6},{8,9},{9,8},{10,11... | collective-permute-start | bytes 2359304 | tf_op jit(solution)/shard_map/ppermute | solution.py:371
  28.1 7.1 %slice-start = ((s8[9437184]{0:T(1024)(128)(4,1)}), s8[4194304]{0:T(1024)(128)(4,1)S(1)}, s32[]{:S(2)}) async-start(s8[9437184]{0:T(1024)(128)(4,1)} %bitcast.3), calls=%async_computation | async-start | bytes 8388608
  28.1 7.1 %slice-start.1 = ((s8[9437184]{0:T(1024)(128)(4,1)}), s8[4194304]{0:T(1024)(128)(4,1)S(1)}, s32[]{:S(2)}) async-start(s8[9437184]{0:T(1024)(128)(4,1)} %bitcast.3), calls=%async_computation.1 | async-start | bytes 8388608
  28.1 7.1 %slice-start.2 = ((s8[9437184]{0:T(1024)(128)(4,1)}), s8[1048576]{0:T(1024)(128)(4,1)S(1)}, s32[]{:S(2)}) async-start(s8[9437184]{0:T(1024)(128)(4,1)} %bitcast.3), calls=%async_computation.2 | async-start | bytes 2097152
  28.1 7.2 %copy-start = (bf16[512,3072]{1,0:T(8,128)(2,1)S(1)}, bf16[512,3072]{1,0:T(8,128)(2,1)}, u32[]{:S(2)}) copy-start(bf16[512,3072]{1,0:T(8,128)(2,1)} %refs_17_.1) | copy-start | bytes 9437188
  36.9 1.9 %collective-permute-start.3 = (bf16[128,1280]{1,0:T(8,128)(2,1)S(1)}, bf16[128,1280]{1,0:T(8,128)(2,1)S(1)}, u32[]{:S(2)}, u32[]{:S(2)}) collective-permute-start(bf16[128,1280]{1,0:T(8,128)(2,1)S(1)} %get-tuple-element.93), channel_id=1, source_target_pairs={{0,1},{1,0},{2,3},{3,2},{4,5},{5,4},{6,7},{7,6},{8,9},{9,8},{10,11... | collective-permute-start | bytes 983048 | tf_op jit(solution)/shard_map/ppermute | solution.py:371
  38.8 10.8 %copy-start.7 = (f32[1,3072]{1,0:T(1,128)S(1)}, f32[1,3072]{1,0:T(1,128)}, u32[]{:S(2)}) copy-start(f32[1,3072]{1,0:T(1,128)} %get-tuple-element.115.sg) | copy-start | bytes 36868
  38.8 10.1 %collective-permute-start.4 = (bf16[128,1280]{1,0:T(8,128)(2,1)S(1)}, bf16[128,1280]{1,0:T(8,128)(2,1)S(1)}, u32[]{:S(2)}, u32[]{:S(2)}) collective-permute-start(bf16[128,1280]{1,0:T(8,128)(2,1)S(1)} %join.3), channel_id=1, source_target_pairs={{0,2},{1,3},{2,0},{3,1},{4,6},{5,7},{6,4},{7,5},{8,10},{9,11},{10,... | collective-permute-start | bytes 983048 | tf_op jit(solution)/shard_map/ppermute | solution.py:374
  44.2 0.7 copy-start.10
  44.2 0.8 copy-start.11
  44.2 0.9 copy-start.12
  44.2 4.8 %collective-permute-start.8 = (bf16[128,1280]{1,0:T(8,128)(2,1)}, bf16[128,1280]{1,0:T(8,128)(2,1)}, u32[]{:S(2)}, u32[]{:S(2)}) collective-permute-start(bf16[128,1280]{1,0:T(8,128)(2,1)} %get-tuple-element.118), channel_id=1, source_target_pairs={{0,1},{1,0},{2,3},{3,2},{4,5},{5,4},{6,7},{7,6},{8,9},{9,8},{10,11... | collective-permute-start | bytes 983048 | tf_op jit(solution)/shard_map/ppermute | solution.py:371
  44.9 1.7 %collective-permute-start.5 = (bf16[128,1024]{1,0:T(8,128)(2,1)}, bf16[128,1024]{1,0:T(8,128)(2,1)S(1)}, u32[]{:S(2)}, u32[]{:S(2)}) collective-permute-start(bf16[128,1024]{1,0:T(8,128)(2,1)} %get-tuple-element.107), channel_id=1, source_target_pairs={{0,1},{1,0},{2,3},{3,2},{4,5},{5,4},{6,7},{7,6},{8,9},{9,8},{10,11... | collective-permute-start | bytes 786440 | tf_op jit(solution)/shard_map/ppermute | solution.py:371
  48.9 0.7 copy-start.5
  49.7 1.0 %copy-start.6 = (bf16[128,1280]{1,0:T(8,128)(2,1)S(1)}, bf16[128,1280]{1,0:T(8,128)(2,1)}, u32[]{:S(2)}) copy-start(bf16[128,1280]{1,0:T(8,128)(2,1)} %copy-done.5) | copy-start | bytes 983044
  51.7 0.7 copy-start.3
  52.5 5.7 %collective-permute-start.9 = (bf16[64,1280]{1,0:T(8,128)(2,1)S(1)}, bf16[64,1280]{1,0:T(8,128)(2,1)S(1)}, u32[]{:S(2)}, u32[]{:S(2)}) collective-permute-start(bf16[64,1280]{1,0:T(8,128)(2,1)S(1)} %get-tuple-element.121), channel_id=1, source_target_pairs={{0,4},{4,0},{8,12},{12,8},{16,20},{20,16},{24,28},{28,24},{1,5},{5... | collective-permute-start | bytes 491528 | tf_op jit(solution)/shard_map/ppermute | solution.py:377
  54.2 5.8 %collective-permute-start.14 = (bf16[128,768]{1,0:T(8,128)(2,1)}, bf16[128,768]{1,0:T(8,128)(2,1)S(1)}, u32[]{:S(2)}, u32[]{:S(2)}) collective-permute-start(bf16[128,768]{1,0:T(8,128)(2,1)} %copy-done.12), channel_id=1, source_target_pairs={{0,1},{1,0},{2,3},{3,2},{4,5},{5,4},{6,7},{7,6},{8,9},{9,8},{10,11... | collective-permute-start | bytes 589832 | tf_op jit(solution)/shard_map/ppermute | solution.py:371
  54.2 8.7 %collective-permute-start.6 = (bf16[128,1024]{1,0:T(8,128)(2,1)}, bf16[128,1024]{1,0:T(8,128)(2,1)S(1)}, u32[]{:S(2)}, u32[]{:S(2)}) collective-permute-start(bf16[128,1024]{1,0:T(8,128)(2,1)} %copy-done.10), channel_id=1, source_target_pairs={{0,1},{1,0},{2,3},{3,2},{4,5},{5,4},{6,7},{7,6},{8,9},{9,8},{10,11... | collective-permute-start | bytes 786440 | tf_op jit(solution)/shard_map/ppermute | solution.py:371
  54.7 8.2 %collective-permute-start.7 = (bf16[128,1024]{1,0:T(8,128)(2,1)S(1)}, bf16[128,1024]{1,0:T(8,128)(2,1)S(1)}, u32[]{:S(2)}, u32[]{:S(2)}) collective-permute-start(bf16[128,1024]{1,0:T(8,128)(2,1)S(1)} %join.4), channel_id=1, source_target_pairs={{0,2},{1,3},{2,0},{3,1},{4,6},{5,7},{6,4},{7,5},{8,10},{9,11},{10,... | collective-permute-start | bytes 786440 | tf_op jit(solution)/shard_map/ppermute | solution.py:374
  58.2 5.8 %collective-permute-start.11 = (bf16[64,1280]{1,0:T(8,128)(2,1)S(1)}, bf16[64,1280]{1,0:T(8,128)(2,1)S(1)}, u32[]{:S(2)}, u32[]{:S(2)}) collective-permute-start(bf16[64,1280]{1,0:T(8,128)(2,1)S(1)} %fusion.4), channel_id=1, source_target_pairs={{0,8},{4,12},{8,0},{12,4},{16,24},{20,28},{24,16},{28,20},{1,9},{5... | collective-permute-start | bytes 491528 | tf_op jit(solution)/shard_map/ppermute | solution.py:442
  60.0 12.9 %collective-permute-start.13 = (bf16[128,768]{1,0:T(8,128)(2,1)}, bf16[128,768]{1,0:T(8,128)(2,1)}, u32[]{:S(2)}, u32[]{:S(2)}) collective-permute-start(bf16[128,768]{1,0:T(8,128)(2,1)} %copy-done.11), channel_id=1, source_target_pairs={{0,1},{1,0},{2,3},{3,2},{4,5},{5,4},{6,7},{7,6},{8,9},{9,8},{10,11... | collective-permute-start | bytes 589832 | tf_op jit(solution)/shard_map/ppermute | solution.py:371
  60.8 12.2 %collective-permute-start.15 = (bf16[128,768]{1,0:T(8,128)(2,1)}, bf16[128,768]{1,0:T(8,128)(2,1)}, u32[]{:S(2)}, u32[]{:S(2)}) collective-permute-start(bf16[128,768]{1,0:T(8,128)(2,1)} %join.5), channel_id=1, source_target_pairs={{0,2},{1,3},{2,0},{3,1},{4,6},{5,7},{6,4},{7,5},{8,10},{9,11},{10,... | collective-permute-start | bytes 589832 | tf_op jit(solution)/shard_map/ppermute | solution.py:374
  63.0 28.2 %copy-start.1 = (f32[128,3072]{1,0:T(8,128)S(1)}, f32[128,3072]{1,0:T(8,128)}, u32[]{:S(2)}) copy-start(f32[128,3072]{1,0:T(8,128)} %x_start.3) | copy-start | bytes 4718596
  63.1 28.2 %copy-start.4 = (f32[64,1280]{1,0:T(8,128)S(1)}, f32[64,1280]{1,0:T(8,128)}, u32[]{:S(2)}) copy-start(f32[64,1280]{1,0:T(8,128)} %copy-done.3) | copy-start | bytes 983044
  63.1 5.1 %collective-permute-start.10 = (bf16[64,1024]{1,0:T(8,128)(2,1)S(1)}, bf16[64,1024]{1,0:T(8,128)(2,1)S(1)}, u32[]{:S(2)}, u32[]{:S(2)}) collective-permute-start(bf16[64,1024]{1,0:T(8,128)(2,1)S(1)} %get-tuple-element.125), channel_id=1, source_target_pairs={{0,4},{4,0},{8,12},{12,8},{16,20},{20,16},{24,28},{28,24},{1,5},{5... | collective-permute-start | bytes 393224 | tf_op jit(solution)/shard_map/ppermute | solution.py:377
  64.0 4.1 %copy-start.13 = (bf16[64,1280]{1,0:T(8,128)(2,1)}, bf16[64,1280]{1,0:T(8,128)(2,1)S(1)}, u32[]{:S(2)}) copy-start(bf16[64,1280]{1,0:T(8,128)(2,1)S(1)} %collective-permute-done.11) | copy-start | bytes 491524
  68.8 6.8 %collective-permute-start.12 = (bf16[64,1024]{1,0:T(8,128)(2,1)}, bf16[64,1024]{1,0:T(8,128)(2,1)}, u32[]{:S(2)}, u32[]{:S(2)}) collective-permute-start(bf16[64,1024]{1,0:T(8,128)(2,1)} %fusion.7), channel_id=1, source_target_pairs={{0,8},{4,12},{8,0},{12,4},{16,24},{20,28},{24,16},{28,20},{1,9},{5... | collective-permute-start | bytes 393224 | tf_op jit(solution)/shard_map/ppermute | solution.py:442
  70.5 10.7 %collective-permute-start.20 = (bf16[64,1280]{1,0:T(8,128)(2,1)}, bf16[64,1280]{1,0:T(8,128)(2,1)S(1)}, u32[]{:S(2)}, u32[]{:S(2)}) collective-permute-start(bf16[64,1280]{1,0:T(8,128)(2,1)} %fusion), channel_id=1, source_target_pairs={{0,16},{4,20},{8,24},{12,28},{16,0},{20,4},{24,8},{28,12},{1,17},{... | collective-permute-start | bytes 491528 | tf_op jit(solution)/shard_map/ppermute | solution.py:442
  74.1 4.7 %collective-permute-start.18 = (bf16[64,768]{1,0:T(8,128)(2,1)S(1)}, bf16[64,768]{1,0:T(8,128)(2,1)S(1)}, u32[]{:S(2)}, u32[]{:S(2)}) collective-permute-start(bf16[64,768]{1,0:T(8,128)(2,1)S(1)} %get-tuple-element.133), channel_id=1, source_target_pairs={{0,4},{4,0},{8,12},{12,8},{16,20},{20,16},{24,28},{28,24},{1,5},{5... | collective-permute-start | bytes 294920 | tf_op jit(solution)/shard_map/ppermute | solution.py:377
  76.6 8.8 %collective-permute-start.16 = (bf16[64,1024]{1,0:T(8,128)(2,1)S(1)}, bf16[64,1024]{1,0:T(8,128)(2,1)S(1)}, u32[]{:S(2)}, u32[]{:S(2)}) collective-permute-start(bf16[64,1024]{1,0:T(8,128)(2,1)S(1)} %fusion.3), channel_id=1, source_target_pairs={{0,16},{4,20},{8,24},{12,28},{16,0},{20,4},{24,8},{28,12},{1,17},{... | collective-permute-start | bytes 393224 | tf_op jit(solution)/shard_map/ppermute | solution.py:442
  78.8 4.8 %collective-permute-start.19 = (bf16[64,768]{1,0:T(8,128)(2,1)S(1)}, bf16[64,768]{1,0:T(8,128)(2,1)S(1)}, u32[]{:S(2)}, u32[]{:S(2)}) collective-permute-start(bf16[64,768]{1,0:T(8,128)(2,1)S(1)} %fusion.8), channel_id=1, source_target_pairs={{0,8},{4,12},{8,0},{12,4},{16,24},{20,28},{24,16},{28,20},{1,9},{5... | collective-permute-start | bytes 294920 | tf_op jit(solution)/shard_map/ppermute | solution.py:442
  82.2 9.1 %collective-permute-start.23 = (bf16[64,1280]{1,0:T(8,128)(2,1)S(1)}, bf16[64,1280]{1,0:T(8,128)(2,1)S(1)}, u32[]{:S(2)}, u32[]{:S(2)}) collective-permute-start(bf16[64,1280]{1,0:T(8,128)(2,1)S(1)} %get-tuple-element.147), channel_id=1, source_target_pairs={{0,4},{4,0},{8,12},{12,8},{16,20},{20,16},{24,28},{28,24},{1,5},{5... | collective-permute-start | bytes 491528 | tf_op jit(solution)/shard_map/ppermute | solution.py:377
  83.6 5.7 %collective-permute-start.21 = (bf16[64,768]{1,0:T(8,128)(2,1)S(1)}, bf16[64,768]{1,0:T(8,128)(2,1)S(1)}, u32[]{:S(2)}, u32[]{:S(2)}) collective-permute-start(bf16[64,768]{1,0:T(8,128)(2,1)S(1)} %fusion.6), channel_id=1, source_target_pairs={{0,16},{4,20},{8,24},{12,28},{16,0},{20,4},{24,8},{28,12},{1,17},{... | collective-permute-start | bytes 294920 | tf_op jit(solution)/shard_map/ppermute | solution.py:442
  86.4 5.9 %collective-permute-start.17 = (bf16[64,1024]{1,0:T(8,128)(2,1)S(1)}, bf16[64,1024]{1,0:T(8,128)(2,1)S(1)}, u32[]{:S(2)}, u32[]{:S(2)}) collective-permute-start(bf16[64,1024]{1,0:T(8,128)(2,1)S(1)} %get-tuple-element.149), channel_id=1, source_target_pairs={{0,4},{4,0},{8,12},{12,8},{16,20},{20,16},{24,28},{28,24},{1,5},{5... | collective-permute-start | bytes 393224 | tf_op jit(solution)/shard_map/ppermute | solution.py:377
  89.3 4.7 %collective-permute-start.22 = (bf16[64,768]{1,0:T(8,128)(2,1)S(1)}, bf16[64,768]{1,0:T(8,128)(2,1)S(1)}, u32[]{:S(2)}, u32[]{:S(2)}) collective-permute-start(bf16[64,768]{1,0:T(8,128)(2,1)S(1)} %get-tuple-element.145), channel_id=1, source_target_pairs={{0,4},{4,0},{8,12},{12,8},{16,20},{20,16},{24,28},{28,24},{1,5},{5... | collective-permute-start | bytes 294920 | tf_op jit(solution)/shard_map/ppermute | solution.py:377

commit v12 on v6

--- a/solution.py
+++ b/solution.py
@@ -297,33 +297,44 @@
     )(parity, keep, sent, sg, *fetched)
 
 
-def finish_kernel(first, parity, x_start, earlier, kept, fetched, other, back, *refs):
-    out, result, sem = refs[-3:]
-    half, count = kept.shape
-    cols = slice(first, first + count)
+def finish_kernel(firsts, parity, x_start, *refs):
+    n = len(firsts)
+    given, rest = refs[: 5 * n], refs[-2 - n :]
+    out, results, sem = rest[0], rest[1 : 1 + n], rest[1 + n]
     p = parity[0]
-    mine = pl.ds(pl.multiple_of(p * half, half), half)
-    rest = pl.ds(pl.multiple_of((1 - p) * half, half), half)
     odd = p.astype(f32)
-    result[mine, :] = x_start[mine, cols] + earlier[...] + kept[...] + odd * fetched[...].astype(f32)
-    result[rest, :] = x_start[rest, cols] + other[...] + back[...].astype(f32)
-    copy = pltpu.make_async_copy(result, out.at[0, :, pl.ds(first, count)], sem)
-    copy.start()
-    copy.wait()
-
-
-def finish_call(parity, x_start, earlier, kept, fetched, other, back, into, first):
+    copies = []
+    for i, first in enumerate(firsts):
+        earlier, kept, fetched, other, back = given[5 * i : 5 * i + 5]
+        half, count = kept.shape
+        cols = slice(first, first + count)
+        mine = pl.ds(pl.multiple_of(p * half, half), half)
+        rest = pl.ds(pl.multiple_of((1 - p) * half, half), half)
+        results[i][mine, :] = (
+            x_start[mine, cols] + earlier[...] + kept[...] + odd * fetched[...].astype(f32)
+        )
+        results[i][rest, :] = x_start[rest, cols] + other[...] + back[...].astype(f32)
+        copies.append(
+            pltpu.make_async_copy(results[i], out.at[0, :, pl.ds(first, count)], sem.at[i])
+        )
+        copies[i].start()
+    for copy in copies:
+        copy.wait()
+
+
+def finish_call(parity, x_start, groups, firsts, into):
     rows, width = x_start.shape
     vm = pl.BlockSpec(memory_space=VM)
     smem = pl.BlockSpec(memory_space=pltpu.SMEM)
     hbm = pl.BlockSpec(memory_space=pltpu.HBM)
-    given = [parity, x_start, earlier, kept, fetched, other, back]
+    given = [parity, x_start] + [one for group in groups for one in group]
     return pl.pallas_call(
-        functools.partial(finish_kernel, first),
-        in_specs=[smem] + [vm] * 6 + [hbm] * len(into),
+        functools.partial(finish_kernel, firsts),
+        in_specs=[smem] + [vm] * (len(given) - 1) + [hbm] * len(into),
         out_specs=hbm,
         out_shape=jax.ShapeDtypeStruct((1, rows, width), f32),
-        scratch_shapes=[VM((rows, kept.shape[1]), f32), pltpu.SemaphoreType.DMA],
+        scratch_shapes=[VM((rows, group[1].shape[1]), f32) for group in groups]
+        + [pltpu.SemaphoreType.DMA((len(groups),))],
         input_output_aliases={len(given): 0} if into else {},
         compiler_params=params(6),
         name="finish",
@@ -351,7 +362,7 @@
     groups = n_step // 2
     half = rows // 2
     unit = width // 24
-    counts = [10 * unit, 8 * unit, 6 * unit]
+    counts = [n * unit for n in (9,8,7)]
     chunks = len(counts)
     firsts = [sum(counts[:c]) for c in range(chunks)]
     qg, kg = q_gain[None, :], k_gain[None, :]
@@ -462,8 +473,13 @@
 
         def finish(fetched):
             given = [held[name] for name in ("earlier", "kept", "fetched", "other")]
-            into = list(written)
-            written[:] = [finish_call(which, x_start, *given, fetched[0], into, firsts[c])]
+            stash.append((firsts[c], given + [fetched[0]]))
+            if len(stash) in (1, chunks):
+                mine = stash[len(stash) - 1 :] if len(stash) == 1 else stash[1:]
+                places = [place for place, _ in mine]
+                groups_in = [group for _, group in mine]
+                into = list(written)
+                written[:] = [finish_call(which, x_start, groups_in, places, into)]
 
         stages = [(drift_of, to_pair), (pair_sum, rounds[0][1])]
         for r in range(len(rounds)):
@@ -477,13 +493,13 @@
     turns = []
     arrival = 2.0
     for c in range(chunks):
-        share = 16.0 * counts[c] / width
+        share = 16.0 * (10 - 2 * c) / 24
         arrival += share
         when = arrival
         for i in range(len(plan[c])):
             turns.append((when, c, i))
             when += 2.2 + share * (1.0 if i == len(plan[c]) - 3 else 0.5)
-    written = []
+    written, stash = [], []
     last = None
     for _, c, i in sorted(turns):
         compute, move = plan[c][i]

time: 93.4 us -> 92 us (0.985)
  waiting for transfers between devices: 26.2 us -> 21.9 us
  starting transfers between devices: 28 us -> 30.8 us
    ppermute x6, waiting for transfers between devices: 9.72 us -> 6.68 us  [along(): lax.ppermute(x, 'step', [(2 * a + i, 2 * b + i) for a, b in pairs for i i...]
    ppermute x6, starting transfers between devices: 6.05 us -> 8.95 us  [to_pair(): return lax.ppermute(x, 'step', [(i, i ^ 1) for i in range(n_step)])]
    pallas_call x3 -> x2, Pallas kernels: 2.68 us -> 2.01 us  [finish_call(): pl.pallas_call(functools.partial(finish_kernel, firsts), in_specs=[smem]...]
  transfers between devices with their start and end apart: 24 -> 24, of which waited for: 13 -> 11; matrix products, arithmetic and copies ran while one was open for 0% -> 0% of each run, Pallas kernels for 24% -> 24%
where the time goes in v12:
time: 92 us; the launch traced here: 91.8 us
  Pallas kernels  35.8 us (39%)
  starting transfers between devices  30.8 us (33%)
  waiting for transfers between devices  21.9 us (24%)
  local copies, waits for them, and re-layouts  1.8 us (2%)
  between operations  1.04 us (1%)
    pallas_call x2, Pallas kernels, project_call(): pl.pallas_call(functools.partial(project_kernel, tile, load, tiles), in_s...  17.6 us
    ppermute x6, starting transfers between devices, along(): lax.ppermute(x, 'step', [(2 * a + i, 2 * b + i) for a, b in pairs for i i...  13.7 us
    ppermute x4, waiting for transfers between devices, to_chip(): lax.ppermute(x, 'seq', [(i, (i + 2 * offset) % n_seq) for i in range(n_se...  9.39 us
    ppermute x6, starting transfers between devices, to_pair(): return lax.ppermute(x, 'step', [(i, i ^ 1) for i in range(n_step)])  8.95 us
    ppermute x4, starting transfers between devices, to_chip(): lax.ppermute(x, 'seq', [(i, (i + 2 * offset) % n_seq) for i in range(n_se...  6.77 us
    ppermute x6, waiting for transfers between devices, along(): lax.ppermute(x, 'step', [(2 * a + i, 2 * b + i) for a, b in pairs for i i...  6.68 us
    pallas_call x2, Pallas kernels, out_call(): pl.pallas_call(functools.partial(out_kernel, plan), in_specs=[vm] * len(g...  5.25 us
    pallas_call x1, Pallas kernels, norm_call(): pl.pallas_call(norm_kernel, in_specs=[smem, smem, hbm, hbm], out_specs=[v...  3.71 us
  transfers between devices with their start and end apart: 24, of which 11 were waited for; matrix products, arithmetic and copies ran while one was open for 0% of the time, Pallas kernels for 24%

profile of v12, /device:TPU:0, one launch (start us, length us, event | category | flops | bytes accessed | tf_op | source)
XLA Modules:
  0.0 91.8 jit_solution(2981293932542848354)
XLA Ops:
  0.7 3.7 %norm.1 = (bf16[128,3072]{1,0:T(8,128)(2,1)}, f32[1,3072]{1,0:T(1,128)}) custom-call(s32[1]{0:T(128)S(6)} %copy.14.t_ref, f32[50]{0:T(128)} %size_ref.1, f32[1,128,3072]{2,1,0:T(8,128)} %x_hbm.1, f32[50,9216]{1,0:T(8,128)} %mod_hbm.1), custom_call_target="tpu_custom_call" | custom-call | flops 3932160 | tf_op jit(solution)/shard_map/norm/pallas_call | solution.py:56
  4.4 0.5 collective-permute-start.1
  4.9 2.6 %collective-permute-start = (bf16[128,3072]{1,0:T(8,128)(2,1)}, bf16[128,3072]{1,0:T(8,128)(2,1)S(1)}, u32[]{:S(2)}, u32[]{:S(2)}) collective-permute-start(bf16[128,3072]{1,0:T(8,128)(2,1)} %get-tuple-element.75.m0), channel_id=1, source_target_pairs={{0,2},{1,3},{2,0},{3,1},{4,6},{5,7},{6,4},{7,5},{8,10},{9,11},{10,... | collective-permute-start | bytes 2359304 | tf_op jit(solution)/shard_map/ppermute | solution.py:374
  7.5 0.0 collective-permute-done.1.m1
  7.5 0.0 copy-start.2
  7.5 1.1 %copy-done.2 = bf16[128,3072]{1,0:T(8,128)(2,1)S(1)} copy-done((bf16[128,3072]{1,0:T(8,128)(2,1)S(1)}, bf16[128,3072]{1,0:T(8,128)(2,1)}, u32[]{:S(2)}) %copy-start.2) | copy-done | bytes 786456
  8.7 12.4 %project.2 = (bf16[256,512]{1,0:T(8,128)(2,1)S(1)}, bf16[256,512]{1,0:T(8,128)(2,1)S(1)}, bf16[256,512]{1,0:T(8,128)(2,1)S(1)}, bf16[256,1536]{1,0:T(8,128)(2,1)...) custom-call(bf16[128,3072]{1,0:T(8,128)(2,1)S(1)} %copy-done.2, ...), custom_call_target="tpu_custom_call" | custom-call | flops 4831838208 | tf_op jit(solution)/shard_map/project/pallas_call | solution.py:151
  21.1 4.8 %collective-permute-done.m0 = bf16[128,3072]{1,0:T(8,128)(2,1)S(1)} collective-permute-done((bf16[128,3072]{1,0:T(8,128)(2,1)}, bf16[128,3072]{1,0:T(8,128)(2,1)S(1)}, u32[]{:S(2)}, u32[]{:S(2)}) %collective-permute-start) | collective-permute-done | bytes 786464 | tf_op jit(solution)/shard_map/ppermute | solution.py:374
  25.9 0.0 collective-permute-start.2
  25.9 2.3 %collective-permute-done.2.m1 = bf16[128,3072]{1,0:T(8,128)(2,1)S(1)} collective-permute-done((bf16[128,3072]{1,0:T(8,128)(2,1)S(1)}, bf16[128,3072]{1,0:T(8,128)(2,1)S(1)}, u32[]{:S(2)}, u32[]{:S(2)}) %collective-permute-start.2) | collective-permute-done | bytes 786464 | tf_op jit(solution)/shard_map/ppermute | solution.py:371
  28.2 5.2 %project.3 = (bf16[256,512]{1,0:T(8,128)(2,1)S(1)}, bf16[256,512]{1,0:T(8,128)(2,1)S(1)}, bf16[256,512]{1,0:T(8,128)(2,1)S(1)}, bf16[256,1536]{1,0:T(8,128)(2,1)S(1)}) custom-call(bf16[128,3072]{1,0:T(8,128)(2,1)S(1)} %collective-permute-done.m0, bf16[128,3072]{1,0:T(8,128)(2,1)S(1)} %collective-permute-done.2.m1, f32[1,128]{1,0:T(1,128)S(1)} %bitcast.6, ...), custom_call_target="tpu_custom_call" | custom-call | flops 4831838208 | tf_op jit(solution)/shard_map/project/pallas_call | solution.py:151
  33.4 1.9 %attend.2.refs_0_.refs_4_ = bf16[256,512]{1,0:T(8,128)(2,1)S(1)} custom-call(bf16[256,512]{1,0:T(8,128)(2,1)S(1)} %get-tuple-element.85.refs_0_, bf16[256,512]{1,0:T(8,128)(2,1)S(1)} %get-tuple-element.86.refs_1_, bf16[256,512]{1,0:T(8,128)(2,1)S(1)} %get-tuple-element.87.refs_2_, bf16[256,512]{1,0:T(8,128)(2,1)S(1)} %get-tuple-element.88.refs_3_, ...), custom_call_target="tpu_custom_call" | custom-call | flops 805306368 | tf_op jit(solution)/shard_map/attend/pallas_call | solution.py:191
  35.3 1.5 %project_out.2 = (f32[128,1152]{1,0:T(8,128)S(1)}, bf16[128,1152]{1,0:T(8,128)(2,1)S(1)}) custom-call(bf16[256,512]{1,0:T(8,128)(2,1)S(1)} %attend.2.refs_0_.refs_4_, bf16[256,1536]{1,0:T(8,128)(2,1)S(1)} %get-tuple-element.100.refs_1_.refs_5_, bf16[512,3072]{1,0:T(8,128)(2,1)S(1)} %copy-done, bf16[1536,3072]{1,0:T(8,128)(2,1)S(1)} %bitcast.4), custom_call_target="tpu_custom_call" | custom-call | flops 1207959552 | tf_op jit(solution)/shard_map/project_out/pallas_call | solution.py:235
  36.9 0.2 collective-permute-start.3
  37.1 1.7 %attend.3.refs_8_.refs_12_.refs_16_ = bf16[256,512]{1,0:T(8,128)(2,1)S(1)} custom-call(bf16[256,512]{1,0:T(8,128)(2,1)S(1)} %get-tuple-element.94.refs_0_, bf16[256,512]{1,0:T(8,128)(2,1)S(1)} %get-tuple-element.86.refs_1_, bf16[256,512]{1,0:T(8,128)(2,1)S(1)} %get-tuple-element.87.refs_2_, bf16[256,512]{1,0:T(8,128)(2,1)S(1)} %get-tuple-element.88.refs_3_, ...), custom_call_target="tpu_custom_call" | custom-call | flops 805306368 | tf_op jit(solution)/shard_map/attend/pallas_call | solution.py:191
  38.8 0.0 collective-permute-done.3.sent
  38.8 0.1 join.3
  38.8 1.8 %collective-permute-start.4 = (bf16[128,1152]{1,0:T(8,128)(2,1)S(1)}, bf16[128,1152]{1,0:T(8,128)(2,1)S(1)}, u32[]{:S(2)}, u32[]{:S(2)}) collective-permute-start(bf16[128,1152]{1,0:T(8,128)(2,1)S(1)} %join.3), channel_id=1, source_target_pairs={{0,2},{1,3},{2,0},{3,1},{4,6},{5,7},{6,4},{7,5},{8,10},{9,11},{10,... | collective-permute-start | bytes 884744 | tf_op jit(solution)/shard_map/ppermute | solution.py:374
  40.7 3.7 %project_out.3 = (f32[128,1024]{1,0:T(8,128)S(1)}, bf16[128,1024]{1,0:T(8,128)(2,1)S(1)}, f32[128,896]{1,0:T(8,128)S(1)}, bf16[128,896]{1,0:T(8,128)(2,1)}, f32[...) custom-call(bf16[256,512]{1,0:T(8,128)(2,1)S(1)} %attend.2.refs_0_.r, ...), custom_call_target="tpu_custom_call" | custom-call | flops 2818572288 | tf_op jit(solution)/shard_map/project_out/pallas_call | solution.py:235
  44.4 0.1 collective-permute-start.5
  44.5 0.6 copy-done.6
  45.1 0.1 collective-permute-start.8
  45.2 0.8 collective-permute-done.5.sent
  45.9 2.3 %collective-permute-done.4.refs_0_ = bf16[128,1152]{1,0:T(8,128)(2,1)S(1)} collective-permute-done((bf16[128,1152]{1,0:T(8,128)(2,1)S(1)}, bf16[128,1152]{1,0:T(8,128)(2,1)S(1)}, u32[]{:S(2)}, u32[]{:S(2)}) %collective-permute-start.4) | collective-permute-done | bytes 294944 | tf_op jit(solution)/shard_map/ppermute | solution.py:374
  48.2 0.8 join.4
  49.0 1.7 %collective-permute-start.7 = (bf16[128,1024]{1,0:T(8,128)(2,1)}, bf16[128,1024]{1,0:T(8,128)(2,1)S(1)}, u32[]{:S(2)}, u32[]{:S(2)}) collective-permute-start(bf16[128,1024]{1,0:T(8,128)(2,1)} %join.4), channel_id=1, source_target_pairs={{0,2},{1,3},{2,0},{3,1},{4,6},{5,7},{6,4},{7,5},{8,10},{9,11},{10,... | collective-permute-start | bytes 786440 | tf_op jit(solution)/shard_map/ppermute | solution.py:374
  50.7 0.5 collective-permute-start.11
  51.2 0.0 collective-permute-done.8.sent
  51.2 0.7 drift.3
  51.9 1.5 %collective-permute-start.13 = (bf16[64,1152]{1,0:T(8,128)(2,1)}, bf16[64,1152]{1,0:T(8,128)(2,1)S(1)}, u32[]{:S(2)}, u32[]{:S(2)}) collective-permute-start(bf16[64,1152]{1,0:T(8,128)(2,1)} %get-tuple-element.120), channel_id=1, source_target_pairs={{0,4},{4,0},{8,12},{12,8},{16,20},{20,16},{24,28},{28,24},{1,5},{5... | collective-permute-start | bytes 442376 | tf_op jit(solution)/shard_map/ppermute | solution.py:377
  53.4 1.0 %join.5 = bf16[128,896]{1,0:T(8,128)(2,1)S(1)} custom-call(f32[128,896]{1,0:T(8,128)S(1)} %get-tuple-element.126.keep, bf16[128,896]{1,0:T(8,128)(2,1)} %collective-permute-done.11.sent), custom_call_target="tpu_custom_call" | custom-call | tf_op jit(solution)/shard_map/join/pallas_call | solution.py:253
  54.4 0.6 collective-permute-start.12
  55.0 1.9 %collective-permute-done.7.refs_0_ = bf16[128,1024]{1,0:T(8,128)(2,1)S(1)} collective-permute-done((bf16[128,1024]{1,0:T(8,128)(2,1)}, bf16[128,1024]{1,0:T(8,128)(2,1)S(1)}, u32[]{:S(2)}, u32[]{:S(2)}) %collective-permute-start.7) | collective-permute-done | bytes 262176 | tf_op jit(solution)/shard_map/ppermute | solution.py:374
  57.0 0.0 collective-permute-done.6.sent
  57.0 1.0 %drift.4 = (f32[64,1024]{1,0:T(8,128)S(1)}, f32[64,1024]{1,0:T(8,128)S(1)}, bf16[64,1024]{1,0:T(8,128)(2,1)S(1)}) custom-call(s32[1]{0:T(128)} %bitcast.parity, f32[128,1024]{1,0:T(8,128)S(1)} %get-tuple-element.113.keep, bf16[128,1024]{1,0:T(8,128)(2,1)} %collective-permute-done.6.sent, f32[1,3072]{1,0:T(1,128)S(1)} %copy-done.3, ...), custom_call_target="tpu_custom_call" | custom-call | tf_op jit(solution)/shard_map/drift/pallas_call | solution.py:286
  58.0 2.4 %collective-permute-start.9 = (bf16[64,1024]{1,0:T(8,128)(2,1)S(1)}, bf16[64,1024]{1,0:T(8,128)(2,1)S(1)}, u32[]{:S(2)}, u32[]{:S(2)}) collective-permute-start(bf16[64,1024]{1,0:T(8,128)(2,1)S(1)} %get-tuple-element.123), channel_id=1, source_target_pairs={{0,4},{4,0},{8,12},{12,8},{16,20},{20,16},{24,28},{28,24},{1,5},{5... | collective-permute-start | bytes 393224 | tf_op jit(solution)/shard_map/ppermute | solution.py:377
  60.5 0.0 copy-start.1
  60.5 1.6 %collective-permute-start.16 = (bf16[64,1152]{1,0:T(8,128)(2,1)S(1)}, bf16[64,1152]{1,0:T(8,128)(2,1)S(1)}, u32[]{:S(2)}, u32[]{:S(2)}) collective-permute-start(bf16[64,1152]{1,0:T(8,128)(2,1)S(1)} %fusion.6), channel_id=1, source_target_pairs={{0,8},{4,12},{8,0},{12,4},{16,24},{20,28},{24,16},{28,20},{1,9},{5... | collective-permute-start | bytes 442376 | tf_op jit(solution)/shard_map/ppermute | solution.py:442
  62.1 0.4 collective-permute-done.12.refs_0_
  62.5 0.0 collective-permute-done.10.sent
  62.5 0.1 drift.5
  62.6 1.3 %collective-permute-start.15 = (bf16[64,896]{1,0:T(8,128)(2,1)S(1)}, bf16[64,896]{1,0:T(8,128)(2,1)S(1)}, u32[]{:S(2)}, u32[]{:S(2)}) collective-permute-start(bf16[64,896]{1,0:T(8,128)(2,1)S(1)} %get-tuple-element.131), channel_id=1, source_target_pairs={{0,4},{4,0},{8,12},{12,8},{16,20},{20,16},{24,28},{28,24},{1,5},{5... | collective-permute-start | bytes 344072 | tf_op jit(solution)/shard_map/ppermute | solution.py:377
  63.9 1.5 %collective-permute-start.14 = (bf16[64,1024]{1,0:T(8,128)(2,1)S(1)}, bf16[64,1024]{1,0:T(8,128)(2,1)S(1)}, u32[]{:S(2)}, u32[]{:S(2)}) collective-permute-start(bf16[64,1024]{1,0:T(8,128)(2,1)S(1)} %fusion.7), channel_id=1, source_target_pairs={{0,8},{4,12},{8,0},{12,4},{16,24},{20,28},{24,16},{28,20},{1,9},{5... | collective-permute-start | bytes 393224 | tf_op jit(solution)/shard_map/ppermute | solution.py:442
  65.4 0.3 collective-permute-done.16
  65.7 0.1 fusion
  65.7 2.6 %collective-permute-start.18 = (bf16[64,1152]{1,0:T(8,128)(2,1)S(1)}, bf16[64,1152]{1,0:T(8,128)(2,1)S(1)}, u32[]{:S(2)}, u32[]{:S(2)}) collective-permute-start(bf16[64,1152]{1,0:T(8,128)(2,1)S(1)} %fusion), channel_id=1, source_target_pairs={{0,16},{4,20},{8,24},{12,28},{16,0},{20,4},{24,8},{28,12},{1,17},{... | collective-permute-start | bytes 442376 | tf_op jit(solution)/shard_map/ppermute | solution.py:442
  68.4 1.6 %collective-permute-start.19 = (bf16[64,896]{1,0:T(8,128)(2,1)S(1)}, bf16[64,896]{1,0:T(8,128)(2,1)S(1)}, u32[]{:S(2)}, u32[]{:S(2)}) collective-permute-start(bf16[64,896]{1,0:T(8,128)(2,1)S(1)} %fusion.8), channel_id=1, source_target_pairs={{0,8},{4,12},{8,0},{12,4},{16,24},{20,28},{24,16},{28,20},{1,9},{5... | collective-permute-start | bytes 344072 | tf_op jit(solution)/shard_map/ppermute | solution.py:442
  70.0 1.0 %collective-permute-done.14 = bf16[64,1024]{1,0:T(8,128)(2,1)S(1)} collective-permute-done((bf16[64,1024]{1,0:T(8,128)(2,1)S(1)}, bf16[64,1024]{1,0:T(8,128)(2,1)S(1)}, u32[]{:S(2)}, u32[]{:S(2)}) %collective-permute-start.14) | collective-permute-done | bytes 131104 | tf_op jit(solution)/shard_map/ppermute | solution.py:442
  71.0 0.1 fusion.3
  71.1 2.9 %collective-permute-start.17 = (bf16[64,1024]{1,0:T(8,128)(2,1)S(1)}, bf16[64,1024]{1,0:T(8,128)(2,1)S(1)}, u32[]{:S(2)}, u32[]{:S(2)}) collective-permute-start(bf16[64,1024]{1,0:T(8,128)(2,1)S(1)} %fusion.3), channel_id=1, source_target_pairs={{0,16},{4,20},{8,24},{12,28},{16,0},{20,4},{24,8},{28,12},{1,17},{... | collective-permute-start | bytes 393224 | tf_op jit(solution)/shard_map/ppermute | solution.py:442
  73.9 1.1 %collective-permute-done.19 = bf16[64,896]{1,0:T(8,128)(2,1)S(1)} collective-permute-done((bf16[64,896]{1,0:T(8,128)(2,1)S(1)}, bf16[64,896]{1,0:T(8,128)(2,1)S(1)}, u32[]{:S(2)}, u32[]{:S(2)}) %collective-permute-start.19) | collective-permute-done | bytes 114720 | tf_op jit(solution)/shard_map/ppermute | solution.py:442
  75.1 3.4 %collective-permute-start.21 = (bf16[64,896]{1,0:T(8,128)(2,1)S(1)}, bf16[64,896]{1,0:T(8,128)(2,1)S(1)}, u32[]{:S(2)}, u32[]{:S(2)}) collective-permute-start(bf16[64,896]{1,0:T(8,128)(2,1)S(1)} %fusion.4), channel_id=1, source_target_pairs={{0,16},{4,20},{8,24},{12,28},{16,0},{20,4},{24,8},{28,12},{1,17},{... | collective-permute-start | bytes 344072 | tf_op jit(solution)/shard_map/ppermute | solution.py:442
  78.5 0.1 add_convert_fusion
  78.6 1.0 %collective-permute-start.23 = (bf16[64,1152]{1,0:T(8,128)(2,1)S(1)}, bf16[64,1152]{1,0:T(8,128)(2,1)S(1)}, u32[]{:S(2)}, u32[]{:S(2)}) collective-permute-start(bf16[64,1152]{1,0:T(8,128)(2,1)S(1)} %get-tuple-element.149), channel_id=1, source_target_pairs={{0,4},{4,0},{8,12},{12,8},{16,20},{20,16},{24,28},{28,24},{1,5},{5... | collective-permute-start | bytes 442376 | tf_op jit(solution)/shard_map/ppermute | solution.py:377
  79.6 4.3 %collective-permute-done.17 = bf16[64,1024]{1,0:T(8,128)(2,1)S(1)} collective-permute-done((bf16[64,1024]{1,0:T(8,128)(2,1)S(1)}, bf16[64,1024]{1,0:T(8,128)(2,1)S(1)}, u32[]{:S(2)}, u32[]{:S(2)}) %collective-permute-start.17) | collective-permute-done | bytes 131104 | tf_op jit(solution)/shard_map/ppermute | solution.py:442
  83.9 0.1 add_convert_fusion.1
  84.0 1.6 %collective-permute-start.20 = (bf16[64,1024]{1,0:T(8,128)(2,1)S(1)}, bf16[64,1024]{1,0:T(8,128)(2,1)S(1)}, u32[]{:S(2)}, u32[]{:S(2)}) collective-permute-start(bf16[64,1024]{1,0:T(8,128)(2,1)S(1)} %get-tuple-element.147), channel_id=1, source_target_pairs={{0,4},{4,0},{8,12},{12,8},{16,20},{20,16},{24,28},{28,24},{1,5},{5... | collective-permute-start | bytes 393224 | tf_op jit(solution)/shard_map/ppermute | solution.py:377
  85.6 0.0 collective-permute-done.21
  85.6 0.1 add_convert_fusion.2
  85.7 1.1 %collective-permute-start.22 = (bf16[64,896]{1,0:T(8,128)(2,1)S(1)}, bf16[64,896]{1,0:T(8,128)(2,1)S(1)}, u32[]{:S(2)}, u32[]{:S(2)}) collective-permute-start(bf16[64,896]{1,0:T(8,128)(2,1)S(1)} %get-tuple-element.145), channel_id=1, source_target_pairs={{0,4},{4,0},{8,12},{12,8},{16,20},{20,16},{24,28},{28,24},{1,5},{5... | collective-permute-start | bytes 344072 | tf_op jit(solution)/shard_map/ppermute | solution.py:377
  86.8 0.0 collective-permute-done.23.refs_4_
  86.8 0.9 %finish.2.refs_10_ = f32[1,128,3072]{2,1,0:T(8,128)} custom-call(s32[1]{0:T(128)} %bitcast.parity, f32[128,3072]{1,0:T(8,128)S(1)} %copy-done.1, f32[64,1152]{1,0:T(8,128)S(1)} %get-tuple-element.150.refs_0_, f32[64,1152]{1,0:T(8,128)S(1)} %get-tuple-element.128.refs_1_, bf16[64,1152]{1,0:T(8,128)(2,1)S(1)} %collective-permute-done.13.refs_2_, ...), custom_call_target="tpu_custom_call" | custom-call | tf_op jit(solution)/shard_map/finish/pallas_call | solution.py:331
  87.8 2.8 %collective-permute-done.22.refs_9_ = bf16[64,896]{1,0:T(8,128)(2,1)S(1)} collective-permute-done((bf16[64,896]{1,0:T(8,128)(2,1)S(1)}, bf16[64,896]{1,0:T(8,128)(2,1)S(1)}, u32[]{:S(2)}, u32[]{:S(2)}) %collective-permute-start.22) | collective-permute-done | bytes 114720 | tf_op jit(solution)/shard_map/ppermute | solution.py:377
  90.5 1.1 %finish.3 = f32[1,128,3072]{2,1,0:T(8,128)} custom-call(s32[1]{0:T(128)} %bitcast.parity, f32[128,3072]{1,0:T(8,128)S(1)} %copy-done.1, f32[64,1024]{1,0:T(8,128)S(1)} %get-tuple-element.148.refs_0_, f32[64,1024]{1,0:T(8,128)S(1)} %get-tuple-element.122.refs_1_, ...), custom_call_target="tpu_custom_call", output_to_operand_aliasing={{}: (12, {})} | custom-call | tf_op jit(solution)/shard_map/finish/pallas_call | solution.py:331
  (29 shorter events, 0.2 us)
Async XLA Ops:
  0.0 7.5 %copy-start.4 = (f32[128]{0:T(128)S(1)}, f32[128]{0:T(128)}, u32[]{:S(2)}) copy-start(f32[128]{0:T(128)} %param.16) | copy-start | bytes 1540
  0.0 7.5 %copy-start.5 = (f32[128]{0:T(128)S(1)}, f32[128]{0:T(128)}, u32[]{:S(2)}) copy-start(f32[128]{0:T(128)} %param.17) | copy-start | bytes 1540
  4.4 3.1 %collective-permute-start.1 = (bf16[128,3072]{1,0:T(8,128)(2,1)}, bf16[128,3072]{1,0:T(8,128)(2,1)S(1)}, u32[]{:S(2)}, u32[]{:S(2)}) collective-permute-start(bf16[128,3072]{1,0:T(8,128)(2,1)} %get-tuple-element.75.m0), channel_id=1, source_target_pairs={{0,1},{1,0},{2,3},{3,2},{4,5},{5,4},{6,7},{7,6},{8,9},{9,8},{10,11... | collective-permute-start | bytes 2359304 | tf_op jit(solution)/shard_map/ppermute | solution.py:371
  4.9 20.9 %collective-permute-start = (bf16[128,3072]{1,0:T(8,128)(2,1)}, bf16[128,3072]{1,0:T(8,128)(2,1)S(1)}, u32[]{:S(2)}, u32[]{:S(2)}) collective-permute-start(bf16[128,3072]{1,0:T(8,128)(2,1)} %get-tuple-element.75.m0), channel_id=1, source_target_pairs={{0,2},{1,3},{2,0},{3,1},{4,6},{5,7},{6,4},{7,5},{8,10},{9,11},{10,... | collective-permute-start | bytes 2359304 | tf_op jit(solution)/shard_map/ppermute | solution.py:374
  7.5 1.2 %copy-start.2 = (bf16[128,3072]{1,0:T(8,128)(2,1)S(1)}, bf16[128,3072]{1,0:T(8,128)(2,1)}, u32[]{:S(2)}) copy-start(bf16[128,3072]{1,0:T(8,128)(2,1)} %get-tuple-element.75.m0) | copy-start | bytes 2359300
  25.9 2.3 %collective-permute-start.2 = (bf16[128,3072]{1,0:T(8,128)(2,1)S(1)}, bf16[128,3072]{1,0:T(8,128)(2,1)S(1)}, u32[]{:S(2)}, u32[]{:S(2)}) collective-permute-start(bf16[128,3072]{1,0:T(8,128)(2,1)S(1)} %collective-permute-done.m0), channel_id=1, source_target_pairs={{0,1},{1,0},{2,3},{3,2},{4,5},{5,4},{6,7},{7,6},{8,9},{9,8},{10,11... | collective-permute-start | bytes 2359304 | tf_op jit(solution)/shard_map/ppermute | solution.py:371
  28.1 7.1 %slice-start = ((s8[9437184]{0:T(1024)(128)(4,1)}), s8[4194304]{0:T(1024)(128)(4,1)S(1)}, s32[]{:S(2)}) async-start(s8[9437184]{0:T(1024)(128)(4,1)} %bitcast.3), calls=%async_computation | async-start | bytes 8388608
  28.1 7.1 %slice-start.1 = ((s8[9437184]{0:T(1024)(128)(4,1)}), s8[4194304]{0:T(1024)(128)(4,1)S(1)}, s32[]{:S(2)}) async-start(s8[9437184]{0:T(1024)(128)(4,1)} %bitcast.3), calls=%async_computation.1 | async-start | bytes 8388608
  28.1 7.1 %slice-start.2 = ((s8[9437184]{0:T(1024)(128)(4,1)}), s8[1048576]{0:T(1024)(128)(4,1)S(1)}, s32[]{:S(2)}) async-start(s8[9437184]{0:T(1024)(128)(4,1)} %bitcast.3), calls=%async_computation.2 | async-start | bytes 2097152
  28.1 7.2 %copy-start = (bf16[512,3072]{1,0:T(8,128)(2,1)S(1)}, bf16[512,3072]{1,0:T(8,128)(2,1)}, u32[]{:S(2)}) copy-start(bf16[512,3072]{1,0:T(8,128)(2,1)} %refs_17_.1) | copy-start | bytes 9437188
  36.9 1.9 %collective-permute-start.3 = (bf16[128,1152]{1,0:T(8,128)(2,1)S(1)}, bf16[128,1152]{1,0:T(8,128)(2,1)S(1)}, u32[]{:S(2)}, u32[]{:S(2)}) collective-permute-start(bf16[128,1152]{1,0:T(8,128)(2,1)S(1)} %get-tuple-element.93), channel_id=1, source_target_pairs={{0,1},{1,0},{2,3},{3,2},{4,5},{5,4},{6,7},{7,6},{8,9},{9,8},{10,11... | collective-permute-start | bytes 884744 | tf_op jit(solution)/shard_map/ppermute | solution.py:371
  38.8 12.4 %copy-start.3 = (f32[1,3072]{1,0:T(1,128)S(1)}, f32[1,3072]{1,0:T(1,128)}, u32[]{:S(2)}) copy-start(f32[1,3072]{1,0:T(1,128)} %get-tuple-element.115.sg) | copy-start | bytes 36868
  38.8 9.4 %collective-permute-start.4 = (bf16[128,1152]{1,0:T(8,128)(2,1)S(1)}, bf16[128,1152]{1,0:T(8,128)(2,1)S(1)}, u32[]{:S(2)}, u32[]{:S(2)}) collective-permute-start(bf16[128,1152]{1,0:T(8,128)(2,1)S(1)} %join.3), channel_id=1, source_target_pairs={{0,2},{1,3},{2,0},{3,1},{4,6},{5,7},{6,4},{7,5},{8,10},{9,11},{10,... | collective-permute-start | bytes 884744 | tf_op jit(solution)/shard_map/ppermute | solution.py:374
  44.4 0.7 copy-start.6
  44.4 1.5 %collective-permute-start.5 = (bf16[128,1024]{1,0:T(8,128)(2,1)S(1)}, bf16[128,1024]{1,0:T(8,128)(2,1)S(1)}, u32[]{:S(2)}, u32[]{:S(2)}) collective-permute-start(bf16[128,1024]{1,0:T(8,128)(2,1)S(1)} %get-tuple-element.107), channel_id=1, source_target_pairs={{0,1},{1,0},{2,3},{3,2},{4,5},{5,4},{6,7},{7,6},{8,9},{9,8},{10,11... | collective-permute-start | bytes 786440 | tf_op jit(solution)/shard_map/ppermute | solution.py:371
  45.1 6.1 %collective-permute-start.8 = (bf16[128,1152]{1,0:T(8,128)(2,1)S(1)}, bf16[128,1152]{1,0:T(8,128)(2,1)S(1)}, u32[]{:S(2)}, u32[]{:S(2)}) collective-permute-start(bf16[128,1152]{1,0:T(8,128)(2,1)S(1)} %get-tuple-element.118), channel_id=1, source_target_pairs={{0,1},{1,0},{2,3},{3,2},{4,5},{5,4},{6,7},{7,6},{8,9},{9,8},{10,11... | collective-permute-start | bytes 884744 | tf_op jit(solution)/shard_map/ppermute | solution.py:371
  49.0 8.0 %collective-permute-start.7 = (bf16[128,1024]{1,0:T(8,128)(2,1)}, bf16[128,1024]{1,0:T(8,128)(2,1)S(1)}, u32[]{:S(2)}, u32[]{:S(2)}) collective-permute-start(bf16[128,1024]{1,0:T(8,128)(2,1)} %join.4), channel_id=1, source_target_pairs={{0,2},{1,3},{2,0},{3,1},{4,6},{5,7},{6,4},{7,5},{8,10},{9,11},{10,... | collective-permute-start | bytes 786440 | tf_op jit(solution)/shard_map/ppermute | solution.py:374
  50.7 6.3 %collective-permute-start.6 = (bf16[128,1024]{1,0:T(8,128)(2,1)}, bf16[128,1024]{1,0:T(8,128)(2,1)}, u32[]{:S(2)}, u32[]{:S(2)}) collective-permute-start(bf16[128,1024]{1,0:T(8,128)(2,1)} %get-tuple-element.114), channel_id=1, source_target_pairs={{0,1},{1,0},{2,3},{3,2},{4,5},{5,4},{6,7},{7,6},{8,9},{9,8},{10,11... | collective-permute-start | bytes 786440 | tf_op jit(solution)/shard_map/ppermute | solution.py:371
  50.7 2.7 %collective-permute-start.11 = (bf16[128,896]{1,0:T(8,128)(2,1)}, bf16[128,896]{1,0:T(8,128)(2,1)}, u32[]{:S(2)}, u32[]{:S(2)}) collective-permute-start(bf16[128,896]{1,0:T(8,128)(2,1)} %get-tuple-element.127), channel_id=1, source_target_pairs={{0,1},{1,0},{2,3},{3,2},{4,5},{5,4},{6,7},{7,6},{8,9},{9,8},{10,11... | collective-permute-start | bytes 688136 | tf_op jit(solution)/shard_map/ppermute | solution.py:371
  51.9 8.5 %collective-permute-start.13 = (bf16[64,1152]{1,0:T(8,128)(2,1)}, bf16[64,1152]{1,0:T(8,128)(2,1)S(1)}, u32[]{:S(2)}, u32[]{:S(2)}) collective-permute-start(bf16[64,1152]{1,0:T(8,128)(2,1)} %get-tuple-element.120), channel_id=1, source_target_pairs={{0,4},{4,0},{8,12},{12,8},{16,20},{20,16},{24,28},{28,24},{1,5},{5... | collective-permute-start | bytes 442376 | tf_op jit(solution)/shard_map/ppermute | solution.py:377
  53.4 9.1 %collective-permute-start.10 = (bf16[128,896]{1,0:T(8,128)(2,1)}, bf16[128,896]{1,0:T(8,128)(2,1)S(1)}, u32[]{:S(2)}, u32[]{:S(2)}) collective-permute-start(bf16[128,896]{1,0:T(8,128)(2,1)} %copy-done.6), channel_id=1, source_target_pairs={{0,1},{1,0},{2,3},{3,2},{4,5},{5,4},{6,7},{7,6},{8,9},{9,8},{10,11... | collective-permute-start | bytes 688136 | tf_op jit(solution)/shard_map/ppermute | solution.py:371
  54.4 8.1 %collective-permute-start.12 = (bf16[128,896]{1,0:T(8,128)(2,1)S(1)}, bf16[128,896]{1,0:T(8,128)(2,1)S(1)}, u32[]{:S(2)}, u32[]{:S(2)}) collective-permute-start(bf16[128,896]{1,0:T(8,128)(2,1)S(1)} %join.5), channel_id=1, source_target_pairs={{0,2},{1,3},{2,0},{3,1},{4,6},{5,7},{6,4},{7,5},{8,10},{9,11},{10,... | collective-permute-start | bytes 688136 | tf_op jit(solution)/shard_map/ppermute | solution.py:374
  58.0 5.8 %collective-permute-start.9 = (bf16[64,1024]{1,0:T(8,128)(2,1)S(1)}, bf16[64,1024]{1,0:T(8,128)(2,1)S(1)}, u32[]{:S(2)}, u32[]{:S(2)}) collective-permute-start(bf16[64,1024]{1,0:T(8,128)(2,1)S(1)} %get-tuple-element.123), channel_id=1, source_target_pairs={{0,4},{4,0},{8,12},{12,8},{16,20},{20,16},{24,28},{28,24},{1,5},{5... | collective-permute-start | bytes 393224 | tf_op jit(solution)/shard_map/ppermute | solution.py:377
  60.5 26.4 %copy-start.1 = (f32[128,3072]{1,0:T(8,128)S(1)}, f32[128,3072]{1,0:T(8,128)}, u32[]{:S(2)}) copy-start(f32[128,3072]{1,0:T(8,128)} %x_start.3) | copy-start | bytes 4718596
  60.5 5.2 %collective-permute-start.16 = (bf16[64,1152]{1,0:T(8,128)(2,1)S(1)}, bf16[64,1152]{1,0:T(8,128)(2,1)S(1)}, u32[]{:S(2)}, u32[]{:S(2)}) collective-permute-start(bf16[64,1152]{1,0:T(8,128)(2,1)S(1)} %fusion.6), channel_id=1, source_target_pairs={{0,8},{4,12},{8,0},{12,4},{16,24},{20,28},{24,16},{28,20},{1,9},{5... | collective-permute-start | bytes 442376 | tf_op jit(solution)/shard_map/ppermute | solution.py:442
  62.6 5.8 %collective-permute-start.15 = (bf16[64,896]{1,0:T(8,128)(2,1)S(1)}, bf16[64,896]{1,0:T(8,128)(2,1)S(1)}, u32[]{:S(2)}, u32[]{:S(2)}) collective-permute-start(bf16[64,896]{1,0:T(8,128)(2,1)S(1)} %get-tuple-element.131), channel_id=1, source_target_pairs={{0,4},{4,0},{8,12},{12,8},{16,20},{20,16},{24,28},{28,24},{1,5},{5... | collective-permute-start | bytes 344072 | tf_op jit(solution)/shard_map/ppermute | solution.py:377
  63.9 7.1 %collective-permute-start.14 = (bf16[64,1024]{1,0:T(8,128)(2,1)S(1)}, bf16[64,1024]{1,0:T(8,128)(2,1)S(1)}, u32[]{:S(2)}, u32[]{:S(2)}) collective-permute-start(bf16[64,1024]{1,0:T(8,128)(2,1)S(1)} %fusion.7), channel_id=1, source_target_pairs={{0,8},{4,12},{8,0},{12,4},{16,24},{20,28},{24,16},{28,20},{1,9},{5... | collective-permute-start | bytes 393224 | tf_op jit(solution)/shard_map/ppermute | solution.py:442
  65.7 12.7 %collective-permute-start.18 = (bf16[64,1152]{1,0:T(8,128)(2,1)S(1)}, bf16[64,1152]{1,0:T(8,128)(2,1)S(1)}, u32[]{:S(2)}, u32[]{:S(2)}) collective-permute-start(bf16[64,1152]{1,0:T(8,128)(2,1)S(1)} %fusion), channel_id=1, source_target_pairs={{0,16},{4,20},{8,24},{12,28},{16,0},{20,4},{24,8},{28,12},{1,17},{... | collective-permute-start | bytes 442376 | tf_op jit(solution)/shard_map/ppermute | solution.py:442
  68.4 6.7 %collective-permute-start.19 = (bf16[64,896]{1,0:T(8,128)(2,1)S(1)}, bf16[64,896]{1,0:T(8,128)(2,1)S(1)}, u32[]{:S(2)}, u32[]{:S(2)}) collective-permute-start(bf16[64,896]{1,0:T(8,128)(2,1)S(1)} %fusion.8), channel_id=1, source_target_pairs={{0,8},{4,12},{8,0},{12,4},{16,24},{20,28},{24,16},{28,20},{1,9},{5... | collective-permute-start | bytes 344072 | tf_op jit(solution)/shard_map/ppermute | solution.py:442
  71.1 12.8 %collective-permute-start.17 = (bf16[64,1024]{1,0:T(8,128)(2,1)S(1)}, bf16[64,1024]{1,0:T(8,128)(2,1)S(1)}, u32[]{:S(2)}, u32[]{:S(2)}) collective-permute-start(bf16[64,1024]{1,0:T(8,128)(2,1)S(1)} %fusion.3), channel_id=1, source_target_pairs={{0,16},{4,20},{8,24},{12,28},{16,0},{20,4},{24,8},{28,12},{1,17},{... | collective-permute-start | bytes 393224 | tf_op jit(solution)/shard_map/ppermute | solution.py:442
  75.1 10.5 %collective-permute-start.21 = (bf16[64,896]{1,0:T(8,128)(2,1)S(1)}, bf16[64,896]{1,0:T(8,128)(2,1)S(1)}, u32[]{:S(2)}, u32[]{:S(2)}) collective-permute-start(bf16[64,896]{1,0:T(8,128)(2,1)S(1)} %fusion.4), channel_id=1, source_target_pairs={{0,16},{4,20},{8,24},{12,28},{16,0},{20,4},{24,8},{28,12},{1,17},{... | collective-permute-start | bytes 344072 | tf_op jit(solution)/shard_map/ppermute | solution.py:442
  78.6 8.3 %collective-permute-start.23 = (bf16[64,1152]{1,0:T(8,128)(2,1)S(1)}, bf16[64,1152]{1,0:T(8,128)(2,1)S(1)}, u32[]{:S(2)}, u32[]{:S(2)}) collective-permute-start(bf16[64,1152]{1,0:T(8,128)(2,1)S(1)} %get-tuple-element.149), channel_id=1, source_target_pairs={{0,4},{4,0},{8,12},{12,8},{16,20},{20,16},{24,28},{28,24},{1,5},{5... | collective-permute-start | bytes 442376 | tf_op jit(solution)/shard_map/ppermute | solution.py:377
  84.0 6.6 %collective-permute-start.20 = (bf16[64,1024]{1,0:T(8,128)(2,1)S(1)}, bf16[64,1024]{1,0:T(8,128)(2,1)S(1)}, u32[]{:S(2)}, u32[]{:S(2)}) collective-permute-start(bf16[64,1024]{1,0:T(8,128)(2,1)S(1)} %get-tuple-element.147), channel_id=1, source_target_pairs={{0,4},{4,0},{8,12},{12,8},{16,20},{20,16},{24,28},{28,24},{1,5},{5... | collective-permute-start | bytes 393224 | tf_op jit(solution)/shard_map/ppermute | solution.py:377
  85.7 4.9 %collective-permute-start.22 = (bf16[64,896]{1,0:T(8,128)(2,1)S(1)}, bf16[64,896]{1,0:T(8,128)(2,1)S(1)}, u32[]{:S(2)}, u32[]{:S(2)}) collective-permute-start(bf16[64,896]{1,0:T(8,128)(2,1)S(1)} %get-tuple-element.145), channel_id=1, source_target_pairs={{0,4},{4,0},{8,12},{12,8},{16,20},{20,16},{24,28},{28,24},{1,5},{5... | collective-permute-start | bytes 344072 | tf_op jit(solution)/shard_map/ppermute | solution.py:377

commit v13 on v12

--- a/solution.py
+++ b/solution.py
@@ -23,7 +23,7 @@
     return pl.CostEstimate(flops=flops, transcendentals=0, bytes_accessed=moved)
 
 
-def norm_kernel(t_ref, size_ref, x_hbm, mod_hbm, m_ref, sg_ref, x_ref, mod_ref, sem):
+def norm_kernel(t_ref, size_ref, x_hbm, mod_hbm, m_hbm, sg_ref, x_ref, m_ref, mod_ref, sem, out_sem):
     width = x_hbm.shape[-1]
     pieces = sem.shape[0] - 1
     block = x_hbm.shape[1] // pieces
@@ -46,6 +46,11 @@
         center = x - jnp.mean(x, axis=-1, keepdims=True)
         spread = jnp.mean(center * center, axis=-1, keepdims=True)
         m_ref[here, :] = (center * lax.rsqrt(spread + eps) * scale + shift).astype(bf16)
+        rows = pl.ds(i * block, block)
+        copies[i] = pltpu.make_async_copy(m_ref.at[rows, :], m_hbm.at[rows, :], out_sem.at[i])
+        copies[i].start()
+    for copy in copies:
+        copy.wait()
 
 
 def norm_call(t_idx, trajectory, mod_table, step_sizes):
@@ -56,15 +61,17 @@
     return pl.pallas_call(
         norm_kernel,
         in_specs=[smem, smem, hbm, hbm],
-        out_specs=[vm, vm],
+        out_specs=[hbm, vm],
         out_shape=[
             jax.ShapeDtypeStruct((rows, width), bf16),
             jax.ShapeDtypeStruct((1, width), f32),
         ],
         scratch_shapes=[
             VM((rows, width), f32),
+            VM((rows, width), bf16),
             VM((1, 3 * width), f32),
             pltpu.SemaphoreType.DMA((5,)),
+            pltpu.SemaphoreType.DMA((4,)),
         ],
         compiler_params=params(60),
         cost_estimate=cost(10 * rows * width, 0),
@@ -166,24 +173,28 @@
     v_refs = refs[1 + pairs : 1 + 2 * pairs]
     out = refs[1 + 2 * pairs]
     scale = math.log2(math.e) / math.sqrt(head)
-    for h in range(q_ref.shape[1] // head):
-        cols = slice(h * head, (h + 1) * head)
-        q = q_ref[:, cols]
-        scores = [
-            lax.dot_general(q, k[:, cols], (((1,), (1,)), ((), ())), preferred_element_type=f32)
+    heads = [slice(at, at + head) for at in range(0, q_ref.shape[1], head)]
+    scores = [
+        [
+            lax.dot_general(
+                q_ref[:, cols], k[:, cols], (((1,), (1,)), ((), ())), preferred_element_type=f32
+            )
             for k in k_refs
         ]
-        top = functools.reduce(
-            jnp.maximum, [jnp.max(s, axis=-1, keepdims=True) for s in scores]
+        for cols in heads
+    ]
+    tops = [
+        functools.reduce(jnp.maximum, [jnp.max(s, axis=-1, keepdims=True) for s in one])
+        for one in scores
+    ]
+    weights = [[jnp.exp2((s - top) * scale) for s in one] for one, top in zip(scores, tops)]
+    totals = [sum(jnp.sum(w, axis=-1, keepdims=True) for w in one) for one in weights]
+    for cols, one, total in zip(heads, weights, totals):
+        mixed = sum(
+            jnp.dot(w.astype(bf16), v[:, cols], preferred_element_type=f32)
+            for w, v in zip(one, v_refs)
         )
-        weights = [jnp.exp2((s - top) * scale) for s in scores]
-        total = sum(jnp.sum(w, axis=-1, keepdims=True) for w in weights)
-        inverse = 1.0 / total
-        mixed = sum(
-            jnp.dot((w * inverse).astype(bf16), v[:, cols], preferred_element_type=f32)
-            for w, v in zip(weights, v_refs)
-        )
-        out[:, cols] = mixed.astype(bf16)
+        out[:, cols] = (mixed / total).astype(bf16)
 
 
 def attend_call(q, ks, vs, head):

time: 92 us -> 91 us (0.989)
  waiting for transfers between devices: 21.9 us -> 23.3 us
  starting transfers between devices: 30.8 us -> 29.5 us
  Pallas kernels: 35.8 us -> 34.7 us
    pallas_call x2, Pallas kernels: 3.58 us -> 1.97 us  [attend_call(): pl.pallas_call(functools.partial(attend_kernel, len(ks), head), in_specs=...]
    ppermute x6, starting transfers between devices: 13.7 us -> 12.7 us  [along(): lax.ppermute(x, 'step', [(2 * a + i, 2 * b + i) for a, b in pairs for i i...]
where the time goes in v13:
time: 91 us; the launch traced here: 90.8 us
  Pallas kernels  34.7 us (38%)
  starting transfers between devices  29.5 us (32%)
  waiting for transfers between devices  23.3 us (26%)
  local copies, waits for them, and re-layouts  1.87 us (2%)
  between operations  1.04 us (1%)
    pallas_call x2, Pallas kernels, project_call(): pl.pallas_call(functools.partial(project_kernel, tile, load, tiles), in_s...  17.6 us
    ppermute x6, starting transfers between devices, along(): lax.ppermute(x, 'step', [(2 * a + i, 2 * b + i) for a, b in pairs for i i...  12.7 us
    ppermute x4, waiting for transfers between devices, to_chip(): lax.ppermute(x, 'seq', [(i, (i + 2 * offset) % n_seq) for i in range(n_se...  9.52 us
    ppermute x6, starting transfers between devices, to_pair(): return lax.ppermute(x, 'step', [(i, i ^ 1) for i in range(n_step)])  8.76 us
    ppermute x6, waiting for transfers between devices, along(): lax.ppermute(x, 'step', [(2 * a + i, 2 * b + i) for a, b in pairs for i i...  6.83 us
    ppermute x4, starting transfers between devices, to_chip(): lax.ppermute(x, 'seq', [(i, (i + 2 * offset) % n_seq) for i in range(n_se...  6.74 us
    pallas_call x2, Pallas kernels, out_call(): pl.pallas_call(functools.partial(out_kernel, plan), in_specs=[vm] * len(g...  5.25 us
    pallas_call x1, Pallas kernels, norm_call(): pl.pallas_call(norm_kernel, in_specs=[smem, smem, hbm, hbm], out_specs=[h...  4.18 us
  transfers between devices with their start and end apart: 24, of which 11 were waited for; matrix products, arithmetic and copies ran while one was open for 0% of the time, Pallas kernels for 24%

profile of v13, /device:TPU:0, one launch (start us, length us, event | category | flops | bytes accessed | tf_op | source)
XLA Modules:
  0.0 90.8 jit_solution(2800711225622496409)
XLA Ops:
  0.7 4.2 %norm.1 = (bf16[128,3072]{1,0:T(8,128)(2,1)}, f32[1,3072]{1,0:T(1,128)}) custom-call(s32[1]{0:T(128)S(6)} %copy.14.t_ref, f32[50]{0:T(128)} %size_ref.1, f32[1,128,3072]{2,1,0:T(8,128)} %x_hbm.1, f32[50,9216]{1,0:T(8,128)} %mod_hbm.1), custom_call_target="tpu_custom_call" | custom-call | flops 3932160 | tf_op jit(solution)/shard_map/norm/pallas_call | solution.py:61
  4.9 0.5 collective-permute-start.1
  5.4 2.6 %collective-permute-start = (bf16[128,3072]{1,0:T(8,128)(2,1)}, bf16[128,3072]{1,0:T(8,128)(2,1)S(1)}, u32[]{:S(2)}, u32[]{:S(2)}) collective-permute-start(bf16[128,3072]{1,0:T(8,128)(2,1)} %get-tuple-element.75.m0), channel_id=1, source_target_pairs={{0,2},{1,3},{2,0},{3,1},{4,6},{5,7},{6,4},{7,5},{8,10},{9,11},{10,... | collective-permute-start | bytes 2359304 | tf_op jit(solution)/shard_map/ppermute | solution.py:385
  8.0 0.0 collective-permute-done.1.m1
  8.0 0.0 copy-start.2
  8.0 1.1 %copy-done.2 = bf16[128,3072]{1,0:T(8,128)(2,1)S(1)} copy-done((bf16[128,3072]{1,0:T(8,128)(2,1)S(1)}, bf16[128,3072]{1,0:T(8,128)(2,1)}, u32[]{:S(2)}) %copy-start.2) | copy-done | bytes 786456
  9.2 12.4 %project.2 = (bf16[256,512]{1,0:T(8,128)(2,1)S(1)}, bf16[256,512]{1,0:T(8,128)(2,1)S(1)}, bf16[256,512]{1,0:T(8,128)(2,1)S(1)}, bf16[256,1536]{1,0:T(8,128)(2,1)...) custom-call(bf16[128,3072]{1,0:T(8,128)(2,1)S(1)} %copy-done.2, ...), custom_call_target="tpu_custom_call" | custom-call | flops 4831838208 | tf_op jit(solution)/shard_map/project/pallas_call | solution.py:158
  21.5 4.8 %collective-permute-done.m0 = bf16[128,3072]{1,0:T(8,128)(2,1)S(1)} collective-permute-done((bf16[128,3072]{1,0:T(8,128)(2,1)}, bf16[128,3072]{1,0:T(8,128)(2,1)S(1)}, u32[]{:S(2)}, u32[]{:S(2)}) %collective-permute-start) | collective-permute-done | bytes 786464 | tf_op jit(solution)/shard_map/ppermute | solution.py:385
  26.3 0.0 collective-permute-start.2
  26.3 2.3 %collective-permute-done.2.m1 = bf16[128,3072]{1,0:T(8,128)(2,1)S(1)} collective-permute-done((bf16[128,3072]{1,0:T(8,128)(2,1)S(1)}, bf16[128,3072]{1,0:T(8,128)(2,1)S(1)}, u32[]{:S(2)}, u32[]{:S(2)}) %collective-permute-start.2) | collective-permute-done | bytes 786464 | tf_op jit(solution)/shard_map/ppermute | solution.py:382
  28.6 5.2 %project.3 = (bf16[256,512]{1,0:T(8,128)(2,1)S(1)}, bf16[256,512]{1,0:T(8,128)(2,1)S(1)}, bf16[256,512]{1,0:T(8,128)(2,1)S(1)}, bf16[256,1536]{1,0:T(8,128)(2,1)S(1)}) custom-call(bf16[128,3072]{1,0:T(8,128)(2,1)S(1)} %collective-permute-done.m0, bf16[128,3072]{1,0:T(8,128)(2,1)S(1)} %collective-permute-done.2.m1, f32[1,128]{1,0:T(1,128)S(1)} %bitcast.6, ...), custom_call_target="tpu_custom_call" | custom-call | flops 4831838208 | tf_op jit(solution)/shard_map/project/pallas_call | solution.py:158
  33.9 1.1 %attend.2.refs_0_.refs_4_ = bf16[256,512]{1,0:T(8,128)(2,1)S(1)} custom-call(bf16[256,512]{1,0:T(8,128)(2,1)S(1)} %get-tuple-element.85.refs_0_, bf16[256,512]{1,0:T(8,128)(2,1)S(1)} %get-tuple-element.86.refs_1_, bf16[256,512]{1,0:T(8,128)(2,1)S(1)} %get-tuple-element.87.refs_2_, bf16[256,512]{1,0:T(8,128)(2,1)S(1)} %get-tuple-element.88.refs_3_, ...), custom_call_target="tpu_custom_call" | custom-call | flops 805306368 | tf_op jit(solution)/shard_map/attend/pallas_call | solution.py:202
  35.0 1.5 %project_out.2 = (f32[128,1152]{1,0:T(8,128)S(1)}, bf16[128,1152]{1,0:T(8,128)(2,1)S(1)}) custom-call(bf16[256,512]{1,0:T(8,128)(2,1)S(1)} %attend.2.refs_0_.refs_4_, bf16[256,1536]{1,0:T(8,128)(2,1)S(1)} %get-tuple-element.100.refs_1_.refs_5_, bf16[512,3072]{1,0:T(8,128)(2,1)S(1)} %copy-done, bf16[1536,3072]{1,0:T(8,128)(2,1)S(1)} %bitcast.4), custom_call_target="tpu_custom_call" | custom-call | flops 1207959552 | tf_op jit(solution)/shard_map/project_out/pallas_call | solution.py:246
  36.5 0.2 collective-permute-start.3
  36.7 0.9 attend.3.refs_8_.refs_12_.refs_16_
  37.6 0.6 collective-permute-done.3.sent
  38.2 0.1 join.3
  38.3 1.8 %collective-permute-start.4 = (bf16[128,1152]{1,0:T(8,128)(2,1)S(1)}, bf16[128,1152]{1,0:T(8,128)(2,1)S(1)}, u32[]{:S(2)}, u32[]{:S(2)}) collective-permute-start(bf16[128,1152]{1,0:T(8,128)(2,1)S(1)} %join.3), channel_id=1, source_target_pairs={{0,2},{1,3},{2,0},{3,1},{4,6},{5,7},{6,4},{7,5},{8,10},{9,11},{10,... | collective-permute-start | bytes 884744 | tf_op jit(solution)/shard_map/ppermute | solution.py:385
  40.1 3.7 %project_out.3 = (f32[128,1024]{1,0:T(8,128)S(1)}, bf16[128,1024]{1,0:T(8,128)(2,1)S(1)}, f32[128,896]{1,0:T(8,128)S(1)}, bf16[128,896]{1,0:T(8,128)(2,1)}, f32[...) custom-call(bf16[256,512]{1,0:T(8,128)(2,1)S(1)} %attend.2.refs_0_.r, ...), custom_call_target="tpu_custom_call" | custom-call | flops 2818572288 | tf_op jit(solution)/shard_map/project_out/pallas_call | solution.py:246
  43.8 0.7 copy-done.6
  44.5 0.8 collective-permute-done.5.sent
  45.3 2.1 %collective-permute-done.4.refs_0_ = bf16[128,1152]{1,0:T(8,128)(2,1)S(1)} collective-permute-done((bf16[128,1152]{1,0:T(8,128)(2,1)S(1)}, bf16[128,1152]{1,0:T(8,128)(2,1)S(1)}, u32[]{:S(2)}, u32[]{:S(2)}) %collective-permute-start.4) | collective-permute-done | bytes 294944 | tf_op jit(solution)/shard_map/ppermute | solution.py:385
  47.4 0.8 join.4
  48.2 1.7 %collective-permute-start.7 = (bf16[128,1024]{1,0:T(8,128)(2,1)}, bf16[128,1024]{1,0:T(8,128)(2,1)S(1)}, u32[]{:S(2)}, u32[]{:S(2)}) collective-permute-start(bf16[128,1024]{1,0:T(8,128)(2,1)} %join.4), channel_id=1, source_target_pairs={{0,2},{1,3},{2,0},{3,1},{4,6},{5,7},{6,4},{7,5},{8,10},{9,11},{10,... | collective-permute-start | bytes 786440 | tf_op jit(solution)/shard_map/ppermute | solution.py:385
  49.9 0.5 collective-permute-start.11
  50.4 0.0 collective-permute-done.8.sent
  50.4 0.7 drift.3
  51.1 1.5 %collective-permute-start.13 = (bf16[64,1152]{1,0:T(8,128)(2,1)}, bf16[64,1152]{1,0:T(8,128)(2,1)S(1)}, u32[]{:S(2)}, u32[]{:S(2)}) collective-permute-start(bf16[64,1152]{1,0:T(8,128)(2,1)} %get-tuple-element.120), channel_id=1, source_target_pairs={{0,4},{4,0},{8,12},{12,8},{16,20},{20,16},{24,28},{28,24},{1,5},{5... | collective-permute-start | bytes 442376 | tf_op jit(solution)/shard_map/ppermute | solution.py:388
  52.6 0.0 collective-permute-done.11.sent
  52.6 1.0 %join.5 = bf16[128,896]{1,0:T(8,128)(2,1)S(1)} custom-call(f32[128,896]{1,0:T(8,128)S(1)} %get-tuple-element.126.keep, bf16[128,896]{1,0:T(8,128)(2,1)} %collective-permute-done.11.sent), custom_call_target="tpu_custom_call" | custom-call | tf_op jit(solution)/shard_map/join/pallas_call | solution.py:264
  53.6 0.6 collective-permute-start.12
  54.2 1.7 %collective-permute-done.7.refs_0_ = bf16[128,1024]{1,0:T(8,128)(2,1)S(1)} collective-permute-done((bf16[128,1024]{1,0:T(8,128)(2,1)}, bf16[128,1024]{1,0:T(8,128)(2,1)S(1)}, u32[]{:S(2)}, u32[]{:S(2)}) %collective-permute-start.7) | collective-permute-done | bytes 262176 | tf_op jit(solution)/shard_map/ppermute | solution.py:385
  55.9 0.0 collective-permute-done.6.sent
  55.9 1.0 %drift.4 = (f32[64,1024]{1,0:T(8,128)S(1)}, f32[64,1024]{1,0:T(8,128)S(1)}, bf16[64,1024]{1,0:T(8,128)(2,1)S(1)}) custom-call(s32[1]{0:T(128)} %bitcast.parity, f32[128,1024]{1,0:T(8,128)S(1)} %get-tuple-element.113.keep, bf16[128,1024]{1,0:T(8,128)(2,1)} %collective-permute-done.6.sent, f32[1,3072]{1,0:T(1,128)S(1)} %copy-done.3, ...), custom_call_target="tpu_custom_call" | custom-call | tf_op jit(solution)/shard_map/drift/pallas_call | solution.py:297
  57.0 2.1 %collective-permute-start.9 = (bf16[64,1024]{1,0:T(8,128)(2,1)S(1)}, bf16[64,1024]{1,0:T(8,128)(2,1)S(1)}, u32[]{:S(2)}, u32[]{:S(2)}) collective-permute-start(bf16[64,1024]{1,0:T(8,128)(2,1)S(1)} %get-tuple-element.123), channel_id=1, source_target_pairs={{0,4},{4,0},{8,12},{12,8},{16,20},{20,16},{24,28},{28,24},{1,5},{5... | collective-permute-start | bytes 393224 | tf_op jit(solution)/shard_map/ppermute | solution.py:388
  59.1 0.0 copy-start.1
  59.1 1.6 %collective-permute-start.16 = (bf16[64,1152]{1,0:T(8,128)(2,1)S(1)}, bf16[64,1152]{1,0:T(8,128)(2,1)S(1)}, u32[]{:S(2)}, u32[]{:S(2)}) collective-permute-start(bf16[64,1152]{1,0:T(8,128)(2,1)S(1)} %fusion.6), channel_id=1, source_target_pairs={{0,8},{4,12},{8,0},{12,4},{16,24},{20,28},{24,16},{28,20},{1,9},{5... | collective-permute-start | bytes 442376 | tf_op jit(solution)/shard_map/ppermute | solution.py:453
  60.7 1.0 %collective-permute-done.12.refs_0_ = bf16[128,896]{1,0:T(8,128)(2,1)S(1)} collective-permute-done((bf16[128,896]{1,0:T(8,128)(2,1)S(1)}, bf16[128,896]{1,0:T(8,128)(2,1)S(1)}, u32[]{:S(2)}, u32[]{:S(2)}) %collective-permute-start.12) | collective-permute-done | bytes 229408 | tf_op jit(solution)/shard_map/ppermute | solution.py:385
  61.7 0.0 collective-permute-done.10.sent
  61.7 0.1 drift.5
  61.8 0.9 collective-permute-start.15
  62.7 0.0 collective-permute-done.9.refs_2_
  62.7 1.6 %collective-permute-start.14 = (bf16[64,1024]{1,0:T(8,128)(2,1)S(1)}, bf16[64,1024]{1,0:T(8,128)(2,1)S(1)}, u32[]{:S(2)}, u32[]{:S(2)}) collective-permute-start(bf16[64,1024]{1,0:T(8,128)(2,1)S(1)} %fusion.7), channel_id=1, source_target_pairs={{0,8},{4,12},{8,0},{12,4},{16,24},{20,28},{24,16},{28,20},{1,9},{5... | collective-permute-start | bytes 393224 | tf_op jit(solution)/shard_map/ppermute | solution.py:453
  64.4 0.0 collective-permute-done.16
  64.4 0.1 fusion
  64.4 2.6 %collective-permute-start.18 = (bf16[64,1152]{1,0:T(8,128)(2,1)S(1)}, bf16[64,1152]{1,0:T(8,128)(2,1)S(1)}, u32[]{:S(2)}, u32[]{:S(2)}) collective-permute-start(bf16[64,1152]{1,0:T(8,128)(2,1)S(1)} %fusion), channel_id=1, source_target_pairs={{0,16},{4,20},{8,24},{12,28},{16,0},{20,4},{24,8},{28,12},{1,17},{... | collective-permute-start | bytes 442376 | tf_op jit(solution)/shard_map/ppermute | solution.py:453
  67.1 1.6 %collective-permute-start.19 = (bf16[64,896]{1,0:T(8,128)(2,1)S(1)}, bf16[64,896]{1,0:T(8,128)(2,1)S(1)}, u32[]{:S(2)}, u32[]{:S(2)}) collective-permute-start(bf16[64,896]{1,0:T(8,128)(2,1)S(1)} %fusion.8), channel_id=1, source_target_pairs={{0,8},{4,12},{8,0},{12,4},{16,24},{20,28},{24,16},{28,20},{1,9},{5... | collective-permute-start | bytes 344072 | tf_op jit(solution)/shard_map/ppermute | solution.py:453
  68.7 1.2 %collective-permute-done.14 = bf16[64,1024]{1,0:T(8,128)(2,1)S(1)} collective-permute-done((bf16[64,1024]{1,0:T(8,128)(2,1)S(1)}, bf16[64,1024]{1,0:T(8,128)(2,1)S(1)}, u32[]{:S(2)}, u32[]{:S(2)}) %collective-permute-start.14) | collective-permute-done | bytes 131104 | tf_op jit(solution)/shard_map/ppermute | solution.py:453
  69.9 0.1 fusion.3
  69.9 2.0 %collective-permute-start.17 = (bf16[64,1024]{1,0:T(8,128)(2,1)S(1)}, bf16[64,1024]{1,0:T(8,128)(2,1)S(1)}, u32[]{:S(2)}, u32[]{:S(2)}) collective-permute-start(bf16[64,1024]{1,0:T(8,128)(2,1)S(1)} %fusion.3), channel_id=1, source_target_pairs={{0,16},{4,20},{8,24},{12,28},{16,0},{20,4},{24,8},{28,12},{1,17},{... | collective-permute-start | bytes 393224 | tf_op jit(solution)/shard_map/ppermute | solution.py:453
  72.0 1.9 %collective-permute-done.19 = bf16[64,896]{1,0:T(8,128)(2,1)S(1)} collective-permute-done((bf16[64,896]{1,0:T(8,128)(2,1)S(1)}, bf16[64,896]{1,0:T(8,128)(2,1)S(1)}, u32[]{:S(2)}, u32[]{:S(2)}) %collective-permute-start.19) | collective-permute-done | bytes 114720 | tf_op jit(solution)/shard_map/ppermute | solution.py:453
  73.9 3.2 %collective-permute-start.21 = (bf16[64,896]{1,0:T(8,128)(2,1)S(1)}, bf16[64,896]{1,0:T(8,128)(2,1)S(1)}, u32[]{:S(2)}, u32[]{:S(2)}) collective-permute-start(bf16[64,896]{1,0:T(8,128)(2,1)S(1)} %fusion.4), channel_id=1, source_target_pairs={{0,16},{4,20},{8,24},{12,28},{16,0},{20,4},{24,8},{28,12},{1,17},{... | collective-permute-start | bytes 344072 | tf_op jit(solution)/shard_map/ppermute | solution.py:453
  77.1 0.1 add_convert_fusion
  77.2 1.5 %collective-permute-start.23 = (bf16[64,1152]{1,0:T(8,128)(2,1)S(1)}, bf16[64,1152]{1,0:T(8,128)(2,1)S(1)}, u32[]{:S(2)}, u32[]{:S(2)}) collective-permute-start(bf16[64,1152]{1,0:T(8,128)(2,1)S(1)} %get-tuple-element.149), channel_id=1, source_target_pairs={{0,4},{4,0},{8,12},{12,8},{16,20},{20,16},{24,28},{28,24},{1,5},{5... | collective-permute-start | bytes 442376 | tf_op jit(solution)/shard_map/ppermute | solution.py:388
  78.7 3.7 %collective-permute-done.17 = bf16[64,1024]{1,0:T(8,128)(2,1)S(1)} collective-permute-done((bf16[64,1024]{1,0:T(8,128)(2,1)S(1)}, bf16[64,1024]{1,0:T(8,128)(2,1)S(1)}, u32[]{:S(2)}, u32[]{:S(2)}) %collective-permute-start.17) | collective-permute-done | bytes 131104 | tf_op jit(solution)/shard_map/ppermute | solution.py:453
  82.4 0.1 add_convert_fusion.1
  82.5 1.6 %collective-permute-start.20 = (bf16[64,1024]{1,0:T(8,128)(2,1)S(1)}, bf16[64,1024]{1,0:T(8,128)(2,1)S(1)}, u32[]{:S(2)}, u32[]{:S(2)}) collective-permute-start(bf16[64,1024]{1,0:T(8,128)(2,1)S(1)} %get-tuple-element.147), channel_id=1, source_target_pairs={{0,4},{4,0},{8,12},{12,8},{16,20},{20,16},{24,28},{28,24},{1,5},{5... | collective-permute-start | bytes 393224 | tf_op jit(solution)/shard_map/ppermute | solution.py:388
  84.1 0.0 collective-permute-done.21
  84.1 0.1 add_convert_fusion.2
  84.2 1.2 %collective-permute-start.22 = (bf16[64,896]{1,0:T(8,128)(2,1)S(1)}, bf16[64,896]{1,0:T(8,128)(2,1)S(1)}, u32[]{:S(2)}, u32[]{:S(2)}) collective-permute-start(bf16[64,896]{1,0:T(8,128)(2,1)S(1)} %get-tuple-element.145), channel_id=1, source_target_pairs={{0,4},{4,0},{8,12},{12,8},{16,20},{20,16},{24,28},{28,24},{1,5},{5... | collective-permute-start | bytes 344072 | tf_op jit(solution)/shard_map/ppermute | solution.py:388
  85.4 0.0 collective-permute-done.23.refs_4_
  85.4 0.9 %finish.2.refs_10_ = f32[1,128,3072]{2,1,0:T(8,128)} custom-call(s32[1]{0:T(128)} %bitcast.parity, f32[128,3072]{1,0:T(8,128)S(1)} %copy-done.1, f32[64,1152]{1,0:T(8,128)S(1)} %get-tuple-element.150.refs_0_, f32[64,1152]{1,0:T(8,128)S(1)} %get-tuple-element.128.refs_1_, bf16[64,1152]{1,0:T(8,128)(2,1)S(1)} %collective-permute-done.13.refs_2_, ...), custom_call_target="tpu_custom_call" | custom-call | tf_op jit(solution)/shard_map/finish/pallas_call | solution.py:342
  86.3 3.2 %collective-permute-done.22.refs_9_ = bf16[64,896]{1,0:T(8,128)(2,1)S(1)} collective-permute-done((bf16[64,896]{1,0:T(8,128)(2,1)S(1)}, bf16[64,896]{1,0:T(8,128)(2,1)S(1)}, u32[]{:S(2)}, u32[]{:S(2)}) %collective-permute-start.22) | collective-permute-done | bytes 114720 | tf_op jit(solution)/shard_map/ppermute | solution.py:388
  89.6 1.1 %finish.3 = f32[1,128,3072]{2,1,0:T(8,128)} custom-call(s32[1]{0:T(128)} %bitcast.parity, f32[128,3072]{1,0:T(8,128)S(1)} %copy-done.1, f32[64,1024]{1,0:T(8,128)S(1)} %get-tuple-element.148.refs_0_, f32[64,1024]{1,0:T(8,128)S(1)} %get-tuple-element.122.refs_1_, ...), custom_call_target="tpu_custom_call", output_to_operand_aliasing={{}: (12, {})} | custom-call | tf_op jit(solution)/shard_map/finish/pallas_call | solution.py:342
  (29 shorter events, 0.2 us)
Async XLA Ops:
  0.0 8.0 %copy-start.4 = (f32[128]{0:T(128)S(1)}, f32[128]{0:T(128)}, u32[]{:S(2)}) copy-start(f32[128]{0:T(128)} %param.16) | copy-start | bytes 1540
  0.0 8.0 %copy-start.5 = (f32[128]{0:T(128)S(1)}, f32[128]{0:T(128)}, u32[]{:S(2)}) copy-start(f32[128]{0:T(128)} %param.17) | copy-start | bytes 1540
  4.9 3.1 %collective-permute-start.1 = (bf16[128,3072]{1,0:T(8,128)(2,1)}, bf16[128,3072]{1,0:T(8,128)(2,1)S(1)}, u32[]{:S(2)}, u32[]{:S(2)}) collective-permute-start(bf16[128,3072]{1,0:T(8,128)(2,1)} %get-tuple-element.75.m0), channel_id=1, source_target_pairs={{0,1},{1,0},{2,3},{3,2},{4,5},{5,4},{6,7},{7,6},{8,9},{9,8},{10,11... | collective-permute-start | bytes 2359304 | tf_op jit(solution)/shard_map/ppermute | solution.py:382
  5.4 20.9 %collective-permute-start = (bf16[128,3072]{1,0:T(8,128)(2,1)}, bf16[128,3072]{1,0:T(8,128)(2,1)S(1)}, u32[]{:S(2)}, u32[]{:S(2)}) collective-permute-start(bf16[128,3072]{1,0:T(8,128)(2,1)} %get-tuple-element.75.m0), channel_id=1, source_target_pairs={{0,2},{1,3},{2,0},{3,1},{4,6},{5,7},{6,4},{7,5},{8,10},{9,11},{10,... | collective-permute-start | bytes 2359304 | tf_op jit(solution)/shard_map/ppermute | solution.py:385
  8.0 1.2 %copy-start.2 = (bf16[128,3072]{1,0:T(8,128)(2,1)S(1)}, bf16[128,3072]{1,0:T(8,128)(2,1)}, u32[]{:S(2)}) copy-start(bf16[128,3072]{1,0:T(8,128)(2,1)} %get-tuple-element.75.m0) | copy-start | bytes 2359300
  26.3 2.3 %collective-permute-start.2 = (bf16[128,3072]{1,0:T(8,128)(2,1)S(1)}, bf16[128,3072]{1,0:T(8,128)(2,1)S(1)}, u32[]{:S(2)}, u32[]{:S(2)}) collective-permute-start(bf16[128,3072]{1,0:T(8,128)(2,1)S(1)} %collective-permute-done.m0), channel_id=1, source_target_pairs={{0,1},{1,0},{2,3},{3,2},{4,5},{5,4},{6,7},{7,6},{8,9},{9,8},{10,11... | collective-permute-start | bytes 2359304 | tf_op jit(solution)/shard_map/ppermute | solution.py:382
  28.6 6.3 %slice-start = ((s8[9437184]{0:T(1024)(128)(4,1)}), s8[4194304]{0:T(1024)(128)(4,1)S(1)}, s32[]{:S(2)}) async-start(s8[9437184]{0:T(1024)(128)(4,1)} %bitcast.3), calls=%async_computation | async-start | bytes 8388608
  28.6 6.4 %slice-start.1 = ((s8[9437184]{0:T(1024)(128)(4,1)}), s8[4194304]{0:T(1024)(128)(4,1)S(1)}, s32[]{:S(2)}) async-start(s8[9437184]{0:T(1024)(128)(4,1)} %bitcast.3), calls=%async_computation.1 | async-start | bytes 8388608
  28.6 6.4 %slice-start.2 = ((s8[9437184]{0:T(1024)(128)(4,1)}), s8[1048576]{0:T(1024)(128)(4,1)S(1)}, s32[]{:S(2)}) async-start(s8[9437184]{0:T(1024)(128)(4,1)} %bitcast.3), calls=%async_computation.2 | async-start | bytes 2097152
  28.6 6.4 %copy-start = (bf16[512,3072]{1,0:T(8,128)(2,1)S(1)}, bf16[512,3072]{1,0:T(8,128)(2,1)}, u32[]{:S(2)}) copy-start(bf16[512,3072]{1,0:T(8,128)(2,1)} %refs_17_.1) | copy-start | bytes 9437188
  36.5 1.6 %collective-permute-start.3 = (bf16[128,1152]{1,0:T(8,128)(2,1)S(1)}, bf16[128,1152]{1,0:T(8,128)(2,1)S(1)}, u32[]{:S(2)}, u32[]{:S(2)}) collective-permute-start(bf16[128,1152]{1,0:T(8,128)(2,1)S(1)} %get-tuple-element.93), channel_id=1, source_target_pairs={{0,1},{1,0},{2,3},{3,2},{4,5},{5,4},{6,7},{7,6},{8,9},{9,8},{10,11... | collective-permute-start | bytes 884744 | tf_op jit(solution)/shard_map/ppermute | solution.py:382
  38.2 12.2 %copy-start.3 = (f32[1,3072]{1,0:T(1,128)S(1)}, f32[1,3072]{1,0:T(1,128)}, u32[]{:S(2)}) copy-start(f32[1,3072]{1,0:T(1,128)} %get-tuple-element.115.sg) | copy-start | bytes 36868
  38.3 9.1 %collective-permute-start.4 = (bf16[128,1152]{1,0:T(8,128)(2,1)S(1)}, bf16[128,1152]{1,0:T(8,128)(2,1)S(1)}, u32[]{:S(2)}, u32[]{:S(2)}) collective-permute-start(bf16[128,1152]{1,0:T(8,128)(2,1)S(1)} %join.3), channel_id=1, source_target_pairs={{0,2},{1,3},{2,0},{3,1},{4,6},{5,7},{6,4},{7,5},{8,10},{9,11},{10,... | collective-permute-start | bytes 884744 | tf_op jit(solution)/shard_map/ppermute | solution.py:385
  43.8 0.7 copy-start.6
  43.8 1.5 %collective-permute-start.5 = (bf16[128,1024]{1,0:T(8,128)(2,1)S(1)}, bf16[128,1024]{1,0:T(8,128)(2,1)S(1)}, u32[]{:S(2)}, u32[]{:S(2)}) collective-permute-start(bf16[128,1024]{1,0:T(8,128)(2,1)S(1)} %get-tuple-element.107), channel_id=1, source_target_pairs={{0,1},{1,0},{2,3},{3,2},{4,5},{5,4},{6,7},{7,6},{8,9},{9,8},{10,11... | collective-permute-start | bytes 786440 | tf_op jit(solution)/shard_map/ppermute | solution.py:382
  44.5 5.9 %collective-permute-start.8 = (bf16[128,1152]{1,0:T(8,128)(2,1)S(1)}, bf16[128,1152]{1,0:T(8,128)(2,1)S(1)}, u32[]{:S(2)}, u32[]{:S(2)}) collective-permute-start(bf16[128,1152]{1,0:T(8,128)(2,1)S(1)} %get-tuple-element.118), channel_id=1, source_target_pairs={{0,1},{1,0},{2,3},{3,2},{4,5},{5,4},{6,7},{7,6},{8,9},{9,8},{10,11... | collective-permute-start | bytes 884744 | tf_op jit(solution)/shard_map/ppermute | solution.py:382
  48.2 7.8 %collective-permute-start.7 = (bf16[128,1024]{1,0:T(8,128)(2,1)}, bf16[128,1024]{1,0:T(8,128)(2,1)S(1)}, u32[]{:S(2)}, u32[]{:S(2)}) collective-permute-start(bf16[128,1024]{1,0:T(8,128)(2,1)} %join.4), channel_id=1, source_target_pairs={{0,2},{1,3},{2,0},{3,1},{4,6},{5,7},{6,4},{7,5},{8,10},{9,11},{10,... | collective-permute-start | bytes 786440 | tf_op jit(solution)/shard_map/ppermute | solution.py:385
  49.9 6.0 %collective-permute-start.6 = (bf16[128,1024]{1,0:T(8,128)(2,1)}, bf16[128,1024]{1,0:T(8,128)(2,1)}, u32[]{:S(2)}, u32[]{:S(2)}) collective-permute-start(bf16[128,1024]{1,0:T(8,128)(2,1)} %get-tuple-element.114), channel_id=1, source_target_pairs={{0,1},{1,0},{2,3},{3,2},{4,5},{5,4},{6,7},{7,6},{8,9},{9,8},{10,11... | collective-permute-start | bytes 786440 | tf_op jit(solution)/shard_map/ppermute | solution.py:382
  49.9 2.7 %collective-permute-start.11 = (bf16[128,896]{1,0:T(8,128)(2,1)}, bf16[128,896]{1,0:T(8,128)(2,1)}, u32[]{:S(2)}, u32[]{:S(2)}) collective-permute-start(bf16[128,896]{1,0:T(8,128)(2,1)} %get-tuple-element.127), channel_id=1, source_target_pairs={{0,1},{1,0},{2,3},{3,2},{4,5},{5,4},{6,7},{7,6},{8,9},{9,8},{10,11... | collective-permute-start | bytes 688136 | tf_op jit(solution)/shard_map/ppermute | solution.py:382
  51.1 7.9 %collective-permute-start.13 = (bf16[64,1152]{1,0:T(8,128)(2,1)}, bf16[64,1152]{1,0:T(8,128)(2,1)S(1)}, u32[]{:S(2)}, u32[]{:S(2)}) collective-permute-start(bf16[64,1152]{1,0:T(8,128)(2,1)} %get-tuple-element.120), channel_id=1, source_target_pairs={{0,4},{4,0},{8,12},{12,8},{16,20},{20,16},{24,28},{28,24},{1,5},{5... | collective-permute-start | bytes 442376 | tf_op jit(solution)/shard_map/ppermute | solution.py:388
  52.6 9.1 %collective-permute-start.10 = (bf16[128,896]{1,0:T(8,128)(2,1)}, bf16[128,896]{1,0:T(8,128)(2,1)S(1)}, u32[]{:S(2)}, u32[]{:S(2)}) collective-permute-start(bf16[128,896]{1,0:T(8,128)(2,1)} %copy-done.6), channel_id=1, source_target_pairs={{0,1},{1,0},{2,3},{3,2},{4,5},{5,4},{6,7},{7,6},{8,9},{9,8},{10,11... | collective-permute-start | bytes 688136 | tf_op jit(solution)/shard_map/ppermute | solution.py:382
  53.6 8.1 %collective-permute-start.12 = (bf16[128,896]{1,0:T(8,128)(2,1)S(1)}, bf16[128,896]{1,0:T(8,128)(2,1)S(1)}, u32[]{:S(2)}, u32[]{:S(2)}) collective-permute-start(bf16[128,896]{1,0:T(8,128)(2,1)S(1)} %join.5), channel_id=1, source_target_pairs={{0,2},{1,3},{2,0},{3,1},{4,6},{5,7},{6,4},{7,5},{8,10},{9,11},{10,... | collective-permute-start | bytes 688136 | tf_op jit(solution)/shard_map/ppermute | solution.py:385
  57.0 5.7 %collective-permute-start.9 = (bf16[64,1024]{1,0:T(8,128)(2,1)S(1)}, bf16[64,1024]{1,0:T(8,128)(2,1)S(1)}, u32[]{:S(2)}, u32[]{:S(2)}) collective-permute-start(bf16[64,1024]{1,0:T(8,128)(2,1)S(1)} %get-tuple-element.123), channel_id=1, source_target_pairs={{0,4},{4,0},{8,12},{12,8},{16,20},{20,16},{24,28},{28,24},{1,5},{5... | collective-permute-start | bytes 393224 | tf_op jit(solution)/shard_map/ppermute | solution.py:388
  59.1 26.3 %copy-start.1 = (f32[128,3072]{1,0:T(8,128)S(1)}, f32[128,3072]{1,0:T(8,128)}, u32[]{:S(2)}) copy-start(f32[128,3072]{1,0:T(8,128)} %x_start.3) | copy-start | bytes 4718596
  59.1 5.3 %collective-permute-start.16 = (bf16[64,1152]{1,0:T(8,128)(2,1)S(1)}, bf16[64,1152]{1,0:T(8,128)(2,1)S(1)}, u32[]{:S(2)}, u32[]{:S(2)}) collective-permute-start(bf16[64,1152]{1,0:T(8,128)(2,1)S(1)} %fusion.6), channel_id=1, source_target_pairs={{0,8},{4,12},{8,0},{12,4},{16,24},{20,28},{24,16},{28,20},{1,9},{5... | collective-permute-start | bytes 442376 | tf_op jit(solution)/shard_map/ppermute | solution.py:453
  61.8 5.3 %collective-permute-start.15 = (bf16[64,896]{1,0:T(8,128)(2,1)S(1)}, bf16[64,896]{1,0:T(8,128)(2,1)S(1)}, u32[]{:S(2)}, u32[]{:S(2)}) collective-permute-start(bf16[64,896]{1,0:T(8,128)(2,1)S(1)} %get-tuple-element.131), channel_id=1, source_target_pairs={{0,4},{4,0},{8,12},{12,8},{16,20},{20,16},{24,28},{28,24},{1,5},{5... | collective-permute-start | bytes 344072 | tf_op jit(solution)/shard_map/ppermute | solution.py:388
  62.7 7.2 %collective-permute-start.14 = (bf16[64,1024]{1,0:T(8,128)(2,1)S(1)}, bf16[64,1024]{1,0:T(8,128)(2,1)S(1)}, u32[]{:S(2)}, u32[]{:S(2)}) collective-permute-start(bf16[64,1024]{1,0:T(8,128)(2,1)S(1)} %fusion.7), channel_id=1, source_target_pairs={{0,8},{4,12},{8,0},{12,4},{16,24},{20,28},{24,16},{28,20},{1,9},{5... | collective-permute-start | bytes 393224 | tf_op jit(solution)/shard_map/ppermute | solution.py:453
  64.4 12.7 %collective-permute-start.18 = (bf16[64,1152]{1,0:T(8,128)(2,1)S(1)}, bf16[64,1152]{1,0:T(8,128)(2,1)S(1)}, u32[]{:S(2)}, u32[]{:S(2)}) collective-permute-start(bf16[64,1152]{1,0:T(8,128)(2,1)S(1)} %fusion), channel_id=1, source_target_pairs={{0,16},{4,20},{8,24},{12,28},{16,0},{20,4},{24,8},{28,12},{1,17},{... | collective-permute-start | bytes 442376 | tf_op jit(solution)/shard_map/ppermute | solution.py:453
  67.1 6.8 %collective-permute-start.19 = (bf16[64,896]{1,0:T(8,128)(2,1)S(1)}, bf16[64,896]{1,0:T(8,128)(2,1)S(1)}, u32[]{:S(2)}, u32[]{:S(2)}) collective-permute-start(bf16[64,896]{1,0:T(8,128)(2,1)S(1)} %fusion.8), channel_id=1, source_target_pairs={{0,8},{4,12},{8,0},{12,4},{16,24},{20,28},{24,16},{28,20},{1,9},{5... | collective-permute-start | bytes 344072 | tf_op jit(solution)/shard_map/ppermute | solution.py:453
  69.9 12.5 %collective-permute-start.17 = (bf16[64,1024]{1,0:T(8,128)(2,1)S(1)}, bf16[64,1024]{1,0:T(8,128)(2,1)S(1)}, u32[]{:S(2)}, u32[]{:S(2)}) collective-permute-start(bf16[64,1024]{1,0:T(8,128)(2,1)S(1)} %fusion.3), channel_id=1, source_target_pairs={{0,16},{4,20},{8,24},{12,28},{16,0},{20,4},{24,8},{28,12},{1,17},{... | collective-permute-start | bytes 393224 | tf_op jit(solution)/shard_map/ppermute | solution.py:453
  73.9 10.2 %collective-permute-start.21 = (bf16[64,896]{1,0:T(8,128)(2,1)S(1)}, bf16[64,896]{1,0:T(8,128)(2,1)S(1)}, u32[]{:S(2)}, u32[]{:S(2)}) collective-permute-start(bf16[64,896]{1,0:T(8,128)(2,1)S(1)} %fusion.4), channel_id=1, source_target_pairs={{0,16},{4,20},{8,24},{12,28},{16,0},{20,4},{24,8},{28,12},{1,17},{... | collective-permute-start | bytes 344072 | tf_op jit(solution)/shard_map/ppermute | solution.py:453
  77.2 8.2 %collective-permute-start.23 = (bf16[64,1152]{1,0:T(8,128)(2,1)S(1)}, bf16[64,1152]{1,0:T(8,128)(2,1)S(1)}, u32[]{:S(2)}, u32[]{:S(2)}) collective-permute-start(bf16[64,1152]{1,0:T(8,128)(2,1)S(1)} %get-tuple-element.149), channel_id=1, source_target_pairs={{0,4},{4,0},{8,12},{12,8},{16,20},{20,16},{24,28},{28,24},{1,5},{5... | collective-permute-start | bytes 442376 | tf_op jit(solution)/shard_map/ppermute | solution.py:388
  82.5 7.1 %collective-permute-start.20 = (bf16[64,1024]{1,0:T(8,128)(2,1)S(1)}, bf16[64,1024]{1,0:T(8,128)(2,1)S(1)}, u32[]{:S(2)}, u32[]{:S(2)}) collective-permute-start(bf16[64,1024]{1,0:T(8,128)(2,1)S(1)} %get-tuple-element.147), channel_id=1, source_target_pairs={{0,4},{4,0},{8,12},{12,8},{16,20},{20,16},{24,28},{28,24},{1,5},{5... | collective-permute-start | bytes 393224 | tf_op jit(solution)/shard_map/ppermute | solution.py:388
  84.2 5.4 %collective-permute-start.22 = (bf16[64,896]{1,0:T(8,128)(2,1)S(1)}, bf16[64,896]{1,0:T(8,128)(2,1)S(1)}, u32[]{:S(2)}, u32[]{:S(2)}) collective-permute-start(bf16[64,896]{1,0:T(8,128)(2,1)S(1)} %get-tuple-element.145), channel_id=1, source_target_pairs={{0,4},{4,0},{8,12},{12,8},{16,20},{20,16},{24,28},{28,24},{1,5},{5... | collective-permute-start | bytes 344072 | tf_op jit(solution)/shard_map/ppermute | solution.py:388

commit v14 on v13

--- a/solution.py
+++ b/solution.py
@@ -23,7 +23,7 @@
     return pl.CostEstimate(flops=flops, transcendentals=0, bytes_accessed=moved)
 
 
-def norm_kernel(t_ref, size_ref, x_hbm, mod_hbm, m_hbm, sg_ref, x_ref, m_ref, mod_ref, sem, out_sem):
+def norm_kernel(t_ref, size_ref, x_hbm, mod_hbm, top_ref, low_ref, sg_ref, x_ref, mod_ref, sem):
     width = x_hbm.shape[-1]
     pieces = sem.shape[0] - 1
     block = x_hbm.shape[1] // pieces
@@ -45,12 +45,12 @@
         x = x_ref[here, :]
         center = x - jnp.mean(x, axis=-1, keepdims=True)
         spread = jnp.mean(center * center, axis=-1, keepdims=True)
-        m_ref[here, :] = (center * lax.rsqrt(spread + eps) * scale + shift).astype(bf16)
-        rows = pl.ds(i * block, block)
-        copies[i] = pltpu.make_async_copy(m_ref.at[rows, :], m_hbm.at[rows, :], out_sem.at[i])
-        copies[i].start()
-    for copy in copies:
-        copy.wait()
+        m = (center * lax.rsqrt(spread + eps) * scale + shift).astype(bf16)
+        if 2 * i < pieces:
+            top_ref[here, :] = m
+        else:
+            at = i * block - top_ref.shape[0]
+            low_ref[at : at + block, :] = m
 
 
 def norm_call(t_idx, trajectory, mod_table, step_sizes):
@@ -61,17 +61,16 @@
     return pl.pallas_call(
         norm_kernel,
         in_specs=[smem, smem, hbm, hbm],
-        out_specs=[hbm, vm],
+        out_specs=[vm, vm, vm],
         out_shape=[
-            jax.ShapeDtypeStruct((rows, width), bf16),
+            jax.ShapeDtypeStruct((rows // 2, width), bf16),
+            jax.ShapeDtypeStruct((rows // 2, width), bf16),
             jax.ShapeDtypeStruct((1, width), f32),
         ],
         scratch_shapes=[
             VM((rows, width), f32),
-            VM((rows, width), bf16),
             VM((1, 3 * width), f32),
             pltpu.SemaphoreType.DMA((5,)),
-            pltpu.SemaphoreType.DMA((4,)),
         ],
         compiler_params=params(60),
         cost_estimate=cost(10 * rows * width, 0),
@@ -79,14 +78,15 @@
     )(t_idx, step_sizes, trajectory, mod_table)
 
 
-def project_kernel(tile, load, tiles, m0, m1, qg, kg, *refs):
+def project_kernel(tile, load, tiles, m0, m1, m2, m3, qg, kg, *refs):
     if load:
         wq_hbm, wm_hbm, wb_hbm, q, k, v, act, low, high = refs[:9]
         held, rows, wb, sem = refs[9:-3], refs[-3], refs[-2], refs[-1]
     else:
         held = refs[:tiles]
         q, k, v, act, rows = refs[tiles:]
-    half = m0.shape[0]
+    quarter = m0.shape[0]
+    half = 2 * quarter
     head = qg.shape[1]
     n_q = q.shape[1] // tile
     copies = []
@@ -103,8 +103,8 @@
             here = (slice(None), pl.ds(at, span))
             copies.append(pltpu.make_async_copy(wb_hbm.at[here], wb.at[here], sem.at[len(copies)]))
             copies[-1].start()
-    rows[:half] = m0[...]
-    rows[half:] = m1[...]
+    for i, m in enumerate((m0, m1, m2, m3)):
+        rows[i * quarter : (i + 1) * quarter] = m[...]
 
     def normed(y, gain):
         parts = []
@@ -137,8 +137,8 @@
             high[:, cols] = y[half:]
 
 
-def project_call(m0, m1, q_gain, k_gain, w_qkv, w_mlp_in, w_out_mlp, held):
-    half, width = m0.shape
+def project_call(given, q_gain, k_gain, w_qkv, w_mlp_in, w_out_mlp, held):
+    half, width = 2 * given[0].shape[0], given[0].shape[1]
     heads = w_qkv.shape[2]
     hidden = w_mlp_in.shape[1]
     tile = min(512, heads)
@@ -157,14 +157,14 @@
         scratch.append(pltpu.SemaphoreType.DMA((tiles + 4,)))
     return pl.pallas_call(
         functools.partial(project_kernel, tile, load, tiles),
-        in_specs=[vm] * 4 + ([hbm] * 3 if load else [vm] * tiles),
+        in_specs=[vm] * 6 + ([hbm] * 3 if load else [vm] * tiles),
         out_specs=[vm] * len(shapes),
         out_shape=shapes,
         scratch_shapes=scratch,
         compiler_params=params(27 if load else 9),
         cost_estimate=cost(2 * rows * width * (3 * heads + hidden), 0),
         name="project",
-    )(m0, m1, q_gain, k_gain, *([w_qkv, w_mlp_in, w_out_mlp] if load else held))
+    )(*given, q_gain, k_gain, *([w_qkv, w_mlp_in, w_out_mlp] if load else held))
 
 
 def attend_kernel(pairs, head, *refs):
@@ -395,15 +395,21 @@
     which = parity[None]
     offsets = range(1, chips)
 
-    mine, sg = norm_call(t_idx, trajectory, mod_table, step_sizes)
-    far = [to_chip(mine, j) for j in offsets]
+    *mine, sg = norm_call(t_idx, trajectory, mod_table, step_sizes)
+    far = [[to_chip(part, j) for part in mine] for j in offsets]
+    given = mine + [to_core(part) for part in mine]
     q0, k0, v0, act0, low0, high0, *held = project_call(
-        mine, to_core(mine), qg, kg, w_qkv, w_mlp_in, w_out_mlp, None
+        given, qg, kg, w_qkv, w_mlp_in, w_out_mlp, None
     )
-    far, low0, high0 = tied(far, low0, high0)
+    given = []
+    for top, low in far:
+        top, q0 = tied(top, q0)
+        next_top = to_core(top)
+        low, next_top = tied(low, next_top)
+        given.append([top, low, next_top, to_core(low)])
     qs, ks, vs, acts = [], [k0], [v0], []
-    for block in far:
-        q, k, v, act = project_call(block, to_core(block), qg, kg, w_qkv, w_mlp_in, w_out_mlp, held)
+    for blocks in given:
+        q, k, v, act = project_call(blocks, qg, kg, w_qkv, w_mlp_in, w_out_mlp, held)
         qs.append(q)
         ks.append(k)
         vs.append(v)

time: 91 us -> 90 us (0.989)
  waiting for transfers between devices: 23.3 us -> 20.2 us
  local copies, waits for them, and re-layouts: 1.87 us -> 4.1 us
    ppermute x4 -> x5, waiting for transfers between devices: 9.52 us -> 6.86 us  [to_chip(): lax.ppermute(x, 'seq', [(i, (i + 2 * offset) % n_seq) for i in range(n_se...]
    unnamed x20 -> x30, local copies, waits for them, and re-layouts: 1.87 us -> 4.1 us
    ppermute x8 -> x10, waiting for transfers between devices: 3.7 us -> 3.14 us  [to_core(): return lax.ppermute(x, 'seq', [(i, i ^ 1) for i in range(n_seq)])]
    ppermute x4 -> x5, starting transfers between devices: 6.74 us -> 7.1 us  [to_chip(): lax.ppermute(x, 'seq', [(i, (i + 2 * offset) % n_seq) for i in range(n_se...]
  transfers between devices with their start and end apart: 24 -> 27, of which waited for: 11 -> 11; matrix products, arithmetic and copies ran while one was open for 0% -> 0% of each run, Pallas kernels for 24% -> 24%
where the time goes in v14:
time: 90 us; the launch traced here: 89.7 us
  Pallas kernels  34.1 us (38%)
  starting transfers between devices  29.8 us (33%)
  waiting for transfers between devices  20.2 us (22%)
  local copies, waits for them, and re-layouts  4.1 us (5%)
  between operations  1.09 us (1%)
    pallas_call x2, Pallas kernels, project_call(): pl.pallas_call(functools.partial(project_kernel, tile, load, tiles), in_s...  17.6 us
    ppermute x6, starting transfers between devices, along(): lax.ppermute(x, 'step', [(2 * a + i, 2 * b + i) for a, b in pairs for i i...  12.6 us
    ppermute x6, starting transfers between devices, to_pair(): return lax.ppermute(x, 'step', [(i, i ^ 1) for i in range(n_step)])  8.84 us
    ppermute x5, starting transfers between devices, to_chip(): lax.ppermute(x, 'seq', [(i, (i + 2 * offset) % n_seq) for i in range(n_se...  7.1 us
    ppermute x6, waiting for transfers between devices, along(): lax.ppermute(x, 'step', [(2 * a + i, 2 * b + i) for a, b in pairs for i i...  6.95 us
    ppermute x5, waiting for transfers between devices, to_chip(): lax.ppermute(x, 'seq', [(i, (i + 2 * offset) % n_seq) for i in range(n_se...  6.86 us
    pallas_call x2, Pallas kernels, out_call(): pl.pallas_call(functools.partial(out_kernel, plan), in_specs=[vm] * len(g...  5.25 us
    unnamed x30, local copies, waits for them, and re-layouts  4.1 us
  transfers between devices with their start and end apart: 27, of which 11 were waited for; matrix products, arithmetic and copies ran while one was open for 0% of the time, Pallas kernels for 24%

profile of v14, /device:TPU:0, one launch (start us, length us, event | category | flops | bytes accessed | tf_op | source)
XLA Modules:
  0.0 89.7 jit_solution(4212963153870976763)
XLA Ops:
  0.7 3.6 %norm.1 = (bf16[64,3072]{1,0:T(8,128)(2,1)}, bf16[64,3072]{1,0:T(8,128)(2,1)}, f32[1,3072]{1,0:T(1,128)}) custom-call(s32[1]{0:T(128)S(6)} %copy.14.t_ref, f32[50]{0:T(128)} %size_ref.1, f32[1,128,3072]{2,1,0:T(8,128)} %x_hbm.1, f32[50,9216]{1,0:T(8,128)} %mod_hbm.1), custom_call_target="tpu_custom_call" | custom-call | flops 3932160 | tf_op jit(solution)/shard_map/norm/pallas_call | solution.py:61
  4.3 0.5 collective-permute-start.1
  4.8 0.1 collective-permute-start.2
  4.9 2.9 %collective-permute-start = (bf16[64,3072]{1,0:T(8,128)(2,1)}, bf16[64,3072]{1,0:T(8,128)(2,1)S(1)}, u32[]{:S(2)}, u32[]{:S(2)}) collective-permute-start(bf16[64,3072]{1,0:T(8,128)(2,1)} %get-tuple-element.77.m0), channel_id=1, source_target_pairs={{0,2},{1,3},{2,0},{3,1},{4,6},{5,7},{6,4},{7,5},{8,10},{9,11},{10,... | collective-permute-start | bytes 1179656 | tf_op jit(solution)/shard_map/ppermute | solution.py:385
  7.8 0.0 collective-permute-start.3
  7.8 0.0 collective-permute-done.1.m2
  7.9 0.0 collective-permute-done.2.m3
  7.9 1.0 %copy-done.2 = bf16[64,3072]{1,0:T(8,128)(2,1)S(1)} copy-done((bf16[64,3072]{1,0:T(8,128)(2,1)S(1)}, bf16[64,3072]{1,0:T(8,128)(2,1)}, u32[]{:S(2)}) %copy-start.2) | copy-done | bytes 393240
  8.9 1.0 %copy-done.3 = bf16[64,3072]{1,0:T(8,128)(2,1)S(1)} copy-done((bf16[64,3072]{1,0:T(8,128)(2,1)S(1)}, bf16[64,3072]{1,0:T(8,128)(2,1)}, u32[]{:S(2)}) %copy-start.3) | copy-done | bytes 393240
  9.9 12.4 %project.2 = (bf16[256,512]{1,0:T(8,128)(2,1)S(1)}, bf16[256,512]{1,0:T(8,128)(2,1)S(1)}, bf16[256,512]{1,0:T(8,128)(2,1)S(1)}, bf16[256,1536]{1,0:T(8,128)(2,1)...) custom-call(bf16[64,3072]{1,0:T(8,128)(2,1)S(1)} %copy-done.3, ...), custom_call_target="tpu_custom_call" | custom-call | flops 4831838208 | tf_op jit(solution)/shard_map/project/pallas_call | solution.py:158
  22.3 0.0 copy-start.7
  22.3 0.7 copy-done.7
  23.0 0.7 copy-done.9
  23.7 0.0 collective-permute-done.m0
  23.7 0.0 collective-permute-start.4
  23.7 2.1 %collective-permute-done.3.m1 = bf16[64,3072]{1,0:T(8,128)(2,1)S(1)} collective-permute-done((bf16[64,3072]{1,0:T(8,128)(2,1)}, bf16[64,3072]{1,0:T(8,128)(2,1)S(1)}, u32[]{:S(2)}, u32[]{:S(2)}) %collective-permute-start.3) | collective-permute-done | bytes 393248 | tf_op jit(solution)/shard_map/ppermute | solution.py:385
  25.8 1.7 %collective-permute-done.5.m3 = bf16[64,3072]{1,0:T(8,128)(2,1)S(1)} collective-permute-done((bf16[64,3072]{1,0:T(8,128)(2,1)S(1)}, bf16[64,3072]{1,0:T(8,128)(2,1)S(1)}, u32[]{:S(2)}, u32[]{:S(2)}) %collective-permute-start.5) | collective-permute-done | bytes 393248 | tf_op jit(solution)/shard_map/ppermute | solution.py:382
  27.6 0.0 copy-start
  27.6 5.2 %project.3 = (bf16[256,512]{1,0:T(8,128)(2,1)S(1)}, bf16[256,512]{1,0:T(8,128)(2,1)S(1)}, bf16[256,512]{1,0:T(8,128)(2,1)S(1)}, bf16[256,1536]{1,0:T(8,128)(2,1)S(1)}) custom-call(bf16[64,3072]{1,0:T(8,128)(2,1)S(1)} %collective-permute-done.m0, bf16[64,3072]{1,0:T(8,128)(2,1)S(1)} %collective-permute-done.3.m1, ...), custom_call_target="tpu_custom_call" | custom-call | flops 4831838208 | tf_op jit(solution)/shard_map/project/pallas_call | solution.py:158
  32.8 1.1 %attend.2.refs_0_.refs_4_ = bf16[256,512]{1,0:T(8,128)(2,1)S(1)} custom-call(bf16[256,512]{1,0:T(8,128)(2,1)S(1)} %get-tuple-element.89.refs_0_, bf16[256,512]{1,0:T(8,128)(2,1)S(1)} %copy-done.8, bf16[256,512]{1,0:T(8,128)(2,1)S(1)} %get-tuple-element.91.refs_2_, bf16[256,512]{1,0:T(8,128)(2,1)S(1)} %copy-done.10, ...), custom_call_target="tpu_custom_call" | custom-call | flops 805306368 | tf_op jit(solution)/shard_map/attend/pallas_call | solution.py:202
  34.0 1.5 %project_out.2 = (f32[128,1152]{1,0:T(8,128)S(1)}, bf16[128,1152]{1,0:T(8,128)(2,1)S(1)}) custom-call(bf16[256,512]{1,0:T(8,128)(2,1)S(1)} %attend.2.refs_0_.refs_4_, bf16[256,1536]{1,0:T(8,128)(2,1)S(1)} %get-tuple-element.104.refs_1_.refs_5_, bf16[512,3072]{1,0:T(8,128)(2,1)S(1)} %copy-done, bf16[1536,3072]{1,0:T(8,128)(2,1)S(1)} %bitcast.4), custom_call_target="tpu_custom_call" | custom-call | flops 1207959552 | tf_op jit(solution)/shard_map/project_out/pallas_call | solution.py:246
  35.5 0.2 collective-permute-start.6
  35.7 0.9 attend.3.refs_8_.refs_12_.refs_16_
  36.6 0.6 collective-permute-done.6.sent
  37.2 0.1 join.3
  37.2 1.8 %collective-permute-start.7 = (bf16[128,1152]{1,0:T(8,128)(2,1)S(1)}, bf16[128,1152]{1,0:T(8,128)(2,1)S(1)}, u32[]{:S(2)}, u32[]{:S(2)}) collective-permute-start(bf16[128,1152]{1,0:T(8,128)(2,1)S(1)} %join.3), channel_id=1, source_target_pairs={{0,2},{1,3},{2,0},{3,1},{4,6},{5,7},{6,4},{7,5},{8,10},{9,11},{10,... | collective-permute-start | bytes 884744 | tf_op jit(solution)/shard_map/ppermute | solution.py:385
  39.0 3.7 %project_out.3 = (f32[128,1024]{1,0:T(8,128)S(1)}, bf16[128,1024]{1,0:T(8,128)(2,1)S(1)}, f32[128,896]{1,0:T(8,128)S(1)}, bf16[128,896]{1,0:T(8,128)(2,1)}, f32[...) custom-call(bf16[256,512]{1,0:T(8,128)(2,1)S(1)} %attend.2.refs_0_.r, ...), custom_call_target="tpu_custom_call" | custom-call | flops 2818572288 | tf_op jit(solution)/shard_map/project_out/pallas_call | solution.py:246
  42.7 0.7 copy-done.11
  43.4 0.8 collective-permute-done.8.sent
  44.3 2.1 %collective-permute-done.7.refs_0_ = bf16[128,1152]{1,0:T(8,128)(2,1)S(1)} collective-permute-done((bf16[128,1152]{1,0:T(8,128)(2,1)S(1)}, bf16[128,1152]{1,0:T(8,128)(2,1)S(1)}, u32[]{:S(2)}, u32[]{:S(2)}) %collective-permute-start.7) | collective-permute-done | bytes 294944 | tf_op jit(solution)/shard_map/ppermute | solution.py:385
  46.3 0.7 join.4
  47.1 1.7 %collective-permute-start.10 = (bf16[128,1024]{1,0:T(8,128)(2,1)}, bf16[128,1024]{1,0:T(8,128)(2,1)S(1)}, u32[]{:S(2)}, u32[]{:S(2)}) collective-permute-start(bf16[128,1024]{1,0:T(8,128)(2,1)} %join.4), channel_id=1, source_target_pairs={{0,2},{1,3},{2,0},{3,1},{4,6},{5,7},{6,4},{7,5},{8,10},{9,11},{10,... | collective-permute-start | bytes 786440 | tf_op jit(solution)/shard_map/ppermute | solution.py:385
  48.8 0.5 collective-permute-start.14
  49.3 0.7 drift.3
  50.1 1.5 %collective-permute-start.16 = (bf16[64,1152]{1,0:T(8,128)(2,1)}, bf16[64,1152]{1,0:T(8,128)(2,1)S(1)}, u32[]{:S(2)}, u32[]{:S(2)}) collective-permute-start(bf16[64,1152]{1,0:T(8,128)(2,1)} %get-tuple-element.124), channel_id=1, source_target_pairs={{0,4},{4,0},{8,12},{12,8},{16,20},{20,16},{24,28},{28,24},{1,5},{5... | collective-permute-start | bytes 442376 | tf_op jit(solution)/shard_map/ppermute | solution.py:388
  51.6 1.0 %join.5 = bf16[128,896]{1,0:T(8,128)(2,1)S(1)} custom-call(f32[128,896]{1,0:T(8,128)S(1)} %get-tuple-element.130.keep, bf16[128,896]{1,0:T(8,128)(2,1)} %collective-permute-done.14.sent), custom_call_target="tpu_custom_call" | custom-call | tf_op jit(solution)/shard_map/join/pallas_call | solution.py:264
  52.6 0.6 collective-permute-start.15
  53.1 1.7 %collective-permute-done.10.refs_0_ = bf16[128,1024]{1,0:T(8,128)(2,1)S(1)} collective-permute-done((bf16[128,1024]{1,0:T(8,128)(2,1)}, bf16[128,1024]{1,0:T(8,128)(2,1)S(1)}, u32[]{:S(2)}, u32[]{:S(2)}) %collective-permute-start.10) | collective-permute-done | bytes 262176 | tf_op jit(solution)/shard_map/ppermute | solution.py:385
  54.8 1.0 %drift.4 = (f32[64,1024]{1,0:T(8,128)S(1)}, f32[64,1024]{1,0:T(8,128)S(1)}, bf16[64,1024]{1,0:T(8,128)(2,1)S(1)}) custom-call(s32[1]{0:T(128)} %bitcast.parity, f32[128,1024]{1,0:T(8,128)S(1)} %get-tuple-element.117.keep, bf16[128,1024]{1,0:T(8,128)(2,1)} %collective-permute-done.9.sent, f32[1,3072]{1,0:T(1,128)S(1)} %copy-done.4, ...), custom_call_target="tpu_custom_call" | custom-call | tf_op jit(solution)/shard_map/drift/pallas_call | solution.py:297
  55.9 2.1 %collective-permute-start.12 = (bf16[64,1024]{1,0:T(8,128)(2,1)S(1)}, bf16[64,1024]{1,0:T(8,128)(2,1)S(1)}, u32[]{:S(2)}, u32[]{:S(2)}) collective-permute-start(bf16[64,1024]{1,0:T(8,128)(2,1)S(1)} %get-tuple-element.127), channel_id=1, source_target_pairs={{0,4},{4,0},{8,12},{12,8},{16,20},{20,16},{24,28},{28,24},{1,5},{5... | collective-permute-start | bytes 393224 | tf_op jit(solution)/shard_map/ppermute | solution.py:388
  58.0 0.0 copy-start.1
  58.0 1.6 %collective-permute-start.19 = (bf16[64,1152]{1,0:T(8,128)(2,1)S(1)}, bf16[64,1152]{1,0:T(8,128)(2,1)S(1)}, u32[]{:S(2)}, u32[]{:S(2)}) collective-permute-start(bf16[64,1152]{1,0:T(8,128)(2,1)S(1)} %fusion.6), channel_id=1, source_target_pairs={{0,8},{4,12},{8,0},{12,4},{16,24},{20,28},{24,16},{28,20},{1,9},{5... | collective-permute-start | bytes 442376 | tf_op jit(solution)/shard_map/ppermute | solution.py:459
  59.7 1.0 %collective-permute-done.15.refs_0_ = bf16[128,896]{1,0:T(8,128)(2,1)S(1)} collective-permute-done((bf16[128,896]{1,0:T(8,128)(2,1)S(1)}, bf16[128,896]{1,0:T(8,128)(2,1)S(1)}, u32[]{:S(2)}, u32[]{:S(2)}) %collective-permute-start.15) | collective-permute-done | bytes 229408 | tf_op jit(solution)/shard_map/ppermute | solution.py:385
  60.6 0.1 drift.5
  60.7 0.9 collective-permute-start.18
  61.6 1.6 %collective-permute-start.17 = (bf16[64,1024]{1,0:T(8,128)(2,1)S(1)}, bf16[64,1024]{1,0:T(8,128)(2,1)S(1)}, u32[]{:S(2)}, u32[]{:S(2)}) collective-permute-start(bf16[64,1024]{1,0:T(8,128)(2,1)S(1)} %fusion.7), channel_id=1, source_target_pairs={{0,8},{4,12},{8,0},{12,4},{16,24},{20,28},{24,16},{28,20},{1,9},{5... | collective-permute-start | bytes 393224 | tf_op jit(solution)/shard_map/ppermute | solution.py:459
  63.3 0.1 fusion
  63.3 2.7 %collective-permute-start.21 = (bf16[64,1152]{1,0:T(8,128)(2,1)S(1)}, bf16[64,1152]{1,0:T(8,128)(2,1)S(1)}, u32[]{:S(2)}, u32[]{:S(2)}) collective-permute-start(bf16[64,1152]{1,0:T(8,128)(2,1)S(1)} %fusion), channel_id=1, source_target_pairs={{0,16},{4,20},{8,24},{12,28},{16,0},{20,4},{24,8},{28,12},{1,17},{... | collective-permute-start | bytes 442376 | tf_op jit(solution)/shard_map/ppermute | solution.py:459
  66.0 1.6 %collective-permute-start.22 = (bf16[64,896]{1,0:T(8,128)(2,1)S(1)}, bf16[64,896]{1,0:T(8,128)(2,1)S(1)}, u32[]{:S(2)}, u32[]{:S(2)}) collective-permute-start(bf16[64,896]{1,0:T(8,128)(2,1)S(1)} %fusion.8), channel_id=1, source_target_pairs={{0,8},{4,12},{8,0},{12,4},{16,24},{20,28},{24,16},{28,20},{1,9},{5... | collective-permute-start | bytes 344072 | tf_op jit(solution)/shard_map/ppermute | solution.py:459
  67.6 1.3 %collective-permute-done.17 = bf16[64,1024]{1,0:T(8,128)(2,1)S(1)} collective-permute-done((bf16[64,1024]{1,0:T(8,128)(2,1)S(1)}, bf16[64,1024]{1,0:T(8,128)(2,1)S(1)}, u32[]{:S(2)}, u32[]{:S(2)}) %collective-permute-start.17) | collective-permute-done | bytes 131104 | tf_op jit(solution)/shard_map/ppermute | solution.py:459
  68.9 0.1 fusion.3
  69.0 1.9 %collective-permute-start.20 = (bf16[64,1024]{1,0:T(8,128)(2,1)S(1)}, bf16[64,1024]{1,0:T(8,128)(2,1)S(1)}, u32[]{:S(2)}, u32[]{:S(2)}) collective-permute-start(bf16[64,1024]{1,0:T(8,128)(2,1)S(1)} %fusion.3), channel_id=1, source_target_pairs={{0,16},{4,20},{8,24},{12,28},{16,0},{20,4},{24,8},{28,12},{1,17},{... | collective-permute-start | bytes 393224 | tf_op jit(solution)/shard_map/ppermute | solution.py:459
  70.8 2.0 %collective-permute-done.22 = bf16[64,896]{1,0:T(8,128)(2,1)S(1)} collective-permute-done((bf16[64,896]{1,0:T(8,128)(2,1)S(1)}, bf16[64,896]{1,0:T(8,128)(2,1)S(1)}, u32[]{:S(2)}, u32[]{:S(2)}) %collective-permute-start.22) | collective-permute-done | bytes 114720 | tf_op jit(solution)/shard_map/ppermute | solution.py:459
  72.9 3.2 %collective-permute-start.24 = (bf16[64,896]{1,0:T(8,128)(2,1)S(1)}, bf16[64,896]{1,0:T(8,128)(2,1)S(1)}, u32[]{:S(2)}, u32[]{:S(2)}) collective-permute-start(bf16[64,896]{1,0:T(8,128)(2,1)S(1)} %fusion.4), channel_id=1, source_target_pairs={{0,16},{4,20},{8,24},{12,28},{16,0},{20,4},{24,8},{28,12},{1,17},{... | collective-permute-start | bytes 344072 | tf_op jit(solution)/shard_map/ppermute | solution.py:459
  76.1 0.1 add_convert_fusion
  76.2 1.5 %collective-permute-start.26 = (bf16[64,1152]{1,0:T(8,128)(2,1)S(1)}, bf16[64,1152]{1,0:T(8,128)(2,1)S(1)}, u32[]{:S(2)}, u32[]{:S(2)}) collective-permute-start(bf16[64,1152]{1,0:T(8,128)(2,1)S(1)} %get-tuple-element.153), channel_id=1, source_target_pairs={{0,4},{4,0},{8,12},{12,8},{16,20},{20,16},{24,28},{28,24},{1,5},{5... | collective-permute-start | bytes 442376 | tf_op jit(solution)/shard_map/ppermute | solution.py:388
  77.7 3.6 %collective-permute-done.20 = bf16[64,1024]{1,0:T(8,128)(2,1)S(1)} collective-permute-done((bf16[64,1024]{1,0:T(8,128)(2,1)S(1)}, bf16[64,1024]{1,0:T(8,128)(2,1)S(1)}, u32[]{:S(2)}, u32[]{:S(2)}) %collective-permute-start.20) | collective-permute-done | bytes 131104 | tf_op jit(solution)/shard_map/ppermute | solution.py:459
  81.3 0.1 add_convert_fusion.1
  81.4 1.8 %collective-permute-start.23 = (bf16[64,1024]{1,0:T(8,128)(2,1)S(1)}, bf16[64,1024]{1,0:T(8,128)(2,1)S(1)}, u32[]{:S(2)}, u32[]{:S(2)}) collective-permute-start(bf16[64,1024]{1,0:T(8,128)(2,1)S(1)} %get-tuple-element.151), channel_id=1, source_target_pairs={{0,4},{4,0},{8,12},{12,8},{16,20},{20,16},{24,28},{28,24},{1,5},{5... | collective-permute-start | bytes 393224 | tf_op jit(solution)/shard_map/ppermute | solution.py:388
  83.1 0.1 add_convert_fusion.2
  83.2 1.1 %collective-permute-start.25 = (bf16[64,896]{1,0:T(8,128)(2,1)S(1)}, bf16[64,896]{1,0:T(8,128)(2,1)S(1)}, u32[]{:S(2)}, u32[]{:S(2)}) collective-permute-start(bf16[64,896]{1,0:T(8,128)(2,1)S(1)} %get-tuple-element.149), channel_id=1, source_target_pairs={{0,4},{4,0},{8,12},{12,8},{16,20},{20,16},{24,28},{28,24},{1,5},{5... | collective-permute-start | bytes 344072 | tf_op jit(solution)/shard_map/ppermute | solution.py:388
  84.3 0.9 %finish.2.refs_10_ = f32[1,128,3072]{2,1,0:T(8,128)} custom-call(s32[1]{0:T(128)} %bitcast.parity, f32[128,3072]{1,0:T(8,128)S(1)} %copy-done.1, f32[64,1152]{1,0:T(8,128)S(1)} %get-tuple-element.154.refs_0_, f32[64,1152]{1,0:T(8,128)S(1)} %get-tuple-element.132.refs_1_, bf16[64,1152]{1,0:T(8,128)(2,1)S(1)} %collective-permute-done.16.refs_2_, ...), custom_call_target="tpu_custom_call" | custom-call | tf_op jit(solution)/shard_map/finish/pallas_call | solution.py:342
  85.3 3.2 %collective-permute-done.25.refs_9_ = bf16[64,896]{1,0:T(8,128)(2,1)S(1)} collective-permute-done((bf16[64,896]{1,0:T(8,128)(2,1)S(1)}, bf16[64,896]{1,0:T(8,128)(2,1)S(1)}, u32[]{:S(2)}, u32[]{:S(2)}) %collective-permute-start.25) | collective-permute-done | bytes 114720 | tf_op jit(solution)/shard_map/ppermute | solution.py:388
  88.5 1.1 %finish.3 = f32[1,128,3072]{2,1,0:T(8,128)} custom-call(s32[1]{0:T(128)} %bitcast.parity, f32[128,3072]{1,0:T(8,128)S(1)} %copy-done.1, f32[64,1024]{1,0:T(8,128)S(1)} %get-tuple-element.152.refs_0_, f32[64,1024]{1,0:T(8,128)S(1)} %get-tuple-element.126.refs_1_, ...), custom_call_target="tpu_custom_call", output_to_operand_aliasing={{}: (12, {})} | custom-call | tf_op jit(solution)/shard_map/finish/pallas_call | solution.py:342
  (45 shorter events, 0.2 us)
Async XLA Ops:
  0.0 7.9 %copy-start.5 = (f32[128]{0:T(128)S(1)}, f32[128]{0:T(128)}, u32[]{:S(2)}) copy-start(f32[128]{0:T(128)} %param.16) | copy-start | bytes 1540
  0.0 7.9 %copy-start.6 = (f32[128]{0:T(128)S(1)}, f32[128]{0:T(128)}, u32[]{:S(2)}) copy-start(f32[128]{0:T(128)} %param.17) | copy-start | bytes 1540
  4.3 3.6 %collective-permute-start.1 = (bf16[64,3072]{1,0:T(8,128)(2,1)}, bf16[64,3072]{1,0:T(8,128)(2,1)S(1)}, u32[]{:S(2)}, u32[]{:S(2)}) collective-permute-start(bf16[64,3072]{1,0:T(8,128)(2,1)} %get-tuple-element.77.m0), channel_id=1, source_target_pairs={{0,1},{1,0},{2,3},{3,2},{4,5},{5,4},{6,7},{7,6},{8,9},{9,8},{10,11... | collective-permute-start | bytes 1179656 | tf_op jit(solution)/shard_map/ppermute | solution.py:382
  4.8 3.1 %collective-permute-start.2 = (bf16[64,3072]{1,0:T(8,128)(2,1)}, bf16[64,3072]{1,0:T(8,128)(2,1)S(1)}, u32[]{:S(2)}, u32[]{:S(2)}) collective-permute-start(bf16[64,3072]{1,0:T(8,128)(2,1)} %get-tuple-element.78.m1), channel_id=1, source_target_pairs={{0,1},{1,0},{2,3},{3,2},{4,5},{5,4},{6,7},{7,6},{8,9},{9,8},{10,11... | collective-permute-start | bytes 1179656 | tf_op jit(solution)/shard_map/ppermute | solution.py:382
  4.9 18.8 %collective-permute-start = (bf16[64,3072]{1,0:T(8,128)(2,1)}, bf16[64,3072]{1,0:T(8,128)(2,1)S(1)}, u32[]{:S(2)}, u32[]{:S(2)}) collective-permute-start(bf16[64,3072]{1,0:T(8,128)(2,1)} %get-tuple-element.77.m0), channel_id=1, source_target_pairs={{0,2},{1,3},{2,0},{3,1},{4,6},{5,7},{6,4},{7,5},{8,10},{9,11},{10,... | collective-permute-start | bytes 1179656 | tf_op jit(solution)/shard_map/ppermute | solution.py:385
  7.8 18.0 %collective-permute-start.3 = (bf16[64,3072]{1,0:T(8,128)(2,1)}, bf16[64,3072]{1,0:T(8,128)(2,1)S(1)}, u32[]{:S(2)}, u32[]{:S(2)}) collective-permute-start(bf16[64,3072]{1,0:T(8,128)(2,1)} %get-tuple-element.78.m1), channel_id=1, source_target_pairs={{0,2},{1,3},{2,0},{3,1},{4,6},{5,7},{6,4},{7,5},{8,10},{9,11},{10,... | collective-permute-start | bytes 1179656 | tf_op jit(solution)/shard_map/ppermute | solution.py:385
  7.9 1.0 %copy-start.2 = (bf16[64,3072]{1,0:T(8,128)(2,1)S(1)}, bf16[64,3072]{1,0:T(8,128)(2,1)}, u32[]{:S(2)}) copy-start(bf16[64,3072]{1,0:T(8,128)(2,1)} %get-tuple-element.78.m1) | copy-start | bytes 1179652
  8.9 1.0 %copy-start.3 = (bf16[64,3072]{1,0:T(8,128)(2,1)S(1)}, bf16[64,3072]{1,0:T(8,128)(2,1)}, u32[]{:S(2)}) copy-start(bf16[64,3072]{1,0:T(8,128)(2,1)} %get-tuple-element.77.m0) | copy-start | bytes 1179652
  22.3 0.7 copy-start.7
  23.0 0.7 copy-start.9
  23.7 2.1 %collective-permute-start.4 = (bf16[64,3072]{1,0:T(8,128)(2,1)S(1)}, bf16[64,3072]{1,0:T(8,128)(2,1)S(1)}, u32[]{:S(2)}, u32[]{:S(2)}) collective-permute-start(bf16[64,3072]{1,0:T(8,128)(2,1)S(1)} %collective-permute-done.m0), channel_id=1, source_target_pairs={{0,1},{1,0},{2,3},{3,2},{4,5},{5,4},{6,7},{7,6},{8,9},{9,8},{10,11... | collective-permute-start | bytes 1179656 | tf_op jit(solution)/shard_map/ppermute | solution.py:382
  25.8 1.7 %collective-permute-start.5 = (bf16[64,3072]{1,0:T(8,128)(2,1)S(1)}, bf16[64,3072]{1,0:T(8,128)(2,1)S(1)}, u32[]{:S(2)}, u32[]{:S(2)}) collective-permute-start(bf16[64,3072]{1,0:T(8,128)(2,1)S(1)} %collective-permute-done.3.m1), channel_id=1, source_target_pairs={{0,1},{1,0},{2,3},{3,2},{4,5},{5,4},{6,7},{7,6},{8,9},{9,8},{10,11... | collective-permute-start | bytes 1179656 | tf_op jit(solution)/shard_map/ppermute | solution.py:382
  27.5 6.4 %slice-start = ((s8[9437184]{0:T(1024)(128)(4,1)}), s8[4194304]{0:T(1024)(128)(4,1)S(1)}, s32[]{:S(2)}) async-start(s8[9437184]{0:T(1024)(128)(4,1)} %bitcast.3), calls=%async_computation | async-start | bytes 8388608
  27.5 5.3 %copy-start.8 = (bf16[256,512]{1,0:T(8,128)(2,1)S(1)}, bf16[256,512]{1,0:T(8,128)(2,1)}, u32[]{:S(2)}) copy-start(bf16[256,512]{1,0:T(8,128)(2,1)} %copy-done.7) | copy-start | bytes 786436
  27.5 5.3 %copy-start.10 = (bf16[256,512]{1,0:T(8,128)(2,1)S(1)}, bf16[256,512]{1,0:T(8,128)(2,1)}, u32[]{:S(2)}) copy-start(bf16[256,512]{1,0:T(8,128)(2,1)} %copy-done.9) | copy-start | bytes 786436
  27.5 6.4 %slice-start.1 = ((s8[9437184]{0:T(1024)(128)(4,1)}), s8[4194304]{0:T(1024)(128)(4,1)S(1)}, s32[]{:S(2)}) async-start(s8[9437184]{0:T(1024)(128)(4,1)} %bitcast.3), calls=%async_computation.1 | async-start | bytes 8388608
  27.5 6.4 %slice-start.2 = ((s8[9437184]{0:T(1024)(128)(4,1)}), s8[1048576]{0:T(1024)(128)(4,1)S(1)}, s32[]{:S(2)}) async-start(s8[9437184]{0:T(1024)(128)(4,1)} %bitcast.3), calls=%async_computation.2 | async-start | bytes 2097152
  27.6 6.4 %copy-start = (bf16[512,3072]{1,0:T(8,128)(2,1)S(1)}, bf16[512,3072]{1,0:T(8,128)(2,1)}, u32[]{:S(2)}) copy-start(bf16[512,3072]{1,0:T(8,128)(2,1)} %refs_17_.1) | copy-start | bytes 9437188
  35.5 1.6 %collective-permute-start.6 = (bf16[128,1152]{1,0:T(8,128)(2,1)S(1)}, bf16[128,1152]{1,0:T(8,128)(2,1)S(1)}, u32[]{:S(2)}, u32[]{:S(2)}) collective-permute-start(bf16[128,1152]{1,0:T(8,128)(2,1)S(1)} %get-tuple-element.97), channel_id=1, source_target_pairs={{0,1},{1,0},{2,3},{3,2},{4,5},{5,4},{6,7},{7,6},{8,9},{9,8},{10,11... | collective-permute-start | bytes 884744 | tf_op jit(solution)/shard_map/ppermute | solution.py:382
  37.2 9.1 %collective-permute-start.7 = (bf16[128,1152]{1,0:T(8,128)(2,1)S(1)}, bf16[128,1152]{1,0:T(8,128)(2,1)S(1)}, u32[]{:S(2)}, u32[]{:S(2)}) collective-permute-start(bf16[128,1152]{1,0:T(8,128)(2,1)S(1)} %join.3), channel_id=1, source_target_pairs={{0,2},{1,3},{2,0},{3,1},{4,6},{5,7},{6,4},{7,5},{8,10},{9,11},{10,... | collective-permute-start | bytes 884744 | tf_op jit(solution)/shard_map/ppermute | solution.py:385
  39.0 10.3 %copy-start.4 = (f32[1,3072]{1,0:T(1,128)S(1)}, f32[1,3072]{1,0:T(1,128)}, u32[]{:S(2)}) copy-start(f32[1,3072]{1,0:T(1,128)} %get-tuple-element.119.sg) | copy-start | bytes 36868
  42.7 0.7 copy-start.11
  42.7 1.5 %collective-permute-start.8 = (bf16[128,1024]{1,0:T(8,128)(2,1)S(1)}, bf16[128,1024]{1,0:T(8,128)(2,1)S(1)}, u32[]{:S(2)}, u32[]{:S(2)}) collective-permute-start(bf16[128,1024]{1,0:T(8,128)(2,1)S(1)} %get-tuple-element.111), channel_id=1, source_target_pairs={{0,1},{1,0},{2,3},{3,2},{4,5},{5,4},{6,7},{7,6},{8,9},{9,8},{10,11... | collective-permute-start | bytes 786440 | tf_op jit(solution)/shard_map/ppermute | solution.py:382
  43.4 5.9 %collective-permute-start.11 = (bf16[128,1152]{1,0:T(8,128)(2,1)S(1)}, bf16[128,1152]{1,0:T(8,128)(2,1)S(1)}, u32[]{:S(2)}, u32[]{:S(2)}) collective-permute-start(bf16[128,1152]{1,0:T(8,128)(2,1)S(1)} %get-tuple-element.122), channel_id=1, source_target_pairs={{0,1},{1,0},{2,3},{3,2},{4,5},{5,4},{6,7},{7,6},{8,9},{9,8},{10,11... | collective-permute-start | bytes 884744 | tf_op jit(solution)/shard_map/ppermute | solution.py:382
  47.1 7.7 %collective-permute-start.10 = (bf16[128,1024]{1,0:T(8,128)(2,1)}, bf16[128,1024]{1,0:T(8,128)(2,1)S(1)}, u32[]{:S(2)}, u32[]{:S(2)}) collective-permute-start(bf16[128,1024]{1,0:T(8,128)(2,1)} %join.4), channel_id=1, source_target_pairs={{0,2},{1,3},{2,0},{3,1},{4,6},{5,7},{6,4},{7,5},{8,10},{9,11},{10,... | collective-permute-start | bytes 786440 | tf_op jit(solution)/shard_map/ppermute | solution.py:385
  48.8 6.0 %collective-permute-start.9 = (bf16[128,1024]{1,0:T(8,128)(2,1)}, bf16[128,1024]{1,0:T(8,128)(2,1)}, u32[]{:S(2)}, u32[]{:S(2)}) collective-permute-start(bf16[128,1024]{1,0:T(8,128)(2,1)} %get-tuple-element.118), channel_id=1, source_target_pairs={{0,1},{1,0},{2,3},{3,2},{4,5},{5,4},{6,7},{7,6},{8,9},{9,8},{10,11... | collective-permute-start | bytes 786440 | tf_op jit(solution)/shard_map/ppermute | solution.py:382
  48.8 2.8 %collective-permute-start.14 = (bf16[128,896]{1,0:T(8,128)(2,1)}, bf16[128,896]{1,0:T(8,128)(2,1)}, u32[]{:S(2)}, u32[]{:S(2)}) collective-permute-start(bf16[128,896]{1,0:T(8,128)(2,1)} %get-tuple-element.131), channel_id=1, source_target_pairs={{0,1},{1,0},{2,3},{3,2},{4,5},{5,4},{6,7},{7,6},{8,9},{9,8},{10,11... | collective-permute-start | bytes 688136 | tf_op jit(solution)/shard_map/ppermute | solution.py:382
  50.1 7.9 %collective-permute-start.16 = (bf16[64,1152]{1,0:T(8,128)(2,1)}, bf16[64,1152]{1,0:T(8,128)(2,1)S(1)}, u32[]{:S(2)}, u32[]{:S(2)}) collective-permute-start(bf16[64,1152]{1,0:T(8,128)(2,1)} %get-tuple-element.124), channel_id=1, source_target_pairs={{0,4},{4,0},{8,12},{12,8},{16,20},{20,16},{24,28},{28,24},{1,5},{5... | collective-permute-start | bytes 442376 | tf_op jit(solution)/shard_map/ppermute | solution.py:388
  51.6 9.1 %collective-permute-start.13 = (bf16[128,896]{1,0:T(8,128)(2,1)}, bf16[128,896]{1,0:T(8,128)(2,1)S(1)}, u32[]{:S(2)}, u32[]{:S(2)}) collective-permute-start(bf16[128,896]{1,0:T(8,128)(2,1)} %copy-done.11), channel_id=1, source_target_pairs={{0,1},{1,0},{2,3},{3,2},{4,5},{5,4},{6,7},{7,6},{8,9},{9,8},{10,11... | collective-permute-start | bytes 688136 | tf_op jit(solution)/shard_map/ppermute | solution.py:382
  52.6 8.1 %collective-permute-start.15 = (bf16[128,896]{1,0:T(8,128)(2,1)S(1)}, bf16[128,896]{1,0:T(8,128)(2,1)S(1)}, u32[]{:S(2)}, u32[]{:S(2)}) collective-permute-start(bf16[128,896]{1,0:T(8,128)(2,1)S(1)} %join.5), channel_id=1, source_target_pairs={{0,2},{1,3},{2,0},{3,1},{4,6},{5,7},{6,4},{7,5},{8,10},{9,11},{10,... | collective-permute-start | bytes 688136 | tf_op jit(solution)/shard_map/ppermute | solution.py:385
  55.9 5.7 %collective-permute-start.12 = (bf16[64,1024]{1,0:T(8,128)(2,1)S(1)}, bf16[64,1024]{1,0:T(8,128)(2,1)S(1)}, u32[]{:S(2)}, u32[]{:S(2)}) collective-permute-start(bf16[64,1024]{1,0:T(8,128)(2,1)S(1)} %get-tuple-element.127), channel_id=1, source_target_pairs={{0,4},{4,0},{8,12},{12,8},{16,20},{20,16},{24,28},{28,24},{1,5},{5... | collective-permute-start | bytes 393224 | tf_op jit(solution)/shard_map/ppermute | solution.py:388
  58.0 26.3 %copy-start.1 = (f32[128,3072]{1,0:T(8,128)S(1)}, f32[128,3072]{1,0:T(8,128)}, u32[]{:S(2)}) copy-start(f32[128,3072]{1,0:T(8,128)} %x_start.3) | copy-start | bytes 4718596
  58.0 5.3 %collective-permute-start.19 = (bf16[64,1152]{1,0:T(8,128)(2,1)S(1)}, bf16[64,1152]{1,0:T(8,128)(2,1)S(1)}, u32[]{:S(2)}, u32[]{:S(2)}) collective-permute-start(bf16[64,1152]{1,0:T(8,128)(2,1)S(1)} %fusion.6), channel_id=1, source_target_pairs={{0,8},{4,12},{8,0},{12,4},{16,24},{20,28},{24,16},{28,20},{1,9},{5... | collective-permute-start | bytes 442376 | tf_op jit(solution)/shard_map/ppermute | solution.py:459
  60.7 5.3 %collective-permute-start.18 = (bf16[64,896]{1,0:T(8,128)(2,1)S(1)}, bf16[64,896]{1,0:T(8,128)(2,1)S(1)}, u32[]{:S(2)}, u32[]{:S(2)}) collective-permute-start(bf16[64,896]{1,0:T(8,128)(2,1)S(1)} %get-tuple-element.135), channel_id=1, source_target_pairs={{0,4},{4,0},{8,12},{12,8},{16,20},{20,16},{24,28},{28,24},{1,5},{5... | collective-permute-start | bytes 344072 | tf_op jit(solution)/shard_map/ppermute | solution.py:388
  61.6 7.3 %collective-permute-start.17 = (bf16[64,1024]{1,0:T(8,128)(2,1)S(1)}, bf16[64,1024]{1,0:T(8,128)(2,1)S(1)}, u32[]{:S(2)}, u32[]{:S(2)}) collective-permute-start(bf16[64,1024]{1,0:T(8,128)(2,1)S(1)} %fusion.7), channel_id=1, source_target_pairs={{0,8},{4,12},{8,0},{12,4},{16,24},{20,28},{24,16},{28,20},{1,9},{5... | collective-permute-start | bytes 393224 | tf_op jit(solution)/shard_map/ppermute | solution.py:459
  63.3 12.7 %collective-permute-start.21 = (bf16[64,1152]{1,0:T(8,128)(2,1)S(1)}, bf16[64,1152]{1,0:T(8,128)(2,1)S(1)}, u32[]{:S(2)}, u32[]{:S(2)}) collective-permute-start(bf16[64,1152]{1,0:T(8,128)(2,1)S(1)} %fusion), channel_id=1, source_target_pairs={{0,16},{4,20},{8,24},{12,28},{16,0},{20,4},{24,8},{28,12},{1,17},{... | collective-permute-start | bytes 442376 | tf_op jit(solution)/shard_map/ppermute | solution.py:459
  66.0 6.8 %collective-permute-start.22 = (bf16[64,896]{1,0:T(8,128)(2,1)S(1)}, bf16[64,896]{1,0:T(8,128)(2,1)S(1)}, u32[]{:S(2)}, u32[]{:S(2)}) collective-permute-start(bf16[64,896]{1,0:T(8,128)(2,1)S(1)} %fusion.8), channel_id=1, source_target_pairs={{0,8},{4,12},{8,0},{12,4},{16,24},{20,28},{24,16},{28,20},{1,9},{5... | collective-permute-start | bytes 344072 | tf_op jit(solution)/shard_map/ppermute | solution.py:459
  69.0 12.3 %collective-permute-start.20 = (bf16[64,1024]{1,0:T(8,128)(2,1)S(1)}, bf16[64,1024]{1,0:T(8,128)(2,1)S(1)}, u32[]{:S(2)}, u32[]{:S(2)}) collective-permute-start(bf16[64,1024]{1,0:T(8,128)(2,1)S(1)} %fusion.3), channel_id=1, source_target_pairs={{0,16},{4,20},{8,24},{12,28},{16,0},{20,4},{24,8},{28,12},{1,17},{... | collective-permute-start | bytes 393224 | tf_op jit(solution)/shard_map/ppermute | solution.py:459
  72.9 10.2 %collective-permute-start.24 = (bf16[64,896]{1,0:T(8,128)(2,1)S(1)}, bf16[64,896]{1,0:T(8,128)(2,1)S(1)}, u32[]{:S(2)}, u32[]{:S(2)}) collective-permute-start(bf16[64,896]{1,0:T(8,128)(2,1)S(1)} %fusion.4), channel_id=1, source_target_pairs={{0,16},{4,20},{8,24},{12,28},{16,0},{20,4},{24,8},{28,12},{1,17},{... | collective-permute-start | bytes 344072 | tf_op jit(solution)/shard_map/ppermute | solution.py:459
  76.2 8.2 %collective-permute-start.26 = (bf16[64,1152]{1,0:T(8,128)(2,1)S(1)}, bf16[64,1152]{1,0:T(8,128)(2,1)S(1)}, u32[]{:S(2)}, u32[]{:S(2)}) collective-permute-start(bf16[64,1152]{1,0:T(8,128)(2,1)S(1)} %get-tuple-element.153), channel_id=1, source_target_pairs={{0,4},{4,0},{8,12},{12,8},{16,20},{20,16},{24,28},{28,24},{1,5},{5... | collective-permute-start | bytes 442376 | tf_op jit(solution)/shard_map/ppermute | solution.py:388
  81.4 7.1 %collective-permute-start.23 = (bf16[64,1024]{1,0:T(8,128)(2,1)S(1)}, bf16[64,1024]{1,0:T(8,128)(2,1)S(1)}, u32[]{:S(2)}, u32[]{:S(2)}) collective-permute-start(bf16[64,1024]{1,0:T(8,128)(2,1)S(1)} %get-tuple-element.151), channel_id=1, source_target_pairs={{0,4},{4,0},{8,12},{12,8},{16,20},{20,16},{24,28},{28,24},{1,5},{5... | collective-permute-start | bytes 393224 | tf_op jit(solution)/shard_map/ppermute | solution.py:388
  83.2 5.3 %collective-permute-start.25 = (bf16[64,896]{1,0:T(8,128)(2,1)S(1)}, bf16[64,896]{1,0:T(8,128)(2,1)S(1)}, u32[]{:S(2)}, u32[]{:S(2)}) collective-permute-start(bf16[64,896]{1,0:T(8,128)(2,1)S(1)} %get-tuple-element.149), channel_id=1, source_target_pairs={{0,4},{4,0},{8,12},{12,8},{16,20},{20,16},{24,28},{28,24},{1,5},{5... | collective-permute-start | bytes 344072 | tf_op jit(solution)/shard_map/ppermute | solution.py:388

commit v15 on v14

--- a/solution.py
+++ b/solution.py
@@ -28,13 +28,13 @@
     pieces = sem.shape[0] - 1
     block = x_hbm.shape[1] // pieces
     t = t_ref[0]
-    mod_copy = pltpu.make_async_copy(mod_hbm.at[pl.ds(t, 1), :], mod_ref, sem.at[pieces])
-    mod_copy.start()
     copies = []
     for i in range(pieces):
         here = pl.ds(i * block, block)
         copies.append(pltpu.make_async_copy(x_hbm.at[0, here, :], x_ref.at[here, :], sem.at[i]))
         copies[i].start()
+    mod_copy = pltpu.make_async_copy(mod_hbm.at[pl.ds(t, 1), :], mod_ref, sem.at[pieces])
+    mod_copy.start()
     mod_copy.wait()
     shift = mod_ref[:, :width]
     scale = 1.0 + mod_ref[:, width : 2 * width]
@@ -373,7 +373,7 @@
     groups = n_step // 2
     half = rows // 2
     unit = width // 24
-    counts = [n * unit for n in (9,8,7)]
+    counts = [n * unit for n in (8, 7, 9)]
     chunks = len(counts)
     firsts = [sum(counts[:c]) for c in range(chunks)]
     qg, kg = q_gain[None, :], k_gain[None, :]
@@ -520,6 +520,8 @@
     last = None
     for _, c, i in sorted(turns):
         compute, move = plan[c][i]
+        if c == chunks - 1 and i == len(plan[c]) - 2:
+            inbox[c], inbox[0] = tied(inbox[c], inbox[0])
         fetched = inbox[c]
         if last is not None:
             fetched, last = tied(fetched, last)

time: 90 us -> 93 us (1.033)
  waiting for transfers between devices: 20.2 us -> 25.1 us
  starting transfers between devices: 29.8 us -> 28 us
  Pallas kernels: 34.1 us -> 32.8 us
  local copies, waits for them, and re-layouts: 4.1 us -> 5.28 us
    ppermute x6, waiting for transfers between devices: 3.22 us -> 9.42 us  [to_pair(): return lax.ppermute(x, 'step', [(i, i ^ 1) for i in range(n_step)])]
    ppermute x6, waiting for transfers between devices: 6.95 us -> 5.47 us  [along(): lax.ppermute(x, 'step', [(2 * a + i, 2 * b + i) for a, b in pairs for i i...]
    unnamed x30 -> x34, local copies, waits for them, and re-layouts: 4.1 us -> 5.28 us
    ppermute x6, starting transfers between devices: 8.84 us -> 7.78 us  [to_pair(): return lax.ppermute(x, 'step', [(i, i ^ 1) for i in range(n_step)])]
    pallas_call x3, Pallas kernels: 1.78 us -> 0.85 us  [join_call(): pl.pallas_call(join_kernel, in_specs=[vm, vm], out_specs=vm, out_shape=ja...]
  transfers between devices with their start and end apart: 27 -> 27, of which waited for: 11 -> 12; matrix products, arithmetic and copies ran while one was open for 0% -> 0% of each run, Pallas kernels for 24% -> 22%
where the time goes in v15:
time: 93 us; the launch traced here: 92.7 us
  Pallas kernels  32.8 us (35%)
  starting transfers between devices  28 us (30%)
  waiting for transfers between devices  25.1 us (27%)
  local copies, waits for them, and re-layouts  5.28 us (6%)
  between operations  1.1 us (1%)
    pallas_call x2, Pallas kernels, project_call(): pl.pallas_call(functools.partial(project_kernel, tile, load, tiles), in_s...  17.6 us
    ppermute x6, starting transfers between devices, along(): lax.ppermute(x, 'step', [(2 * a + i, 2 * b + i) for a, b in pairs for i i...  11.8 us
    ppermute x6, waiting for transfers between devices, to_pair(): return lax.ppermute(x, 'step', [(i, i ^ 1) for i in range(n_step)])  9.42 us
    ppermute x6, starting transfers between devices, to_pair(): return lax.ppermute(x, 'step', [(i, i ^ 1) for i in range(n_step)])  7.78 us
    ppermute x5, waiting for transfers between devices, to_chip(): lax.ppermute(x, 'seq', [(i, (i + 2 * offset) % n_seq) for i in range(n_se...  7.18 us
    ppermute x5, starting transfers between devices, to_chip(): lax.ppermute(x, 'seq', [(i, (i + 2 * offset) % n_seq) for i in range(n_se...  7.08 us
    ppermute x6, waiting for transfers between devices, along(): lax.ppermute(x, 'step', [(2 * a + i, 2 * b + i) for a, b in pairs for i i...  5.47 us
    unnamed x34, local copies, waits for them, and re-layouts  5.28 us
  transfers between devices with their start and end apart: 27, of which 12 were waited for; matrix products, arithmetic and copies ran while one was open for 0% of the time, Pallas kernels for 22%

profile of v15, /device:TPU:0, one launch (start us, length us, event | category | flops | bytes accessed | tf_op | source)
XLA Modules:
  0.0 92.7 jit_solution(14419594068192027659)
XLA Ops:
  0.7 3.8 %norm.1 = (bf16[64,3072]{1,0:T(8,128)(2,1)}, bf16[64,3072]{1,0:T(8,128)(2,1)}, f32[1,3072]{1,0:T(1,128)}) custom-call(s32[1]{0:T(128)S(6)} %copy.14.t_ref, f32[50]{0:T(128)} %size_ref.1, f32[1,128,3072]{2,1,0:T(8,128)} %x_hbm.1, f32[50,9216]{1,0:T(8,128)} %mod_hbm.1), custom_call_target="tpu_custom_call" | custom-call | flops 3932160 | tf_op jit(solution)/shard_map/norm/pallas_call | solution.py:61
  4.5 0.5 collective-permute-start.1
  5.0 0.1 collective-permute-start.2
  5.1 2.9 %collective-permute-start = (bf16[64,3072]{1,0:T(8,128)(2,1)}, bf16[64,3072]{1,0:T(8,128)(2,1)S(1)}, u32[]{:S(2)}, u32[]{:S(2)}) collective-permute-start(bf16[64,3072]{1,0:T(8,128)(2,1)} %get-tuple-element.79.m0), channel_id=1, source_target_pairs={{0,2},{1,3},{2,0},{3,1},{4,6},{5,7},{6,4},{7,5},{8,10},{9,11},{10,... | collective-permute-start | bytes 1179656 | tf_op jit(solution)/shard_map/ppermute | solution.py:385
  8.1 0.0 collective-permute-start.3
  8.1 0.0 collective-permute-done.2.m3
  8.1 1.0 %copy-done.2 = bf16[64,3072]{1,0:T(8,128)(2,1)S(1)} copy-done((bf16[64,3072]{1,0:T(8,128)(2,1)S(1)}, bf16[64,3072]{1,0:T(8,128)(2,1)}, u32[]{:S(2)}) %copy-start.2) | copy-done | bytes 393240
  9.1 1.0 %copy-done.3 = bf16[64,3072]{1,0:T(8,128)(2,1)S(1)} copy-done((bf16[64,3072]{1,0:T(8,128)(2,1)S(1)}, bf16[64,3072]{1,0:T(8,128)(2,1)}, u32[]{:S(2)}) %copy-start.3) | copy-done | bytes 393240
  10.1 12.4 %project.2 = (bf16[256,512]{1,0:T(8,128)(2,1)S(1)}, bf16[256,512]{1,0:T(8,128)(2,1)S(1)}, bf16[256,512]{1,0:T(8,128)(2,1)S(1)}, bf16[256,1536]{1,0:T(8,128)(2,1)...) custom-call(bf16[64,3072]{1,0:T(8,128)(2,1)S(1)} %copy-done.3, ...), custom_call_target="tpu_custom_call" | custom-call | flops 4831838208 | tf_op jit(solution)/shard_map/project/pallas_call | solution.py:158
  22.5 0.0 copy-start.10
  22.5 0.7 copy-done.10
  23.2 0.7 copy-done.12
  23.9 2.1 %collective-permute-done.3.m1 = bf16[64,3072]{1,0:T(8,128)(2,1)S(1)} collective-permute-done((bf16[64,3072]{1,0:T(8,128)(2,1)}, bf16[64,3072]{1,0:T(8,128)(2,1)S(1)}, u32[]{:S(2)}, u32[]{:S(2)}) %collective-permute-start.3) | collective-permute-done | bytes 393248 | tf_op jit(solution)/shard_map/ppermute | solution.py:385
  26.0 0.0 collective-permute-done.4.m2
  26.0 0.0 collective-permute-start.5
  26.0 1.7 %collective-permute-done.5.m3 = bf16[64,3072]{1,0:T(8,128)(2,1)S(1)} collective-permute-done((bf16[64,3072]{1,0:T(8,128)(2,1)S(1)}, bf16[64,3072]{1,0:T(8,128)(2,1)S(1)}, u32[]{:S(2)}, u32[]{:S(2)}) %collective-permute-start.5) | collective-permute-done | bytes 393248 | tf_op jit(solution)/shard_map/ppermute | solution.py:382
  27.8 0.0 copy-start
  27.8 5.2 %project.3 = (bf16[256,512]{1,0:T(8,128)(2,1)S(1)}, bf16[256,512]{1,0:T(8,128)(2,1)S(1)}, bf16[256,512]{1,0:T(8,128)(2,1)S(1)}, bf16[256,1536]{1,0:T(8,128)(2,1)S(1)}) custom-call(bf16[64,3072]{1,0:T(8,128)(2,1)S(1)} %collective-permute-done.m0, bf16[64,3072]{1,0:T(8,128)(2,1)S(1)} %collective-permute-done.3.m1, ...), custom_call_target="tpu_custom_call" | custom-call | flops 4831838208 | tf_op jit(solution)/shard_map/project/pallas_call | solution.py:158
  33.1 1.1 %attend.2.refs_0_.refs_4_ = bf16[256,512]{1,0:T(8,128)(2,1)S(1)} custom-call(bf16[256,512]{1,0:T(8,128)(2,1)S(1)} %get-tuple-element.91.refs_0_, bf16[256,512]{1,0:T(8,128)(2,1)S(1)} %copy-done.11, bf16[256,512]{1,0:T(8,128)(2,1)S(1)} %get-tuple-element.93.refs_2_, bf16[256,512]{1,0:T(8,128)(2,1)S(1)} %copy-done.13, ...), custom_call_target="tpu_custom_call" | custom-call | flops 805306368 | tf_op jit(solution)/shard_map/attend/pallas_call | solution.py:202
  34.2 1.2 %project_out.2 = (f32[128,1024]{1,0:T(8,128)S(1)}, bf16[128,1024]{1,0:T(8,128)(2,1)S(1)}) custom-call(bf16[256,512]{1,0:T(8,128)(2,1)S(1)} %attend.2.refs_0_.refs_4_, bf16[256,1536]{1,0:T(8,128)(2,1)S(1)} %get-tuple-element.106.refs_1_.refs_5_, bf16[512,3072]{1,0:T(8,128)(2,1)S(1)} %copy-done, bf16[1536,3072]{1,0:T(8,128)(2,1)S(1)} %bitcast.4), custom_call_target="tpu_custom_call" | custom-call | flops 1073741824 | tf_op jit(solution)/shard_map/project_out/pallas_call | solution.py:246
  35.5 0.2 collective-permute-start.6
  35.7 0.9 attend.3.refs_8_.refs_12_.refs_16_
  36.5 0.5 collective-permute-done.6.sent
  37.1 1.8 %collective-permute-start.7 = (bf16[128,1024]{1,0:T(8,128)(2,1)S(1)}, bf16[128,1024]{1,0:T(8,128)(2,1)S(1)}, u32[]{:S(2)}, u32[]{:S(2)}) collective-permute-start(bf16[128,1024]{1,0:T(8,128)(2,1)S(1)} %join.3), channel_id=1, source_target_pairs={{0,2},{1,3},{2,0},{3,1},{4,6},{5,7},{6,4},{7,5},{8,10},{9,11},{10,... | collective-permute-start | bytes 786440 | tf_op jit(solution)/shard_map/ppermute | solution.py:385
  38.9 3.9 %project_out.3 = (f32[128,896]{1,0:T(8,128)S(1)}, bf16[128,896]{1,0:T(8,128)(2,1)S(1)}, f32[128,1152]{1,0:T(8,128)S(1)}, bf16[128,1152]{1,0:T(8,128)(2,1)}, f32[...) custom-call(bf16[256,512]{1,0:T(8,128)(2,1)S(1)} %attend.2.refs_0_.r, ...), custom_call_target="tpu_custom_call" | custom-call | flops 2952790016 | tf_op jit(solution)/shard_map/project_out/pallas_call | solution.py:246
  42.9 0.5 collective-permute-start.11
  43.4 0.2 copy-done.9
  43.6 0.8 collective-permute-done.8.sent
  44.3 1.2 %collective-permute-done.7.refs_0_ = bf16[128,1024]{1,0:T(8,128)(2,1)S(1)} collective-permute-done((bf16[128,1024]{1,0:T(8,128)(2,1)S(1)}, bf16[128,1024]{1,0:T(8,128)(2,1)S(1)}, u32[]{:S(2)}, u32[]{:S(2)}) %collective-permute-start.7) | collective-permute-done | bytes 262176 | tf_op jit(solution)/shard_map/ppermute | solution.py:385
  45.5 0.7 join.4
  46.3 1.7 %collective-permute-start.10 = (bf16[128,896]{1,0:T(8,128)(2,1)}, bf16[128,896]{1,0:T(8,128)(2,1)}, u32[]{:S(2)}, u32[]{:S(2)}) collective-permute-start(bf16[128,896]{1,0:T(8,128)(2,1)} %join.4), channel_id=1, source_target_pairs={{0,2},{1,3},{2,0},{3,1},{4,6},{5,7},{6,4},{7,5},{8,10},{9,11},{10,... | collective-permute-start | bytes 688136 | tf_op jit(solution)/shard_map/ppermute | solution.py:385
  48.0 0.7 copy-done.4
  48.7 0.9 %copy-done.5 = bf16[128,1024]{1,0:T(8,128)(2,1)S(1)} copy-done((bf16[128,1024]{1,0:T(8,128)(2,1)S(1)}, bf16[128,1024]{1,0:T(8,128)(2,1)}, u32[]{:S(2)}) %copy-start.5) | copy-done | bytes 262168
  49.7 0.1 drift.3
  49.8 1.6 %collective-permute-start.16 = (bf16[64,1024]{1,0:T(8,128)(2,1)S(1)}, bf16[64,1024]{1,0:T(8,128)(2,1)S(1)}, u32[]{:S(2)}, u32[]{:S(2)}) collective-permute-start(bf16[64,1024]{1,0:T(8,128)(2,1)S(1)} %get-tuple-element.126), channel_id=1, source_target_pairs={{0,4},{4,0},{8,12},{12,8},{16,20},{20,16},{24,28},{28,24},{1,5},{5... | collective-permute-start | bytes 393224 | tf_op jit(solution)/shard_map/ppermute | solution.py:388
  51.4 0.1 join.5
  51.4 0.6 collective-permute-start.15
  52.0 1.4 %collective-permute-done.10.refs_0_ = bf16[128,896]{1,0:T(8,128)(2,1)} collective-permute-done((bf16[128,896]{1,0:T(8,128)(2,1)}, bf16[128,896]{1,0:T(8,128)(2,1)}, u32[]{:S(2)}, u32[]{:S(2)}) %collective-permute-start.10) | collective-permute-done | bytes 229408 | tf_op jit(solution)/shard_map/ppermute | solution.py:385
  53.4 1.1 %drift.4 = (f32[64,896]{1,0:T(8,128)S(1)}, f32[64,896]{1,0:T(8,128)S(1)}, bf16[64,896]{1,0:T(8,128)(2,1)S(1)}) custom-call(s32[1]{0:T(128)} %bitcast.parity, f32[128,896]{1,0:T(8,128)S(1)} %get-tuple-element.119.keep, bf16[128,896]{1,0:T(8,128)(2,1)} %collective-permute-done.9.sent, f32[1,3072]{1,0:T(1,128)S(1)} %copy-done.6, ...), custom_call_target="tpu_custom_call" | custom-call | tf_op jit(solution)/shard_map/drift/pallas_call | solution.py:297
  54.6 2.2 %collective-permute-start.12 = (bf16[64,896]{1,0:T(8,128)(2,1)S(1)}, bf16[64,896]{1,0:T(8,128)(2,1)S(1)}, u32[]{:S(2)}, u32[]{:S(2)}) collective-permute-start(bf16[64,896]{1,0:T(8,128)(2,1)S(1)} %get-tuple-element.129), channel_id=1, source_target_pairs={{0,4},{4,0},{8,12},{12,8},{16,20},{20,16},{24,28},{28,24},{1,5},{5... | collective-permute-start | bytes 344072 | tf_op jit(solution)/shard_map/ppermute | solution.py:388
  56.8 1.4 %collective-permute-start.19 = (bf16[64,1024]{1,0:T(8,128)(2,1)S(1)}, bf16[64,1024]{1,0:T(8,128)(2,1)S(1)}, u32[]{:S(2)}, u32[]{:S(2)}) collective-permute-start(bf16[64,1024]{1,0:T(8,128)(2,1)S(1)} %fusion.7), channel_id=1, source_target_pairs={{0,8},{4,12},{8,0},{12,4},{16,24},{20,28},{24,16},{28,20},{1,9},{5... | collective-permute-start | bytes 393224 | tf_op jit(solution)/shard_map/ppermute | solution.py:459
  58.2 2.4 %collective-permute-done.15.refs_0_ = bf16[128,1152]{1,0:T(8,128)(2,1)S(1)} collective-permute-done((bf16[128,1152]{1,0:T(8,128)(2,1)S(1)}, bf16[128,1152]{1,0:T(8,128)(2,1)S(1)}, u32[]{:S(2)}, u32[]{:S(2)}) %collective-permute-start.15) | collective-permute-done | bytes 294944 | tf_op jit(solution)/shard_map/ppermute | solution.py:385
  60.6 0.1 drift.5
  60.7 0.0 copy-start.1
  60.8 0.8 collective-permute-start.18
  61.6 1.6 %collective-permute-start.17 = (bf16[64,896]{1,0:T(8,128)(2,1)S(1)}, bf16[64,896]{1,0:T(8,128)(2,1)S(1)}, u32[]{:S(2)}, u32[]{:S(2)}) collective-permute-start(bf16[64,896]{1,0:T(8,128)(2,1)S(1)} %fusion.8), channel_id=1, source_target_pairs={{0,8},{4,12},{8,0},{12,4},{16,24},{20,28},{24,16},{28,20},{1,9},{5... | collective-permute-start | bytes 344072 | tf_op jit(solution)/shard_map/ppermute | solution.py:459
  63.3 2.6 %collective-permute-start.21 = (bf16[64,1024]{1,0:T(8,128)(2,1)S(1)}, bf16[64,1024]{1,0:T(8,128)(2,1)S(1)}, u32[]{:S(2)}, u32[]{:S(2)}) collective-permute-start(bf16[64,1024]{1,0:T(8,128)(2,1)S(1)} %fusion.2), channel_id=1, source_target_pairs={{0,16},{4,20},{8,24},{12,28},{16,0},{20,4},{24,8},{28,12},{1,17},{... | collective-permute-start | bytes 393224 | tf_op jit(solution)/shard_map/ppermute | solution.py:459
  65.9 0.1 collective-permute-done.18.refs_7_
  66.0 1.6 %collective-permute-start.22 = (bf16[64,1152]{1,0:T(8,128)(2,1)S(1)}, bf16[64,1152]{1,0:T(8,128)(2,1)S(1)}, u32[]{:S(2)}, u32[]{:S(2)}) collective-permute-start(bf16[64,1152]{1,0:T(8,128)(2,1)S(1)} %fusion.6), channel_id=1, source_target_pairs={{0,8},{4,12},{8,0},{12,4},{16,24},{20,28},{24,16},{28,20},{1,9},{5... | collective-permute-start | bytes 442376 | tf_op jit(solution)/shard_map/ppermute | solution.py:459
  67.7 2.7 %collective-permute-start.20 = (bf16[64,896]{1,0:T(8,128)(2,1)S(1)}, bf16[64,896]{1,0:T(8,128)(2,1)S(1)}, u32[]{:S(2)}, u32[]{:S(2)}) collective-permute-start(bf16[64,896]{1,0:T(8,128)(2,1)S(1)} %fusion.5), channel_id=1, source_target_pairs={{0,16},{4,20},{8,24},{12,28},{16,0},{20,4},{24,8},{28,12},{1,17},{... | collective-permute-start | bytes 344072 | tf_op jit(solution)/shard_map/ppermute | solution.py:459
  70.4 3.7 %collective-permute-done.22 = bf16[64,1152]{1,0:T(8,128)(2,1)S(1)} collective-permute-done((bf16[64,1152]{1,0:T(8,128)(2,1)S(1)}, bf16[64,1152]{1,0:T(8,128)(2,1)S(1)}, u32[]{:S(2)}, u32[]{:S(2)}) %collective-permute-start.22) | collective-permute-done | bytes 147488 | tf_op jit(solution)/shard_map/ppermute | solution.py:459
  74.1 0.1 fusion
  74.2 1.7 %collective-permute-start.24 = (bf16[64,1152]{1,0:T(8,128)(2,1)S(1)}, bf16[64,1152]{1,0:T(8,128)(2,1)S(1)}, u32[]{:S(2)}, u32[]{:S(2)}) collective-permute-start(bf16[64,1152]{1,0:T(8,128)(2,1)S(1)} %fusion), channel_id=1, source_target_pairs={{0,16},{4,20},{8,24},{12,28},{16,0},{20,4},{24,8},{28,12},{1,17},{... | collective-permute-start | bytes 442376 | tf_op jit(solution)/shard_map/ppermute | solution.py:459
  75.9 0.1 add_convert_fusion.1
  76.0 1.2 %collective-permute-start.25 = (bf16[64,1024]{1,0:T(8,128)(2,1)S(1)}, bf16[64,1024]{1,0:T(8,128)(2,1)S(1)}, u32[]{:S(2)}, u32[]{:S(2)}) collective-permute-start(bf16[64,1024]{1,0:T(8,128)(2,1)S(1)} %get-tuple-element.157), channel_id=1, source_target_pairs={{0,4},{4,0},{8,12},{12,8},{16,20},{20,16},{24,28},{28,24},{1,5},{5... | collective-permute-start | bytes 393224 | tf_op jit(solution)/shard_map/ppermute | solution.py:388
  77.2 0.1 add_convert_fusion.2
  77.2 3.8 %collective-permute-done.25.refs_4_ = bf16[64,1024]{1,0:T(8,128)(2,1)S(1)} collective-permute-done((bf16[64,1024]{1,0:T(8,128)(2,1)S(1)}, bf16[64,1024]{1,0:T(8,128)(2,1)S(1)}, u32[]{:S(2)}, u32[]{:S(2)}) %collective-permute-start.25) | collective-permute-done | bytes 131104 | tf_op jit(solution)/shard_map/ppermute | solution.py:388
  81.0 1.7 %collective-permute-done.24 = bf16[64,1152]{1,0:T(8,128)(2,1)S(1)} collective-permute-done((bf16[64,1152]{1,0:T(8,128)(2,1)S(1)}, bf16[64,1152]{1,0:T(8,128)(2,1)S(1)}, u32[]{:S(2)}, u32[]{:S(2)}) %collective-permute-start.24) | collective-permute-done | bytes 147488 | tf_op jit(solution)/shard_map/ppermute | solution.py:459
  82.8 0.1 add_convert_fusion
  82.9 1.2 %collective-permute-start.26 = (bf16[64,1152]{1,0:T(8,128)(2,1)S(1)}, bf16[64,1152]{1,0:T(8,128)(2,1)S(1)}, u32[]{:S(2)}, u32[]{:S(2)}) collective-permute-start(bf16[64,1152]{1,0:T(8,128)(2,1)S(1)} %get-tuple-element.153), channel_id=1, source_target_pairs={{0,4},{4,0},{8,12},{12,8},{16,20},{20,16},{24,28},{28,24},{1,5},{5... | collective-permute-start | bytes 442376 | tf_op jit(solution)/shard_map/ppermute | solution.py:388
  84.0 0.9 collective-permute-start.23
  85.0 5.6 %collective-permute-done.23.refs_4_ = bf16[64,896]{1,0:T(8,128)(2,1)S(1)} collective-permute-done((bf16[64,896]{1,0:T(8,128)(2,1)S(1)}, bf16[64,896]{1,0:T(8,128)(2,1)S(1)}, u32[]{:S(2)}, u32[]{:S(2)}) %collective-permute-start.23) | collective-permute-done | bytes 114720 | tf_op jit(solution)/shard_map/ppermute | solution.py:388
  90.5 0.9 finish.2.refs_10_
  91.4 1.1 %finish.3 = f32[1,128,3072]{2,1,0:T(8,128)} custom-call(s32[1]{0:T(128)} %bitcast.parity, f32[128,3072]{1,0:T(8,128)S(1)} %copy-done.1, f32[64,896]{1,0:T(8,128)S(1)} %get-tuple-element.156.refs_0_, f32[64,896]{1,0:T(8,128)S(1)} %get-tuple-element.128.refs_1_, bf16[64,896]{1,0:T(8,128)(2,1)S(1)} %collective-permute-done.12.refs_2_, ...), custom_call_target="tpu_custom_call", output_to_operand_aliasing={{}: (12, {})} | custom-call | tf_op jit(solution)/shard_map/finish/pallas_call | solution.py:342
  (49 shorter events, 0.3 us)
Async XLA Ops:
  0.0 8.1 %copy-start.7 = (f32[128]{0:T(128)S(1)}, f32[128]{0:T(128)}, u32[]{:S(2)}) copy-start(f32[128]{0:T(128)} %param.16) | copy-start | bytes 1540
  0.0 8.1 %copy-start.8 = (f32[128]{0:T(128)S(1)}, f32[128]{0:T(128)}, u32[]{:S(2)}) copy-start(f32[128]{0:T(128)} %param.17) | copy-start | bytes 1540
  4.5 3.6 %collective-permute-start.1 = (bf16[64,3072]{1,0:T(8,128)(2,1)}, bf16[64,3072]{1,0:T(8,128)(2,1)S(1)}, u32[]{:S(2)}, u32[]{:S(2)}) collective-permute-start(bf16[64,3072]{1,0:T(8,128)(2,1)} %get-tuple-element.79.m0), channel_id=1, source_target_pairs={{0,1},{1,0},{2,3},{3,2},{4,5},{5,4},{6,7},{7,6},{8,9},{9,8},{10,11... | collective-permute-start | bytes 1179656 | tf_op jit(solution)/shard_map/ppermute | solution.py:382
  5.0 3.1 %collective-permute-start.2 = (bf16[64,3072]{1,0:T(8,128)(2,1)}, bf16[64,3072]{1,0:T(8,128)(2,1)S(1)}, u32[]{:S(2)}, u32[]{:S(2)}) collective-permute-start(bf16[64,3072]{1,0:T(8,128)(2,1)} %get-tuple-element.80.m1), channel_id=1, source_target_pairs={{0,1},{1,0},{2,3},{3,2},{4,5},{5,4},{6,7},{7,6},{8,9},{9,8},{10,11... | collective-permute-start | bytes 1179656 | tf_op jit(solution)/shard_map/ppermute | solution.py:382
  5.1 18.8 %collective-permute-start = (bf16[64,3072]{1,0:T(8,128)(2,1)}, bf16[64,3072]{1,0:T(8,128)(2,1)S(1)}, u32[]{:S(2)}, u32[]{:S(2)}) collective-permute-start(bf16[64,3072]{1,0:T(8,128)(2,1)} %get-tuple-element.79.m0), channel_id=1, source_target_pairs={{0,2},{1,3},{2,0},{3,1},{4,6},{5,7},{6,4},{7,5},{8,10},{9,11},{10,... | collective-permute-start | bytes 1179656 | tf_op jit(solution)/shard_map/ppermute | solution.py:385
  8.1 18.0 %collective-permute-start.3 = (bf16[64,3072]{1,0:T(8,128)(2,1)}, bf16[64,3072]{1,0:T(8,128)(2,1)S(1)}, u32[]{:S(2)}, u32[]{:S(2)}) collective-permute-start(bf16[64,3072]{1,0:T(8,128)(2,1)} %get-tuple-element.80.m1), channel_id=1, source_target_pairs={{0,2},{1,3},{2,0},{3,1},{4,6},{5,7},{6,4},{7,5},{8,10},{9,11},{10,... | collective-permute-start | bytes 1179656 | tf_op jit(solution)/shard_map/ppermute | solution.py:385
  8.1 1.0 %copy-start.2 = (bf16[64,3072]{1,0:T(8,128)(2,1)S(1)}, bf16[64,3072]{1,0:T(8,128)(2,1)}, u32[]{:S(2)}) copy-start(bf16[64,3072]{1,0:T(8,128)(2,1)} %get-tuple-element.80.m1) | copy-start | bytes 1179652
  9.1 1.0 %copy-start.3 = (bf16[64,3072]{1,0:T(8,128)(2,1)S(1)}, bf16[64,3072]{1,0:T(8,128)(2,1)}, u32[]{:S(2)}) copy-start(bf16[64,3072]{1,0:T(8,128)(2,1)} %get-tuple-element.79.m0) | copy-start | bytes 1179652
  22.5 0.7 copy-start.10
  23.2 0.7 copy-start.12
  23.9 2.1 %collective-permute-start.4 = (bf16[64,3072]{1,0:T(8,128)(2,1)S(1)}, bf16[64,3072]{1,0:T(8,128)(2,1)S(1)}, u32[]{:S(2)}, u32[]{:S(2)}) collective-permute-start(bf16[64,3072]{1,0:T(8,128)(2,1)S(1)} %collective-permute-done.m0), channel_id=1, source_target_pairs={{0,1},{1,0},{2,3},{3,2},{4,5},{5,4},{6,7},{7,6},{8,9},{9,8},{10,11... | collective-permute-start | bytes 1179656 | tf_op jit(solution)/shard_map/ppermute | solution.py:382
  26.0 1.7 %collective-permute-start.5 = (bf16[64,3072]{1,0:T(8,128)(2,1)S(1)}, bf16[64,3072]{1,0:T(8,128)(2,1)S(1)}, u32[]{:S(2)}, u32[]{:S(2)}) collective-permute-start(bf16[64,3072]{1,0:T(8,128)(2,1)S(1)} %collective-permute-done.3.m1), channel_id=1, source_target_pairs={{0,1},{1,0},{2,3},{3,2},{4,5},{5,4},{6,7},{7,6},{8,9},{9,8},{10,11... | collective-permute-start | bytes 1179656 | tf_op jit(solution)/shard_map/ppermute | solution.py:382
  27.8 6.4 %slice-start = ((s8[9437184]{0:T(1024)(128)(4,1)}), s8[4194304]{0:T(1024)(128)(4,1)S(1)}, s32[]{:S(2)}) async-start(s8[9437184]{0:T(1024)(128)(4,1)} %bitcast.3), calls=%async_computation | async-start | bytes 8388608
  27.8 5.3 %copy-start.11 = (bf16[256,512]{1,0:T(8,128)(2,1)S(1)}, bf16[256,512]{1,0:T(8,128)(2,1)}, u32[]{:S(2)}) copy-start(bf16[256,512]{1,0:T(8,128)(2,1)} %copy-done.10) | copy-start | bytes 786436
  27.8 5.3 %copy-start.13 = (bf16[256,512]{1,0:T(8,128)(2,1)S(1)}, bf16[256,512]{1,0:T(8,128)(2,1)}, u32[]{:S(2)}) copy-start(bf16[256,512]{1,0:T(8,128)(2,1)} %copy-done.12) | copy-start | bytes 786436
  27.8 6.4 %slice-start.1 = ((s8[9437184]{0:T(1024)(128)(4,1)}), s8[4194304]{0:T(1024)(128)(4,1)S(1)}, s32[]{:S(2)}) async-start(s8[9437184]{0:T(1024)(128)(4,1)} %bitcast.3), calls=%async_computation.1 | async-start | bytes 8388608
  27.8 6.4 %slice-start.2 = ((s8[9437184]{0:T(1024)(128)(4,1)}), s8[1048576]{0:T(1024)(128)(4,1)S(1)}, s32[]{:S(2)}) async-start(s8[9437184]{0:T(1024)(128)(4,1)} %bitcast.3), calls=%async_computation.2 | async-start | bytes 2097152
  27.8 6.4 %copy-start = (bf16[512,3072]{1,0:T(8,128)(2,1)S(1)}, bf16[512,3072]{1,0:T(8,128)(2,1)}, u32[]{:S(2)}) copy-start(bf16[512,3072]{1,0:T(8,128)(2,1)} %refs_17_.1) | copy-start | bytes 9437188
  35.5 1.6 %collective-permute-start.6 = (bf16[128,1024]{1,0:T(8,128)(2,1)S(1)}, bf16[128,1024]{1,0:T(8,128)(2,1)S(1)}, u32[]{:S(2)}, u32[]{:S(2)}) collective-permute-start(bf16[128,1024]{1,0:T(8,128)(2,1)S(1)} %get-tuple-element.99), channel_id=1, source_target_pairs={{0,1},{1,0},{2,3},{3,2},{4,5},{5,4},{6,7},{7,6},{8,9},{9,8},{10,11... | collective-permute-start | bytes 786440 | tf_op jit(solution)/shard_map/ppermute | solution.py:382
  37.1 8.4 %collective-permute-start.7 = (bf16[128,1024]{1,0:T(8,128)(2,1)S(1)}, bf16[128,1024]{1,0:T(8,128)(2,1)S(1)}, u32[]{:S(2)}, u32[]{:S(2)}) collective-permute-start(bf16[128,1024]{1,0:T(8,128)(2,1)S(1)} %join.3), channel_id=1, source_target_pairs={{0,2},{1,3},{2,0},{3,1},{4,6},{5,7},{6,4},{7,5},{8,10},{9,11},{10,... | collective-permute-start | bytes 786440 | tf_op jit(solution)/shard_map/ppermute | solution.py:385
  38.9 9.8 %copy-start.6 = (f32[1,3072]{1,0:T(1,128)S(1)}, f32[1,3072]{1,0:T(1,128)}, u32[]{:S(2)}) copy-start(f32[1,3072]{1,0:T(1,128)} %get-tuple-element.121.sg) | copy-start | bytes 36868
  42.8 0.7 copy-start.9
  42.8 1.5 %collective-permute-start.8 = (bf16[128,896]{1,0:T(8,128)(2,1)S(1)}, bf16[128,896]{1,0:T(8,128)(2,1)S(1)}, u32[]{:S(2)}, u32[]{:S(2)}) collective-permute-start(bf16[128,896]{1,0:T(8,128)(2,1)S(1)} %get-tuple-element.113), channel_id=1, source_target_pairs={{0,1},{1,0},{2,3},{3,2},{4,5},{5,4},{6,7},{7,6},{8,9},{9,8},{10,11... | collective-permute-start | bytes 688136 | tf_op jit(solution)/shard_map/ppermute | solution.py:382
  42.9 5.2 %collective-permute-start.11 = (bf16[128,1024]{1,0:T(8,128)(2,1)S(1)}, bf16[128,1024]{1,0:T(8,128)(2,1)S(1)}, u32[]{:S(2)}, u32[]{:S(2)}) collective-permute-start(bf16[128,1024]{1,0:T(8,128)(2,1)S(1)} %get-tuple-element.124), channel_id=1, source_target_pairs={{0,1},{1,0},{2,3},{3,2},{4,5},{5,4},{6,7},{7,6},{8,9},{9,8},{10,11... | collective-permute-start | bytes 786440 | tf_op jit(solution)/shard_map/ppermute | solution.py:382
  43.6 7.8 %collective-permute-start.14 = (bf16[128,1152]{1,0:T(8,128)(2,1)}, bf16[128,1152]{1,0:T(8,128)(2,1)S(1)}, u32[]{:S(2)}, u32[]{:S(2)}) collective-permute-start(bf16[128,1152]{1,0:T(8,128)(2,1)} %get-tuple-element.133), channel_id=1, source_target_pairs={{0,1},{1,0},{2,3},{3,2},{4,5},{5,4},{6,7},{7,6},{8,9},{9,8},{10,11... | collective-permute-start | bytes 884744 | tf_op jit(solution)/shard_map/ppermute | solution.py:382
  46.3 7.1 %collective-permute-start.10 = (bf16[128,896]{1,0:T(8,128)(2,1)}, bf16[128,896]{1,0:T(8,128)(2,1)}, u32[]{:S(2)}, u32[]{:S(2)}) collective-permute-start(bf16[128,896]{1,0:T(8,128)(2,1)} %join.4), channel_id=1, source_target_pairs={{0,2},{1,3},{2,0},{3,1},{4,6},{5,7},{6,4},{7,5},{8,10},{9,11},{10,... | collective-permute-start | bytes 688136 | tf_op jit(solution)/shard_map/ppermute | solution.py:385
  48.0 5.4 %collective-permute-start.9 = (bf16[128,896]{1,0:T(8,128)(2,1)}, bf16[128,896]{1,0:T(8,128)(2,1)}, u32[]{:S(2)}, u32[]{:S(2)}) collective-permute-start(bf16[128,896]{1,0:T(8,128)(2,1)} %get-tuple-element.120), channel_id=1, source_target_pairs={{0,1},{1,0},{2,3},{3,2},{4,5},{5,4},{6,7},{7,6},{8,9},{9,8},{10,11... | collective-permute-start | bytes 688136 | tf_op jit(solution)/shard_map/ppermute | solution.py:382
  48.0 0.7 copy-start.4
  48.7 1.0 %copy-start.5 = (bf16[128,1024]{1,0:T(8,128)(2,1)S(1)}, bf16[128,1024]{1,0:T(8,128)(2,1)}, u32[]{:S(2)}) copy-start(bf16[128,1024]{1,0:T(8,128)(2,1)} %copy-done.4) | copy-start | bytes 786436
  49.8 6.9 %collective-permute-start.16 = (bf16[64,1024]{1,0:T(8,128)(2,1)S(1)}, bf16[64,1024]{1,0:T(8,128)(2,1)S(1)}, u32[]{:S(2)}, u32[]{:S(2)}) collective-permute-start(bf16[64,1024]{1,0:T(8,128)(2,1)S(1)} %get-tuple-element.126), channel_id=1, source_target_pairs={{0,4},{4,0},{8,12},{12,8},{16,20},{20,16},{24,28},{28,24},{1,5},{5... | collective-permute-start | bytes 393224 | tf_op jit(solution)/shard_map/ppermute | solution.py:388
  51.4 9.2 %collective-permute-start.15 = (bf16[128,1152]{1,0:T(8,128)(2,1)S(1)}, bf16[128,1152]{1,0:T(8,128)(2,1)S(1)}, u32[]{:S(2)}, u32[]{:S(2)}) collective-permute-start(bf16[128,1152]{1,0:T(8,128)(2,1)S(1)} %join.5), channel_id=1, source_target_pairs={{0,2},{1,3},{2,0},{3,1},{4,6},{5,7},{6,4},{7,5},{8,10},{9,11},{10,... | collective-permute-start | bytes 884744 | tf_op jit(solution)/shard_map/ppermute | solution.py:385
  52.0 8.6 %collective-permute-start.13 = (bf16[128,1152]{1,0:T(8,128)(2,1)}, bf16[128,1152]{1,0:T(8,128)(2,1)S(1)}, u32[]{:S(2)}, u32[]{:S(2)}) collective-permute-start(bf16[128,1152]{1,0:T(8,128)(2,1)} %copy-done.9), channel_id=1, source_target_pairs={{0,1},{1,0},{2,3},{3,2},{4,5},{5,4},{6,7},{7,6},{8,9},{9,8},{10,11... | collective-permute-start | bytes 884744 | tf_op jit(solution)/shard_map/ppermute | solution.py:382
  54.6 7.0 %collective-permute-start.12 = (bf16[64,896]{1,0:T(8,128)(2,1)S(1)}, bf16[64,896]{1,0:T(8,128)(2,1)S(1)}, u32[]{:S(2)}, u32[]{:S(2)}) collective-permute-start(bf16[64,896]{1,0:T(8,128)(2,1)S(1)} %get-tuple-element.129), channel_id=1, source_target_pairs={{0,4},{4,0},{8,12},{12,8},{16,20},{20,16},{24,28},{28,24},{1,5},{5... | collective-permute-start | bytes 344072 | tf_op jit(solution)/shard_map/ppermute | solution.py:388
  56.8 6.4 %collective-permute-start.19 = (bf16[64,1024]{1,0:T(8,128)(2,1)S(1)}, bf16[64,1024]{1,0:T(8,128)(2,1)S(1)}, u32[]{:S(2)}, u32[]{:S(2)}) collective-permute-start(bf16[64,1024]{1,0:T(8,128)(2,1)S(1)} %fusion.7), channel_id=1, source_target_pairs={{0,8},{4,12},{8,0},{12,4},{16,24},{20,28},{24,16},{28,20},{1,9},{5... | collective-permute-start | bytes 393224 | tf_op jit(solution)/shard_map/ppermute | solution.py:459
  60.7 29.8 %copy-start.1 = (f32[128,3072]{1,0:T(8,128)S(1)}, f32[128,3072]{1,0:T(8,128)}, u32[]{:S(2)}) copy-start(f32[128,3072]{1,0:T(8,128)} %x_start.3) | copy-start | bytes 4718596
  60.8 5.2 %collective-permute-start.18 = (bf16[64,1152]{1,0:T(8,128)(2,1)S(1)}, bf16[64,1152]{1,0:T(8,128)(2,1)S(1)}, u32[]{:S(2)}, u32[]{:S(2)}) collective-permute-start(bf16[64,1152]{1,0:T(8,128)(2,1)S(1)} %get-tuple-element.137), channel_id=1, source_target_pairs={{0,4},{4,0},{8,12},{12,8},{16,20},{20,16},{24,28},{28,24},{1,5},{5... | collective-permute-start | bytes 442376 | tf_op jit(solution)/shard_map/ppermute | solution.py:388
  61.6 6.1 %collective-permute-start.17 = (bf16[64,896]{1,0:T(8,128)(2,1)S(1)}, bf16[64,896]{1,0:T(8,128)(2,1)S(1)}, u32[]{:S(2)}, u32[]{:S(2)}) collective-permute-start(bf16[64,896]{1,0:T(8,128)(2,1)S(1)} %fusion.8), channel_id=1, source_target_pairs={{0,8},{4,12},{8,0},{12,4},{16,24},{20,28},{24,16},{28,20},{1,9},{5... | collective-permute-start | bytes 344072 | tf_op jit(solution)/shard_map/ppermute | solution.py:459
  63.3 12.7 %collective-permute-start.21 = (bf16[64,1024]{1,0:T(8,128)(2,1)S(1)}, bf16[64,1024]{1,0:T(8,128)(2,1)S(1)}, u32[]{:S(2)}, u32[]{:S(2)}) collective-permute-start(bf16[64,1024]{1,0:T(8,128)(2,1)S(1)} %fusion.2), channel_id=1, source_target_pairs={{0,16},{4,20},{8,24},{12,28},{16,0},{20,4},{24,8},{28,12},{1,17},{... | collective-permute-start | bytes 393224 | tf_op jit(solution)/shard_map/ppermute | solution.py:459
  66.0 8.1 %collective-permute-start.22 = (bf16[64,1152]{1,0:T(8,128)(2,1)S(1)}, bf16[64,1152]{1,0:T(8,128)(2,1)S(1)}, u32[]{:S(2)}, u32[]{:S(2)}) collective-permute-start(bf16[64,1152]{1,0:T(8,128)(2,1)S(1)} %fusion.6), channel_id=1, source_target_pairs={{0,8},{4,12},{8,0},{12,4},{16,24},{20,28},{24,16},{28,20},{1,9},{5... | collective-permute-start | bytes 442376 | tf_op jit(solution)/shard_map/ppermute | solution.py:459
  67.7 9.5 %collective-permute-start.20 = (bf16[64,896]{1,0:T(8,128)(2,1)S(1)}, bf16[64,896]{1,0:T(8,128)(2,1)S(1)}, u32[]{:S(2)}, u32[]{:S(2)}) collective-permute-start(bf16[64,896]{1,0:T(8,128)(2,1)S(1)} %fusion.5), channel_id=1, source_target_pairs={{0,16},{4,20},{8,24},{12,28},{16,0},{20,4},{24,8},{28,12},{1,17},{... | collective-permute-start | bytes 344072 | tf_op jit(solution)/shard_map/ppermute | solution.py:459
  74.2 8.6 %collective-permute-start.24 = (bf16[64,1152]{1,0:T(8,128)(2,1)S(1)}, bf16[64,1152]{1,0:T(8,128)(2,1)S(1)}, u32[]{:S(2)}, u32[]{:S(2)}) collective-permute-start(bf16[64,1152]{1,0:T(8,128)(2,1)S(1)} %fusion), channel_id=1, source_target_pairs={{0,16},{4,20},{8,24},{12,28},{16,0},{20,4},{24,8},{28,12},{1,17},{... | collective-permute-start | bytes 442376 | tf_op jit(solution)/shard_map/ppermute | solution.py:459
  76.0 5.0 %collective-permute-start.25 = (bf16[64,1024]{1,0:T(8,128)(2,1)S(1)}, bf16[64,1024]{1,0:T(8,128)(2,1)S(1)}, u32[]{:S(2)}, u32[]{:S(2)}) collective-permute-start(bf16[64,1024]{1,0:T(8,128)(2,1)S(1)} %get-tuple-element.157), channel_id=1, source_target_pairs={{0,4},{4,0},{8,12},{12,8},{16,20},{20,16},{24,28},{28,24},{1,5},{5... | collective-permute-start | bytes 393224 | tf_op jit(solution)/shard_map/ppermute | solution.py:388
  82.9 8.5 %collective-permute-start.26 = (bf16[64,1152]{1,0:T(8,128)(2,1)S(1)}, bf16[64,1152]{1,0:T(8,128)(2,1)S(1)}, u32[]{:S(2)}, u32[]{:S(2)}) collective-permute-start(bf16[64,1152]{1,0:T(8,128)(2,1)S(1)} %get-tuple-element.153), channel_id=1, source_target_pairs={{0,4},{4,0},{8,12},{12,8},{16,20},{20,16},{24,28},{28,24},{1,5},{5... | collective-permute-start | bytes 442376 | tf_op jit(solution)/shard_map/ppermute | solution.py:388
  84.0 6.5 %collective-permute-start.23 = (bf16[64,896]{1,0:T(8,128)(2,1)S(1)}, bf16[64,896]{1,0:T(8,128)(2,1)S(1)}, u32[]{:S(2)}, u32[]{:S(2)}) collective-permute-start(bf16[64,896]{1,0:T(8,128)(2,1)S(1)} %get-tuple-element.155), channel_id=1, source_target_pairs={{0,4},{4,0},{8,12},{12,8},{16,20},{20,16},{24,28},{28,24},{1,5},{5... | collective-permute-start | bytes 344072 | tf_op jit(solution)/shard_map/ppermute | solution.py:388

commit v16 on v14

--- a/solution.py
+++ b/solution.py
@@ -373,7 +373,7 @@
     groups = n_step // 2
     half = rows // 2
     unit = width // 24
-    counts = [n * unit for n in (9,8,7)]
+    counts = [n * unit for n in (7, 6, 6, 5)]
     chunks = len(counts)
     firsts = [sum(counts[:c]) for c in range(chunks)]
     qg, kg = q_gain[None, :], k_gain[None, :]
@@ -453,7 +453,9 @@
     to_chips(ready)
     for c in range(2, chunks):
         here = slice((c - 1) * others, c * others)
-        to_chips(joined(parts[here], sent[here]))
+        sent[here], ready = tied(sent[here], ready)
+        ready = joined(parts[here], sent[here])
+        to_chips(ready)
 
     def along(pairs):
         return lambda x: lax.ppermute(x, "step", [(2 * a + i, 2 * b + i) for a, b in pairs for i in (0, 1)])
@@ -491,8 +493,8 @@
         def finish(fetched):
             given = [held[name] for name in ("earlier", "kept", "fetched", "other")]
             stash.append((firsts[c], given + [fetched[0]]))
-            if len(stash) in (1, chunks):
-                mine = stash[len(stash) - 1 :] if len(stash) == 1 else stash[1:]
+            if len(stash) != chunks - 1:
+                mine = stash[-1:] if len(stash) < chunks else stash[-2:]
                 places = [place for place, _ in mine]
                 groups_in = [group for _, group in mine]
                 into = list(written)
@@ -510,7 +512,7 @@
     turns = []
     arrival = 2.0
     for c in range(chunks):
-        share = 16.0 * (10 - 2 * c) / 24
+        share = 16.0 * counts[c] / width
         arrival += share
         when = arrival
         for i in range(len(plan[c])):

time: 90 us -> 93.7 us (1.041)
  starting transfers between devices: 29.8 us -> 33.4 us
  Pallas kernels: 34.1 us -> 35.5 us
    ppermute x6 -> x8, starting transfers between devices: 8.84 us -> 13.2 us  [to_pair(): return lax.ppermute(x, 'step', [(i, i ^ 1) for i in range(n_step)])]
    ppermute x6 -> x8, starting transfers between devices: 12.6 us -> 9.14 us  [along(): lax.ppermute(x, 'step', [(2 * a + i, 2 * b + i) for a, b in pairs for i i...]
    ppermute x5 -> x6, starting transfers between devices: 7.1 us -> 8.61 us  [to_chip(): lax.ppermute(x, 'seq', [(i, (i + 2 * offset) % n_seq) for i in range(n_se...]
    ppermute x10 -> x12, starting transfers between devices: 1.32 us -> 2.45 us  [to_core(): return lax.ppermute(x, 'seq', [(i, i ^ 1) for i in range(n_seq)])]
    pallas_call x3 -> x4, Pallas kernels: 1.78 us -> 2.69 us  [join_call(): pl.pallas_call(join_kernel, in_specs=[vm, vm], out_specs=vm, out_shape=ja...]
    ppermute x6 -> x8, waiting for transfers between devices: 6.95 us -> 6.18 us  [along(): lax.ppermute(x, 'step', [(2 * a + i, 2 * b + i) for a, b in pairs for i i...]
    unnamed x30 -> x32, local copies, waits for them, and re-layouts: 4.1 us -> 3.44 us
    ppermute x6 -> x8, waiting for transfers between devices: 3.22 us -> 3.87 us  [to_pair(): return lax.ppermute(x, 'step', [(i, i ^ 1) for i in range(n_step)])]
  transfers between devices with their start and end apart: 27 -> 34, of which waited for: 11 -> 12; matrix products, arithmetic and copies ran while one was open for 0% -> 0% of each run, Pallas kernels for 24% -> 25%
where the time goes in v16:
time: 93.7 us; the launch traced here: 93.4 us
  Pallas kernels  35.5 us (38%)
  starting transfers between devices  33.4 us (36%)
  waiting for transfers between devices  19.5 us (21%)
  local copies, waits for them, and re-layouts  3.44 us (4%)
  between operations  1.17 us (1%)
    pallas_call x2, Pallas kernels, project_call(): pl.pallas_call(functools.partial(project_kernel, tile, load, tiles), in_s...  17.6 us
    ppermute x8, starting transfers between devices, to_pair(): return lax.ppermute(x, 'step', [(i, i ^ 1) for i in range(n_step)])  13.2 us
    ppermute x8, starting transfers between devices, along(): lax.ppermute(x, 'step', [(2 * a + i, 2 * b + i) for a, b in pairs for i i...  9.14 us
    ppermute x6, starting transfers between devices, to_chip(): lax.ppermute(x, 'seq', [(i, (i + 2 * offset) % n_seq) for i in range(n_se...  8.61 us
    ppermute x6, waiting for transfers between devices, to_chip(): lax.ppermute(x, 'seq', [(i, (i + 2 * offset) % n_seq) for i in range(n_se...  6.33 us
    ppermute x8, waiting for transfers between devices, along(): lax.ppermute(x, 'step', [(2 * a + i, 2 * b + i) for a, b in pairs for i i...  6.18 us
    pallas_call x2, Pallas kernels, out_call(): pl.pallas_call(functools.partial(out_kernel, plan), in_specs=[vm] * len(g...  5.11 us
    ppermute x8, waiting for transfers between devices, to_pair(): return lax.ppermute(x, 'step', [(i, i ^ 1) for i in range(n_step)])  3.87 us
  transfers between devices with their start and end apart: 34, of which 12 were waited for; matrix products, arithmetic and copies ran while one was open for 0% of the time, Pallas kernels for 25%

profile of v16, /device:TPU:0, one launch (start us, length us, event | category | flops | bytes accessed | tf_op | source)
XLA Modules:
  0.0 93.4 jit_solution(17572618720045959670)
XLA Ops:
  0.7 3.6 %norm.1 = (bf16[64,3072]{1,0:T(8,128)(2,1)}, bf16[64,3072]{1,0:T(8,128)(2,1)}, f32[1,3072]{1,0:T(1,128)}) custom-call(s32[1]{0:T(128)S(6)} %copy.16.t_ref, f32[50]{0:T(128)} %size_ref.1, f32[1,128,3072]{2,1,0:T(8,128)} %x_hbm.1, f32[50,9216]{1,0:T(8,128)} %mod_hbm.1), custom_call_target="tpu_custom_call" | custom-call | flops 3932160 | tf_op jit(solution)/shard_map/norm/pallas_call | solution.py:61
  4.3 0.5 collective-permute-start.1
  4.8 0.1 collective-permute-start.2
  4.9 2.9 %collective-permute-start = (bf16[64,3072]{1,0:T(8,128)(2,1)}, bf16[64,3072]{1,0:T(8,128)(2,1)S(1)}, u32[]{:S(2)}, u32[]{:S(2)}) collective-permute-start(bf16[64,3072]{1,0:T(8,128)(2,1)} %get-tuple-element.92.m0), channel_id=1, source_target_pairs={{0,2},{1,3},{2,0},{3,1},{4,6},{5,7},{6,4},{7,5},{8,10},{9,11},{10,... | collective-permute-start | bytes 1179656 | tf_op jit(solution)/shard_map/ppermute | solution.py:385
  7.9 1.0 %copy-done.2 = bf16[64,3072]{1,0:T(8,128)(2,1)S(1)} copy-done((bf16[64,3072]{1,0:T(8,128)(2,1)S(1)}, bf16[64,3072]{1,0:T(8,128)(2,1)}, u32[]{:S(2)}) %copy-start.2) | copy-done | bytes 393240
  8.9 1.0 %copy-done.3 = bf16[64,3072]{1,0:T(8,128)(2,1)S(1)} copy-done((bf16[64,3072]{1,0:T(8,128)(2,1)S(1)}, bf16[64,3072]{1,0:T(8,128)(2,1)}, u32[]{:S(2)}) %copy-start.3) | copy-done | bytes 393240
  9.9 12.4 %project.2 = (bf16[256,512]{1,0:T(8,128)(2,1)S(1)}, bf16[256,512]{1,0:T(8,128)(2,1)S(1)}, bf16[256,512]{1,0:T(8,128)(2,1)S(1)}, bf16[256,1536]{1,0:T(8,128)(2,1)...) custom-call(bf16[64,3072]{1,0:T(8,128)(2,1)S(1)} %copy-done.3, ...), custom_call_target="tpu_custom_call" | custom-call | flops 4831838208 | tf_op jit(solution)/shard_map/project/pallas_call | solution.py:158
  22.3 0.7 copy-done.7
  23.0 0.7 copy-done.9
  23.7 2.1 %collective-permute-done.3.m1 = bf16[64,3072]{1,0:T(8,128)(2,1)S(1)} collective-permute-done((bf16[64,3072]{1,0:T(8,128)(2,1)}, bf16[64,3072]{1,0:T(8,128)(2,1)S(1)}, u32[]{:S(2)}, u32[]{:S(2)}) %collective-permute-start.3) | collective-permute-done | bytes 393248 | tf_op jit(solution)/shard_map/ppermute | solution.py:385
  25.8 1.7 %collective-permute-done.5.m3 = bf16[64,3072]{1,0:T(8,128)(2,1)S(1)} collective-permute-done((bf16[64,3072]{1,0:T(8,128)(2,1)S(1)}, bf16[64,3072]{1,0:T(8,128)(2,1)S(1)}, u32[]{:S(2)}, u32[]{:S(2)}) %collective-permute-start.5) | collective-permute-done | bytes 393248 | tf_op jit(solution)/shard_map/ppermute | solution.py:382
  27.6 5.2 %project.3 = (bf16[256,512]{1,0:T(8,128)(2,1)S(1)}, bf16[256,512]{1,0:T(8,128)(2,1)S(1)}, bf16[256,512]{1,0:T(8,128)(2,1)S(1)}, bf16[256,1536]{1,0:T(8,128)(2,1)S(1)}) custom-call(bf16[64,3072]{1,0:T(8,128)(2,1)S(1)} %collective-permute-done.m0, bf16[64,3072]{1,0:T(8,128)(2,1)S(1)} %collective-permute-done.3.m1, ...), custom_call_target="tpu_custom_call" | custom-call | flops 4831838208 | tf_op jit(solution)/shard_map/project/pallas_call | solution.py:158
  32.8 1.1 %attend.2.refs_0_.refs_4_.refs_8_ = bf16[256,512]{1,0:T(8,128)(2,1)S(1)} custom-call(bf16[256,512]{1,0:T(8,128)(2,1)S(1)} %get-tuple-element.104.refs_0_, bf16[256,512]{1,0:T(8,128)(2,1)S(1)} %copy-done.8, bf16[256,512]{1,0:T(8,128)(2,1)S(1)} %get-tuple-element.106.refs_2_, bf16[256,512]{1,0:T(8,128)(2,1)S(1)} %copy-done.10, ...), custom_call_target="tpu_custom_call" | custom-call | flops 805306368 | tf_op jit(solution)/shard_map/attend/pallas_call | solution.py:202
  34.0 1.3 %project_out.2 = (f32[128,896]{1,0:T(8,128)S(1)}, bf16[128,896]{1,0:T(8,128)(2,1)S(1)}) custom-call(bf16[256,512]{1,0:T(8,128)(2,1)S(1)} %attend.2.refs_0_.refs_4_.refs_8_, bf16[256,1536]{1,0:T(8,128)(2,1)S(1)} %get-tuple-element.119.refs_1_.refs_5_.refs_9_, bf16[512,3072]{1,0:T(8,128)(2,1)S(1)} %copy-done, bf16[1536,3072]{1,0:T(8,128)(2,1)S(1)} %bitcast.4), custom_call_target="tpu_custom_call" | custom-call | flops 939524096 | tf_op jit(solution)/shard_map/project_out/pallas_call | solution.py:246
  35.2 0.2 collective-permute-start.6
  35.4 0.9 attend.3.refs_12_.refs_16_.refs_20_.refs_24_
  36.3 0.5 collective-permute-done.6.sent
  36.8 1.8 %collective-permute-start.7 = (bf16[128,896]{1,0:T(8,128)(2,1)S(1)}, bf16[128,896]{1,0:T(8,128)(2,1)S(1)}, u32[]{:S(2)}, u32[]{:S(2)}) collective-permute-start(bf16[128,896]{1,0:T(8,128)(2,1)S(1)} %join.4), channel_id=1, source_target_pairs={{0,2},{1,3},{2,0},{3,1},{4,6},{5,7},{6,4},{7,5},{8,10},{9,11},{10,... | collective-permute-start | bytes 688136 | tf_op jit(solution)/shard_map/ppermute | solution.py:385
  38.6 3.9 %project_out.3 = (f32[128,768]{1,0:T(8,128)S(1)}, bf16[128,768]{1,0:T(8,128)(2,1)S(1)}, f32[128,768]{1,0:T(8,128)S(1)}, bf16[128,768]{1,0:T(8,128)(2,1)}, f32[12...) custom-call(bf16[256,512]{1,0:T(8,128)(2,1)S(1)} %attend.2.refs_0_.r, ...), custom_call_target="tpu_custom_call" | custom-call | flops 3087007744 | tf_op jit(solution)/shard_map/project_out/pallas_call | solution.py:246
  42.5 0.5 collective-permute-start.12
  43.0 0.1 collective-permute-start.10
  43.1 0.9 collective-permute-done.8.sent
  43.9 0.6 collective-permute-done.7.refs_0_
  44.5 0.7 join.5
  45.3 1.7 %collective-permute-start.15 = (bf16[128,768]{1,0:T(8,128)(2,1)}, bf16[128,768]{1,0:T(8,128)(2,1)S(1)}, u32[]{:S(2)}, u32[]{:S(2)}) collective-permute-start(bf16[128,768]{1,0:T(8,128)(2,1)} %join.5), channel_id=1, source_target_pairs={{0,2},{1,3},{2,0},{3,1},{4,6},{5,7},{6,4},{7,5},{8,10},{9,11},{10,... | collective-permute-start | bytes 589832 | tf_op jit(solution)/shard_map/ppermute | solution.py:385
  47.0 0.5 collective-permute-start.18
  47.5 0.7 drift.4
  48.2 1.5 %collective-permute-start.13 = (bf16[64,896]{1,0:T(8,128)(2,1)}, bf16[64,896]{1,0:T(8,128)(2,1)S(1)}, u32[]{:S(2)}, u32[]{:S(2)}) collective-permute-start(bf16[64,896]{1,0:T(8,128)(2,1)} %get-tuple-element.145), channel_id=1, source_target_pairs={{0,4},{4,0},{8,12},{12,8},{16,20},{20,16},{24,28},{28,24},{1,5},{5... | collective-permute-start | bytes 344072 | tf_op jit(solution)/shard_map/ppermute | solution.py:388
  49.7 1.0 %join.6 = bf16[128,768]{1,0:T(8,128)(2,1)S(1)} custom-call(f32[128,768]{1,0:T(8,128)S(1)} %get-tuple-element.137.keep, bf16[128,768]{1,0:T(8,128)(2,1)} %collective-permute-done.10.sent), custom_call_target="tpu_custom_call" | custom-call | tf_op jit(solution)/shard_map/join/pallas_call | solution.py:264
  50.7 0.6 collective-permute-start.17
  51.3 1.0 %join.7 = bf16[128,640]{1,0:T(8,128)(2,1)S(1)} custom-call(f32[128,640]{1,0:T(8,128)S(1)} %get-tuple-element.156.keep, bf16[128,640]{1,0:T(8,128)(2,1)} %collective-permute-done.18.sent), custom_call_target="tpu_custom_call" | custom-call | tf_op jit(solution)/shard_map/join/pallas_call | solution.py:264
  52.2 1.1 %collective-permute-start.11 = (bf16[128,768]{1,0:T(8,128)(2,1)S(1)}, bf16[128,768]{1,0:T(8,128)(2,1)S(1)}, u32[]{:S(2)}, u32[]{:S(2)}) collective-permute-start(bf16[128,768]{1,0:T(8,128)(2,1)S(1)} %join.6), channel_id=1, source_target_pairs={{0,2},{1,3},{2,0},{3,1},{4,6},{5,7},{6,4},{7,5},{8,10},{9,11},{10,... | collective-permute-start | bytes 589832 | tf_op jit(solution)/shard_map/ppermute | solution.py:385
  53.3 1.0 %collective-permute-start.19 = (bf16[128,640]{1,0:T(8,128)(2,1)S(1)}, bf16[128,640]{1,0:T(8,128)(2,1)S(1)}, u32[]{:S(2)}, u32[]{:S(2)}) collective-permute-start(bf16[128,640]{1,0:T(8,128)(2,1)S(1)} %join.7), channel_id=1, source_target_pairs={{0,2},{1,3},{2,0},{3,1},{4,6},{5,7},{6,4},{7,5},{8,10},{9,11},{10,... | collective-permute-start | bytes 491528 | tf_op jit(solution)/shard_map/ppermute | solution.py:385
  54.3 1.0 %drift.5 = (f32[64,768]{1,0:T(8,128)S(1)}, f32[64,768]{1,0:T(8,128)S(1)}, bf16[64,768]{1,0:T(8,128)(2,1)S(1)}) custom-call(s32[1]{0:T(128)} %bitcast.parity, f32[128,768]{1,0:T(8,128)S(1)} %get-tuple-element.146.keep, bf16[128,768]{1,0:T(8,128)(2,1)} %collective-permute-done.14.sent, f32[1,3072]{1,0:T(1,128)S(1)} %copy-done.4, ...), custom_call_target="tpu_custom_call" | custom-call | tf_op jit(solution)/shard_map/drift/pallas_call | solution.py:297
  55.4 1.1 %collective-permute-start.21 = (bf16[64,768]{1,0:T(8,128)(2,1)S(1)}, bf16[64,768]{1,0:T(8,128)(2,1)S(1)}, u32[]{:S(2)}, u32[]{:S(2)}) collective-permute-start(bf16[64,768]{1,0:T(8,128)(2,1)S(1)} %get-tuple-element.149), channel_id=1, source_target_pairs={{0,4},{4,0},{8,12},{12,8},{16,20},{20,16},{24,28},{28,24},{1,5},{5... | collective-permute-start | bytes 294920 | tf_op jit(solution)/shard_map/ppermute | solution.py:388
  56.5 3.6 %collective-permute-done.11.refs_0_ = bf16[128,768]{1,0:T(8,128)(2,1)S(1)} collective-permute-done((bf16[128,768]{1,0:T(8,128)(2,1)S(1)}, bf16[128,768]{1,0:T(8,128)(2,1)S(1)}, u32[]{:S(2)}, u32[]{:S(2)}) %collective-permute-start.11) | collective-permute-done | bytes 196640 | tf_op jit(solution)/shard_map/ppermute | solution.py:385
  60.1 1.6 %collective-permute-start.20 = (bf16[64,896]{1,0:T(8,128)(2,1)S(1)}, bf16[64,896]{1,0:T(8,128)(2,1)S(1)}, u32[]{:S(2)}, u32[]{:S(2)}) collective-permute-start(bf16[64,896]{1,0:T(8,128)(2,1)S(1)} %fusion.8), channel_id=1, source_target_pairs={{0,8},{4,12},{8,0},{12,4},{16,24},{20,28},{24,16},{28,20},{1,9},{5... | collective-permute-start | bytes 344072 | tf_op jit(solution)/shard_map/ppermute | solution.py:461
  61.7 0.1 drift.6
  61.7 1.1 %collective-permute-start.16 = (bf16[64,768]{1,0:T(8,128)(2,1)S(1)}, bf16[64,768]{1,0:T(8,128)(2,1)S(1)}, u32[]{:S(2)}, u32[]{:S(2)}) collective-permute-start(bf16[64,768]{1,0:T(8,128)(2,1)S(1)} %get-tuple-element.153), channel_id=1, source_target_pairs={{0,4},{4,0},{8,12},{12,8},{16,20},{20,16},{24,28},{28,24},{1,5},{5... | collective-permute-start | bytes 294920 | tf_op jit(solution)/shard_map/ppermute | solution.py:388
  62.9 0.5 collective-permute-start.25
  63.4 1.4 %collective-permute-done.20 = bf16[64,896]{1,0:T(8,128)(2,1)S(1)} collective-permute-done((bf16[64,896]{1,0:T(8,128)(2,1)S(1)}, bf16[64,896]{1,0:T(8,128)(2,1)S(1)}, u32[]{:S(2)}, u32[]{:S(2)}) %collective-permute-start.20) | collective-permute-done | bytes 114720 | tf_op jit(solution)/shard_map/ppermute | solution.py:461
  64.9 2.7 %collective-permute-start.23 = (bf16[64,896]{1,0:T(8,128)(2,1)S(1)}, bf16[64,896]{1,0:T(8,128)(2,1)S(1)}, u32[]{:S(2)}, u32[]{:S(2)}) collective-permute-start(bf16[64,896]{1,0:T(8,128)(2,1)S(1)} %fusion), channel_id=1, source_target_pairs={{0,16},{4,20},{8,24},{12,28},{16,0},{20,4},{24,8},{28,12},{1,17},{... | collective-permute-start | bytes 344072 | tf_op jit(solution)/shard_map/ppermute | solution.py:461
  67.6 0.1 drift.7
  67.7 2.3 %collective-permute-start.24 = (bf16[64,640]{1,0:T(8,128)(2,1)S(1)}, bf16[64,640]{1,0:T(8,128)(2,1)S(1)}, u32[]{:S(2)}, u32[]{:S(2)}) collective-permute-start(bf16[64,640]{1,0:T(8,128)(2,1)S(1)} %get-tuple-element.163), channel_id=1, source_target_pairs={{0,4},{4,0},{8,12},{12,8},{16,20},{20,16},{24,28},{28,24},{1,5},{5... | collective-permute-start | bytes 245768 | tf_op jit(solution)/shard_map/ppermute | solution.py:388
  70.0 0.5 collective-permute-start.22
  70.5 0.9 collective-permute-start.29
  71.4 1.2 %collective-permute-done.24.refs_7_ = bf16[64,640]{1,0:T(8,128)(2,1)S(1)} collective-permute-done((bf16[64,640]{1,0:T(8,128)(2,1)S(1)}, bf16[64,640]{1,0:T(8,128)(2,1)S(1)}, u32[]{:S(2)}, u32[]{:S(2)}) %collective-permute-start.24) | collective-permute-done | bytes 81952 | tf_op jit(solution)/shard_map/ppermute | solution.py:388
  72.6 2.0 %collective-permute-start.28 = (bf16[64,640]{1,0:T(8,128)(2,1)S(1)}, bf16[64,640]{1,0:T(8,128)(2,1)S(1)}, u32[]{:S(2)}, u32[]{:S(2)}) collective-permute-start(bf16[64,640]{1,0:T(8,128)(2,1)S(1)} %fusion.11), channel_id=1, source_target_pairs={{0,8},{4,12},{8,0},{12,4},{16,24},{20,28},{24,16},{28,20},{1,9},{5... | collective-permute-start | bytes 245768 | tf_op jit(solution)/shard_map/ppermute | solution.py:461
  74.6 0.1 add_convert_fusion
  74.7 4.9 %collective-permute-start.33 = (bf16[64,896]{1,0:T(8,128)(2,1)S(1)}, bf16[64,896]{1,0:T(8,128)(2,1)S(1)}, u32[]{:S(2)}, u32[]{:S(2)}) collective-permute-start(bf16[64,896]{1,0:T(8,128)(2,1)S(1)} %get-tuple-element.185), channel_id=1, source_target_pairs={{0,4},{4,0},{8,12},{12,8},{16,20},{20,16},{24,28},{28,24},{1,5},{5... | collective-permute-start | bytes 344072 | tf_op jit(solution)/shard_map/ppermute | solution.py:388
  79.6 0.1 collective-permute-start.26
  79.7 0.1 add_convert_fusion.1
  79.8 2.1 %collective-permute-start.32 = (bf16[64,768]{1,0:T(8,128)(2,1)S(1)}, bf16[64,768]{1,0:T(8,128)(2,1)S(1)}, u32[]{:S(2)}, u32[]{:S(2)}) collective-permute-start(bf16[64,768]{1,0:T(8,128)(2,1)S(1)} %get-tuple-element.181), channel_id=1, source_target_pairs={{0,4},{4,0},{8,12},{12,8},{16,20},{20,16},{24,28},{28,24},{1,5},{5... | collective-permute-start | bytes 294920 | tf_op jit(solution)/shard_map/ppermute | solution.py:388
  81.9 0.9 %collective-permute-start.30 = (bf16[64,640]{1,0:T(8,128)(2,1)S(1)}, bf16[64,640]{1,0:T(8,128)(2,1)S(1)}, u32[]{:S(2)}, u32[]{:S(2)}) collective-permute-start(bf16[64,640]{1,0:T(8,128)(2,1)S(1)} %fusion.7), channel_id=1, source_target_pairs={{0,16},{4,20},{8,24},{12,28},{16,0},{20,4},{24,8},{28,12},{1,17},{... | collective-permute-start | bytes 245768 | tf_op jit(solution)/shard_map/ppermute | solution.py:461
  82.9 2.3 %collective-permute-done.26 = bf16[64,768]{1,0:T(8,128)(2,1)S(1)} collective-permute-done((bf16[64,768]{1,0:T(8,128)(2,1)S(1)}, bf16[64,768]{1,0:T(8,128)(2,1)S(1)}, u32[]{:S(2)}, u32[]{:S(2)}) %collective-permute-start.26) | collective-permute-done | bytes 98336 | tf_op jit(solution)/shard_map/ppermute | solution.py:461
  85.2 0.1 add_convert_fusion.2
  85.3 0.1 collective-permute-start.27
  85.4 2.4 %collective-permute-done.30 = bf16[64,640]{1,0:T(8,128)(2,1)S(1)} collective-permute-done((bf16[64,640]{1,0:T(8,128)(2,1)S(1)}, bf16[64,640]{1,0:T(8,128)(2,1)S(1)}, u32[]{:S(2)}, u32[]{:S(2)}) %collective-permute-start.30) | collective-permute-done | bytes 81952 | tf_op jit(solution)/shard_map/ppermute | solution.py:461
  87.8 0.1 collective-permute-start.31
  87.9 0.9 finish.3.refs_5_
  88.8 0.8 finish.4.refs_10_
  89.6 0.3 collective-permute-done.27.refs_4_
  90.0 2.4 %collective-permute-done.31.refs_9_ = bf16[64,640]{1,0:T(8,128)(2,1)S(1)} collective-permute-done((bf16[64,640]{1,0:T(8,128)(2,1)S(1)}, bf16[64,640]{1,0:T(8,128)(2,1)S(1)}, u32[]{:S(2)}, u32[]{:S(2)}) %collective-permute-start.31) | collective-permute-done | bytes 81952 | tf_op jit(solution)/shard_map/ppermute | solution.py:388
  92.3 0.9 %finish.5 = f32[1,128,3072]{2,1,0:T(8,128)} custom-call(s32[1]{0:T(128)} %bitcast.parity, f32[128,3072]{1,0:T(8,128)S(1)} %copy-done.1, f32[64,768]{1,0:T(8,128)S(1)} %get-tuple-element.184.refs_0_, f32[64,768]{1,0:T(8,128)S(1)} %get-tuple-element.152.refs_1_, bf16[64,768]{1,0:T(8,128)(2,1)S(1)} %collective-permute-done.16.refs_2_, ...), custom_call_target="tpu_custom_call", output_to_operand_aliasing={{}: (12, {})} | custom-call | tf_op jit(solution)/shard_map/finish/pallas_call | solution.py:342
  (67 shorter events, 0.5 us)
Async XLA Ops:
  0.0 7.9 %copy-start.5 = (f32[128]{0:T(128)S(1)}, f32[128]{0:T(128)}, u32[]{:S(2)}) copy-start(f32[128]{0:T(128)} %param.16) | copy-start | bytes 1540
  0.0 7.9 %copy-start.6 = (f32[128]{0:T(128)S(1)}, f32[128]{0:T(128)}, u32[]{:S(2)}) copy-start(f32[128]{0:T(128)} %param.17) | copy-start | bytes 1540
  4.3 3.6 %collective-permute-start.1 = (bf16[64,3072]{1,0:T(8,128)(2,1)}, bf16[64,3072]{1,0:T(8,128)(2,1)S(1)}, u32[]{:S(2)}, u32[]{:S(2)}) collective-permute-start(bf16[64,3072]{1,0:T(8,128)(2,1)} %get-tuple-element.92.m0), channel_id=1, source_target_pairs={{0,1},{1,0},{2,3},{3,2},{4,5},{5,4},{6,7},{7,6},{8,9},{9,8},{10,11... | collective-permute-start | bytes 1179656 | tf_op jit(solution)/shard_map/ppermute | solution.py:382
  4.8 3.1 %collective-permute-start.2 = (bf16[64,3072]{1,0:T(8,128)(2,1)}, bf16[64,3072]{1,0:T(8,128)(2,1)S(1)}, u32[]{:S(2)}, u32[]{:S(2)}) collective-permute-start(bf16[64,3072]{1,0:T(8,128)(2,1)} %get-tuple-element.93.m1), channel_id=1, source_target_pairs={{0,1},{1,0},{2,3},{3,2},{4,5},{5,4},{6,7},{7,6},{8,9},{9,8},{10,11... | collective-permute-start | bytes 1179656 | tf_op jit(solution)/shard_map/ppermute | solution.py:382
  4.9 18.8 %collective-permute-start = (bf16[64,3072]{1,0:T(8,128)(2,1)}, bf16[64,3072]{1,0:T(8,128)(2,1)S(1)}, u32[]{:S(2)}, u32[]{:S(2)}) collective-permute-start(bf16[64,3072]{1,0:T(8,128)(2,1)} %get-tuple-element.92.m0), channel_id=1, source_target_pairs={{0,2},{1,3},{2,0},{3,1},{4,6},{5,7},{6,4},{7,5},{8,10},{9,11},{10,... | collective-permute-start | bytes 1179656 | tf_op jit(solution)/shard_map/ppermute | solution.py:385
  7.8 18.0 %collective-permute-start.3 = (bf16[64,3072]{1,0:T(8,128)(2,1)}, bf16[64,3072]{1,0:T(8,128)(2,1)S(1)}, u32[]{:S(2)}, u32[]{:S(2)}) collective-permute-start(bf16[64,3072]{1,0:T(8,128)(2,1)} %get-tuple-element.93.m1), channel_id=1, source_target_pairs={{0,2},{1,3},{2,0},{3,1},{4,6},{5,7},{6,4},{7,5},{8,10},{9,11},{10,... | collective-permute-start | bytes 1179656 | tf_op jit(solution)/shard_map/ppermute | solution.py:385
  7.9 1.0 %copy-start.2 = (bf16[64,3072]{1,0:T(8,128)(2,1)S(1)}, bf16[64,3072]{1,0:T(8,128)(2,1)}, u32[]{:S(2)}) copy-start(bf16[64,3072]{1,0:T(8,128)(2,1)} %get-tuple-element.93.m1) | copy-start | bytes 1179652
  8.9 1.0 %copy-start.3 = (bf16[64,3072]{1,0:T(8,128)(2,1)S(1)}, bf16[64,3072]{1,0:T(8,128)(2,1)}, u32[]{:S(2)}) copy-start(bf16[64,3072]{1,0:T(8,128)(2,1)} %get-tuple-element.92.m0) | copy-start | bytes 1179652
  22.3 0.7 copy-start.7
  23.0 0.7 copy-start.9
  23.7 2.1 %collective-permute-start.4 = (bf16[64,3072]{1,0:T(8,128)(2,1)S(1)}, bf16[64,3072]{1,0:T(8,128)(2,1)S(1)}, u32[]{:S(2)}, u32[]{:S(2)}) collective-permute-start(bf16[64,3072]{1,0:T(8,128)(2,1)S(1)} %collective-permute-done.m0), channel_id=1, source_target_pairs={{0,1},{1,0},{2,3},{3,2},{4,5},{5,4},{6,7},{7,6},{8,9},{9,8},{10,11... | collective-permute-start | bytes 1179656 | tf_op jit(solution)/shard_map/ppermute | solution.py:382
  25.8 1.7 %collective-permute-start.5 = (bf16[64,3072]{1,0:T(8,128)(2,1)S(1)}, bf16[64,3072]{1,0:T(8,128)(2,1)S(1)}, u32[]{:S(2)}, u32[]{:S(2)}) collective-permute-start(bf16[64,3072]{1,0:T(8,128)(2,1)S(1)} %collective-permute-done.3.m1), channel_id=1, source_target_pairs={{0,1},{1,0},{2,3},{3,2},{4,5},{5,4},{6,7},{7,6},{8,9},{9,8},{10,11... | collective-permute-start | bytes 1179656 | tf_op jit(solution)/shard_map/ppermute | solution.py:382
  27.5 6.4 %slice-start = ((s8[9437184]{0:T(1024)(128)(4,1)}), s8[4194304]{0:T(1024)(128)(4,1)S(1)}, s32[]{:S(2)}) async-start(s8[9437184]{0:T(1024)(128)(4,1)} %bitcast.3), calls=%async_computation | async-start | bytes 8388608
  27.5 5.3 %copy-start.8 = (bf16[256,512]{1,0:T(8,128)(2,1)S(1)}, bf16[256,512]{1,0:T(8,128)(2,1)}, u32[]{:S(2)}) copy-start(bf16[256,512]{1,0:T(8,128)(2,1)} %copy-done.7) | copy-start | bytes 786436
  27.5 5.3 %copy-start.10 = (bf16[256,512]{1,0:T(8,128)(2,1)S(1)}, bf16[256,512]{1,0:T(8,128)(2,1)}, u32[]{:S(2)}) copy-start(bf16[256,512]{1,0:T(8,128)(2,1)} %copy-done.9) | copy-start | bytes 786436
  27.5 6.4 %slice-start.1 = ((s8[9437184]{0:T(1024)(128)(4,1)}), s8[4194304]{0:T(1024)(128)(4,1)S(1)}, s32[]{:S(2)}) async-start(s8[9437184]{0:T(1024)(128)(4,1)} %bitcast.3), calls=%async_computation.1 | async-start | bytes 8388608
  27.5 6.4 %slice-start.2 = ((s8[9437184]{0:T(1024)(128)(4,1)}), s8[1048576]{0:T(1024)(128)(4,1)S(1)}, s32[]{:S(2)}) async-start(s8[9437184]{0:T(1024)(128)(4,1)} %bitcast.3), calls=%async_computation.2 | async-start | bytes 2097152
  27.6 6.4 %copy-start = (bf16[512,3072]{1,0:T(8,128)(2,1)S(1)}, bf16[512,3072]{1,0:T(8,128)(2,1)}, u32[]{:S(2)}) copy-start(bf16[512,3072]{1,0:T(8,128)(2,1)} %refs_25_.1) | copy-start | bytes 9437188
  35.2 1.6 %collective-permute-start.6 = (bf16[128,896]{1,0:T(8,128)(2,1)S(1)}, bf16[128,896]{1,0:T(8,128)(2,1)S(1)}, u32[]{:S(2)}, u32[]{:S(2)}) collective-permute-start(bf16[128,896]{1,0:T(8,128)(2,1)S(1)} %get-tuple-element.112), channel_id=1, source_target_pairs={{0,1},{1,0},{2,3},{3,2},{4,5},{5,4},{6,7},{7,6},{8,9},{9,8},{10,11... | collective-permute-start | bytes 688136 | tf_op jit(solution)/shard_map/ppermute | solution.py:382
  36.8 7.7 %collective-permute-start.7 = (bf16[128,896]{1,0:T(8,128)(2,1)S(1)}, bf16[128,896]{1,0:T(8,128)(2,1)S(1)}, u32[]{:S(2)}, u32[]{:S(2)}) collective-permute-start(bf16[128,896]{1,0:T(8,128)(2,1)S(1)} %join.4), channel_id=1, source_target_pairs={{0,2},{1,3},{2,0},{3,1},{4,6},{5,7},{6,4},{7,5},{8,10},{9,11},{10,... | collective-permute-start | bytes 688136 | tf_op jit(solution)/shard_map/ppermute | solution.py:385
  38.6 8.9 %copy-start.4 = (f32[1,3072]{1,0:T(1,128)S(1)}, f32[1,3072]{1,0:T(1,128)}, u32[]{:S(2)}) copy-start(f32[1,3072]{1,0:T(1,128)} %get-tuple-element.136.sg) | copy-start | bytes 36868
  42.5 2.8 %copy-start.11 = (bf16[128,768]{1,0:T(8,128)(2,1)}, bf16[128,768]{1,0:T(8,128)(2,1)S(1)}, u32[]{:S(2)}) copy-start(bf16[128,768]{1,0:T(8,128)(2,1)S(1)} %get-tuple-element.135) | copy-start | bytes 589828
  42.5 4.5 %copy-start.12 = (bf16[128,640]{1,0:T(8,128)(2,1)}, bf16[128,640]{1,0:T(8,128)(2,1)S(1)}, u32[]{:S(2)}) copy-start(bf16[128,640]{1,0:T(8,128)(2,1)S(1)} %get-tuple-element.155) | copy-start | bytes 491524
  42.5 1.4 %collective-permute-start.8 = (bf16[128,768]{1,0:T(8,128)(2,1)S(1)}, bf16[128,768]{1,0:T(8,128)(2,1)S(1)}, u32[]{:S(2)}, u32[]{:S(2)}) collective-permute-start(bf16[128,768]{1,0:T(8,128)(2,1)S(1)} %get-tuple-element.127), channel_id=1, source_target_pairs={{0,1},{1,0},{2,3},{3,2},{4,5},{5,4},{6,7},{7,6},{8,9},{9,8},{10,11... | collective-permute-start | bytes 589832 | tf_op jit(solution)/shard_map/ppermute | solution.py:382
  42.5 5.0 %collective-permute-start.12 = (bf16[128,896]{1,0:T(8,128)(2,1)S(1)}, bf16[128,896]{1,0:T(8,128)(2,1)S(1)}, u32[]{:S(2)}, u32[]{:S(2)}) collective-permute-start(bf16[128,896]{1,0:T(8,128)(2,1)S(1)} %get-tuple-element.142), channel_id=1, source_target_pairs={{0,1},{1,0},{2,3},{3,2},{4,5},{5,4},{6,7},{7,6},{8,9},{9,8},{10,11... | collective-permute-start | bytes 688136 | tf_op jit(solution)/shard_map/ppermute | solution.py:382
  43.0 6.7 %collective-permute-start.10 = (bf16[128,768]{1,0:T(8,128)(2,1)}, bf16[128,768]{1,0:T(8,128)(2,1)}, u32[]{:S(2)}, u32[]{:S(2)}) collective-permute-start(bf16[128,768]{1,0:T(8,128)(2,1)} %get-tuple-element.138), channel_id=1, source_target_pairs={{0,1},{1,0},{2,3},{3,2},{4,5},{5,4},{6,7},{7,6},{8,9},{9,8},{10,11... | collective-permute-start | bytes 589832 | tf_op jit(solution)/shard_map/ppermute | solution.py:382
  45.3 7.0 %collective-permute-start.15 = (bf16[128,768]{1,0:T(8,128)(2,1)}, bf16[128,768]{1,0:T(8,128)(2,1)S(1)}, u32[]{:S(2)}, u32[]{:S(2)}) collective-permute-start(bf16[128,768]{1,0:T(8,128)(2,1)} %join.5), channel_id=1, source_target_pairs={{0,2},{1,3},{2,0},{3,1},{4,6},{5,7},{6,4},{7,5},{8,10},{9,11},{10,... | collective-permute-start | bytes 589832 | tf_op jit(solution)/shard_map/ppermute | solution.py:385
  47.0 6.3 %collective-permute-start.14 = (bf16[128,768]{1,0:T(8,128)(2,1)}, bf16[128,768]{1,0:T(8,128)(2,1)}, u32[]{:S(2)}, u32[]{:S(2)}) collective-permute-start(bf16[128,768]{1,0:T(8,128)(2,1)} %get-tuple-element.147), channel_id=1, source_target_pairs={{0,1},{1,0},{2,3},{3,2},{4,5},{5,4},{6,7},{7,6},{8,9},{9,8},{10,11... | collective-permute-start | bytes 589832 | tf_op jit(solution)/shard_map/ppermute | solution.py:382
  47.0 3.7 %collective-permute-start.18 = (bf16[128,640]{1,0:T(8,128)(2,1)}, bf16[128,640]{1,0:T(8,128)(2,1)}, u32[]{:S(2)}, u32[]{:S(2)}) collective-permute-start(bf16[128,640]{1,0:T(8,128)(2,1)} %get-tuple-element.157), channel_id=1, source_target_pairs={{0,1},{1,0},{2,3},{3,2},{4,5},{5,4},{6,7},{7,6},{8,9},{9,8},{10,11... | collective-permute-start | bytes 491528 | tf_op jit(solution)/shard_map/ppermute | solution.py:382
  48.2 7.1 %collective-permute-start.13 = (bf16[64,896]{1,0:T(8,128)(2,1)}, bf16[64,896]{1,0:T(8,128)(2,1)S(1)}, u32[]{:S(2)}, u32[]{:S(2)}) collective-permute-start(bf16[64,896]{1,0:T(8,128)(2,1)} %get-tuple-element.145), channel_id=1, source_target_pairs={{0,4},{4,0},{8,12},{12,8},{16,20},{20,16},{24,28},{28,24},{1,5},{5... | collective-permute-start | bytes 344072 | tf_op jit(solution)/shard_map/ppermute | solution.py:388
  49.7 11.9 %collective-permute-start.9 = (bf16[128,768]{1,0:T(8,128)(2,1)}, bf16[128,768]{1,0:T(8,128)(2,1)S(1)}, u32[]{:S(2)}, u32[]{:S(2)}) collective-permute-start(bf16[128,768]{1,0:T(8,128)(2,1)} %copy-done.11), channel_id=1, source_target_pairs={{0,1},{1,0},{2,3},{3,2},{4,5},{5,4},{6,7},{7,6},{8,9},{9,8},{10,11... | collective-permute-start | bytes 589832 | tf_op jit(solution)/shard_map/ppermute | solution.py:382
  50.7 16.9 %collective-permute-start.17 = (bf16[128,640]{1,0:T(8,128)(2,1)}, bf16[128,640]{1,0:T(8,128)(2,1)S(1)}, u32[]{:S(2)}, u32[]{:S(2)}) collective-permute-start(bf16[128,640]{1,0:T(8,128)(2,1)} %copy-done.12), channel_id=1, source_target_pairs={{0,1},{1,0},{2,3},{3,2},{4,5},{5,4},{6,7},{7,6},{8,9},{9,8},{10,11... | collective-permute-start | bytes 491528 | tf_op jit(solution)/shard_map/ppermute | solution.py:382
  52.2 7.8 %collective-permute-start.11 = (bf16[128,768]{1,0:T(8,128)(2,1)S(1)}, bf16[128,768]{1,0:T(8,128)(2,1)S(1)}, u32[]{:S(2)}, u32[]{:S(2)}) collective-permute-start(bf16[128,768]{1,0:T(8,128)(2,1)S(1)} %join.6), channel_id=1, source_target_pairs={{0,2},{1,3},{2,0},{3,1},{4,6},{5,7},{6,4},{7,5},{8,10},{9,11},{10,... | collective-permute-start | bytes 589832 | tf_op jit(solution)/shard_map/ppermute | solution.py:385
  53.3 14.2 %collective-permute-start.19 = (bf16[128,640]{1,0:T(8,128)(2,1)S(1)}, bf16[128,640]{1,0:T(8,128)(2,1)S(1)}, u32[]{:S(2)}, u32[]{:S(2)}) collective-permute-start(bf16[128,640]{1,0:T(8,128)(2,1)S(1)} %join.7), channel_id=1, source_target_pairs={{0,2},{1,3},{2,0},{3,1},{4,6},{5,7},{6,4},{7,5},{8,10},{9,11},{10,... | collective-permute-start | bytes 491528 | tf_op jit(solution)/shard_map/ppermute | solution.py:385
  55.4 7.5 %collective-permute-start.21 = (bf16[64,768]{1,0:T(8,128)(2,1)S(1)}, bf16[64,768]{1,0:T(8,128)(2,1)S(1)}, u32[]{:S(2)}, u32[]{:S(2)}) collective-permute-start(bf16[64,768]{1,0:T(8,128)(2,1)S(1)} %get-tuple-element.149), channel_id=1, source_target_pairs={{0,4},{4,0},{8,12},{12,8},{16,20},{20,16},{24,28},{28,24},{1,5},{5... | collective-permute-start | bytes 294920 | tf_op jit(solution)/shard_map/ppermute | solution.py:388
  60.1 4.8 %collective-permute-start.20 = (bf16[64,896]{1,0:T(8,128)(2,1)S(1)}, bf16[64,896]{1,0:T(8,128)(2,1)S(1)}, u32[]{:S(2)}, u32[]{:S(2)}) collective-permute-start(bf16[64,896]{1,0:T(8,128)(2,1)S(1)} %fusion.8), channel_id=1, source_target_pairs={{0,8},{4,12},{8,0},{12,4},{16,24},{20,28},{24,16},{28,20},{1,9},{5... | collective-permute-start | bytes 344072 | tf_op jit(solution)/shard_map/ppermute | solution.py:461
  61.7 8.2 %collective-permute-start.16 = (bf16[64,768]{1,0:T(8,128)(2,1)S(1)}, bf16[64,768]{1,0:T(8,128)(2,1)S(1)}, u32[]{:S(2)}, u32[]{:S(2)}) collective-permute-start(bf16[64,768]{1,0:T(8,128)(2,1)S(1)} %get-tuple-element.153), channel_id=1, source_target_pairs={{0,4},{4,0},{8,12},{12,8},{16,20},{20,16},{24,28},{28,24},{1,5},{5... | collective-permute-start | bytes 294920 | tf_op jit(solution)/shard_map/ppermute | solution.py:388
  62.9 25.0 %copy-start.1 = (f32[128,3072]{1,0:T(8,128)S(1)}, f32[128,3072]{1,0:T(8,128)}, u32[]{:S(2)}) copy-start(f32[128,3072]{1,0:T(8,128)} %x_start.5) | copy-start | bytes 4718596
  62.9 7.5 %collective-permute-start.25 = (bf16[64,768]{1,0:T(8,128)(2,1)S(1)}, bf16[64,768]{1,0:T(8,128)(2,1)S(1)}, u32[]{:S(2)}, u32[]{:S(2)}) collective-permute-start(bf16[64,768]{1,0:T(8,128)(2,1)S(1)} %fusion.9), channel_id=1, source_target_pairs={{0,8},{4,12},{8,0},{12,4},{16,24},{20,28},{24,16},{28,20},{1,9},{5... | collective-permute-start | bytes 294920 | tf_op jit(solution)/shard_map/ppermute | solution.py:461
  64.9 9.7 %collective-permute-start.23 = (bf16[64,896]{1,0:T(8,128)(2,1)S(1)}, bf16[64,896]{1,0:T(8,128)(2,1)S(1)}, u32[]{:S(2)}, u32[]{:S(2)}) collective-permute-start(bf16[64,896]{1,0:T(8,128)(2,1)S(1)} %fusion), channel_id=1, source_target_pairs={{0,16},{4,20},{8,24},{12,28},{16,0},{20,4},{24,8},{28,12},{1,17},{... | collective-permute-start | bytes 344072 | tf_op jit(solution)/shard_map/ppermute | solution.py:461
  67.7 4.9 %collective-permute-start.24 = (bf16[64,640]{1,0:T(8,128)(2,1)S(1)}, bf16[64,640]{1,0:T(8,128)(2,1)S(1)}, u32[]{:S(2)}, u32[]{:S(2)}) collective-permute-start(bf16[64,640]{1,0:T(8,128)(2,1)S(1)} %get-tuple-element.163), channel_id=1, source_target_pairs={{0,4},{4,0},{8,12},{12,8},{16,20},{20,16},{24,28},{28,24},{1,5},{5... | collective-permute-start | bytes 245768 | tf_op jit(solution)/shard_map/ppermute | solution.py:388
  70.0 9.6 %collective-permute-start.22 = (bf16[64,768]{1,0:T(8,128)(2,1)S(1)}, bf16[64,768]{1,0:T(8,128)(2,1)S(1)}, u32[]{:S(2)}, u32[]{:S(2)}) collective-permute-start(bf16[64,768]{1,0:T(8,128)(2,1)S(1)} %fusion.10), channel_id=1, source_target_pairs={{0,8},{4,12},{8,0},{12,4},{16,24},{20,28},{24,16},{28,20},{1,9},{5... | collective-permute-start | bytes 294920 | tf_op jit(solution)/shard_map/ppermute | solution.py:461
  70.5 9.2 %collective-permute-start.29 = (bf16[64,768]{1,0:T(8,128)(2,1)S(1)}, bf16[64,768]{1,0:T(8,128)(2,1)S(1)}, u32[]{:S(2)}, u32[]{:S(2)}) collective-permute-start(bf16[64,768]{1,0:T(8,128)(2,1)S(1)} %fusion.2), channel_id=1, source_target_pairs={{0,16},{4,20},{8,24},{12,28},{16,0},{20,4},{24,8},{28,12},{1,17},{... | collective-permute-start | bytes 294920 | tf_op jit(solution)/shard_map/ppermute | solution.py:461
  72.6 9.3 %collective-permute-start.28 = (bf16[64,640]{1,0:T(8,128)(2,1)S(1)}, bf16[64,640]{1,0:T(8,128)(2,1)S(1)}, u32[]{:S(2)}, u32[]{:S(2)}) collective-permute-start(bf16[64,640]{1,0:T(8,128)(2,1)S(1)} %fusion.11), channel_id=1, source_target_pairs={{0,8},{4,12},{8,0},{12,4},{16,24},{20,28},{24,16},{28,20},{1,9},{5... | collective-permute-start | bytes 245768 | tf_op jit(solution)/shard_map/ppermute | solution.py:461
  74.7 13.2 %collective-permute-start.33 = (bf16[64,896]{1,0:T(8,128)(2,1)S(1)}, bf16[64,896]{1,0:T(8,128)(2,1)S(1)}, u32[]{:S(2)}, u32[]{:S(2)}) collective-permute-start(bf16[64,896]{1,0:T(8,128)(2,1)S(1)} %get-tuple-element.185), channel_id=1, source_target_pairs={{0,4},{4,0},{8,12},{12,8},{16,20},{20,16},{24,28},{28,24},{1,5},{5... | collective-permute-start | bytes 344072 | tf_op jit(solution)/shard_map/ppermute | solution.py:388
  79.6 5.6 %collective-permute-start.26 = (bf16[64,768]{1,0:T(8,128)(2,1)S(1)}, bf16[64,768]{1,0:T(8,128)(2,1)S(1)}, u32[]{:S(2)}, u32[]{:S(2)}) collective-permute-start(bf16[64,768]{1,0:T(8,128)(2,1)S(1)} %fusion.5), channel_id=1, source_target_pairs={{0,16},{4,20},{8,24},{12,28},{16,0},{20,4},{24,8},{28,12},{1,17},{... | collective-permute-start | bytes 294920 | tf_op jit(solution)/shard_map/ppermute | solution.py:461
  79.8 9.0 %collective-permute-start.32 = (bf16[64,768]{1,0:T(8,128)(2,1)S(1)}, bf16[64,768]{1,0:T(8,128)(2,1)S(1)}, u32[]{:S(2)}, u32[]{:S(2)}) collective-permute-start(bf16[64,768]{1,0:T(8,128)(2,1)S(1)} %get-tuple-element.181), channel_id=1, source_target_pairs={{0,4},{4,0},{8,12},{12,8},{16,20},{20,16},{24,28},{28,24},{1,5},{5... | collective-permute-start | bytes 294920 | tf_op jit(solution)/shard_map/ppermute | solution.py:388
  81.9 5.8 %collective-permute-start.30 = (bf16[64,640]{1,0:T(8,128)(2,1)S(1)}, bf16[64,640]{1,0:T(8,128)(2,1)S(1)}, u32[]{:S(2)}, u32[]{:S(2)}) collective-permute-start(bf16[64,640]{1,0:T(8,128)(2,1)S(1)} %fusion.7), channel_id=1, source_target_pairs={{0,16},{4,20},{8,24},{12,28},{16,0},{20,4},{24,8},{28,12},{1,17},{... | collective-permute-start | bytes 245768 | tf_op jit(solution)/shard_map/ppermute | solution.py:461
  85.3 4.7 %collective-permute-start.27 = (bf16[64,768]{1,0:T(8,128)(2,1)S(1)}, bf16[64,768]{1,0:T(8,128)(2,1)S(1)}, u32[]{:S(2)}, u32[]{:S(2)}) collective-permute-start(bf16[64,768]{1,0:T(8,128)(2,1)S(1)} %get-tuple-element.183), channel_id=1, source_target_pairs={{0,4},{4,0},{8,12},{12,8},{16,20},{20,16},{24,28},{28,24},{1,5},{5... | collective-permute-start | bytes 294920 | tf_op jit(solution)/shard_map/ppermute | solution.py:388
  87.8 4.5 %collective-permute-start.31 = (bf16[64,640]{1,0:T(8,128)(2,1)S(1)}, bf16[64,640]{1,0:T(8,128)(2,1)S(1)}, u32[]{:S(2)}, u32[]{:S(2)}) collective-permute-start(bf16[64,640]{1,0:T(8,128)(2,1)S(1)} %get-tuple-element.179), channel_id=1, source_target_pairs={{0,4},{4,0},{8,12},{12,8},{16,20},{20,16},{24,28},{28,24},{1,5},{5... | collective-permute-start | bytes 245768 | tf_op jit(solution)/shard_map/ppermute | solution.py:388

commit v17 on v16

--- a/solution.py
+++ b/solution.py
@@ -493,8 +493,8 @@
         def finish(fetched):
             given = [held[name] for name in ("earlier", "kept", "fetched", "other")]
             stash.append((firsts[c], given + [fetched[0]]))
-            if len(stash) != chunks - 1:
-                mine = stash[-1:] if len(stash) < chunks else stash[-2:]
+            if len(stash) == chunks:
+                mine = stash
                 places = [place for place, _ in mine]
                 groups_in = [group for _, group in mine]
                 into = list(written)
@@ -520,7 +520,10 @@
             when += 2.2 + share * (1.0 if i == len(plan[c]) - 3 else 0.5)
     written, stash = [], []
     last = None
-    for _, c, i in sorted(turns):
+    order = [(c, i) for _, c, i in sorted(turns)]
+    order.remove((0, 2))
+    order.insert(order.index((2, 0)), (0, 2))
+    for c, i in order:
         compute, move = plan[c][i]
         fetched = inbox[c]
         if last is not None:

time: 93.7 us -> 96 us (1.025)
  waiting for transfers between devices: 19.5 us -> 28.8 us
  starting transfers between devices: 33.4 us -> 27.9 us
  Pallas kernels: 35.5 us -> 32.6 us
  local copies, waits for them, and re-layouts: 3.44 us -> 4.83 us
    ppermute x8, waiting for transfers between devices: 6.18 us -> 11.9 us  [along(): lax.ppermute(x, 'step', [(2 * a + i, 2 * b + i) for a, b in pairs for i i...]
    ppermute x8, starting transfers between devices: 13.2 us -> 9.43 us  [to_pair(): return lax.ppermute(x, 'step', [(i, i ^ 1) for i in range(n_step)])]
    ppermute x6, waiting for transfers between devices: 6.33 us -> 8.64 us  [to_chip(): lax.ppermute(x, 'seq', [(i, (i + 2 * offset) % n_seq) for i in range(n_se...]
    ppermute x8, waiting for transfers between devices: 3.87 us -> 5.36 us  [to_pair(): return lax.ppermute(x, 'step', [(i, i ^ 1) for i in range(n_step)])]
    unnamed x32 -> x36, local copies, waits for them, and re-layouts: 3.44 us -> 4.83 us
    pallas_call x3 -> x1, Pallas kernels: 2.63 us -> 1.3 us  [finish_call(): pl.pallas_call(functools.partial(finish_kernel, firsts), in_specs=[smem]...]
    ppermute x8, starting transfers between devices: 9.14 us -> 8 us  [along(): lax.ppermute(x, 'step', [(2 * a + i, 2 * b + i) for a, b in pairs for i i...]
  transfers between devices with their start and end apart: 34 -> 34, of which waited for: 12 -> 12; matrix products, arithmetic and copies ran while one was open for 0% -> 0% of each run, Pallas kernels for 25% -> 21%
where the time goes in v17:
time: 96 us; the launch traced here: 95.7 us
  Pallas kernels  32.6 us (34%)
  waiting for transfers between devices  28.8 us (30%)
  starting transfers between devices  27.9 us (29%)
  local copies, waits for them, and re-layouts  4.83 us (5%)
  between operations  1.15 us (1%)
    pallas_call x2, Pallas kernels, project_call(): pl.pallas_call(functools.partial(project_kernel, tile, load, tiles), in_s...  17.6 us
    ppermute x8, waiting for transfers between devices, along(): lax.ppermute(x, 'step', [(2 * a + i, 2 * b + i) for a, b in pairs for i i...  11.9 us
    ppermute x8, starting transfers between devices, to_pair(): return lax.ppermute(x, 'step', [(i, i ^ 1) for i in range(n_step)])  9.43 us
    ppermute x6, waiting for transfers between devices, to_chip(): lax.ppermute(x, 'seq', [(i, (i + 2 * offset) % n_seq) for i in range(n_se...  8.64 us
    ppermute x6, starting transfers between devices, to_chip(): lax.ppermute(x, 'seq', [(i, (i + 2 * offset) % n_seq) for i in range(n_se...  8.62 us
    ppermute x8, starting transfers between devices, along(): lax.ppermute(x, 'step', [(2 * a + i, 2 * b + i) for a, b in pairs for i i...  8 us
    ppermute x8, waiting for transfers between devices, to_pair(): return lax.ppermute(x, 'step', [(i, i ^ 1) for i in range(n_step)])  5.36 us
    pallas_call x2, Pallas kernels, out_call(): pl.pallas_call(functools.partial(out_kernel, plan), in_specs=[vm] * len(g...  5.1 us
  transfers between devices with their start and end apart: 34, of which 12 were waited for; matrix products, arithmetic and copies ran while one was open for 0% of the time, Pallas kernels for 21%

profile of v17, /device:TPU:0, one launch (start us, length us, event | category | flops | bytes accessed | tf_op | source)
XLA Modules:
  0.0 95.7 jit_solution(15171645621168854901)
XLA Ops:
  0.7 3.6 %norm.1 = (bf16[64,3072]{1,0:T(8,128)(2,1)}, bf16[64,3072]{1,0:T(8,128)(2,1)}, f32[1,3072]{1,0:T(1,128)}) custom-call(s32[1]{0:T(128)S(6)} %copy.12.t_ref, f32[50]{0:T(128)} %size_ref.1, f32[1,128,3072]{2,1,0:T(8,128)} %x_hbm.1, f32[50,9216]{1,0:T(8,128)} %mod_hbm.1), custom_call_target="tpu_custom_call" | custom-call | flops 3932160 | tf_op jit(solution)/shard_map/norm/pallas_call | solution.py:61
  4.3 0.5 collective-permute-start.1
  4.8 0.1 collective-permute-start.2
  4.9 2.9 %collective-permute-start = (bf16[64,3072]{1,0:T(8,128)(2,1)}, bf16[64,3072]{1,0:T(8,128)(2,1)S(1)}, u32[]{:S(2)}, u32[]{:S(2)}) collective-permute-start(bf16[64,3072]{1,0:T(8,128)(2,1)} %get-tuple-element.92.m0), channel_id=1, source_target_pairs={{0,2},{1,3},{2,0},{3,1},{4,6},{5,7},{6,4},{7,5},{8,10},{9,11},{10,... | collective-permute-start | bytes 1179656 | tf_op jit(solution)/shard_map/ppermute | solution.py:385
  7.8 0.0 collective-permute-start.3
  7.9 1.0 %copy-done.2 = bf16[64,3072]{1,0:T(8,128)(2,1)S(1)} copy-done((bf16[64,3072]{1,0:T(8,128)(2,1)S(1)}, bf16[64,3072]{1,0:T(8,128)(2,1)}, u32[]{:S(2)}) %copy-start.2) | copy-done | bytes 393240
  8.9 1.0 %copy-done.3 = bf16[64,3072]{1,0:T(8,128)(2,1)S(1)} copy-done((bf16[64,3072]{1,0:T(8,128)(2,1)S(1)}, bf16[64,3072]{1,0:T(8,128)(2,1)}, u32[]{:S(2)}) %copy-start.3) | copy-done | bytes 393240
  9.9 12.4 %project.2 = (bf16[256,512]{1,0:T(8,128)(2,1)S(1)}, bf16[256,512]{1,0:T(8,128)(2,1)S(1)}, bf16[256,512]{1,0:T(8,128)(2,1)S(1)}, bf16[256,1536]{1,0:T(8,128)(2,1)...) custom-call(bf16[64,3072]{1,0:T(8,128)(2,1)S(1)} %copy-done.3, ...), custom_call_target="tpu_custom_call" | custom-call | flops 4831838208 | tf_op jit(solution)/shard_map/project/pallas_call | solution.py:158
  22.3 0.7 copy-done.7
  23.0 0.7 copy-done.9
  23.7 2.1 %collective-permute-done.3.m1 = bf16[64,3072]{1,0:T(8,128)(2,1)S(1)} collective-permute-done((bf16[64,3072]{1,0:T(8,128)(2,1)}, bf16[64,3072]{1,0:T(8,128)(2,1)S(1)}, u32[]{:S(2)}, u32[]{:S(2)}) %collective-permute-start.3) | collective-permute-done | bytes 393248 | tf_op jit(solution)/shard_map/ppermute | solution.py:385
  25.8 1.7 %collective-permute-done.5.m3 = bf16[64,3072]{1,0:T(8,128)(2,1)S(1)} collective-permute-done((bf16[64,3072]{1,0:T(8,128)(2,1)S(1)}, bf16[64,3072]{1,0:T(8,128)(2,1)S(1)}, u32[]{:S(2)}, u32[]{:S(2)}) %collective-permute-start.5) | collective-permute-done | bytes 393248 | tf_op jit(solution)/shard_map/ppermute | solution.py:382
  27.6 5.2 %project.3 = (bf16[256,512]{1,0:T(8,128)(2,1)S(1)}, bf16[256,512]{1,0:T(8,128)(2,1)S(1)}, bf16[256,512]{1,0:T(8,128)(2,1)S(1)}, bf16[256,1536]{1,0:T(8,128)(2,1)S(1)}) custom-call(bf16[64,3072]{1,0:T(8,128)(2,1)S(1)} %collective-permute-done.m0, bf16[64,3072]{1,0:T(8,128)(2,1)S(1)} %collective-permute-done.3.m1, ...), custom_call_target="tpu_custom_call" | custom-call | flops 4831838208 | tf_op jit(solution)/shard_map/project/pallas_call | solution.py:158
  32.8 1.1 %attend.2.refs_0_.refs_4_.refs_8_ = bf16[256,512]{1,0:T(8,128)(2,1)S(1)} custom-call(bf16[256,512]{1,0:T(8,128)(2,1)S(1)} %get-tuple-element.104.refs_0_, bf16[256,512]{1,0:T(8,128)(2,1)S(1)} %copy-done.8, bf16[256,512]{1,0:T(8,128)(2,1)S(1)} %get-tuple-element.106.refs_2_, bf16[256,512]{1,0:T(8,128)(2,1)S(1)} %copy-done.10, ...), custom_call_target="tpu_custom_call" | custom-call | flops 805306368 | tf_op jit(solution)/shard_map/attend/pallas_call | solution.py:202
  34.0 1.3 %project_out.2 = (f32[128,896]{1,0:T(8,128)S(1)}, bf16[128,896]{1,0:T(8,128)(2,1)S(1)}) custom-call(bf16[256,512]{1,0:T(8,128)(2,1)S(1)} %attend.2.refs_0_.refs_4_.refs_8_, bf16[256,1536]{1,0:T(8,128)(2,1)S(1)} %get-tuple-element.119.refs_1_.refs_5_.refs_9_, bf16[512,3072]{1,0:T(8,128)(2,1)S(1)} %copy-done, bf16[1536,3072]{1,0:T(8,128)(2,1)S(1)} %bitcast.4), custom_call_target="tpu_custom_call" | custom-call | flops 939524096 | tf_op jit(solution)/shard_map/project_out/pallas_call | solution.py:246
  35.2 0.2 collective-permute-start.6
  35.4 0.9 attend.3.refs_12_.refs_16_.refs_20_.refs_24_
  36.3 0.5 collective-permute-done.6.sent
  36.8 1.8 %collective-permute-start.7 = (bf16[128,896]{1,0:T(8,128)(2,1)S(1)}, bf16[128,896]{1,0:T(8,128)(2,1)S(1)}, u32[]{:S(2)}, u32[]{:S(2)}) collective-permute-start(bf16[128,896]{1,0:T(8,128)(2,1)S(1)} %join.4), channel_id=1, source_target_pairs={{0,2},{1,3},{2,0},{3,1},{4,6},{5,7},{6,4},{7,5},{8,10},{9,11},{10,... | collective-permute-start | bytes 688136 | tf_op jit(solution)/shard_map/ppermute | solution.py:385
  38.6 3.8 %project_out.3 = (f32[128,768]{1,0:T(8,128)S(1)}, bf16[128,768]{1,0:T(8,128)(2,1)S(1)}, f32[128,768]{1,0:T(8,128)S(1)}, bf16[128,768]{1,0:T(8,128)(2,1)S(1)}, f3...) custom-call(bf16[256,512]{1,0:T(8,128)(2,1)S(1)} %attend.2.refs_0_.r, ...), custom_call_target="tpu_custom_call" | custom-call | flops 3087007744 | tf_op jit(solution)/shard_map/project_out/pallas_call | solution.py:246
  42.5 0.7 copy-done.12
  43.2 0.7 copy-done.13
  43.8 0.1 copy-done.14
  43.9 0.7 collective-permute-done.8.sent
  44.6 0.7 join.5
  45.4 1.7 %collective-permute-start.12 = (bf16[128,768]{1,0:T(8,128)(2,1)}, bf16[128,768]{1,0:T(8,128)(2,1)S(1)}, u32[]{:S(2)}, u32[]{:S(2)}) collective-permute-start(bf16[128,768]{1,0:T(8,128)(2,1)} %join.5), channel_id=1, source_target_pairs={{0,2},{1,3},{2,0},{3,1},{4,6},{5,7},{6,4},{7,5},{8,10},{9,11},{10,... | collective-permute-start | bytes 589832 | tf_op jit(solution)/shard_map/ppermute | solution.py:385
  47.0 0.1 drift.4
  47.1 1.5 %collective-permute-start.10 = (bf16[64,896]{1,0:T(8,128)(2,1)S(1)}, bf16[64,896]{1,0:T(8,128)(2,1)S(1)}, u32[]{:S(2)}, u32[]{:S(2)}) collective-permute-start(bf16[64,896]{1,0:T(8,128)(2,1)S(1)} %get-tuple-element.139), channel_id=1, source_target_pairs={{0,4},{4,0},{8,12},{12,8},{16,20},{20,16},{24,28},{28,24},{1,5},{5... | collective-permute-start | bytes 344072 | tf_op jit(solution)/shard_map/ppermute | solution.py:388
  48.7 0.2 collective-permute-start.17
  48.9 0.3 collective-permute-start.16
  49.2 3.3 %collective-permute-done.12.refs_0_ = bf16[128,768]{1,0:T(8,128)(2,1)S(1)} collective-permute-done((bf16[128,768]{1,0:T(8,128)(2,1)}, bf16[128,768]{1,0:T(8,128)(2,1)S(1)}, u32[]{:S(2)}, u32[]{:S(2)}) %collective-permute-start.12) | collective-permute-done | bytes 196640 | tf_op jit(solution)/shard_map/ppermute | solution.py:385
  52.5 1.0 %drift.5 = (f32[64,768]{1,0:T(8,128)S(1)}, f32[64,768]{1,0:T(8,128)S(1)}, bf16[64,768]{1,0:T(8,128)(2,1)S(1)}) custom-call(s32[1]{0:T(128)} %bitcast.parity, f32[128,768]{1,0:T(8,128)S(1)} %get-tuple-element.140.keep, bf16[128,768]{1,0:T(8,128)(2,1)} %collective-permute-done.11.sent, f32[1,3072]{1,0:T(1,128)S(1)} %copy-done.4, ...), custom_call_target="tpu_custom_call" | custom-call | tf_op jit(solution)/shard_map/drift/pallas_call | solution.py:297
  53.6 1.6 %collective-permute-start.13 = (bf16[64,896]{1,0:T(8,128)(2,1)S(1)}, bf16[64,896]{1,0:T(8,128)(2,1)S(1)}, u32[]{:S(2)}, u32[]{:S(2)}) collective-permute-start(bf16[64,896]{1,0:T(8,128)(2,1)S(1)} %fusion.8), channel_id=1, source_target_pairs={{0,8},{4,12},{8,0},{12,4},{16,24},{20,28},{24,16},{28,20},{1,9},{5... | collective-permute-start | bytes 344072 | tf_op jit(solution)/shard_map/ppermute | solution.py:461
  55.2 0.5 collective-permute-start.15
  55.8 0.9 collective-permute-start.21
  56.7 0.9 join.7
  57.6 1.3 %collective-permute-start.18 = (bf16[128,640]{1,0:T(8,128)(2,1)S(1)}, bf16[128,640]{1,0:T(8,128)(2,1)S(1)}, u32[]{:S(2)}, u32[]{:S(2)}) collective-permute-start(bf16[128,640]{1,0:T(8,128)(2,1)S(1)} %join.7), channel_id=1, source_target_pairs={{0,2},{1,3},{2,0},{3,1},{4,6},{5,7},{6,4},{7,5},{8,10},{9,11},{10,... | collective-permute-start | bytes 491528 | tf_op jit(solution)/shard_map/ppermute | solution.py:385
  58.9 1.5 %collective-permute-start.19 = (bf16[64,768]{1,0:T(8,128)(2,1)S(1)}, bf16[64,768]{1,0:T(8,128)(2,1)S(1)}, u32[]{:S(2)}, u32[]{:S(2)}) collective-permute-start(bf16[64,768]{1,0:T(8,128)(2,1)S(1)} %get-tuple-element.144), channel_id=1, source_target_pairs={{0,4},{4,0},{8,12},{12,8},{16,20},{20,16},{24,28},{28,24},{1,5},{5... | collective-permute-start | bytes 294920 | tf_op jit(solution)/shard_map/ppermute | solution.py:388
  60.4 3.2 %collective-permute-done.21.refs_0_ = bf16[128,768]{1,0:T(8,128)(2,1)S(1)} collective-permute-done((bf16[128,768]{1,0:T(8,128)(2,1)S(1)}, bf16[128,768]{1,0:T(8,128)(2,1)S(1)}, u32[]{:S(2)}, u32[]{:S(2)}) %collective-permute-start.21) | collective-permute-done | bytes 196640 | tf_op jit(solution)/shard_map/ppermute | solution.py:385
  63.6 2.6 %collective-permute-start.14 = (bf16[64,896]{1,0:T(8,128)(2,1)S(1)}, bf16[64,896]{1,0:T(8,128)(2,1)S(1)}, u32[]{:S(2)}, u32[]{:S(2)}) collective-permute-start(bf16[64,896]{1,0:T(8,128)(2,1)S(1)} %fusion.1), channel_id=1, source_target_pairs={{0,16},{4,20},{8,24},{12,28},{16,0},{20,4},{24,8},{28,12},{1,17},{... | collective-permute-start | bytes 344072 | tf_op jit(solution)/shard_map/ppermute | solution.py:461
  66.2 0.1 drift.6
  66.3 1.6 %collective-permute-start.24 = (bf16[64,768]{1,0:T(8,128)(2,1)S(1)}, bf16[64,768]{1,0:T(8,128)(2,1)S(1)}, u32[]{:S(2)}, u32[]{:S(2)}) collective-permute-start(bf16[64,768]{1,0:T(8,128)(2,1)S(1)} %get-tuple-element.159), channel_id=1, source_target_pairs={{0,4},{4,0},{8,12},{12,8},{16,20},{20,16},{24,28},{28,24},{1,5},{5... | collective-permute-start | bytes 294920 | tf_op jit(solution)/shard_map/ppermute | solution.py:388
  67.9 0.5 collective-permute-start.23
  68.4 0.1 drift.7
  68.5 0.6 collective-permute-start.22
  69.1 1.9 %collective-permute-done.24.refs_12_ = bf16[64,768]{1,0:T(8,128)(2,1)S(1)} collective-permute-done((bf16[64,768]{1,0:T(8,128)(2,1)S(1)}, bf16[64,768]{1,0:T(8,128)(2,1)S(1)}, u32[]{:S(2)}, u32[]{:S(2)}) %collective-permute-start.24) | collective-permute-done | bytes 98336 | tf_op jit(solution)/shard_map/ppermute | solution.py:388
  71.0 1.1 %collective-permute-start.28 = (bf16[64,768]{1,0:T(8,128)(2,1)S(1)}, bf16[64,768]{1,0:T(8,128)(2,1)S(1)}, u32[]{:S(2)}, u32[]{:S(2)}) collective-permute-start(bf16[64,768]{1,0:T(8,128)(2,1)S(1)} %fusion.10), channel_id=1, source_target_pairs={{0,8},{4,12},{8,0},{12,4},{16,24},{20,28},{24,16},{28,20},{1,9},{5... | collective-permute-start | bytes 294920 | tf_op jit(solution)/shard_map/ppermute | solution.py:461
  72.1 0.5 collective-permute-done.23
  72.6 1.3 %collective-permute-start.27 = (bf16[64,768]{1,0:T(8,128)(2,1)S(1)}, bf16[64,768]{1,0:T(8,128)(2,1)S(1)}, u32[]{:S(2)}, u32[]{:S(2)}) collective-permute-start(bf16[64,768]{1,0:T(8,128)(2,1)S(1)} %fusion.2), channel_id=1, source_target_pairs={{0,16},{4,20},{8,24},{12,28},{16,0},{20,4},{24,8},{28,12},{1,17},{... | collective-permute-start | bytes 294920 | tf_op jit(solution)/shard_map/ppermute | solution.py:461
  74.0 0.7 collective-permute-start.26
  74.6 0.1 add_convert_fusion
  74.7 3.0 %collective-permute-done.28 = bf16[64,768]{1,0:T(8,128)(2,1)S(1)} collective-permute-done((bf16[64,768]{1,0:T(8,128)(2,1)S(1)}, bf16[64,768]{1,0:T(8,128)(2,1)S(1)}, u32[]{:S(2)}, u32[]{:S(2)}) %collective-permute-start.28) | collective-permute-done | bytes 98336 | tf_op jit(solution)/shard_map/ppermute | solution.py:461
  77.7 0.1 collective-permute-start.30
  77.9 5.2 %collective-permute-done.27 = bf16[64,768]{1,0:T(8,128)(2,1)S(1)} collective-permute-done((bf16[64,768]{1,0:T(8,128)(2,1)S(1)}, bf16[64,768]{1,0:T(8,128)(2,1)S(1)}, u32[]{:S(2)}, u32[]{:S(2)}) %collective-permute-start.27) | collective-permute-done | bytes 98336 | tf_op jit(solution)/shard_map/ppermute | solution.py:461
  83.0 0.1 add_convert_fusion.2
  83.1 0.1 collective-permute-start.32
  83.2 1.1 %collective-permute-start.25 = (bf16[64,896]{1,0:T(8,128)(2,1)S(1)}, bf16[64,896]{1,0:T(8,128)(2,1)S(1)}, u32[]{:S(2)}, u32[]{:S(2)}) collective-permute-start(bf16[64,896]{1,0:T(8,128)(2,1)S(1)} %get-tuple-element.185), channel_id=1, source_target_pairs={{0,4},{4,0},{8,12},{12,8},{16,20},{20,16},{24,28},{28,24},{1,5},{5... | collective-permute-start | bytes 344072 | tf_op jit(solution)/shard_map/ppermute | solution.py:388
  84.3 1.0 %collective-permute-start.29 = (bf16[64,768]{1,0:T(8,128)(2,1)S(1)}, bf16[64,768]{1,0:T(8,128)(2,1)S(1)}, u32[]{:S(2)}, u32[]{:S(2)}) collective-permute-start(bf16[64,768]{1,0:T(8,128)(2,1)S(1)} %get-tuple-element.183), channel_id=1, source_target_pairs={{0,4},{4,0},{8,12},{12,8},{16,20},{20,16},{24,28},{28,24},{1,5},{5... | collective-permute-start | bytes 294920 | tf_op jit(solution)/shard_map/ppermute | solution.py:388
  85.3 3.2 %collective-permute-done.32 = bf16[64,640]{1,0:T(8,128)(2,1)S(1)} collective-permute-done((bf16[64,640]{1,0:T(8,128)(2,1)S(1)}, bf16[64,640]{1,0:T(8,128)(2,1)S(1)}, u32[]{:S(2)}, u32[]{:S(2)}) %collective-permute-start.32) | collective-permute-done | bytes 81952 | tf_op jit(solution)/shard_map/ppermute | solution.py:461
  88.5 0.1 add_convert_fusion.1
  88.6 1.1 %collective-permute-start.31 = (bf16[64,768]{1,0:T(8,128)(2,1)S(1)}, bf16[64,768]{1,0:T(8,128)(2,1)S(1)}, u32[]{:S(2)}, u32[]{:S(2)}) collective-permute-start(bf16[64,768]{1,0:T(8,128)(2,1)S(1)} %get-tuple-element.181), channel_id=1, source_target_pairs={{0,4},{4,0},{8,12},{12,8},{16,20},{20,16},{24,28},{28,24},{1,5},{5... | collective-permute-start | bytes 294920 | tf_op jit(solution)/shard_map/ppermute | solution.py:388
  89.7 1.1 %collective-permute-start.33 = (bf16[64,640]{1,0:T(8,128)(2,1)S(1)}, bf16[64,640]{1,0:T(8,128)(2,1)S(1)}, u32[]{:S(2)}, u32[]{:S(2)}) collective-permute-start(bf16[64,640]{1,0:T(8,128)(2,1)S(1)} %get-tuple-element.179), channel_id=1, source_target_pairs={{0,4},{4,0},{8,12},{12,8},{16,20},{20,16},{24,28},{28,24},{1,5},{5... | collective-permute-start | bytes 245768 | tf_op jit(solution)/shard_map/ppermute | solution.py:388
  90.8 3.4 %collective-permute-done.33.refs_19_ = bf16[64,640]{1,0:T(8,128)(2,1)S(1)} collective-permute-done((bf16[64,640]{1,0:T(8,128)(2,1)S(1)}, bf16[64,640]{1,0:T(8,128)(2,1)S(1)}, u32[]{:S(2)}, u32[]{:S(2)}) %collective-permute-start.33) | collective-permute-done | bytes 81952 | tf_op jit(solution)/shard_map/ppermute | solution.py:388
  94.3 1.3 %finish.1 = f32[1,128,3072]{2,1,0:T(8,128)} custom-call(s32[1]{0:T(128)} %bitcast.parity, f32[128,3072]{1,0:T(8,128)S(1)} %copy-done.1, f32[64,896]{1,0:T(8,128)S(1)} %get-tuple-element.186.refs_0_, f32[64,896]{1,0:T(8,128)S(1)} %get-tuple-element.138.refs_1_, bf16[64,896]{1,0:T(8,128)(2,1)S(1)} %collective-permute-done.10.refs_2_, ...), custom_call_target="tpu_custom_call" | custom-call | tf_op jit(solution)/shard_map/finish/pallas_call | solution.py:342
  (69 shorter events, 0.5 us)
Async XLA Ops:
  0.0 7.9 %copy-start.5 = (f32[128]{0:T(128)S(1)}, f32[128]{0:T(128)}, u32[]{:S(2)}) copy-start(f32[128]{0:T(128)} %param.16) | copy-start | bytes 1540
  0.0 7.9 %copy-start.6 = (f32[128]{0:T(128)S(1)}, f32[128]{0:T(128)}, u32[]{:S(2)}) copy-start(f32[128]{0:T(128)} %param.17) | copy-start | bytes 1540
  4.3 3.6 %collective-permute-start.1 = (bf16[64,3072]{1,0:T(8,128)(2,1)}, bf16[64,3072]{1,0:T(8,128)(2,1)S(1)}, u32[]{:S(2)}, u32[]{:S(2)}) collective-permute-start(bf16[64,3072]{1,0:T(8,128)(2,1)} %get-tuple-element.92.m0), channel_id=1, source_target_pairs={{0,1},{1,0},{2,3},{3,2},{4,5},{5,4},{6,7},{7,6},{8,9},{9,8},{10,11... | collective-permute-start | bytes 1179656 | tf_op jit(solution)/shard_map/ppermute | solution.py:382
  4.8 3.1 %collective-permute-start.2 = (bf16[64,3072]{1,0:T(8,128)(2,1)}, bf16[64,3072]{1,0:T(8,128)(2,1)S(1)}, u32[]{:S(2)}, u32[]{:S(2)}) collective-permute-start(bf16[64,3072]{1,0:T(8,128)(2,1)} %get-tuple-element.93.m1), channel_id=1, source_target_pairs={{0,1},{1,0},{2,3},{3,2},{4,5},{5,4},{6,7},{7,6},{8,9},{9,8},{10,11... | collective-permute-start | bytes 1179656 | tf_op jit(solution)/shard_map/ppermute | solution.py:382
  4.9 18.8 %collective-permute-start = (bf16[64,3072]{1,0:T(8,128)(2,1)}, bf16[64,3072]{1,0:T(8,128)(2,1)S(1)}, u32[]{:S(2)}, u32[]{:S(2)}) collective-permute-start(bf16[64,3072]{1,0:T(8,128)(2,1)} %get-tuple-element.92.m0), channel_id=1, source_target_pairs={{0,2},{1,3},{2,0},{3,1},{4,6},{5,7},{6,4},{7,5},{8,10},{9,11},{10,... | collective-permute-start | bytes 1179656 | tf_op jit(solution)/shard_map/ppermute | solution.py:385
  7.8 18.0 %collective-permute-start.3 = (bf16[64,3072]{1,0:T(8,128)(2,1)}, bf16[64,3072]{1,0:T(8,128)(2,1)S(1)}, u32[]{:S(2)}, u32[]{:S(2)}) collective-permute-start(bf16[64,3072]{1,0:T(8,128)(2,1)} %get-tuple-element.93.m1), channel_id=1, source_target_pairs={{0,2},{1,3},{2,0},{3,1},{4,6},{5,7},{6,4},{7,5},{8,10},{9,11},{10,... | collective-permute-start | bytes 1179656 | tf_op jit(solution)/shard_map/ppermute | solution.py:385
  7.9 1.0 %copy-start.2 = (bf16[64,3072]{1,0:T(8,128)(2,1)S(1)}, bf16[64,3072]{1,0:T(8,128)(2,1)}, u32[]{:S(2)}) copy-start(bf16[64,3072]{1,0:T(8,128)(2,1)} %get-tuple-element.93.m1) | copy-start | bytes 1179652
  8.9 1.0 %copy-start.3 = (bf16[64,3072]{1,0:T(8,128)(2,1)S(1)}, bf16[64,3072]{1,0:T(8,128)(2,1)}, u32[]{:S(2)}) copy-start(bf16[64,3072]{1,0:T(8,128)(2,1)} %get-tuple-element.92.m0) | copy-start | bytes 1179652
  22.3 0.7 copy-start.7
  23.0 0.7 copy-start.9
  23.7 2.1 %collective-permute-start.4 = (bf16[64,3072]{1,0:T(8,128)(2,1)S(1)}, bf16[64,3072]{1,0:T(8,128)(2,1)S(1)}, u32[]{:S(2)}, u32[]{:S(2)}) collective-permute-start(bf16[64,3072]{1,0:T(8,128)(2,1)S(1)} %collective-permute-done.m0), channel_id=1, source_target_pairs={{0,1},{1,0},{2,3},{3,2},{4,5},{5,4},{6,7},{7,6},{8,9},{9,8},{10,11... | collective-permute-start | bytes 1179656 | tf_op jit(solution)/shard_map/ppermute | solution.py:382
  25.8 1.7 %collective-permute-start.5 = (bf16[64,3072]{1,0:T(8,128)(2,1)S(1)}, bf16[64,3072]{1,0:T(8,128)(2,1)S(1)}, u32[]{:S(2)}, u32[]{:S(2)}) collective-permute-start(bf16[64,3072]{1,0:T(8,128)(2,1)S(1)} %collective-permute-done.3.m1), channel_id=1, source_target_pairs={{0,1},{1,0},{2,3},{3,2},{4,5},{5,4},{6,7},{7,6},{8,9},{9,8},{10,11... | collective-permute-start | bytes 1179656 | tf_op jit(solution)/shard_map/ppermute | solution.py:382
  27.5 6.4 %slice-start = ((s8[9437184]{0:T(1024)(128)(4,1)}), s8[4194304]{0:T(1024)(128)(4,1)S(1)}, s32[]{:S(2)}) async-start(s8[9437184]{0:T(1024)(128)(4,1)} %bitcast.3), calls=%async_computation | async-start | bytes 8388608
  27.5 5.3 %copy-start.8 = (bf16[256,512]{1,0:T(8,128)(2,1)S(1)}, bf16[256,512]{1,0:T(8,128)(2,1)}, u32[]{:S(2)}) copy-start(bf16[256,512]{1,0:T(8,128)(2,1)} %copy-done.7) | copy-start | bytes 786436
  27.5 5.3 %copy-start.10 = (bf16[256,512]{1,0:T(8,128)(2,1)S(1)}, bf16[256,512]{1,0:T(8,128)(2,1)}, u32[]{:S(2)}) copy-start(bf16[256,512]{1,0:T(8,128)(2,1)} %copy-done.9) | copy-start | bytes 786436
  27.5 6.4 %slice-start.1 = ((s8[9437184]{0:T(1024)(128)(4,1)}), s8[4194304]{0:T(1024)(128)(4,1)S(1)}, s32[]{:S(2)}) async-start(s8[9437184]{0:T(1024)(128)(4,1)} %bitcast.3), calls=%async_computation.1 | async-start | bytes 8388608
  27.5 6.4 %slice-start.2 = ((s8[9437184]{0:T(1024)(128)(4,1)}), s8[1048576]{0:T(1024)(128)(4,1)S(1)}, s32[]{:S(2)}) async-start(s8[9437184]{0:T(1024)(128)(4,1)} %bitcast.3), calls=%async_computation.2 | async-start | bytes 2097152
  27.6 6.4 %copy-start = (bf16[512,3072]{1,0:T(8,128)(2,1)S(1)}, bf16[512,3072]{1,0:T(8,128)(2,1)}, u32[]{:S(2)}) copy-start(bf16[512,3072]{1,0:T(8,128)(2,1)} %refs_25_.1) | copy-start | bytes 9437188
  35.2 1.6 %collective-permute-start.6 = (bf16[128,896]{1,0:T(8,128)(2,1)S(1)}, bf16[128,896]{1,0:T(8,128)(2,1)S(1)}, u32[]{:S(2)}, u32[]{:S(2)}) collective-permute-start(bf16[128,896]{1,0:T(8,128)(2,1)S(1)} %get-tuple-element.112), channel_id=1, source_target_pairs={{0,1},{1,0},{2,3},{3,2},{4,5},{5,4},{6,7},{7,6},{8,9},{9,8},{10,11... | collective-permute-start | bytes 688136 | tf_op jit(solution)/shard_map/ppermute | solution.py:382
  36.8 7.8 %collective-permute-start.7 = (bf16[128,896]{1,0:T(8,128)(2,1)S(1)}, bf16[128,896]{1,0:T(8,128)(2,1)S(1)}, u32[]{:S(2)}, u32[]{:S(2)}) collective-permute-start(bf16[128,896]{1,0:T(8,128)(2,1)S(1)} %join.4), channel_id=1, source_target_pairs={{0,2},{1,3},{2,0},{3,1},{4,6},{5,7},{6,4},{7,5},{8,10},{9,11},{10,... | collective-permute-start | bytes 688136 | tf_op jit(solution)/shard_map/ppermute | solution.py:385
  38.6 8.4 %copy-start.4 = (f32[1,3072]{1,0:T(1,128)S(1)}, f32[1,3072]{1,0:T(1,128)}, u32[]{:S(2)}) copy-start(f32[1,3072]{1,0:T(1,128)} %get-tuple-element.136.sg) | copy-start | bytes 36868
  42.5 0.7 copy-start.12
  43.2 0.7 copy-start.13
  43.2 0.7 copy-start.14
  43.2 2.2 %copy-start.11 = (bf16[128,768]{1,0:T(8,128)(2,1)}, bf16[128,768]{1,0:T(8,128)(2,1)S(1)}, u32[]{:S(2)}) copy-start(bf16[128,768]{1,0:T(8,128)(2,1)S(1)} %get-tuple-element.157) | copy-start | bytes 589828
  43.2 1.4 %collective-permute-start.8 = (bf16[128,768]{1,0:T(8,128)(2,1)S(1)}, bf16[128,768]{1,0:T(8,128)(2,1)S(1)}, u32[]{:S(2)}, u32[]{:S(2)}) collective-permute-start(bf16[128,768]{1,0:T(8,128)(2,1)S(1)} %get-tuple-element.127), channel_id=1, source_target_pairs={{0,1},{1,0},{2,3},{3,2},{4,5},{5,4},{6,7},{7,6},{8,9},{9,8},{10,11... | collective-permute-start | bytes 589832 | tf_op jit(solution)/shard_map/ppermute | solution.py:382
  43.9 3.1 %collective-permute-start.9 = (bf16[128,896]{1,0:T(8,128)(2,1)S(1)}, bf16[128,896]{1,0:T(8,128)(2,1)S(1)}, u32[]{:S(2)}, u32[]{:S(2)}) collective-permute-start(bf16[128,896]{1,0:T(8,128)(2,1)S(1)} %get-tuple-element.135), channel_id=1, source_target_pairs={{0,1},{1,0},{2,3},{3,2},{4,5},{5,4},{6,7},{7,6},{8,9},{9,8},{10,11... | collective-permute-start | bytes 688136 | tf_op jit(solution)/shard_map/ppermute | solution.py:382
  45.4 7.2 %collective-permute-start.12 = (bf16[128,768]{1,0:T(8,128)(2,1)}, bf16[128,768]{1,0:T(8,128)(2,1)S(1)}, u32[]{:S(2)}, u32[]{:S(2)}) collective-permute-start(bf16[128,768]{1,0:T(8,128)(2,1)} %join.5), channel_id=1, source_target_pairs={{0,2},{1,3},{2,0},{3,1},{4,6},{5,7},{6,4},{7,5},{8,10},{9,11},{10,... | collective-permute-start | bytes 589832 | tf_op jit(solution)/shard_map/ppermute | solution.py:385
  47.0 5.5 %collective-permute-start.11 = (bf16[128,768]{1,0:T(8,128)(2,1)}, bf16[128,768]{1,0:T(8,128)(2,1)}, u32[]{:S(2)}, u32[]{:S(2)}) collective-permute-start(bf16[128,768]{1,0:T(8,128)(2,1)} %get-tuple-element.141), channel_id=1, source_target_pairs={{0,1},{1,0},{2,3},{3,2},{4,5},{5,4},{6,7},{7,6},{8,9},{9,8},{10,11... | collective-permute-start | bytes 589832 | tf_op jit(solution)/shard_map/ppermute | solution.py:382
  47.1 6.4 %collective-permute-start.10 = (bf16[64,896]{1,0:T(8,128)(2,1)S(1)}, bf16[64,896]{1,0:T(8,128)(2,1)S(1)}, u32[]{:S(2)}, u32[]{:S(2)}) collective-permute-start(bf16[64,896]{1,0:T(8,128)(2,1)S(1)} %get-tuple-element.139), channel_id=1, source_target_pairs={{0,4},{4,0},{8,12},{12,8},{16,20},{20,16},{24,28},{28,24},{1,5},{5... | collective-permute-start | bytes 344072 | tf_op jit(solution)/shard_map/ppermute | solution.py:388
  48.7 7.0 %collective-permute-start.17 = (bf16[128,768]{1,0:T(8,128)(2,1)}, bf16[128,768]{1,0:T(8,128)(2,1)S(1)}, u32[]{:S(2)}, u32[]{:S(2)}) collective-permute-start(bf16[128,768]{1,0:T(8,128)(2,1)} %copy-done.12), channel_id=1, source_target_pairs={{0,1},{1,0},{2,3},{3,2},{4,5},{5,4},{6,7},{7,6},{8,9},{9,8},{10,11... | collective-permute-start | bytes 589832 | tf_op jit(solution)/shard_map/ppermute | solution.py:382
  48.9 7.8 %collective-permute-start.16 = (bf16[128,640]{1,0:T(8,128)(2,1)}, bf16[128,640]{1,0:T(8,128)(2,1)}, u32[]{:S(2)}, u32[]{:S(2)}) collective-permute-start(bf16[128,640]{1,0:T(8,128)(2,1)} %copy-done.14), channel_id=1, source_target_pairs={{0,1},{1,0},{2,3},{3,2},{4,5},{5,4},{6,7},{7,6},{8,9},{9,8},{10,11... | collective-permute-start | bytes 491528 | tf_op jit(solution)/shard_map/ppermute | solution.py:382
  53.6 5.3 %collective-permute-start.13 = (bf16[64,896]{1,0:T(8,128)(2,1)S(1)}, bf16[64,896]{1,0:T(8,128)(2,1)S(1)}, u32[]{:S(2)}, u32[]{:S(2)}) collective-permute-start(bf16[64,896]{1,0:T(8,128)(2,1)S(1)} %fusion.8), channel_id=1, source_target_pairs={{0,8},{4,12},{8,0},{12,4},{16,24},{20,28},{24,16},{28,20},{1,9},{5... | collective-permute-start | bytes 344072 | tf_op jit(solution)/shard_map/ppermute | solution.py:461
  55.2 11.0 %collective-permute-start.20 = (bf16[128,768]{1,0:T(8,128)(2,1)}, bf16[128,768]{1,0:T(8,128)(2,1)S(1)}, u32[]{:S(2)}, u32[]{:S(2)}) collective-permute-start(bf16[128,768]{1,0:T(8,128)(2,1)} %copy-done.11), channel_id=1, source_target_pairs={{0,1},{1,0},{2,3},{3,2},{4,5},{5,4},{6,7},{7,6},{8,9},{9,8},{10,11... | collective-permute-start | bytes 589832 | tf_op jit(solution)/shard_map/ppermute | solution.py:382
  55.2 13.2 %collective-permute-start.15 = (bf16[128,640]{1,0:T(8,128)(2,1)}, bf16[128,640]{1,0:T(8,128)(2,1)S(1)}, u32[]{:S(2)}, u32[]{:S(2)}) collective-permute-start(bf16[128,640]{1,0:T(8,128)(2,1)} %copy-done.13), channel_id=1, source_target_pairs={{0,1},{1,0},{2,3},{3,2},{4,5},{5,4},{6,7},{7,6},{8,9},{9,8},{10,11... | collective-permute-start | bytes 491528 | tf_op jit(solution)/shard_map/ppermute | solution.py:382
  55.8 7.8 %collective-permute-start.21 = (bf16[128,768]{1,0:T(8,128)(2,1)S(1)}, bf16[128,768]{1,0:T(8,128)(2,1)S(1)}, u32[]{:S(2)}, u32[]{:S(2)}) collective-permute-start(bf16[128,768]{1,0:T(8,128)(2,1)S(1)} %join.6), channel_id=1, source_target_pairs={{0,2},{1,3},{2,0},{3,1},{4,6},{5,7},{6,4},{7,5},{8,10},{9,11},{10,... | collective-permute-start | bytes 589832 | tf_op jit(solution)/shard_map/ppermute | solution.py:385
  57.6 10.8 %collective-permute-start.18 = (bf16[128,640]{1,0:T(8,128)(2,1)S(1)}, bf16[128,640]{1,0:T(8,128)(2,1)S(1)}, u32[]{:S(2)}, u32[]{:S(2)}) collective-permute-start(bf16[128,640]{1,0:T(8,128)(2,1)S(1)} %join.7), channel_id=1, source_target_pairs={{0,2},{1,3},{2,0},{3,1},{4,6},{5,7},{6,4},{7,5},{8,10},{9,11},{10,... | collective-permute-start | bytes 491528 | tf_op jit(solution)/shard_map/ppermute | solution.py:385
  58.9 9.0 %collective-permute-start.19 = (bf16[64,768]{1,0:T(8,128)(2,1)S(1)}, bf16[64,768]{1,0:T(8,128)(2,1)S(1)}, u32[]{:S(2)}, u32[]{:S(2)}) collective-permute-start(bf16[64,768]{1,0:T(8,128)(2,1)S(1)} %get-tuple-element.144), channel_id=1, source_target_pairs={{0,4},{4,0},{8,12},{12,8},{16,20},{20,16},{24,28},{28,24},{1,5},{5... | collective-permute-start | bytes 294920 | tf_op jit(solution)/shard_map/ppermute | solution.py:388
  63.6 11.0 %collective-permute-start.14 = (bf16[64,896]{1,0:T(8,128)(2,1)S(1)}, bf16[64,896]{1,0:T(8,128)(2,1)S(1)}, u32[]{:S(2)}, u32[]{:S(2)}) collective-permute-start(bf16[64,896]{1,0:T(8,128)(2,1)S(1)} %fusion.1), channel_id=1, source_target_pairs={{0,16},{4,20},{8,24},{12,28},{16,0},{20,4},{24,8},{28,12},{1,17},{... | collective-permute-start | bytes 344072 | tf_op jit(solution)/shard_map/ppermute | solution.py:461
  66.3 28.0 %copy-start.1 = (f32[128,3072]{1,0:T(8,128)S(1)}, f32[128,3072]{1,0:T(8,128)}, u32[]{:S(2)}) copy-start(f32[128,3072]{1,0:T(8,128)} %x_start.1) | copy-start | bytes 4718596
  66.3 4.7 %collective-permute-start.24 = (bf16[64,768]{1,0:T(8,128)(2,1)S(1)}, bf16[64,768]{1,0:T(8,128)(2,1)S(1)}, u32[]{:S(2)}, u32[]{:S(2)}) collective-permute-start(bf16[64,768]{1,0:T(8,128)(2,1)S(1)} %get-tuple-element.159), channel_id=1, source_target_pairs={{0,4},{4,0},{8,12},{12,8},{16,20},{20,16},{24,28},{28,24},{1,5},{5... | collective-permute-start | bytes 294920 | tf_op jit(solution)/shard_map/ppermute | solution.py:388
  67.9 4.7 %collective-permute-start.23 = (bf16[64,768]{1,0:T(8,128)(2,1)S(1)}, bf16[64,768]{1,0:T(8,128)(2,1)S(1)}, u32[]{:S(2)}, u32[]{:S(2)}) collective-permute-start(bf16[64,768]{1,0:T(8,128)(2,1)S(1)} %fusion.9), channel_id=1, source_target_pairs={{0,8},{4,12},{8,0},{12,4},{16,24},{20,28},{24,16},{28,20},{1,9},{5... | collective-permute-start | bytes 294920 | tf_op jit(solution)/shard_map/ppermute | solution.py:461
  68.5 5.5 %collective-permute-start.22 = (bf16[64,640]{1,0:T(8,128)(2,1)S(1)}, bf16[64,640]{1,0:T(8,128)(2,1)S(1)}, u32[]{:S(2)}, u32[]{:S(2)}) collective-permute-start(bf16[64,640]{1,0:T(8,128)(2,1)S(1)} %get-tuple-element.163), channel_id=1, source_target_pairs={{0,4},{4,0},{8,12},{12,8},{16,20},{20,16},{24,28},{28,24},{1,5},{5... | collective-permute-start | bytes 245768 | tf_op jit(solution)/shard_map/ppermute | solution.py:388
  71.0 6.7 %collective-permute-start.28 = (bf16[64,768]{1,0:T(8,128)(2,1)S(1)}, bf16[64,768]{1,0:T(8,128)(2,1)S(1)}, u32[]{:S(2)}, u32[]{:S(2)}) collective-permute-start(bf16[64,768]{1,0:T(8,128)(2,1)S(1)} %fusion.10), channel_id=1, source_target_pairs={{0,8},{4,12},{8,0},{12,4},{16,24},{20,28},{24,16},{28,20},{1,9},{5... | collective-permute-start | bytes 294920 | tf_op jit(solution)/shard_map/ppermute | solution.py:461
  72.6 10.4 %collective-permute-start.27 = (bf16[64,768]{1,0:T(8,128)(2,1)S(1)}, bf16[64,768]{1,0:T(8,128)(2,1)S(1)}, u32[]{:S(2)}, u32[]{:S(2)}) collective-permute-start(bf16[64,768]{1,0:T(8,128)(2,1)S(1)} %fusion.2), channel_id=1, source_target_pairs={{0,16},{4,20},{8,24},{12,28},{16,0},{20,4},{24,8},{28,12},{1,17},{... | collective-permute-start | bytes 294920 | tf_op jit(solution)/shard_map/ppermute | solution.py:461
  74.0 9.1 %collective-permute-start.26 = (bf16[64,640]{1,0:T(8,128)(2,1)S(1)}, bf16[64,640]{1,0:T(8,128)(2,1)S(1)}, u32[]{:S(2)}, u32[]{:S(2)}) collective-permute-start(bf16[64,640]{1,0:T(8,128)(2,1)S(1)} %fusion.11), channel_id=1, source_target_pairs={{0,8},{4,12},{8,0},{12,4},{16,24},{20,28},{24,16},{28,20},{1,9},{5... | collective-permute-start | bytes 245768 | tf_op jit(solution)/shard_map/ppermute | solution.py:461
  77.7 10.8 %collective-permute-start.30 = (bf16[64,768]{1,0:T(8,128)(2,1)S(1)}, bf16[64,768]{1,0:T(8,128)(2,1)S(1)}, u32[]{:S(2)}, u32[]{:S(2)}) collective-permute-start(bf16[64,768]{1,0:T(8,128)(2,1)S(1)} %fusion.4), channel_id=1, source_target_pairs={{0,16},{4,20},{8,24},{12,28},{16,0},{20,4},{24,8},{28,12},{1,17},{... | collective-permute-start | bytes 294920 | tf_op jit(solution)/shard_map/ppermute | solution.py:461
  83.1 5.4 %collective-permute-start.32 = (bf16[64,640]{1,0:T(8,128)(2,1)S(1)}, bf16[64,640]{1,0:T(8,128)(2,1)S(1)}, u32[]{:S(2)}, u32[]{:S(2)}) collective-permute-start(bf16[64,640]{1,0:T(8,128)(2,1)S(1)} %fusion.6), channel_id=1, source_target_pairs={{0,16},{4,20},{8,24},{12,28},{16,0},{20,4},{24,8},{28,12},{1,17},{... | collective-permute-start | bytes 245768 | tf_op jit(solution)/shard_map/ppermute | solution.py:461
  83.2 7.6 %collective-permute-start.25 = (bf16[64,896]{1,0:T(8,128)(2,1)S(1)}, bf16[64,896]{1,0:T(8,128)(2,1)S(1)}, u32[]{:S(2)}, u32[]{:S(2)}) collective-permute-start(bf16[64,896]{1,0:T(8,128)(2,1)S(1)} %get-tuple-element.185), channel_id=1, source_target_pairs={{0,4},{4,0},{8,12},{12,8},{16,20},{20,16},{24,28},{28,24},{1,5},{5... | collective-permute-start | bytes 344072 | tf_op jit(solution)/shard_map/ppermute | solution.py:388
  84.3 6.5 %collective-permute-start.29 = (bf16[64,768]{1,0:T(8,128)(2,1)S(1)}, bf16[64,768]{1,0:T(8,128)(2,1)S(1)}, u32[]{:S(2)}, u32[]{:S(2)}) collective-permute-start(bf16[64,768]{1,0:T(8,128)(2,1)S(1)} %get-tuple-element.183), channel_id=1, source_target_pairs={{0,4},{4,0},{8,12},{12,8},{16,20},{20,16},{24,28},{28,24},{1,5},{5... | collective-permute-start | bytes 294920 | tf_op jit(solution)/shard_map/ppermute | solution.py:388
  88.6 5.7 %collective-permute-start.31 = (bf16[64,768]{1,0:T(8,128)(2,1)S(1)}, bf16[64,768]{1,0:T(8,128)(2,1)S(1)}, u32[]{:S(2)}, u32[]{:S(2)}) collective-permute-start(bf16[64,768]{1,0:T(8,128)(2,1)S(1)} %get-tuple-element.181), channel_id=1, source_target_pairs={{0,4},{4,0},{8,12},{12,8},{16,20},{20,16},{24,28},{28,24},{1,5},{5... | collective-permute-start | bytes 294920 | tf_op jit(solution)/shard_map/ppermute | solution.py:388
  89.7 4.5 %collective-permute-start.33 = (bf16[64,640]{1,0:T(8,128)(2,1)S(1)}, bf16[64,640]{1,0:T(8,128)(2,1)S(1)}, u32[]{:S(2)}, u32[]{:S(2)}) collective-permute-start(bf16[64,640]{1,0:T(8,128)(2,1)S(1)} %get-tuple-element.179), channel_id=1, source_target_pairs={{0,4},{4,0},{8,12},{12,8},{16,20},{20,16},{24,28},{28,24},{1,5},{5... | collective-permute-start | bytes 245768 | tf_op jit(solution)/shard_map/ppermute | solution.py:388

commit v18 on v14

--- a/solution.py
+++ b/solution.py
@@ -373,7 +373,7 @@
     groups = n_step // 2
     half = rows // 2
     unit = width // 24
-    counts = [n * unit for n in (9,8,7)]
+    counts = [n * unit for n in (9, 7, 8)]
     chunks = len(counts)
     firsts = [sum(counts[:c]) for c in range(chunks)]
     qg, kg = q_gain[None, :], k_gain[None, :]

time: 90 us -> 91.7 us (1.019)
  waiting for transfers between devices: 20.2 us -> 24.1 us
    ppermute x6, waiting for transfers between devices: 6.95 us -> 9.28 us  [along(): lax.ppermute(x, 'step', [(2 * a + i, 2 * b + i) for a, b in pairs for i i...]
    ppermute x6, waiting for transfers between devices: 3.22 us -> 4.64 us  [to_pair(): return lax.ppermute(x, 'step', [(i, i ^ 1) for i in range(n_step)])]
    pallas_call x3, Pallas kernels: 1.78 us -> 0.84 us  [join_call(): pl.pallas_call(join_kernel, in_specs=[vm, vm], out_specs=vm, out_shape=ja...]
  transfers between devices with their start and end apart: 27 -> 27, of which waited for: 11 -> 13; matrix products, arithmetic and copies ran while one was open for 0% -> 0% of each run, Pallas kernels for 24% -> 23%
where the time goes in v18:
time: 91.7 us; the launch traced here: 91.4 us
  Pallas kernels  33.3 us (36%)
  starting transfers between devices  29.1 us (32%)
  waiting for transfers between devices  24.1 us (26%)
  local copies, waits for them, and re-layouts  3.43 us (4%)
  between operations  1.09 us (1%)
    pallas_call x2, Pallas kernels, project_call(): pl.pallas_call(functools.partial(project_kernel, tile, load, tiles), in_s...  17.6 us
    ppermute x6, starting transfers between devices, along(): lax.ppermute(x, 'step', [(2 * a + i, 2 * b + i) for a, b in pairs for i i...  11.9 us
    ppermute x6, waiting for transfers between devices, along(): lax.ppermute(x, 'step', [(2 * a + i, 2 * b + i) for a, b in pairs for i i...  9.28 us
    ppermute x6, starting transfers between devices, to_pair(): return lax.ppermute(x, 'step', [(i, i ^ 1) for i in range(n_step)])  8.53 us
    ppermute x5, starting transfers between devices, to_chip(): lax.ppermute(x, 'seq', [(i, (i + 2 * offset) % n_seq) for i in range(n_se...  7.1 us
    ppermute x5, waiting for transfers between devices, to_chip(): lax.ppermute(x, 'seq', [(i, (i + 2 * offset) % n_seq) for i in range(n_se...  6.93 us
    pallas_call x2, Pallas kernels, out_call(): pl.pallas_call(functools.partial(out_kernel, plan), in_specs=[vm] * len(g...  5.25 us
    ppermute x6, waiting for transfers between devices, to_pair(): return lax.ppermute(x, 'step', [(i, i ^ 1) for i in range(n_step)])  4.64 us
  transfers between devices with their start and end apart: 27, of which 13 were waited for; matrix products, arithmetic and copies ran while one was open for 0% of the time, Pallas kernels for 23%

profile of v18, /device:TPU:0, one launch (start us, length us, event | category | flops | bytes accessed | tf_op | source)
XLA Modules:
  0.0 91.4 jit_solution(2244434649808041144)
XLA Ops:
  0.7 3.6 %norm.1 = (bf16[64,3072]{1,0:T(8,128)(2,1)}, bf16[64,3072]{1,0:T(8,128)(2,1)}, f32[1,3072]{1,0:T(1,128)}) custom-call(s32[1]{0:T(128)S(6)} %copy.14.t_ref, f32[50]{0:T(128)} %size_ref.1, f32[1,128,3072]{2,1,0:T(8,128)} %x_hbm.1, f32[50,9216]{1,0:T(8,128)} %mod_hbm.1), custom_call_target="tpu_custom_call" | custom-call | flops 3932160 | tf_op jit(solution)/shard_map/norm/pallas_call | solution.py:61
  4.3 0.5 collective-permute-start.1
  4.8 0.1 collective-permute-start.2
  4.9 2.9 %collective-permute-start = (bf16[64,3072]{1,0:T(8,128)(2,1)}, bf16[64,3072]{1,0:T(8,128)(2,1)S(1)}, u32[]{:S(2)}, u32[]{:S(2)}) collective-permute-start(bf16[64,3072]{1,0:T(8,128)(2,1)} %get-tuple-element.77.m0), channel_id=1, source_target_pairs={{0,2},{1,3},{2,0},{3,1},{4,6},{5,7},{6,4},{7,5},{8,10},{9,11},{10,... | collective-permute-start | bytes 1179656 | tf_op jit(solution)/shard_map/ppermute | solution.py:385
  7.8 0.0 collective-permute-start.3
  7.8 0.0 collective-permute-done.1.m2
  7.9 0.0 collective-permute-done.2.m3
  7.9 1.0 %copy-done.2 = bf16[64,3072]{1,0:T(8,128)(2,1)S(1)} copy-done((bf16[64,3072]{1,0:T(8,128)(2,1)S(1)}, bf16[64,3072]{1,0:T(8,128)(2,1)}, u32[]{:S(2)}) %copy-start.2) | copy-done | bytes 393240
  8.9 1.0 %copy-done.3 = bf16[64,3072]{1,0:T(8,128)(2,1)S(1)} copy-done((bf16[64,3072]{1,0:T(8,128)(2,1)S(1)}, bf16[64,3072]{1,0:T(8,128)(2,1)}, u32[]{:S(2)}) %copy-start.3) | copy-done | bytes 393240
  9.9 12.4 %project.2 = (bf16[256,512]{1,0:T(8,128)(2,1)S(1)}, bf16[256,512]{1,0:T(8,128)(2,1)S(1)}, bf16[256,512]{1,0:T(8,128)(2,1)S(1)}, bf16[256,1536]{1,0:T(8,128)(2,1)...) custom-call(bf16[64,3072]{1,0:T(8,128)(2,1)S(1)} %copy-done.3, ...), custom_call_target="tpu_custom_call" | custom-call | flops 4831838208 | tf_op jit(solution)/shard_map/project/pallas_call | solution.py:158
  22.3 0.0 copy-start.8
  22.3 0.7 copy-done.8
  23.0 0.7 copy-done.10
  23.7 2.1 %collective-permute-done.3.m1 = bf16[64,3072]{1,0:T(8,128)(2,1)S(1)} collective-permute-done((bf16[64,3072]{1,0:T(8,128)(2,1)}, bf16[64,3072]{1,0:T(8,128)(2,1)S(1)}, u32[]{:S(2)}, u32[]{:S(2)}) %collective-permute-start.3) | collective-permute-done | bytes 393248 | tf_op jit(solution)/shard_map/ppermute | solution.py:385
  25.8 1.7 %collective-permute-done.5.m3 = bf16[64,3072]{1,0:T(8,128)(2,1)S(1)} collective-permute-done((bf16[64,3072]{1,0:T(8,128)(2,1)S(1)}, bf16[64,3072]{1,0:T(8,128)(2,1)S(1)}, u32[]{:S(2)}, u32[]{:S(2)}) %collective-permute-start.5) | collective-permute-done | bytes 393248 | tf_op jit(solution)/shard_map/ppermute | solution.py:382
  27.6 0.0 copy-start
  27.6 5.2 %project.3 = (bf16[256,512]{1,0:T(8,128)(2,1)S(1)}, bf16[256,512]{1,0:T(8,128)(2,1)S(1)}, bf16[256,512]{1,0:T(8,128)(2,1)S(1)}, bf16[256,1536]{1,0:T(8,128)(2,1)S(1)}) custom-call(bf16[64,3072]{1,0:T(8,128)(2,1)S(1)} %collective-permute-done.m0, bf16[64,3072]{1,0:T(8,128)(2,1)S(1)} %collective-permute-done.3.m1, ...), custom_call_target="tpu_custom_call" | custom-call | flops 4831838208 | tf_op jit(solution)/shard_map/project/pallas_call | solution.py:158
  32.8 1.1 %attend.2.refs_0_.refs_4_ = bf16[256,512]{1,0:T(8,128)(2,1)S(1)} custom-call(bf16[256,512]{1,0:T(8,128)(2,1)S(1)} %get-tuple-element.89.refs_0_, bf16[256,512]{1,0:T(8,128)(2,1)S(1)} %copy-done.9, bf16[256,512]{1,0:T(8,128)(2,1)S(1)} %get-tuple-element.91.refs_2_, bf16[256,512]{1,0:T(8,128)(2,1)S(1)} %copy-done.11, ...), custom_call_target="tpu_custom_call" | custom-call | flops 805306368 | tf_op jit(solution)/shard_map/attend/pallas_call | solution.py:202
  34.0 1.5 %project_out.2 = (f32[128,1152]{1,0:T(8,128)S(1)}, bf16[128,1152]{1,0:T(8,128)(2,1)S(1)}) custom-call(bf16[256,512]{1,0:T(8,128)(2,1)S(1)} %attend.2.refs_0_.refs_4_, bf16[256,1536]{1,0:T(8,128)(2,1)S(1)} %get-tuple-element.104.refs_1_.refs_5_, bf16[512,3072]{1,0:T(8,128)(2,1)S(1)} %copy-done, bf16[1536,3072]{1,0:T(8,128)(2,1)S(1)} %bitcast.4), custom_call_target="tpu_custom_call" | custom-call | flops 1207959552 | tf_op jit(solution)/shard_map/project_out/pallas_call | solution.py:246
  35.5 0.2 collective-permute-start.6
  35.7 0.9 attend.3.refs_8_.refs_12_.refs_16_
  36.6 0.6 collective-permute-done.6.sent
  37.2 0.1 join.3
  37.2 1.8 %collective-permute-start.7 = (bf16[128,1152]{1,0:T(8,128)(2,1)S(1)}, bf16[128,1152]{1,0:T(8,128)(2,1)S(1)}, u32[]{:S(2)}, u32[]{:S(2)}) collective-permute-start(bf16[128,1152]{1,0:T(8,128)(2,1)S(1)} %join.3), channel_id=1, source_target_pairs={{0,2},{1,3},{2,0},{3,1},{4,6},{5,7},{6,4},{7,5},{8,10},{9,11},{10,... | collective-permute-start | bytes 884744 | tf_op jit(solution)/shard_map/ppermute | solution.py:385
  39.0 3.7 %project_out.3 = (f32[128,896]{1,0:T(8,128)S(1)}, bf16[128,896]{1,0:T(8,128)(2,1)S(1)}, f32[128,1024]{1,0:T(8,128)S(1)}, bf16[128,1024]{1,0:T(8,128)(2,1)}, f32[...) custom-call(bf16[256,512]{1,0:T(8,128)(2,1)S(1)} %attend.2.refs_0_.r, ...), custom_call_target="tpu_custom_call" | custom-call | flops 2818572288 | tf_op jit(solution)/shard_map/project_out/pallas_call | solution.py:246
  42.7 0.5 collective-permute-start.11
  43.3 0.0 collective-permute-start.14
  43.3 1.0 %collective-permute-done.8.sent = bf16[128,896]{1,0:T(8,128)(2,1)S(1)} collective-permute-done((bf16[128,896]{1,0:T(8,128)(2,1)S(1)}, bf16[128,896]{1,0:T(8,128)(2,1)S(1)}, u32[]{:S(2)}, u32[]{:S(2)}) %collective-permute-start.8) | collective-permute-done | bytes 229408 | tf_op jit(solution)/shard_map/ppermute | solution.py:382
  44.2 2.1 %collective-permute-done.7.refs_0_ = bf16[128,1152]{1,0:T(8,128)(2,1)S(1)} collective-permute-done((bf16[128,1152]{1,0:T(8,128)(2,1)S(1)}, bf16[128,1152]{1,0:T(8,128)(2,1)S(1)}, u32[]{:S(2)}, u32[]{:S(2)}) %collective-permute-start.7) | collective-permute-done | bytes 294944 | tf_op jit(solution)/shard_map/ppermute | solution.py:385
  46.3 0.7 join.4
  47.1 1.7 %collective-permute-start.10 = (bf16[128,896]{1,0:T(8,128)(2,1)}, bf16[128,896]{1,0:T(8,128)(2,1)}, u32[]{:S(2)}, u32[]{:S(2)}) collective-permute-start(bf16[128,896]{1,0:T(8,128)(2,1)} %join.4), channel_id=1, source_target_pairs={{0,2},{1,3},{2,0},{3,1},{4,6},{5,7},{6,4},{7,5},{8,10},{9,11},{10,... | collective-permute-start | bytes 688136 | tf_op jit(solution)/shard_map/ppermute | solution.py:385
  48.8 0.7 drift.3
  49.6 1.5 %collective-permute-start.16 = (bf16[64,1152]{1,0:T(8,128)(2,1)}, bf16[64,1152]{1,0:T(8,128)(2,1)S(1)}, u32[]{:S(2)}, u32[]{:S(2)}) collective-permute-start(bf16[64,1152]{1,0:T(8,128)(2,1)} %get-tuple-element.124), channel_id=1, source_target_pairs={{0,4},{4,0},{8,12},{12,8},{16,20},{20,16},{24,28},{28,24},{1,5},{5... | collective-permute-start | bytes 442376 | tf_op jit(solution)/shard_map/ppermute | solution.py:388
  51.1 0.2 collective-permute-start.13
  51.3 0.6 collective-permute-start.15
  51.9 2.5 %collective-permute-done.10.refs_0_ = bf16[128,896]{1,0:T(8,128)(2,1)} collective-permute-done((bf16[128,896]{1,0:T(8,128)(2,1)}, bf16[128,896]{1,0:T(8,128)(2,1)}, u32[]{:S(2)}, u32[]{:S(2)}) %collective-permute-start.10) | collective-permute-done | bytes 229408 | tf_op jit(solution)/shard_map/ppermute | solution.py:385
  54.5 1.1 %drift.4 = (f32[64,896]{1,0:T(8,128)S(1)}, f32[64,896]{1,0:T(8,128)S(1)}, bf16[64,896]{1,0:T(8,128)(2,1)S(1)}) custom-call(s32[1]{0:T(128)} %bitcast.parity, f32[128,896]{1,0:T(8,128)S(1)} %get-tuple-element.117.keep, bf16[128,896]{1,0:T(8,128)(2,1)} %collective-permute-done.9.sent, f32[1,3072]{1,0:T(1,128)S(1)} %copy-done.4, ...), custom_call_target="tpu_custom_call" | custom-call | tf_op jit(solution)/shard_map/drift/pallas_call | solution.py:297
  55.6 2.5 %collective-permute-start.12 = (bf16[64,896]{1,0:T(8,128)(2,1)S(1)}, bf16[64,896]{1,0:T(8,128)(2,1)S(1)}, u32[]{:S(2)}, u32[]{:S(2)}) collective-permute-start(bf16[64,896]{1,0:T(8,128)(2,1)S(1)} %get-tuple-element.127), channel_id=1, source_target_pairs={{0,4},{4,0},{8,12},{12,8},{16,20},{20,16},{24,28},{28,24},{1,5},{5... | collective-permute-start | bytes 344072 | tf_op jit(solution)/shard_map/ppermute | solution.py:388
  58.1 0.0 copy-start.1
  58.1 1.6 %collective-permute-start.19 = (bf16[64,1152]{1,0:T(8,128)(2,1)S(1)}, bf16[64,1152]{1,0:T(8,128)(2,1)S(1)}, u32[]{:S(2)}, u32[]{:S(2)}) collective-permute-start(bf16[64,1152]{1,0:T(8,128)(2,1)S(1)} %fusion.6), channel_id=1, source_target_pairs={{0,8},{4,12},{8,0},{12,4},{16,24},{20,28},{24,16},{28,20},{1,9},{5... | collective-permute-start | bytes 442376 | tf_op jit(solution)/shard_map/ppermute | solution.py:459
  59.8 0.1 collective-permute-done.15.refs_0_
  59.9 0.1 drift.5
  60.0 1.6 %collective-permute-start.18 = (bf16[64,1024]{1,0:T(8,128)(2,1)S(1)}, bf16[64,1024]{1,0:T(8,128)(2,1)S(1)}, u32[]{:S(2)}, u32[]{:S(2)}) collective-permute-start(bf16[64,1024]{1,0:T(8,128)(2,1)S(1)} %get-tuple-element.135), channel_id=1, source_target_pairs={{0,4},{4,0},{8,12},{12,8},{16,20},{20,16},{24,28},{28,24},{1,5},{5... | collective-permute-start | bytes 393224 | tf_op jit(solution)/shard_map/ppermute | solution.py:388
  61.7 1.6 %collective-permute-start.17 = (bf16[64,896]{1,0:T(8,128)(2,1)S(1)}, bf16[64,896]{1,0:T(8,128)(2,1)S(1)}, u32[]{:S(2)}, u32[]{:S(2)}) collective-permute-start(bf16[64,896]{1,0:T(8,128)(2,1)S(1)} %fusion.8), channel_id=1, source_target_pairs={{0,8},{4,12},{8,0},{12,4},{16,24},{20,28},{24,16},{28,20},{1,9},{5... | collective-permute-start | bytes 344072 | tf_op jit(solution)/shard_map/ppermute | solution.py:459
  63.3 0.1 collective-permute-done.19
  63.4 0.1 fusion
  63.5 2.6 %collective-permute-start.21 = (bf16[64,1152]{1,0:T(8,128)(2,1)S(1)}, bf16[64,1152]{1,0:T(8,128)(2,1)S(1)}, u32[]{:S(2)}, u32[]{:S(2)}) collective-permute-start(bf16[64,1152]{1,0:T(8,128)(2,1)S(1)} %fusion), channel_id=1, source_target_pairs={{0,16},{4,20},{8,24},{12,28},{16,0},{20,4},{24,8},{28,12},{1,17},{... | collective-permute-start | bytes 442376 | tf_op jit(solution)/shard_map/ppermute | solution.py:459
  66.1 1.7 %collective-permute-start.22 = (bf16[64,1024]{1,0:T(8,128)(2,1)S(1)}, bf16[64,1024]{1,0:T(8,128)(2,1)S(1)}, u32[]{:S(2)}, u32[]{:S(2)}) collective-permute-start(bf16[64,1024]{1,0:T(8,128)(2,1)S(1)} %fusion.7), channel_id=1, source_target_pairs={{0,8},{4,12},{8,0},{12,4},{16,24},{20,28},{24,16},{28,20},{1,9},{5... | collective-permute-start | bytes 393224 | tf_op jit(solution)/shard_map/ppermute | solution.py:459
  67.8 0.9 %collective-permute-done.17 = bf16[64,896]{1,0:T(8,128)(2,1)S(1)} collective-permute-done((bf16[64,896]{1,0:T(8,128)(2,1)S(1)}, bf16[64,896]{1,0:T(8,128)(2,1)S(1)}, u32[]{:S(2)}, u32[]{:S(2)}) %collective-permute-start.17) | collective-permute-done | bytes 114720 | tf_op jit(solution)/shard_map/ppermute | solution.py:459
  68.8 1.7 %collective-permute-start.20 = (bf16[64,896]{1,0:T(8,128)(2,1)S(1)}, bf16[64,896]{1,0:T(8,128)(2,1)S(1)}, u32[]{:S(2)}, u32[]{:S(2)}) collective-permute-start(bf16[64,896]{1,0:T(8,128)(2,1)S(1)} %fusion.5), channel_id=1, source_target_pairs={{0,16},{4,20},{8,24},{12,28},{16,0},{20,4},{24,8},{28,12},{1,17},{... | collective-permute-start | bytes 344072 | tf_op jit(solution)/shard_map/ppermute | solution.py:459
  70.5 2.6 %collective-permute-done.22 = bf16[64,1024]{1,0:T(8,128)(2,1)S(1)} collective-permute-done((bf16[64,1024]{1,0:T(8,128)(2,1)S(1)}, bf16[64,1024]{1,0:T(8,128)(2,1)S(1)}, u32[]{:S(2)}, u32[]{:S(2)}) %collective-permute-start.22) | collective-permute-done | bytes 131104 | tf_op jit(solution)/shard_map/ppermute | solution.py:459
  73.1 0.1 fusion.2
  73.1 2.6 %collective-permute-start.24 = (bf16[64,1024]{1,0:T(8,128)(2,1)S(1)}, bf16[64,1024]{1,0:T(8,128)(2,1)S(1)}, u32[]{:S(2)}, u32[]{:S(2)}) collective-permute-start(bf16[64,1024]{1,0:T(8,128)(2,1)S(1)} %fusion.2), channel_id=1, source_target_pairs={{0,16},{4,20},{8,24},{12,28},{16,0},{20,4},{24,8},{28,12},{1,17},{... | collective-permute-start | bytes 393224 | tf_op jit(solution)/shard_map/ppermute | solution.py:459
  75.7 0.1 add_convert_fusion
  75.8 0.9 collective-permute-start.26
  76.7 1.9 %collective-permute-done.20 = bf16[64,896]{1,0:T(8,128)(2,1)S(1)} collective-permute-done((bf16[64,896]{1,0:T(8,128)(2,1)S(1)}, bf16[64,896]{1,0:T(8,128)(2,1)S(1)}, u32[]{:S(2)}, u32[]{:S(2)}) %collective-permute-start.20) | collective-permute-done | bytes 114720 | tf_op jit(solution)/shard_map/ppermute | solution.py:459
  78.6 0.1 add_convert_fusion.2
  78.6 3.8 %collective-permute-done.24 = bf16[64,1024]{1,0:T(8,128)(2,1)S(1)} collective-permute-done((bf16[64,1024]{1,0:T(8,128)(2,1)S(1)}, bf16[64,1024]{1,0:T(8,128)(2,1)S(1)}, u32[]{:S(2)}, u32[]{:S(2)}) %collective-permute-start.24) | collective-permute-done | bytes 131104 | tf_op jit(solution)/shard_map/ppermute | solution.py:459
  82.4 0.1 add_convert_fusion.1
  82.5 1.6 %collective-permute-start.25 = (bf16[64,1024]{1,0:T(8,128)(2,1)S(1)}, bf16[64,1024]{1,0:T(8,128)(2,1)S(1)}, u32[]{:S(2)}, u32[]{:S(2)}) collective-permute-start(bf16[64,1024]{1,0:T(8,128)(2,1)S(1)} %get-tuple-element.149), channel_id=1, source_target_pairs={{0,4},{4,0},{8,12},{12,8},{16,20},{20,16},{24,28},{28,24},{1,5},{5... | collective-permute-start | bytes 393224 | tf_op jit(solution)/shard_map/ppermute | solution.py:388
  84.1 0.5 collective-permute-start.23
  84.6 0.9 %finish.2.refs_10_ = f32[1,128,3072]{2,1,0:T(8,128)} custom-call(s32[1]{0:T(128)} %bitcast.parity, f32[128,3072]{1,0:T(8,128)S(1)} %copy-done.1, f32[64,1152]{1,0:T(8,128)S(1)} %get-tuple-element.154.refs_0_, f32[64,1152]{1,0:T(8,128)S(1)} %get-tuple-element.132.refs_1_, bf16[64,1152]{1,0:T(8,128)(2,1)S(1)} %collective-permute-done.16.refs_2_, ...), custom_call_target="tpu_custom_call" | custom-call | tf_op jit(solution)/shard_map/finish/pallas_call | solution.py:342
  85.5 4.6 %collective-permute-done.23.refs_4_ = bf16[64,896]{1,0:T(8,128)(2,1)S(1)} collective-permute-done((bf16[64,896]{1,0:T(8,128)(2,1)S(1)}, bf16[64,896]{1,0:T(8,128)(2,1)S(1)}, u32[]{:S(2)}, u32[]{:S(2)}) %collective-permute-start.23) | collective-permute-done | bytes 114720 | tf_op jit(solution)/shard_map/ppermute | solution.py:388
  90.2 1.1 %finish.3 = f32[1,128,3072]{2,1,0:T(8,128)} custom-call(s32[1]{0:T(128)} %bitcast.parity, f32[128,3072]{1,0:T(8,128)S(1)} %copy-done.1, f32[64,896]{1,0:T(8,128)S(1)} %get-tuple-element.152.refs_0_, f32[64,896]{1,0:T(8,128)S(1)} %get-tuple-element.126.refs_1_, bf16[64,896]{1,0:T(8,128)(2,1)S(1)} %collective-permute-done.12.refs_2_, ...), custom_call_target="tpu_custom_call", output_to_operand_aliasing={{}: (12, {})} | custom-call | tf_op jit(solution)/shard_map/finish/pallas_call | solution.py:342
  (45 shorter events, 0.2 us)
Async XLA Ops:
  0.0 7.9 %copy-start.5 = (f32[128]{0:T(128)S(1)}, f32[128]{0:T(128)}, u32[]{:S(2)}) copy-start(f32[128]{0:T(128)} %param.16) | copy-start | bytes 1540
  0.0 7.9 %copy-start.6 = (f32[128]{0:T(128)S(1)}, f32[128]{0:T(128)}, u32[]{:S(2)}) copy-start(f32[128]{0:T(128)} %param.17) | copy-start | bytes 1540
  4.3 3.6 %collective-permute-start.1 = (bf16[64,3072]{1,0:T(8,128)(2,1)}, bf16[64,3072]{1,0:T(8,128)(2,1)S(1)}, u32[]{:S(2)}, u32[]{:S(2)}) collective-permute-start(bf16[64,3072]{1,0:T(8,128)(2,1)} %get-tuple-element.77.m0), channel_id=1, source_target_pairs={{0,1},{1,0},{2,3},{3,2},{4,5},{5,4},{6,7},{7,6},{8,9},{9,8},{10,11... | collective-permute-start | bytes 1179656 | tf_op jit(solution)/shard_map/ppermute | solution.py:382
  4.8 3.1 %collective-permute-start.2 = (bf16[64,3072]{1,0:T(8,128)(2,1)}, bf16[64,3072]{1,0:T(8,128)(2,1)S(1)}, u32[]{:S(2)}, u32[]{:S(2)}) collective-permute-start(bf16[64,3072]{1,0:T(8,128)(2,1)} %get-tuple-element.78.m1), channel_id=1, source_target_pairs={{0,1},{1,0},{2,3},{3,2},{4,5},{5,4},{6,7},{7,6},{8,9},{9,8},{10,11... | collective-permute-start | bytes 1179656 | tf_op jit(solution)/shard_map/ppermute | solution.py:382
  4.9 18.8 %collective-permute-start = (bf16[64,3072]{1,0:T(8,128)(2,1)}, bf16[64,3072]{1,0:T(8,128)(2,1)S(1)}, u32[]{:S(2)}, u32[]{:S(2)}) collective-permute-start(bf16[64,3072]{1,0:T(8,128)(2,1)} %get-tuple-element.77.m0), channel_id=1, source_target_pairs={{0,2},{1,3},{2,0},{3,1},{4,6},{5,7},{6,4},{7,5},{8,10},{9,11},{10,... | collective-permute-start | bytes 1179656 | tf_op jit(solution)/shard_map/ppermute | solution.py:385
  7.8 18.0 %collective-permute-start.3 = (bf16[64,3072]{1,0:T(8,128)(2,1)}, bf16[64,3072]{1,0:T(8,128)(2,1)S(1)}, u32[]{:S(2)}, u32[]{:S(2)}) collective-permute-start(bf16[64,3072]{1,0:T(8,128)(2,1)} %get-tuple-element.78.m1), channel_id=1, source_target_pairs={{0,2},{1,3},{2,0},{3,1},{4,6},{5,7},{6,4},{7,5},{8,10},{9,11},{10,... | collective-permute-start | bytes 1179656 | tf_op jit(solution)/shard_map/ppermute | solution.py:385
  7.9 1.0 %copy-start.2 = (bf16[64,3072]{1,0:T(8,128)(2,1)S(1)}, bf16[64,3072]{1,0:T(8,128)(2,1)}, u32[]{:S(2)}) copy-start(bf16[64,3072]{1,0:T(8,128)(2,1)} %get-tuple-element.78.m1) | copy-start | bytes 1179652
  8.9 1.0 %copy-start.3 = (bf16[64,3072]{1,0:T(8,128)(2,1)S(1)}, bf16[64,3072]{1,0:T(8,128)(2,1)}, u32[]{:S(2)}) copy-start(bf16[64,3072]{1,0:T(8,128)(2,1)} %get-tuple-element.77.m0) | copy-start | bytes 1179652
  22.3 0.7 copy-start.8
  23.0 0.7 copy-start.10
  23.7 2.1 %collective-permute-start.4 = (bf16[64,3072]{1,0:T(8,128)(2,1)S(1)}, bf16[64,3072]{1,0:T(8,128)(2,1)S(1)}, u32[]{:S(2)}, u32[]{:S(2)}) collective-permute-start(bf16[64,3072]{1,0:T(8,128)(2,1)S(1)} %collective-permute-done.m0), channel_id=1, source_target_pairs={{0,1},{1,0},{2,3},{3,2},{4,5},{5,4},{6,7},{7,6},{8,9},{9,8},{10,11... | collective-permute-start | bytes 1179656 | tf_op jit(solution)/shard_map/ppermute | solution.py:382
  25.8 1.7 %collective-permute-start.5 = (bf16[64,3072]{1,0:T(8,128)(2,1)S(1)}, bf16[64,3072]{1,0:T(8,128)(2,1)S(1)}, u32[]{:S(2)}, u32[]{:S(2)}) collective-permute-start(bf16[64,3072]{1,0:T(8,128)(2,1)S(1)} %collective-permute-done.3.m1), channel_id=1, source_target_pairs={{0,1},{1,0},{2,3},{3,2},{4,5},{5,4},{6,7},{7,6},{8,9},{9,8},{10,11... | collective-permute-start | bytes 1179656 | tf_op jit(solution)/shard_map/ppermute | solution.py:382
  27.5 6.4 %slice-start = ((s8[9437184]{0:T(1024)(128)(4,1)}), s8[4194304]{0:T(1024)(128)(4,1)S(1)}, s32[]{:S(2)}) async-start(s8[9437184]{0:T(1024)(128)(4,1)} %bitcast.3), calls=%async_computation | async-start | bytes 8388608
  27.5 5.3 %copy-start.9 = (bf16[256,512]{1,0:T(8,128)(2,1)S(1)}, bf16[256,512]{1,0:T(8,128)(2,1)}, u32[]{:S(2)}) copy-start(bf16[256,512]{1,0:T(8,128)(2,1)} %copy-done.8) | copy-start | bytes 786436
  27.5 5.3 %copy-start.11 = (bf16[256,512]{1,0:T(8,128)(2,1)S(1)}, bf16[256,512]{1,0:T(8,128)(2,1)}, u32[]{:S(2)}) copy-start(bf16[256,512]{1,0:T(8,128)(2,1)} %copy-done.10) | copy-start | bytes 786436
  27.5 6.4 %slice-start.1 = ((s8[9437184]{0:T(1024)(128)(4,1)}), s8[4194304]{0:T(1024)(128)(4,1)S(1)}, s32[]{:S(2)}) async-start(s8[9437184]{0:T(1024)(128)(4,1)} %bitcast.3), calls=%async_computation.1 | async-start | bytes 8388608
  27.5 6.4 %slice-start.2 = ((s8[9437184]{0:T(1024)(128)(4,1)}), s8[1048576]{0:T(1024)(128)(4,1)S(1)}, s32[]{:S(2)}) async-start(s8[9437184]{0:T(1024)(128)(4,1)} %bitcast.3), calls=%async_computation.2 | async-start | bytes 2097152
  27.6 6.4 %copy-start = (bf16[512,3072]{1,0:T(8,128)(2,1)S(1)}, bf16[512,3072]{1,0:T(8,128)(2,1)}, u32[]{:S(2)}) copy-start(bf16[512,3072]{1,0:T(8,128)(2,1)} %refs_17_.1) | copy-start | bytes 9437188
  35.5 1.6 %collective-permute-start.6 = (bf16[128,1152]{1,0:T(8,128)(2,1)S(1)}, bf16[128,1152]{1,0:T(8,128)(2,1)S(1)}, u32[]{:S(2)}, u32[]{:S(2)}) collective-permute-start(bf16[128,1152]{1,0:T(8,128)(2,1)S(1)} %get-tuple-element.97), channel_id=1, source_target_pairs={{0,1},{1,0},{2,3},{3,2},{4,5},{5,4},{6,7},{7,6},{8,9},{9,8},{10,11... | collective-permute-start | bytes 884744 | tf_op jit(solution)/shard_map/ppermute | solution.py:382
  37.2 9.1 %collective-permute-start.7 = (bf16[128,1152]{1,0:T(8,128)(2,1)S(1)}, bf16[128,1152]{1,0:T(8,128)(2,1)S(1)}, u32[]{:S(2)}, u32[]{:S(2)}) collective-permute-start(bf16[128,1152]{1,0:T(8,128)(2,1)S(1)} %join.3), channel_id=1, source_target_pairs={{0,2},{1,3},{2,0},{3,1},{4,6},{5,7},{6,4},{7,5},{8,10},{9,11},{10,... | collective-permute-start | bytes 884744 | tf_op jit(solution)/shard_map/ppermute | solution.py:385
  39.0 9.8 %copy-start.4 = (f32[1,3072]{1,0:T(1,128)S(1)}, f32[1,3072]{1,0:T(1,128)}, u32[]{:S(2)}) copy-start(f32[1,3072]{1,0:T(1,128)} %get-tuple-element.119.sg) | copy-start | bytes 36868
  42.7 4.3 %copy-start.7 = (bf16[128,1024]{1,0:T(8,128)(2,1)}, bf16[128,1024]{1,0:T(8,128)(2,1)S(1)}, u32[]{:S(2)}) copy-start(bf16[128,1024]{1,0:T(8,128)(2,1)S(1)} %get-tuple-element.129) | copy-start | bytes 786436
  42.7 1.5 %collective-permute-start.8 = (bf16[128,896]{1,0:T(8,128)(2,1)S(1)}, bf16[128,896]{1,0:T(8,128)(2,1)S(1)}, u32[]{:S(2)}, u32[]{:S(2)}) collective-permute-start(bf16[128,896]{1,0:T(8,128)(2,1)S(1)} %get-tuple-element.111), channel_id=1, source_target_pairs={{0,1},{1,0},{2,3},{3,2},{4,5},{5,4},{6,7},{7,6},{8,9},{9,8},{10,11... | collective-permute-start | bytes 688136 | tf_op jit(solution)/shard_map/ppermute | solution.py:382
  42.7 6.1 %collective-permute-start.11 = (bf16[128,1152]{1,0:T(8,128)(2,1)S(1)}, bf16[128,1152]{1,0:T(8,128)(2,1)S(1)}, u32[]{:S(2)}, u32[]{:S(2)}) collective-permute-start(bf16[128,1152]{1,0:T(8,128)(2,1)S(1)} %get-tuple-element.122), channel_id=1, source_target_pairs={{0,1},{1,0},{2,3},{3,2},{4,5},{5,4},{6,7},{7,6},{8,9},{9,8},{10,11... | collective-permute-start | bytes 884744 | tf_op jit(solution)/shard_map/ppermute | solution.py:382
  43.3 8.0 %collective-permute-start.14 = (bf16[128,1024]{1,0:T(8,128)(2,1)}, bf16[128,1024]{1,0:T(8,128)(2,1)S(1)}, u32[]{:S(2)}, u32[]{:S(2)}) collective-permute-start(bf16[128,1024]{1,0:T(8,128)(2,1)} %get-tuple-element.131), channel_id=1, source_target_pairs={{0,1},{1,0},{2,3},{3,2},{4,5},{5,4},{6,7},{7,6},{8,9},{9,8},{10,11... | collective-permute-start | bytes 786440 | tf_op jit(solution)/shard_map/ppermute | solution.py:382
  47.1 7.4 %collective-permute-start.10 = (bf16[128,896]{1,0:T(8,128)(2,1)}, bf16[128,896]{1,0:T(8,128)(2,1)}, u32[]{:S(2)}, u32[]{:S(2)}) collective-permute-start(bf16[128,896]{1,0:T(8,128)(2,1)} %join.4), channel_id=1, source_target_pairs={{0,2},{1,3},{2,0},{3,1},{4,6},{5,7},{6,4},{7,5},{8,10},{9,11},{10,... | collective-permute-start | bytes 688136 | tf_op jit(solution)/shard_map/ppermute | solution.py:385
  48.8 5.6 %collective-permute-start.9 = (bf16[128,896]{1,0:T(8,128)(2,1)}, bf16[128,896]{1,0:T(8,128)(2,1)}, u32[]{:S(2)}, u32[]{:S(2)}) collective-permute-start(bf16[128,896]{1,0:T(8,128)(2,1)} %get-tuple-element.118), channel_id=1, source_target_pairs={{0,1},{1,0},{2,3},{3,2},{4,5},{5,4},{6,7},{7,6},{8,9},{9,8},{10,11... | collective-permute-start | bytes 688136 | tf_op jit(solution)/shard_map/ppermute | solution.py:382
  49.6 8.5 %collective-permute-start.16 = (bf16[64,1152]{1,0:T(8,128)(2,1)}, bf16[64,1152]{1,0:T(8,128)(2,1)S(1)}, u32[]{:S(2)}, u32[]{:S(2)}) collective-permute-start(bf16[64,1152]{1,0:T(8,128)(2,1)} %get-tuple-element.124), channel_id=1, source_target_pairs={{0,4},{4,0},{8,12},{12,8},{16,20},{20,16},{24,28},{28,24},{1,5},{5... | collective-permute-start | bytes 442376 | tf_op jit(solution)/shard_map/ppermute | solution.py:388
  51.1 8.8 %collective-permute-start.13 = (bf16[128,1024]{1,0:T(8,128)(2,1)}, bf16[128,1024]{1,0:T(8,128)(2,1)S(1)}, u32[]{:S(2)}, u32[]{:S(2)}) collective-permute-start(bf16[128,1024]{1,0:T(8,128)(2,1)} %copy-done.7), channel_id=1, source_target_pairs={{0,1},{1,0},{2,3},{3,2},{4,5},{5,4},{6,7},{7,6},{8,9},{9,8},{10,11... | collective-permute-start | bytes 786440 | tf_op jit(solution)/shard_map/ppermute | solution.py:382
  51.3 8.6 %collective-permute-start.15 = (bf16[128,1024]{1,0:T(8,128)(2,1)S(1)}, bf16[128,1024]{1,0:T(8,128)(2,1)S(1)}, u32[]{:S(2)}, u32[]{:S(2)}) collective-permute-start(bf16[128,1024]{1,0:T(8,128)(2,1)S(1)} %join.5), channel_id=1, source_target_pairs={{0,2},{1,3},{2,0},{3,1},{4,6},{5,7},{6,4},{7,5},{8,10},{9,11},{10,... | collective-permute-start | bytes 786440 | tf_op jit(solution)/shard_map/ppermute | solution.py:385
  55.6 6.0 %collective-permute-start.12 = (bf16[64,896]{1,0:T(8,128)(2,1)S(1)}, bf16[64,896]{1,0:T(8,128)(2,1)S(1)}, u32[]{:S(2)}, u32[]{:S(2)}) collective-permute-start(bf16[64,896]{1,0:T(8,128)(2,1)S(1)} %get-tuple-element.127), channel_id=1, source_target_pairs={{0,4},{4,0},{8,12},{12,8},{16,20},{20,16},{24,28},{28,24},{1,5},{5... | collective-permute-start | bytes 344072 | tf_op jit(solution)/shard_map/ppermute | solution.py:388
  58.1 26.5 %copy-start.1 = (f32[128,3072]{1,0:T(8,128)S(1)}, f32[128,3072]{1,0:T(8,128)}, u32[]{:S(2)}) copy-start(f32[128,3072]{1,0:T(8,128)} %x_start.3) | copy-start | bytes 4718596
  58.1 5.3 %collective-permute-start.19 = (bf16[64,1152]{1,0:T(8,128)(2,1)S(1)}, bf16[64,1152]{1,0:T(8,128)(2,1)S(1)}, u32[]{:S(2)}, u32[]{:S(2)}) collective-permute-start(bf16[64,1152]{1,0:T(8,128)(2,1)S(1)} %fusion.6), channel_id=1, source_target_pairs={{0,8},{4,12},{8,0},{12,4},{16,24},{20,28},{24,16},{28,20},{1,9},{5... | collective-permute-start | bytes 442376 | tf_op jit(solution)/shard_map/ppermute | solution.py:459
  60.0 6.1 %collective-permute-start.18 = (bf16[64,1024]{1,0:T(8,128)(2,1)S(1)}, bf16[64,1024]{1,0:T(8,128)(2,1)S(1)}, u32[]{:S(2)}, u32[]{:S(2)}) collective-permute-start(bf16[64,1024]{1,0:T(8,128)(2,1)S(1)} %get-tuple-element.135), channel_id=1, source_target_pairs={{0,4},{4,0},{8,12},{12,8},{16,20},{20,16},{24,28},{28,24},{1,5},{5... | collective-permute-start | bytes 393224 | tf_op jit(solution)/shard_map/ppermute | solution.py:388
  61.7 7.1 %collective-permute-start.17 = (bf16[64,896]{1,0:T(8,128)(2,1)S(1)}, bf16[64,896]{1,0:T(8,128)(2,1)S(1)}, u32[]{:S(2)}, u32[]{:S(2)}) collective-permute-start(bf16[64,896]{1,0:T(8,128)(2,1)S(1)} %fusion.8), channel_id=1, source_target_pairs={{0,8},{4,12},{8,0},{12,4},{16,24},{20,28},{24,16},{28,20},{1,9},{5... | collective-permute-start | bytes 344072 | tf_op jit(solution)/shard_map/ppermute | solution.py:459
  63.5 12.3 %collective-permute-start.21 = (bf16[64,1152]{1,0:T(8,128)(2,1)S(1)}, bf16[64,1152]{1,0:T(8,128)(2,1)S(1)}, u32[]{:S(2)}, u32[]{:S(2)}) collective-permute-start(bf16[64,1152]{1,0:T(8,128)(2,1)S(1)} %fusion), channel_id=1, source_target_pairs={{0,16},{4,20},{8,24},{12,28},{16,0},{20,4},{24,8},{28,12},{1,17},{... | collective-permute-start | bytes 442376 | tf_op jit(solution)/shard_map/ppermute | solution.py:459
  66.1 6.9 %collective-permute-start.22 = (bf16[64,1024]{1,0:T(8,128)(2,1)S(1)}, bf16[64,1024]{1,0:T(8,128)(2,1)S(1)}, u32[]{:S(2)}, u32[]{:S(2)}) collective-permute-start(bf16[64,1024]{1,0:T(8,128)(2,1)S(1)} %fusion.7), channel_id=1, source_target_pairs={{0,8},{4,12},{8,0},{12,4},{16,24},{20,28},{24,16},{28,20},{1,9},{5... | collective-permute-start | bytes 393224 | tf_op jit(solution)/shard_map/ppermute | solution.py:459
  68.8 9.8 %collective-permute-start.20 = (bf16[64,896]{1,0:T(8,128)(2,1)S(1)}, bf16[64,896]{1,0:T(8,128)(2,1)S(1)}, u32[]{:S(2)}, u32[]{:S(2)}) collective-permute-start(bf16[64,896]{1,0:T(8,128)(2,1)S(1)} %fusion.5), channel_id=1, source_target_pairs={{0,16},{4,20},{8,24},{12,28},{16,0},{20,4},{24,8},{28,12},{1,17},{... | collective-permute-start | bytes 344072 | tf_op jit(solution)/shard_map/ppermute | solution.py:459
  73.1 9.3 %collective-permute-start.24 = (bf16[64,1024]{1,0:T(8,128)(2,1)S(1)}, bf16[64,1024]{1,0:T(8,128)(2,1)S(1)}, u32[]{:S(2)}, u32[]{:S(2)}) collective-permute-start(bf16[64,1024]{1,0:T(8,128)(2,1)S(1)} %fusion.2), channel_id=1, source_target_pairs={{0,16},{4,20},{8,24},{12,28},{16,0},{20,4},{24,8},{28,12},{1,17},{... | collective-permute-start | bytes 393224 | tf_op jit(solution)/shard_map/ppermute | solution.py:459
  75.8 8.8 %collective-permute-start.26 = (bf16[64,1152]{1,0:T(8,128)(2,1)S(1)}, bf16[64,1152]{1,0:T(8,128)(2,1)S(1)}, u32[]{:S(2)}, u32[]{:S(2)}) collective-permute-start(bf16[64,1152]{1,0:T(8,128)(2,1)S(1)} %get-tuple-element.153), channel_id=1, source_target_pairs={{0,4},{4,0},{8,12},{12,8},{16,20},{20,16},{24,28},{28,24},{1,5},{5... | collective-permute-start | bytes 442376 | tf_op jit(solution)/shard_map/ppermute | solution.py:388
  82.5 7.7 %collective-permute-start.25 = (bf16[64,1024]{1,0:T(8,128)(2,1)S(1)}, bf16[64,1024]{1,0:T(8,128)(2,1)S(1)}, u32[]{:S(2)}, u32[]{:S(2)}) collective-permute-start(bf16[64,1024]{1,0:T(8,128)(2,1)S(1)} %get-tuple-element.149), channel_id=1, source_target_pairs={{0,4},{4,0},{8,12},{12,8},{16,20},{20,16},{24,28},{28,24},{1,5},{5... | collective-permute-start | bytes 393224 | tf_op jit(solution)/shard_map/ppermute | solution.py:388
  84.1 6.1 %collective-permute-start.23 = (bf16[64,896]{1,0:T(8,128)(2,1)S(1)}, bf16[64,896]{1,0:T(8,128)(2,1)S(1)}, u32[]{:S(2)}, u32[]{:S(2)}) collective-permute-start(bf16[64,896]{1,0:T(8,128)(2,1)S(1)} %get-tuple-element.151), channel_id=1, source_target_pairs={{0,4},{4,0},{8,12},{12,8},{16,20},{20,16},{24,28},{28,24},{1,5},{5... | collective-permute-start | bytes 344072 | tf_op jit(solution)/shard_map/ppermute | solution.py:388
